TPU v7x, 32 devices: a whole 2x2x4 slice. The times are simulated.
32 devices in a mesh: lat: 4 (over z), wid: 2 (over core), tok: 4 (over y, x).
Axes of the slice: x: 2, y: 2, z: 4, core: 2. Of those that a mesh axis runs over, the one named last changes fastest.
Arguments:
- resid: bfloat16 [512, 4096], P('tok', 'wid'), may hold values from -6 to 6
- dictionary: bfloat16 [2048, 4096], P('lat', 'wid'), may hold values from -0.1875 to 0.1875
- enc_bias: float32 [2048], P('lat'), may hold values from -3 to 3
- dec_bias: float32 [4096], P('wid'), may hold values from -3 to 3
- active_blocks: int32 [512, 8], P('tok'), may hold values from 0 to 15, all different within a row
- level_bounds: int32 [4], replicated, may hold values from 1 to 16, as said below
Outputs:
- level_losses: float32 [4], replicated
- dict_grad: bfloat16 [4096, 2048], P(('wid', 'tok'), 'lat')
Inputs may be any that keep to these rules, and one draw needn't show every extreme that they name: `active_blocks`: each row names 8 different blocks. `level_bounds`: strictly increasing; the last equals 16.
All inputs are finite; a program needn't handle non-finite values.
Results may differ from a plain program's by a relative error of at most 0.006.
Values sent between devices are 32-bit elements; how exact they have to be, the bound alone decides.
No kernel may reach another device: no remote copies, remote signals or barrier semaphores. Data moves between devices by JAX's collectives and lax.ppermute only.
A program may use at most 192 MiB of HBM per device.

v0:
```python
import jax
import jax.numpy as jnp
from jax import lax
from jax.sharding import PartitionSpec as P

LEVELS = 4


def entering(part, axis, combine, identity):
    place = lax.axis_index(axis)
    gathered = lax.all_gather(part, axis)
    state = jnp.zeros_like(part) + jnp.asarray(identity, part.dtype)

    def one(turn, state):
        return combine(state, lax.dynamic_index_in_dim(gathered, turn, 0, False))

    return lax.fori_loop(0, place, one, state)


def broadcast(array, axis, root):
    mine = lax.axis_index(axis) == root
    return lax.psum(jnp.where(mine, array, jnp.zeros_like(array)), axis)


def gelu_tanh(value):
    return jax.nn.gelu(value, approximate=True)


def add_pair(earlier, later):
    return earlier + later


def body(resid, dictionary, enc_bias, dec_bias, active_blocks, level_bounds):
    row_count, half_width = resid.shape
    lat_count = dictionary.shape[0]
    blocks_here = lat_count // 128
    lat_position = lax.axis_index("lat")
    first_block = lat_position * blocks_here
    local_ids = first_block + jnp.arange(blocks_here, dtype=jnp.int32)
    resid_full = resid.astype(jnp.float32)
    dict_blocks = dictionary.reshape(blocks_here, 128, half_width)
    partial_pre = lax.dot_general(
        resid, dictionary, (((1,), (1,)), ((), ())), preferred_element_type=jnp.float32
    )
    pre = lax.psum(partial_pre, "wid") + enc_bias[None, :]
    hits = jnp.any(active_blocks[:, :, None] == local_ids[None, None, :], axis=1).astype(
        jnp.float32
    )
    act = (gelu_tanh(pre).reshape(row_count, blocks_here, 128) * hits[:, :, None]).astype(
        jnp.bfloat16
    )
    act_flat = act.reshape(row_count, lat_count)
    latent_block = jnp.arange(lat_count, dtype=jnp.int32) // 128
    owners = []
    keeps = []
    for level in range(LEVELS):
        bound = level_bounds[level]
        owners.append((bound - 1) // blocks_here)
        inside = jnp.clip(bound - 1 - first_block, 0, blocks_here - 1)
        keeps.append(latent_block <= inside)
    keeps.append(latent_block >= 0)
    keep_rows = jnp.stack(keeps)
    act_stack = jnp.where(keep_rows[:, None, :], act_flat[None], jnp.zeros((), jnp.bfloat16))
    partials = jnp.dot(
        act_stack.reshape((LEVELS + 1) * row_count, lat_count),
        dictionary,
        preferred_element_type=jnp.float32,
    )
    partials = partials.reshape(LEVELS + 1, row_count, half_width)
    zeros_field = jnp.zeros((row_count, half_width), jnp.float32)
    earlier = entering(partials[LEVELS], "lat", add_pair, zeros_field)
    own_errors = []
    squares = []
    for level in range(LEVELS):
        mine = owners[level] == lat_position
        error = dec_bias[None, :] + earlier + partials[level] - resid_full
        own_errors.append(jnp.where(mine, error, 0.0))
        squares.append(jnp.where(mine, jnp.sum(error * error), 0.0))
    include = (level_bounds[:, None] > local_ids[None, :]).astype(jnp.float32)
    err_sum = None
    for level in range(LEVELS):
        level_err = broadcast(own_errors[level], "lat", owners[level])
        term = include[level][:, None, None] * level_err[None]
        err_sum = term if err_sum is None else err_sum + term
    err_half = err_sum.astype(jnp.bfloat16)
    partial_adjoint = jnp.einsum(
        "ktd,kcd->tkc", err_half, dict_blocks, preferred_element_type=jnp.float32
    )
    g_act = lax.psum(partial_adjoint.reshape(row_count, lat_count), "wid")
    mask_full = jnp.broadcast_to(hits[:, :, None], (row_count, blocks_here, 128)).reshape(
        row_count, lat_count
    )
    _, pull = jax.vjp(gelu_tanh, pre)
    g_pre = pull(g_act * mask_full)[0].astype(jnp.bfloat16)
    decode_term = jnp.einsum("ktd,tkc->dkc", err_half, act, preferred_element_type=jnp.float32)
    encode_term = lax.dot_general(
        resid, g_pre, (((0,), (0,)), ((), ())), preferred_element_type=jnp.float32
    )
    grad_share = lax.psum_scatter(
        decode_term.reshape(half_width // lax.axis_size("tok") * lax.axis_size("tok"), lat_count)
        + encode_term,
        "tok",
        scatter_dimension=0,
        tiled=True,
    )
    total_sq = lax.psum(jnp.stack(squares), ("lat", "wid", "tok"))
    level_losses = total_sq / (row_count * lax.axis_size("tok") * half_width * lax.axis_size("wid"))
    return (level_losses, grad_share.astype(jnp.bfloat16))


def solution(mesh):
    return jax.shard_map(
        body,
        mesh=mesh,
        in_specs=(P("tok", "wid"), P("lat", "wid"), P("lat"), P("wid"), P("tok", None), P()),
        out_specs=(P(), P(("wid", "tok"), "lat")),
        check_vma=False,
    )
```

profile of v0, /device:TPU:0, one launch (start us, length us, event | category | flops | bytes accessed | tf_op | source)
XLA Modules:
  0.0 376.8 jit_solution(13981214905266907909)
XLA Ops:
  7.2 1.5 copy-done
  8.8 2.6 fusion.25
  11.4 0.0 all-gather.3.cloned.1.call-start
  11.4 1.5 fusion.23
  12.9 0.8 compare_reduce_fusion
  16.2 0.1 copy.17
  16.4 16.0 %all-reduce.5.cloned.1.call-done = f32[128,512]{1,0:T(8,128)} async-done(((f32[128,512]{1,0:T(8,128)}), f32[128,512]{1,0:T(8,128)}) %all-reduce.5.cloned.1.call-update) | async-done | bytes 262160 | tf_op jit(solution)/shard_map/psum | solution.py:45
  32.5 1.8 multiply_convert_fusion.1
  34.3 1.6 fusion.26
  35.8 2.3 copy-done.1
  38.1 1.0 slice.60
  39.4 81.9 %all-gather.3.cloned.1.call-done = f32[512,2048]{1,0:T(8,128)} async-done(((f32[128,2048]{1,0:T(8,128)}), f32[512,2048]{1,0:T(8,128)}) %all-gather.3.cloned.1.call-update) | async-done | bytes 4194320 | tf_op jit(solution)/shard_map/all_gather | solution.py:11
  121.3 0.1 broadcast.226
  121.4 0.7 copy-done.6
  122.1 5.8 %select_select_fusion.3 = (f32[128,2048]{1,0:T(8,128)}, f32[128,2048]{1,0:T(8,128)}, f32[128,2048]{1,0:T(8,128)}, f32[128,2048]{1,0:T(8,128)}, f32[]{:T(128)}, /*index=5*/f32[]{:T(128)}, f32[]{:T(128)}, f32[]{:T(128)}) fusion(pred[]{:T(512)S(6)} %eq.37, pred[]{:T(512)S(6)} %eq.44, bf16[128,2048]{1,0:T(8,128)(2,1)} %param.8, f32[640,2048]{1,0:T(8,128)} %copy-done.1, ...), kind=kLoop, calls=%fused_computation.14 | loop fusion | flops 6815740 | bytes 9969688 | tf_op jit(solution)/shard_map/jit(_where)/select_n | solution.py:22
  127.9 0.0 all-reduce.7.cloned.1.call-start
  128.0 0.6 copy-done.5
  128.5 0.1 compare_convert_fusion
  128.6 0.2 copy-done.3
  128.9 0.1 copy.18
  129.0 157.4 %all-reduce.9.cloned.1.call-done = (f32[128,2048]{1,0:T(8,128)}, f32[128,2048]{1,0:T(8,128)}, f32[128,2048]{1,0:T(8,128)}, f32[128,2048]{1,0:T(8,128)}) async-done(((f32[128,2048]{1,0:T(8,128)}, f32[128,2048]{1,0:T(8,128)}, f32[128,2048]{1,0:T(8,128)}, f32[128,2048]{1,0:T(8,128)}), (f32[128,2048]{1,0:T(8,128)}, f32[128,2048]{1,0:T(8,128)}, f32[128,2048]{1,0:T(8,128)}, ...) | async-done | bytes 4194320 | tf_op jit(solution)/shard_map/psum | solution.py:22
  286.4 3.5 fusion.24
  289.9 0.8 copy.19
  290.9 5.7 %fusion.7 = f32[4,128,2048]{2,1,0:T(8,128)} fusion(f32[128,4,128]{0,2,1:T(8,128)S(1)} %bitcast.43, f32[128,4]{0,1:T(4,128)S(1)} %convert_element_type.29, f32[128,2048]{1,0:T(8,128)} %get-tuple-element.42, f32[4]{0:T(128)S(1)} %get-tuple-element.57, f32[128,2048]{1,0:T(8,128)} %get-tuple-element.43, f32[4]{0:T(128)S(1)} %get-tuple-element.58, ...), kind=kOutput, calls=%fused_computation.32 | convolution fusion | flops 276955136 | bytes 8652864 | tf_op jit(solution)/shard_map/ktd,tkc->dkc/dot_general | solution.py:95
  296.5 11.6 %all-reduce.7.cloned.1.call-done = f32[128,512]{1,0:T(8,128)} async-done(((f32[128,512]{1,0:T(8,128)}), f32[128,512]{1,0:T(8,128)}) %all-reduce.7.cloned.1.call-update) | async-done | bytes 262160 | tf_op jit(solution)/shard_map/psum | solution.py:89
  308.1 5.1 %bitcast_add_fusion.1 = f32[2048,512]{0,1:T(8,128)} fusion(f32[4,128,2048]{2,1,0:T(8,128)} %fusion.7, bf16[128,2048]{1,0:T(8,128)(2,1)S(1)} %copy-done.2, f32[128,512]{1,0:T(8,128)} %all-reduce.7.cloned.1.call-done, f32[128,512]{1,0:T(8,128)S(1)} %copy.17, f32[128,512]{1,0:T(8,128)S(1)} %copy-done.4, f32[512]{0:T(512)S(1)} %copy-done.7), kind=kOutput, calls=%fused_computation.1 | convolution fusion | flops 270925824 | bytes 9701376 | tf_op jit(solution)/shard_map/dot_general | solution.py:96
  315.8 0.1 pad_maximum_fusion
  315.9 40.7 %psum.50 = f32[4]{0:T(128)S(1)} all-reduce(f32[4]{0:T(128)S(1)} %pad_maximum_fusion), channel_id=1, replica_groups=mesh['lat'=4,'wid'=2,'tok'=4] {'lat','wid','tok'}, use_global_device_ids=true, to_apply=%region_8.9 | all-reduce | flops 4 | bytes 32 | tf_op jit(solution)/shard_map/psum | solution.py:106
  356.6 0.5 broadcast_multiply_fusion
  357.1 10.9 %reduce-scatter.2.cloned.1.call-done = f32[512,512]{0,1:T(8,128)} async-done(((f32[2048,512]{0,1:T(8,128)}), f32[512,512]{0,1:T(8,128)}) %reduce-scatter.2.cloned.1.call-update) | async-done | bytes 1048592 | tf_op jit(solution)/shard_map/reduce_scatter | solution.py:99
  368.0 1.3 convert_element_type.36
  369.3 1.0 copy.16
  (29 shorter events, 0.4 us)
Async XLA Ops:
  7.2 1.6 copy-start
  7.2 25.3 %all-reduce.5.cloned.1.call-start = ((), (), s32[]{:S(2)}) async-start(), calls=%async_computation.1 | async-start | bytes 524288 | tf_op jit(solution)/shard_map/psum | solution.py:45
  11.4 109.9 %all-gather.3.cloned.1.call-start = ((), (), s32[]{:S(2)}) async-start(), calls=%async_computation.4 | async-start | bytes 5242880 | tf_op jit(solution)/shard_map/all_gather | solution.py:11
  35.8 2.3 copy-start.1
  39.2 247.2 %all-reduce.9.cloned.1.call-start = ((), (), s32[]{:S(2)}) async-start(), calls=%async_computation.5 | async-start | bytes 8388608 | tf_op jit(solution)/shard_map/psum | solution.py:22
  121.4 0.7 copy-start.6
  127.9 0.7 copy-start.5
  127.9 1.0 copy-start.3
  127.9 180.2 %all-reduce.7.cloned.1.call-start = ((), (), s32[]{:S(2)}) async-start(), calls=%async_computation.2 | async-start | bytes 524288 | tf_op jit(solution)/shard_map/psum | solution.py:89
  290.8 77.2 %reduce-scatter.2.cloned.1.call-start = ((), (), s32[]{:S(2)}) async-start(), calls=%async_computation.3 | async-start | bytes 5242880 | tf_op jit(solution)/shard_map/reduce_scatter | solution.py:99
  290.8 17.3 %copy-start.2 = (bf16[128,2048]{1,0:T(8,128)(2,1)S(1)}, bf16[128,2048]{1,0:T(8,128)(2,1)}, u32[]{:S(2)}) copy-start(bf16[128,2048]{1,0:T(8,128)(2,1)} %param.8) | copy-start | bytes 1572868
  290.8 17.3 %copy-start.4 = (f32[128,512]{1,0:T(8,128)S(1)}, f32[128,512]{1,0:T(8,128)}, u32[]{:S(2)}) copy-start(f32[128,512]{1,0:T(8,128)} %all-reduce.5.cloned.1.call-done) | copy-start | bytes 786436
  290.8 17.3 %copy-start.7 = (f32[512]{0:T(512)S(1)}, f32[512]{0:T(512)}, u32[]{:S(2)}) copy-start(f32[512]{0:T(512)} %param.10) | copy-start | bytes 6148
Sparse Core Ops, SparseCore 0:
  11.5 20.9 all-reduce.4
  39.3 81.9 all-gather.2
  128.0 158.3 all-reduce.8
  290.9 17.1 all-reduce.6
  313.4 54.5 reduce-scatter.1
where the time goes:
time: 377 us
  waiting for transfers between devices  278 us (74%)
  blocking collectives  40.7 us (11%)
  between operations  19.1 us (5%)
  matrix products  18.4 us (5%)
  other arithmetic  10.4 us (3%)
  local copies, waits for them, and re-layouts  10.1 us (3%)
    psum x1, waiting for transfers between devices, broadcast(): return lax.psum(jnp.where(mine, array, jnp.zeros_like(array)), axis)  157 us
    all_gather x1, waiting for transfers between devices, entering(): gathered = lax.all_gather(part, axis)  81.9 us
    psum x1, blocking collectives, body(): total_sq = lax.psum(jnp.stack(squares), ('lat', 'wid', 'tok'))  40.7 us
    psum x1, waiting for transfers between devices, body(): pre = lax.psum(partial_pre, 'wid') + enc_bias[None, :]  16 us
    psum x1, waiting for transfers between devices, body(): g_act = lax.psum(partial_adjoint.reshape(row_count, lat_count), 'wid')  11.6 us
    reduce_scatter x1, waiting for transfers between devices, body(): lax.psum_scatter(decode_term.reshape(half_width // lax.axis_size('tok') *...  10.9 us
  transfers between devices with their start and end apart: 5, of which 5 were waited for; matrix products, arithmetic and copies ran while one was open for 2% of the time, Pallas kernels for 0%

commit v1 on v0

v1 whole, which is shorter than its diff:
```python
import functools

import jax
import jax.numpy as jnp
from jax import lax
from jax.experimental import pallas as pl
from jax.experimental.pallas import tpu as pltpu
from jax.sharding import PartitionSpec as P

LEVELS = 4
BLOCK = 128
GELU_C = 0.7978845608028654
GELU_A = 0.044715

VMEM = pl.BlockSpec(memory_space=pltpu.VMEM)
SMEM = pl.BlockSpec(memory_space=pltpu.SMEM)


def f32(shape):
    return jax.ShapeDtypeStruct(shape, jnp.float32)


def call(kernel, out_shape, in_specs, flops=0, scratch=()):
    outs = out_shape if isinstance(out_shape, (list, tuple)) else [out_shape]
    size = sum(o.size * o.dtype.itemsize for o in outs)
    return pl.pallas_call(
        kernel,
        out_shape=out_shape,
        in_specs=in_specs,
        out_specs=jax.tree.map(lambda _: VMEM, out_shape),
        scratch_shapes=list(scratch),
        compiler_params=pltpu.CompilerParams(vmem_limit_bytes=40 * 1024 * 1024),
        cost_estimate=pl.CostEstimate(flops=flops, bytes_accessed=2 * size, transcendentals=0),
    )


def block_mask(active_ref, first, lats):
    ids = first + lax.broadcasted_iota(jnp.int32, (1, lats), 1) // BLOCK
    hit = None
    for q in range(active_ref.shape[1]):
        same = active_ref[:, q : q + 1] == ids
        hit = same if hit is None else hit | same
    return hit


def activate_kernel(first_ref, mine, other, bias, active, pre_out, act_out):
    first = first_ref[0]
    pre = mine[...] + other[...] + bias[...]
    pre_out[...] = pre
    inner = GELU_C * (pre + GELU_A * (pre * pre * pre))
    gelu = 0.5 * pre * (1.0 + jnp.tanh(inner))
    act_out[...] = jnp.where(block_mask(active, first, pre.shape[1]), gelu, 0.0)


def g_pre_kernel(first_ref, pre_ref, mine, other, active, out):
    first = first_ref[0]
    pre = pre_ref[...]
    inner = GELU_C * (pre + GELU_A * (pre * pre * pre))
    slope = GELU_C * (1.0 + 3.0 * GELU_A * (pre * pre))
    bend = jnp.tanh(inner)
    deriv = 0.5 * (1.0 + bend) + 0.5 * pre * (1.0 - bend * bend) * slope
    hit = block_mask(active, first, pre.shape[1])
    out[...] = jnp.where(hit, deriv * (mine[...] + other[...]), 0.0)


def block_weights(first, bounds, count):
    return [
        [(first + i < bounds[m]).astype(jnp.float32) for i in range(count)]
        for m in range(LEVELS)
    ]


def block_parts(act_ref, dict_ref, count):
    parts = []
    for i in range(count):
        span = slice(i * BLOCK, (i + 1) * BLOCK)
        parts.append(
            jnp.dot(
                act_ref[:, span].astype(jnp.bfloat16),
                dict_ref[span, :],
                preferred_element_type=jnp.float32,
            )
        )
    return parts


def weighted(weights, parts):
    total = None
    for weight, part in zip(weights, parts):
        term = weight * part
        total = term if total is None else total + term
    return total


def project_kernel(first_ref, bounds_ref, act, dictionary, up_out, down_out):
    first = first_ref[0]
    bounds = [bounds_ref[m] for m in range(LEVELS)]
    count = dictionary.shape[0] // BLOCK
    below = block_weights(first, bounds, count)
    parts = block_parts(act, dictionary, count)
    up_out[...] = functools.reduce(jnp.add, parts)
    down_out[...] = weighted(
        [functools.reduce(jnp.add, [below[m][i] for m in range(LEVELS)]) for i in range(count)], parts
    )


def error_kernel(
    first_ref, bounds_ref, act, dictionary, earlier, later, resid, bias, err_out, gact_out, sq_out
):
    first = first_ref[0]
    bounds = [bounds_ref[m] for m in range(LEVELS)]
    count = dictionary.shape[0] // BLOCK
    below = block_weights(first, bounds, count)
    parts = block_parts(act, dictionary, count)
    base = bias[...] - resid[...] + earlier[...]
    for m in range(LEVELS):
        last = bounds[m] - 1 - first
        mine = jnp.logical_and(last >= 0, last < count).astype(jnp.float32)
        err = base + weighted(below[m], parts)
        sq_out[m : m + 1, :] = mine * jnp.sum(err * err, axis=0, keepdims=True)
    tail = later[...]
    for i in range(count):
        pair = [
            functools.reduce(jnp.add, [below[m][i] * below[m][i2] for m in range(LEVELS)])
            for i2 in range(count)
        ]
        own = functools.reduce(jnp.add, [below[m][i] for m in range(LEVELS)])
        err = (own * base + tail + weighted(pair, parts)).astype(jnp.bfloat16)
        err_out[i] = err
        span = slice(i * BLOCK, (i + 1) * BLOCK)
        gact_out[:, span] = lax.dot_general(
            err, dictionary[span, :], (((1,), (1,)), ((), ())), preferred_element_type=jnp.float32
        )


def decode_kernel(*refs):
    chunks = (len(refs) - 1) // 2
    errs, acts, out = refs[:chunks], refs[chunks : 2 * chunks], refs[-1]
    for i in range(errs[0].shape[0]):
        span = slice(i * BLOCK, (i + 1) * BLOCK)
        err = jnp.concatenate([e[i] for e in errs], axis=0)
        act = jnp.concatenate([a[:, span].astype(jnp.bfloat16) for a in acts], axis=0)
        out[:, span] = lax.dot_general(
            err, act, (((0,), (0,)), ((), ())), preferred_element_type=jnp.float32
        )


def encode_kernel(*refs):
    chunks = (len(refs) - 2) // 2
    resids, grads, base, out = refs[:chunks], refs[chunks : 2 * chunks], refs[-2], refs[-1]
    resid = jnp.concatenate([r[...].astype(jnp.bfloat16) for r in resids], axis=0)
    grad = jnp.concatenate([g[...].astype(jnp.bfloat16) for g in grads], axis=0)
    total = base[...] + lax.dot_general(
        resid, grad, (((0,), (0,)), ((), ())), preferred_element_type=jnp.float32
    )
    out[...] = total.astype(jnp.bfloat16)


def pick(index, choices):
    values = sorted(choices)
    result = choices[values[0]]
    for value in values[1:]:
        result = jnp.where(index == value, choices[value], result)
    return result


def body(resid, dictionary, enc_bias, dec_bias, active_blocks, level_bounds):
    rows, half = resid.shape
    lats = dictionary.shape[0]
    n_lat, n_wid, n_tok = lax.axis_size("lat"), lax.axis_size("wid"), lax.axis_size("tok")
    lat, tok = lax.axis_index("lat"), lax.axis_index("tok")
    width = half // n_tok
    count = lats // BLOCK
    first = (lat * count).astype(jnp.int32).reshape(1)
    swap = [(w, w ^ 1) for w in range(n_wid)]

    def across(array, c):
        return lax.ppermute(array, "tok", [(t, t ^ c) for t in range(n_tok)])

    partial = lax.dot_general(
        resid, dictionary, (((1,), (1,)), ((), ())), preferred_element_type=jnp.float32
    )
    other = lax.ppermute(partial, "wid", swap)
    square = (rows, lats)
    pre, act = call(activate_kernel, [f32(square), f32(square)], [SMEM, VMEM, VMEM, VMEM, VMEM])(
        first, partial, other, enc_bias.reshape(1, lats), active_blocks
    )
    acts = [act] + [across(act, c) for c in range(1, n_tok)]

    dict_here = lax.dynamic_slice(dictionary, (0, tok * width), (lats, width))
    bias_here = lax.dynamic_slice(dec_bias, (tok * width,), (width,)).reshape(1, width)
    resids = []
    for c in range(n_tok):
        piece = lax.dynamic_slice(resid, (0, (tok ^ c) * width), (rows, width)).astype(jnp.float32)
        resids.append(piece if c == 0 else across(piece, c))

    tile = (rows, width)
    flops = 2 * rows * lats * width
    ups, downs = [], []
    for c in range(n_tok):
        up, down = call(project_kernel, [f32(tile), f32(tile)], [SMEM, SMEM, VMEM, VMEM], flops)(
            first, level_bounds, acts[c], dict_here
        )
        ups.append(up)
        downs.append(down)

    from_end = n_lat - 1 - lat
    got_up, got_down = [], []
    for step in range(n_tok + n_lat - 2):
        places = [p for p in range(n_lat - 1) if 0 <= step - p < n_tok]
        send_up = pick(lat, {p: ups[step - p] for p in places})
        send_down = pick(from_end, {p: downs[step - p] for p in places})
        if step > 0:
            send_up = send_up + got_up[-1]
            send_down = send_down + got_down[-1]
        got_up.append(lax.ppermute(send_up, "lat", [(p, p + 1) for p in places]))
        got_down.append(
            lax.ppermute(send_down, "lat", [(n_lat - 1 - p, n_lat - 2 - p) for p in places])
        )

    errs, gacts, squares = [], [], []
    for c in range(n_tok):
        earlier = pick(lat, {p: got_up[c + p - 1] for p in range(1, n_lat)})
        later = pick(from_end, {p: got_down[c + p - 1] for p in range(1, n_lat)})
        err, gact, square_sums = call(
            error_kernel,
            [
                jax.ShapeDtypeStruct((count,) + tile, jnp.bfloat16),
                f32(square),
                f32((LEVELS, width)),
            ],
            [SMEM, SMEM] + [VMEM] * 6,
            2 * flops,
        )(first, level_bounds, acts[c], dict_here, earlier, later, resids[c], bias_here)
        errs.append(err)
        gacts.append(gact if c == 0 else across(gact, c))
        squares.append(square_sums)

    gact_half = functools.reduce(jnp.add, gacts)
    gact_other = lax.ppermute(gact_half, "wid", swap)
    g_pre = call(g_pre_kernel, f32(square), [SMEM] + [VMEM] * 4)(
        first, pre, gact_half, gact_other, active_blocks
    )
    g_pres = [g_pre] + [across(g_pre, c) for c in range(1, n_tok)]
    decoded = call(decode_kernel, f32((width, lats)), [VMEM] * (2 * n_tok), 2 * n_tok * flops)(
        *errs, *acts
    )
    grad = call(
        encode_kernel,
        jax.ShapeDtypeStruct((width, lats), jnp.bfloat16),
        [VMEM] * (2 * n_tok + 1),
        2 * n_tok * flops,
    )(*resids, *g_pres, decoded)

    total = jnp.sum(functools.reduce(jnp.add, squares), axis=1)
    for axis in ("wid", "tok", "lat"):
        size, gap = lax.axis_size(axis), 1
        while gap < size:
            total = total + lax.ppermute(total, axis, [(p, p ^ gap) for p in range(size)])
            gap *= 2
    level_losses = total / (rows * n_tok * half * n_wid)
    return (level_losses, grad)


def solution(mesh):
    return jax.shard_map(
        body,
        mesh=mesh,
        in_specs=(P("tok", "wid"), P("lat", "wid"), P("lat"), P("wid"), P("tok", None), P()),
        out_specs=(P(), P(("wid", "tok"), "lat")),
        check_vma=False,
    )
```

time: 377 us -> 124 us (0.33)
  waiting for transfers between devices: 278 us -> 40.2 us
  starting transfers between devices: 0.2 us -> 47.6 us
  blocking collectives: 40.7 us -> 0 us
  between operations: 19.1 us -> 1.1 us
  matrix products: 18.4 us -> 1.87 us
  Pallas kernels: 0 us -> 16 us
  local copies, waits for them, and re-layouts: 10.1 us -> 4.72 us
    psum x3 -> x0, waiting for transfers between devices: 185 us -> none  [the longest x1 157 us: broadcast(): return lax.psum(jnp.where(mine, array, jnp.zeros_like(array)), axis)]
    all_gather x1 -> x0, waiting for transfers between devices: 81.9 us -> none  [entering(): gathered = lax.all_gather(part, axis)]
    ppermute x0 -> x31, starting transfers between devices: none -> 47.6 us  [the longest x6 20.3 us: body(): got_up.append(lax.ppermute(send_up, 'lat', [(p, p + 1) for p in places]))]
    psum x1 -> x0, blocking collectives: 40.7 us -> none  [body(): total_sq = lax.psum(jnp.stack(squares), ('lat', 'wid', 'tok'))]
    ppermute x0 -> x31, waiting for transfers between devices: none -> 40.2 us  [the longest x5 19.3 us: body(): lax.ppermute(total, axis, [(p, p ^ gap) for p in range(size)])]
    pallas_call x0 -> x12, Pallas kernels: none -> 16 us  [the longest x4 7.89 us: body(): call(error_kernel, [jax.ShapeDtypeStruct((count,) + tile, jnp.bfloat16),...]
    dot_general x4 -> x0, matrix products: 15.8 us -> none  [the longest x1 5.67 us: body(): jnp.einsum('ktd,tkc->dkc', err_half, act, preferred_element_type=jnp.floa...]
    reduce_scatter x1 -> x0, waiting for transfers between devices: 10.9 us -> none  [body(): lax.psum_scatter(decode_term.reshape(half_width // lax.axis_size('tok') *...]
  transfers between devices with their start and end apart: 5 -> 31, of which waited for: 5 -> 14; matrix products, arithmetic and copies ran while one was open for 2% -> 11% of each run, Pallas kernels for 0% -> 11%
where the time goes in v1:
time: 124 us
  starting transfers between devices  47.6 us (38%)
  waiting for transfers between devices  40.2 us (32%)
  Pallas kernels  16 us (13%)
  other arithmetic  12.3 us (10%)
  local copies, waits for them, and re-layouts  4.72 us (4%)
  matrix products  1.87 us (2%)
    ppermute x6, starting transfers between devices, body(): got_up.append(lax.ppermute(send_up, 'lat', [(p, p + 1) for p in places]))  20.3 us
    ppermute x5, waiting for transfers between devices, body(): lax.ppermute(total, axis, [(p, p ^ gap) for p in range(size)])  19.3 us
    ppermute x12, starting transfers between devices, across(): return lax.ppermute(array, 'tok', [(t, t ^ c) for t in range(n_tok)])  16.6 us
    ppermute x6, waiting for transfers between devices, body(): lax.ppermute(send_down, 'lat', [(n_lat - 1 - p, n_lat - 2 - p) for p in p...  10.9 us
    pallas_call x4, Pallas kernels, body(): call(error_kernel, [jax.ShapeDtypeStruct((count,) + tile, jnp.bfloat16),...  7.89 us
    ppermute x6, starting transfers between devices, body(): lax.ppermute(send_down, 'lat', [(n_lat - 1 - p, n_lat - 2 - p) for p in p...  7.51 us
    ppermute x12, waiting for transfers between devices, across(): return lax.ppermute(array, 'tok', [(t, t ^ c) for t in range(n_tok)])  4.24 us
    pallas_call x4, Pallas kernels, body(): call(project_kernel, [f32(tile), f32(tile)], [SMEM, SMEM, VMEM, VMEM], fl...  4.02 us
  transfers between devices with their start and end apart: 31, of which 14 were waited for; matrix products, arithmetic and copies ran while one was open for 11% of the time, Pallas kernels for 11%

profile of v1, /device:TPU:0, one launch (start us, length us, event | category | flops | bytes accessed | tf_op | source)
XLA Modules:
  0.0 123.7 jit_solution(18147274264949609595)
XLA Ops:
  0.7 1.6 %copy-done = bf16[512,2048]{1,0:T(8,128)(2,1)S(1)} copy-done((bf16[512,2048]{1,0:T(8,128)(2,1)S(1)}, bf16[512,2048]{1,0:T(8,128)(2,1)}, u32[]{:S(2)}) %copy-start) | copy-done | bytes 2097176
  2.2 1.9 %fusion.mine = f32[128,512]{1,0:T(8,128)S(1)} fusion(bf16[128,2048]{1,0:T(8,128)(2,1)} %param.6, bf16[512,2048]{1,0:T(8,128)(2,1)S(1)} %copy-done), kind=kOutput, calls=%fused_computation.24 | convolution fusion | flops 268435456 | bytes 2883584 | tf_op jit(solution)/shard_map/dot_general | solution.py:180
  6.9 2.9 %collective-permute-start.1 = (f32[128,512]{1,0:T(8,128)S(1)}, f32[128,512]{1,0:T(8,128)S(1)}, u32[]{:S(2)}, u32[]{:S(2)}) collective-permute-start(f32[128,512]{1,0:T(8,128)S(1)} %get-tuple-element.24.act.refs_4_), channel_id=1, source_target_pairs={{0,1},{1,0},{2,3},{3,2},{4,5},{5,4},{6,7},{7,6},{8,9},{9,8},{10,11... | collective-permute-start | bytes 786440 | tf_op jit(solution)/shard_map/ppermute | solution.py:178
  9.8 1.5 %shard_map.78 = (f32[128,512]{1,0:T(8,128)}, f32[128,512]{1,0:T(8,128)S(1)}) custom-call(s32[1]{0:T(128)} %bitcast.first_ref, s32[4]{0:T(128)S(1)} %copy-done.14, f32[128,512]{1,0:T(8,128)S(1)} %get-tuple-element.24.act.refs_4_, bf16[512,512]{1,0:T(8,128)(2,1)S(1)} %constant_dynamic-slice_fusion.dictionary), custom_call_target="tpu_custom_call" | custom-call | flops 67108864 | bytes 1048576 | tf_op jit(solution)/shard_map/pallas_call | solution.py:201
  12.0 4.2 %collective-permute-start.3 = (f32[128,512]{1,0:T(8,128)}, f32[128,512]{1,0:T(8,128)}, u32[]{:S(2)}, u32[]{:S(2)}) collective-permute-start(f32[128,512]{1,0:T(8,128)} %get-tuple-element.25), channel_id=1, source_target_pairs={{0,8},{1,9},{2,10},{3,11},{4,12},{5,13},{6,14},{7,15}} | collective-permute-start | bytes 786440 | tf_op jit(solution)/shard_map/ppermute | solution.py:216
  16.2 1.5 %collective-permute-start.2 = (f32[128,512]{1,0:T(8,128)S(1)}, f32[128,512]{1,0:T(8,128)S(1)}, u32[]{:S(2)}, u32[]{:S(2)}) collective-permute-start(f32[128,512]{1,0:T(8,128)S(1)} %get-tuple-element.24.act.refs_4_), channel_id=1, source_target_pairs={{0,2},{1,3},{2,0},{3,1},{4,6},{5,7},{6,4},{7,5},{8,10},{9,11},{10,... | collective-permute-start | bytes 786440 | tf_op jit(solution)/shard_map/ppermute | solution.py:178
  21.4 1.7 %select_add_fusion.6 = f32[128,512]{1,0:T(8,128)} fusion(f32[128,512]{1,0:T(8,128)} %collective-permute-done.3, f32[128,512]{1,0:T(8,128)} %get-tuple-element.25, f32[128,512]{1,0:T(8,128)S(1)} %get-tuple-element.26, pred[]{:T(512)S(6)} %eq.14), kind=kLoop, calls=%fused_computation.15 | loop fusion | flops 131072 | bytes 1048577 | tf_op jit(solution)/shard_map/add | solution.py:214
  23.1 5.2 %collective-permute-start.4 = (f32[128,512]{1,0:T(8,128)}, f32[128,512]{1,0:T(8,128)}, u32[]{:S(2)}, u32[]{:S(2)}) collective-permute-start(f32[128,512]{1,0:T(8,128)} %select_add_fusion.6), channel_id=1, source_target_pairs={{0,8},{8,16},{1,9},{9,17},{2,10},{10,18},{3,11},{11,19},{4,12},{12... | collective-permute-start | bytes 786440 | tf_op jit(solution)/shard_map/ppermute | solution.py:216
  28.3 1.5 %collective-permute-start.9 = (f32[128,512]{1,0:T(8,128)S(1)}, f32[128,512]{1,0:T(8,128)S(1)}, u32[]{:S(2)}, u32[]{:S(2)}) collective-permute-start(f32[128,512]{1,0:T(8,128)S(1)} %get-tuple-element.24.act.refs_4_), channel_id=1, source_target_pairs={{0,3},{1,2},{2,1},{3,0},{4,7},{5,6},{6,5},{7,4},{8,11},{9,10},{10,... | collective-permute-start | bytes 786440 | tf_op jit(solution)/shard_map/ppermute | solution.py:178
  33.6 4.5 %collective-permute-start.5 = (f32[128,512]{1,0:T(8,128)S(1)}, f32[128,512]{1,0:T(8,128)S(1)}, u32[]{:S(2)}, u32[]{:S(2)}) collective-permute-start(f32[128,512]{1,0:T(8,128)S(1)} %select_add_fusion.7), channel_id=1, source_target_pairs={{0,8},{8,16},{16,24},{1,9},{9,17},{17,25},{2,10},{10,18},{18,26},{... | collective-permute-start | bytes 786440 | tf_op jit(solution)/shard_map/ppermute | solution.py:216
  40.4 1.5 %collective-permute-done.5 = f32[128,512]{1,0:T(8,128)S(1)} collective-permute-done((f32[128,512]{1,0:T(8,128)S(1)}, f32[128,512]{1,0:T(8,128)S(1)}, u32[]{:S(2)}, u32[]{:S(2)}) %collective-permute-start.5) | collective-permute-done | bytes 262176 | tf_op jit(solution)/shard_map/ppermute | solution.py:216
  42.1 4.4 %collective-permute-start.10 = (f32[128,512]{1,0:T(8,128)S(1)}, f32[128,512]{1,0:T(8,128)S(1)}, u32[]{:S(2)}, u32[]{:S(2)}) collective-permute-start(f32[128,512]{1,0:T(8,128)S(1)} %select_add_fusion.3), channel_id=1, source_target_pairs={{0,8},{8,16},{16,24},{1,9},{9,17},{17,25},{2,10},{10,18},{18,26},{... | collective-permute-start | bytes 786440 | tf_op jit(solution)/shard_map/ppermute | solution.py:216
  48.8 1.5 %collective-permute-done.10 = f32[128,512]{1,0:T(8,128)S(1)} collective-permute-done((f32[128,512]{1,0:T(8,128)S(1)}, f32[128,512]{1,0:T(8,128)S(1)}, u32[]{:S(2)}, u32[]{:S(2)}) %collective-permute-start.10) | collective-permute-done | bytes 262176 | tf_op jit(solution)/shard_map/ppermute | solution.py:216
  51.1 4.7 %collective-permute-done.11 = f32[128,512]{1,0:T(8,128)S(1)} collective-permute-done((f32[128,512]{1,0:T(8,128)S(1)}, f32[128,512]{1,0:T(8,128)S(1)}, u32[]{:S(2)}, u32[]{:S(2)}) %collective-permute-start.11) | collective-permute-done | bytes 262176 | tf_op jit(solution)/shard_map/ppermute | solution.py:218
  60.1 2.0 %dynamic-slice_convert_fusion.2 = (f32[128,512]{1,0:T(8,128)}, f32[128,512]{1,0:T(8,128)S(1)}, f32[128,512]{1,0:T(8,128)}, f32[128,512]{1,0:T(8,128)}) fusion(bf16[128,2048]{1,0:T(8,128)(2,1)} %param.6, s32[]{:T(128)S(6)} %select_n.165, s32[]{:T(128)S(6)} %select_n.140, s32[]{:T(128)S(6)} %select_n.177, s32[]{:T(128)S(6)} %select_n.172), kind=kLoop, calls=%fused_computation.19 | loop fusion | flops 262144 | bytes 1572880 | tf_op jit(solution)/shard_map/convert_element_type | solution.py:194
  62.7 2.4 %collective-permute-start.18 = (f32[128,512]{1,0:T(8,128)}, f32[128,512]{1,0:T(8,128)}, u32[]{:S(2)}, u32[]{:S(2)}) collective-permute-start(f32[128,512]{1,0:T(8,128)} %get-tuple-element.48), channel_id=1, source_target_pairs={{0,3},{1,2},{2,1},{3,0},{4,7},{5,6},{6,5},{7,4},{8,11},{9,10},{10,... | collective-permute-start | bytes 786440 | tf_op jit(solution)/shard_map/ppermute | solution.py:178
  67.5 1.5 %collective-permute-start.17 = (f32[128,512]{1,0:T(8,128)S(1)}, f32[128,512]{1,0:T(8,128)S(1)}, u32[]{:S(2)}, u32[]{:S(2)}) collective-permute-start(f32[128,512]{1,0:T(8,128)S(1)} %add.91), channel_id=1, source_target_pairs={{8,0},{9,1},{10,2},{11,3},{12,4},{13,5},{14,6},{15,7}} | collective-permute-start | bytes 786440 | tf_op jit(solution)/shard_map/ppermute | solution.py:218
  69.0 1.5 %select_select_fusion.5 = (f32[128,512]{1,0:T(8,128)S(1)}, f32[128,512]{1,0:T(8,128)S(1)}, f32[128,512]{1,0:T(8,128)S(1)}, f32[128,512]{1,0:T(8,128)S(1)}) fusion(f32[128,512]{1,0:T(8,128)} %copy-done.24, f32[128,512]{1,0:T(8,128)} %copy-done.19, f32[128,512]{1,0:T(8,128)} %collective-permute-done.4, pred[]{:T(512)S(6)} %eq.13, pred[]{:T(512)S(6)} %eq.12, ...), kind=kLoop, calls=%fused_computation.9 | loop fusion | flops 524288 | bytes 2621442 | tf_op jit(solution)/shard_map/jit(_where)/select_n | solution.py:163
  70.5 5.3 %collective-permute-done.17 = f32[128,512]{1,0:T(8,128)S(1)} collective-permute-done((f32[128,512]{1,0:T(8,128)S(1)}, f32[128,512]{1,0:T(8,128)S(1)}, u32[]{:S(2)}, u32[]{:S(2)}) %collective-permute-start.17) | collective-permute-done | bytes 262176 | tf_op jit(solution)/shard_map/ppermute | solution.py:218
  77.1 2.1 %shard_map.83 = (bf16[4,128,512]{2,1,0:T(8,128)(2,1)S(1)}, f32[128,512]{1,0:T(8,128)S(1)}, f32[4,512]{1,0:T(4,128)S(1)}) custom-call(s32[1]{0:T(128)} %bitcast.first_ref, s32[4]{0:T(128)S(1)} %copy-done.14, f32[128,512]{1,0:T(8,128)S(1)} %collective-permute-done.1.act.refs_5_, bf16[512,512]{1,0:T(8,128)(2,1)S(1)} %constant_dynamic-slice_fusion.dictionary, ...), custom_call_target="tpu_custom_call" | custom-call | flops 134217728 | bytes 1589248 | tf_op jit(solution)/shard_map/pallas_call | solution.py:225
  79.8 2.1 %shard_map.85 = (bf16[4,128,512]{2,1,0:T(8,128)(2,1)S(1)}, f32[128,512]{1,0:T(8,128)S(1)}, f32[4,512]{1,0:T(4,128)S(1)}) custom-call(s32[1]{0:T(128)} %bitcast.first_ref, s32[4]{0:T(128)S(1)} %copy-done.14, f32[128,512]{1,0:T(8,128)S(1)} %copy-done.4, bf16[512,512]{1,0:T(8,128)(2,1)S(1)} %constant_dynamic-slice_fusion.dictionary, ...), custom_call_target="tpu_custom_call" | custom-call | flops 134217728 | bytes 1589248 | tf_op jit(solution)/shard_map/pallas_call | solution.py:225
  81.8 2.5 %collective-permute-start.26 = (f32[128,512]{1,0:T(8,128)S(1)}, f32[128,512]{1,0:T(8,128)S(1)}, u32[]{:S(2)}, u32[]{:S(2)}) collective-permute-start(f32[128,512]{1,0:T(8,128)S(1)} %get-tuple-element.41), channel_id=1, source_target_pairs={{0,3},{1,2},{2,1},{3,0},{4,7},{5,6},{6,5},{7,4},{8,11},{9,10},{10,... | collective-permute-start | bytes 786440 | tf_op jit(solution)/shard_map/ppermute | solution.py:178
  84.4 2.1 %shard_map.84 = (bf16[4,128,512]{2,1,0:T(8,128)(2,1)S(1)}, f32[128,512]{1,0:T(8,128)S(1)}, f32[4,512]{1,0:T(4,128)S(1)}) custom-call(s32[1]{0:T(128)} %bitcast.first_ref, s32[4]{0:T(128)S(1)} %copy-done.14, f32[128,512]{1,0:T(8,128)S(1)} %copy-done.2, bf16[512,512]{1,0:T(8,128)(2,1)S(1)} %constant_dynamic-slice_fusion.dictionary, ...), custom_call_target="tpu_custom_call" | custom-call | flops 134217728 | bytes 1589248 | tf_op jit(solution)/shard_map/pallas_call | solution.py:225
  87.0 1.6 %shard_map.81 = (bf16[4,128,512]{2,1,0:T(8,128)(2,1)S(1)}, f32[128,512]{1,0:T(8,128)S(1)}, f32[4,512]{1,0:T(4,128)S(1)}) custom-call(s32[1]{0:T(128)} %bitcast.first_ref, s32[4]{0:T(128)S(1)} %copy-done.14, f32[128,512]{1,0:T(8,128)S(1)} %get-tuple-element.24.act.refs_4_, bf16[512,512]{1,0:T(8,128)(2,1)S(1)} %constant_dynamic-slice_fusion.dictionary, ...), custom_call_target="tpu_custom_call" | custom-call | flops 134217728 | bytes 1589248 | tf_op jit(solution)/shard_map/pallas_call | solution.py:225
  89.4 3.5 %collective-permute-done.25 = f32[128,512]{1,0:T(8,128)S(1)} collective-permute-done((f32[128,512]{1,0:T(8,128)S(1)}, f32[128,512]{1,0:T(8,128)S(1)}, u32[]{:S(2)}, u32[]{:S(2)}) %collective-permute-start.25) | collective-permute-done | bytes 262176 | tf_op jit(solution)/shard_map/ppermute | solution.py:178
  95.1 1.6 %collective-permute-start.30 = (f32[128,512]{1,0:T(8,128)S(1)}, f32[128,512]{1,0:T(8,128)S(1)}, u32[]{:S(2)}, u32[]{:S(2)}) collective-permute-start(f32[128,512]{1,0:T(8,128)S(1)} %shard_map.86.refs_4_), channel_id=1, source_target_pairs={{0,3},{1,2},{2,1},{3,0},{4,7},{5,6},{6,5},{7,4},{8,11},{9,10},{10,... | collective-permute-start | bytes 786440 | tf_op jit(solution)/shard_map/ppermute | solution.py:178
  97.2 1.5 %collective-permute-start.28 = (f32[128,512]{1,0:T(8,128)S(1)}, f32[128,512]{1,0:T(8,128)S(1)}, u32[]{:S(2)}, u32[]{:S(2)}) collective-permute-start(f32[128,512]{1,0:T(8,128)S(1)} %shard_map.86.refs_4_), channel_id=1, source_target_pairs={{0,1},{1,0},{2,3},{3,2},{4,5},{5,4},{6,7},{7,6},{8,9},{9,8},{10,11... | collective-permute-start | bytes 786440 | tf_op jit(solution)/shard_map/ppermute | solution.py:178
  100.1 9.2 %collective-permute-done.20 = f32[4]{0:T(128)S(1)} collective-permute-done((f32[4]{0:T(128)S(1)}, f32[4]{0:T(128)S(1)}, u32[]{:S(2)}, u32[]{:S(2)}) %collective-permute-start.20) | collective-permute-done | bytes 48 | tf_op jit(solution)/shard_map/ppermute | solution.py:259
  110.7 2.1 %collective-permute-done.21 = f32[4]{0:T(128)S(1)} collective-permute-done((f32[4]{0:T(128)S(1)}, f32[4]{0:T(128)S(1)}, u32[]{:S(2)}, u32[]{:S(2)}) %collective-permute-start.21) | collective-permute-done | bytes 48 | tf_op jit(solution)/shard_map/ppermute | solution.py:259
  112.8 3.5 %collective-permute-done.22 = f32[4]{0:T(128)S(1)} collective-permute-done((f32[4]{0:T(128)S(1)}, f32[4]{0:T(128)S(1)}, u32[]{:S(2)}, u32[]{:S(2)}) %collective-permute-start.22) | collective-permute-done | bytes 48 | tf_op jit(solution)/shard_map/ppermute | solution.py:259
  116.4 4.4 %collective-permute-done.23 = f32[4]{0:T(128)S(1)} collective-permute-done((f32[4]{0:T(128)S(1)}, f32[4]{0:T(128)S(1)}, u32[]{:S(2)}, u32[]{:S(2)}) %collective-permute-start.23) | collective-permute-done | bytes 48 | tf_op jit(solution)/shard_map/ppermute | solution.py:259
  121.3 2.4 %shard_map.88 = bf16[512,512]{1,0:T(8,128)(2,1)} custom-call(f32[128,512]{1,0:T(8,128)S(1)} %get-tuple-element.47.resid.refs_0_, f32[128,512]{1,0:T(8,128)} %collective-permute-done.12.resid.refs_1_, f32[128,512]{1,0:T(8,128)} %collective-permute-done.15.resid.refs_2_, f32[128,512]{1,0:T(8,128)} %collective-permute-done.18.resid.refs_3_, ...), custom_call_target="tpu_custom_call" | custom-call | flops 536870912 | bytes 1048576 | tf_op jit(solution)/shard_map/pallas_call | solution.py:248
  (118 shorter events, 32.7 us)
Async XLA Ops:
  4.1 1.7 %collective-permute-start = (f32[128,512]{1,0:T(8,128)S(1)}, f32[128,512]{1,0:T(8,128)S(1)}, u32[]{:S(2)}, u32[]{:S(2)}) collective-permute-start(f32[128,512]{1,0:T(8,128)S(1)} %fusion.mine), channel_id=1, source_target_pairs={{0,4},{4,0},{1,5},{5,1},{2,6},{6,2},{3,7},{7,3},{8,12},{12,8},{9,1... | collective-permute-start | bytes 786440 | tf_op jit(solution)/shard_map/ppermute | solution.py:183
  6.9 12.2 %collective-permute-start.1 = (f32[128,512]{1,0:T(8,128)S(1)}, f32[128,512]{1,0:T(8,128)S(1)}, u32[]{:S(2)}, u32[]{:S(2)}) collective-permute-start(f32[128,512]{1,0:T(8,128)S(1)} %get-tuple-element.24.act.refs_4_), channel_id=1, source_target_pairs={{0,1},{1,0},{2,3},{3,2},{4,5},{5,4},{6,7},{7,6},{8,9},{9,8},{10,11... | collective-permute-start | bytes 786440 | tf_op jit(solution)/shard_map/ppermute | solution.py:178
  12.0 9.4 %collective-permute-start.3 = (f32[128,512]{1,0:T(8,128)}, f32[128,512]{1,0:T(8,128)}, u32[]{:S(2)}, u32[]{:S(2)}) collective-permute-start(f32[128,512]{1,0:T(8,128)} %get-tuple-element.25), channel_id=1, source_target_pairs={{0,8},{1,9},{2,10},{3,11},{4,12},{5,13},{6,14},{7,15}} | collective-permute-start | bytes 786440 | tf_op jit(solution)/shard_map/ppermute | solution.py:216
  16.2 15.5 %collective-permute-start.2 = (f32[128,512]{1,0:T(8,128)S(1)}, f32[128,512]{1,0:T(8,128)S(1)}, u32[]{:S(2)}, u32[]{:S(2)}) collective-permute-start(f32[128,512]{1,0:T(8,128)S(1)} %get-tuple-element.24.act.refs_4_), channel_id=1, source_target_pairs={{0,2},{1,3},{2,0},{3,1},{4,6},{5,7},{6,4},{7,5},{8,10},{9,11},{10,... | collective-permute-start | bytes 786440 | tf_op jit(solution)/shard_map/ppermute | solution.py:178
  17.7 12.1 %collective-permute-start.6 = (f32[128,512]{1,0:T(8,128)}, f32[128,512]{1,0:T(8,128)}, u32[]{:S(2)}, u32[]{:S(2)}) collective-permute-start(f32[128,512]{1,0:T(8,128)} %copy-done.10), channel_id=1, source_target_pairs={{24,16},{25,17},{26,18},{27,19},{28,20},{29,21},{30,22},{31,23}} | collective-permute-start | bytes 786440 | tf_op jit(solution)/shard_map/ppermute | solution.py:218
  23.1 9.5 %collective-permute-start.4 = (f32[128,512]{1,0:T(8,128)}, f32[128,512]{1,0:T(8,128)}, u32[]{:S(2)}, u32[]{:S(2)}) collective-permute-start(f32[128,512]{1,0:T(8,128)} %select_add_fusion.6), channel_id=1, source_target_pairs={{0,8},{8,16},{1,9},{9,17},{2,10},{10,18},{3,11},{11,19},{4,12},{12... | collective-permute-start | bytes 786440 | tf_op jit(solution)/shard_map/ppermute | solution.py:216
  28.3 9.8 %collective-permute-start.9 = (f32[128,512]{1,0:T(8,128)S(1)}, f32[128,512]{1,0:T(8,128)S(1)}, u32[]{:S(2)}, u32[]{:S(2)}) collective-permute-start(f32[128,512]{1,0:T(8,128)S(1)} %get-tuple-element.24.act.refs_4_), channel_id=1, source_target_pairs={{0,3},{1,2},{2,1},{3,0},{4,7},{5,6},{6,5},{7,4},{8,11},{9,10},{10,... | collective-permute-start | bytes 786440 | tf_op jit(solution)/shard_map/ppermute | solution.py:178
  30.9 8.1 %collective-permute-start.7 = (f32[128,512]{1,0:T(8,128)S(1)}, f32[128,512]{1,0:T(8,128)S(1)}, u32[]{:S(2)}, u32[]{:S(2)}) collective-permute-start(f32[128,512]{1,0:T(8,128)S(1)} %select_add_fusion.4), channel_id=1, source_target_pairs={{24,16},{16,8},{25,17},{17,9},{26,18},{18,10},{27,19},{19,11},{28,... | collective-permute-start | bytes 786440 | tf_op jit(solution)/shard_map/ppermute | solution.py:218
  33.6 8.3 %collective-permute-start.5 = (f32[128,512]{1,0:T(8,128)S(1)}, f32[128,512]{1,0:T(8,128)S(1)}, u32[]{:S(2)}, u32[]{:S(2)}) collective-permute-start(f32[128,512]{1,0:T(8,128)S(1)} %select_add_fusion.7), channel_id=1, source_target_pairs={{0,8},{8,16},{16,24},{1,9},{9,17},{17,25},{2,10},{10,18},{18,26},{... | collective-permute-start | bytes 786440 | tf_op jit(solution)/shard_map/ppermute | solution.py:216
  39.0 16.8 %copy-start.5 = (f32[128,512]{1,0:T(8,128)}, f32[128,512]{1,0:T(8,128)S(1)}, u32[]{:S(2)}) copy-start(f32[128,512]{1,0:T(8,128)S(1)} %get-tuple-element.33) | copy-start | bytes 786436
  39.1 8.3 %collective-permute-start.8 = (f32[128,512]{1,0:T(8,128)S(1)}, f32[128,512]{1,0:T(8,128)S(1)}, u32[]{:S(2)}, u32[]{:S(2)}) collective-permute-start(f32[128,512]{1,0:T(8,128)S(1)} %select_add_fusion.5), channel_id=1, source_target_pairs={{24,16},{16,8},{8,0},{25,17},{17,9},{9,1},{26,18},{18,10},{10,2},{... | collective-permute-start | bytes 786440 | tf_op jit(solution)/shard_map/ppermute | solution.py:218
  42.1 8.3 %collective-permute-start.10 = (f32[128,512]{1,0:T(8,128)S(1)}, f32[128,512]{1,0:T(8,128)S(1)}, u32[]{:S(2)}, u32[]{:S(2)}) collective-permute-start(f32[128,512]{1,0:T(8,128)S(1)} %select_add_fusion.3), channel_id=1, source_target_pairs={{0,8},{8,16},{16,24},{1,9},{9,17},{17,25},{2,10},{10,18},{18,26},{... | collective-permute-start | bytes 786440 | tf_op jit(solution)/shard_map/ppermute | solution.py:216
  47.5 8.3 %collective-permute-start.11 = (f32[128,512]{1,0:T(8,128)S(1)}, f32[128,512]{1,0:T(8,128)S(1)}, u32[]{:S(2)}, u32[]{:S(2)}) collective-permute-start(f32[128,512]{1,0:T(8,128)S(1)} %select_add_fusion.2), channel_id=1, source_target_pairs={{24,16},{16,8},{8,0},{25,17},{17,9},{9,1},{26,18},{18,10},{10,2},{... | collective-permute-start | bytes 786440 | tf_op jit(solution)/shard_map/ppermute | solution.py:218
  50.4 7.5 %collective-permute-start.13 = (f32[128,512]{1,0:T(8,128)S(1)}, f32[128,512]{1,0:T(8,128)S(1)}, u32[]{:S(2)}, u32[]{:S(2)}) collective-permute-start(f32[128,512]{1,0:T(8,128)S(1)} %select_add_fusion.1), channel_id=1, source_target_pairs={{8,16},{16,24},{9,17},{17,25},{10,18},{18,26},{11,19},{19,27},{12,... | collective-permute-start | bytes 786440 | tf_op jit(solution)/shard_map/ppermute | solution.py:216
  56.6 9.9 %collective-permute-start.14 = (f32[128,512]{1,0:T(8,128)}, f32[128,512]{1,0:T(8,128)}, u32[]{:S(2)}, u32[]{:S(2)}) collective-permute-start(f32[128,512]{1,0:T(8,128)} %select_add_fusion), channel_id=1, source_target_pairs={{16,8},{8,0},{17,9},{9,1},{18,10},{10,2},{19,11},{11,3},{20,12},{1... | collective-permute-start | bytes 786440 | tf_op jit(solution)/shard_map/ppermute | solution.py:218
  58.7 10.3 %collective-permute-start.16 = (f32[128,512]{1,0:T(8,128)}, f32[128,512]{1,0:T(8,128)}, u32[]{:S(2)}, u32[]{:S(2)}) collective-permute-start(f32[128,512]{1,0:T(8,128)} %add.90), channel_id=1, source_target_pairs={{16,24},{17,25},{18,26},{19,27},{20,28},{21,29},{22,30},{23,31}} | collective-permute-start | bytes 786440 | tf_op jit(solution)/shard_map/ppermute | solution.py:216
  62.1 14.9 %collective-permute-start.12 = (f32[128,512]{1,0:T(8,128)}, f32[128,512]{1,0:T(8,128)}, u32[]{:S(2)}, u32[]{:S(2)}) collective-permute-start(f32[128,512]{1,0:T(8,128)} %get-tuple-element.46), channel_id=1, source_target_pairs={{0,1},{1,0},{2,3},{3,2},{4,5},{5,4},{6,7},{7,6},{8,9},{9,8},{10,11... | collective-permute-start | bytes 786440 | tf_op jit(solution)/shard_map/ppermute | solution.py:178
  62.7 17.1 %collective-permute-start.18 = (f32[128,512]{1,0:T(8,128)}, f32[128,512]{1,0:T(8,128)}, u32[]{:S(2)}, u32[]{:S(2)}) collective-permute-start(f32[128,512]{1,0:T(8,128)} %get-tuple-element.48), channel_id=1, source_target_pairs={{0,3},{1,2},{2,1},{3,0},{4,7},{5,6},{6,5},{7,4},{8,11},{9,10},{10,... | collective-permute-start | bytes 786440 | tf_op jit(solution)/shard_map/ppermute | solution.py:178
  65.1 19.2 %collective-permute-start.15 = (f32[128,512]{1,0:T(8,128)}, f32[128,512]{1,0:T(8,128)}, u32[]{:S(2)}, u32[]{:S(2)}) collective-permute-start(f32[128,512]{1,0:T(8,128)} %get-tuple-element.49), channel_id=1, source_target_pairs={{0,2},{1,3},{2,0},{3,1},{4,6},{5,7},{6,4},{7,5},{8,10},{9,11},{10,... | collective-permute-start | bytes 786440 | tf_op jit(solution)/shard_map/ppermute | solution.py:178
  67.5 8.3 %collective-permute-start.17 = (f32[128,512]{1,0:T(8,128)S(1)}, f32[128,512]{1,0:T(8,128)S(1)}, u32[]{:S(2)}, u32[]{:S(2)}) collective-permute-start(f32[128,512]{1,0:T(8,128)S(1)} %add.91), channel_id=1, source_target_pairs={{8,0},{9,1},{10,2},{11,3},{12,4},{13,5},{14,6},{15,7}} | collective-permute-start | bytes 786440 | tf_op jit(solution)/shard_map/ppermute | solution.py:218
  79.2 9.5 %collective-permute-start.24 = (f32[128,512]{1,0:T(8,128)S(1)}, f32[128,512]{1,0:T(8,128)S(1)}, u32[]{:S(2)}, u32[]{:S(2)}) collective-permute-start(f32[128,512]{1,0:T(8,128)S(1)} %get-tuple-element.39), channel_id=1, source_target_pairs={{0,1},{1,0},{2,3},{3,2},{4,5},{5,4},{6,7},{7,6},{8,9},{9,8},{10,11... | collective-permute-start | bytes 786440 | tf_op jit(solution)/shard_map/ppermute | solution.py:178
  81.8 7.5 %collective-permute-start.26 = (f32[128,512]{1,0:T(8,128)S(1)}, f32[128,512]{1,0:T(8,128)S(1)}, u32[]{:S(2)}, u32[]{:S(2)}) collective-permute-start(f32[128,512]{1,0:T(8,128)S(1)} %get-tuple-element.41), channel_id=1, source_target_pairs={{0,3},{1,2},{2,1},{3,0},{4,7},{5,6},{6,5},{7,4},{8,11},{9,10},{10,... | collective-permute-start | bytes 786440 | tf_op jit(solution)/shard_map/ppermute | solution.py:178
  86.5 6.4 %collective-permute-start.25 = (f32[128,512]{1,0:T(8,128)S(1)}, f32[128,512]{1,0:T(8,128)S(1)}, u32[]{:S(2)}, u32[]{:S(2)}) collective-permute-start(f32[128,512]{1,0:T(8,128)S(1)} %get-tuple-element.40), channel_id=1, source_target_pairs={{0,2},{1,3},{2,0},{3,1},{4,6},{5,7},{6,4},{7,5},{8,10},{9,11},{10,... | collective-permute-start | bytes 786440 | tf_op jit(solution)/shard_map/ppermute | solution.py:178
  93.0 1.6 %collective-permute-start.27 = (f32[128,512]{1,0:T(8,128)S(1)}, f32[128,512]{1,0:T(8,128)S(1)}, u32[]{:S(2)}, u32[]{:S(2)}) collective-permute-start(f32[128,512]{1,0:T(8,128)S(1)} %add_add_fusion.mine), channel_id=1, source_target_pairs={{0,4},{4,0},{1,5},{5,1},{2,6},{6,2},{3,7},{7,3},{8,12},{12,8},{9,1... | collective-permute-start | bytes 786440 | tf_op jit(solution)/shard_map/ppermute | solution.py:240
  93.2 6.2 %collective-permute-start.19 = (f32[4]{0:T(128)S(1)}, f32[4]{0:T(128)S(1)}, u32[]{:S(2)}, u32[]{:S(2)}) collective-permute-start(f32[4]{0:T(128)S(1)} %add_reduce_fusion), channel_id=1, source_target_pairs={{0,4},{4,0},{1,5},{5,1},{2,6},{6,2},{3,7},{7,3},{8,12},{12,8},{9,1... | collective-permute-start | bytes 56 | tf_op jit(solution)/shard_map/ppermute | solution.py:259
  95.1 26.2 %collective-permute-start.30 = (f32[128,512]{1,0:T(8,128)S(1)}, f32[128,512]{1,0:T(8,128)S(1)}, u32[]{:S(2)}, u32[]{:S(2)}) collective-permute-start(f32[128,512]{1,0:T(8,128)S(1)} %shard_map.86.refs_4_), channel_id=1, source_target_pairs={{0,3},{1,2},{2,1},{3,0},{4,7},{5,6},{6,5},{7,4},{8,11},{9,10},{10,... | collective-permute-start | bytes 786440 | tf_op jit(solution)/shard_map/ppermute | solution.py:178
  96.7 24.6 %collective-permute-start.29 = (f32[128,512]{1,0:T(8,128)S(1)}, f32[128,512]{1,0:T(8,128)S(1)}, u32[]{:S(2)}, u32[]{:S(2)}) collective-permute-start(f32[128,512]{1,0:T(8,128)S(1)} %shard_map.86.refs_4_), channel_id=1, source_target_pairs={{0,2},{1,3},{2,0},{3,1},{4,6},{5,7},{6,4},{7,5},{8,10},{9,11},{10,... | collective-permute-start | bytes 786440 | tf_op jit(solution)/shard_map/ppermute | solution.py:178
  97.2 24.1 %collective-permute-start.28 = (f32[128,512]{1,0:T(8,128)S(1)}, f32[128,512]{1,0:T(8,128)S(1)}, u32[]{:S(2)}, u32[]{:S(2)}) collective-permute-start(f32[128,512]{1,0:T(8,128)S(1)} %shard_map.86.refs_4_), channel_id=1, source_target_pairs={{0,1},{1,0},{2,3},{3,2},{4,5},{5,4},{6,7},{7,6},{8,9},{9,8},{10,11... | collective-permute-start | bytes 786440 | tf_op jit(solution)/shard_map/ppermute | solution.py:178
  99.4 9.8 %collective-permute-start.20 = (f32[4]{0:T(128)S(1)}, f32[4]{0:T(128)S(1)}, u32[]{:S(2)}, u32[]{:S(2)}) collective-permute-start(f32[4]{0:T(128)S(1)} %add.94), channel_id=1, source_target_pairs={{0,1},{1,0},{2,3},{3,2},{4,5},{5,4},{6,7},{7,6},{8,9},{9,8},{10,11... | collective-permute-start | bytes 56 | tf_op jit(solution)/shard_map/ppermute | solution.py:259
  109.3 3.5 %collective-permute-start.21 = (f32[4]{0:T(128)S(1)}, f32[4]{0:T(128)S(1)}, u32[]{:S(2)}, u32[]{:S(2)}) collective-permute-start(f32[4]{0:T(128)S(1)} %add.95), channel_id=1, source_target_pairs={{0,2},{1,3},{2,0},{3,1},{4,6},{5,7},{6,4},{7,5},{8,10},{9,11},{10,... | collective-permute-start | bytes 56 | tf_op jit(solution)/shard_map/ppermute | solution.py:259
  112.8 3.5 %collective-permute-start.22 = (f32[4]{0:T(128)S(1)}, f32[4]{0:T(128)S(1)}, u32[]{:S(2)}, u32[]{:S(2)}) collective-permute-start(f32[4]{0:T(128)S(1)} %add.96), channel_id=1, source_target_pairs={{0,8},{8,0},{16,24},{24,16},{1,9},{9,1},{17,25},{25,17},{2,10},{10... | collective-permute-start | bytes 56 | tf_op jit(solution)/shard_map/ppermute | solution.py:259
  116.3 4.4 %collective-permute-start.23 = (f32[4]{0:T(128)S(1)}, f32[4]{0:T(128)S(1)}, u32[]{:S(2)}, u32[]{:S(2)}) collective-permute-start(f32[4]{0:T(128)S(1)} %add.97), channel_id=1, source_target_pairs={{0,16},{8,24},{16,0},{24,8},{1,17},{9,25},{17,1},{25,9},{2,18},{10... | collective-permute-start | bytes 56 | tf_op jit(solution)/shard_map/ppermute | solution.py:259
  (25 other events, 178.9 us)

commit v2 on v0

v2 whole, which is shorter than its diff:
```python
import functools

import jax
import jax.numpy as jnp
from jax import lax
from jax.experimental import pallas as pl
from jax.experimental.pallas import tpu as pltpu
from jax.sharding import PartitionSpec as P

LEVELS = 4
BLOCK = 128
LOSS_ROWS = 8
GELU_C = 0.7978845608028654
GELU_A = 0.044715

FIRST, LAT, WID, TOK, BOUND = 0, 1, 2, 3, 4

VMEM = pl.BlockSpec(memory_space=pltpu.VMEM)
SMEM = pl.BlockSpec(memory_space=pltpu.SMEM)
HBM = pl.BlockSpec(memory_space=pltpu.HBM)
ANY = pl.BlockSpec(memory_space=pl.ANY)


def f32(*shape):
    return jax.ShapeDtypeStruct(shape, jnp.float32)


def bf16(*shape):
    return jax.ShapeDtypeStruct(shape, jnp.bfloat16)


def call(kernel, outs, scalars, arrays, after=(), specs=None, out_specs=None, scratch=(), flops=0):
    skip = slice(1 + len(arrays), 1 + len(arrays) + len(after))

    def run(*refs):
        kernel(*refs[: skip.start], *refs[skip.stop :])

    return pl.pallas_call(
        run,
        out_shape=outs,
        in_specs=[SMEM] + list(specs or [VMEM] * len(arrays)) + [ANY] * len(after),
        out_specs=out_specs or [VMEM] * len(outs),
        scratch_shapes=list(scratch),
        compiler_params=pltpu.CompilerParams(vmem_limit_bytes=12 * 1024 * 1024),
        cost_estimate=pl.CostEstimate(flops=flops, bytes_accessed=1 << 20, transcendentals=0),
    )(scalars, *arrays, *after)


def total_of(terms):
    return functools.reduce(jnp.add, terms)


def pre_kernel(scal, resid, dictionary, partial_out, dict_out, resid_v, dict_v, sems):
    pieces, _, width = dict_v.shape
    here = pl.ds(pl.multiple_of(scal[TOK] * width, width), width)
    copies = [pltpu.make_async_copy(resid, resid_v, sems.at[pieces])]
    for i in range(pieces):
        cols = pl.ds(i * width, width)
        copies.append(pltpu.make_async_copy(dictionary.at[:, cols], dict_v.at[i], sems.at[i]))
    copies.append(pltpu.make_async_copy(dictionary.at[:, here], dict_out, sems.at[pieces + 1]))
    for copy in copies:
        copy.start()
    copies[0].wait()
    total = None
    for i in range(pieces):
        copies[1 + i].wait()
        term = lax.dot_general(
            resid_v[:, i * width : (i + 1) * width],
            dict_v[i],
            (((1,), (1,)), ((), ())),
            preferred_element_type=jnp.float32,
        )
        total = term if total is None else total + term
    partial_out[...] = total
    copies[-1].wait()


def pieces_kernel(offsets, scal, resid, bias, bias_out, *outs):
    width = outs[0].shape[1]

    def cols(t):
        return pl.ds(pl.multiple_of(t * width, width), width)

    bias_out[...] = bias[:, cols(scal[TOK])]
    for (first, second), out in zip(offsets, outs):
        away = jnp.where(scal[WID] == 0, first, second)
        out[...] = resid[:, cols(scal[TOK] ^ away)].astype(jnp.float32)


def block_mask(active, first, lats):
    ids = first + lax.broadcasted_iota(jnp.int32, (1, lats), 1) // BLOCK
    hit = None
    for q in range(active.shape[1]):
        same = active[:, q : q + 1] == ids
        hit = same if hit is None else hit | same
    return hit


def activate_kernel(scal, mine, other, bias, active, pre_out, act_out):
    pre = mine[...] + other[...] + bias[...]
    pre_out[...] = pre
    inner = GELU_C * (pre + GELU_A * (pre * pre * pre))
    gelu = 0.5 * pre * (1.0 + jnp.tanh(inner))
    act_out[...] = jnp.where(block_mask(active[...], scal[FIRST], pre.shape[1]), gelu, 0.0)


def g_pre_kernel(scal, pre_ref, mine, other, active, loss, loss_other, out):
    pre = pre_ref[...]
    inner = GELU_C * (pre + GELU_A * (pre * pre * pre))
    slope = GELU_C * (1.0 + 3.0 * GELU_A * (pre * pre))
    bend = jnp.tanh(inner)
    deriv = 0.5 * (1.0 + bend) + 0.5 * pre * (1.0 - bend * bend) * slope
    hit = block_mask(active[...], scal[FIRST], pre.shape[1])
    rows = pre.shape[0]
    out[:rows, :] = jnp.where(hit, deriv * (mine[...] + other[...]), 0.0)
    out[rows:, :] = jnp.zeros_like(out[rows:, :])
    out[rows:, :BLOCK] = loss[...] + loss_other[...]


def last_blocks(scal, count):
    return [jnp.minimum(scal[BOUND + m] - 1 - scal[FIRST], count - 1) for m in range(LEVELS)]


def ending(lasts, i):
    return total_of([(last == i).astype(jnp.float32) for last in lasts])


def running_parts(act, dict_ref):
    sums = []
    for i in range(dict_ref.shape[0] // BLOCK):
        span = slice(i * BLOCK, (i + 1) * BLOCK)
        part = jnp.dot(
            act[:, span].astype(jnp.bfloat16), dict_ref[span, :], preferred_element_type=jnp.float32
        )
        sums.append(sums[-1] + part if sums else part)
    return sums


def project_kernel(spans, scal, act, dictionary, up_out, *down_outs):
    sums = running_parts(act[...], dictionary)
    lasts = last_blocks(scal, len(sums))
    up_out[...] = sums[-1]
    down = total_of([ending(lasts, i) * s for i, s in enumerate(sums)])
    for span, out in zip(spans, down_outs):
        out[...] = down[span, :]


def message_kernel(up, n_lat, places, has_got, scal, *refs):
    out = refs[-1]
    index = scal[LAT] if up else n_lat - 1 - scal[LAT]
    for place, piece in zip(places, refs[has_got:-1]):

        @pl.when(index == place)
        def _():
            rows = piece.shape[0]
            out[:rows, :] = piece[...] + refs[0][:rows, :] if place else piece[...]


def square_sums(scal, shifted, count):
    squares = []
    for v in shifted:
        lanes = jnp.sum(v * v, axis=0, keepdims=True)
        squares.append(total_of([lanes[:, i : i + BLOCK] for i in range(0, lanes.shape[1], BLOCK)]))
    rows = []
    for m in range(LEVELS):
        last = scal[BOUND + m] - 1 - scal[FIRST]
        rows.append(total_of([jnp.where(last == i, s, 0.0) for i, s in enumerate(squares)]))
    return jnp.concatenate(rows + [jnp.zeros((LOSS_ROWS - LEVELS, BLOCK), jnp.float32)], axis=0)


def add_chosen(index, choices, refs, span, target):
    for place, ref in zip(choices, refs):
        chosen = index == place if len(choices) < 4 else index >= 1

        @pl.when(chosen)
        def _():
            target[...] += ref[span, :]


def loss_kernel(spans, places, scal, bias, dictionary, *refs):
    refs = list(refs)
    out = refs.pop(-2)
    base = refs.pop()
    total = None
    for span in spans:
        act, resid = refs.pop(0), refs.pop(0)
        earlier = [refs.pop(0) for _ in range(len(places) if len(places) < 4 else 1)]
        rows = span.stop - span.start
        view = base.at[:rows, :]
        view[...] = bias[...] - resid[span, :]
        add_chosen(scal[LAT], places, earlier, span, view)
        sums = running_parts(act[span, :], dictionary)
        shifted = [view[...] + s for s in sums]
        term = square_sums(scal, shifted, len(sums))
        total = term if total is None else total + term
    out[...] = total_of([total] + [ref[...] for ref in refs])


def error_kernel(
    n_lat, up_places, down_places, span, squared, scal, act, dictionary, resid, bias, *refs
):
    refs = list(refs)
    earlier = [refs.pop(0) for _ in range(len(up_places) if len(up_places) < 4 else 1)]
    later = [refs.pop(0) for _ in range(len(down_places) if len(down_places) < 4 else 1)]
    base, tail = refs[-2:]
    err_out, gact_out = refs[:2]
    rows = span.stop - span.start
    base[...] = bias[...] - resid[span, :]
    add_chosen(scal[LAT], up_places, earlier, span, base)
    tail[...] = jnp.zeros_like(tail)
    add_chosen(n_lat - 1 - scal[LAT], down_places, later, slice(0, rows), tail)
    sums = running_parts(act[span, :], dictionary)
    count = len(sums)
    shifted = [base[...] + s for s in sums]
    if squared:
        refs[2][...] = square_sums(scal, shifted, count)
    lasts = last_blocks(scal, count)
    err = tail[...]
    for i in reversed(range(count)):
        err = err + ending(lasts, i) * shifted[i]
        rounded = err.astype(jnp.bfloat16)
        err_out[i] = rounded
        cols = slice(i * BLOCK, (i + 1) * BLOCK)
        gact_out[:, cols] = lax.dot_general(
            rounded,
            dictionary[cols, :],
            (((1,), (1,)), ((), ())),
            preferred_element_type=jnp.float32,
        )


def sum_kernel(cut, scal, head, tail, *rest):
    others, out = rest[:-1], rest[-1]
    out[:cut, :] = head[...] + total_of([o[:cut, :] for o in others])
    out[cut:, :] = tail[...] + total_of([o[cut:, :] for o in others])


def add_kernel(scal, one, two, out):
    out[...] = one[...] + two[...]


def decode_kernel(spans, has_base, scal, *refs):
    n = len(spans)
    errs, acts, out = refs[:n], refs[n : 2 * n], refs[-1]
    for i in range(errs[0].shape[0]):
        cols = slice(i * BLOCK, (i + 1) * BLOCK)
        err = jnp.concatenate([e[i] for e in errs], axis=0)
        act = jnp.concatenate(
            [a[s, cols].astype(jnp.bfloat16) for a, s in zip(acts, spans)], axis=0
        )
        term = lax.dot_general(err, act, (((0,), (0,)), ((), ())), preferred_element_type=jnp.float32)
        out[:, cols] = refs[2 * n][:, cols] + term if has_base else term


def encode_kernel(scale, scal, *refs):
    n = (len(refs) - 3) // 2
    resids, grads, base, out, loss_out = refs[:n], refs[n : 2 * n], refs[-3], refs[-2], refs[-1]
    rows = resids[0].shape[0]
    resid = jnp.concatenate([r[...].astype(jnp.bfloat16) for r in resids], axis=0)
    grad = jnp.concatenate([g[:rows, :].astype(jnp.bfloat16) for g in grads], axis=0)
    total = base[...] + lax.dot_general(
        resid, grad, (((0,), (0,)), ((), ())), preferred_element_type=jnp.float32
    )
    out[...] = total.astype(jnp.bfloat16)
    lanes = total_of([g[rows:, :BLOCK] for g in grads])
    for m in range(LEVELS):
        loss_out[m] = jnp.sum(lanes[m : m + 1, :]) * scale


def pick(index, choices):
    values = sorted(choices)
    result = choices[values[0]]
    for value in values[1:]:
        result = jnp.where(index == value, choices[value], result)
    return result


def body(resid, dictionary, enc_bias, dec_bias, active_blocks, level_bounds):
    rows, half = resid.shape
    lats = dictionary.shape[0]
    n_lat, n_wid, n_tok = lax.axis_size("lat"), lax.axis_size("wid"), lax.axis_size("tok")
    lat, wid, tok = lax.axis_index("lat"), lax.axis_index("wid"), lax.axis_index("tok")
    width = half // n_tok
    count = lats // BLOCK
    cut = rows // 2
    places = jnp.stack([lat * count, lat, wid, tok]).astype(jnp.int32)
    scal = jnp.concatenate([places, level_bounds])
    work = 2 * rows * lats * width

    def offset(w, q):
        return (0, 2, 1, 3)[q] if w and n_tok == 4 else q

    def across(array, q):
        pairs = [
            (w * n_tok + t, w * n_tok + (t ^ offset(w, q)))
            for w in range(n_wid)
            for t in range(n_tok)
        ]
        return lax.ppermute(array, ("wid", "tok"), pairs)

    def swap(array):
        return lax.ppermute(array, "wid", [(w, w ^ 1) for w in range(n_wid)])

    def gather(array):
        if n_tok != 4:
            return [array] + [across(array, q) for q in range(1, n_tok)]
        near = across(array, 1)
        far = across(array, 3)
        return [array, near, swap(near), far]

    partial, dict_here = call(
        pre_kernel,
        [f32(rows, lats), bf16(lats, width)],
        scal,
        (resid, dictionary),
        specs=[HBM, HBM],
        scratch=[
            pltpu.VMEM((rows, half), jnp.bfloat16),
            pltpu.VMEM((n_tok, lats, width), jnp.bfloat16),
            pltpu.SemaphoreType.DMA((n_tok + 2,)),
        ],
    )
    partial_other = swap(partial)
    bias_here, *pieces = call(
        functools.partial(pieces_kernel, [(offset(0, q), offset(1, q)) for q in range(n_tok)]),
        [f32(1, width)] + [f32(rows, width)] * n_tok,
        scal,
        (resid, dec_bias.reshape(1, half)),
        after=(partial,),
    )
    pre, act = call(
        activate_kernel,
        [f32(rows, lats)] * 2,
        scal,
        (partial, partial_other, enc_bias.reshape(1, lats), active_blocks),
        after=(bias_here,),
    )
    acts = gather(act)
    resids = [piece if q == 0 else across(piece, q) for q, piece in enumerate(pieces)]

    order = [0, 1, 3, 2] if n_tok == 4 else list(range(n_tok))
    chunks = [(0, slice(0, cut))] + [(q, slice(0, rows)) for q in order[1:]] + [(0, slice(cut, rows))]
    n_chunks = len(chunks)
    ups, downs = [], []
    for q in order:
        spans = [span for c, span in chunks if c == q]
        up, *down = call(
            functools.partial(project_kernel, spans),
            [f32(rows, width)] + [f32(s.stop - s.start, width) for s in spans],
            scal,
            (acts[q], dict_here),
            flops=work,
        )
        ups.append(up)
        downs.append(down)
    downs = [downs[0][0]] + [d[0] for d in downs[1:]] + [downs[0][1]]

    def send(pieces, got, step, up, after):
        at = [p for p in range(n_lat - 1) if 0 <= step - p < len(pieces)]
        sent = pieces[0]
        if step:
            options = [pieces[step - p] for p in at]
            sent = call(
                functools.partial(message_kernel, up, n_lat, at, 1),
                [f32(max(o.shape[0] for o in options), width)],
                scal,
                (got[-1], *options),
                after=after,
            )[0]
        if up:
            pairs = [(p, p + 1) for p in at]
        else:
            pairs = [(n_lat - 1 - p, n_lat - 2 - p) for p in at]
        got.append(lax.ppermute(sent, "lat", pairs))
        return sent

    def choose(index, got, c):
        choices = {p: got[c + p - 1] for p in range(1, n_lat)}
        if n_lat <= 4:
            return list(choices), list(choices.values())
        size = min(a.shape[0] for a in choices.values())
        one = pick(index, {p: a[:size] for p, a in choices.items()})
        return [1, 2, 3, 4], [one]

    def errors(c, after, squared):
        q, span = chunks[c]
        size = span.stop - span.start
        up_places, earlier = choose(lat, got_up, order.index(q))
        down_places, later = choose(n_lat - 1 - lat, got_down, c)
        return call(
            functools.partial(error_kernel, n_lat, up_places, down_places, span, squared),
            [bf16(count, size, width), f32(size, lats)]
            + ([f32(LOSS_ROWS, BLOCK)] if squared else []),
            scal,
            (acts[q], dict_here, resids[q], bias_here, *earlier, *later),
            after=after,
            scratch=[pltpu.VMEM((size, width), jnp.float32)] * 2,
            flops=2 * work,
        )

    got_up, got_down = [], []
    errs, gacts, squares = [], [], []
    up_steps, down_steps = len(ups) + n_lat - 2, n_chunks + n_lat - 2
    ahead = []
    for step in range(down_steps + 1):
        sent = None
        if step < up_steps:
            sent = send(ups, got_up, step, True, ahead)
            ahead = []
        if step < down_steps:
            sent = send(downs, got_down, step, False, ahead)
        c = step - (n_lat - 1)
        ahead = []
        if step == up_steps:
            open_spans = [(q, span) for q, span in (chunks[-2], chunks[-1])]
            items = []
            for q, span in open_spans:
                up_places, earlier = choose(lat, got_up, order.index(q))
                items += [acts[q], resids[q], *earlier]
            loss = call(
                functools.partial(loss_kernel, [s for _, s in open_spans], up_places),
                [f32(LOSS_ROWS, BLOCK)],
                scal,
                (bias_here, dict_here, *items, *squares),
                after=(sent,) if sent is not None else (),
                scratch=[pltpu.VMEM((rows, width), jnp.float32)],
                flops=work,
            )[0]
        if c >= 0:
            q, span = chunks[c]
            err, gact, *square = errors(
                c, (sent,) if sent is not None else (), c < n_chunks - 2
            )
            errs.append(err)
            gacts.append(gact if q == 0 else across(gact, q))
            squares += square
            ahead = [err]

    gap = 1
    while gap < n_lat:
        other = lax.ppermute(loss, "lat", [(p, p ^ gap) for p in range(n_lat)])
        loss = call(add_kernel, [f32(LOSS_ROWS, BLOCK)], scal, (loss, other))[0]
        gap *= 2

    mine = call(
        functools.partial(sum_kernel, cut),
        [f32(rows, lats)],
        scal,
        (gacts[0], gacts[-1], *gacts[1:-1]),
    )[0]
    g_pre = call(
        g_pre_kernel,
        [f32(rows + LOSS_ROWS, lats)],
        scal,
        (pre, mine, swap(mine), active_blocks, loss, swap(loss)),
    )[0]
    g_pres = gather(g_pre)

    def decode(items, base, after):
        return call(
            functools.partial(decode_kernel, [chunks[c][1] for c in items], len(base)),
            [f32(width, lats)],
            scal,
            (*[errs[c] for c in items], *[acts[chunks[c][0]] for c in items], *base),
            after=after,
            flops=n_tok * work,
        )[0]

    decoded = decode(range(n_chunks), (), ())
    grad, losses = call(
        functools.partial(encode_kernel, 1.0 / (rows * n_tok * half * n_wid)),
        [bf16(width, lats), f32(LEVELS)],
        scal,
        (*resids, *g_pres, decoded),
        out_specs=[VMEM, SMEM],
        flops=n_tok * work,
    )
    return (losses, grad)


def solution(mesh):
    return jax.shard_map(
        body,
        mesh=mesh,
        in_specs=(P("tok", "wid"), P("lat", "wid"), P("lat"), P("wid"), P("tok", None), P()),
        out_specs=(P(), P(("wid", "tok"), "lat")),
        check_vma=False,
    )
```

time: 377 us -> 113 us (0.30)
  waiting for transfers between devices: 278 us -> 32.8 us
  starting transfers between devices: 0.2 us -> 49.4 us
  blocking collectives: 40.7 us -> 0 us
  Pallas kernels: 0 us -> 25.9 us
  matrix products: 18.4 us -> 0 us
  between operations: 19.1 us -> 1.14 us
  other arithmetic: 10.4 us -> 0 us
  local copies, waits for them, and re-layouts: 10.1 us -> 3.49 us
    psum x3 -> x0, waiting for transfers between devices: 185 us -> none  [the longest x1 157 us: broadcast(): return lax.psum(jnp.where(mine, array, jnp.zeros_like(array)), axis)]
    all_gather x1 -> x0, waiting for transfers between devices: 81.9 us -> none  [entering(): gathered = lax.all_gather(part, axis)]
    ppermute x0 -> x30, starting transfers between devices: none -> 49.4 us  [the longest x13 26.3 us: send(): got.append(lax.ppermute(sent, 'lat', pairs))]
    psum x1 -> x0, blocking collectives: 40.7 us -> none  [body(): total_sq = lax.psum(jnp.stack(squares), ('lat', 'wid', 'tok'))]
    ppermute x0 -> x30, waiting for transfers between devices: none -> 32.8 us  [the longest x13 17.9 us: send(): got.append(lax.ppermute(sent, 'lat', pairs))]
    pallas_call x0 -> x30, Pallas kernels: none -> 25.9 us  [call(): pl.pallas_call(run, out_shape=outs, in_specs=[SMEM] + list(specs or [VMEM...]
    dot_general x5 -> x0, matrix products: 18.4 us -> none  [the longest x1 5.67 us: body(): jnp.einsum('ktd,tkc->dkc', err_half, act, preferred_element_type=jnp.floa...]
    reduce_scatter x1 -> x0, waiting for transfers between devices: 10.9 us -> none  [body(): lax.psum_scatter(decode_term.reshape(half_width // lax.axis_size('tok') *...]
  transfers between devices with their start and end apart: 5 -> 30, of which waited for: 5 -> 12; matrix products, arithmetic and copies ran while one was open for 2% -> 0% of each run, Pallas kernels for 0% -> 17%
where the time goes in v2:
time: 113 us
  starting transfers between devices  49.4 us (44%)
  waiting for transfers between devices  32.8 us (29%)
  Pallas kernels  25.9 us (23%)
  local copies, waits for them, and re-layouts  3.49 us (3%)
  between operations  1.14 us (1%)
    ppermute x13, starting transfers between devices, send(): got.append(lax.ppermute(sent, 'lat', pairs))  26.3 us
    pallas_call x30, Pallas kernels, call(): pl.pallas_call(run, out_shape=outs, in_specs=[SMEM] + list(specs or [VMEM...  25.9 us
    ppermute x10, starting transfers between devices, across(): return lax.ppermute(array, ('wid', 'tok'), pairs)  18.8 us
    ppermute x13, waiting for transfers between devices, send(): got.append(lax.ppermute(sent, 'lat', pairs))  17.9 us
    ppermute x10, waiting for transfers between devices, across(): return lax.ppermute(array, ('wid', 'tok'), pairs)  8.69 us
    ppermute x2, waiting for transfers between devices, body(): other = lax.ppermute(loss, 'lat', [(p, p ^ gap) for p in range(n_lat)])  4.65 us
    ppermute x2, starting transfers between devices, body(): other = lax.ppermute(loss, 'lat', [(p, p ^ gap) for p in range(n_lat)])  3.59 us
    unnamed x13, local copies, waits for them, and re-layouts  2.75 us
  transfers between devices with their start and end apart: 30, of which 12 were waited for; matrix products, arithmetic and copies ran while one was open for 0% of the time, Pallas kernels for 17%

profile of v2, /device:TPU:0, one launch (start us, length us, event | category | flops | bytes accessed | tf_op | source)
XLA Modules:
  0.0 112.7 jit_solution(13614603732213611214)
XLA Ops:
  1.4 1.6 %copy-done = bf16[512,2048]{1,0:T(8,128)(2,1)S(1)} copy-done((bf16[512,2048]{1,0:T(8,128)(2,1)S(1)}, bf16[512,2048]{1,0:T(8,128)(2,1)}, u32[]{:S(2)}) %copy-start) | copy-done | bytes 2097176
  4.0 1.9 %shard_map.77 = (f32[128,512]{1,0:T(8,128)S(1)}, bf16[512,512]{1,0:T(8,128)(2,1)S(1)}) custom-call(s32[8]{0:T(128)S(1)} %concatenate.3.refs_0_, bf16[128,2048]{1,0:T(8,128)(2,1)S(1)} %copy-done.1, bf16[512,2048]{1,0:T(8,128)(2,1)S(1)} %copy-done), custom_call_target="tpu_custom_call" | custom-call | bytes 1048576 | tf_op jit(solution)/shard_map/pallas_call | solution.py:38
  8.6 2.9 %collective-permute-start.5 = (f32[128,512]{1,0:T(8,128)S(1)}, f32[128,512]{1,0:T(8,128)S(1)}, u32[]{:S(2)}, u32[]{:S(2)}) collective-permute-start(f32[128,512]{1,0:T(8,128)S(1)} %get-tuple-element.42.refs_1_.refs_8_.refs_6_.refs_10_), channel_id=1, source_target_pairs={{0,1},{1,0},{2,3},{3,2},{4,6},{5,7},{6,4},{7,5},{8,9},{9,8},{10,11... | collective-permute-start | bytes 786440 | tf_op jit(solution)/shard_map/ppermute | solution.py:299
  12.4 3.5 %collective-permute-start.4 = (f32[128,512]{1,0:T(8,128)S(1)}, f32[128,512]{1,0:T(8,128)S(1)}, u32[]{:S(2)}, u32[]{:S(2)}) collective-permute-start(f32[128,512]{1,0:T(8,128)S(1)} %get-tuple-element.44.refs_3_.refs_4_), channel_id=1, source_target_pairs={{0,8},{1,9},{2,10},{3,11},{4,12},{5,13},{6,14},{7,15}} | collective-permute-start | bytes 786440 | tf_op jit(solution)/shard_map/ppermute | solution.py:374
  16.5 1.6 %collective-permute-start.7 = (f32[128,512]{1,0:T(8,128)S(1)}, f32[128,512]{1,0:T(8,128)S(1)}, u32[]{:S(2)}, u32[]{:S(2)}) collective-permute-start(f32[128,512]{1,0:T(8,128)S(1)} %get-tuple-element.42.refs_1_.refs_8_.refs_6_.refs_10_), channel_id=1, source_target_pairs={{0,3},{1,2},{2,1},{3,0},{4,7},{5,6},{6,5},{7,4},{8,11},{9,10},{10,... | collective-permute-start | bytes 786440 | tf_op jit(solution)/shard_map/ppermute | solution.py:299
  22.0 4.4 %collective-permute-start.6 = (f32[128,512]{1,0:T(8,128)S(1)}, f32[128,512]{1,0:T(8,128)S(1)}, u32[]{:S(2)}, u32[]{:S(2)}) collective-permute-start(f32[128,512]{1,0:T(8,128)S(1)} %shard_map.82), channel_id=1, source_target_pairs={{0,8},{8,16},{1,9},{9,17},{2,10},{10,18},{3,11},{11,19},{4,12},{12... | collective-permute-start | bytes 786440 | tf_op jit(solution)/shard_map/ppermute | solution.py:374
  28.0 1.3 %collective-permute-start.11 = (f32[128,512]{1,0:T(8,128)S(1)}, f32[128,512]{1,0:T(8,128)S(1)}, u32[]{:S(2)}, u32[]{:S(2)}) collective-permute-start(f32[128,512]{1,0:T(8,128)S(1)} %shard_map.86), channel_id=1, source_target_pairs={{24,16},{16,8},{8,0},{25,17},{17,9},{9,1},{26,18},{18,10},{10,2},{... | collective-permute-start | bytes 786440 | tf_op jit(solution)/shard_map/ppermute | solution.py:374
  29.3 1.9 %collective-permute-done.6.refs_1_.refs_6_.refs_5_.refs_11_ = f32[128,512]{1,0:T(8,128)S(1)} collective-permute-done((f32[128,512]{1,0:T(8,128)S(1)}, f32[128,512]{1,0:T(8,128)S(1)}, u32[]{:S(2)}, u32[]{:S(2)}) %collective-permute-start.6) | collective-permute-done | bytes 262176 | tf_op jit(solution)/shard_map/ppermute | solution.py:374
  31.7 4.6 %collective-permute-start.8 = (f32[128,512]{1,0:T(8,128)S(1)}, f32[128,512]{1,0:T(8,128)S(1)}, u32[]{:S(2)}, u32[]{:S(2)}) collective-permute-start(f32[128,512]{1,0:T(8,128)S(1)} %shard_map.84), channel_id=1, source_target_pairs={{0,8},{8,16},{16,24},{1,9},{9,17},{17,25},{2,10},{10,18},{18,26},{... | collective-permute-start | bytes 786440 | tf_op jit(solution)/shard_map/ppermute | solution.py:374
  37.2 1.5 %collective-permute-done.11.refs_1_.refs_10_.refs_8_.refs_9_ = f32[128,512]{1,0:T(8,128)S(1)} collective-permute-done((f32[128,512]{1,0:T(8,128)S(1)}, f32[128,512]{1,0:T(8,128)S(1)}, u32[]{:S(2)}, u32[]{:S(2)}) %collective-permute-start.11) | collective-permute-done | bytes 262176 | tf_op jit(solution)/shard_map/ppermute | solution.py:374
  39.3 1.3 %collective-permute-start.13 = (f32[128,512]{1,0:T(8,128)S(1)}, f32[128,512]{1,0:T(8,128)S(1)}, u32[]{:S(2)}, u32[]{:S(2)}) collective-permute-start(f32[128,512]{1,0:T(8,128)S(1)} %shard_map.88.refs_11_), channel_id=1, source_target_pairs={{24,16},{16,8},{8,0},{25,17},{17,9},{9,1},{26,18},{18,10},{10,2},{... | collective-permute-start | bytes 786440 | tf_op jit(solution)/shard_map/ppermute | solution.py:374
  41.2 4.6 %collective-permute-start.16 = (f32[128,512]{1,0:T(8,128)S(1)}, f32[128,512]{1,0:T(8,128)S(1)}, u32[]{:S(2)}, u32[]{:S(2)}) collective-permute-start(f32[128,512]{1,0:T(8,128)S(1)} %shard_map.92), channel_id=1, source_target_pairs={{0,8},{8,16},{16,24},{1,9},{9,17},{17,25},{2,10},{10,18},{18,26},{... | collective-permute-start | bytes 786440 | tf_op jit(solution)/shard_map/ppermute | solution.py:374
  45.8 3.5 %collective-permute-start = (f32[128,512]{1,0:T(8,128)S(1)}, f32[128,512]{1,0:T(8,128)S(1)}, u32[]{:S(2)}, u32[]{:S(2)}) collective-permute-start(f32[128,512]{1,0:T(8,128)S(1)} %get-tuple-element.37), channel_id=1, source_target_pairs={{0,1},{1,0},{2,3},{3,2},{4,6},{5,7},{6,4},{7,5},{8,9},{9,8},{10,11... | collective-permute-start | bytes 786440 | tf_op jit(solution)/shard_map/ppermute | solution.py:299
  51.0 1.3 %collective-permute-start.14 = (f32[128,512]{1,0:T(8,128)S(1)}, f32[128,512]{1,0:T(8,128)S(1)}, u32[]{:S(2)}, u32[]{:S(2)}) collective-permute-start(f32[128,512]{1,0:T(8,128)S(1)} %shard_map.90.refs_11_), channel_id=1, source_target_pairs={{24,16},{16,8},{8,0},{25,17},{17,9},{9,1},{26,18},{18,10},{10,2},{... | collective-permute-start | bytes 786440 | tf_op jit(solution)/shard_map/ppermute | solution.py:374
  53.6 2.8 %collective-permute-start.2 = (f32[128,512]{1,0:T(8,128)S(1)}, f32[128,512]{1,0:T(8,128)S(1)}, u32[]{:S(2)}, u32[]{:S(2)}) collective-permute-start(f32[128,512]{1,0:T(8,128)S(1)} %get-tuple-element.39), channel_id=1, source_target_pairs={{0,3},{1,2},{2,1},{3,0},{4,7},{5,6},{6,5},{7,4},{8,11},{9,10},{10,... | collective-permute-start | bytes 786440 | tf_op jit(solution)/shard_map/ppermute | solution.py:299
  57.7 1.6 %collective-permute-done.14.refs_1_.refs_10_.refs_8_.refs_9_ = f32[128,512]{1,0:T(8,128)S(1)} collective-permute-done((f32[128,512]{1,0:T(8,128)S(1)}, f32[128,512]{1,0:T(8,128)S(1)}, u32[]{:S(2)}, u32[]{:S(2)}) %collective-permute-start.14) | collective-permute-done | bytes 262176 | tf_op jit(solution)/shard_map/ppermute | solution.py:374
  59.8 1.3 %collective-permute-start.15 = (f32[128,512]{1,0:T(8,128)S(1)}, f32[128,512]{1,0:T(8,128)S(1)}, u32[]{:S(2)}, u32[]{:S(2)}) collective-permute-start(f32[128,512]{1,0:T(8,128)S(1)} %shard_map.91.refs_11_), channel_id=1, source_target_pairs={{16,8},{8,0},{17,9},{9,1},{18,10},{10,2},{19,11},{11,3},{20,12},{1... | collective-permute-start | bytes 786440 | tf_op jit(solution)/shard_map/ppermute | solution.py:374
  62.4 1.4 %collective-permute-start.19 = (f32[128,512]{1,0:T(8,128)S(1)}, f32[128,512]{1,0:T(8,128)S(1)}, u32[]{:S(2)}, u32[]{:S(2)}) collective-permute-start(f32[128,512]{1,0:T(8,128)S(1)} %get-tuple-element.57), channel_id=1, source_target_pairs={{0,1},{1,0},{2,3},{3,2},{4,6},{5,7},{6,4},{7,5},{8,9},{9,8},{10,11... | collective-permute-start | bytes 786440 | tf_op jit(solution)/shard_map/ppermute | solution.py:299
  65.0 1.4 %collective-permute-start.20 = (f32[128,512]{1,0:T(8,128)S(1)}, f32[128,512]{1,0:T(8,128)S(1)}, u32[]{:S(2)}, u32[]{:S(2)}) collective-permute-start(f32[128,512]{1,0:T(8,128)S(1)} %get-tuple-element.58), channel_id=1, source_target_pairs={{0,3},{1,2},{2,1},{3,0},{4,7},{5,6},{6,5},{7,4},{8,11},{9,10},{10,... | collective-permute-start | bytes 786440 | tf_op jit(solution)/shard_map/ppermute | solution.py:299
  66.5 3.5 %collective-permute-done.15.refs_1_.refs_9_.refs_10_ = f32[128,512]{1,0:T(8,128)S(1)} collective-permute-done((f32[128,512]{1,0:T(8,128)S(1)}, f32[128,512]{1,0:T(8,128)S(1)}, u32[]{:S(2)}, u32[]{:S(2)}) %collective-permute-start.15) | collective-permute-done | bytes 262176 | tf_op jit(solution)/shard_map/ppermute | solution.py:374
  71.9 1.3 %collective-permute-start.18 = (f32[64,512]{1,0:T(8,128)S(1)}, f32[64,512]{1,0:T(8,128)S(1)}, u32[]{:S(2)}, u32[]{:S(2)}) collective-permute-start(f32[64,512]{1,0:T(8,128)S(1)} %shard_map.95.refs_11_.refs_16_), channel_id=1, source_target_pairs={{8,0},{9,1},{10,2},{11,3},{12,4},{13,5},{14,6},{15,7}} | collective-permute-start | bytes 393224 | tf_op jit(solution)/shard_map/ppermute | solution.py:374
  73.1 8.1 %collective-permute-done.18.refs_10_ = f32[64,512]{1,0:T(8,128)S(1)} collective-permute-done((f32[64,512]{1,0:T(8,128)S(1)}, f32[64,512]{1,0:T(8,128)S(1)}, u32[]{:S(2)}, u32[]{:S(2)}) %collective-permute-start.18) | collective-permute-done | bytes 131104 | tf_op jit(solution)/shard_map/ppermute | solution.py:374
  84.3 1.3 %collective-permute-start.24 = (f32[8,128]{1,0:T(8,128)S(1)}, f32[8,128]{1,0:T(8,128)S(1)}, u32[]{:S(2)}, u32[]{:S(2)}) collective-permute-start(f32[8,128]{1,0:T(8,128)S(1)} %shard_map.101.refs_1_), channel_id=1, source_target_pairs={{0,8},{8,0},{16,24},{24,16},{1,9},{9,1},{17,25},{25,17},{2,10},{10... | collective-permute-start | bytes 12296 | tf_op jit(solution)/shard_map/ppermute | solution.py:441
  85.6 2.4 %collective-permute-done.24.refs_2_ = f32[8,128]{1,0:T(8,128)S(1)} collective-permute-done((f32[8,128]{1,0:T(8,128)S(1)}, f32[8,128]{1,0:T(8,128)S(1)}, u32[]{:S(2)}, u32[]{:S(2)}) %collective-permute-start.24) | collective-permute-done | bytes 4128 | tf_op jit(solution)/shard_map/ppermute | solution.py:441
  88.5 2.3 %collective-permute-start.25 = (f32[8,128]{1,0:T(8,128)S(1)}, f32[8,128]{1,0:T(8,128)S(1)}, u32[]{:S(2)}, u32[]{:S(2)}) collective-permute-start(f32[8,128]{1,0:T(8,128)S(1)} %shard_map.102.refs_1_), channel_id=1, source_target_pairs={{0,16},{8,24},{16,0},{24,8},{1,17},{9,25},{17,1},{25,9},{2,18},{10... | collective-permute-start | bytes 12296 | tf_op jit(solution)/shard_map/ppermute | solution.py:441
  90.8 2.3 %collective-permute-done.25.refs_2_ = f32[8,128]{1,0:T(8,128)S(1)} collective-permute-done((f32[8,128]{1,0:T(8,128)S(1)}, f32[8,128]{1,0:T(8,128)S(1)}, u32[]{:S(2)}, u32[]{:S(2)}) %collective-permute-start.25) | collective-permute-done | bytes 4128 | tf_op jit(solution)/shard_map/ppermute | solution.py:441
  95.9 3.5 %collective-permute-start.27 = (f32[136,512]{1,0:T(8,128)S(1)}, f32[136,512]{1,0:T(8,128)S(1)}, u32[]{:S(2)}, u32[]{:S(2)}) collective-permute-start(f32[136,512]{1,0:T(8,128)S(1)} %shard_map.104.refs_5_), channel_id=1, source_target_pairs={{0,1},{1,0},{2,3},{3,2},{4,6},{5,7},{6,4},{7,5},{8,9},{9,8},{10,11... | collective-permute-start | bytes 835592 | tf_op jit(solution)/shard_map/ppermute | solution.py:299
  99.4 1.5 %collective-permute-start.29 = (f32[136,512]{1,0:T(8,128)S(1)}, f32[136,512]{1,0:T(8,128)S(1)}, u32[]{:S(2)}, u32[]{:S(2)}) collective-permute-start(f32[136,512]{1,0:T(8,128)S(1)} %shard_map.104.refs_5_), channel_id=1, source_target_pairs={{0,3},{1,2},{2,1},{3,0},{4,7},{5,6},{6,5},{7,4},{8,11},{9,10},{10,... | collective-permute-start | bytes 835592 | tf_op jit(solution)/shard_map/ppermute | solution.py:299
  100.9 4.9 %collective-permute-done.27.refs_6_ = f32[136,512]{1,0:T(8,128)S(1)} collective-permute-done((f32[136,512]{1,0:T(8,128)S(1)}, f32[136,512]{1,0:T(8,128)S(1)}, u32[]{:S(2)}, u32[]{:S(2)}) %collective-permute-start.27) | collective-permute-done | bytes 278560 | tf_op jit(solution)/shard_map/ppermute | solution.py:299
  105.8 1.3 %shard_map.105.refs_9_ = f32[512,512]{1,0:T(8,128)S(1)} custom-call(s32[8]{0:T(128)S(1)} %concatenate.3.refs_0_, bf16[4,64,512]{2,1,0:T(8,128)(2,1)S(1)} %get-tuple-element.54.refs_4_.refs_1_, bf16[4,128,512]{2,1,0:T(8,128)(2,1)S(1)} %get-tuple-element.59.refs_3_.refs_2_, bf16[4,128,512]{2,1,0:T(8,128)(2,1)S(1)} %get-tuple-element.55.refs_3_, ...), custom_call_target="tpu_custom_call" | custom-call | flops 268435456 | bytes 1048576 | tf_op jit(solution)/shard_map/pallas_call | solution.py:38
  107.1 3.8 %collective-permute-done.29.refs_8_ = f32[136,512]{1,0:T(8,128)S(1)} collective-permute-done((f32[136,512]{1,0:T(8,128)S(1)}, f32[136,512]{1,0:T(8,128)S(1)}, u32[]{:S(2)}, u32[]{:S(2)}) %collective-permute-start.29) | collective-permute-done | bytes 278560 | tf_op jit(solution)/shard_map/ppermute | solution.py:299
  110.9 1.8 %shard_map.106 = (bf16[512,512]{1,0:T(8,128)(2,1)}, f32[4]{0:T(128)}) custom-call(s32[8]{0:T(128)S(1)} %concatenate.3.refs_0_, f32[128,512]{1,0:T(8,128)S(1)} %get-tuple-element.36.refs_3_.refs_9_.refs_1_, f32[128,512]{1,0:T(8,128)S(1)} %collective-permute-done.refs_3_.refs_2_, f32[128,512]{1,0:T(8,128)S(1)} %collective-permute-done.1.refs_3_.refs_4_, ...), custom_call_target="tpu_custom_call" | custom-call | flops 268435456 | bytes 1048576 | tf_op jit(solution)/shard_map/pallas_call | solution.py:38
  (72 shorter events, 29.3 us)
Async XLA Ops:
  0.6 5.9 %copy-start.3 = (f32[2048]{0:T(1024)S(1)}, f32[2048]{0:T(1024)}, u32[]{:S(2)}) copy-start(f32[2048]{0:T(1024)} %param.9) | copy-start | bytes 24580
  0.7 7.0 %copy-start.4 = (f32[512]{0:T(512)S(1)}, f32[512]{0:T(512)}, u32[]{:S(2)}) copy-start(f32[512]{0:T(512)} %param.8) | copy-start | bytes 6148
  6.0 1.7 %collective-permute-start.3 = (f32[128,512]{1,0:T(8,128)S(1)}, f32[128,512]{1,0:T(8,128)S(1)}, u32[]{:S(2)}, u32[]{:S(2)}) collective-permute-start(f32[128,512]{1,0:T(8,128)S(1)} %get-tuple-element.35.refs_3_.refs_1_), channel_id=1, source_target_pairs={{0,4},{4,0},{1,5},{5,1},{2,6},{6,2},{3,7},{7,3},{8,12},{12,8},{9,1... | collective-permute-start | bytes 786440 | tf_op jit(solution)/shard_map/ppermute | solution.py:302
  8.6 9.5 %collective-permute-start.5 = (f32[128,512]{1,0:T(8,128)S(1)}, f32[128,512]{1,0:T(8,128)S(1)}, u32[]{:S(2)}, u32[]{:S(2)}) collective-permute-start(f32[128,512]{1,0:T(8,128)S(1)} %get-tuple-element.42.refs_1_.refs_8_.refs_6_.refs_10_), channel_id=1, source_target_pairs={{0,1},{1,0},{2,3},{3,2},{4,6},{5,7},{6,4},{7,5},{8,9},{9,8},{10,11... | collective-permute-start | bytes 786440 | tf_op jit(solution)/shard_map/ppermute | solution.py:299
  12.4 9.1 %collective-permute-start.4 = (f32[128,512]{1,0:T(8,128)S(1)}, f32[128,512]{1,0:T(8,128)S(1)}, u32[]{:S(2)}, u32[]{:S(2)}) collective-permute-start(f32[128,512]{1,0:T(8,128)S(1)} %get-tuple-element.44.refs_3_.refs_4_), channel_id=1, source_target_pairs={{0,8},{1,9},{2,10},{3,11},{4,12},{5,13},{6,14},{7,15}} | collective-permute-start | bytes 786440 | tf_op jit(solution)/shard_map/ppermute | solution.py:374
  15.9 3.1 %collective-permute-start.9 = (f32[64,512]{1,0:T(8,128)S(1)}, f32[64,512]{1,0:T(8,128)S(1)}, u32[]{:S(2)}, u32[]{:S(2)}) collective-permute-start(f32[64,512]{1,0:T(8,128)S(1)} %get-tuple-element.47.refs_3_.refs_4_), channel_id=1, source_target_pairs={{24,16},{25,17},{26,18},{27,19},{28,20},{29,21},{30,22},{31,23}} | collective-permute-start | bytes 393224 | tf_op jit(solution)/shard_map/ppermute | solution.py:374
  16.5 10.0 %collective-permute-start.7 = (f32[128,512]{1,0:T(8,128)S(1)}, f32[128,512]{1,0:T(8,128)S(1)}, u32[]{:S(2)}, u32[]{:S(2)}) collective-permute-start(f32[128,512]{1,0:T(8,128)S(1)} %get-tuple-element.42.refs_1_.refs_8_.refs_6_.refs_10_), channel_id=1, source_target_pairs={{0,3},{1,2},{2,1},{3,0},{4,7},{5,6},{6,5},{7,4},{8,11},{9,10},{10,... | collective-permute-start | bytes 786440 | tf_op jit(solution)/shard_map/ppermute | solution.py:299
  19.5 7.9 %collective-permute-start.10 = (f32[128,512]{1,0:T(8,128)S(1)}, f32[128,512]{1,0:T(8,128)S(1)}, u32[]{:S(2)}, u32[]{:S(2)}) collective-permute-start(f32[128,512]{1,0:T(8,128)S(1)} %shard_map.85), channel_id=1, source_target_pairs={{24,16},{16,8},{25,17},{17,9},{26,18},{18,10},{27,19},{19,11},{28,... | collective-permute-start | bytes 786440 | tf_op jit(solution)/shard_map/ppermute | solution.py:374
  22.0 9.1 %collective-permute-start.6 = (f32[128,512]{1,0:T(8,128)S(1)}, f32[128,512]{1,0:T(8,128)S(1)}, u32[]{:S(2)}, u32[]{:S(2)}) collective-permute-start(f32[128,512]{1,0:T(8,128)S(1)} %shard_map.82), channel_id=1, source_target_pairs={{0,8},{8,16},{1,9},{9,17},{2,10},{10,18},{3,11},{11,19},{4,12},{12... | collective-permute-start | bytes 786440 | tf_op jit(solution)/shard_map/ppermute | solution.py:374
  26.4 9.9 %collective-permute-start.12 = (f32[128,512]{1,0:T(8,128)S(1)}, f32[128,512]{1,0:T(8,128)S(1)}, u32[]{:S(2)}, u32[]{:S(2)}) collective-permute-start(f32[128,512]{1,0:T(8,128)S(1)} %collective-permute-done.5.refs_1_.refs_7_), channel_id=1, source_target_pairs={{0,4},{4,0},{1,5},{5,1},{2,6},{6,2},{3,7},{7,3},{8,12},{12,8},{9,1... | collective-permute-start | bytes 786440 | tf_op jit(solution)/shard_map/ppermute | solution.py:302
  28.0 10.8 %collective-permute-start.11 = (f32[128,512]{1,0:T(8,128)S(1)}, f32[128,512]{1,0:T(8,128)S(1)}, u32[]{:S(2)}, u32[]{:S(2)}) collective-permute-start(f32[128,512]{1,0:T(8,128)S(1)} %shard_map.86), channel_id=1, source_target_pairs={{24,16},{16,8},{8,0},{25,17},{17,9},{9,1},{26,18},{18,10},{10,2},{... | collective-permute-start | bytes 786440 | tf_op jit(solution)/shard_map/ppermute | solution.py:374
  31.7 8.9 %collective-permute-start.8 = (f32[128,512]{1,0:T(8,128)S(1)}, f32[128,512]{1,0:T(8,128)S(1)}, u32[]{:S(2)}, u32[]{:S(2)}) collective-permute-start(f32[128,512]{1,0:T(8,128)S(1)} %shard_map.84), channel_id=1, source_target_pairs={{0,8},{8,16},{16,24},{1,9},{9,17},{17,25},{2,10},{10,18},{18,26},{... | collective-permute-start | bytes 786440 | tf_op jit(solution)/shard_map/ppermute | solution.py:374
  39.3 11.1 %collective-permute-start.13 = (f32[128,512]{1,0:T(8,128)S(1)}, f32[128,512]{1,0:T(8,128)S(1)}, u32[]{:S(2)}, u32[]{:S(2)}) collective-permute-start(f32[128,512]{1,0:T(8,128)S(1)} %shard_map.88.refs_11_), channel_id=1, source_target_pairs={{24,16},{16,8},{8,0},{25,17},{17,9},{9,1},{26,18},{18,10},{10,2},{... | collective-permute-start | bytes 786440 | tf_op jit(solution)/shard_map/ppermute | solution.py:374
  41.2 11.1 %collective-permute-start.16 = (f32[128,512]{1,0:T(8,128)S(1)}, f32[128,512]{1,0:T(8,128)S(1)}, u32[]{:S(2)}, u32[]{:S(2)}) collective-permute-start(f32[128,512]{1,0:T(8,128)S(1)} %shard_map.92), channel_id=1, source_target_pairs={{0,8},{8,16},{16,24},{1,9},{9,17},{17,25},{2,10},{10,18},{18,26},{... | collective-permute-start | bytes 786440 | tf_op jit(solution)/shard_map/ppermute | solution.py:374
  45.8 10.6 %collective-permute-start = (f32[128,512]{1,0:T(8,128)S(1)}, f32[128,512]{1,0:T(8,128)S(1)}, u32[]{:S(2)}, u32[]{:S(2)}) collective-permute-start(f32[128,512]{1,0:T(8,128)S(1)} %get-tuple-element.37), channel_id=1, source_target_pairs={{0,1},{1,0},{2,3},{3,2},{4,6},{5,7},{6,4},{7,5},{8,9},{9,8},{10,11... | collective-permute-start | bytes 786440 | tf_op jit(solution)/shard_map/ppermute | solution.py:299
  51.0 8.3 %collective-permute-start.14 = (f32[128,512]{1,0:T(8,128)S(1)}, f32[128,512]{1,0:T(8,128)S(1)}, u32[]{:S(2)}, u32[]{:S(2)}) collective-permute-start(f32[128,512]{1,0:T(8,128)S(1)} %shard_map.90.refs_11_), channel_id=1, source_target_pairs={{24,16},{16,8},{8,0},{25,17},{17,9},{9,1},{26,18},{18,10},{10,2},{... | collective-permute-start | bytes 786440 | tf_op jit(solution)/shard_map/ppermute | solution.py:374
  52.9 8.3 %collective-permute-start.17 = (f32[128,512]{1,0:T(8,128)S(1)}, f32[128,512]{1,0:T(8,128)S(1)}, u32[]{:S(2)}, u32[]{:S(2)}) collective-permute-start(f32[128,512]{1,0:T(8,128)S(1)} %shard_map.93), channel_id=1, source_target_pairs={{8,16},{16,24},{9,17},{17,25},{10,18},{18,26},{11,19},{19,27},{12,... | collective-permute-start | bytes 786440 | tf_op jit(solution)/shard_map/ppermute | solution.py:374
  53.6 16.9 %collective-permute-start.1 = (f32[128,512]{1,0:T(8,128)S(1)}, f32[128,512]{1,0:T(8,128)S(1)}, u32[]{:S(2)}, u32[]{:S(2)}) collective-permute-start(f32[128,512]{1,0:T(8,128)S(1)} %get-tuple-element.38), channel_id=1, source_target_pairs={{0,2},{1,3},{2,0},{3,1},{4,5},{5,4},{6,7},{7,6},{8,10},{9,11},{10,... | collective-permute-start | bytes 786440 | tf_op jit(solution)/shard_map/ppermute | solution.py:299
  53.6 10.1 %collective-permute-start.2 = (f32[128,512]{1,0:T(8,128)S(1)}, f32[128,512]{1,0:T(8,128)S(1)}, u32[]{:S(2)}, u32[]{:S(2)}) collective-permute-start(f32[128,512]{1,0:T(8,128)S(1)} %get-tuple-element.39), channel_id=1, source_target_pairs={{0,3},{1,2},{2,1},{3,0},{4,7},{5,6},{6,5},{7,4},{8,11},{9,10},{10,... | collective-permute-start | bytes 786440 | tf_op jit(solution)/shard_map/ppermute | solution.py:299
  59.8 10.1 %collective-permute-start.15 = (f32[128,512]{1,0:T(8,128)S(1)}, f32[128,512]{1,0:T(8,128)S(1)}, u32[]{:S(2)}, u32[]{:S(2)}) collective-permute-start(f32[128,512]{1,0:T(8,128)S(1)} %shard_map.91.refs_11_), channel_id=1, source_target_pairs={{16,8},{8,0},{17,9},{9,1},{18,10},{10,2},{19,11},{11,3},{20,12},{1... | collective-permute-start | bytes 786440 | tf_op jit(solution)/shard_map/ppermute | solution.py:374
  61.7 8.8 %collective-permute-start.21 = (f32[128,512]{1,0:T(8,128)S(1)}, f32[128,512]{1,0:T(8,128)S(1)}, u32[]{:S(2)}, u32[]{:S(2)}) collective-permute-start(f32[128,512]{1,0:T(8,128)S(1)} %shard_map.98), channel_id=1, source_target_pairs={{16,24},{17,25},{18,26},{19,27},{20,28},{21,29},{22,30},{23,31}} | collective-permute-start | bytes 786440 | tf_op jit(solution)/shard_map/ppermute | solution.py:374
  62.4 20.0 %collective-permute-start.19 = (f32[128,512]{1,0:T(8,128)S(1)}, f32[128,512]{1,0:T(8,128)S(1)}, u32[]{:S(2)}, u32[]{:S(2)}) collective-permute-start(f32[128,512]{1,0:T(8,128)S(1)} %get-tuple-element.57), channel_id=1, source_target_pairs={{0,1},{1,0},{2,3},{3,2},{4,6},{5,7},{6,4},{7,5},{8,9},{9,8},{10,11... | collective-permute-start | bytes 786440 | tf_op jit(solution)/shard_map/ppermute | solution.py:299
  65.0 17.4 %collective-permute-start.20 = (f32[128,512]{1,0:T(8,128)S(1)}, f32[128,512]{1,0:T(8,128)S(1)}, u32[]{:S(2)}, u32[]{:S(2)}) collective-permute-start(f32[128,512]{1,0:T(8,128)S(1)} %get-tuple-element.58), channel_id=1, source_target_pairs={{0,3},{1,2},{2,1},{3,0},{4,7},{5,6},{6,5},{7,4},{8,11},{9,10},{10,... | collective-permute-start | bytes 786440 | tf_op jit(solution)/shard_map/ppermute | solution.py:299
  71.7 10.7 %collective-permute-start.22 = (f32[128,512]{1,0:T(8,128)S(1)}, f32[128,512]{1,0:T(8,128)S(1)}, u32[]{:S(2)}, u32[]{:S(2)}) collective-permute-start(f32[128,512]{1,0:T(8,128)S(1)} %get-tuple-element.60), channel_id=1, source_target_pairs={{0,2},{1,3},{2,0},{3,1},{4,5},{5,4},{6,7},{7,6},{8,10},{9,11},{10,... | collective-permute-start | bytes 786440 | tf_op jit(solution)/shard_map/ppermute | solution.py:299
  71.9 9.4 %collective-permute-start.18 = (f32[64,512]{1,0:T(8,128)S(1)}, f32[64,512]{1,0:T(8,128)S(1)}, u32[]{:S(2)}, u32[]{:S(2)}) collective-permute-start(f32[64,512]{1,0:T(8,128)S(1)} %shard_map.95.refs_11_.refs_16_), channel_id=1, source_target_pairs={{8,0},{9,1},{10,2},{11,3},{12,4},{13,5},{14,6},{15,7}} | collective-permute-start | bytes 393224 | tf_op jit(solution)/shard_map/ppermute | solution.py:374
  83.0 11.8 %collective-permute-start.23 = (f32[128,512]{1,0:T(8,128)S(1)}, f32[128,512]{1,0:T(8,128)S(1)}, u32[]{:S(2)}, u32[]{:S(2)}) collective-permute-start(f32[128,512]{1,0:T(8,128)S(1)} %shard_map.100.refs_2_), channel_id=1, source_target_pairs={{0,4},{4,0},{1,5},{5,1},{2,6},{6,2},{3,7},{7,3},{8,12},{12,8},{9,1... | collective-permute-start | bytes 786440 | tf_op jit(solution)/shard_map/ppermute | solution.py:302
  84.3 3.7 %collective-permute-start.24 = (f32[8,128]{1,0:T(8,128)S(1)}, f32[8,128]{1,0:T(8,128)S(1)}, u32[]{:S(2)}, u32[]{:S(2)}) collective-permute-start(f32[8,128]{1,0:T(8,128)S(1)} %shard_map.101.refs_1_), channel_id=1, source_target_pairs={{0,8},{8,0},{16,24},{24,16},{1,9},{9,1},{17,25},{25,17},{2,10},{10... | collective-permute-start | bytes 12296 | tf_op jit(solution)/shard_map/ppermute | solution.py:441
  88.5 4.6 %collective-permute-start.25 = (f32[8,128]{1,0:T(8,128)S(1)}, f32[8,128]{1,0:T(8,128)S(1)}, u32[]{:S(2)}, u32[]{:S(2)}) collective-permute-start(f32[8,128]{1,0:T(8,128)S(1)} %shard_map.102.refs_1_), channel_id=1, source_target_pairs={{0,16},{8,24},{16,0},{24,8},{1,17},{9,25},{17,1},{25,9},{2,18},{10... | collective-permute-start | bytes 12296 | tf_op jit(solution)/shard_map/ppermute | solution.py:441
  93.6 1.2 %collective-permute-start.26 = (f32[8,128]{1,0:T(8,128)S(1)}, f32[8,128]{1,0:T(8,128)S(1)}, u32[]{:S(2)}, u32[]{:S(2)}) collective-permute-start(f32[8,128]{1,0:T(8,128)S(1)} %shard_map.103.refs_5_), channel_id=1, source_target_pairs={{0,4},{4,0},{1,5},{5,1},{2,6},{6,2},{3,7},{7,3},{8,12},{12,8},{9,1... | collective-permute-start | bytes 12296 | tf_op jit(solution)/shard_map/ppermute | solution.py:302
  95.9 9.9 %collective-permute-start.27 = (f32[136,512]{1,0:T(8,128)S(1)}, f32[136,512]{1,0:T(8,128)S(1)}, u32[]{:S(2)}, u32[]{:S(2)}) collective-permute-start(f32[136,512]{1,0:T(8,128)S(1)} %shard_map.104.refs_5_), channel_id=1, source_target_pairs={{0,1},{1,0},{2,3},{3,2},{4,6},{5,7},{6,4},{7,5},{8,9},{9,8},{10,11... | collective-permute-start | bytes 835592 | tf_op jit(solution)/shard_map/ppermute | solution.py:299
  99.4 11.5 %collective-permute-start.29 = (f32[136,512]{1,0:T(8,128)S(1)}, f32[136,512]{1,0:T(8,128)S(1)}, u32[]{:S(2)}, u32[]{:S(2)}) collective-permute-start(f32[136,512]{1,0:T(8,128)S(1)} %shard_map.104.refs_5_), channel_id=1, source_target_pairs={{0,3},{1,2},{2,1},{3,0},{4,7},{5,6},{6,5},{7,4},{8,11},{9,10},{10,... | collective-permute-start | bytes 835592 | tf_op jit(solution)/shard_map/ppermute | solution.py:299
  105.8 5.1 %collective-permute-start.28 = (f32[136,512]{1,0:T(8,128)S(1)}, f32[136,512]{1,0:T(8,128)S(1)}, u32[]{:S(2)}, u32[]{:S(2)}) collective-permute-start(f32[136,512]{1,0:T(8,128)S(1)} %collective-permute-done.27.refs_6_), channel_id=1, source_target_pairs={{0,4},{4,0},{1,5},{5,1},{2,6},{6,2},{3,7},{7,3},{8,12},{12,8},{9,1... | collective-permute-start | bytes 835592 | tf_op jit(solution)/shard_map/ppermute | solution.py:302
  (4 other events, 11.0 us)

commit v3 on v0

v3 whole, which is shorter than its diff:
```python
import functools

import jax
import jax.numpy as jnp
from jax import lax
from jax.experimental import pallas as pl
from jax.experimental.pallas import tpu as pltpu
from jax.sharding import PartitionSpec as P

LEVELS = 4
BLOCK = 128
LOSS_ROWS = 8
GELU_C = 0.7978845608028654
GELU_A = 0.044715

VMEM = pl.BlockSpec(memory_space=pltpu.VMEM)
SMEM = pl.BlockSpec(memory_space=pltpu.SMEM)
HBM = pl.BlockSpec(memory_space=pltpu.HBM)
ANY = pl.BlockSpec(memory_space=pl.ANY)


def f32(*shape):
    return jax.ShapeDtypeStruct(shape, jnp.float32)


def bf16(*shape):
    return jax.ShapeDtypeStruct(shape, jnp.bfloat16)


def call(kernel, outs, arrays, after=(), specs=None, out_specs=None, scratch=(), flops=0, mib=12):
    skip = slice(len(arrays), len(arrays) + len(after))

    def run(*refs):
        kernel(*refs[: skip.start], *refs[skip.stop :])

    return pl.pallas_call(
        run,
        out_shape=outs,
        in_specs=list(specs or [VMEM] * len(arrays)) + [ANY] * len(after),
        out_specs=out_specs or [VMEM] * len(outs),
        scratch_shapes=list(scratch),
        compiler_params=pltpu.CompilerParams(vmem_limit_bytes=mib * 1024 * 1024),
        cost_estimate=pl.CostEstimate(flops=flops, bytes_accessed=1 << 20, transcendentals=0),
    )(*arrays, *after)


def total_of(terms):
    return functools.reduce(jnp.add, terms)


def place_in_chain():
    lat = lax.axis_index("lat")
    return jnp.where(lax.axis_index("wid") == 0, lat, lax.axis_size("lat") - 1 - lat)


def level_table(bounds, count, out):
    lasts = bounds[...] - 1 - lax.axis_index("lat") * count
    upward = lax.axis_index("wid") == 0

    def put(row, value):
        out[row : row + 1, :] = jnp.broadcast_to(value, (1, BLOCK))

    for i in range(count):
        hits = (jnp.minimum(lasts, count - 1) == i).astype(jnp.float32)
        ending = jnp.sum(hits, axis=1, keepdims=True)
        put(i, ending)
        put(count + i, jnp.where(upward, jnp.full_like(ending, float(i == count - 1)), ending))
    for m in range(LEVELS):
        for i in range(count):
            put((2 + m) * count + i, (lasts[:, m : m + 1] == i).astype(jnp.float32))


def pre_kernel(
    resid, dictionary, bounds, partial_out, dict_out, table_out, resid_v, dict_v, sems
):
    pieces, lats, width = dict_v.shape
    here = pl.ds(pl.multiple_of(lax.axis_index("tok") * width, width), width)
    copies = [pltpu.make_async_copy(resid, resid_v, sems.at[pieces])]
    for i in range(pieces):
        cols = pl.ds(i * width, width)
        copies.append(pltpu.make_async_copy(dictionary.at[:, cols], dict_v.at[i], sems.at[i]))
    copies.append(pltpu.make_async_copy(dictionary.at[:, here], dict_out, sems.at[pieces + 1]))
    for copy in copies:
        copy.start()
    level_table(bounds, lats // BLOCK, table_out)
    copies[0].wait()
    total = None
    for i in range(pieces):
        copies[1 + i].wait()
        term = lax.dot_general(
            resid_v[:, i * width : (i + 1) * width],
            dict_v[i],
            (((1,), (1,)), ((), ())),
            preferred_element_type=jnp.float32,
        )
        total = term if total is None else total + term
    partial_out[...] = total
    copies[-1].wait()


def widen_kernel(array, out):
    out[...] = array[...].astype(jnp.float32)


def pieces_kernel(resid, bias, bias_out, *outs):
    width = outs[0].shape[1]
    tok = lax.axis_index("tok")

    def cols(t):
        return pl.ds(pl.multiple_of(t * width, width), width)

    bias_out[...] = bias[:, cols(tok)]
    for q, out in enumerate(outs):
        out[...] = resid[:, cols(tok ^ q)].astype(jnp.float32)


def block_mask(active, lats):
    first = lax.axis_index("lat") * (lats // BLOCK)
    ids = first + lax.broadcasted_iota(jnp.int32, (1, lats), 1) // BLOCK
    hit = None
    for q in range(active.shape[1]):
        same = active[:, q : q + 1] == ids
        hit = same if hit is None else hit | same
    return hit


def activate_kernel(mine, other, bias, active, pre_out, act_out):
    pre = mine[...] + other[...] + bias[...]
    pre_out[...] = pre
    inner = GELU_C * (pre + GELU_A * (pre * pre * pre))
    gelu = 0.5 * pre * (1.0 + jnp.tanh(inner))
    act_out[...] = jnp.where(block_mask(active[...], pre.shape[1]), gelu, 0.0)


def half_of(wid, rows):
    return pl.ds(pl.multiple_of(wid * (rows // 2), rows // 2), rows // 2)


def g_pre_kernel(pre_ref, active, loss, *refs):
    terms, out = refs[:-1], refs[-1]
    mine = half_of(lax.axis_index("wid"), pre_ref.shape[0])
    pre = pre_ref[mine, :]
    inner = GELU_C * (pre + GELU_A * (pre * pre * pre))
    slope = GELU_C * (1.0 + 3.0 * GELU_A * (pre * pre))
    bend = jnp.tanh(inner)
    deriv = 0.5 * (1.0 + bend) + 0.5 * pre * (1.0 - bend * bend) * slope
    hit = block_mask(active[mine, :], pre.shape[1])
    rows = pre.shape[0]
    out[:rows, :] = jnp.where(hit, deriv * total_of([t[...] for t in terms]), 0.0)
    out[rows:, :] = jnp.zeros_like(out[rows:, :])
    out[rows:, :BLOCK] = loss[...]


def running_parts(act, dict_ref):
    sums = []
    for i in range(dict_ref.shape[0] // BLOCK):
        span = slice(i * BLOCK, (i + 1) * BLOCK)
        part = jnp.dot(
            act[:, span], dict_ref[span, :].astype(jnp.bfloat16), preferred_element_type=jnp.float32
        )
        sums.append(sums[-1] + part if sums else part)
    return sums


def project_kernel(own, other, table, *refs):
    acts, rows_out, out = refs[:-2], refs[-2], refs[-1]
    rows = acts[0][...]
    if len(acts) > 1:
        rows = jnp.where(lax.axis_index("wid") == 0, rows, acts[1][...])
    rows = rows.astype(jnp.bfloat16)
    rows_out[...] = rows
    width = own.shape[1]
    for side, dict_ref in enumerate((own, other)):
        sums = running_parts(rows, dict_ref)
        count = len(sums)
        out[:, side * width : (side + 1) * width] = total_of(
            [table[count + i : count + i + 1, :1] * s for i, s in enumerate(sums)]
        )


def message_kernel(places, got, *refs):
    out = refs[-1]
    index = place_in_chain()
    for place, piece in zip(places, refs[:-1]):

        @pl.when(index == place)
        def _():
            out[...] = piece[...] + got[...] if place else piece[...]


def choose_kernel(places, *refs):
    arrived, own_out, hand_out = refs[:-2], refs[-2], refs[-1]
    width = own_out.shape[1]
    index = place_in_chain()

    @pl.when(index == 0)
    def _():
        own_out[...] = jnp.zeros_like(own_out)
        hand_out[...] = jnp.zeros_like(hand_out)

    for place, ref in zip(places, arrived):

        @pl.when(index == place if len(arrived) > 1 else index > 0)
        def _():
            own_out[...] = ref[:, :width]
            hand_out[...] = ref[:, width:]


def square_sums(table, shifted):
    count = len(shifted)
    squares = []
    for v in shifted:
        lanes = jnp.sum(v * v, axis=0, keepdims=True)
        squares.append(total_of([lanes[:, i : i + BLOCK] for i in range(0, lanes.shape[1], BLOCK)]))
    rows = []
    for m in range(LEVELS):
        at = (2 + m) * count
        rows.append(total_of([table[at + i : at + i + 1, :] * s for i, s in enumerate(squares)]))
    return jnp.concatenate(rows + [jnp.zeros((LOSS_ROWS - LEVELS, BLOCK), jnp.float32)], axis=0)


def error_kernel(act, dictionary, resid, bias, table, mine, other, *refs):
    before, (err_out, keep_out, give_out, loss_out) = refs[:-4], refs[-4:]
    upward = lax.axis_index("wid") == 0
    earlier = jnp.where(upward, mine[...], other[...])
    later = jnp.where(upward, other[...], mine[...])
    base = bias[...] - resid[...] + earlier
    sums = running_parts(act[...], dictionary)
    shifted = [base + s for s in sums]
    loss_out[...] = total_of([square_sums(table, shifted)] + [b[...] for b in before])
    err = later
    for i in reversed(range(len(sums))):
        err = err + table[i : i + 1, :1] * shifted[i]
        rounded = err.astype(jnp.bfloat16)
        err_out[i] = rounded
        cols = slice(i * BLOCK, (i + 1) * BLOCK)
        gact = lax.dot_general(
            rounded,
            dictionary[cols, :],
            (((1,), (1,)), ((), ())),
            preferred_element_type=jnp.float32,
        )
        half = gact.shape[0] // 2
        keep_out[:, cols] = jnp.where(upward, gact[:half, :], gact[half:, :])
        give_out[:, cols] = jnp.where(upward, gact[half:, :], gact[:half, :])


def add_kernel(*refs):
    refs[-1][...] = total_of([ref[...] for ref in refs[:-1]])


def decode_kernel(*refs):
    n = (len(refs) - 1) // 2
    errs, acts, out = refs[:n], refs[n : 2 * n], refs[-1]
    for i in range(errs[0].shape[0]):
        cols = slice(i * BLOCK, (i + 1) * BLOCK)
        err = jnp.concatenate([e[i] for e in errs], axis=0)
        act = jnp.concatenate([a[:, cols] for a in acts], axis=0)
        out[:, cols] = lax.dot_general(
            err, act, (((0,), (0,)), ((), ())), preferred_element_type=jnp.float32
        )


def encode_kernel(scale, *refs):
    n = (len(refs) - 3) // 3
    resids, grads, base, out, loss_out = refs[:n], refs[n : 3 * n], refs[-3], refs[-2], refs[-1]
    rows = resids[0].shape[0]
    wid = lax.axis_index("wid")
    halves = [half_of(wid, rows), half_of(1 - wid, rows)]
    resid = jnp.concatenate([r[h, :].astype(jnp.bfloat16) for h in halves for r in resids], axis=0)
    grad = jnp.concatenate([g[: rows // 2, :].astype(jnp.bfloat16) for g in grads], axis=0)
    total = base[...] + lax.dot_general(
        resid, grad, (((0,), (0,)), ((), ())), preferred_element_type=jnp.float32
    )
    out[...] = total.astype(jnp.bfloat16)
    lanes = total_of([g[rows // 2 :, :BLOCK] for g in grads])
    for m in range(LEVELS):
        loss_out[m] = jnp.sum(lanes[m : m + 1, :]) * scale


def pick(index, choices):
    values = sorted(choices)
    result = choices[values[0]]
    for value in values[1:]:
        result = jnp.where(index == value, choices[value], result)
    return result


def body(resid, dictionary, enc_bias, dec_bias, active_blocks, level_bounds):
    rows, half = resid.shape
    lats = dictionary.shape[0]
    n_lat, n_wid, n_tok = lax.axis_size("lat"), lax.axis_size("wid"), lax.axis_size("tok")
    width = half // n_tok
    count = lats // BLOCK
    work = 2 * rows * lats * width

    def across(array, q):
        return lax.ppermute(array, "tok", [(t, t ^ q) for t in range(n_tok)])

    def swap(array):
        return lax.ppermute(array, "wid", [(w, w ^ 1) for w in range(n_wid)])

    def gather(array):
        if n_tok != 4:
            return [(array,)] + [(across(array, q),) for q in range(1, n_tok)]
        pairs = [(w * n_tok + t, w * n_tok + (t ^ (1 + w))) for w in range(n_wid) for t in range(n_tok)]
        near = lax.ppermute(array, ("wid", "tok"), pairs)
        far = across(array, 3)
        other = swap(near)
        return [(array,), (near, other), (other, near), (far,)]

    partial, dict_here, table = call(
        pre_kernel,
        [f32(rows, lats), bf16(lats, width), f32((2 + LEVELS) * count, BLOCK)],
        (resid, dictionary, level_bounds.reshape(1, LEVELS)),
        specs=[HBM, HBM, VMEM],
        scratch=[
            pltpu.VMEM((rows, half), jnp.bfloat16),
            pltpu.VMEM((n_tok, lats, width), jnp.bfloat16),
            pltpu.SemaphoreType.DMA((n_tok + 2,)),
        ],
        mib=62,
    )
    partial_other = swap(partial)
    dict_wide = call(widen_kernel, [f32(lats, width)], (dict_here,), after=(partial,))[0]
    dict_other = swap(dict_wide)
    pre, act = call(
        activate_kernel,
        [f32(rows, lats)] * 2,
        (partial, partial_other, enc_bias.reshape(1, lats), active_blocks),
        after=(dict_wide,),
    )
    gathered = gather(act)
    bias_here, *pieces = call(
        pieces_kernel,
        [f32(1, width)] + [f32(rows, width)] * n_tok,
        (resid, dec_bias.reshape(1, half)),
        after=(act,),
    )
    resids = [piece if q == 0 else across(piece, q) for q, piece in enumerate(pieces)]

    order = [0, 1, 3, 2] if n_tok == 4 else list(range(n_tok))
    acts, sums = {}, []
    for q in order:
        acts[q], passed = call(
            project_kernel,
            [bf16(rows, lats), f32(rows, 2 * width)],
            (dict_here, dict_other, table, *gathered[q]),
            flops=2 * work,
        )
        sums.append(passed)

    got, sent = [], []
    errs, gacts, loss = {}, [], ()
    for step in range(n_tok + 2 * (n_lat - 1)):
        if step < n_tok + n_lat - 2:
            at = [p for p in range(n_lat - 1) if 0 <= step - p < n_tok]
            message = sums[0]
            if step:
                done = step - n_lat
                after = [errs[order[done]]] if done >= 0 else []
                if 0 <= step - n_lat + 1 < n_tok - 1:
                    after.append(resids[order[step - n_lat + 2]])
                message = call(
                    functools.partial(message_kernel, at),
                    [f32(rows, 2 * width)],
                    (got[-1], *[sums[step - p] for p in at]),
                    after=after,
                )[0]
            pairs = []
            for p in at:
                pairs.append((2 * p, 2 * (p + 1)))
                pairs.append((2 * (n_lat - 1 - p) + 1, 2 * (n_lat - 2 - p) + 1))
            got.append(lax.ppermute(message, ("lat", "wid"), pairs))
            sent = [message]
        c = step - (n_lat - 1)
        if not 0 <= c < n_tok:
            continue
        q = order[c]
        places = list(range(1, n_lat))
        arrived = [got[c + p - 1] for p in places]
        if n_lat > 4:
            arrived = [pick(place_in_chain(), dict(zip(places, arrived)))]
        mine, hand = call(
            functools.partial(choose_kernel, places), [f32(rows, width)] * 2, arrived, after=sent
        )
        errs[q], keep, give, loss_here = call(
            error_kernel,
            [bf16(count, rows, width)] + [f32(rows // 2, lats)] * 2 + [f32(LOSS_ROWS, BLOCK)],
            (acts[q], dict_here, resids[q], bias_here, table, mine, swap(hand), *loss),
            flops=2 * work,
        )
        loss = (loss_here,)
        if q == 0:
            gacts += [keep, swap(give)]
        else:
            gacts.append(across(call(add_kernel, [f32(rows // 2, lats)], (keep, swap(give)))[0], q))
        sent = []

    loss, gap = loss[0], 1
    while gap < n_lat:
        other = lax.ppermute(loss, "lat", [(p, p ^ gap) for p in range(n_lat)])
        loss = call(add_kernel, [f32(LOSS_ROWS, BLOCK)], (loss, other))[0]
        gap *= 2

    g_pre = call(
        g_pre_kernel, [f32(rows // 2 + LOSS_ROWS, lats)], (pre, active_blocks, loss, *gacts)
    )[0]
    mine = [across(g_pre, q) if q else g_pre for q in range(n_tok)]
    others = [swap(g) for g in mine]
    decoded = call(
        decode_kernel,
        [f32(width, lats)],
        (*[errs[q] for q in order], *[acts[q] for q in order]),
        flops=n_tok * work,
    )[0]
    grad, losses = call(
        functools.partial(encode_kernel, 1.0 / (rows * n_tok * half * n_wid)),
        [bf16(width, lats), f32(LEVELS)],
        (*resids, *mine, *others, decoded),
        out_specs=[VMEM, SMEM],
        flops=n_tok * work,
    )
    return (losses, grad)


def solution(mesh):
    return jax.shard_map(
        body,
        mesh=mesh,
        in_specs=(P("tok", "wid"), P("lat", "wid"), P("lat"), P("wid"), P("tok", None), P()),
        out_specs=(P(), P(("wid", "tok"), "lat")),
        check_vma=False,
    )
```

time: 377 us -> 106 us (0.28)
  waiting for transfers between devices: 278 us -> 49.8 us
  starting transfers between devices: 0.2 us -> 41.4 us
  blocking collectives: 40.7 us -> 0 us
  matrix products: 18.4 us -> 0 us
  between operations: 19.1 us -> 0.99 us
  Pallas kernels: 0 us -> 12.6 us
  other arithmetic: 10.4 us -> 0 us
  local copies, waits for them, and re-layouts: 10.1 us -> 1.17 us
    psum x3 -> x0, waiting for transfers between devices: 185 us -> none  [the longest x1 157 us: broadcast(): return lax.psum(jnp.where(mine, array, jnp.zeros_like(array)), axis)]
    all_gather x1 -> x0, waiting for transfers between devices: 81.9 us -> none  [entering(): gathered = lax.all_gather(part, axis)]
    ppermute x0 -> x34, waiting for transfers between devices: none -> 49.8 us  [the longest x10 32.4 us: across(): return lax.ppermute(array, 'tok', [(t, t ^ q) for t in range(n_tok)])]
    ppermute x0 -> x34, starting transfers between devices: none -> 41.4 us  [the longest x6 15.2 us: body(): got.append(lax.ppermute(message, ('lat', 'wid'), pairs))]
    psum x1 -> x0, blocking collectives: 40.7 us -> none  [body(): total_sq = lax.psum(jnp.stack(squares), ('lat', 'wid', 'tok'))]
    dot_general x5 -> x0, matrix products: 18.4 us -> none  [the longest x1 5.67 us: body(): jnp.einsum('ktd,tkc->dkc', err_half, act, preferred_element_type=jnp.floa...]
    pallas_call x0 -> x29, Pallas kernels: none -> 12.6 us  [call(): pl.pallas_call(run, out_shape=outs, in_specs=list(specs or [VMEM] * len(a...]
    reduce_scatter x1 -> x0, waiting for transfers between devices: 10.9 us -> none  [body(): lax.psum_scatter(decode_term.reshape(half_width // lax.axis_size('tok') *...]
  transfers between devices with their start and end apart: 5 -> 34, of which waited for: 5 -> 16; matrix products, arithmetic and copies ran while one was open for 2% -> 0% of each run, Pallas kernels for 0% -> 7%
where the time goes in v3:
time: 106 us
  waiting for transfers between devices  49.8 us (47%)
  starting transfers between devices  41.4 us (39%)
  Pallas kernels  12.6 us (12%)
  local copies, waits for them, and re-layouts  1.17 us (1%)
    ppermute x10, waiting for transfers between devices, across(): return lax.ppermute(array, 'tok', [(t, t ^ q) for t in range(n_tok)])  32.4 us
    ppermute x6, starting transfers between devices, body(): got.append(lax.ppermute(message, ('lat', 'wid'), pairs))  15.2 us
    pallas_call x29, Pallas kernels, call(): pl.pallas_call(run, out_shape=outs, in_specs=list(specs or [VMEM] * len(a...  12.6 us
    ppermute x15, starting transfers between devices, swap(): return lax.ppermute(array, 'wid', [(w, w ^ 1) for w in range(n_wid)])  12 us
    ppermute x10, starting transfers between devices, across(): return lax.ppermute(array, 'tok', [(t, t ^ q) for t in range(n_tok)])  11.1 us
    ppermute x2, waiting for transfers between devices, body(): other = lax.ppermute(loss, 'lat', [(p, p ^ gap) for p in range(n_lat)])  7.66 us
    ppermute x15, waiting for transfers between devices, swap(): return lax.ppermute(array, 'wid', [(w, w ^ 1) for w in range(n_wid)])  4.99 us
    ppermute x6, waiting for transfers between devices, body(): got.append(lax.ppermute(message, ('lat', 'wid'), pairs))  4.4 us
  transfers between devices with their start and end apart: 34, of which 16 were waited for; matrix products, arithmetic and copies ran while one was open for 0% of the time, Pallas kernels for 7%

profile of v3, /device:TPU:0, one launch (start us, length us, event | category | flops | bytes accessed | tf_op | source)
XLA Modules:
  0.0 106.0 jit_solution(8597953947924747082)
XLA Ops:
  0.7 3.8 %shard_map.77 = (f32[128,512]{1,0:T(8,128)}, bf16[512,512]{1,0:T(8,128)(2,1)}, f32[24,128]{1,0:T(8,128)}) custom-call(bf16[128,2048]{1,0:T(8,128)(2,1)} %refs_0_.3, bf16[512,2048]{1,0:T(8,128)(2,1)} %refs_1_.2, s32[1,4]{1,0:T(1,128)} %bitcast.5), custom_call_target="tpu_custom_call" | custom-call | bytes 1048576 | tf_op jit(solution)/shard_map/pallas_call | solution.py:36
  4.5 1.0 copy-done
  6.3 2.6 %collective-permute-done.refs_1_ = f32[128,512]{1,0:T(8,128)S(1)} collective-permute-done((f32[128,512]{1,0:T(8,128)}, f32[128,512]{1,0:T(8,128)S(1)}, u32[]{:S(2)}, u32[]{:S(2)}) %collective-permute-start) | collective-permute-done | bytes 262176 | tf_op jit(solution)/shard_map/ppermute | solution.py:301
  8.9 1.4 %shard_map.79 = (f32[128,512]{1,0:T(8,128)S(1)}, f32[128,512]{1,0:T(8,128)S(1)}) custom-call(f32[128,512]{1,0:T(8,128)} %get-tuple-element.46.refs_1_.refs_0_, f32[128,512]{1,0:T(8,128)S(1)} %collective-permute-done.refs_1_, f32[1,512]{1,0:T(1,128)S(1)} %bitcast.4, s32[128,8]{1,0:T(8,128)S(1)} %copy.8.refs_3_.refs_1_, f32[512,512]{1,0:T(8,128)S(1)} %shard_map.78.refs_4_), custom_call_target="tpu_custom_call" | custom-call | bytes 1048576 | tf_op jit(solution)/shard_map/pallas_call | solution.py:36
  10.3 2.7 %collective-permute-start.5 = (f32[128,512]{1,0:T(8,128)S(1)}, f32[128,512]{1,0:T(8,128)S(1)}, u32[]{:S(2)}, u32[]{:S(2)}) collective-permute-start(f32[128,512]{1,0:T(8,128)S(1)} %get-tuple-element.48.refs_2_.refs_3_), channel_id=1, source_target_pairs={{0,1},{1,0},{2,3},{3,2},{4,6},{5,7},{6,4},{7,5},{8,9},{9,8},{10,11... | collective-permute-start | bytes 786440 | tf_op jit(solution)/shard_map/ppermute | solution.py:307
  13.5 3.5 %collective-permute-start.7 = (f32[128,1024]{1,0:T(8,128)S(1)}, f32[128,1024]{1,0:T(8,128)S(1)}, u32[]{:S(2)}, u32[]{:S(2)}) collective-permute-start(f32[128,1024]{1,0:T(8,128)S(1)} %get-tuple-element.57.refs_2_.refs_3_), channel_id=1, source_target_pairs={{0,8},{28,20},{1,9},{29,21},{2,10},{30,22},{3,11},{31,23}} | collective-permute-start | bytes 1572872 | tf_op jit(solution)/shard_map/ppermute | solution.py:374
  17.3 1.5 %collective-permute-done.6.refs_3_.refs_4_ = f32[128,512]{1,0:T(8,128)S(1)} collective-permute-done((f32[128,512]{1,0:T(8,128)S(1)}, f32[128,512]{1,0:T(8,128)S(1)}, u32[]{:S(2)}, u32[]{:S(2)}) %collective-permute-start.6) | collective-permute-done | bytes 262176 | tf_op jit(solution)/shard_map/ppermute | solution.py:301
  19.4 4.3 %collective-permute-done.7.refs_0_ = f32[128,1024]{1,0:T(8,128)S(1)} collective-permute-done((f32[128,1024]{1,0:T(8,128)S(1)}, f32[128,1024]{1,0:T(8,128)S(1)}, u32[]{:S(2)}, u32[]{:S(2)}) %collective-permute-start.7) | collective-permute-done | bytes 524320 | tf_op jit(solution)/shard_map/ppermute | solution.py:374
  23.7 4.6 %collective-permute-start.8 = (f32[128,1024]{1,0:T(8,128)S(1)}, f32[128,1024]{1,0:T(8,128)S(1)}, u32[]{:S(2)}, u32[]{:S(2)}) collective-permute-start(f32[128,1024]{1,0:T(8,128)S(1)} %shard_map.84), channel_id=1, source_target_pairs={{0,8},{28,20},{8,16},{20,12},{1,9},{29,21},{9,17},{21,13},{2,10},{... | collective-permute-start | bytes 1572872 | tf_op jit(solution)/shard_map/ppermute | solution.py:374
  28.3 1.6 %collective-permute-start.9 = (f32[128,512]{1,0:T(8,128)S(1)}, f32[128,512]{1,0:T(8,128)S(1)}, u32[]{:S(2)}, u32[]{:S(2)}) collective-permute-start(f32[128,512]{1,0:T(8,128)S(1)} %get-tuple-element.48.refs_2_.refs_3_), channel_id=1, source_target_pairs={{0,3},{1,2},{2,1},{3,0},{4,7},{5,6},{6,5},{7,4},{8,11},{9,10},{10,... | collective-permute-start | bytes 786440 | tf_op jit(solution)/shard_map/ppermute | solution.py:298
  29.8 8.4 %collective-permute-done.9.refs_3_ = f32[128,512]{1,0:T(8,128)S(1)} collective-permute-done((f32[128,512]{1,0:T(8,128)S(1)}, f32[128,512]{1,0:T(8,128)S(1)}, u32[]{:S(2)}, u32[]{:S(2)}) %collective-permute-start.9) | collective-permute-done | bytes 262176 | tf_op jit(solution)/shard_map/ppermute | solution.py:298
  38.8 1.3 %collective-permute-start.10 = (f32[128,1024]{1,0:T(8,128)S(1)}, f32[128,1024]{1,0:T(8,128)S(1)}, u32[]{:S(2)}, u32[]{:S(2)}) collective-permute-start(f32[128,1024]{1,0:T(8,128)S(1)} %shard_map.86), channel_id=1, source_target_pairs={{0,8},{28,20},{8,16},{20,12},{16,24},{12,4},{1,9},{29,21},{9,17},{... | collective-permute-start | bytes 1572872 | tf_op jit(solution)/shard_map/ppermute | solution.py:374
  40.8 5.9 %collective-permute-done.1.refs_4_.refs_2_.refs_1_ = f32[128,512]{1,0:T(8,128)S(1)} collective-permute-done((f32[128,512]{1,0:T(8,128)S(1)}, f32[128,512]{1,0:T(8,128)S(1)}, u32[]{:S(2)}, u32[]{:S(2)}) %collective-permute-start.1) | collective-permute-done | bytes 262176 | tf_op jit(solution)/shard_map/ppermute | solution.py:298
  46.9 4.4 %collective-permute-start.11 = (f32[128,1024]{1,0:T(8,128)S(1)}, f32[128,1024]{1,0:T(8,128)S(1)}, u32[]{:S(2)}, u32[]{:S(2)}) collective-permute-start(f32[128,1024]{1,0:T(8,128)S(1)} %shard_map.87.refs_3_), channel_id=1, source_target_pairs={{0,8},{28,20},{8,16},{20,12},{16,24},{12,4},{1,9},{29,21},{9,17},{... | collective-permute-start | bytes 1572872 | tf_op jit(solution)/shard_map/ppermute | solution.py:374
  51.4 1.5 %collective-permute-start.3 = (f32[128,512]{1,0:T(8,128)S(1)}, f32[128,512]{1,0:T(8,128)S(1)}, u32[]{:S(2)}, u32[]{:S(2)}) collective-permute-start(f32[128,512]{1,0:T(8,128)S(1)} %get-tuple-element.52), channel_id=1, source_target_pairs={{0,3},{1,2},{2,1},{3,0},{4,7},{5,6},{6,5},{7,4},{8,11},{9,10},{10,... | collective-permute-start | bytes 786440 | tf_op jit(solution)/shard_map/ppermute | solution.py:298
  53.6 7.5 %collective-permute-done.3.refs_4_.refs_2_.refs_3_ = f32[128,512]{1,0:T(8,128)S(1)} collective-permute-done((f32[128,512]{1,0:T(8,128)S(1)}, f32[128,512]{1,0:T(8,128)S(1)}, u32[]{:S(2)}, u32[]{:S(2)}) %collective-permute-start.3) | collective-permute-done | bytes 262176 | tf_op jit(solution)/shard_map/ppermute | solution.py:298
  61.1 0.7 collective-permute-start.13
  62.2 0.8 collective-permute-start.2
  64.1 6.5 %collective-permute-done.2.refs_3_.refs_2_ = f32[128,512]{1,0:T(8,128)S(1)} collective-permute-done((f32[128,512]{1,0:T(8,128)S(1)}, f32[128,512]{1,0:T(8,128)S(1)}, u32[]{:S(2)}, u32[]{:S(2)}) %collective-permute-start.2) | collective-permute-done | bytes 262176 | tf_op jit(solution)/shard_map/ppermute | solution.py:298
  70.6 0.7 collective-permute-start.15
  71.4 0.8 collective-permute-start.17
  72.2 8.5 %collective-permute-start.16 = (f32[128,512]{1,0:T(8,128)S(1)}, f32[128,512]{1,0:T(8,128)S(1)}, u32[]{:S(2)}, u32[]{:S(2)}) collective-permute-start(f32[128,512]{1,0:T(8,128)S(1)} %get-tuple-element.71), channel_id=1, source_target_pairs={{0,4},{4,0},{1,5},{5,1},{2,6},{6,2},{3,7},{7,3},{8,12},{12,8},{9,1... | collective-permute-start | bytes 786440 | tf_op jit(solution)/shard_map/ppermute | solution.py:301
  83.5 2.2 %collective-permute-start.24 = (f32[64,512]{1,0:T(8,128)S(1)}, f32[64,512]{1,0:T(8,128)S(1)}, u32[]{:S(2)}, u32[]{:S(2)}) collective-permute-start(f32[64,512]{1,0:T(8,128)S(1)} %shard_map.101), channel_id=1, source_target_pairs={{0,3},{1,2},{2,1},{3,0},{4,7},{5,6},{6,5},{7,4},{8,11},{9,10},{10,... | collective-permute-start | bytes 393224 | tf_op jit(solution)/shard_map/ppermute | solution.py:298
  85.7 1.3 %collective-permute-start.26 = (f32[64,512]{1,0:T(8,128)S(1)}, f32[64,512]{1,0:T(8,128)S(1)}, u32[]{:S(2)}, u32[]{:S(2)}) collective-permute-start(f32[64,512]{1,0:T(8,128)S(1)} %shard_map.102), channel_id=1, source_target_pairs={{0,2},{1,3},{2,0},{3,1},{4,6},{5,7},{6,4},{7,5},{8,10},{9,11},{10,... | collective-permute-start | bytes 393224 | tf_op jit(solution)/shard_map/ppermute | solution.py:298
  87.0 3.6 %collective-permute-done.18.refs_1_ = f32[8,128]{1,0:T(8,128)S(1)} collective-permute-done((f32[8,128]{1,0:T(8,128)S(1)}, f32[8,128]{1,0:T(8,128)S(1)}, u32[]{:S(2)}, u32[]{:S(2)}) %collective-permute-start.18) | collective-permute-done | bytes 4128 | tf_op jit(solution)/shard_map/ppermute | solution.py:402
  91.1 4.1 %collective-permute-done.19.refs_1_ = f32[8,128]{1,0:T(8,128)S(1)} collective-permute-done((f32[8,128]{1,0:T(8,128)S(1)}, f32[8,128]{1,0:T(8,128)S(1)}, u32[]{:S(2)}, u32[]{:S(2)}) %collective-permute-start.19) | collective-permute-done | bytes 4128 | tf_op jit(solution)/shard_map/ppermute | solution.py:402
  95.4 1.5 %collective-permute-start.29 = (f32[72,512]{1,0:T(8,128)S(1)}, f32[72,512]{1,0:T(8,128)S(1)}, u32[]{:S(2)}, u32[]{:S(2)}) collective-permute-start(f32[72,512]{1,0:T(8,128)S(1)} %shard_map.103.refs_4_), channel_id=1, source_target_pairs={{0,3},{1,2},{2,1},{3,0},{4,7},{5,6},{6,5},{7,4},{8,11},{9,10},{10,... | collective-permute-start | bytes 442376 | tf_op jit(solution)/shard_map/ppermute | solution.py:298
  97.1 1.9 %collective-permute-start.27 = (f32[72,512]{1,0:T(8,128)S(1)}, f32[72,512]{1,0:T(8,128)S(1)}, u32[]{:S(2)}, u32[]{:S(2)}) collective-permute-start(f32[72,512]{1,0:T(8,128)S(1)} %shard_map.103.refs_4_), channel_id=1, source_target_pairs={{0,1},{1,0},{2,3},{3,2},{4,5},{5,4},{6,7},{7,6},{8,9},{9,8},{10,11... | collective-permute-start | bytes 442376 | tf_op jit(solution)/shard_map/ppermute | solution.py:298
  99.0 2.7 %collective-permute-done.29.refs_7_ = f32[72,512]{1,0:T(8,128)S(1)} collective-permute-done((f32[72,512]{1,0:T(8,128)S(1)}, f32[72,512]{1,0:T(8,128)S(1)}, u32[]{:S(2)}, u32[]{:S(2)}) %collective-permute-start.29) | collective-permute-done | bytes 147488 | tf_op jit(solution)/shard_map/ppermute | solution.py:298
  101.6 1.5 %collective-permute-done.28.refs_6_ = f32[72,512]{1,0:T(8,128)S(1)} collective-permute-done((f32[72,512]{1,0:T(8,128)S(1)}, f32[72,512]{1,0:T(8,128)S(1)}, u32[]{:S(2)}, u32[]{:S(2)}) %collective-permute-start.28) | collective-permute-done | bytes 147488 | tf_op jit(solution)/shard_map/ppermute | solution.py:298
  103.6 0.8 shard_map.104.refs_12_
  104.7 1.3 %shard_map.105 = (bf16[512,512]{1,0:T(8,128)(2,1)}, f32[4]{0:T(128)}) custom-call(f32[128,512]{1,0:T(8,128)S(1)} %get-tuple-element.49.refs_2_.refs_0_, f32[128,512]{1,0:T(8,128)S(1)} %collective-permute-done.1.refs_4_.refs_2_.refs_1_, f32[128,512]{1,0:T(8,128)S(1)} %collective-permute-done.2.refs_3_.refs_2_, ...), custom_call_target="tpu_custom_call" | custom-call | flops 268435456 | bytes 1048576 | tf_op jit(solution)/shard_map/pallas_call | solution.py:36
  (80 shorter events, 10.3 us)
Async XLA Ops:
  5.6 7.4 %collective-permute-start.4 = (f32[512,512]{1,0:T(8,128)S(1)}, f32[512,512]{1,0:T(8,128)S(1)}, u32[]{:S(2)}, u32[]{:S(2)}) collective-permute-start(f32[512,512]{1,0:T(8,128)S(1)} %shard_map.78.refs_4_), channel_id=1, source_target_pairs={{0,4},{4,0},{1,5},{5,1},{2,6},{6,2},{3,7},{7,3},{8,12},{12,8},{9,1... | collective-permute-start | bytes 3145736 | tf_op jit(solution)/shard_map/ppermute | solution.py:301
  6.1 2.8 %collective-permute-start = (f32[128,512]{1,0:T(8,128)}, f32[128,512]{1,0:T(8,128)S(1)}, u32[]{:S(2)}, u32[]{:S(2)}) collective-permute-start(f32[128,512]{1,0:T(8,128)} %get-tuple-element.46.refs_1_.refs_0_), channel_id=1, source_target_pairs={{0,4},{4,0},{1,5},{5,1},{2,6},{6,2},{3,7},{7,3},{8,12},{12,8},{9,1... | collective-permute-start | bytes 786440 | tf_op jit(solution)/shard_map/ppermute | solution.py:301
  10.3 7.0 %collective-permute-start.5 = (f32[128,512]{1,0:T(8,128)S(1)}, f32[128,512]{1,0:T(8,128)S(1)}, u32[]{:S(2)}, u32[]{:S(2)}) collective-permute-start(f32[128,512]{1,0:T(8,128)S(1)} %get-tuple-element.48.refs_2_.refs_3_), channel_id=1, source_target_pairs={{0,1},{1,0},{2,3},{3,2},{4,6},{5,7},{6,4},{7,5},{8,9},{9,8},{10,11... | collective-permute-start | bytes 786440 | tf_op jit(solution)/shard_map/ppermute | solution.py:307
  13.5 10.2 %collective-permute-start.7 = (f32[128,1024]{1,0:T(8,128)S(1)}, f32[128,1024]{1,0:T(8,128)S(1)}, u32[]{:S(2)}, u32[]{:S(2)}) collective-permute-start(f32[128,1024]{1,0:T(8,128)S(1)} %get-tuple-element.57.refs_2_.refs_3_), channel_id=1, source_target_pairs={{0,8},{28,20},{1,9},{29,21},{2,10},{30,22},{3,11},{31,23}} | collective-permute-start | bytes 1572872 | tf_op jit(solution)/shard_map/ppermute | solution.py:374
  23.7 15.1 %collective-permute-start.8 = (f32[128,1024]{1,0:T(8,128)S(1)}, f32[128,1024]{1,0:T(8,128)S(1)}, u32[]{:S(2)}, u32[]{:S(2)}) collective-permute-start(f32[128,1024]{1,0:T(8,128)S(1)} %shard_map.84), channel_id=1, source_target_pairs={{0,8},{28,20},{8,16},{20,12},{1,9},{29,21},{9,17},{21,13},{2,10},{... | collective-permute-start | bytes 1572872 | tf_op jit(solution)/shard_map/ppermute | solution.py:374
  28.3 10.0 %collective-permute-start.9 = (f32[128,512]{1,0:T(8,128)S(1)}, f32[128,512]{1,0:T(8,128)S(1)}, u32[]{:S(2)}, u32[]{:S(2)}) collective-permute-start(f32[128,512]{1,0:T(8,128)S(1)} %get-tuple-element.48.refs_2_.refs_3_), channel_id=1, source_target_pairs={{0,3},{1,2},{2,1},{3,0},{4,7},{5,6},{6,5},{7,4},{8,11},{9,10},{10,... | collective-permute-start | bytes 786440 | tf_op jit(solution)/shard_map/ppermute | solution.py:298
  38.8 8.0 %collective-permute-start.10 = (f32[128,1024]{1,0:T(8,128)S(1)}, f32[128,1024]{1,0:T(8,128)S(1)}, u32[]{:S(2)}, u32[]{:S(2)}) collective-permute-start(f32[128,1024]{1,0:T(8,128)S(1)} %shard_map.86), channel_id=1, source_target_pairs={{0,8},{28,20},{8,16},{20,12},{16,24},{12,4},{1,9},{29,21},{9,17},{... | collective-permute-start | bytes 1572872 | tf_op jit(solution)/shard_map/ppermute | solution.py:374
  40.3 6.4 %collective-permute-start.1 = (f32[128,512]{1,0:T(8,128)S(1)}, f32[128,512]{1,0:T(8,128)S(1)}, u32[]{:S(2)}, u32[]{:S(2)}) collective-permute-start(f32[128,512]{1,0:T(8,128)S(1)} %get-tuple-element.50), channel_id=1, source_target_pairs={{0,1},{1,0},{2,3},{3,2},{4,5},{5,4},{6,7},{7,6},{8,9},{9,8},{10,11... | collective-permute-start | bytes 786440 | tf_op jit(solution)/shard_map/ppermute | solution.py:298
  46.9 14.2 %collective-permute-start.11 = (f32[128,1024]{1,0:T(8,128)S(1)}, f32[128,1024]{1,0:T(8,128)S(1)}, u32[]{:S(2)}, u32[]{:S(2)}) collective-permute-start(f32[128,1024]{1,0:T(8,128)S(1)} %shard_map.87.refs_3_), channel_id=1, source_target_pairs={{0,8},{28,20},{8,16},{20,12},{16,24},{12,4},{1,9},{29,21},{9,17},{... | collective-permute-start | bytes 1572872 | tf_op jit(solution)/shard_map/ppermute | solution.py:374
  51.4 1.6 %collective-permute-start.12 = (f32[128,512]{1,0:T(8,128)S(1)}, f32[128,512]{1,0:T(8,128)S(1)}, u32[]{:S(2)}, u32[]{:S(2)}) collective-permute-start(f32[128,512]{1,0:T(8,128)S(1)} %get-tuple-element.63), channel_id=1, source_target_pairs={{0,4},{4,0},{1,5},{5,1},{2,6},{6,2},{3,7},{7,3},{8,12},{12,8},{9,1... | collective-permute-start | bytes 786440 | tf_op jit(solution)/shard_map/ppermute | solution.py:301
  51.4 9.6 %collective-permute-start.3 = (f32[128,512]{1,0:T(8,128)S(1)}, f32[128,512]{1,0:T(8,128)S(1)}, u32[]{:S(2)}, u32[]{:S(2)}) collective-permute-start(f32[128,512]{1,0:T(8,128)S(1)} %get-tuple-element.52), channel_id=1, source_target_pairs={{0,3},{1,2},{2,1},{3,0},{4,7},{5,6},{6,5},{7,4},{8,11},{9,10},{10,... | collective-permute-start | bytes 786440 | tf_op jit(solution)/shard_map/ppermute | solution.py:298
  61.1 9.6 %collective-permute-start.13 = (f32[128,1024]{1,0:T(8,128)S(1)}, f32[128,1024]{1,0:T(8,128)S(1)}, u32[]{:S(2)}, u32[]{:S(2)}) collective-permute-start(f32[128,1024]{1,0:T(8,128)S(1)} %shard_map.90.refs_3_), channel_id=1, source_target_pairs={{8,16},{20,12},{16,24},{12,4},{9,17},{21,13},{17,25},{13,5},{10,18... | collective-permute-start | bytes 1572872 | tf_op jit(solution)/shard_map/ppermute | solution.py:374
  61.8 1.6 %collective-permute-start.14 = (f32[128,512]{1,0:T(8,128)S(1)}, f32[128,512]{1,0:T(8,128)S(1)}, u32[]{:S(2)}, u32[]{:S(2)}) collective-permute-start(f32[128,512]{1,0:T(8,128)S(1)} %get-tuple-element.67), channel_id=1, source_target_pairs={{0,4},{4,0},{1,5},{5,1},{2,6},{6,2},{3,7},{7,3},{8,12},{12,8},{9,1... | collective-permute-start | bytes 786440 | tf_op jit(solution)/shard_map/ppermute | solution.py:301
  62.2 8.5 %collective-permute-start.2 = (f32[128,512]{1,0:T(8,128)S(1)}, f32[128,512]{1,0:T(8,128)S(1)}, u32[]{:S(2)}, u32[]{:S(2)}) collective-permute-start(f32[128,512]{1,0:T(8,128)S(1)} %get-tuple-element.51), channel_id=1, source_target_pairs={{0,2},{1,3},{2,0},{3,1},{4,6},{5,7},{6,4},{7,5},{8,10},{9,11},{10,... | collective-permute-start | bytes 786440 | tf_op jit(solution)/shard_map/ppermute | solution.py:298
  70.6 1.5 %collective-permute-start.15 = (f32[128,1024]{1,0:T(8,128)S(1)}, f32[128,1024]{1,0:T(8,128)S(1)}, u32[]{:S(2)}, u32[]{:S(2)}) collective-permute-start(f32[128,1024]{1,0:T(8,128)S(1)} %shard_map.93.refs_3_), channel_id=1, source_target_pairs={{16,24},{12,4},{17,25},{13,5},{18,26},{14,6},{19,27},{15,7}} | collective-permute-start | bytes 1572872 | tf_op jit(solution)/shard_map/ppermute | solution.py:374
  71.4 9.4 %collective-permute-start.17 = (f32[128,512]{1,0:T(8,128)S(1)}, f32[128,512]{1,0:T(8,128)S(1)}, u32[]{:S(2)}, u32[]{:S(2)}) collective-permute-start(f32[128,512]{1,0:T(8,128)S(1)} %get-tuple-element.74), channel_id=1, source_target_pairs={{0,4},{4,0},{1,5},{5,1},{2,6},{6,2},{3,7},{7,3},{8,12},{12,8},{9,1... | collective-permute-start | bytes 786440 | tf_op jit(solution)/shard_map/ppermute | solution.py:301
  72.2 9.8 %collective-permute-start.16 = (f32[128,512]{1,0:T(8,128)S(1)}, f32[128,512]{1,0:T(8,128)S(1)}, u32[]{:S(2)}, u32[]{:S(2)}) collective-permute-start(f32[128,512]{1,0:T(8,128)S(1)} %get-tuple-element.71), channel_id=1, source_target_pairs={{0,4},{4,0},{1,5},{5,1},{2,6},{6,2},{3,7},{7,3},{8,12},{12,8},{9,1... | collective-permute-start | bytes 786440 | tf_op jit(solution)/shard_map/ppermute | solution.py:301
  80.8 2.5 %collective-permute-start.21 = (f32[64,512]{1,0:T(8,128)S(1)}, f32[64,512]{1,0:T(8,128)S(1)}, u32[]{:S(2)}, u32[]{:S(2)}) collective-permute-start(f32[64,512]{1,0:T(8,128)S(1)} %get-tuple-element.81), channel_id=1, source_target_pairs={{0,4},{4,0},{1,5},{5,1},{2,6},{6,2},{3,7},{7,3},{8,12},{12,8},{9,1... | collective-permute-start | bytes 393224 | tf_op jit(solution)/shard_map/ppermute | solution.py:301
  81.5 1.9 %collective-permute-start.23 = (f32[64,512]{1,0:T(8,128)S(1)}, f32[64,512]{1,0:T(8,128)S(1)}, u32[]{:S(2)}, u32[]{:S(2)}) collective-permute-start(f32[64,512]{1,0:T(8,128)S(1)} %get-tuple-element.83), channel_id=1, source_target_pairs={{0,4},{4,0},{1,5},{5,1},{2,6},{6,2},{3,7},{7,3},{8,12},{12,8},{9,1... | collective-permute-start | bytes 393224 | tf_op jit(solution)/shard_map/ppermute | solution.py:301
  82.7 3.0 %collective-permute-start.25 = (f32[64,512]{1,0:T(8,128)S(1)}, f32[64,512]{1,0:T(8,128)S(1)}, u32[]{:S(2)}, u32[]{:S(2)}) collective-permute-start(f32[64,512]{1,0:T(8,128)S(1)} %get-tuple-element.85), channel_id=1, source_target_pairs={{0,4},{4,0},{1,5},{5,1},{2,6},{6,2},{3,7},{7,3},{8,12},{12,8},{9,1... | collective-permute-start | bytes 393224 | tf_op jit(solution)/shard_map/ppermute | solution.py:301
  83.0 12.1 %collective-permute-start.20 = (f32[64,512]{1,0:T(8,128)S(1)}, f32[64,512]{1,0:T(8,128)S(1)}, u32[]{:S(2)}, u32[]{:S(2)}) collective-permute-start(f32[64,512]{1,0:T(8,128)S(1)} %get-tuple-element.79), channel_id=1, source_target_pairs={{0,4},{4,0},{1,5},{5,1},{2,6},{6,2},{3,7},{7,3},{8,12},{12,8},{9,1... | collective-permute-start | bytes 393224 | tf_op jit(solution)/shard_map/ppermute | solution.py:301
  83.3 11.9 %collective-permute-start.22 = (f32[64,512]{1,0:T(8,128)S(1)}, f32[64,512]{1,0:T(8,128)S(1)}, u32[]{:S(2)}, u32[]{:S(2)}) collective-permute-start(f32[64,512]{1,0:T(8,128)S(1)} %shard_map.100), channel_id=1, source_target_pairs={{0,1},{1,0},{2,3},{3,2},{4,5},{5,4},{6,7},{7,6},{8,9},{9,8},{10,11... | collective-permute-start | bytes 393224 | tf_op jit(solution)/shard_map/ppermute | solution.py:298
  83.5 11.7 %collective-permute-start.24 = (f32[64,512]{1,0:T(8,128)S(1)}, f32[64,512]{1,0:T(8,128)S(1)}, u32[]{:S(2)}, u32[]{:S(2)}) collective-permute-start(f32[64,512]{1,0:T(8,128)S(1)} %shard_map.101), channel_id=1, source_target_pairs={{0,3},{1,2},{2,1},{3,0},{4,7},{5,6},{6,5},{7,4},{8,11},{9,10},{10,... | collective-permute-start | bytes 393224 | tf_op jit(solution)/shard_map/ppermute | solution.py:298
  85.7 9.5 %collective-permute-start.26 = (f32[64,512]{1,0:T(8,128)S(1)}, f32[64,512]{1,0:T(8,128)S(1)}, u32[]{:S(2)}, u32[]{:S(2)}) collective-permute-start(f32[64,512]{1,0:T(8,128)S(1)} %shard_map.102), channel_id=1, source_target_pairs={{0,2},{1,3},{2,0},{3,1},{4,6},{5,7},{6,4},{7,5},{8,10},{9,11},{10,... | collective-permute-start | bytes 393224 | tf_op jit(solution)/shard_map/ppermute | solution.py:298
  87.0 3.6 %collective-permute-start.18 = (f32[8,128]{1,0:T(8,128)S(1)}, f32[8,128]{1,0:T(8,128)S(1)}, u32[]{:S(2)}, u32[]{:S(2)}) collective-permute-start(f32[8,128]{1,0:T(8,128)S(1)} %get-tuple-element.77.refs_0_), channel_id=1, source_target_pairs={{0,8},{8,0},{16,24},{24,16},{1,9},{9,1},{17,25},{25,17},{2,10},{10... | collective-permute-start | bytes 12296 | tf_op jit(solution)/shard_map/ppermute | solution.py:402
  90.6 4.5 %collective-permute-start.19 = (f32[8,128]{1,0:T(8,128)S(1)}, f32[8,128]{1,0:T(8,128)S(1)}, u32[]{:S(2)}, u32[]{:S(2)}) collective-permute-start(f32[8,128]{1,0:T(8,128)S(1)} %shard_map.98.refs_0_), channel_id=1, source_target_pairs={{0,16},{8,24},{16,0},{24,8},{1,17},{9,25},{17,1},{25,9},{2,18},{10... | collective-permute-start | bytes 12296 | tf_op jit(solution)/shard_map/ppermute | solution.py:402
  95.4 6.2 %collective-permute-start.29 = (f32[72,512]{1,0:T(8,128)S(1)}, f32[72,512]{1,0:T(8,128)S(1)}, u32[]{:S(2)}, u32[]{:S(2)}) collective-permute-start(f32[72,512]{1,0:T(8,128)S(1)} %shard_map.103.refs_4_), channel_id=1, source_target_pairs={{0,3},{1,2},{2,1},{3,0},{4,7},{5,6},{6,5},{7,4},{8,11},{9,10},{10,... | collective-permute-start | bytes 442376 | tf_op jit(solution)/shard_map/ppermute | solution.py:298
  96.9 6.2 %collective-permute-start.28 = (f32[72,512]{1,0:T(8,128)S(1)}, f32[72,512]{1,0:T(8,128)S(1)}, u32[]{:S(2)}, u32[]{:S(2)}) collective-permute-start(f32[72,512]{1,0:T(8,128)S(1)} %shard_map.103.refs_4_), channel_id=1, source_target_pairs={{0,2},{1,3},{2,0},{3,1},{4,6},{5,7},{6,4},{7,5},{8,10},{9,11},{10,... | collective-permute-start | bytes 442376 | tf_op jit(solution)/shard_map/ppermute | solution.py:298
  97.1 6.1 %collective-permute-start.27 = (f32[72,512]{1,0:T(8,128)S(1)}, f32[72,512]{1,0:T(8,128)S(1)}, u32[]{:S(2)}, u32[]{:S(2)}) collective-permute-start(f32[72,512]{1,0:T(8,128)S(1)} %shard_map.103.refs_4_), channel_id=1, source_target_pairs={{0,1},{1,0},{2,3},{3,2},{4,5},{5,4},{6,7},{7,6},{8,9},{9,8},{10,11... | collective-permute-start | bytes 442376 | tf_op jit(solution)/shard_map/ppermute | solution.py:298
  99.0 5.4 %collective-permute-start.30 = (f32[72,512]{1,0:T(8,128)S(1)}, f32[72,512]{1,0:T(8,128)S(1)}, u32[]{:S(2)}, u32[]{:S(2)}) collective-permute-start(f32[72,512]{1,0:T(8,128)S(1)} %shard_map.103.refs_4_), channel_id=1, source_target_pairs={{0,4},{4,0},{1,5},{5,1},{2,6},{6,2},{3,7},{7,3},{8,12},{12,8},{9,1... | collective-permute-start | bytes 442376 | tf_op jit(solution)/shard_map/ppermute | solution.py:301
  101.6 2.8 %collective-permute-start.33 = (f32[72,512]{1,0:T(8,128)S(1)}, f32[72,512]{1,0:T(8,128)S(1)}, u32[]{:S(2)}, u32[]{:S(2)}) collective-permute-start(f32[72,512]{1,0:T(8,128)S(1)} %collective-permute-done.29.refs_7_), channel_id=1, source_target_pairs={{0,4},{4,0},{1,5},{5,1},{2,6},{6,2},{3,7},{7,3},{8,12},{12,8},{9,1... | collective-permute-start | bytes 442376 | tf_op jit(solution)/shard_map/ppermute | solution.py:301
  103.1 1.6 %collective-permute-start.31 = (f32[72,512]{1,0:T(8,128)S(1)}, f32[72,512]{1,0:T(8,128)S(1)}, u32[]{:S(2)}, u32[]{:S(2)}) collective-permute-start(f32[72,512]{1,0:T(8,128)S(1)} %collective-permute-done.27.refs_5_), channel_id=1, source_target_pairs={{0,4},{4,0},{1,5},{5,1},{2,6},{6,2},{3,7},{7,3},{8,12},{12,8},{9,1... | collective-permute-start | bytes 442376 | tf_op jit(solution)/shard_map/ppermute | solution.py:301
  (9 other events, 65.7 us)

commit v4 on v3

--- a/solution.py
+++ b/solution.py
@@ -27,7 +27,7 @@
     return jax.ShapeDtypeStruct(shape, jnp.bfloat16)
 
 
-def call(kernel, outs, arrays, after=(), specs=None, out_specs=None, scratch=(), flops=0, mib=12):
+def call(kernel, outs, arrays, after=(), specs=None, out_specs=None, scratch=()):
     skip = slice(len(arrays), len(arrays) + len(after))
 
     def run(*refs):
@@ -39,9 +39,13 @@
         in_specs=list(specs or [VMEM] * len(arrays)) + [ANY] * len(after),
         out_specs=out_specs or [VMEM] * len(outs),
         scratch_shapes=list(scratch),
-        compiler_params=pltpu.CompilerParams(vmem_limit_bytes=mib * 1024 * 1024),
-        cost_estimate=pl.CostEstimate(flops=flops, bytes_accessed=1 << 20, transcendentals=0),
+        compiler_params=pltpu.CompilerParams(vmem_limit_bytes=12 * 1024 * 1024),
+        cost_estimate=pl.CostEstimate(flops=0, bytes_accessed=1 << 10, transcendentals=0),
     )(*arrays, *after)
+
+
+def in_hbm(array):
+    return pltpu.with_memory_space_constraint(array, pltpu.HBM)
 
 
 def total_of(terms):
@@ -71,35 +75,41 @@
 
 
 def pre_kernel(
-    resid, dictionary, bounds, partial_out, dict_out, table_out, resid_v, dict_v, sems
+    resid, dictionary, partial_out, dict_out, resid_v, dict_v, sems
 ):
     pieces, lats, width = dict_v.shape
-    here = pl.ds(pl.multiple_of(lax.axis_index("tok") * width, width), width)
-    copies = [pltpu.make_async_copy(resid, resid_v, sems.at[pieces])]
-    for i in range(pieces):
+    ahead = 3
+
+    def copies(i):
         cols = pl.ds(i * width, width)
-        copies.append(pltpu.make_async_copy(dictionary.at[:, cols], dict_v.at[i], sems.at[i]))
-    copies.append(pltpu.make_async_copy(dictionary.at[:, here], dict_out, sems.at[pieces + 1]))
-    for copy in copies:
-        copy.start()
-    level_table(bounds, lats // BLOCK, table_out)
-    copies[0].wait()
+        return (
+            pltpu.make_async_copy(resid.at[:, cols], resid_v.at[i], sems.at[0, i]),
+            pltpu.make_async_copy(dictionary.at[:, cols], dict_v.at[i], sems.at[1, i]),
+        )
+
+    for i in range(min(ahead, pieces)):
+        for copy in copies(i):
+            copy.start()
     total = None
     for i in range(pieces):
-        copies[1 + i].wait()
+        for copy in copies(i):
+            copy.wait()
+        if i + ahead < pieces:
+            for copy in copies(i + ahead):
+                copy.start()
         term = lax.dot_general(
-            resid_v[:, i * width : (i + 1) * width],
-            dict_v[i],
-            (((1,), (1,)), ((), ())),
-            preferred_element_type=jnp.float32,
+            resid_v[i], dict_v[i], (((1,), (1,)), ((), ())), preferred_element_type=jnp.float32
         )
         total = term if total is None else total + term
     partial_out[...] = total
-    copies[-1].wait()
-
-
-def widen_kernel(array, out):
+    parts = dict_out.shape[1] // width
+    for i in range(parts):
+        dict_out[:, i * width : (i + 1) * width] = dict_v[lax.axis_index("tok") * parts + i]
+
+
+def widen_kernel(array, bounds, out, table_out):
     out[...] = array[...].astype(jnp.float32)
+    level_table(bounds, array.shape[0] // BLOCK, table_out)
 
 
 def pieces_kernel(resid, bias, bias_out, *outs):
@@ -115,28 +125,34 @@
 
 
 def block_mask(active, lats):
-    first = lax.axis_index("lat") * (lats // BLOCK)
-    ids = first + lax.broadcasted_iota(jnp.int32, (1, lats), 1) // BLOCK
-    hit = None
-    for q in range(active.shape[1]):
-        same = active[:, q : q + 1] == ids
-        hit = same if hit is None else hit | same
-    return hit
-
-
-def activate_kernel(mine, other, bias, active, pre_out, act_out):
+    count = lats // BLOCK
+    ids = lax.axis_index("lat") * count + lax.broadcasted_iota(jnp.int32, (count, 1), 0)
+    hits = total_of([(active[q : q + 1, :] == ids).astype(jnp.float32) for q in range(active.shape[0])])
+    spread = lax.broadcasted_iota(jnp.int32, (count, lats), 1) // BLOCK
+    spread = (spread == lax.broadcasted_iota(jnp.int32, (count, lats), 0)).astype(jnp.bfloat16)
+    return lax.dot_general(
+        hits.astype(jnp.bfloat16),
+        spread,
+        (((0,), (0,)), ((), ())),
+        preferred_element_type=jnp.float32,
+    )
+
+
+def activate_kernel(mine, other, bias, active, pre_out, act_out, mask_out):
     pre = mine[...] + other[...] + bias[...]
     pre_out[...] = pre
     inner = GELU_C * (pre + GELU_A * (pre * pre * pre))
     gelu = 0.5 * pre * (1.0 + jnp.tanh(inner))
-    act_out[...] = jnp.where(block_mask(active[...], pre.shape[1]), gelu, 0.0)
+    mask = block_mask(active[...], pre.shape[1])
+    mask_out[...] = mask
+    act_out[...] = jnp.where(mask > 0.0, gelu, 0.0)
 
 
 def half_of(wid, rows):
     return pl.ds(pl.multiple_of(wid * (rows // 2), rows // 2), rows // 2)
 
 
-def g_pre_kernel(pre_ref, active, loss, *refs):
+def g_pre_kernel(pre_ref, mask, loss, *refs):
     terms, out = refs[:-1], refs[-1]
     mine = half_of(lax.axis_index("wid"), pre_ref.shape[0])
     pre = pre_ref[mine, :]
@@ -144,7 +160,7 @@
     slope = GELU_C * (1.0 + 3.0 * GELU_A * (pre * pre))
     bend = jnp.tanh(inner)
     deriv = 0.5 * (1.0 + bend) + 0.5 * pre * (1.0 - bend * bend) * slope
-    hit = block_mask(active[mine, :], pre.shape[1])
+    hit = mask[mine, :] > 0.0
     rows = pre.shape[0]
     out[:rows, :] = jnp.where(hit, deriv * total_of([t[...] for t in terms]), 0.0)
     out[rows:, :] = jnp.zeros_like(out[rows:, :])
@@ -162,20 +178,17 @@
     return sums
 
 
-def project_kernel(own, other, table, *refs):
-    acts, rows_out, out = refs[:-2], refs[-2], refs[-1]
-    rows = acts[0][...]
-    if len(acts) > 1:
-        rows = jnp.where(lax.axis_index("wid") == 0, rows, acts[1][...])
-    rows = rows.astype(jnp.bfloat16)
-    rows_out[...] = rows
-    width = own.shape[1]
-    for side, dict_ref in enumerate((own, other)):
-        sums = running_parts(rows, dict_ref)
-        count = len(sums)
-        out[:, side * width : (side + 1) * width] = total_of(
-            [table[count + i : count + i + 1, :1] * s for i, s in enumerate(sums)]
-        )
+def round_kernel(*refs):
+    rows = refs[0][...]
+    if len(refs) > 2:
+        rows = jnp.where(lax.axis_index("wid") == 0, rows, refs[1][...])
+    refs[-1][...] = rows.astype(jnp.bfloat16)
+
+
+def project_kernel(act, dictionary, table, out):
+    sums = running_parts(act[...], dictionary)
+    count = len(sums)
+    out[...] = total_of([table[count + i : count + i + 1, :1] * s for i, s in enumerate(sums)])
 
 
 def message_kernel(places, got, *refs):
@@ -189,21 +202,18 @@
 
 
 def choose_kernel(places, *refs):
-    arrived, own_out, hand_out = refs[:-2], refs[-2], refs[-1]
-    width = own_out.shape[1]
+    arrived, out = refs[:-1], refs[-1]
     index = place_in_chain()
 
     @pl.when(index == 0)
     def _():
-        own_out[...] = jnp.zeros_like(own_out)
-        hand_out[...] = jnp.zeros_like(hand_out)
+        out[...] = jnp.zeros_like(out)
 
     for place, ref in zip(places, arrived):
 
         @pl.when(index == place if len(arrived) > 1 else index > 0)
         def _():
-            own_out[...] = ref[:, :width]
-            hand_out[...] = ref[:, width:]
+            out[...] = ref[...]
 
 
 def square_sums(table, shifted):
@@ -292,7 +302,6 @@
     n_lat, n_wid, n_tok = lax.axis_size("lat"), lax.axis_size("wid"), lax.axis_size("tok")
     width = half // n_tok
     count = lats // BLOCK
-    work = 2 * rows * lats * width
 
     def across(array, q):
         return lax.ppermute(array, "tok", [(t, t ^ q) for t in range(n_tok)])
@@ -309,25 +318,29 @@
         other = swap(near)
         return [(array,), (near, other), (other, near), (far,)]
 
-    partial, dict_here, table = call(
+    partial, dict_here = call(
         pre_kernel,
-        [f32(rows, lats), bf16(lats, width), f32((2 + LEVELS) * count, BLOCK)],
-        (resid, dictionary, level_bounds.reshape(1, LEVELS)),
-        specs=[HBM, HBM, VMEM],
+        [f32(rows, lats), bf16(lats, width)],
+        (in_hbm(resid), in_hbm(dictionary)),
+        specs=[HBM, HBM],
         scratch=[
-            pltpu.VMEM((rows, half), jnp.bfloat16),
-            pltpu.VMEM((n_tok, lats, width), jnp.bfloat16),
-            pltpu.SemaphoreType.DMA((n_tok + 2,)),
+            pltpu.VMEM((2 * n_tok, rows, width // 2), jnp.bfloat16),
+            pltpu.VMEM((2 * n_tok, lats, width // 2), jnp.bfloat16),
+            pltpu.SemaphoreType.DMA((2, 2 * n_tok)),
         ],
-        mib=62,
     )
     partial_other = swap(partial)
-    dict_wide = call(widen_kernel, [f32(lats, width)], (dict_here,), after=(partial,))[0]
+    dict_wide, table = call(
+        widen_kernel,
+        [f32(lats, width), f32((2 + LEVELS) * count, BLOCK)],
+        (dict_here, level_bounds.reshape(1, LEVELS)),
+        after=(partial_other,),
+    )
     dict_other = swap(dict_wide)
-    pre, act = call(
+    pre, act, mask = call(
         activate_kernel,
-        [f32(rows, lats)] * 2,
-        (partial, partial_other, enc_bias.reshape(1, lats), active_blocks),
+        [f32(rows, lats)] * 3,
+        (partial, partial_other, enc_bias.reshape(1, lats), active_blocks.T),
         after=(dict_wide,),
     )
     gathered = gather(act)
@@ -340,62 +353,85 @@
     resids = [piece if q == 0 else across(piece, q) for q, piece in enumerate(pieces)]
 
     order = [0, 1, 3, 2] if n_tok == 4 else list(range(n_tok))
-    acts, sums = {}, []
-    for q in order:
-        acts[q], passed = call(
-            project_kernel,
-            [bf16(rows, lats), f32(rows, 2 * width)],
-            (dict_here, dict_other, table, *gathered[q]),
-            flops=2 * work,
-        )
-        sums.append(passed)
-
-    got, sent = [], []
+    steps = n_tok + n_lat - 2
+    places = list(range(1, n_lat))
+    acts, sums, got, sent = {}, ([], []), ([], []), []
     errs, gacts, loss = {}, [], ()
-    for step in range(n_tok + 2 * (n_lat - 1)):
-        if step < n_tok + n_lat - 2:
+    waits = {step: [] for step in range(steps)}
+    for place, q in enumerate(order[1:]):
+        waits[2 + min(place, 1)].append(resids[q])
+    for step in range(steps + 1):
+        for side, dict_ref in enumerate((dict_here, dict_other)):
+            if step == steps:
+                break
+            if step == 0:
+                q = order[0]
+                if side == 0:
+                    acts[q] = call(round_kernel, [bf16(rows, lats)], gathered[q])[0]
+                sums[side].append(
+                    call(
+                        project_kernel,
+                        [f32(rows, width)],
+                        (acts[q], dict_ref, table),
+                        after=sent,
+                    )[0]
+                )
             at = [p for p in range(n_lat - 1) if 0 <= step - p < n_tok]
-            message = sums[0]
+            message = sums[side][0]
             if step:
-                done = step - n_lat
-                after = [errs[order[done]]] if done >= 0 else []
-                if 0 <= step - n_lat + 1 < n_tok - 1:
-                    after.append(resids[order[step - n_lat + 2]])
                 message = call(
                     functools.partial(message_kernel, at),
-                    [f32(rows, 2 * width)],
-                    (got[-1], *[sums[step - p] for p in at]),
-                    after=after,
+                    [f32(rows, width)],
+                    (got[side][-1], *[sums[side][step - p] for p in at]),
+                    after=sent + (waits[step] if side == 0 else []),
                 )[0]
             pairs = []
             for p in at:
                 pairs.append((2 * p, 2 * (p + 1)))
                 pairs.append((2 * (n_lat - 1 - p) + 1, 2 * (n_lat - 2 - p) + 1))
-            got.append(lax.ppermute(message, ("lat", "wid"), pairs))
+            got[side].append(lax.ppermute(message, ("lat", "wid"), pairs))
             sent = [message]
+        if step + 1 < n_tok:
+            q = order[step + 1]
+            acts[q] = call(round_kernel, [bf16(rows, lats)], gathered[q], after=sent)[0]
+            for side, dict_ref in enumerate((dict_here, dict_other)):
+                sums[side].append(
+                    call(
+                        project_kernel, [f32(rows, width)], (acts[q], dict_ref, table)
+                    )[0]
+                )
         c = step - (n_lat - 1)
-        if not 0 <= c < n_tok:
+        if c < 0:
             continue
         q = order[c]
-        places = list(range(1, n_lat))
-        arrived = [got[c + p - 1] for p in places]
-        if n_lat > 4:
-            arrived = [pick(place_in_chain(), dict(zip(places, arrived)))]
-        mine, hand = call(
-            functools.partial(choose_kernel, places), [f32(rows, width)] * 2, arrived, after=sent
-        )
+        ahead = sent + [got[0][step]] if step < steps else []
+        if c:
+            ahead.append(added)
+        if c > 1:
+            ahead.append(gacts[-2])
+        chosen = []
+        for side in (1, 0):
+            arrived = [got[side][c + p - 1] for p in places]
+            if n_lat > 4:
+                arrived = [pick(place_in_chain(), dict(zip(places, arrived)))]
+            chosen.append(
+                call(
+                    functools.partial(choose_kernel, places),
+                    [f32(rows, width)],
+                    arrived,
+                    after=ahead,
+                )[0]
+            )
+        hand, mine = chosen
         errs[q], keep, give, loss_here = call(
             error_kernel,
             [bf16(count, rows, width)] + [f32(rows // 2, lats)] * 2 + [f32(LOSS_ROWS, BLOCK)],
             (acts[q], dict_here, resids[q], bias_here, table, mine, swap(hand), *loss),
-            flops=2 * work,
         )
         loss = (loss_here,)
-        if q == 0:
-            gacts += [keep, swap(give)]
-        else:
-            gacts.append(across(call(add_kernel, [f32(rows // 2, lats)], (keep, swap(give)))[0], q))
-        sent = []
+        waits.setdefault(step + 2, []).append(errs[q])
+        added = call(add_kernel, [f32(rows // 2, lats)], (keep, swap(give)))[0]
+        gacts.append(across(added, q) if q else added)
 
     loss, gap = loss[0], 1
     while gap < n_lat:
@@ -404,7 +440,7 @@
         gap *= 2
 
     g_pre = call(
-        g_pre_kernel, [f32(rows // 2 + LOSS_ROWS, lats)], (pre, active_blocks, loss, *gacts)
+        g_pre_kernel, [f32(rows // 2 + LOSS_ROWS, lats)], (pre, mask, loss, *gacts)
     )[0]
     mine = [across(g_pre, q) if q else g_pre for q in range(n_tok)]
     others = [swap(g) for g in mine]
@@ -412,14 +448,12 @@
         decode_kernel,
         [f32(width, lats)],
         (*[errs[q] for q in order], *[acts[q] for q in order]),
-        flops=n_tok * work,
     )[0]
     grad, losses = call(
         functools.partial(encode_kernel, 1.0 / (rows * n_tok * half * n_wid)),
         [bf16(width, lats), f32(LEVELS)],
         (*resids, *mine, *others, decoded),
         out_specs=[VMEM, SMEM],
-        flops=n_tok * work,
     )
     return (losses, grad)
 

time: 106 us -> 104 us (0.981)
  waiting for transfers between devices: 49.8 us -> 27.8 us
  starting transfers between devices: 41.4 us -> 62.5 us
  local copies, waits for them, and re-layouts: 1.17 us -> 0.02 us
    ppermute x10, waiting for transfers between devices: 32.4 us -> 9.77 us  [across(): return lax.ppermute(array, 'tok', [(t, t ^ q) for t in range(n_tok)])]
    ppermute x6 -> x12, starting transfers between devices: 15.2 us -> 26.9 us  [body(): got[side].append(lax.ppermute(message, ('lat', 'wid'), pairs))]
    ppermute x2, starting transfers between devices: 0.45 us -> 7.33 us  [body(): other = lax.ppermute(loss, 'lat', [(p, p ^ gap) for p in range(n_lat)])]
    ppermute x2, waiting for transfers between devices: 7.66 us -> 3.17 us  [body(): other = lax.ppermute(loss, 'lat', [(p, p ^ gap) for p in range(n_lat)])]
    ppermute x1, waiting for transfers between devices: 0.34 us -> 4.33 us  [gather(): near = lax.ppermute(array, ('wid', 'tok'), pairs)]
    ppermute x10, starting transfers between devices: 11.1 us -> 14 us  [across(): return lax.ppermute(array, 'tok', [(t, t ^ q) for t in range(n_tok)])]
    ppermute x6 -> x12, waiting for transfers between devices: 4.4 us -> 5.85 us  [body(): got[side].append(lax.ppermute(message, ('lat', 'wid'), pairs))]
    unnamed x15 -> x10, local copies, waits for them, and re-layouts: 1.17 us -> 0.02 us
  transfers between devices with their start and end apart: 34 -> 40, of which waited for: 16 -> 15; matrix products, arithmetic and copies ran while one was open for 0% -> 0% of each run, Pallas kernels for 7% -> 6%
where the time goes in v4:
time: 104 us; the launch traced here: 103 us
  starting transfers between devices  62.5 us (60%)
  waiting for transfers between devices  27.8 us (27%)
  Pallas kernels  12 us (12%)
  between operations  1.22 us (1%)
    ppermute x12, starting transfers between devices, body(): got[side].append(lax.ppermute(message, ('lat', 'wid'), pairs))  26.9 us
    ppermute x10, starting transfers between devices, across(): return lax.ppermute(array, 'tok', [(t, t ^ q) for t in range(n_tok)])  14 us
    pallas_call x47, Pallas kernels, call(): pl.pallas_call(run, out_shape=outs, in_specs=list(specs or [VMEM] * len(a...  12 us
    ppermute x15, starting transfers between devices, swap(): return lax.ppermute(array, 'wid', [(w, w ^ 1) for w in range(n_wid)])  11.5 us
    ppermute x10, waiting for transfers between devices, across(): return lax.ppermute(array, 'tok', [(t, t ^ q) for t in range(n_tok)])  9.77 us
    ppermute x2, starting transfers between devices, body(): other = lax.ppermute(loss, 'lat', [(p, p ^ gap) for p in range(n_lat)])  7.33 us
    ppermute x12, waiting for transfers between devices, body(): got[side].append(lax.ppermute(message, ('lat', 'wid'), pairs))  5.85 us
    ppermute x15, waiting for transfers between devices, swap(): return lax.ppermute(array, 'wid', [(w, w ^ 1) for w in range(n_wid)])  4.64 us
  transfers between devices with their start and end apart: 40, of which 15 were waited for; matrix products, arithmetic and copies ran while one was open for 0% of the time, Pallas kernels for 6%

profile of v4, /device:TPU:0, one launch (start us, length us, event | category | flops | bytes accessed | tf_op | source)
XLA Modules:
  0.0 103.5 jit_solution(12034925232686721885)
XLA Ops:
  0.7 3.5 %shard_map.77 = (f32[128,512]{1,0:T(8,128)S(1)}, bf16[512,512]{1,0:T(8,128)(2,1)S(1)}) custom-call(bf16[128,2048]{1,0:T(8,128)(2,1)} %refs_0_.3, bf16[512,2048]{1,0:T(8,128)(2,1)} %refs_1_.1), custom_call_target="tpu_custom_call" | custom-call | bytes 1024 | tf_op jit(solution)/shard_map/pallas_call | solution.py:36
  6.7 2.7 %collective-permute-start.4 = (f32[128,512]{1,0:T(8,128)S(1)}, f32[128,512]{1,0:T(8,128)S(1)}, u32[]{:S(2)}, u32[]{:S(2)}) collective-permute-start(f32[128,512]{1,0:T(8,128)S(1)} %get-tuple-element.35.refs_2_.refs_0_), channel_id=1, source_target_pairs={{0,1},{1,0},{2,3},{3,2},{4,6},{5,7},{6,4},{7,5},{8,9},{9,8},{10,11... | collective-permute-start | bytes 786440 | tf_op jit(solution)/shard_map/ppermute | solution.py:316
  9.4 4.3 %collective-permute-done.4.refs_0_.refs_1_ = f32[128,512]{1,0:T(8,128)S(1)} collective-permute-done((f32[128,512]{1,0:T(8,128)S(1)}, f32[128,512]{1,0:T(8,128)S(1)}, u32[]{:S(2)}, u32[]{:S(2)}) %collective-permute-start.4) | collective-permute-done | bytes 262176 | tf_op jit(solution)/shard_map/ppermute | solution.py:316
  14.1 4.0 %collective-permute-start.8 = (f32[128,512]{1,0:T(8,128)S(1)}, f32[128,512]{1,0:T(8,128)S(1)}, u32[]{:S(2)}, u32[]{:S(2)}) collective-permute-start(f32[128,512]{1,0:T(8,128)S(1)} %shard_map.82.refs_3_.refs_2_), channel_id=1, source_target_pairs={{0,8},{28,20},{1,9},{29,21},{2,10},{30,22},{3,11},{31,23}} | collective-permute-start | bytes 786440 | tf_op jit(solution)/shard_map/ppermute | solution.py:392
  18.1 2.5 %collective-permute-start.10 = (f32[128,512]{1,0:T(8,128)S(1)}, f32[128,512]{1,0:T(8,128)S(1)}, u32[]{:S(2)}, u32[]{:S(2)}) collective-permute-start(f32[128,512]{1,0:T(8,128)S(1)} %get-tuple-element.35.refs_2_.refs_0_), channel_id=1, source_target_pairs={{0,3},{1,2},{2,1},{3,0},{4,7},{5,6},{6,5},{7,4},{8,11},{9,10},{10,... | collective-permute-start | bytes 786440 | tf_op jit(solution)/shard_map/ppermute | solution.py:307
  20.9 1.3 %collective-permute-start.7 = (f32[128,512]{1,0:T(8,128)S(1)}, f32[128,512]{1,0:T(8,128)S(1)}, u32[]{:S(2)}, u32[]{:S(2)}) collective-permute-start(f32[128,512]{1,0:T(8,128)S(1)} %shard_map.83.refs_2_.refs_3_), channel_id=1, source_target_pairs={{0,8},{28,20},{1,9},{29,21},{2,10},{30,22},{3,11},{31,23}} | collective-permute-start | bytes 786440 | tf_op jit(solution)/shard_map/ppermute | solution.py:392
  23.3 3.1 %collective-permute-start.11 = (f32[128,512]{1,0:T(8,128)S(1)}, f32[128,512]{1,0:T(8,128)S(1)}, u32[]{:S(2)}, u32[]{:S(2)}) collective-permute-start(f32[128,512]{1,0:T(8,128)S(1)} %shard_map.87.refs_3_), channel_id=1, source_target_pairs={{0,8},{28,20},{8,16},{20,12},{1,9},{29,21},{9,17},{21,13},{2,10},{... | collective-permute-start | bytes 786440 | tf_op jit(solution)/shard_map/ppermute | solution.py:392
  26.4 1.6 %collective-permute-start.2 = (f32[128,512]{1,0:T(8,128)S(1)}, f32[128,512]{1,0:T(8,128)S(1)}, u32[]{:S(2)}, u32[]{:S(2)}) collective-permute-start(f32[128,512]{1,0:T(8,128)S(1)} %get-tuple-element.38), channel_id=1, source_target_pairs={{0,2},{1,3},{2,0},{3,1},{4,6},{5,7},{6,4},{7,5},{8,10},{9,11},{10,... | collective-permute-start | bytes 786440 | tf_op jit(solution)/shard_map/ppermute | solution.py:307
  28.3 2.2 %collective-permute-start.9 = (f32[128,512]{1,0:T(8,128)S(1)}, f32[128,512]{1,0:T(8,128)S(1)}, u32[]{:S(2)}, u32[]{:S(2)}) collective-permute-start(f32[128,512]{1,0:T(8,128)S(1)} %shard_map.88.refs_1_.refs_4_), channel_id=1, source_target_pairs={{0,8},{28,20},{8,16},{20,12},{1,9},{29,21},{9,17},{21,13},{2,10},{... | collective-permute-start | bytes 786440 | tf_op jit(solution)/shard_map/ppermute | solution.py:392
  30.5 1.2 %collective-permute-start.3 = (f32[128,512]{1,0:T(8,128)S(1)}, f32[128,512]{1,0:T(8,128)S(1)}, u32[]{:S(2)}, u32[]{:S(2)}) collective-permute-start(f32[128,512]{1,0:T(8,128)S(1)} %get-tuple-element.39), channel_id=1, source_target_pairs={{0,3},{1,2},{2,1},{3,0},{4,7},{5,6},{6,5},{7,4},{8,11},{9,10},{10,... | collective-permute-start | bytes 786440 | tf_op jit(solution)/shard_map/ppermute | solution.py:307
  32.1 1.4 %collective-permute-done.1.refs_5_.refs_2_.refs_1_ = f32[128,512]{1,0:T(8,128)S(1)} collective-permute-done((f32[128,512]{1,0:T(8,128)S(1)}, f32[128,512]{1,0:T(8,128)S(1)}, u32[]{:S(2)}, u32[]{:S(2)}) %collective-permute-start.1) | collective-permute-done | bytes 262176 | tf_op jit(solution)/shard_map/ppermute | solution.py:307
  33.5 1.8 %collective-permute-start.12 = (f32[128,512]{1,0:T(8,128)S(1)}, f32[128,512]{1,0:T(8,128)S(1)}, u32[]{:S(2)}, u32[]{:S(2)}) collective-permute-start(f32[128,512]{1,0:T(8,128)S(1)} %shard_map.92.refs_4_), channel_id=1, source_target_pairs={{0,8},{28,20},{8,16},{20,12},{16,24},{12,4},{1,9},{29,21},{9,17},{... | collective-permute-start | bytes 786440 | tf_op jit(solution)/shard_map/ppermute | solution.py:392
  35.6 3.2 %collective-permute-start.14 = (f32[128,512]{1,0:T(8,128)S(1)}, f32[128,512]{1,0:T(8,128)S(1)}, u32[]{:S(2)}, u32[]{:S(2)}) collective-permute-start(f32[128,512]{1,0:T(8,128)S(1)} %shard_map.93.refs_2_.refs_4_), channel_id=1, source_target_pairs={{0,8},{28,20},{8,16},{20,12},{16,24},{12,4},{1,9},{29,21},{9,17},{... | collective-permute-start | bytes 786440 | tf_op jit(solution)/shard_map/ppermute | solution.py:392
  39.3 4.3 %collective-permute-start.13 = (f32[128,512]{1,0:T(8,128)S(1)}, f32[128,512]{1,0:T(8,128)S(1)}, u32[]{:S(2)}, u32[]{:S(2)}) collective-permute-start(f32[128,512]{1,0:T(8,128)S(1)} %shard_map.96.refs_4_), channel_id=1, source_target_pairs={{0,8},{28,20},{8,16},{20,12},{16,24},{12,4},{1,9},{29,21},{9,17},{... | collective-permute-start | bytes 786440 | tf_op jit(solution)/shard_map/ppermute | solution.py:392
  43.9 3.5 %collective-permute-done.13.refs_0_.refs_4_.refs_2_.refs_1_ = f32[128,512]{1,0:T(8,128)S(1)} collective-permute-done((f32[128,512]{1,0:T(8,128)S(1)}, f32[128,512]{1,0:T(8,128)S(1)}, u32[]{:S(2)}, u32[]{:S(2)}) %collective-permute-start.13) | collective-permute-done | bytes 262176 | tf_op jit(solution)/shard_map/ppermute | solution.py:392
  47.5 4.4 %collective-permute-start.16 = (f32[128,512]{1,0:T(8,128)S(1)}, f32[128,512]{1,0:T(8,128)S(1)}, u32[]{:S(2)}, u32[]{:S(2)}) collective-permute-start(f32[128,512]{1,0:T(8,128)S(1)} %shard_map.98.refs_3_), channel_id=1, source_target_pairs={{0,8},{28,20},{8,16},{20,12},{16,24},{12,4},{1,9},{29,21},{9,17},{... | collective-permute-start | bytes 786440 | tf_op jit(solution)/shard_map/ppermute | solution.py:392
  53.5 2.3 %collective-permute-done.16.refs_0_.refs_2_.refs_1_ = f32[128,512]{1,0:T(8,128)S(1)} collective-permute-done((f32[128,512]{1,0:T(8,128)S(1)}, f32[128,512]{1,0:T(8,128)S(1)}, u32[]{:S(2)}, u32[]{:S(2)}) %collective-permute-start.16) | collective-permute-done | bytes 262176 | tf_op jit(solution)/shard_map/ppermute | solution.py:392
  55.9 2.9 %collective-permute-start.21 = (f32[128,512]{1,0:T(8,128)S(1)}, f32[128,512]{1,0:T(8,128)S(1)}, u32[]{:S(2)}, u32[]{:S(2)}) collective-permute-start(f32[128,512]{1,0:T(8,128)S(1)} %shard_map.108), channel_id=1, source_target_pairs={{0,4},{4,0},{1,5},{5,1},{2,6},{6,2},{3,7},{7,3},{8,12},{12,8},{9,1... | collective-permute-start | bytes 786440 | tf_op jit(solution)/shard_map/ppermute | solution.py:310
  60.9 1.3 %collective-permute-start.22 = (f32[64,512]{1,0:T(8,128)S(1)}, f32[64,512]{1,0:T(8,128)S(1)}, u32[]{:S(2)}, u32[]{:S(2)}) collective-permute-start(f32[64,512]{1,0:T(8,128)S(1)} %get-tuple-element.49), channel_id=1, source_target_pairs={{0,4},{4,0},{1,5},{5,1},{2,6},{6,2},{3,7},{7,3},{8,12},{12,8},{9,1... | collective-permute-start | bytes 393224 | tf_op jit(solution)/shard_map/ppermute | solution.py:310
  63.3 5.5 %collective-permute-start.23 = (f32[128,512]{1,0:T(8,128)S(1)}, f32[128,512]{1,0:T(8,128)S(1)}, u32[]{:S(2)}, u32[]{:S(2)}) collective-permute-start(f32[128,512]{1,0:T(8,128)S(1)} %shard_map.112), channel_id=1, source_target_pairs={{0,4},{4,0},{1,5},{5,1},{2,6},{6,2},{3,7},{7,3},{8,12},{12,8},{9,1... | collective-permute-start | bytes 786440 | tf_op jit(solution)/shard_map/ppermute | solution.py:310
  71.1 1.5 %collective-permute-start.25 = (f32[64,512]{1,0:T(8,128)S(1)}, f32[64,512]{1,0:T(8,128)S(1)}, u32[]{:S(2)}, u32[]{:S(2)}) collective-permute-start(f32[64,512]{1,0:T(8,128)S(1)} %shard_map.110.refs_5_), channel_id=1, source_target_pairs={{0,1},{1,0},{2,3},{3,2},{4,5},{5,4},{6,7},{7,6},{8,9},{9,8},{10,11... | collective-permute-start | bytes 393224 | tf_op jit(solution)/shard_map/ppermute | solution.py:307
  72.6 4.0 %collective-permute-done.25.refs_4_ = f32[64,512]{1,0:T(8,128)S(1)} collective-permute-done((f32[64,512]{1,0:T(8,128)S(1)}, f32[64,512]{1,0:T(8,128)S(1)}, u32[]{:S(2)}, u32[]{:S(2)}) %collective-permute-start.25) | collective-permute-done | bytes 131104 | tf_op jit(solution)/shard_map/ppermute | solution.py:307
  76.8 1.5 %collective-permute-done.27.refs_6_ = f32[128,512]{1,0:T(8,128)S(1)} collective-permute-done((f32[128,512]{1,0:T(8,128)S(1)}, f32[128,512]{1,0:T(8,128)S(1)}, u32[]{:S(2)}, u32[]{:S(2)}) %collective-permute-start.27) | collective-permute-done | bytes 262176 | tf_op jit(solution)/shard_map/ppermute | solution.py:310
  79.1 1.9 %collective-permute-start.30 = (f32[64,512]{1,0:T(8,128)S(1)}, f32[64,512]{1,0:T(8,128)S(1)}, u32[]{:S(2)}, u32[]{:S(2)}) collective-permute-start(f32[64,512]{1,0:T(8,128)S(1)} %shard_map.114.refs_3_), channel_id=1, source_target_pairs={{0,3},{1,2},{2,1},{3,0},{4,7},{5,6},{6,5},{7,4},{8,11},{9,10},{10,... | collective-permute-start | bytes 393224 | tf_op jit(solution)/shard_map/ppermute | solution.py:307
  82.2 2.2 %collective-permute-start.28 = (f32[8,128]{1,0:T(8,128)S(1)}, f32[8,128]{1,0:T(8,128)S(1)}, u32[]{:S(2)}, u32[]{:S(2)}) collective-permute-start(f32[8,128]{1,0:T(8,128)S(1)} %get-tuple-element.54.refs_0_), channel_id=1, source_target_pairs={{0,8},{8,0},{16,24},{24,16},{1,9},{9,1},{17,25},{25,17},{2,10},{10... | collective-permute-start | bytes 12296 | tf_op jit(solution)/shard_map/ppermute | solution.py:438
  84.4 1.6 %collective-permute-done.28.refs_1_ = f32[8,128]{1,0:T(8,128)S(1)} collective-permute-done((f32[8,128]{1,0:T(8,128)S(1)}, f32[8,128]{1,0:T(8,128)S(1)}, u32[]{:S(2)}, u32[]{:S(2)}) %collective-permute-start.28) | collective-permute-done | bytes 4128 | tf_op jit(solution)/shard_map/ppermute | solution.py:438
  86.0 5.2 %collective-permute-start.29 = (f32[8,128]{1,0:T(8,128)S(1)}, f32[8,128]{1,0:T(8,128)S(1)}, u32[]{:S(2)}, u32[]{:S(2)}) collective-permute-start(f32[8,128]{1,0:T(8,128)S(1)} %shard_map.118.refs_0_), channel_id=1, source_target_pairs={{0,16},{8,24},{16,0},{24,8},{1,17},{9,25},{17,1},{25,9},{2,18},{10... | collective-permute-start | bytes 12296 | tf_op jit(solution)/shard_map/ppermute | solution.py:438
  91.1 1.6 %collective-permute-done.29.refs_1_ = f32[8,128]{1,0:T(8,128)S(1)} collective-permute-done((f32[8,128]{1,0:T(8,128)S(1)}, f32[8,128]{1,0:T(8,128)S(1)}, u32[]{:S(2)}, u32[]{:S(2)}) %collective-permute-start.29) | collective-permute-done | bytes 4128 | tf_op jit(solution)/shard_map/ppermute | solution.py:438
  94.7 1.7 %collective-permute-start.35 = (f32[72,512]{1,0:T(8,128)S(1)}, f32[72,512]{1,0:T(8,128)S(1)}, u32[]{:S(2)}, u32[]{:S(2)}) collective-permute-start(f32[72,512]{1,0:T(8,128)S(1)} %shard_map.121.refs_4_), channel_id=1, source_target_pairs={{0,3},{1,2},{2,1},{3,0},{4,7},{5,6},{6,5},{7,4},{8,11},{9,10},{10,... | collective-permute-start | bytes 442376 | tf_op jit(solution)/shard_map/ppermute | solution.py:307
  96.4 1.9 %collective-permute-done.33.refs_5_ = f32[72,512]{1,0:T(8,128)S(1)} collective-permute-done((f32[72,512]{1,0:T(8,128)S(1)}, f32[72,512]{1,0:T(8,128)S(1)}, u32[]{:S(2)}, u32[]{:S(2)}) %collective-permute-start.33) | collective-permute-done | bytes 147488 | tf_op jit(solution)/shard_map/ppermute | solution.py:307
  99.2 1.6 %collective-permute-done.35.refs_7_ = f32[72,512]{1,0:T(8,128)S(1)} collective-permute-done((f32[72,512]{1,0:T(8,128)S(1)}, f32[72,512]{1,0:T(8,128)S(1)}, u32[]{:S(2)}, u32[]{:S(2)}) %collective-permute-start.35) | collective-permute-done | bytes 147488 | tf_op jit(solution)/shard_map/ppermute | solution.py:307
  102.2 1.3 %shard_map.123 = (bf16[512,512]{1,0:T(8,128)(2,1)}, f32[4]{0:T(128)}) custom-call(f32[128,512]{1,0:T(8,128)S(1)} %get-tuple-element.36.refs_2_.refs_0_, f32[128,512]{1,0:T(8,128)S(1)} %collective-permute-done.1.refs_5_.refs_2_.refs_1_, f32[128,512]{1,0:T(8,128)S(1)} %collective-permute-done.2.refs_6_.refs_2_, ...), custom_call_target="tpu_custom_call" | custom-call | bytes 1024 | tf_op jit(solution)/shard_map/pallas_call | solution.py:36
  (105 shorter events, 19.3 us)
Async XLA Ops:
  6.0 14.6 %collective-permute-start.6 = (f32[512,512]{1,0:T(8,128)S(1)}, f32[512,512]{1,0:T(8,128)S(1)}, u32[]{:S(2)}, u32[]{:S(2)}) collective-permute-start(f32[512,512]{1,0:T(8,128)S(1)} %get-tuple-element.34.refs_4_), channel_id=1, source_target_pairs={{0,4},{4,0},{1,5},{5,1},{2,6},{6,2},{3,7},{7,3},{8,12},{12,8},{9,1... | collective-permute-start | bytes 3145736 | tf_op jit(solution)/shard_map/ppermute | solution.py:310
  6.7 7.0 %collective-permute-start.4 = (f32[128,512]{1,0:T(8,128)S(1)}, f32[128,512]{1,0:T(8,128)S(1)}, u32[]{:S(2)}, u32[]{:S(2)}) collective-permute-start(f32[128,512]{1,0:T(8,128)S(1)} %get-tuple-element.35.refs_2_.refs_0_), channel_id=1, source_target_pairs={{0,1},{1,0},{2,3},{3,2},{4,6},{5,7},{6,4},{7,5},{8,9},{9,8},{10,11... | collective-permute-start | bytes 786440 | tf_op jit(solution)/shard_map/ppermute | solution.py:316
  13.8 9.2 %collective-permute-start.5 = (f32[128,512]{1,0:T(8,128)S(1)}, f32[128,512]{1,0:T(8,128)S(1)}, u32[]{:S(2)}, u32[]{:S(2)}) collective-permute-start(f32[128,512]{1,0:T(8,128)S(1)} %collective-permute-done.4.refs_0_.refs_1_), channel_id=1, source_target_pairs={{0,4},{4,0},{1,5},{5,1},{2,6},{6,2},{3,7},{7,3},{8,12},{12,8},{9,1... | collective-permute-start | bytes 786440 | tf_op jit(solution)/shard_map/ppermute | solution.py:310
  14.1 9.2 %collective-permute-start.8 = (f32[128,512]{1,0:T(8,128)S(1)}, f32[128,512]{1,0:T(8,128)S(1)}, u32[]{:S(2)}, u32[]{:S(2)}) collective-permute-start(f32[128,512]{1,0:T(8,128)S(1)} %shard_map.82.refs_3_.refs_2_), channel_id=1, source_target_pairs={{0,8},{28,20},{1,9},{29,21},{2,10},{30,22},{3,11},{31,23}} | collective-permute-start | bytes 786440 | tf_op jit(solution)/shard_map/ppermute | solution.py:392
  18.1 12.4 %collective-permute-start.10 = (f32[128,512]{1,0:T(8,128)S(1)}, f32[128,512]{1,0:T(8,128)S(1)}, u32[]{:S(2)}, u32[]{:S(2)}) collective-permute-start(f32[128,512]{1,0:T(8,128)S(1)} %get-tuple-element.35.refs_2_.refs_0_), channel_id=1, source_target_pairs={{0,3},{1,2},{2,1},{3,0},{4,7},{5,6},{6,5},{7,4},{8,11},{9,10},{10,... | collective-permute-start | bytes 786440 | tf_op jit(solution)/shard_map/ppermute | solution.py:307
  20.9 7.4 %collective-permute-start.7 = (f32[128,512]{1,0:T(8,128)S(1)}, f32[128,512]{1,0:T(8,128)S(1)}, u32[]{:S(2)}, u32[]{:S(2)}) collective-permute-start(f32[128,512]{1,0:T(8,128)S(1)} %shard_map.83.refs_2_.refs_3_), channel_id=1, source_target_pairs={{0,8},{28,20},{1,9},{29,21},{2,10},{30,22},{3,11},{31,23}} | collective-permute-start | bytes 786440 | tf_op jit(solution)/shard_map/ppermute | solution.py:392
  22.3 11.1 %collective-permute-start.1 = (f32[128,512]{1,0:T(8,128)S(1)}, f32[128,512]{1,0:T(8,128)S(1)}, u32[]{:S(2)}, u32[]{:S(2)}) collective-permute-start(f32[128,512]{1,0:T(8,128)S(1)} %get-tuple-element.37), channel_id=1, source_target_pairs={{0,1},{1,0},{2,3},{3,2},{4,5},{5,4},{6,7},{7,6},{8,9},{9,8},{10,11... | collective-permute-start | bytes 786440 | tf_op jit(solution)/shard_map/ppermute | solution.py:307
  23.3 10.1 %collective-permute-start.11 = (f32[128,512]{1,0:T(8,128)S(1)}, f32[128,512]{1,0:T(8,128)S(1)}, u32[]{:S(2)}, u32[]{:S(2)}) collective-permute-start(f32[128,512]{1,0:T(8,128)S(1)} %shard_map.87.refs_3_), channel_id=1, source_target_pairs={{0,8},{28,20},{8,16},{20,12},{1,9},{29,21},{9,17},{21,13},{2,10},{... | collective-permute-start | bytes 786440 | tf_op jit(solution)/shard_map/ppermute | solution.py:392
  26.4 12.8 %collective-permute-start.2 = (f32[128,512]{1,0:T(8,128)S(1)}, f32[128,512]{1,0:T(8,128)S(1)}, u32[]{:S(2)}, u32[]{:S(2)}) collective-permute-start(f32[128,512]{1,0:T(8,128)S(1)} %get-tuple-element.38), channel_id=1, source_target_pairs={{0,2},{1,3},{2,0},{3,1},{4,6},{5,7},{6,4},{7,5},{8,10},{9,11},{10,... | collective-permute-start | bytes 786440 | tf_op jit(solution)/shard_map/ppermute | solution.py:307
  28.3 7.2 %collective-permute-start.9 = (f32[128,512]{1,0:T(8,128)S(1)}, f32[128,512]{1,0:T(8,128)S(1)}, u32[]{:S(2)}, u32[]{:S(2)}) collective-permute-start(f32[128,512]{1,0:T(8,128)S(1)} %shard_map.88.refs_1_.refs_4_), channel_id=1, source_target_pairs={{0,8},{28,20},{8,16},{20,12},{1,9},{29,21},{9,17},{21,13},{2,10},{... | collective-permute-start | bytes 786440 | tf_op jit(solution)/shard_map/ppermute | solution.py:392
  30.5 8.7 %collective-permute-start.3 = (f32[128,512]{1,0:T(8,128)S(1)}, f32[128,512]{1,0:T(8,128)S(1)}, u32[]{:S(2)}, u32[]{:S(2)}) collective-permute-start(f32[128,512]{1,0:T(8,128)S(1)} %get-tuple-element.39), channel_id=1, source_target_pairs={{0,3},{1,2},{2,1},{3,0},{4,7},{5,6},{6,5},{7,4},{8,11},{9,10},{10,... | collective-permute-start | bytes 786440 | tf_op jit(solution)/shard_map/ppermute | solution.py:307
  33.5 5.7 %collective-permute-start.12 = (f32[128,512]{1,0:T(8,128)S(1)}, f32[128,512]{1,0:T(8,128)S(1)}, u32[]{:S(2)}, u32[]{:S(2)}) collective-permute-start(f32[128,512]{1,0:T(8,128)S(1)} %shard_map.92.refs_4_), channel_id=1, source_target_pairs={{0,8},{28,20},{8,16},{20,12},{16,24},{12,4},{1,9},{29,21},{9,17},{... | collective-permute-start | bytes 786440 | tf_op jit(solution)/shard_map/ppermute | solution.py:392
  35.6 8.2 %collective-permute-start.14 = (f32[128,512]{1,0:T(8,128)S(1)}, f32[128,512]{1,0:T(8,128)S(1)}, u32[]{:S(2)}, u32[]{:S(2)}) collective-permute-start(f32[128,512]{1,0:T(8,128)S(1)} %shard_map.93.refs_2_.refs_4_), channel_id=1, source_target_pairs={{0,8},{28,20},{8,16},{20,12},{16,24},{12,4},{1,9},{29,21},{9,17},{... | collective-permute-start | bytes 786440 | tf_op jit(solution)/shard_map/ppermute | solution.py:392
  39.3 8.2 %collective-permute-start.13 = (f32[128,512]{1,0:T(8,128)S(1)}, f32[128,512]{1,0:T(8,128)S(1)}, u32[]{:S(2)}, u32[]{:S(2)}) collective-permute-start(f32[128,512]{1,0:T(8,128)S(1)} %shard_map.96.refs_4_), channel_id=1, source_target_pairs={{0,8},{28,20},{8,16},{20,12},{16,24},{12,4},{1,9},{29,21},{9,17},{... | collective-permute-start | bytes 786440 | tf_op jit(solution)/shard_map/ppermute | solution.py:392
  47.5 5.3 %collective-permute-start.17 = (f32[128,512]{1,0:T(8,128)S(1)}, f32[128,512]{1,0:T(8,128)S(1)}, u32[]{:S(2)}, u32[]{:S(2)}) collective-permute-start(f32[128,512]{1,0:T(8,128)S(1)} %shard_map.102), channel_id=1, source_target_pairs={{0,4},{4,0},{1,5},{5,1},{2,6},{6,2},{3,7},{7,3},{8,12},{12,8},{9,1... | collective-permute-start | bytes 786440 | tf_op jit(solution)/shard_map/ppermute | solution.py:310
  47.5 8.3 %collective-permute-start.16 = (f32[128,512]{1,0:T(8,128)S(1)}, f32[128,512]{1,0:T(8,128)S(1)}, u32[]{:S(2)}, u32[]{:S(2)}) collective-permute-start(f32[128,512]{1,0:T(8,128)S(1)} %shard_map.98.refs_3_), channel_id=1, source_target_pairs={{0,8},{28,20},{8,16},{20,12},{16,24},{12,4},{1,9},{29,21},{9,17},{... | collective-permute-start | bytes 786440 | tf_op jit(solution)/shard_map/ppermute | solution.py:392
  52.0 3.9 %collective-permute-start.15 = (f32[128,512]{1,0:T(8,128)S(1)}, f32[128,512]{1,0:T(8,128)S(1)}, u32[]{:S(2)}, u32[]{:S(2)}) collective-permute-start(f32[128,512]{1,0:T(8,128)S(1)} %shard_map.99.refs_3_), channel_id=1, source_target_pairs={{8,16},{20,12},{16,24},{12,4},{9,17},{21,13},{17,25},{13,5},{10,18... | collective-permute-start | bytes 786440 | tf_op jit(solution)/shard_map/ppermute | solution.py:392
  55.9 4.3 %collective-permute-start.21 = (f32[128,512]{1,0:T(8,128)S(1)}, f32[128,512]{1,0:T(8,128)S(1)}, u32[]{:S(2)}, u32[]{:S(2)}) collective-permute-start(f32[128,512]{1,0:T(8,128)S(1)} %shard_map.108), channel_id=1, source_target_pairs={{0,4},{4,0},{1,5},{5,1},{2,6},{6,2},{3,7},{7,3},{8,12},{12,8},{9,1... | collective-permute-start | bytes 786440 | tf_op jit(solution)/shard_map/ppermute | solution.py:310
  58.8 3.4 %collective-permute-start.19 = (f32[128,512]{1,0:T(8,128)S(1)}, f32[128,512]{1,0:T(8,128)S(1)}, u32[]{:S(2)}, u32[]{:S(2)}) collective-permute-start(f32[128,512]{1,0:T(8,128)S(1)} %shard_map.100.refs_2_.refs_3_), channel_id=1, source_target_pairs={{8,16},{20,12},{16,24},{12,4},{9,17},{21,13},{17,25},{13,5},{10,18... | collective-permute-start | bytes 786440 | tf_op jit(solution)/shard_map/ppermute | solution.py:392
  59.5 3.8 %collective-permute-start.18 = (f32[128,512]{1,0:T(8,128)S(1)}, f32[128,512]{1,0:T(8,128)S(1)}, u32[]{:S(2)}, u32[]{:S(2)}) collective-permute-start(f32[128,512]{1,0:T(8,128)S(1)} %shard_map.104.refs_2_), channel_id=1, source_target_pairs={{16,24},{12,4},{17,25},{13,5},{18,26},{14,6},{19,27},{15,7}} | collective-permute-start | bytes 786440 | tf_op jit(solution)/shard_map/ppermute | solution.py:392
  63.3 6.7 %collective-permute-start.23 = (f32[128,512]{1,0:T(8,128)S(1)}, f32[128,512]{1,0:T(8,128)S(1)}, u32[]{:S(2)}, u32[]{:S(2)}) collective-permute-start(f32[128,512]{1,0:T(8,128)S(1)} %shard_map.112), channel_id=1, source_target_pairs={{0,4},{4,0},{1,5},{5,1},{2,6},{6,2},{3,7},{7,3},{8,12},{12,8},{9,1... | collective-permute-start | bytes 786440 | tf_op jit(solution)/shard_map/ppermute | solution.py:310
  68.8 3.8 %collective-permute-start.26 = (f32[128,512]{1,0:T(8,128)S(1)}, f32[128,512]{1,0:T(8,128)S(1)}, u32[]{:S(2)}, u32[]{:S(2)}) collective-permute-start(f32[128,512]{1,0:T(8,128)S(1)} %shard_map.105.refs_3_), channel_id=1, source_target_pairs={{16,24},{12,4},{17,25},{13,5},{18,26},{14,6},{19,27},{15,7}} | collective-permute-start | bytes 786440 | tf_op jit(solution)/shard_map/ppermute | solution.py:392
  71.1 5.5 %collective-permute-start.25 = (f32[64,512]{1,0:T(8,128)S(1)}, f32[64,512]{1,0:T(8,128)S(1)}, u32[]{:S(2)}, u32[]{:S(2)}) collective-permute-start(f32[64,512]{1,0:T(8,128)S(1)} %shard_map.110.refs_5_), channel_id=1, source_target_pairs={{0,1},{1,0},{2,3},{3,2},{4,5},{5,4},{6,7},{7,6},{8,9},{9,8},{10,11... | collective-permute-start | bytes 393224 | tf_op jit(solution)/shard_map/ppermute | solution.py:307
  79.1 13.6 %collective-permute-start.30 = (f32[64,512]{1,0:T(8,128)S(1)}, f32[64,512]{1,0:T(8,128)S(1)}, u32[]{:S(2)}, u32[]{:S(2)}) collective-permute-start(f32[64,512]{1,0:T(8,128)S(1)} %shard_map.114.refs_3_), channel_id=1, source_target_pairs={{0,3},{1,2},{2,1},{3,0},{4,7},{5,6},{6,5},{7,4},{8,11},{9,10},{10,... | collective-permute-start | bytes 393224 | tf_op jit(solution)/shard_map/ppermute | solution.py:307
  81.1 11.7 %collective-permute-start.32 = (f32[64,512]{1,0:T(8,128)S(1)}, f32[64,512]{1,0:T(8,128)S(1)}, u32[]{:S(2)}, u32[]{:S(2)}) collective-permute-start(f32[64,512]{1,0:T(8,128)S(1)} %shard_map.120), channel_id=1, source_target_pairs={{0,2},{1,3},{2,0},{3,1},{4,6},{5,7},{6,4},{7,5},{8,10},{9,11},{10,... | collective-permute-start | bytes 393224 | tf_op jit(solution)/shard_map/ppermute | solution.py:307
  82.2 3.7 %collective-permute-start.28 = (f32[8,128]{1,0:T(8,128)S(1)}, f32[8,128]{1,0:T(8,128)S(1)}, u32[]{:S(2)}, u32[]{:S(2)}) collective-permute-start(f32[8,128]{1,0:T(8,128)S(1)} %get-tuple-element.54.refs_0_), channel_id=1, source_target_pairs={{0,8},{8,0},{16,24},{24,16},{1,9},{9,1},{17,25},{25,17},{2,10},{10... | collective-permute-start | bytes 12296 | tf_op jit(solution)/shard_map/ppermute | solution.py:438
  86.0 6.8 %collective-permute-start.29 = (f32[8,128]{1,0:T(8,128)S(1)}, f32[8,128]{1,0:T(8,128)S(1)}, u32[]{:S(2)}, u32[]{:S(2)}) collective-permute-start(f32[8,128]{1,0:T(8,128)S(1)} %shard_map.118.refs_0_), channel_id=1, source_target_pairs={{0,16},{8,24},{16,0},{24,8},{1,17},{9,25},{17,1},{25,9},{2,18},{10... | collective-permute-start | bytes 12296 | tf_op jit(solution)/shard_map/ppermute | solution.py:438
  92.8 5.5 %collective-permute-start.33 = (f32[72,512]{1,0:T(8,128)S(1)}, f32[72,512]{1,0:T(8,128)S(1)}, u32[]{:S(2)}, u32[]{:S(2)}) collective-permute-start(f32[72,512]{1,0:T(8,128)S(1)} %shard_map.121.refs_4_), channel_id=1, source_target_pairs={{0,1},{1,0},{2,3},{3,2},{4,5},{5,4},{6,7},{7,6},{8,9},{9,8},{10,11... | collective-permute-start | bytes 442376 | tf_op jit(solution)/shard_map/ppermute | solution.py:307
  93.5 5.8 %collective-permute-start.34 = (f32[72,512]{1,0:T(8,128)S(1)}, f32[72,512]{1,0:T(8,128)S(1)}, u32[]{:S(2)}, u32[]{:S(2)}) collective-permute-start(f32[72,512]{1,0:T(8,128)S(1)} %shard_map.121.refs_4_), channel_id=1, source_target_pairs={{0,2},{1,3},{2,0},{3,1},{4,6},{5,7},{6,4},{7,5},{8,10},{9,11},{10,... | collective-permute-start | bytes 442376 | tf_op jit(solution)/shard_map/ppermute | solution.py:307
  94.7 6.1 %collective-permute-start.35 = (f32[72,512]{1,0:T(8,128)S(1)}, f32[72,512]{1,0:T(8,128)S(1)}, u32[]{:S(2)}, u32[]{:S(2)}) collective-permute-start(f32[72,512]{1,0:T(8,128)S(1)} %shard_map.121.refs_4_), channel_id=1, source_target_pairs={{0,3},{1,2},{2,1},{3,0},{4,7},{5,6},{6,5},{7,4},{8,11},{9,10},{10,... | collective-permute-start | bytes 442376 | tf_op jit(solution)/shard_map/ppermute | solution.py:307
  96.4 5.2 %collective-permute-start.36 = (f32[72,512]{1,0:T(8,128)S(1)}, f32[72,512]{1,0:T(8,128)S(1)}, u32[]{:S(2)}, u32[]{:S(2)}) collective-permute-start(f32[72,512]{1,0:T(8,128)S(1)} %shard_map.121.refs_4_), channel_id=1, source_target_pairs={{0,4},{4,0},{1,5},{5,1},{2,6},{6,2},{3,7},{7,3},{8,12},{12,8},{9,1... | collective-permute-start | bytes 442376 | tf_op jit(solution)/shard_map/ppermute | solution.py:310
  98.4 3.2 %collective-permute-start.37 = (f32[72,512]{1,0:T(8,128)S(1)}, f32[72,512]{1,0:T(8,128)S(1)}, u32[]{:S(2)}, u32[]{:S(2)}) collective-permute-start(f32[72,512]{1,0:T(8,128)S(1)} %collective-permute-done.33.refs_5_), channel_id=1, source_target_pairs={{0,4},{4,0},{1,5},{5,1},{2,6},{6,2},{3,7},{7,3},{8,12},{12,8},{9,1... | collective-permute-start | bytes 442376 | tf_op jit(solution)/shard_map/ppermute | solution.py:310
  (13 other events, 64.2 us)

commit v5 on v4

--- a/solution.py
+++ b/solution.py
@@ -74,34 +74,28 @@
             put((2 + m) * count + i, (lasts[:, m : m + 1] == i).astype(jnp.float32))
 
 
-def pre_kernel(
-    resid, dictionary, partial_out, dict_out, resid_v, dict_v, sems
-):
-    pieces, lats, width = dict_v.shape
-    ahead = 3
-
-    def copies(i):
+def pre_kernel(resid, dictionary, partial_out, dict_out, resid_v, dict_v, sems):
+    pieces, _, width = dict_v.shape
+    copies = []
+    for i in range(pieces):
         cols = pl.ds(i * width, width)
-        return (
-            pltpu.make_async_copy(resid.at[:, cols], resid_v.at[i], sems.at[0, i]),
-            pltpu.make_async_copy(dictionary.at[:, cols], dict_v.at[i], sems.at[1, i]),
-        )
-
-    for i in range(min(ahead, pieces)):
-        for copy in copies(i):
+        copies.append(
+            (
+                pltpu.make_async_copy(resid.at[:, cols], resid_v.at[i], sems.at[0, i]),
+                pltpu.make_async_copy(dictionary.at[:, cols], dict_v.at[i], sems.at[1, i]),
+            )
+        )
+        for copy in copies[-1]:
             copy.start()
     total = None
     for i in range(pieces):
-        for copy in copies(i):
+        for copy in copies[i]:
             copy.wait()
-        if i + ahead < pieces:
-            for copy in copies(i + ahead):
-                copy.start()
         term = lax.dot_general(
-            resid_v[i], dict_v[i], (((1,), (1,)), ((), ())), preferred_element_type=jnp.float32
+            dict_v[i], resid_v[i], (((1,), (1,)), ((), ())), preferred_element_type=jnp.float32
         )
         total = term if total is None else total + term
-    partial_out[...] = total
+    partial_out[...] = total.T
     parts = dict_out.shape[1] // width
     for i in range(parts):
         dict_out[:, i * width : (i + 1) * width] = dict_v[lax.axis_index("tok") * parts + i]
@@ -178,30 +172,38 @@
     return sums
 
 
-def round_kernel(*refs):
-    rows = refs[0][...]
-    if len(refs) > 2:
-        rows = jnp.where(lax.axis_index("wid") == 0, rows, refs[1][...])
-    refs[-1][...] = rows.astype(jnp.bfloat16)
-
-
-def project_kernel(act, dictionary, table, out):
-    sums = running_parts(act[...], dictionary)
-    count = len(sums)
-    out[...] = total_of([table[count + i : count + i + 1, :1] * s for i, s in enumerate(sums)])
-
-
-def message_kernel(places, got, *refs):
+def round_kernel(act, out):
+    out[...] = act[...].astype(jnp.bfloat16)
+
+
+def project_kernel(act, table, *refs):
+    dicts, out = refs[:-1], refs[-1]
+    for side, dictionary in enumerate(dicts):
+        sums = running_parts(act[...], dictionary)
+        count = len(sums)
+        width = dictionary.shape[1]
+        out[:, side * width : (side + 1) * width] = total_of(
+            [table[count + i : count + i + 1, :1] * s for i, s in enumerate(sums)]
+        )
+
+
+def columns(ref, col, width):
+    return ref[:, col * width : (col + 1) * width]
+
+
+def message_kernel(places, cols, got, *refs):
     out = refs[-1]
+    width = out.shape[1]
     index = place_in_chain()
-    for place, piece in zip(places, refs[:-1]):
+    for place, piece, col in zip(places, refs[:-1], cols[1:]):
 
         @pl.when(index == place)
         def _():
-            out[...] = piece[...] + got[...] if place else piece[...]
-
-
-def choose_kernel(places, *refs):
+            own = columns(piece, col, width)
+            out[...] = own + columns(got, cols[0], width) if place else own
+
+
+def choose_kernel(places, cols, *refs):
     arrived, out = refs[:-1], refs[-1]
     index = place_in_chain()
 
@@ -209,11 +211,11 @@
     def _():
         out[...] = jnp.zeros_like(out)
 
-    for place, ref in zip(places, arrived):
+    for place, ref, col in zip(places, arrived, cols):
 
         @pl.when(index == place if len(arrived) > 1 else index > 0)
         def _():
-            out[...] = ref[...]
+            out[...] = columns(ref, col, out.shape[1])
 
 
 def square_sums(table, shifted):
@@ -309,15 +311,6 @@
     def swap(array):
         return lax.ppermute(array, "wid", [(w, w ^ 1) for w in range(n_wid)])
 
-    def gather(array):
-        if n_tok != 4:
-            return [(array,)] + [(across(array, q),) for q in range(1, n_tok)]
-        pairs = [(w * n_tok + t, w * n_tok + (t ^ (1 + w))) for w in range(n_wid) for t in range(n_tok)]
-        near = lax.ppermute(array, ("wid", "tok"), pairs)
-        far = across(array, 3)
-        other = swap(near)
-        return [(array,), (near, other), (other, near), (far,)]
-
     partial, dict_here = call(
         pre_kernel,
         [f32(rows, lats), bf16(lats, width)],
@@ -343,7 +336,6 @@
         (partial, partial_other, enc_bias.reshape(1, lats), active_blocks.T),
         after=(dict_wide,),
     )
-    gathered = gather(act)
     bias_here, *pieces = call(
         pieces_kernel,
         [f32(1, width)] + [f32(rows, width)] * n_tok,
@@ -355,83 +347,93 @@
     order = [0, 1, 3, 2] if n_tok == 4 else list(range(n_tok))
     steps = n_tok + n_lat - 2
     places = list(range(1, n_lat))
-    acts, sums, got, sent = {}, ([], []), ([], []), []
-    errs, gacts, loss = {}, [], ()
+    acts, errs, hands, gives, gacts, loss = {}, {}, [], [], [], ()
+    sums, got, sent = ([], []), ([], []), []
     waits = {step: [] for step in range(steps)}
     for place, q in enumerate(order[1:]):
-        waits[2 + min(place, 1)].append(resids[q])
+        waits[min(3 + place, steps - 1)].append(resids[q])
+
+    def project(q, dicts):
+        shape = [f32(rows, width * len(dicts))]
+        return call(project_kernel, shape, (acts[q], table, *dicts))[0]
+
     for step in range(steps + 1):
-        for side, dict_ref in enumerate((dict_here, dict_other)):
-            if step == steps:
-                break
-            if step == 0:
-                q = order[0]
-                if side == 0:
-                    acts[q] = call(round_kernel, [bf16(rows, lats)], gathered[q])[0]
-                sums[side].append(
+        at = [p for p in range(n_lat - 1) if 0 <= step - p < n_tok]
+        pairs = []
+        for p in at:
+            pairs.append((2 * p, 2 * (p + 1)))
+            pairs.append((2 * (n_lat - 1 - p) + 1, 2 * (n_lat - 2 - p) + 1))
+        if step == 0:
+            acts[order[0]] = call(round_kernel, [bf16(rows, lats)], (act,))[0]
+            message = project(order[0], (dict_here, dict_other))
+            arrived = lax.ppermute(message, ("lat", "wid"), pairs)
+            for side in range(2):
+                sums[side].append((message, side))
+                got[side].append((arrived, side))
+            sent = [arrived]
+        elif step < steps:
+            for side in range(2):
+                items = [got[side][-1], *[sums[side][step - p] for p in at]]
+                message = call(
+                    functools.partial(message_kernel, at, [col for _, col in items]),
+                    [f32(rows, width)],
+                    [array for array, _ in items],
+                    after=sent + (waits[step] if side == 0 else []) if step > 1 else (),
+                )[0]
+                got[side].append((lax.ppermute(message, ("lat", "wid"), pairs), 0))
+                sent = [message]
+        if step + 1 < n_tok:
+            q = order[step + 1]
+            gathered = across(act, q)
+            acts[q] = call(round_kernel, [bf16(rows, lats)], (gathered,), after=sent)[0]
+            for side, dict_ref in enumerate((dict_here, dict_other)):
+                sums[side].append((project(q, (dict_ref,)), 0))
+        ready = []
+        c = step - (n_lat - 1)
+        if c >= 0:
+            chosen = []
+            for side in (1, 0):
+                items = [got[side][c + p - 1] for p in places]
+                if n_lat > 4:
+                    items = [a[:, col * width : (col + 1) * width] for a, col in items]
+                    items = [(pick(place_in_chain(), dict(zip(places, items))), 0)]
+                chosen.append(
                     call(
-                        project_kernel,
+                        functools.partial(choose_kernel, places, [col for _, col in items]),
                         [f32(rows, width)],
-                        (acts[q], dict_ref, table),
-                        after=sent,
+                        [array for array, _ in items],
+                        after=sent if step < steps else ready_before,
                     )[0]
                 )
-            at = [p for p in range(n_lat - 1) if 0 <= step - p < n_tok]
-            message = sums[side][0]
-            if step:
-                message = call(
-                    functools.partial(message_kernel, at),
-                    [f32(rows, width)],
-                    (got[side][-1], *[sums[side][step - p] for p in at]),
-                    after=sent + (waits[step] if side == 0 else []),
-                )[0]
-            pairs = []
-            for p in at:
-                pairs.append((2 * p, 2 * (p + 1)))
-                pairs.append((2 * (n_lat - 1 - p) + 1, 2 * (n_lat - 2 - p) + 1))
-            got[side].append(lax.ppermute(message, ("lat", "wid"), pairs))
-            sent = [message]
-        if step + 1 < n_tok:
-            q = order[step + 1]
-            acts[q] = call(round_kernel, [bf16(rows, lats)], gathered[q], after=sent)[0]
-            for side, dict_ref in enumerate((dict_here, dict_other)):
-                sums[side].append(
-                    call(
-                        project_kernel, [f32(rows, width)], (acts[q], dict_ref, table)
-                    )[0]
-                )
-        c = step - (n_lat - 1)
-        if c < 0:
-            continue
-        q = order[c]
-        ahead = sent + [got[0][step]] if step < steps else []
-        if c:
-            ahead.append(added)
-        if c > 1:
-            ahead.append(gacts[-2])
-        chosen = []
-        for side in (1, 0):
-            arrived = [got[side][c + p - 1] for p in places]
-            if n_lat > 4:
-                arrived = [pick(place_in_chain(), dict(zip(places, arrived)))]
-            chosen.append(
-                call(
-                    functools.partial(choose_kernel, places),
-                    [f32(rows, width)],
-                    arrived,
-                    after=ahead,
-                )[0]
+            hands.append((swap(chosen[0]), chosen[1]))
+            ready += chosen
+        stages = [c - 1] if step < steps - 1 else [c - 1, c] if step < steps else [c]
+        for c in stages:
+            if c < 0:
+                continue
+            q = order[c]
+            errs[q], keep, give, loss_here = call(
+                error_kernel,
+                [bf16(count, rows, width)] + [f32(rows // 2, lats)] * 2 + [f32(LOSS_ROWS, BLOCK)],
+                (acts[q], dict_here, resids[q], bias_here, table, hands[c][1], hands[c][0], *loss),
+                after=sent if step < steps else (),
             )
-        hand, mine = chosen
-        errs[q], keep, give, loss_here = call(
-            error_kernel,
-            [bf16(count, rows, width)] + [f32(rows // 2, lats)] * 2 + [f32(LOSS_ROWS, BLOCK)],
-            (acts[q], dict_here, resids[q], bias_here, table, mine, swap(hand), *loss),
-        )
-        loss = (loss_here,)
-        waits.setdefault(step + 2, []).append(errs[q])
-        added = call(add_kernel, [f32(rows // 2, lats)], (keep, swap(give)))[0]
-        gacts.append(across(added, q) if q else added)
+            loss = (loss_here,)
+            gives.append((keep, swap(give)))
+            ready.append(errs[q])
+        stages = [c - 2] if step < steps - 1 else [c - 2, c - 1, c] if step < steps else [c]
+        for c in stages:
+            if c < 0:
+                continue
+            q = order[c]
+            added = call(
+                add_kernel, [f32(rows // 2, lats)], gives[c], after=sent if step < steps else ()
+            )[0]
+            gacts.append(across(added, q) if q else added)
+            ready.append(added)
+        if step + 1 < steps:
+            waits[step + 1] += ready
+        ready_before = ready
 
     loss, gap = loss[0], 1
     while gap < n_lat:

time: 104 us -> 91.8 us (0.88)
  starting transfers between devices: 62.5 us -> 55 us
  waiting for transfers between devices: 27.8 us -> 24.2 us
    ppermute x13 -> x11, waiting for transfers between devices: 10.2 us -> 1.62 us  [the longest x10 1.62 us: body(): got[side].append((lax.ppermute(message, ('lat', 'wid'), pairs), 0))]
    ppermute x13 -> x11, starting transfers between devices: 29.6 us -> 22.6 us  [the longest x10 17.8 us: body(): got[side].append((lax.ppermute(message, ('lat', 'wid'), pairs), 0))]
    ppermute x2, starting transfers between devices: 7.33 us -> 1.55 us  [body(): other = lax.ppermute(loss, 'lat', [(p, p ^ gap) for p in range(n_lat)])]
    ppermute x2, waiting for transfers between devices: 3.17 us -> 6.56 us  [body(): other = lax.ppermute(loss, 'lat', [(p, p ^ gap) for p in range(n_lat)])]
    ppermute x10 -> x12, starting transfers between devices: 14 us -> 17.1 us  [across(): return lax.ppermute(array, 'tok', [(t, t ^ q) for t in range(n_tok)])]
    ppermute x15 -> x14, starting transfers between devices: 11.5 us -> 13.6 us  [swap(): return lax.ppermute(array, 'wid', [(w, w ^ 1) for w in range(n_wid)])]
    ppermute x10 -> x12, waiting for transfers between devices: 9.77 us -> 11.1 us  [across(): return lax.ppermute(array, 'tok', [(t, t ^ q) for t in range(n_tok)])]
    pallas_call x47 -> x46, Pallas kernels: 12 us -> 11.1 us  [call(): pl.pallas_call(run, out_shape=outs, in_specs=list(specs or [VMEM] * len(a...]
  transfers between devices with their start and end apart: 40 -> 39, of which waited for: 15 -> 13; matrix products, arithmetic and copies ran while one was open for 0% -> 0% of each run, Pallas kernels for 6% -> 6%
where the time goes in v5:
time: 91.8 us; the launch traced here: 91.5 us
  starting transfers between devices  55 us (60%)
  waiting for transfers between devices  24.2 us (26%)
  Pallas kernels  11.1 us (12%)
  between operations  1.19 us (1%)
    ppermute x10, starting transfers between devices, body(): got[side].append((lax.ppermute(message, ('lat', 'wid'), pairs), 0))  17.8 us
    ppermute x12, starting transfers between devices, across(): return lax.ppermute(array, 'tok', [(t, t ^ q) for t in range(n_tok)])  17.1 us
    ppermute x14, starting transfers between devices, swap(): return lax.ppermute(array, 'wid', [(w, w ^ 1) for w in range(n_wid)])  13.6 us
    ppermute x12, waiting for transfers between devices, across(): return lax.ppermute(array, 'tok', [(t, t ^ q) for t in range(n_tok)])  11.1 us
    pallas_call x46, Pallas kernels, call(): pl.pallas_call(run, out_shape=outs, in_specs=list(specs or [VMEM] * len(a...  11.1 us
    ppermute x2, waiting for transfers between devices, body(): other = lax.ppermute(loss, 'lat', [(p, p ^ gap) for p in range(n_lat)])  6.56 us
    ppermute x1, starting transfers between devices, body(): arrived = lax.ppermute(message, ('lat', 'wid'), pairs)  4.87 us
    ppermute x14, waiting for transfers between devices, swap(): return lax.ppermute(array, 'wid', [(w, w ^ 1) for w in range(n_wid)])  4.85 us
  transfers between devices with their start and end apart: 39, of which 13 were waited for; matrix products, arithmetic and copies ran while one was open for 0% of the time, Pallas kernels for 6%

profile of v5, /device:TPU:0, one launch (start us, length us, event | category | flops | bytes accessed | tf_op | source)
XLA Modules:
  0.0 91.5 jit_solution(1325024379820502503)
XLA Ops:
  0.7 2.9 %shard_map.77 = (f32[128,512]{1,0:T(8,128)S(1)}, bf16[512,512]{1,0:T(8,128)(2,1)S(1)}) custom-call(bf16[128,2048]{1,0:T(8,128)(2,1)} %refs_0_.3, bf16[512,2048]{1,0:T(8,128)(2,1)} %refs_1_.1), custom_call_target="tpu_custom_call" | custom-call | bytes 1024 | tf_op jit(solution)/shard_map/pallas_call | solution.py:36
  4.1 1.2 %collective-permute-done.refs_2_.refs_1_ = f32[128,512]{1,0:T(8,128)S(1)} collective-permute-done((f32[128,512]{1,0:T(8,128)S(1)}, f32[128,512]{1,0:T(8,128)S(1)}, u32[]{:S(2)}, u32[]{:S(2)}) %collective-permute-start) | collective-permute-done | bytes 262176 | tf_op jit(solution)/shard_map/ppermute | solution.py:312
  6.1 2.0 %collective-permute-done.5.refs_3_.refs_2_ = f32[512,512]{1,0:T(8,128)S(1)} collective-permute-done((f32[512,512]{1,0:T(8,128)S(1)}, f32[512,512]{1,0:T(8,128)S(1)}, u32[]{:S(2)}, u32[]{:S(2)}) %collective-permute-start.5) | collective-permute-done | bytes 1048608 | tf_op jit(solution)/shard_map/ppermute | solution.py:312
  8.6 4.9 %collective-permute-start.6 = (f32[128,1024]{1,0:T(8,128)S(1)}, f32[128,1024]{1,0:T(8,128)S(1)}, u32[]{:S(2)}, u32[]{:S(2)}) collective-permute-start(f32[128,1024]{1,0:T(8,128)S(1)} %shard_map.82.refs_2_.refs_3_), channel_id=1, source_target_pairs={{0,8},{28,20},{1,9},{29,21},{2,10},{30,22},{3,11},{31,23}} | collective-permute-start | bytes 1572872 | tf_op jit(solution)/shard_map/ppermute | solution.py:369
  13.5 1.6 %collective-permute-start.7 = (f32[128,512]{1,0:T(8,128)S(1)}, f32[128,512]{1,0:T(8,128)S(1)}, u32[]{:S(2)}, u32[]{:S(2)}) collective-permute-start(f32[128,512]{1,0:T(8,128)S(1)} %get-tuple-element.35.refs_2_.refs_0_), channel_id=1, source_target_pairs={{0,1},{1,0},{2,3},{3,2},{4,5},{5,4},{6,7},{7,6},{8,9},{9,8},{10,11... | collective-permute-start | bytes 786440 | tf_op jit(solution)/shard_map/ppermute | solution.py:309
  15.0 1.5 %collective-permute-start.9 = (f32[128,512]{1,0:T(8,128)S(1)}, f32[128,512]{1,0:T(8,128)S(1)}, u32[]{:S(2)}, u32[]{:S(2)}) collective-permute-start(f32[128,512]{1,0:T(8,128)S(1)} %get-tuple-element.35.refs_2_.refs_0_), channel_id=1, source_target_pairs={{0,3},{1,2},{2,1},{3,0},{4,7},{5,6},{6,5},{7,4},{8,11},{9,10},{10,... | collective-permute-start | bytes 786440 | tf_op jit(solution)/shard_map/ppermute | solution.py:309
  16.5 5.1 %collective-permute-done.7.refs_0_ = f32[128,512]{1,0:T(8,128)S(1)} collective-permute-done((f32[128,512]{1,0:T(8,128)S(1)}, f32[128,512]{1,0:T(8,128)S(1)}, u32[]{:S(2)}, u32[]{:S(2)}) %collective-permute-start.7) | collective-permute-done | bytes 262176 | tf_op jit(solution)/shard_map/ppermute | solution.py:309
  22.0 3.0 %collective-permute-start.10 = (f32[128,512]{1,0:T(8,128)S(1)}, f32[128,512]{1,0:T(8,128)S(1)}, u32[]{:S(2)}, u32[]{:S(2)}) collective-permute-start(f32[128,512]{1,0:T(8,128)S(1)} %shard_map.89), channel_id=1, source_target_pairs={{0,8},{28,20},{8,16},{20,12},{1,9},{29,21},{9,17},{21,13},{2,10},{... | collective-permute-start | bytes 786440 | tf_op jit(solution)/shard_map/ppermute | solution.py:383
  25.4 2.4 %collective-permute-start.8 = (f32[128,512]{1,0:T(8,128)S(1)}, f32[128,512]{1,0:T(8,128)S(1)}, u32[]{:S(2)}, u32[]{:S(2)}) collective-permute-start(f32[128,512]{1,0:T(8,128)S(1)} %shard_map.85.refs_1_.refs_4_), channel_id=1, source_target_pairs={{0,8},{28,20},{8,16},{20,12},{1,9},{29,21},{9,17},{21,13},{2,10},{... | collective-permute-start | bytes 786440 | tf_op jit(solution)/shard_map/ppermute | solution.py:383
  27.8 1.6 %collective-permute-start.4 = (f32[128,512]{1,0:T(8,128)S(1)}, f32[128,512]{1,0:T(8,128)S(1)}, u32[]{:S(2)}, u32[]{:S(2)}) collective-permute-start(f32[128,512]{1,0:T(8,128)S(1)} %get-tuple-element.35.refs_2_.refs_0_), channel_id=1, source_target_pairs={{0,2},{1,3},{2,0},{3,1},{4,6},{5,7},{6,4},{7,5},{8,10},{9,11},{10,... | collective-permute-start | bytes 786440 | tf_op jit(solution)/shard_map/ppermute | solution.py:309
  29.4 1.6 %collective-permute-start.1 = (f32[128,512]{1,0:T(8,128)S(1)}, f32[128,512]{1,0:T(8,128)S(1)}, u32[]{:S(2)}, u32[]{:S(2)}) collective-permute-start(f32[128,512]{1,0:T(8,128)S(1)} %get-tuple-element.37), channel_id=1, source_target_pairs={{0,1},{1,0},{2,3},{3,2},{4,5},{5,4},{6,7},{7,6},{8,9},{9,8},{10,11... | collective-permute-start | bytes 786440 | tf_op jit(solution)/shard_map/ppermute | solution.py:309
  31.7 1.9 %collective-permute-start.11 = (f32[128,512]{1,0:T(8,128)S(1)}, f32[128,512]{1,0:T(8,128)S(1)}, u32[]{:S(2)}, u32[]{:S(2)}) collective-permute-start(f32[128,512]{1,0:T(8,128)S(1)} %shard_map.91.refs_4_), channel_id=1, source_target_pairs={{0,8},{28,20},{8,16},{20,12},{16,24},{12,4},{1,9},{29,21},{9,17},{... | collective-permute-start | bytes 786440 | tf_op jit(solution)/shard_map/ppermute | solution.py:383
  33.7 2.5 %collective-permute-start.13 = (f32[128,512]{1,0:T(8,128)S(1)}, f32[128,512]{1,0:T(8,128)S(1)}, u32[]{:S(2)}, u32[]{:S(2)}) collective-permute-start(f32[128,512]{1,0:T(8,128)S(1)} %shard_map.92.refs_1_.refs_4_), channel_id=1, source_target_pairs={{0,8},{28,20},{8,16},{20,12},{16,24},{12,4},{1,9},{29,21},{9,17},{... | collective-permute-start | bytes 786440 | tf_op jit(solution)/shard_map/ppermute | solution.py:383
  36.2 2.5 %collective-permute-start.3 = (f32[128,512]{1,0:T(8,128)S(1)}, f32[128,512]{1,0:T(8,128)S(1)}, u32[]{:S(2)}, u32[]{:S(2)}) collective-permute-start(f32[128,512]{1,0:T(8,128)S(1)} %get-tuple-element.39), channel_id=1, source_target_pairs={{0,3},{1,2},{2,1},{3,0},{4,7},{5,6},{6,5},{7,4},{8,11},{9,10},{10,... | collective-permute-start | bytes 786440 | tf_op jit(solution)/shard_map/ppermute | solution.py:309
  39.4 2.5 %collective-permute-start.12 = (f32[128,512]{1,0:T(8,128)S(1)}, f32[128,512]{1,0:T(8,128)S(1)}, u32[]{:S(2)}, u32[]{:S(2)}) collective-permute-start(f32[128,512]{1,0:T(8,128)S(1)} %shard_map.95.refs_4_), channel_id=1, source_target_pairs={{0,8},{28,20},{8,16},{20,12},{16,24},{12,4},{1,9},{29,21},{9,17},{... | collective-permute-start | bytes 786440 | tf_op jit(solution)/shard_map/ppermute | solution.py:383
  42.0 2.7 %collective-permute-start.15 = (f32[128,512]{1,0:T(8,128)S(1)}, f32[128,512]{1,0:T(8,128)S(1)}, u32[]{:S(2)}, u32[]{:S(2)}) collective-permute-start(f32[128,512]{1,0:T(8,128)S(1)} %shard_map.97.refs_3_), channel_id=1, source_target_pairs={{0,8},{28,20},{8,16},{20,12},{16,24},{12,4},{1,9},{29,21},{9,17},{... | collective-permute-start | bytes 786440 | tf_op jit(solution)/shard_map/ppermute | solution.py:383
  44.7 1.4 %collective-permute-start.2 = (f32[128,512]{1,0:T(8,128)S(1)}, f32[128,512]{1,0:T(8,128)S(1)}, u32[]{:S(2)}, u32[]{:S(2)}) collective-permute-start(f32[128,512]{1,0:T(8,128)S(1)} %get-tuple-element.38), channel_id=1, source_target_pairs={{0,2},{1,3},{2,0},{3,1},{4,6},{5,7},{6,4},{7,5},{8,10},{9,11},{10,... | collective-permute-start | bytes 786440 | tf_op jit(solution)/shard_map/ppermute | solution.py:309
  47.0 1.6 %collective-permute-done.15.refs_0_.refs_2_.refs_1_ = f32[128,512]{1,0:T(8,128)S(1)} collective-permute-done((f32[128,512]{1,0:T(8,128)S(1)}, f32[128,512]{1,0:T(8,128)S(1)}, u32[]{:S(2)}, u32[]{:S(2)}) %collective-permute-start.15) | collective-permute-done | bytes 262176 | tf_op jit(solution)/shard_map/ppermute | solution.py:383
  51.2 5.5 %collective-permute-start.20 = (f32[128,512]{1,0:T(8,128)S(1)}, f32[128,512]{1,0:T(8,128)S(1)}, u32[]{:S(2)}, u32[]{:S(2)}) collective-permute-start(f32[128,512]{1,0:T(8,128)S(1)} %shard_map.107.refs_3_), channel_id=1, source_target_pairs={{0,4},{4,0},{1,5},{5,1},{2,6},{6,2},{3,7},{7,3},{8,12},{12,8},{9,1... | collective-permute-start | bytes 786440 | tf_op jit(solution)/shard_map/ppermute | solution.py:312
  61.2 2.8 %collective-permute-start.25 = (f32[128,512]{1,0:T(8,128)S(1)}, f32[128,512]{1,0:T(8,128)S(1)}, u32[]{:S(2)}, u32[]{:S(2)}) collective-permute-start(f32[128,512]{1,0:T(8,128)S(1)} %shard_map.115), channel_id=1, source_target_pairs={{0,4},{4,0},{1,5},{5,1},{2,6},{6,2},{3,7},{7,3},{8,12},{12,8},{9,1... | collective-permute-start | bytes 786440 | tf_op jit(solution)/shard_map/ppermute | solution.py:312
  64.0 1.1 %collective-permute-done.25.refs_6_ = f32[128,512]{1,0:T(8,128)S(1)} collective-permute-done((f32[128,512]{1,0:T(8,128)S(1)}, f32[128,512]{1,0:T(8,128)S(1)}, u32[]{:S(2)}, u32[]{:S(2)}) %collective-permute-start.25) | collective-permute-done | bytes 262176 | tf_op jit(solution)/shard_map/ppermute | solution.py:312
  65.8 2.2 %collective-permute-start.30 = (f32[64,512]{1,0:T(8,128)S(1)}, f32[64,512]{1,0:T(8,128)S(1)}, u32[]{:S(2)}, u32[]{:S(2)}) collective-permute-start(f32[64,512]{1,0:T(8,128)S(1)} %get-tuple-element.58), channel_id=1, source_target_pairs={{0,4},{4,0},{1,5},{5,1},{2,6},{6,2},{3,7},{7,3},{8,12},{12,8},{9,1... | collective-permute-start | bytes 393224 | tf_op jit(solution)/shard_map/ppermute | solution.py:312
  68.1 1.5 %collective-permute-start.28 = (f32[64,512]{1,0:T(8,128)S(1)}, f32[64,512]{1,0:T(8,128)S(1)}, u32[]{:S(2)}, u32[]{:S(2)}) collective-permute-start(f32[64,512]{1,0:T(8,128)S(1)} %shard_map.112.refs_8_), channel_id=1, source_target_pairs={{0,1},{1,0},{2,3},{3,2},{4,5},{5,4},{6,7},{7,6},{8,9},{9,8},{10,11... | collective-permute-start | bytes 393224 | tf_op jit(solution)/shard_map/ppermute | solution.py:309
  70.3 1.3 %collective-permute-start.31 = (f32[64,512]{1,0:T(8,128)S(1)}, f32[64,512]{1,0:T(8,128)S(1)}, u32[]{:S(2)}, u32[]{:S(2)}) collective-permute-start(f32[64,512]{1,0:T(8,128)S(1)} %shard_map.119), channel_id=1, source_target_pairs={{0,2},{1,3},{2,0},{3,1},{4,6},{5,7},{6,4},{7,5},{8,10},{9,11},{10,... | collective-permute-start | bytes 393224 | tf_op jit(solution)/shard_map/ppermute | solution.py:309
  71.6 3.6 %collective-permute-done.26.refs_1_ = f32[8,128]{1,0:T(8,128)S(1)} collective-permute-done((f32[8,128]{1,0:T(8,128)S(1)}, f32[8,128]{1,0:T(8,128)S(1)}, u32[]{:S(2)}, u32[]{:S(2)}) %collective-permute-start.26) | collective-permute-done | bytes 4128 | tf_op jit(solution)/shard_map/ppermute | solution.py:440
  75.2 1.5 %collective-permute-start.27 = (f32[8,128]{1,0:T(8,128)S(1)}, f32[8,128]{1,0:T(8,128)S(1)}, u32[]{:S(2)}, u32[]{:S(2)}) collective-permute-start(f32[8,128]{1,0:T(8,128)S(1)} %shard_map.117.refs_0_), channel_id=1, source_target_pairs={{0,16},{8,24},{16,0},{24,8},{1,17},{9,25},{17,1},{25,9},{2,18},{10... | collective-permute-start | bytes 12296 | tf_op jit(solution)/shard_map/ppermute | solution.py:440
  76.8 3.0 %collective-permute-done.27.refs_1_ = f32[8,128]{1,0:T(8,128)S(1)} collective-permute-done((f32[8,128]{1,0:T(8,128)S(1)}, f32[8,128]{1,0:T(8,128)S(1)}, u32[]{:S(2)}, u32[]{:S(2)}) %collective-permute-start.27) | collective-permute-done | bytes 4128 | tf_op jit(solution)/shard_map/ppermute | solution.py:440
  79.9 1.6 %collective-permute-start.32 = (f32[72,512]{1,0:T(8,128)S(1)}, f32[72,512]{1,0:T(8,128)S(1)}, u32[]{:S(2)}, u32[]{:S(2)}) collective-permute-start(f32[72,512]{1,0:T(8,128)S(1)} %shard_map.120.refs_4_), channel_id=1, source_target_pairs={{0,1},{1,0},{2,3},{3,2},{4,5},{5,4},{6,7},{7,6},{8,9},{9,8},{10,11... | collective-permute-start | bytes 442376 | tf_op jit(solution)/shard_map/ppermute | solution.py:309
  82.0 1.5 %collective-permute-start.34 = (f32[72,512]{1,0:T(8,128)S(1)}, f32[72,512]{1,0:T(8,128)S(1)}, u32[]{:S(2)}, u32[]{:S(2)}) collective-permute-start(f32[72,512]{1,0:T(8,128)S(1)} %shard_map.120.refs_4_), channel_id=1, source_target_pairs={{0,3},{1,2},{2,1},{3,0},{4,7},{5,6},{6,5},{7,4},{8,11},{9,10},{10,... | collective-permute-start | bytes 442376 | tf_op jit(solution)/shard_map/ppermute | solution.py:309
  83.5 1.9 %collective-permute-done.32.refs_5_ = f32[72,512]{1,0:T(8,128)S(1)} collective-permute-done((f32[72,512]{1,0:T(8,128)S(1)}, f32[72,512]{1,0:T(8,128)S(1)}, u32[]{:S(2)}, u32[]{:S(2)}) %collective-permute-start.32) | collective-permute-done | bytes 147488 | tf_op jit(solution)/shard_map/ppermute | solution.py:309
  85.4 3.1 %collective-permute-done.33.refs_6_ = f32[72,512]{1,0:T(8,128)S(1)} collective-permute-done((f32[72,512]{1,0:T(8,128)S(1)}, f32[72,512]{1,0:T(8,128)S(1)}, u32[]{:S(2)}, u32[]{:S(2)}) %collective-permute-start.33) | collective-permute-done | bytes 147488 | tf_op jit(solution)/shard_map/ppermute | solution.py:309
  90.1 1.3 %shard_map.122 = (bf16[512,512]{1,0:T(8,128)(2,1)}, f32[4]{0:T(128)}) custom-call(f32[128,512]{1,0:T(8,128)S(1)} %get-tuple-element.36.refs_2_.refs_0_, f32[128,512]{1,0:T(8,128)S(1)} %collective-permute-done.1.refs_5_.refs_2_.refs_1_, f32[128,512]{1,0:T(8,128)S(1)} %collective-permute-done.2.refs_3_.refs_2_, ...), custom_call_target="tpu_custom_call" | custom-call | bytes 1024 | tf_op jit(solution)/shard_map/pallas_call | solution.py:36
  (102 shorter events, 15.4 us)
Async XLA Ops:
  8.6 13.0 %collective-permute-start.6 = (f32[128,1024]{1,0:T(8,128)S(1)}, f32[128,1024]{1,0:T(8,128)S(1)}, u32[]{:S(2)}, u32[]{:S(2)}) collective-permute-start(f32[128,1024]{1,0:T(8,128)S(1)} %shard_map.82.refs_2_.refs_3_), channel_id=1, source_target_pairs={{0,8},{28,20},{1,9},{29,21},{2,10},{30,22},{3,11},{31,23}} | collective-permute-start | bytes 1572872 | tf_op jit(solution)/shard_map/ppermute | solution.py:369
  13.5 8.1 %collective-permute-start.7 = (f32[128,512]{1,0:T(8,128)S(1)}, f32[128,512]{1,0:T(8,128)S(1)}, u32[]{:S(2)}, u32[]{:S(2)}) collective-permute-start(f32[128,512]{1,0:T(8,128)S(1)} %get-tuple-element.35.refs_2_.refs_0_), channel_id=1, source_target_pairs={{0,1},{1,0},{2,3},{3,2},{4,5},{5,4},{6,7},{7,6},{8,9},{9,8},{10,11... | collective-permute-start | bytes 786440 | tf_op jit(solution)/shard_map/ppermute | solution.py:309
  15.0 16.0 %collective-permute-start.9 = (f32[128,512]{1,0:T(8,128)S(1)}, f32[128,512]{1,0:T(8,128)S(1)}, u32[]{:S(2)}, u32[]{:S(2)}) collective-permute-start(f32[128,512]{1,0:T(8,128)S(1)} %get-tuple-element.35.refs_2_.refs_0_), channel_id=1, source_target_pairs={{0,3},{1,2},{2,1},{3,0},{4,7},{5,6},{6,5},{7,4},{8,11},{9,10},{10,... | collective-permute-start | bytes 786440 | tf_op jit(solution)/shard_map/ppermute | solution.py:309
  22.0 9.6 %collective-permute-start.10 = (f32[128,512]{1,0:T(8,128)S(1)}, f32[128,512]{1,0:T(8,128)S(1)}, u32[]{:S(2)}, u32[]{:S(2)}) collective-permute-start(f32[128,512]{1,0:T(8,128)S(1)} %shard_map.89), channel_id=1, source_target_pairs={{0,8},{28,20},{8,16},{20,12},{1,9},{29,21},{9,17},{21,13},{2,10},{... | collective-permute-start | bytes 786440 | tf_op jit(solution)/shard_map/ppermute | solution.py:383
  25.4 8.2 %collective-permute-start.8 = (f32[128,512]{1,0:T(8,128)S(1)}, f32[128,512]{1,0:T(8,128)S(1)}, u32[]{:S(2)}, u32[]{:S(2)}) collective-permute-start(f32[128,512]{1,0:T(8,128)S(1)} %shard_map.85.refs_1_.refs_4_), channel_id=1, source_target_pairs={{0,8},{28,20},{8,16},{20,12},{1,9},{29,21},{9,17},{21,13},{2,10},{... | collective-permute-start | bytes 786440 | tf_op jit(solution)/shard_map/ppermute | solution.py:383
  27.8 10.9 %collective-permute-start.4 = (f32[128,512]{1,0:T(8,128)S(1)}, f32[128,512]{1,0:T(8,128)S(1)}, u32[]{:S(2)}, u32[]{:S(2)}) collective-permute-start(f32[128,512]{1,0:T(8,128)S(1)} %get-tuple-element.35.refs_2_.refs_0_), channel_id=1, source_target_pairs={{0,2},{1,3},{2,0},{3,1},{4,6},{5,7},{6,4},{7,5},{8,10},{9,11},{10,... | collective-permute-start | bytes 786440 | tf_op jit(solution)/shard_map/ppermute | solution.py:309
  29.4 9.9 %collective-permute-start.1 = (f32[128,512]{1,0:T(8,128)S(1)}, f32[128,512]{1,0:T(8,128)S(1)}, u32[]{:S(2)}, u32[]{:S(2)}) collective-permute-start(f32[128,512]{1,0:T(8,128)S(1)} %get-tuple-element.37), channel_id=1, source_target_pairs={{0,1},{1,0},{2,3},{3,2},{4,5},{5,4},{6,7},{7,6},{8,9},{9,8},{10,11... | collective-permute-start | bytes 786440 | tf_op jit(solution)/shard_map/ppermute | solution.py:309
  31.7 7.6 %collective-permute-start.11 = (f32[128,512]{1,0:T(8,128)S(1)}, f32[128,512]{1,0:T(8,128)S(1)}, u32[]{:S(2)}, u32[]{:S(2)}) collective-permute-start(f32[128,512]{1,0:T(8,128)S(1)} %shard_map.91.refs_4_), channel_id=1, source_target_pairs={{0,8},{28,20},{8,16},{20,12},{16,24},{12,4},{1,9},{29,21},{9,17},{... | collective-permute-start | bytes 786440 | tf_op jit(solution)/shard_map/ppermute | solution.py:383
  33.7 8.2 %collective-permute-start.13 = (f32[128,512]{1,0:T(8,128)S(1)}, f32[128,512]{1,0:T(8,128)S(1)}, u32[]{:S(2)}, u32[]{:S(2)}) collective-permute-start(f32[128,512]{1,0:T(8,128)S(1)} %shard_map.92.refs_1_.refs_4_), channel_id=1, source_target_pairs={{0,8},{28,20},{8,16},{20,12},{16,24},{12,4},{1,9},{29,21},{9,17},{... | collective-permute-start | bytes 786440 | tf_op jit(solution)/shard_map/ppermute | solution.py:383
  36.2 10.1 %collective-permute-start.3 = (f32[128,512]{1,0:T(8,128)S(1)}, f32[128,512]{1,0:T(8,128)S(1)}, u32[]{:S(2)}, u32[]{:S(2)}) collective-permute-start(f32[128,512]{1,0:T(8,128)S(1)} %get-tuple-element.39), channel_id=1, source_target_pairs={{0,3},{1,2},{2,1},{3,0},{4,7},{5,6},{6,5},{7,4},{8,11},{9,10},{10,... | collective-permute-start | bytes 786440 | tf_op jit(solution)/shard_map/ppermute | solution.py:309
  39.4 6.9 %collective-permute-start.12 = (f32[128,512]{1,0:T(8,128)S(1)}, f32[128,512]{1,0:T(8,128)S(1)}, u32[]{:S(2)}, u32[]{:S(2)}) collective-permute-start(f32[128,512]{1,0:T(8,128)S(1)} %shard_map.95.refs_4_), channel_id=1, source_target_pairs={{0,8},{28,20},{8,16},{20,12},{16,24},{12,4},{1,9},{29,21},{9,17},{... | collective-permute-start | bytes 786440 | tf_op jit(solution)/shard_map/ppermute | solution.py:383
  42.0 6.6 %collective-permute-start.15 = (f32[128,512]{1,0:T(8,128)S(1)}, f32[128,512]{1,0:T(8,128)S(1)}, u32[]{:S(2)}, u32[]{:S(2)}) collective-permute-start(f32[128,512]{1,0:T(8,128)S(1)} %shard_map.97.refs_3_), channel_id=1, source_target_pairs={{0,8},{28,20},{8,16},{20,12},{16,24},{12,4},{1,9},{29,21},{9,17},{... | collective-permute-start | bytes 786440 | tf_op jit(solution)/shard_map/ppermute | solution.py:383
  44.7 6.4 %collective-permute-start.2 = (f32[128,512]{1,0:T(8,128)S(1)}, f32[128,512]{1,0:T(8,128)S(1)}, u32[]{:S(2)}, u32[]{:S(2)}) collective-permute-start(f32[128,512]{1,0:T(8,128)S(1)} %get-tuple-element.38), channel_id=1, source_target_pairs={{0,2},{1,3},{2,0},{3,1},{4,6},{5,7},{6,4},{7,5},{8,10},{9,11},{10,... | collective-permute-start | bytes 786440 | tf_op jit(solution)/shard_map/ppermute | solution.py:309
  46.1 3.5 %collective-permute-start.16 = (f32[128,512]{1,0:T(8,128)S(1)}, f32[128,512]{1,0:T(8,128)S(1)}, u32[]{:S(2)}, u32[]{:S(2)}) collective-permute-start(f32[128,512]{1,0:T(8,128)S(1)} %shard_map.98.refs_5_), channel_id=1, source_target_pairs={{0,4},{4,0},{1,5},{5,1},{2,6},{6,2},{3,7},{7,3},{8,12},{12,8},{9,1... | collective-permute-start | bytes 786440 | tf_op jit(solution)/shard_map/ppermute | solution.py:312
  46.3 4.9 %collective-permute-start.14 = (f32[128,512]{1,0:T(8,128)S(1)}, f32[128,512]{1,0:T(8,128)S(1)}, u32[]{:S(2)}, u32[]{:S(2)}) collective-permute-start(f32[128,512]{1,0:T(8,128)S(1)} %shard_map.100.refs_3_), channel_id=1, source_target_pairs={{8,16},{20,12},{16,24},{12,4},{9,17},{21,13},{17,25},{13,5},{10,18... | collective-permute-start | bytes 786440 | tf_op jit(solution)/shard_map/ppermute | solution.py:383
  49.3 8.8 %collective-permute-start.19 = (f32[128,512]{1,0:T(8,128)S(1)}, f32[128,512]{1,0:T(8,128)S(1)}, u32[]{:S(2)}, u32[]{:S(2)}) collective-permute-start(f32[128,512]{1,0:T(8,128)S(1)} %shard_map.102.refs_4_), channel_id=1, source_target_pairs={{0,4},{4,0},{1,5},{5,1},{2,6},{6,2},{3,7},{7,3},{8,12},{12,8},{9,1... | collective-permute-start | bytes 786440 | tf_op jit(solution)/shard_map/ppermute | solution.py:312
  51.2 7.7 %collective-permute-start.20 = (f32[128,512]{1,0:T(8,128)S(1)}, f32[128,512]{1,0:T(8,128)S(1)}, u32[]{:S(2)}, u32[]{:S(2)}) collective-permute-start(f32[128,512]{1,0:T(8,128)S(1)} %shard_map.107.refs_3_), channel_id=1, source_target_pairs={{0,4},{4,0},{1,5},{5,1},{2,6},{6,2},{3,7},{7,3},{8,12},{12,8},{9,1... | collective-permute-start | bytes 786440 | tf_op jit(solution)/shard_map/ppermute | solution.py:312
  56.8 4.4 %collective-permute-start.24 = (f32[128,512]{1,0:T(8,128)S(1)}, f32[128,512]{1,0:T(8,128)S(1)}, u32[]{:S(2)}, u32[]{:S(2)}) collective-permute-start(f32[128,512]{1,0:T(8,128)S(1)} %shard_map.106.refs_3_.refs_8_.refs_2_), channel_id=1, source_target_pairs={{16,24},{12,4},{17,25},{13,5},{18,26},{14,6},{19,27},{15,7}} | collective-permute-start | bytes 786440 | tf_op jit(solution)/shard_map/ppermute | solution.py:383
  57.4 3.4 %collective-permute-start.21 = (f32[64,512]{1,0:T(8,128)S(1)}, f32[64,512]{1,0:T(8,128)S(1)}, u32[]{:S(2)}, u32[]{:S(2)}) collective-permute-start(f32[64,512]{1,0:T(8,128)S(1)} %get-tuple-element.50), channel_id=1, source_target_pairs={{0,4},{4,0},{1,5},{5,1},{2,6},{6,2},{3,7},{7,3},{8,12},{12,8},{9,1... | collective-permute-start | bytes 393224 | tf_op jit(solution)/shard_map/ppermute | solution.py:312
  60.1 3.9 %collective-permute-start.17 = (f32[128,512]{1,0:T(8,128)S(1)}, f32[128,512]{1,0:T(8,128)S(1)}, u32[]{:S(2)}, u32[]{:S(2)}) collective-permute-start(f32[128,512]{1,0:T(8,128)S(1)} %shard_map.105.refs_2_), channel_id=1, source_target_pairs={{16,24},{12,4},{17,25},{13,5},{18,26},{14,6},{19,27},{15,7}} | collective-permute-start | bytes 786440 | tf_op jit(solution)/shard_map/ppermute | solution.py:383
  61.2 3.9 %collective-permute-start.25 = (f32[128,512]{1,0:T(8,128)S(1)}, f32[128,512]{1,0:T(8,128)S(1)}, u32[]{:S(2)}, u32[]{:S(2)}) collective-permute-start(f32[128,512]{1,0:T(8,128)S(1)} %shard_map.115), channel_id=1, source_target_pairs={{0,4},{4,0},{1,5},{5,1},{2,6},{6,2},{3,7},{7,3},{8,12},{12,8},{9,1... | collective-permute-start | bytes 786440 | tf_op jit(solution)/shard_map/ppermute | solution.py:312
  65.8 4.5 %collective-permute-start.30 = (f32[64,512]{1,0:T(8,128)S(1)}, f32[64,512]{1,0:T(8,128)S(1)}, u32[]{:S(2)}, u32[]{:S(2)}) collective-permute-start(f32[64,512]{1,0:T(8,128)S(1)} %get-tuple-element.58), channel_id=1, source_target_pairs={{0,4},{4,0},{1,5},{5,1},{2,6},{6,2},{3,7},{7,3},{8,12},{12,8},{9,1... | collective-permute-start | bytes 393224 | tf_op jit(solution)/shard_map/ppermute | solution.py:312
  68.1 11.7 %collective-permute-start.28 = (f32[64,512]{1,0:T(8,128)S(1)}, f32[64,512]{1,0:T(8,128)S(1)}, u32[]{:S(2)}, u32[]{:S(2)}) collective-permute-start(f32[64,512]{1,0:T(8,128)S(1)} %shard_map.112.refs_8_), channel_id=1, source_target_pairs={{0,1},{1,0},{2,3},{3,2},{4,5},{5,4},{6,7},{7,6},{8,9},{9,8},{10,11... | collective-permute-start | bytes 393224 | tf_op jit(solution)/shard_map/ppermute | solution.py:309
  69.5 10.2 %collective-permute-start.29 = (f32[64,512]{1,0:T(8,128)S(1)}, f32[64,512]{1,0:T(8,128)S(1)}, u32[]{:S(2)}, u32[]{:S(2)}) collective-permute-start(f32[64,512]{1,0:T(8,128)S(1)} %shard_map.113.refs_9_), channel_id=1, source_target_pairs={{0,3},{1,2},{2,1},{3,0},{4,7},{5,6},{6,5},{7,4},{8,11},{9,10},{10,... | collective-permute-start | bytes 393224 | tf_op jit(solution)/shard_map/ppermute | solution.py:309
  70.3 9.5 %collective-permute-start.31 = (f32[64,512]{1,0:T(8,128)S(1)}, f32[64,512]{1,0:T(8,128)S(1)}, u32[]{:S(2)}, u32[]{:S(2)}) collective-permute-start(f32[64,512]{1,0:T(8,128)S(1)} %shard_map.119), channel_id=1, source_target_pairs={{0,2},{1,3},{2,0},{3,1},{4,6},{5,7},{6,4},{7,5},{8,10},{9,11},{10,... | collective-permute-start | bytes 393224 | tf_op jit(solution)/shard_map/ppermute | solution.py:309
  71.6 3.6 %collective-permute-start.26 = (f32[8,128]{1,0:T(8,128)S(1)}, f32[8,128]{1,0:T(8,128)S(1)}, u32[]{:S(2)}, u32[]{:S(2)}) collective-permute-start(f32[8,128]{1,0:T(8,128)S(1)} %get-tuple-element.56.refs_0_), channel_id=1, source_target_pairs={{0,8},{8,0},{16,24},{24,16},{1,9},{9,1},{17,25},{25,17},{2,10},{10... | collective-permute-start | bytes 12296 | tf_op jit(solution)/shard_map/ppermute | solution.py:440
  75.2 4.5 %collective-permute-start.27 = (f32[8,128]{1,0:T(8,128)S(1)}, f32[8,128]{1,0:T(8,128)S(1)}, u32[]{:S(2)}, u32[]{:S(2)}) collective-permute-start(f32[8,128]{1,0:T(8,128)S(1)} %shard_map.117.refs_0_), channel_id=1, source_target_pairs={{0,16},{8,24},{16,0},{24,8},{1,17},{9,25},{17,1},{25,9},{2,18},{10... | collective-permute-start | bytes 12296 | tf_op jit(solution)/shard_map/ppermute | solution.py:440
  79.9 5.5 %collective-permute-start.32 = (f32[72,512]{1,0:T(8,128)S(1)}, f32[72,512]{1,0:T(8,128)S(1)}, u32[]{:S(2)}, u32[]{:S(2)}) collective-permute-start(f32[72,512]{1,0:T(8,128)S(1)} %shard_map.120.refs_4_), channel_id=1, source_target_pairs={{0,1},{1,0},{2,3},{3,2},{4,5},{5,4},{6,7},{7,6},{8,9},{9,8},{10,11... | collective-permute-start | bytes 442376 | tf_op jit(solution)/shard_map/ppermute | solution.py:309
  81.5 7.1 %collective-permute-start.33 = (f32[72,512]{1,0:T(8,128)S(1)}, f32[72,512]{1,0:T(8,128)S(1)}, u32[]{:S(2)}, u32[]{:S(2)}) collective-permute-start(f32[72,512]{1,0:T(8,128)S(1)} %shard_map.120.refs_4_), channel_id=1, source_target_pairs={{0,2},{1,3},{2,0},{3,1},{4,6},{5,7},{6,4},{7,5},{8,10},{9,11},{10,... | collective-permute-start | bytes 442376 | tf_op jit(solution)/shard_map/ppermute | solution.py:309
  82.0 6.6 %collective-permute-start.34 = (f32[72,512]{1,0:T(8,128)S(1)}, f32[72,512]{1,0:T(8,128)S(1)}, u32[]{:S(2)}, u32[]{:S(2)}) collective-permute-start(f32[72,512]{1,0:T(8,128)S(1)} %shard_map.120.refs_4_), channel_id=1, source_target_pairs={{0,3},{1,2},{2,1},{3,0},{4,7},{5,6},{6,5},{7,4},{8,11},{9,10},{10,... | collective-permute-start | bytes 442376 | tf_op jit(solution)/shard_map/ppermute | solution.py:309
  83.5 6.4 %collective-permute-start.35 = (f32[72,512]{1,0:T(8,128)S(1)}, f32[72,512]{1,0:T(8,128)S(1)}, u32[]{:S(2)}, u32[]{:S(2)}) collective-permute-start(f32[72,512]{1,0:T(8,128)S(1)} %shard_map.120.refs_4_), channel_id=1, source_target_pairs={{0,4},{4,0},{1,5},{5,1},{2,6},{6,2},{3,7},{7,3},{8,12},{12,8},{9,1... | collective-permute-start | bytes 442376 | tf_op jit(solution)/shard_map/ppermute | solution.py:312
  85.4 4.4 %collective-permute-start.36 = (f32[72,512]{1,0:T(8,128)S(1)}, f32[72,512]{1,0:T(8,128)S(1)}, u32[]{:S(2)}, u32[]{:S(2)}) collective-permute-start(f32[72,512]{1,0:T(8,128)S(1)} %collective-permute-done.32.refs_5_), channel_id=1, source_target_pairs={{0,4},{4,0},{1,5},{5,1},{2,6},{6,2},{3,7},{7,3},{8,12},{12,8},{9,1... | collective-permute-start | bytes 442376 | tf_op jit(solution)/shard_map/ppermute | solution.py:312
  (12 other events, 43.3 us)

commit v6 on v5

--- a/solution.py
+++ b/solution.py
@@ -10,6 +10,7 @@
 LEVELS = 4
 BLOCK = 128
 LOSS_ROWS = 8
+LOSS_PART = 4
 GELU_C = 0.7978845608028654
 GELU_A = 0.044715
 
@@ -158,7 +159,7 @@
     rows = pre.shape[0]
     out[:rows, :] = jnp.where(hit, deriv * total_of([t[...] for t in terms]), 0.0)
     out[rows:, :] = jnp.zeros_like(out[rows:, :])
-    out[rows:, :BLOCK] = loss[...]
+    out[rows:, :BLOCK] = loss[:LOSS_ROWS, :BLOCK]
 
 
 def running_parts(act, dict_ref):
@@ -257,6 +258,11 @@
         give_out[:, cols] = jnp.where(upward, gact[half:, :], gact[:half, :])
 
 
+def spread_kernel(loss, out):
+    out[...] = jnp.zeros_like(out)
+    out[:LOSS_ROWS, :BLOCK] = loss[...]
+
+
 def add_kernel(*refs):
     refs[-1][...] = total_of([ref[...] for ref in refs[:-1]])
 
@@ -336,6 +342,7 @@
         (partial, partial_other, enc_bias.reshape(1, lats), active_blocks.T),
         after=(dict_wide,),
     )
+    gathered = [act] + [across(act, q) for q in range(1, n_tok)]
     bias_here, *pieces = call(
         pieces_kernel,
         [f32(1, width)] + [f32(rows, width)] * n_tok,
@@ -365,12 +372,11 @@
             pairs.append((2 * (n_lat - 1 - p) + 1, 2 * (n_lat - 2 - p) + 1))
         if step == 0:
             acts[order[0]] = call(round_kernel, [bf16(rows, lats)], (act,))[0]
-            message = project(order[0], (dict_here, dict_other))
-            arrived = lax.ppermute(message, ("lat", "wid"), pairs)
-            for side in range(2):
-                sums[side].append((message, side))
-                got[side].append((arrived, side))
-            sent = [arrived]
+            for side, dict_ref in enumerate((dict_here, dict_other)):
+                message = project(order[0], (dict_ref,))
+                sums[side].append((message, 0))
+                got[side].append((lax.ppermute(message, ("lat", "wid"), pairs), 0))
+                sent = [message]
         elif step < steps:
             for side in range(2):
                 items = [got[side][-1], *[sums[side][step - p] for p in at]]
@@ -384,15 +390,14 @@
                 sent = [message]
         if step + 1 < n_tok:
             q = order[step + 1]
-            gathered = across(act, q)
-            acts[q] = call(round_kernel, [bf16(rows, lats)], (gathered,), after=sent)[0]
+            acts[q] = call(round_kernel, [bf16(rows, lats)], (gathered[q],), after=sent)[0]
             for side, dict_ref in enumerate((dict_here, dict_other)):
                 sums[side].append((project(q, (dict_ref,)), 0))
         ready = []
         c = step - (n_lat - 1)
         if c >= 0:
             chosen = []
-            for side in (1, 0):
+            for side in (1, 0) if step < steps else (0, 1):
                 items = [got[side][c + p - 1] for p in places]
                 if n_lat > 4:
                     items = [a[:, col * width : (col + 1) * width] for a, col in items]
@@ -402,12 +407,13 @@
                         functools.partial(choose_kernel, places, [col for _, col in items]),
                         [f32(rows, width)],
                         [array for array, _ in items],
-                        after=sent if step < steps else ready_before,
+                        after=sent if step < steps else ready_before + chosen,
                     )[0]
                 )
-            hands.append((swap(chosen[0]), chosen[1]))
+            hand, mine = chosen if step < steps else chosen[::-1]
+            hands.append((swap(hand), mine))
             ready += chosen
-        stages = [c - 1] if step < steps - 1 else [c - 1, c] if step < steps else [c]
+        stages = [c - 1] if step < steps else [c - 1, c]
         for c in stages:
             if c < 0:
                 continue
@@ -421,7 +427,7 @@
             loss = (loss_here,)
             gives.append((keep, swap(give)))
             ready.append(errs[q])
-        stages = [c - 2] if step < steps - 1 else [c - 2, c - 1, c] if step < steps else [c]
+        stages = range(n_tok) if step == steps else []
         for c in stages:
             if c < 0:
                 continue
@@ -435,10 +441,10 @@
             waits[step + 1] += ready
         ready_before = ready
 
-    loss, gap = loss[0], 1
+    loss, gap = call(spread_kernel, [f32(rows // LOSS_PART, lats)], loss)[0], 1
     while gap < n_lat:
         other = lax.ppermute(loss, "lat", [(p, p ^ gap) for p in range(n_lat)])
-        loss = call(add_kernel, [f32(LOSS_ROWS, BLOCK)], (loss, other))[0]
+        loss = call(add_kernel, [f32(*loss.shape)], (loss, other))[0]
         gap *= 2
 
     g_pre = call(

time: 91.8 us -> 86.6 us (0.943)
  waiting for transfers between devices: 24.2 us -> 14.4 us
  starting transfers between devices: 55 us -> 58.5 us
    ppermute x12, waiting for transfers between devices: 11.1 us -> 5.22 us  [across(): return lax.ppermute(array, 'tok', [(t, t ^ q) for t in range(n_tok)])]
    ppermute x10 -> x12, starting transfers between devices: 17.8 us -> 23.4 us  [body(): got[side].append((lax.ppermute(message, ('lat', 'wid'), pairs), 0))]
    ppermute x1 -> x0, starting transfers between devices: 4.87 us -> none  [body(): arrived = lax.ppermute(message, ('lat', 'wid'), pairs)]
    ppermute x14, waiting for transfers between devices: 4.85 us -> 1.48 us  [swap(): return lax.ppermute(array, 'wid', [(w, w ^ 1) for w in range(n_wid)])]
    ppermute x12, starting transfers between devices: 17.1 us -> 19.6 us  [across(): return lax.ppermute(array, 'tok', [(t, t ^ q) for t in range(n_tok)])]
    pallas_call x46 -> x48, Pallas kernels: 11.1 us -> 11.2 us  [call(): pl.pallas_call(run, out_shape=outs, in_specs=list(specs or [VMEM] * len(a...]
  transfers between devices with their start and end apart: 39 -> 40, of which waited for: 13 -> 11; matrix products, arithmetic and copies ran while one was open for 0% -> 0% of each run, Pallas kernels for 6% -> 8%
where the time goes in v6:
time: 86.6 us; the launch traced here: 85.4 us
  starting transfers between devices  58.5 us (68%)
  waiting for transfers between devices  14.4 us (17%)
  Pallas kernels  11.2 us (13%)
  between operations  1.25 us (1%)
    ppermute x12, starting transfers between devices, body(): got[side].append((lax.ppermute(message, ('lat', 'wid'), pairs), 0))  23.4 us
    ppermute x12, starting transfers between devices, across(): return lax.ppermute(array, 'tok', [(t, t ^ q) for t in range(n_tok)])  19.6 us
    ppermute x14, starting transfers between devices, swap(): return lax.ppermute(array, 'wid', [(w, w ^ 1) for w in range(n_wid)])  13.7 us
    pallas_call x48, Pallas kernels, call(): pl.pallas_call(run, out_shape=outs, in_specs=list(specs or [VMEM] * len(a...  11.2 us
    ppermute x2, waiting for transfers between devices, body(): other = lax.ppermute(loss, 'lat', [(p, p ^ gap) for p in range(n_lat)])  6.09 us
    ppermute x12, waiting for transfers between devices, across(): return lax.ppermute(array, 'tok', [(t, t ^ q) for t in range(n_tok)])  5.22 us
    ppermute x2, starting transfers between devices, body(): other = lax.ppermute(loss, 'lat', [(p, p ^ gap) for p in range(n_lat)])  1.9 us
  transfers between devices with their start and end apart: 40, of which 11 were waited for; matrix products, arithmetic and copies ran while one was open for 0% of the time, Pallas kernels for 8%

profile of v6, /device:TPU:0, one launch (start us, length us, event | category | flops | bytes accessed | tf_op | source)
XLA Modules:
  0.0 85.4 jit_solution(7920846937942062559)
XLA Ops:
  0.7 2.9 %shard_map.77 = (f32[128,512]{1,0:T(8,128)S(1)}, bf16[512,512]{1,0:T(8,128)(2,1)S(1)}) custom-call(bf16[128,2048]{1,0:T(8,128)(2,1)} %refs_0_.3, bf16[512,2048]{1,0:T(8,128)(2,1)} %refs_1_.1), custom_call_target="tpu_custom_call" | custom-call | bytes 1024 | tf_op jit(solution)/shard_map/pallas_call | solution.py:37
  4.1 1.2 %collective-permute-done.refs_2_.refs_1_ = f32[128,512]{1,0:T(8,128)S(1)} collective-permute-done((f32[128,512]{1,0:T(8,128)S(1)}, f32[128,512]{1,0:T(8,128)S(1)}, u32[]{:S(2)}, u32[]{:S(2)}) %collective-permute-start) | collective-permute-done | bytes 262176 | tf_op jit(solution)/shard_map/ppermute | solution.py:318
  6.1 2.7 %collective-permute-start.7 = (f32[128,512]{1,0:T(8,128)S(1)}, f32[128,512]{1,0:T(8,128)S(1)}, u32[]{:S(2)}, u32[]{:S(2)}) collective-permute-start(f32[128,512]{1,0:T(8,128)S(1)} %get-tuple-element.35.refs_2_.refs_0_), channel_id=1, source_target_pairs={{0,1},{1,0},{2,3},{3,2},{4,5},{5,4},{6,7},{7,6},{8,9},{9,8},{10,11... | collective-permute-start | bytes 786440 | tf_op jit(solution)/shard_map/ppermute | solution.py:315
  9.1 3.5 %collective-permute-start.10 = (f32[128,512]{1,0:T(8,128)S(1)}, f32[128,512]{1,0:T(8,128)S(1)}, u32[]{:S(2)}, u32[]{:S(2)}) collective-permute-start(f32[128,512]{1,0:T(8,128)S(1)} %shard_map.88.refs_2_.refs_3_), channel_id=1, source_target_pairs={{0,8},{28,20},{1,9},{29,21},{2,10},{30,22},{3,11},{31,23}} | collective-permute-start | bytes 786440 | tf_op jit(solution)/shard_map/ppermute | solution.py:378
  12.9 1.3 %collective-permute-start.6 = (f32[128,512]{1,0:T(8,128)S(1)}, f32[128,512]{1,0:T(8,128)S(1)}, u32[]{:S(2)}, u32[]{:S(2)}) collective-permute-start(f32[128,512]{1,0:T(8,128)S(1)} %shard_map.82.refs_1_.refs_2_.refs_3_), channel_id=1, source_target_pairs={{0,8},{28,20},{1,9},{29,21},{2,10},{30,22},{3,11},{31,23}} | collective-permute-start | bytes 786440 | tf_op jit(solution)/shard_map/ppermute | solution.py:378
  14.2 1.6 %collective-permute-start.9 = (f32[128,512]{1,0:T(8,128)S(1)}, f32[128,512]{1,0:T(8,128)S(1)}, u32[]{:S(2)}, u32[]{:S(2)}) collective-permute-start(f32[128,512]{1,0:T(8,128)S(1)} %get-tuple-element.35.refs_2_.refs_0_), channel_id=1, source_target_pairs={{0,3},{1,2},{2,1},{3,0},{4,7},{5,6},{6,5},{7,4},{8,11},{9,10},{10,... | collective-permute-start | bytes 786440 | tf_op jit(solution)/shard_map/ppermute | solution.py:315
  16.5 4.4 %collective-permute-start.11 = (f32[128,512]{1,0:T(8,128)S(1)}, f32[128,512]{1,0:T(8,128)S(1)}, u32[]{:S(2)}, u32[]{:S(2)}) collective-permute-start(f32[128,512]{1,0:T(8,128)S(1)} %shard_map.90), channel_id=1, source_target_pairs={{0,8},{28,20},{8,16},{20,12},{1,9},{29,21},{9,17},{21,13},{2,10},{... | collective-permute-start | bytes 786440 | tf_op jit(solution)/shard_map/ppermute | solution.py:389
  21.2 2.5 %collective-permute-start.8 = (f32[128,512]{1,0:T(8,128)S(1)}, f32[128,512]{1,0:T(8,128)S(1)}, u32[]{:S(2)}, u32[]{:S(2)}) collective-permute-start(f32[128,512]{1,0:T(8,128)S(1)} %shard_map.85.refs_1_.refs_4_), channel_id=1, source_target_pairs={{0,8},{28,20},{8,16},{20,12},{1,9},{29,21},{9,17},{21,13},{2,10},{... | collective-permute-start | bytes 786440 | tf_op jit(solution)/shard_map/ppermute | solution.py:389
  23.7 2.0 %collective-permute-start.4 = (f32[128,512]{1,0:T(8,128)S(1)}, f32[128,512]{1,0:T(8,128)S(1)}, u32[]{:S(2)}, u32[]{:S(2)}) collective-permute-start(f32[128,512]{1,0:T(8,128)S(1)} %get-tuple-element.35.refs_2_.refs_0_), channel_id=1, source_target_pairs={{0,2},{1,3},{2,0},{3,1},{4,6},{5,7},{6,4},{7,5},{8,10},{9,11},{10,... | collective-permute-start | bytes 786440 | tf_op jit(solution)/shard_map/ppermute | solution.py:315
  25.8 1.6 %collective-permute-start.1 = (f32[128,512]{1,0:T(8,128)S(1)}, f32[128,512]{1,0:T(8,128)S(1)}, u32[]{:S(2)}, u32[]{:S(2)}) collective-permute-start(f32[128,512]{1,0:T(8,128)S(1)} %get-tuple-element.37), channel_id=1, source_target_pairs={{0,1},{1,0},{2,3},{3,2},{4,5},{5,4},{6,7},{7,6},{8,9},{9,8},{10,11... | collective-permute-start | bytes 786440 | tf_op jit(solution)/shard_map/ppermute | solution.py:315
  27.8 1.9 %collective-permute-start.12 = (f32[128,512]{1,0:T(8,128)S(1)}, f32[128,512]{1,0:T(8,128)S(1)}, u32[]{:S(2)}, u32[]{:S(2)}) collective-permute-start(f32[128,512]{1,0:T(8,128)S(1)} %shard_map.92.refs_4_), channel_id=1, source_target_pairs={{0,8},{28,20},{8,16},{20,12},{16,24},{12,4},{1,9},{29,21},{9,17},{... | collective-permute-start | bytes 786440 | tf_op jit(solution)/shard_map/ppermute | solution.py:389
  30.1 2.0 %collective-permute-start.14 = (f32[128,512]{1,0:T(8,128)S(1)}, f32[128,512]{1,0:T(8,128)S(1)}, u32[]{:S(2)}, u32[]{:S(2)}) collective-permute-start(f32[128,512]{1,0:T(8,128)S(1)} %shard_map.93.refs_1_.refs_4_), channel_id=1, source_target_pairs={{0,8},{28,20},{8,16},{20,12},{16,24},{12,4},{1,9},{29,21},{9,17},{... | collective-permute-start | bytes 786440 | tf_op jit(solution)/shard_map/ppermute | solution.py:389
  32.0 2.9 %collective-permute-start.3 = (f32[128,512]{1,0:T(8,128)S(1)}, f32[128,512]{1,0:T(8,128)S(1)}, u32[]{:S(2)}, u32[]{:S(2)}) collective-permute-start(f32[128,512]{1,0:T(8,128)S(1)} %get-tuple-element.39), channel_id=1, source_target_pairs={{0,3},{1,2},{2,1},{3,0},{4,7},{5,6},{6,5},{7,4},{8,11},{9,10},{10,... | collective-permute-start | bytes 786440 | tf_op jit(solution)/shard_map/ppermute | solution.py:315
  35.4 2.6 %collective-permute-start.13 = (f32[128,512]{1,0:T(8,128)S(1)}, f32[128,512]{1,0:T(8,128)S(1)}, u32[]{:S(2)}, u32[]{:S(2)}) collective-permute-start(f32[128,512]{1,0:T(8,128)S(1)} %shard_map.96.refs_4_), channel_id=1, source_target_pairs={{0,8},{28,20},{8,16},{20,12},{16,24},{12,4},{1,9},{29,21},{9,17},{... | collective-permute-start | bytes 786440 | tf_op jit(solution)/shard_map/ppermute | solution.py:389
  38.4 2.4 %collective-permute-start.16 = (f32[128,512]{1,0:T(8,128)S(1)}, f32[128,512]{1,0:T(8,128)S(1)}, u32[]{:S(2)}, u32[]{:S(2)}) collective-permute-start(f32[128,512]{1,0:T(8,128)S(1)} %shard_map.98.refs_3_), channel_id=1, source_target_pairs={{0,8},{28,20},{8,16},{20,12},{16,24},{12,4},{1,9},{29,21},{9,17},{... | collective-permute-start | bytes 786440 | tf_op jit(solution)/shard_map/ppermute | solution.py:389
  40.8 1.5 %collective-permute-start.2 = (f32[128,512]{1,0:T(8,128)S(1)}, f32[128,512]{1,0:T(8,128)S(1)}, u32[]{:S(2)}, u32[]{:S(2)}) collective-permute-start(f32[128,512]{1,0:T(8,128)S(1)} %get-tuple-element.38), channel_id=1, source_target_pairs={{0,2},{1,3},{2,0},{3,1},{4,6},{5,7},{6,4},{7,5},{8,10},{9,11},{10,... | collective-permute-start | bytes 786440 | tf_op jit(solution)/shard_map/ppermute | solution.py:315
  43.3 1.4 %collective-permute-done.16.refs_0_.refs_2_.refs_1_ = f32[128,512]{1,0:T(8,128)S(1)} collective-permute-done((f32[128,512]{1,0:T(8,128)S(1)}, f32[128,512]{1,0:T(8,128)S(1)}, u32[]{:S(2)}, u32[]{:S(2)}) %collective-permute-start.16) | collective-permute-done | bytes 262176 | tf_op jit(solution)/shard_map/ppermute | solution.py:389
  46.5 0.7 collective-permute-done.2.refs_3_.refs_2_
  48.7 5.7 %collective-permute-start.23 = (f32[128,512]{1,0:T(8,128)S(1)}, f32[128,512]{1,0:T(8,128)S(1)}, u32[]{:S(2)}, u32[]{:S(2)}) collective-permute-start(f32[128,512]{1,0:T(8,128)S(1)} %shard_map.108.refs_3_), channel_id=1, source_target_pairs={{0,4},{4,0},{1,5},{5,1},{2,6},{6,2},{3,7},{7,3},{8,12},{12,8},{9,1... | collective-permute-start | bytes 786440 | tf_op jit(solution)/shard_map/ppermute | solution.py:318
  55.2 4.9 %collective-permute-start.22 = (f32[128,512]{1,0:T(8,128)S(1)}, f32[128,512]{1,0:T(8,128)S(1)}, u32[]{:S(2)}, u32[]{:S(2)}) collective-permute-start(f32[128,512]{1,0:T(8,128)S(1)} %shard_map.112), channel_id=1, source_target_pairs={{0,4},{4,0},{1,5},{5,1},{2,6},{6,2},{3,7},{7,3},{8,12},{12,8},{9,1... | collective-permute-start | bytes 786440 | tf_op jit(solution)/shard_map/ppermute | solution.py:318
  62.6 1.6 %collective-permute-start.28 = (f32[64,512]{1,0:T(8,128)S(1)}, f32[64,512]{1,0:T(8,128)S(1)}, u32[]{:S(2)}, u32[]{:S(2)}) collective-permute-start(f32[64,512]{1,0:T(8,128)S(1)} %shard_map.119), channel_id=1, source_target_pairs={{0,1},{1,0},{2,3},{3,2},{4,5},{5,4},{6,7},{7,6},{8,9},{9,8},{10,11... | collective-permute-start | bytes 393224 | tf_op jit(solution)/shard_map/ppermute | solution.py:315
  64.9 1.5 %collective-permute-start.32 = (f32[64,512]{1,0:T(8,128)S(1)}, f32[64,512]{1,0:T(8,128)S(1)}, u32[]{:S(2)}, u32[]{:S(2)}) collective-permute-start(f32[64,512]{1,0:T(8,128)S(1)} %shard_map.121), channel_id=1, source_target_pairs={{0,2},{1,3},{2,0},{3,1},{4,6},{5,7},{6,4},{7,5},{8,10},{9,11},{10,... | collective-permute-start | bytes 393224 | tf_op jit(solution)/shard_map/ppermute | solution.py:315
  66.4 2.1 %collective-permute-done.24.refs_1_ = f32[32,512]{1,0:T(8,128)S(1)} collective-permute-done((f32[32,512]{1,0:T(8,128)S(1)}, f32[32,512]{1,0:T(8,128)S(1)}, u32[]{:S(2)}, u32[]{:S(2)}) %collective-permute-start.24) | collective-permute-done | bytes 65568 | tf_op jit(solution)/shard_map/ppermute | solution.py:446
  68.5 1.9 %collective-permute-start.25 = (f32[32,512]{1,0:T(8,128)S(1)}, f32[32,512]{1,0:T(8,128)S(1)}, u32[]{:S(2)}, u32[]{:S(2)}) collective-permute-start(f32[32,512]{1,0:T(8,128)S(1)} %shard_map.116.refs_0_), channel_id=1, source_target_pairs={{0,16},{8,24},{16,0},{24,8},{1,17},{9,25},{17,1},{25,9},{2,18},{10... | collective-permute-start | bytes 196616 | tf_op jit(solution)/shard_map/ppermute | solution.py:446
  70.4 4.0 %collective-permute-done.25.refs_1_ = f32[32,512]{1,0:T(8,128)S(1)} collective-permute-done((f32[32,512]{1,0:T(8,128)S(1)}, f32[32,512]{1,0:T(8,128)S(1)}, u32[]{:S(2)}, u32[]{:S(2)}) %collective-permute-start.25) | collective-permute-done | bytes 65568 | tf_op jit(solution)/shard_map/ppermute | solution.py:446
  74.6 1.4 %collective-permute-start.35 = (f32[72,512]{1,0:T(8,128)S(1)}, f32[72,512]{1,0:T(8,128)S(1)}, u32[]{:S(2)}, u32[]{:S(2)}) collective-permute-start(f32[72,512]{1,0:T(8,128)S(1)} %shard_map.122.refs_4_), channel_id=1, source_target_pairs={{0,3},{1,2},{2,1},{3,0},{4,7},{5,6},{6,5},{7,4},{8,11},{9,10},{10,... | collective-permute-start | bytes 442376 | tf_op jit(solution)/shard_map/ppermute | solution.py:315
  75.9 0.7 collective-permute-start.34
  76.7 1.5 %collective-permute-start.33 = (f32[72,512]{1,0:T(8,128)S(1)}, f32[72,512]{1,0:T(8,128)S(1)}, u32[]{:S(2)}, u32[]{:S(2)}) collective-permute-start(f32[72,512]{1,0:T(8,128)S(1)} %shard_map.122.refs_4_), channel_id=1, source_target_pairs={{0,1},{1,0},{2,3},{3,2},{4,5},{5,4},{6,7},{7,6},{8,9},{9,8},{10,11... | collective-permute-start | bytes 442376 | tf_op jit(solution)/shard_map/ppermute | solution.py:315
  78.1 3.2 %collective-permute-done.35.refs_7_ = f32[72,512]{1,0:T(8,128)S(1)} collective-permute-done((f32[72,512]{1,0:T(8,128)S(1)}, f32[72,512]{1,0:T(8,128)S(1)}, u32[]{:S(2)}, u32[]{:S(2)}) %collective-permute-start.35) | collective-permute-done | bytes 147488 | tf_op jit(solution)/shard_map/ppermute | solution.py:315
  81.4 1.1 %collective-permute-done.34.refs_6_ = f32[72,512]{1,0:T(8,128)S(1)} collective-permute-done((f32[72,512]{1,0:T(8,128)S(1)}, f32[72,512]{1,0:T(8,128)S(1)}, u32[]{:S(2)}, u32[]{:S(2)}) %collective-permute-start.34) | collective-permute-done | bytes 147488 | tf_op jit(solution)/shard_map/ppermute | solution.py:315
  83.0 0.8 shard_map.123.refs_12_
  84.1 1.3 %shard_map.124 = (bf16[512,512]{1,0:T(8,128)(2,1)}, f32[4]{0:T(128)}) custom-call(f32[128,512]{1,0:T(8,128)S(1)} %get-tuple-element.36.refs_2_.refs_0_, f32[128,512]{1,0:T(8,128)S(1)} %collective-permute-done.1.refs_5_.refs_2_.refs_1_, f32[128,512]{1,0:T(8,128)S(1)} %collective-permute-done.2.refs_3_.refs_2_, ...), custom_call_target="tpu_custom_call" | custom-call | bytes 1024 | tf_op jit(solution)/shard_map/pallas_call | solution.py:37
  (106 shorter events, 13.3 us)
Async XLA Ops:
  5.4 7.2 %collective-permute-start.5 = (f32[512,512]{1,0:T(8,128)S(1)}, f32[512,512]{1,0:T(8,128)S(1)}, u32[]{:S(2)}, u32[]{:S(2)}) collective-permute-start(f32[512,512]{1,0:T(8,128)S(1)} %get-tuple-element.34.refs_4_), channel_id=1, source_target_pairs={{0,4},{4,0},{1,5},{5,1},{2,6},{6,2},{3,7},{7,3},{8,12},{12,8},{9,1... | collective-permute-start | bytes 3145736 | tf_op jit(solution)/shard_map/ppermute | solution.py:318
  6.1 9.8 %collective-permute-start.7 = (f32[128,512]{1,0:T(8,128)S(1)}, f32[128,512]{1,0:T(8,128)S(1)}, u32[]{:S(2)}, u32[]{:S(2)}) collective-permute-start(f32[128,512]{1,0:T(8,128)S(1)} %get-tuple-element.35.refs_2_.refs_0_), channel_id=1, source_target_pairs={{0,1},{1,0},{2,3},{3,2},{4,5},{5,4},{6,7},{7,6},{8,9},{9,8},{10,11... | collective-permute-start | bytes 786440 | tf_op jit(solution)/shard_map/ppermute | solution.py:315
  9.1 7.4 %collective-permute-start.10 = (f32[128,512]{1,0:T(8,128)S(1)}, f32[128,512]{1,0:T(8,128)S(1)}, u32[]{:S(2)}, u32[]{:S(2)}) collective-permute-start(f32[128,512]{1,0:T(8,128)S(1)} %shard_map.88.refs_2_.refs_3_), channel_id=1, source_target_pairs={{0,8},{28,20},{1,9},{29,21},{2,10},{30,22},{3,11},{31,23}} | collective-permute-start | bytes 786440 | tf_op jit(solution)/shard_map/ppermute | solution.py:378
  12.9 8.3 %collective-permute-start.6 = (f32[128,512]{1,0:T(8,128)S(1)}, f32[128,512]{1,0:T(8,128)S(1)}, u32[]{:S(2)}, u32[]{:S(2)}) collective-permute-start(f32[128,512]{1,0:T(8,128)S(1)} %shard_map.82.refs_1_.refs_2_.refs_3_), channel_id=1, source_target_pairs={{0,8},{28,20},{1,9},{29,21},{2,10},{30,22},{3,11},{31,23}} | collective-permute-start | bytes 786440 | tf_op jit(solution)/shard_map/ppermute | solution.py:378
  14.2 13.2 %collective-permute-start.9 = (f32[128,512]{1,0:T(8,128)S(1)}, f32[128,512]{1,0:T(8,128)S(1)}, u32[]{:S(2)}, u32[]{:S(2)}) collective-permute-start(f32[128,512]{1,0:T(8,128)S(1)} %get-tuple-element.35.refs_2_.refs_0_), channel_id=1, source_target_pairs={{0,3},{1,2},{2,1},{3,0},{4,7},{5,6},{6,5},{7,4},{8,11},{9,10},{10,... | collective-permute-start | bytes 786440 | tf_op jit(solution)/shard_map/ppermute | solution.py:315
  16.5 11.2 %collective-permute-start.11 = (f32[128,512]{1,0:T(8,128)S(1)}, f32[128,512]{1,0:T(8,128)S(1)}, u32[]{:S(2)}, u32[]{:S(2)}) collective-permute-start(f32[128,512]{1,0:T(8,128)S(1)} %shard_map.90), channel_id=1, source_target_pairs={{0,8},{28,20},{8,16},{20,12},{1,9},{29,21},{9,17},{21,13},{2,10},{... | collective-permute-start | bytes 786440 | tf_op jit(solution)/shard_map/ppermute | solution.py:389
  21.2 8.8 %collective-permute-start.8 = (f32[128,512]{1,0:T(8,128)S(1)}, f32[128,512]{1,0:T(8,128)S(1)}, u32[]{:S(2)}, u32[]{:S(2)}) collective-permute-start(f32[128,512]{1,0:T(8,128)S(1)} %shard_map.85.refs_1_.refs_4_), channel_id=1, source_target_pairs={{0,8},{28,20},{8,16},{20,12},{1,9},{29,21},{9,17},{21,13},{2,10},{... | collective-permute-start | bytes 786440 | tf_op jit(solution)/shard_map/ppermute | solution.py:389
  23.7 11.3 %collective-permute-start.4 = (f32[128,512]{1,0:T(8,128)S(1)}, f32[128,512]{1,0:T(8,128)S(1)}, u32[]{:S(2)}, u32[]{:S(2)}) collective-permute-start(f32[128,512]{1,0:T(8,128)S(1)} %get-tuple-element.35.refs_2_.refs_0_), channel_id=1, source_target_pairs={{0,2},{1,3},{2,0},{3,1},{4,6},{5,7},{6,4},{7,5},{8,10},{9,11},{10,... | collective-permute-start | bytes 786440 | tf_op jit(solution)/shard_map/ppermute | solution.py:315
  25.8 9.5 %collective-permute-start.1 = (f32[128,512]{1,0:T(8,128)S(1)}, f32[128,512]{1,0:T(8,128)S(1)}, u32[]{:S(2)}, u32[]{:S(2)}) collective-permute-start(f32[128,512]{1,0:T(8,128)S(1)} %get-tuple-element.37), channel_id=1, source_target_pairs={{0,1},{1,0},{2,3},{3,2},{4,5},{5,4},{6,7},{7,6},{8,9},{9,8},{10,11... | collective-permute-start | bytes 786440 | tf_op jit(solution)/shard_map/ppermute | solution.py:315
  27.8 7.5 %collective-permute-start.12 = (f32[128,512]{1,0:T(8,128)S(1)}, f32[128,512]{1,0:T(8,128)S(1)}, u32[]{:S(2)}, u32[]{:S(2)}) collective-permute-start(f32[128,512]{1,0:T(8,128)S(1)} %shard_map.92.refs_4_), channel_id=1, source_target_pairs={{0,8},{28,20},{8,16},{20,12},{16,24},{12,4},{1,9},{29,21},{9,17},{... | collective-permute-start | bytes 786440 | tf_op jit(solution)/shard_map/ppermute | solution.py:389
  30.1 8.2 %collective-permute-start.14 = (f32[128,512]{1,0:T(8,128)S(1)}, f32[128,512]{1,0:T(8,128)S(1)}, u32[]{:S(2)}, u32[]{:S(2)}) collective-permute-start(f32[128,512]{1,0:T(8,128)S(1)} %shard_map.93.refs_1_.refs_4_), channel_id=1, source_target_pairs={{0,8},{28,20},{8,16},{20,12},{16,24},{12,4},{1,9},{29,21},{9,17},{... | collective-permute-start | bytes 786440 | tf_op jit(solution)/shard_map/ppermute | solution.py:389
  32.0 10.5 %collective-permute-start.3 = (f32[128,512]{1,0:T(8,128)S(1)}, f32[128,512]{1,0:T(8,128)S(1)}, u32[]{:S(2)}, u32[]{:S(2)}) collective-permute-start(f32[128,512]{1,0:T(8,128)S(1)} %get-tuple-element.39), channel_id=1, source_target_pairs={{0,3},{1,2},{2,1},{3,0},{4,7},{5,6},{6,5},{7,4},{8,11},{9,10},{10,... | collective-permute-start | bytes 786440 | tf_op jit(solution)/shard_map/ppermute | solution.py:315
  35.4 7.2 %collective-permute-start.13 = (f32[128,512]{1,0:T(8,128)S(1)}, f32[128,512]{1,0:T(8,128)S(1)}, u32[]{:S(2)}, u32[]{:S(2)}) collective-permute-start(f32[128,512]{1,0:T(8,128)S(1)} %shard_map.96.refs_4_), channel_id=1, source_target_pairs={{0,8},{28,20},{8,16},{20,12},{16,24},{12,4},{1,9},{29,21},{9,17},{... | collective-permute-start | bytes 786440 | tf_op jit(solution)/shard_map/ppermute | solution.py:389
  38.4 6.3 %collective-permute-start.16 = (f32[128,512]{1,0:T(8,128)S(1)}, f32[128,512]{1,0:T(8,128)S(1)}, u32[]{:S(2)}, u32[]{:S(2)}) collective-permute-start(f32[128,512]{1,0:T(8,128)S(1)} %shard_map.98.refs_3_), channel_id=1, source_target_pairs={{0,8},{28,20},{8,16},{20,12},{16,24},{12,4},{1,9},{29,21},{9,17},{... | collective-permute-start | bytes 786440 | tf_op jit(solution)/shard_map/ppermute | solution.py:389
  40.8 6.4 %collective-permute-start.2 = (f32[128,512]{1,0:T(8,128)S(1)}, f32[128,512]{1,0:T(8,128)S(1)}, u32[]{:S(2)}, u32[]{:S(2)}) collective-permute-start(f32[128,512]{1,0:T(8,128)S(1)} %get-tuple-element.38), channel_id=1, source_target_pairs={{0,2},{1,3},{2,0},{3,1},{4,6},{5,7},{6,4},{7,5},{8,10},{9,11},{10,... | collective-permute-start | bytes 786440 | tf_op jit(solution)/shard_map/ppermute | solution.py:315
  42.4 3.5 %collective-permute-start.17 = (f32[128,512]{1,0:T(8,128)S(1)}, f32[128,512]{1,0:T(8,128)S(1)}, u32[]{:S(2)}, u32[]{:S(2)}) collective-permute-start(f32[128,512]{1,0:T(8,128)S(1)} %shard_map.99.refs_5_), channel_id=1, source_target_pairs={{0,4},{4,0},{1,5},{5,1},{2,6},{6,2},{3,7},{7,3},{8,12},{12,8},{9,1... | collective-permute-start | bytes 786440 | tf_op jit(solution)/shard_map/ppermute | solution.py:318
  42.6 4.7 %collective-permute-start.15 = (f32[128,512]{1,0:T(8,128)S(1)}, f32[128,512]{1,0:T(8,128)S(1)}, u32[]{:S(2)}, u32[]{:S(2)}) collective-permute-start(f32[128,512]{1,0:T(8,128)S(1)} %shard_map.101.refs_3_), channel_id=1, source_target_pairs={{8,16},{20,12},{16,24},{12,4},{9,17},{21,13},{17,25},{13,5},{10,18... | collective-permute-start | bytes 786440 | tf_op jit(solution)/shard_map/ppermute | solution.py:389
  45.4 9.0 %collective-permute-start.20 = (f32[128,512]{1,0:T(8,128)S(1)}, f32[128,512]{1,0:T(8,128)S(1)}, u32[]{:S(2)}, u32[]{:S(2)}) collective-permute-start(f32[128,512]{1,0:T(8,128)S(1)} %shard_map.103.refs_4_), channel_id=1, source_target_pairs={{0,4},{4,0},{1,5},{5,1},{2,6},{6,2},{3,7},{7,3},{8,12},{12,8},{9,1... | collective-permute-start | bytes 786440 | tf_op jit(solution)/shard_map/ppermute | solution.py:318
  47.3 7.8 %collective-permute-start.18 = (f32[128,512]{1,0:T(8,128)S(1)}, f32[128,512]{1,0:T(8,128)S(1)}, u32[]{:S(2)}, u32[]{:S(2)}) collective-permute-start(f32[128,512]{1,0:T(8,128)S(1)} %shard_map.106.refs_2_), channel_id=1, source_target_pairs={{16,24},{12,4},{17,25},{13,5},{18,26},{14,6},{19,27},{15,7}} | collective-permute-start | bytes 786440 | tf_op jit(solution)/shard_map/ppermute | solution.py:389
  48.0 7.2 %collective-permute-start.21 = (f32[128,512]{1,0:T(8,128)S(1)}, f32[128,512]{1,0:T(8,128)S(1)}, u32[]{:S(2)}, u32[]{:S(2)}) collective-permute-start(f32[128,512]{1,0:T(8,128)S(1)} %shard_map.107.refs_3_.refs_8_), channel_id=1, source_target_pairs={{16,24},{12,4},{17,25},{13,5},{18,26},{14,6},{19,27},{15,7}} | collective-permute-start | bytes 786440 | tf_op jit(solution)/shard_map/ppermute | solution.py:389
  48.7 11.5 %collective-permute-start.23 = (f32[128,512]{1,0:T(8,128)S(1)}, f32[128,512]{1,0:T(8,128)S(1)}, u32[]{:S(2)}, u32[]{:S(2)}) collective-permute-start(f32[128,512]{1,0:T(8,128)S(1)} %shard_map.108.refs_3_), channel_id=1, source_target_pairs={{0,4},{4,0},{1,5},{5,1},{2,6},{6,2},{3,7},{7,3},{8,12},{12,8},{9,1... | collective-permute-start | bytes 786440 | tf_op jit(solution)/shard_map/ppermute | solution.py:318
  55.2 6.2 %collective-permute-start.22 = (f32[128,512]{1,0:T(8,128)S(1)}, f32[128,512]{1,0:T(8,128)S(1)}, u32[]{:S(2)}, u32[]{:S(2)}) collective-permute-start(f32[128,512]{1,0:T(8,128)S(1)} %shard_map.112), channel_id=1, source_target_pairs={{0,4},{4,0},{1,5},{5,1},{2,6},{6,2},{3,7},{7,3},{8,12},{12,8},{9,1... | collective-permute-start | bytes 786440 | tf_op jit(solution)/shard_map/ppermute | solution.py:318
  62.4 8.0 %collective-permute-start.26 = (f32[64,512]{1,0:T(8,128)S(1)}, f32[64,512]{1,0:T(8,128)S(1)}, u32[]{:S(2)}, u32[]{:S(2)}) collective-permute-start(f32[64,512]{1,0:T(8,128)S(1)} %get-tuple-element.51), channel_id=1, source_target_pairs={{0,4},{4,0},{1,5},{5,1},{2,6},{6,2},{3,7},{7,3},{8,12},{12,8},{9,1... | collective-permute-start | bytes 393224 | tf_op jit(solution)/shard_map/ppermute | solution.py:318
  62.6 11.8 %collective-permute-start.28 = (f32[64,512]{1,0:T(8,128)S(1)}, f32[64,512]{1,0:T(8,128)S(1)}, u32[]{:S(2)}, u32[]{:S(2)}) collective-permute-start(f32[64,512]{1,0:T(8,128)S(1)} %shard_map.119), channel_id=1, source_target_pairs={{0,1},{1,0},{2,3},{3,2},{4,5},{5,4},{6,7},{7,6},{8,9},{9,8},{10,11... | collective-permute-start | bytes 393224 | tf_op jit(solution)/shard_map/ppermute | solution.py:315
  64.2 4.3 %collective-permute-start.24 = (f32[32,512]{1,0:T(8,128)S(1)}, f32[32,512]{1,0:T(8,128)S(1)}, u32[]{:S(2)}, u32[]{:S(2)}) collective-permute-start(f32[32,512]{1,0:T(8,128)S(1)} %shard_map.115.refs_0_), channel_id=1, source_target_pairs={{0,8},{8,0},{16,24},{24,16},{1,9},{9,1},{17,25},{25,17},{2,10},{10... | collective-permute-start | bytes 196616 | tf_op jit(solution)/shard_map/ppermute | solution.py:446
  64.2 10.2 %collective-permute-start.30 = (f32[64,512]{1,0:T(8,128)S(1)}, f32[64,512]{1,0:T(8,128)S(1)}, u32[]{:S(2)}, u32[]{:S(2)}) collective-permute-start(f32[64,512]{1,0:T(8,128)S(1)} %shard_map.120), channel_id=1, source_target_pairs={{0,3},{1,2},{2,1},{3,0},{4,7},{5,6},{6,5},{7,4},{8,11},{9,10},{10,... | collective-permute-start | bytes 393224 | tf_op jit(solution)/shard_map/ppermute | solution.py:315
  64.9 9.6 %collective-permute-start.32 = (f32[64,512]{1,0:T(8,128)S(1)}, f32[64,512]{1,0:T(8,128)S(1)}, u32[]{:S(2)}, u32[]{:S(2)}) collective-permute-start(f32[64,512]{1,0:T(8,128)S(1)} %shard_map.121), channel_id=1, source_target_pairs={{0,2},{1,3},{2,0},{3,1},{4,6},{5,7},{6,4},{7,5},{8,10},{9,11},{10,... | collective-permute-start | bytes 393224 | tf_op jit(solution)/shard_map/ppermute | solution.py:315
  68.5 5.9 %collective-permute-start.25 = (f32[32,512]{1,0:T(8,128)S(1)}, f32[32,512]{1,0:T(8,128)S(1)}, u32[]{:S(2)}, u32[]{:S(2)}) collective-permute-start(f32[32,512]{1,0:T(8,128)S(1)} %shard_map.116.refs_0_), channel_id=1, source_target_pairs={{0,16},{8,24},{16,0},{24,8},{1,17},{9,25},{17,1},{25,9},{2,18},{10... | collective-permute-start | bytes 196616 | tf_op jit(solution)/shard_map/ppermute | solution.py:446
  74.6 6.8 %collective-permute-start.35 = (f32[72,512]{1,0:T(8,128)S(1)}, f32[72,512]{1,0:T(8,128)S(1)}, u32[]{:S(2)}, u32[]{:S(2)}) collective-permute-start(f32[72,512]{1,0:T(8,128)S(1)} %shard_map.122.refs_4_), channel_id=1, source_target_pairs={{0,3},{1,2},{2,1},{3,0},{4,7},{5,6},{6,5},{7,4},{8,11},{9,10},{10,... | collective-permute-start | bytes 442376 | tf_op jit(solution)/shard_map/ppermute | solution.py:315
  75.9 6.5 %collective-permute-start.34 = (f32[72,512]{1,0:T(8,128)S(1)}, f32[72,512]{1,0:T(8,128)S(1)}, u32[]{:S(2)}, u32[]{:S(2)}) collective-permute-start(f32[72,512]{1,0:T(8,128)S(1)} %shard_map.122.refs_4_), channel_id=1, source_target_pairs={{0,2},{1,3},{2,0},{3,1},{4,6},{5,7},{6,4},{7,5},{8,10},{9,11},{10,... | collective-permute-start | bytes 442376 | tf_op jit(solution)/shard_map/ppermute | solution.py:315
  76.7 5.8 %collective-permute-start.33 = (f32[72,512]{1,0:T(8,128)S(1)}, f32[72,512]{1,0:T(8,128)S(1)}, u32[]{:S(2)}, u32[]{:S(2)}) collective-permute-start(f32[72,512]{1,0:T(8,128)S(1)} %shard_map.122.refs_4_), channel_id=1, source_target_pairs={{0,1},{1,0},{2,3},{3,2},{4,5},{5,4},{6,7},{7,6},{8,9},{9,8},{10,11... | collective-permute-start | bytes 442376 | tf_op jit(solution)/shard_map/ppermute | solution.py:315
  78.1 5.6 %collective-permute-start.36 = (f32[72,512]{1,0:T(8,128)S(1)}, f32[72,512]{1,0:T(8,128)S(1)}, u32[]{:S(2)}, u32[]{:S(2)}) collective-permute-start(f32[72,512]{1,0:T(8,128)S(1)} %shard_map.122.refs_4_), channel_id=1, source_target_pairs={{0,4},{4,0},{1,5},{5,1},{2,6},{6,2},{3,7},{7,3},{8,12},{12,8},{9,1... | collective-permute-start | bytes 442376 | tf_op jit(solution)/shard_map/ppermute | solution.py:318
  (13 other events, 53.4 us)

commit v7 on v6

--- a/solution.py
+++ b/solution.py
@@ -427,7 +427,7 @@
             loss = (loss_here,)
             gives.append((keep, swap(give)))
             ready.append(errs[q])
-        stages = range(n_tok) if step == steps else []
+        stages = [1] if step == steps - 1 else [0, *range(2, n_tok)] if step == steps else []
         for c in stages:
             if c < 0:
                 continue
@@ -447,16 +447,19 @@
         loss = call(add_kernel, [f32(*loss.shape)], (loss, other))[0]
         gap *= 2
 
-    g_pre = call(
-        g_pre_kernel, [f32(rows // 2 + LOSS_ROWS, lats)], (pre, mask, loss, *gacts)
-    )[0]
-    mine = [across(g_pre, q) if q else g_pre for q in range(n_tok)]
-    others = [swap(g) for g in mine]
     decoded = call(
         decode_kernel,
         [f32(width, lats)],
         (*[errs[q] for q in order], *[acts[q] for q in order]),
     )[0]
+    g_pre = call(
+        g_pre_kernel,
+        [f32(rows // 2 + LOSS_ROWS, lats)],
+        (pre, mask, loss, *gacts),
+        after=(decoded,),
+    )[0]
+    mine = [across(g_pre, q) if q else g_pre for q in range(n_tok)]
+    others = [swap(g) for g in mine]
     grad, losses = call(
         functools.partial(encode_kernel, 1.0 / (rows * n_tok * half * n_wid)),
         [bf16(width, lats), f32(LEVELS)],

time: 86.6 us -> 86.5 us (level)
  starting transfers between devices: 58.5 us -> 57.2 us
  waiting for transfers between devices: 14.4 us -> 15.6 us
    ppermute x14, waiting for transfers between devices: 1.48 us -> 3.48 us  [swap(): return lax.ppermute(array, 'wid', [(w, w ^ 1) for w in range(n_wid)])]
    ppermute x14, starting transfers between devices: 13.7 us -> 12.4 us  [swap(): return lax.ppermute(array, 'wid', [(w, w ^ 1) for w in range(n_wid)])]
  transfers between devices with their start and end apart: 40 -> 40, of which waited for: 11 -> 13; matrix products, arithmetic and copies ran while one was open for 0% -> 0% of each run, Pallas kernels for 8% -> 8%
where the time goes in v7:
time: 86.5 us; the launch traced here: 85.3 us
  starting transfers between devices  57.2 us (66%)
  waiting for transfers between devices  15.6 us (18%)
  Pallas kernels  11.2 us (13%)
  between operations  1.23 us (1%)
    ppermute x12, starting transfers between devices, body(): got[side].append((lax.ppermute(message, ('lat', 'wid'), pairs), 0))  23.4 us
    ppermute x12, starting transfers between devices, across(): return lax.ppermute(array, 'tok', [(t, t ^ q) for t in range(n_tok)])  19.5 us
    ppermute x14, starting transfers between devices, swap(): return lax.ppermute(array, 'wid', [(w, w ^ 1) for w in range(n_wid)])  12.4 us
    pallas_call x48, Pallas kernels, call(): pl.pallas_call(run, out_shape=outs, in_specs=list(specs or [VMEM] * len(a...  11.2 us
    ppermute x12, waiting for transfers between devices, across(): return lax.ppermute(array, 'tok', [(t, t ^ q) for t in range(n_tok)])  5.3 us
    ppermute x2, waiting for transfers between devices, body(): other = lax.ppermute(loss, 'lat', [(p, p ^ gap) for p in range(n_lat)])  5.25 us
    ppermute x14, waiting for transfers between devices, swap(): return lax.ppermute(array, 'wid', [(w, w ^ 1) for w in range(n_wid)])  3.48 us
    ppermute x2, starting transfers between devices, body(): other = lax.ppermute(loss, 'lat', [(p, p ^ gap) for p in range(n_lat)])  1.98 us
  transfers between devices with their start and end apart: 40, of which 13 were waited for; matrix products, arithmetic and copies ran while one was open for 0% of the time, Pallas kernels for 8%

profile of v7, /device:TPU:0, one launch (start us, length us, event | category | flops | bytes accessed | tf_op | source)
XLA Modules:
  0.0 85.3 jit_solution(10569342026226300289)
XLA Ops:
  0.7 2.9 %shard_map.77 = (f32[128,512]{1,0:T(8,128)S(1)}, bf16[512,512]{1,0:T(8,128)(2,1)S(1)}) custom-call(bf16[128,2048]{1,0:T(8,128)(2,1)} %refs_0_.3, bf16[512,2048]{1,0:T(8,128)(2,1)} %refs_1_.1), custom_call_target="tpu_custom_call" | custom-call | bytes 1024 | tf_op jit(solution)/shard_map/pallas_call | solution.py:37
  4.1 1.2 %collective-permute-done.refs_2_.refs_1_ = f32[128,512]{1,0:T(8,128)S(1)} collective-permute-done((f32[128,512]{1,0:T(8,128)S(1)}, f32[128,512]{1,0:T(8,128)S(1)}, u32[]{:S(2)}, u32[]{:S(2)}) %collective-permute-start) | collective-permute-done | bytes 262176 | tf_op jit(solution)/shard_map/ppermute | solution.py:318
  6.1 2.7 %collective-permute-start.7 = (f32[128,512]{1,0:T(8,128)S(1)}, f32[128,512]{1,0:T(8,128)S(1)}, u32[]{:S(2)}, u32[]{:S(2)}) collective-permute-start(f32[128,512]{1,0:T(8,128)S(1)} %get-tuple-element.35.refs_2_.refs_0_), channel_id=1, source_target_pairs={{0,1},{1,0},{2,3},{3,2},{4,5},{5,4},{6,7},{7,6},{8,9},{9,8},{10,11... | collective-permute-start | bytes 786440 | tf_op jit(solution)/shard_map/ppermute | solution.py:315
  9.1 3.5 %collective-permute-start.10 = (f32[128,512]{1,0:T(8,128)S(1)}, f32[128,512]{1,0:T(8,128)S(1)}, u32[]{:S(2)}, u32[]{:S(2)}) collective-permute-start(f32[128,512]{1,0:T(8,128)S(1)} %shard_map.88.refs_2_.refs_3_), channel_id=1, source_target_pairs={{0,8},{28,20},{1,9},{29,21},{2,10},{30,22},{3,11},{31,23}} | collective-permute-start | bytes 786440 | tf_op jit(solution)/shard_map/ppermute | solution.py:378
  12.9 1.3 %collective-permute-start.6 = (f32[128,512]{1,0:T(8,128)S(1)}, f32[128,512]{1,0:T(8,128)S(1)}, u32[]{:S(2)}, u32[]{:S(2)}) collective-permute-start(f32[128,512]{1,0:T(8,128)S(1)} %shard_map.82.refs_1_.refs_2_.refs_3_), channel_id=1, source_target_pairs={{0,8},{28,20},{1,9},{29,21},{2,10},{30,22},{3,11},{31,23}} | collective-permute-start | bytes 786440 | tf_op jit(solution)/shard_map/ppermute | solution.py:378
  14.2 1.6 %collective-permute-start.9 = (f32[128,512]{1,0:T(8,128)S(1)}, f32[128,512]{1,0:T(8,128)S(1)}, u32[]{:S(2)}, u32[]{:S(2)}) collective-permute-start(f32[128,512]{1,0:T(8,128)S(1)} %get-tuple-element.35.refs_2_.refs_0_), channel_id=1, source_target_pairs={{0,3},{1,2},{2,1},{3,0},{4,7},{5,6},{6,5},{7,4},{8,11},{9,10},{10,... | collective-permute-start | bytes 786440 | tf_op jit(solution)/shard_map/ppermute | solution.py:315
  16.5 4.4 %collective-permute-start.11 = (f32[128,512]{1,0:T(8,128)S(1)}, f32[128,512]{1,0:T(8,128)S(1)}, u32[]{:S(2)}, u32[]{:S(2)}) collective-permute-start(f32[128,512]{1,0:T(8,128)S(1)} %shard_map.90), channel_id=1, source_target_pairs={{0,8},{28,20},{8,16},{20,12},{1,9},{29,21},{9,17},{21,13},{2,10},{... | collective-permute-start | bytes 786440 | tf_op jit(solution)/shard_map/ppermute | solution.py:389
  21.2 2.5 %collective-permute-start.8 = (f32[128,512]{1,0:T(8,128)S(1)}, f32[128,512]{1,0:T(8,128)S(1)}, u32[]{:S(2)}, u32[]{:S(2)}) collective-permute-start(f32[128,512]{1,0:T(8,128)S(1)} %shard_map.85.refs_1_.refs_4_), channel_id=1, source_target_pairs={{0,8},{28,20},{8,16},{20,12},{1,9},{29,21},{9,17},{21,13},{2,10},{... | collective-permute-start | bytes 786440 | tf_op jit(solution)/shard_map/ppermute | solution.py:389
  23.7 2.0 %collective-permute-start.4 = (f32[128,512]{1,0:T(8,128)S(1)}, f32[128,512]{1,0:T(8,128)S(1)}, u32[]{:S(2)}, u32[]{:S(2)}) collective-permute-start(f32[128,512]{1,0:T(8,128)S(1)} %get-tuple-element.35.refs_2_.refs_0_), channel_id=1, source_target_pairs={{0,2},{1,3},{2,0},{3,1},{4,6},{5,7},{6,4},{7,5},{8,10},{9,11},{10,... | collective-permute-start | bytes 786440 | tf_op jit(solution)/shard_map/ppermute | solution.py:315
  25.8 1.6 %collective-permute-start.1 = (f32[128,512]{1,0:T(8,128)S(1)}, f32[128,512]{1,0:T(8,128)S(1)}, u32[]{:S(2)}, u32[]{:S(2)}) collective-permute-start(f32[128,512]{1,0:T(8,128)S(1)} %get-tuple-element.37), channel_id=1, source_target_pairs={{0,1},{1,0},{2,3},{3,2},{4,5},{5,4},{6,7},{7,6},{8,9},{9,8},{10,11... | collective-permute-start | bytes 786440 | tf_op jit(solution)/shard_map/ppermute | solution.py:315
  27.8 1.9 %collective-permute-start.12 = (f32[128,512]{1,0:T(8,128)S(1)}, f32[128,512]{1,0:T(8,128)S(1)}, u32[]{:S(2)}, u32[]{:S(2)}) collective-permute-start(f32[128,512]{1,0:T(8,128)S(1)} %shard_map.92.refs_4_), channel_id=1, source_target_pairs={{0,8},{28,20},{8,16},{20,12},{16,24},{12,4},{1,9},{29,21},{9,17},{... | collective-permute-start | bytes 786440 | tf_op jit(solution)/shard_map/ppermute | solution.py:389
  30.1 2.0 %collective-permute-start.14 = (f32[128,512]{1,0:T(8,128)S(1)}, f32[128,512]{1,0:T(8,128)S(1)}, u32[]{:S(2)}, u32[]{:S(2)}) collective-permute-start(f32[128,512]{1,0:T(8,128)S(1)} %shard_map.93.refs_1_.refs_4_), channel_id=1, source_target_pairs={{0,8},{28,20},{8,16},{20,12},{16,24},{12,4},{1,9},{29,21},{9,17},{... | collective-permute-start | bytes 786440 | tf_op jit(solution)/shard_map/ppermute | solution.py:389
  32.0 2.9 %collective-permute-start.3 = (f32[128,512]{1,0:T(8,128)S(1)}, f32[128,512]{1,0:T(8,128)S(1)}, u32[]{:S(2)}, u32[]{:S(2)}) collective-permute-start(f32[128,512]{1,0:T(8,128)S(1)} %get-tuple-element.39), channel_id=1, source_target_pairs={{0,3},{1,2},{2,1},{3,0},{4,7},{5,6},{6,5},{7,4},{8,11},{9,10},{10,... | collective-permute-start | bytes 786440 | tf_op jit(solution)/shard_map/ppermute | solution.py:315
  35.4 2.6 %collective-permute-start.13 = (f32[128,512]{1,0:T(8,128)S(1)}, f32[128,512]{1,0:T(8,128)S(1)}, u32[]{:S(2)}, u32[]{:S(2)}) collective-permute-start(f32[128,512]{1,0:T(8,128)S(1)} %shard_map.96.refs_4_), channel_id=1, source_target_pairs={{0,8},{28,20},{8,16},{20,12},{16,24},{12,4},{1,9},{29,21},{9,17},{... | collective-permute-start | bytes 786440 | tf_op jit(solution)/shard_map/ppermute | solution.py:389
  38.4 2.4 %collective-permute-start.16 = (f32[128,512]{1,0:T(8,128)S(1)}, f32[128,512]{1,0:T(8,128)S(1)}, u32[]{:S(2)}, u32[]{:S(2)}) collective-permute-start(f32[128,512]{1,0:T(8,128)S(1)} %shard_map.98.refs_3_), channel_id=1, source_target_pairs={{0,8},{28,20},{8,16},{20,12},{16,24},{12,4},{1,9},{29,21},{9,17},{... | collective-permute-start | bytes 786440 | tf_op jit(solution)/shard_map/ppermute | solution.py:389
  40.8 1.5 %collective-permute-start.2 = (f32[128,512]{1,0:T(8,128)S(1)}, f32[128,512]{1,0:T(8,128)S(1)}, u32[]{:S(2)}, u32[]{:S(2)}) collective-permute-start(f32[128,512]{1,0:T(8,128)S(1)} %get-tuple-element.38), channel_id=1, source_target_pairs={{0,2},{1,3},{2,0},{3,1},{4,6},{5,7},{6,4},{7,5},{8,10},{9,11},{10,... | collective-permute-start | bytes 786440 | tf_op jit(solution)/shard_map/ppermute | solution.py:315
  43.3 1.4 %collective-permute-done.16.refs_0_.refs_2_.refs_1_ = f32[128,512]{1,0:T(8,128)S(1)} collective-permute-done((f32[128,512]{1,0:T(8,128)S(1)}, f32[128,512]{1,0:T(8,128)S(1)}, u32[]{:S(2)}, u32[]{:S(2)}) %collective-permute-start.16) | collective-permute-done | bytes 262176 | tf_op jit(solution)/shard_map/ppermute | solution.py:389
  49.3 5.7 %collective-permute-start.21 = (f32[64,512]{1,0:T(8,128)S(1)}, f32[64,512]{1,0:T(8,128)S(1)}, u32[]{:S(2)}, u32[]{:S(2)}) collective-permute-start(f32[64,512]{1,0:T(8,128)S(1)} %get-tuple-element.48), channel_id=1, source_target_pairs={{0,4},{4,0},{1,5},{5,1},{2,6},{6,2},{3,7},{7,3},{8,12},{12,8},{9,1... | collective-permute-start | bytes 393224 | tf_op jit(solution)/shard_map/ppermute | solution.py:318
  55.2 0.8 collective-permute-done.21.refs_1_
  56.1 4.0 %collective-permute-start.23 = (f32[128,512]{1,0:T(8,128)S(1)}, f32[128,512]{1,0:T(8,128)S(1)}, u32[]{:S(2)}, u32[]{:S(2)}) collective-permute-start(f32[128,512]{1,0:T(8,128)S(1)} %shard_map.113), channel_id=1, source_target_pairs={{0,4},{4,0},{1,5},{5,1},{2,6},{6,2},{3,7},{7,3},{8,12},{12,8},{9,1... | collective-permute-start | bytes 786440 | tf_op jit(solution)/shard_map/ppermute | solution.py:318
  62.6 1.5 %collective-permute-start.27 = (f32[64,512]{1,0:T(8,128)S(1)}, f32[64,512]{1,0:T(8,128)S(1)}, u32[]{:S(2)}, u32[]{:S(2)}) collective-permute-start(f32[64,512]{1,0:T(8,128)S(1)} %shard_map.111.refs_6_), channel_id=1, source_target_pairs={{0,1},{1,0},{2,3},{3,2},{4,5},{5,4},{6,7},{7,6},{8,9},{9,8},{10,11... | collective-permute-start | bytes 393224 | tf_op jit(solution)/shard_map/ppermute | solution.py:315
  64.7 1.5 %collective-permute-start.32 = (f32[64,512]{1,0:T(8,128)S(1)}, f32[64,512]{1,0:T(8,128)S(1)}, u32[]{:S(2)}, u32[]{:S(2)}) collective-permute-start(f32[64,512]{1,0:T(8,128)S(1)} %shard_map.121), channel_id=1, source_target_pairs={{0,2},{1,3},{2,0},{3,1},{4,6},{5,7},{6,4},{7,5},{8,10},{9,11},{10,... | collective-permute-start | bytes 393224 | tf_op jit(solution)/shard_map/ppermute | solution.py:315
  66.3 2.1 %collective-permute-done.25.refs_1_ = f32[32,512]{1,0:T(8,128)S(1)} collective-permute-done((f32[32,512]{1,0:T(8,128)S(1)}, f32[32,512]{1,0:T(8,128)S(1)}, u32[]{:S(2)}, u32[]{:S(2)}) %collective-permute-start.25) | collective-permute-done | bytes 65568 | tf_op jit(solution)/shard_map/ppermute | solution.py:446
  68.4 2.0 %collective-permute-start.26 = (f32[32,512]{1,0:T(8,128)S(1)}, f32[32,512]{1,0:T(8,128)S(1)}, u32[]{:S(2)}, u32[]{:S(2)}) collective-permute-start(f32[32,512]{1,0:T(8,128)S(1)} %shard_map.117.refs_0_), channel_id=1, source_target_pairs={{0,16},{8,24},{16,0},{24,8},{1,17},{9,25},{17,1},{25,9},{2,18},{10... | collective-permute-start | bytes 196616 | tf_op jit(solution)/shard_map/ppermute | solution.py:446
  70.4 0.8 shard_map.122.refs_7_.refs_12_
  71.1 3.2 %collective-permute-done.26.refs_1_ = f32[32,512]{1,0:T(8,128)S(1)} collective-permute-done((f32[32,512]{1,0:T(8,128)S(1)}, f32[32,512]{1,0:T(8,128)S(1)}, u32[]{:S(2)}, u32[]{:S(2)}) %collective-permute-start.26) | collective-permute-done | bytes 65568 | tf_op jit(solution)/shard_map/ppermute | solution.py:446
  74.5 1.4 %collective-permute-start.35 = (f32[72,512]{1,0:T(8,128)S(1)}, f32[72,512]{1,0:T(8,128)S(1)}, u32[]{:S(2)}, u32[]{:S(2)}) collective-permute-start(f32[72,512]{1,0:T(8,128)S(1)} %shard_map.123.refs_4_), channel_id=1, source_target_pairs={{0,3},{1,2},{2,1},{3,0},{4,7},{5,6},{6,5},{7,4},{8,11},{9,10},{10,... | collective-permute-start | bytes 442376 | tf_op jit(solution)/shard_map/ppermute | solution.py:315
  76.5 1.5 %collective-permute-start.33 = (f32[72,512]{1,0:T(8,128)S(1)}, f32[72,512]{1,0:T(8,128)S(1)}, u32[]{:S(2)}, u32[]{:S(2)}) collective-permute-start(f32[72,512]{1,0:T(8,128)S(1)} %shard_map.123.refs_4_), channel_id=1, source_target_pairs={{0,1},{1,0},{2,3},{3,2},{4,5},{5,4},{6,7},{7,6},{8,9},{9,8},{10,11... | collective-permute-start | bytes 442376 | tf_op jit(solution)/shard_map/ppermute | solution.py:315
  78.0 3.3 %collective-permute-done.35.refs_7_ = f32[72,512]{1,0:T(8,128)S(1)} collective-permute-done((f32[72,512]{1,0:T(8,128)S(1)}, f32[72,512]{1,0:T(8,128)S(1)}, u32[]{:S(2)}, u32[]{:S(2)}) %collective-permute-start.35) | collective-permute-done | bytes 147488 | tf_op jit(solution)/shard_map/ppermute | solution.py:315
  81.3 1.1 %collective-permute-done.34.refs_6_ = f32[72,512]{1,0:T(8,128)S(1)} collective-permute-done((f32[72,512]{1,0:T(8,128)S(1)}, f32[72,512]{1,0:T(8,128)S(1)}, u32[]{:S(2)}, u32[]{:S(2)}) %collective-permute-start.34) | collective-permute-done | bytes 147488 | tf_op jit(solution)/shard_map/ppermute | solution.py:315
  82.9 0.9 collective-permute-done.38.refs_10_
  84.0 1.3 %shard_map.124 = (bf16[512,512]{1,0:T(8,128)(2,1)}, f32[4]{0:T(128)}) custom-call(f32[128,512]{1,0:T(8,128)S(1)} %get-tuple-element.36.refs_2_.refs_0_, f32[128,512]{1,0:T(8,128)S(1)} %collective-permute-done.1.refs_5_.refs_2_.refs_1_, f32[128,512]{1,0:T(8,128)S(1)} %collective-permute-done.2.refs_3_.refs_2_, ...), custom_call_target="tpu_custom_call" | custom-call | bytes 1024 | tf_op jit(solution)/shard_map/pallas_call | solution.py:37
  (106 shorter events, 14.6 us)
Async XLA Ops:
  5.4 7.2 %collective-permute-start.5 = (f32[512,512]{1,0:T(8,128)S(1)}, f32[512,512]{1,0:T(8,128)S(1)}, u32[]{:S(2)}, u32[]{:S(2)}) collective-permute-start(f32[512,512]{1,0:T(8,128)S(1)} %get-tuple-element.34.refs_4_), channel_id=1, source_target_pairs={{0,4},{4,0},{1,5},{5,1},{2,6},{6,2},{3,7},{7,3},{8,12},{12,8},{9,1... | collective-permute-start | bytes 3145736 | tf_op jit(solution)/shard_map/ppermute | solution.py:318
  6.1 9.8 %collective-permute-start.7 = (f32[128,512]{1,0:T(8,128)S(1)}, f32[128,512]{1,0:T(8,128)S(1)}, u32[]{:S(2)}, u32[]{:S(2)}) collective-permute-start(f32[128,512]{1,0:T(8,128)S(1)} %get-tuple-element.35.refs_2_.refs_0_), channel_id=1, source_target_pairs={{0,1},{1,0},{2,3},{3,2},{4,5},{5,4},{6,7},{7,6},{8,9},{9,8},{10,11... | collective-permute-start | bytes 786440 | tf_op jit(solution)/shard_map/ppermute | solution.py:315
  9.1 7.4 %collective-permute-start.10 = (f32[128,512]{1,0:T(8,128)S(1)}, f32[128,512]{1,0:T(8,128)S(1)}, u32[]{:S(2)}, u32[]{:S(2)}) collective-permute-start(f32[128,512]{1,0:T(8,128)S(1)} %shard_map.88.refs_2_.refs_3_), channel_id=1, source_target_pairs={{0,8},{28,20},{1,9},{29,21},{2,10},{30,22},{3,11},{31,23}} | collective-permute-start | bytes 786440 | tf_op jit(solution)/shard_map/ppermute | solution.py:378
  12.9 8.3 %collective-permute-start.6 = (f32[128,512]{1,0:T(8,128)S(1)}, f32[128,512]{1,0:T(8,128)S(1)}, u32[]{:S(2)}, u32[]{:S(2)}) collective-permute-start(f32[128,512]{1,0:T(8,128)S(1)} %shard_map.82.refs_1_.refs_2_.refs_3_), channel_id=1, source_target_pairs={{0,8},{28,20},{1,9},{29,21},{2,10},{30,22},{3,11},{31,23}} | collective-permute-start | bytes 786440 | tf_op jit(solution)/shard_map/ppermute | solution.py:378
  14.2 13.2 %collective-permute-start.9 = (f32[128,512]{1,0:T(8,128)S(1)}, f32[128,512]{1,0:T(8,128)S(1)}, u32[]{:S(2)}, u32[]{:S(2)}) collective-permute-start(f32[128,512]{1,0:T(8,128)S(1)} %get-tuple-element.35.refs_2_.refs_0_), channel_id=1, source_target_pairs={{0,3},{1,2},{2,1},{3,0},{4,7},{5,6},{6,5},{7,4},{8,11},{9,10},{10,... | collective-permute-start | bytes 786440 | tf_op jit(solution)/shard_map/ppermute | solution.py:315
  16.5 11.2 %collective-permute-start.11 = (f32[128,512]{1,0:T(8,128)S(1)}, f32[128,512]{1,0:T(8,128)S(1)}, u32[]{:S(2)}, u32[]{:S(2)}) collective-permute-start(f32[128,512]{1,0:T(8,128)S(1)} %shard_map.90), channel_id=1, source_target_pairs={{0,8},{28,20},{8,16},{20,12},{1,9},{29,21},{9,17},{21,13},{2,10},{... | collective-permute-start | bytes 786440 | tf_op jit(solution)/shard_map/ppermute | solution.py:389
  21.2 8.8 %collective-permute-start.8 = (f32[128,512]{1,0:T(8,128)S(1)}, f32[128,512]{1,0:T(8,128)S(1)}, u32[]{:S(2)}, u32[]{:S(2)}) collective-permute-start(f32[128,512]{1,0:T(8,128)S(1)} %shard_map.85.refs_1_.refs_4_), channel_id=1, source_target_pairs={{0,8},{28,20},{8,16},{20,12},{1,9},{29,21},{9,17},{21,13},{2,10},{... | collective-permute-start | bytes 786440 | tf_op jit(solution)/shard_map/ppermute | solution.py:389
  23.7 11.3 %collective-permute-start.4 = (f32[128,512]{1,0:T(8,128)S(1)}, f32[128,512]{1,0:T(8,128)S(1)}, u32[]{:S(2)}, u32[]{:S(2)}) collective-permute-start(f32[128,512]{1,0:T(8,128)S(1)} %get-tuple-element.35.refs_2_.refs_0_), channel_id=1, source_target_pairs={{0,2},{1,3},{2,0},{3,1},{4,6},{5,7},{6,4},{7,5},{8,10},{9,11},{10,... | collective-permute-start | bytes 786440 | tf_op jit(solution)/shard_map/ppermute | solution.py:315
  25.8 9.5 %collective-permute-start.1 = (f32[128,512]{1,0:T(8,128)S(1)}, f32[128,512]{1,0:T(8,128)S(1)}, u32[]{:S(2)}, u32[]{:S(2)}) collective-permute-start(f32[128,512]{1,0:T(8,128)S(1)} %get-tuple-element.37), channel_id=1, source_target_pairs={{0,1},{1,0},{2,3},{3,2},{4,5},{5,4},{6,7},{7,6},{8,9},{9,8},{10,11... | collective-permute-start | bytes 786440 | tf_op jit(solution)/shard_map/ppermute | solution.py:315
  27.8 7.5 %collective-permute-start.12 = (f32[128,512]{1,0:T(8,128)S(1)}, f32[128,512]{1,0:T(8,128)S(1)}, u32[]{:S(2)}, u32[]{:S(2)}) collective-permute-start(f32[128,512]{1,0:T(8,128)S(1)} %shard_map.92.refs_4_), channel_id=1, source_target_pairs={{0,8},{28,20},{8,16},{20,12},{16,24},{12,4},{1,9},{29,21},{9,17},{... | collective-permute-start | bytes 786440 | tf_op jit(solution)/shard_map/ppermute | solution.py:389
  30.1 8.2 %collective-permute-start.14 = (f32[128,512]{1,0:T(8,128)S(1)}, f32[128,512]{1,0:T(8,128)S(1)}, u32[]{:S(2)}, u32[]{:S(2)}) collective-permute-start(f32[128,512]{1,0:T(8,128)S(1)} %shard_map.93.refs_1_.refs_4_), channel_id=1, source_target_pairs={{0,8},{28,20},{8,16},{20,12},{16,24},{12,4},{1,9},{29,21},{9,17},{... | collective-permute-start | bytes 786440 | tf_op jit(solution)/shard_map/ppermute | solution.py:389
  32.0 10.5 %collective-permute-start.3 = (f32[128,512]{1,0:T(8,128)S(1)}, f32[128,512]{1,0:T(8,128)S(1)}, u32[]{:S(2)}, u32[]{:S(2)}) collective-permute-start(f32[128,512]{1,0:T(8,128)S(1)} %get-tuple-element.39), channel_id=1, source_target_pairs={{0,3},{1,2},{2,1},{3,0},{4,7},{5,6},{6,5},{7,4},{8,11},{9,10},{10,... | collective-permute-start | bytes 786440 | tf_op jit(solution)/shard_map/ppermute | solution.py:315
  35.4 7.2 %collective-permute-start.13 = (f32[128,512]{1,0:T(8,128)S(1)}, f32[128,512]{1,0:T(8,128)S(1)}, u32[]{:S(2)}, u32[]{:S(2)}) collective-permute-start(f32[128,512]{1,0:T(8,128)S(1)} %shard_map.96.refs_4_), channel_id=1, source_target_pairs={{0,8},{28,20},{8,16},{20,12},{16,24},{12,4},{1,9},{29,21},{9,17},{... | collective-permute-start | bytes 786440 | tf_op jit(solution)/shard_map/ppermute | solution.py:389
  38.4 6.3 %collective-permute-start.16 = (f32[128,512]{1,0:T(8,128)S(1)}, f32[128,512]{1,0:T(8,128)S(1)}, u32[]{:S(2)}, u32[]{:S(2)}) collective-permute-start(f32[128,512]{1,0:T(8,128)S(1)} %shard_map.98.refs_3_), channel_id=1, source_target_pairs={{0,8},{28,20},{8,16},{20,12},{16,24},{12,4},{1,9},{29,21},{9,17},{... | collective-permute-start | bytes 786440 | tf_op jit(solution)/shard_map/ppermute | solution.py:389
  40.8 6.4 %collective-permute-start.2 = (f32[128,512]{1,0:T(8,128)S(1)}, f32[128,512]{1,0:T(8,128)S(1)}, u32[]{:S(2)}, u32[]{:S(2)}) collective-permute-start(f32[128,512]{1,0:T(8,128)S(1)} %get-tuple-element.38), channel_id=1, source_target_pairs={{0,2},{1,3},{2,0},{3,1},{4,6},{5,7},{6,4},{7,5},{8,10},{9,11},{10,... | collective-permute-start | bytes 786440 | tf_op jit(solution)/shard_map/ppermute | solution.py:315
  42.4 3.5 %collective-permute-start.17 = (f32[128,512]{1,0:T(8,128)S(1)}, f32[128,512]{1,0:T(8,128)S(1)}, u32[]{:S(2)}, u32[]{:S(2)}) collective-permute-start(f32[128,512]{1,0:T(8,128)S(1)} %shard_map.99.refs_5_), channel_id=1, source_target_pairs={{0,4},{4,0},{1,5},{5,1},{2,6},{6,2},{3,7},{7,3},{8,12},{12,8},{9,1... | collective-permute-start | bytes 786440 | tf_op jit(solution)/shard_map/ppermute | solution.py:318
  42.6 4.7 %collective-permute-start.15 = (f32[128,512]{1,0:T(8,128)S(1)}, f32[128,512]{1,0:T(8,128)S(1)}, u32[]{:S(2)}, u32[]{:S(2)}) collective-permute-start(f32[128,512]{1,0:T(8,128)S(1)} %shard_map.101.refs_3_), channel_id=1, source_target_pairs={{8,16},{20,12},{16,24},{12,4},{9,17},{21,13},{17,25},{13,5},{10,18... | collective-permute-start | bytes 786440 | tf_op jit(solution)/shard_map/ppermute | solution.py:389
  47.3 8.7 %collective-permute-start.18 = (f32[128,512]{1,0:T(8,128)S(1)}, f32[128,512]{1,0:T(8,128)S(1)}, u32[]{:S(2)}, u32[]{:S(2)}) collective-permute-start(f32[128,512]{1,0:T(8,128)S(1)} %shard_map.106.refs_2_), channel_id=1, source_target_pairs={{16,24},{12,4},{17,25},{13,5},{18,26},{14,6},{19,27},{15,7}} | collective-permute-start | bytes 786440 | tf_op jit(solution)/shard_map/ppermute | solution.py:389
  48.0 8.1 %collective-permute-start.22 = (f32[128,512]{1,0:T(8,128)S(1)}, f32[128,512]{1,0:T(8,128)S(1)}, u32[]{:S(2)}, u32[]{:S(2)}) collective-permute-start(f32[128,512]{1,0:T(8,128)S(1)} %shard_map.107.refs_3_.refs_8_.refs_2_), channel_id=1, source_target_pairs={{16,24},{12,4},{17,25},{13,5},{18,26},{14,6},{19,27},{15,7}} | collective-permute-start | bytes 786440 | tf_op jit(solution)/shard_map/ppermute | solution.py:389
  49.3 6.6 %collective-permute-start.21 = (f32[64,512]{1,0:T(8,128)S(1)}, f32[64,512]{1,0:T(8,128)S(1)}, u32[]{:S(2)}, u32[]{:S(2)}) collective-permute-start(f32[64,512]{1,0:T(8,128)S(1)} %get-tuple-element.48), channel_id=1, source_target_pairs={{0,4},{4,0},{1,5},{5,1},{2,6},{6,2},{3,7},{7,3},{8,12},{12,8},{9,1... | collective-permute-start | bytes 393224 | tf_op jit(solution)/shard_map/ppermute | solution.py:318
  55.0 5.1 %collective-permute-start.24 = (f32[128,512]{1,0:T(8,128)S(1)}, f32[128,512]{1,0:T(8,128)S(1)}, u32[]{:S(2)}, u32[]{:S(2)}) collective-permute-start(f32[128,512]{1,0:T(8,128)S(1)} %shard_map.108.refs_3_), channel_id=1, source_target_pairs={{0,4},{4,0},{1,5},{5,1},{2,6},{6,2},{3,7},{7,3},{8,12},{12,8},{9,1... | collective-permute-start | bytes 786440 | tf_op jit(solution)/shard_map/ppermute | solution.py:318
  56.1 5.2 %collective-permute-start.23 = (f32[128,512]{1,0:T(8,128)S(1)}, f32[128,512]{1,0:T(8,128)S(1)}, u32[]{:S(2)}, u32[]{:S(2)}) collective-permute-start(f32[128,512]{1,0:T(8,128)S(1)} %shard_map.113), channel_id=1, source_target_pairs={{0,4},{4,0},{1,5},{5,1},{2,6},{6,2},{3,7},{7,3},{8,12},{12,8},{9,1... | collective-permute-start | bytes 786440 | tf_op jit(solution)/shard_map/ppermute | solution.py:318
  62.4 7.9 %collective-permute-start.28 = (f32[64,512]{1,0:T(8,128)S(1)}, f32[64,512]{1,0:T(8,128)S(1)}, u32[]{:S(2)}, u32[]{:S(2)}) collective-permute-start(f32[64,512]{1,0:T(8,128)S(1)} %get-tuple-element.53), channel_id=1, source_target_pairs={{0,4},{4,0},{1,5},{5,1},{2,6},{6,2},{3,7},{7,3},{8,12},{12,8},{9,1... | collective-permute-start | bytes 393224 | tf_op jit(solution)/shard_map/ppermute | solution.py:318
  62.6 11.7 %collective-permute-start.27 = (f32[64,512]{1,0:T(8,128)S(1)}, f32[64,512]{1,0:T(8,128)S(1)}, u32[]{:S(2)}, u32[]{:S(2)}) collective-permute-start(f32[64,512]{1,0:T(8,128)S(1)} %shard_map.111.refs_6_), channel_id=1, source_target_pairs={{0,1},{1,0},{2,3},{3,2},{4,5},{5,4},{6,7},{7,6},{8,9},{9,8},{10,11... | collective-permute-start | bytes 393224 | tf_op jit(solution)/shard_map/ppermute | solution.py:315
  64.1 4.3 %collective-permute-start.25 = (f32[32,512]{1,0:T(8,128)S(1)}, f32[32,512]{1,0:T(8,128)S(1)}, u32[]{:S(2)}, u32[]{:S(2)}) collective-permute-start(f32[32,512]{1,0:T(8,128)S(1)} %shard_map.116.refs_0_), channel_id=1, source_target_pairs={{0,8},{8,0},{16,24},{24,16},{1,9},{9,1},{17,25},{25,17},{2,10},{10... | collective-permute-start | bytes 196616 | tf_op jit(solution)/shard_map/ppermute | solution.py:446
  64.1 10.2 %collective-permute-start.30 = (f32[64,512]{1,0:T(8,128)S(1)}, f32[64,512]{1,0:T(8,128)S(1)}, u32[]{:S(2)}, u32[]{:S(2)}) collective-permute-start(f32[64,512]{1,0:T(8,128)S(1)} %shard_map.120), channel_id=1, source_target_pairs={{0,3},{1,2},{2,1},{3,0},{4,7},{5,6},{6,5},{7,4},{8,11},{9,10},{10,... | collective-permute-start | bytes 393224 | tf_op jit(solution)/shard_map/ppermute | solution.py:315
  64.7 9.6 %collective-permute-start.32 = (f32[64,512]{1,0:T(8,128)S(1)}, f32[64,512]{1,0:T(8,128)S(1)}, u32[]{:S(2)}, u32[]{:S(2)}) collective-permute-start(f32[64,512]{1,0:T(8,128)S(1)} %shard_map.121), channel_id=1, source_target_pairs={{0,2},{1,3},{2,0},{3,1},{4,6},{5,7},{6,4},{7,5},{8,10},{9,11},{10,... | collective-permute-start | bytes 393224 | tf_op jit(solution)/shard_map/ppermute | solution.py:315
  68.4 5.9 %collective-permute-start.26 = (f32[32,512]{1,0:T(8,128)S(1)}, f32[32,512]{1,0:T(8,128)S(1)}, u32[]{:S(2)}, u32[]{:S(2)}) collective-permute-start(f32[32,512]{1,0:T(8,128)S(1)} %shard_map.117.refs_0_), channel_id=1, source_target_pairs={{0,16},{8,24},{16,0},{24,8},{1,17},{9,25},{17,1},{25,9},{2,18},{10... | collective-permute-start | bytes 196616 | tf_op jit(solution)/shard_map/ppermute | solution.py:446
  74.5 6.9 %collective-permute-start.35 = (f32[72,512]{1,0:T(8,128)S(1)}, f32[72,512]{1,0:T(8,128)S(1)}, u32[]{:S(2)}, u32[]{:S(2)}) collective-permute-start(f32[72,512]{1,0:T(8,128)S(1)} %shard_map.123.refs_4_), channel_id=1, source_target_pairs={{0,3},{1,2},{2,1},{3,0},{4,7},{5,6},{6,5},{7,4},{8,11},{9,10},{10,... | collective-permute-start | bytes 442376 | tf_op jit(solution)/shard_map/ppermute | solution.py:315
  75.9 6.5 %collective-permute-start.34 = (f32[72,512]{1,0:T(8,128)S(1)}, f32[72,512]{1,0:T(8,128)S(1)}, u32[]{:S(2)}, u32[]{:S(2)}) collective-permute-start(f32[72,512]{1,0:T(8,128)S(1)} %shard_map.123.refs_4_), channel_id=1, source_target_pairs={{0,2},{1,3},{2,0},{3,1},{4,6},{5,7},{6,4},{7,5},{8,10},{9,11},{10,... | collective-permute-start | bytes 442376 | tf_op jit(solution)/shard_map/ppermute | solution.py:315
  76.5 5.9 %collective-permute-start.33 = (f32[72,512]{1,0:T(8,128)S(1)}, f32[72,512]{1,0:T(8,128)S(1)}, u32[]{:S(2)}, u32[]{:S(2)}) collective-permute-start(f32[72,512]{1,0:T(8,128)S(1)} %shard_map.123.refs_4_), channel_id=1, source_target_pairs={{0,1},{1,0},{2,3},{3,2},{4,5},{5,4},{6,7},{7,6},{8,9},{9,8},{10,11... | collective-permute-start | bytes 442376 | tf_op jit(solution)/shard_map/ppermute | solution.py:315
  78.0 4.9 %collective-permute-start.36 = (f32[72,512]{1,0:T(8,128)S(1)}, f32[72,512]{1,0:T(8,128)S(1)}, u32[]{:S(2)}, u32[]{:S(2)}) collective-permute-start(f32[72,512]{1,0:T(8,128)S(1)} %shard_map.123.refs_4_), channel_id=1, source_target_pairs={{0,4},{4,0},{1,5},{5,1},{2,6},{6,2},{3,7},{7,3},{8,12},{12,8},{9,1... | collective-permute-start | bytes 442376 | tf_op jit(solution)/shard_map/ppermute | solution.py:318
  (13 other events, 53.3 us)

commit v8 on v7

--- a/solution.py
+++ b/solution.py
@@ -11,6 +11,7 @@
 BLOCK = 128
 LOSS_ROWS = 8
 LOSS_PART = 4
+GIVE_PARTS = 1
 GELU_C = 0.7978845608028654
 GELU_A = 0.044715
 
@@ -232,8 +233,9 @@
     return jnp.concatenate(rows + [jnp.zeros((LOSS_ROWS - LEVELS, BLOCK), jnp.float32)], axis=0)
 
 
-def error_kernel(act, dictionary, resid, bias, table, mine, other, *refs):
-    before, (err_out, keep_out, give_out, loss_out) = refs[:-4], refs[-4:]
+def error_kernel(loss_count, act, dictionary, resid, bias, table, mine, other, *refs):
+    before, refs = refs[:loss_count], refs[loss_count:]
+    err_out, keep_out, *give_outs, loss_out = refs
     upward = lax.axis_index("wid") == 0
     earlier = jnp.where(upward, mine[...], other[...])
     later = jnp.where(upward, other[...], mine[...])
@@ -255,12 +257,22 @@
         )
         half = gact.shape[0] // 2
         keep_out[:, cols] = jnp.where(upward, gact[:half, :], gact[half:, :])
-        give_out[:, cols] = jnp.where(upward, gact[half:, :], gact[:half, :])
+        given = jnp.where(upward, gact[half:, :], gact[:half, :])
+        for part, give_out in enumerate(give_outs):
+            size = give_out.shape[0]
+            give_out[:, cols] = given[part * size : (part + 1) * size, :]
 
 
 def spread_kernel(loss, out):
     out[...] = jnp.zeros_like(out)
     out[:LOSS_ROWS, :BLOCK] = loss[...]
+
+
+def collect_kernel(keep, *refs):
+    parts, out = refs[:-1], refs[-1]
+    for i, part in enumerate(parts):
+        span = slice(i * part.shape[0], (i + 1) * part.shape[0])
+        out[span, :] = keep[span, :] + part[...]
 
 
 def add_kernel(*refs):
@@ -279,19 +291,29 @@
         )
 
 
-def encode_kernel(scale, *refs):
-    n = (len(refs) - 3) // 3
-    resids, grads, base, out, loss_out = refs[:n], refs[n : 3 * n], refs[-3], refs[-2], refs[-1]
-    rows = resids[0].shape[0]
+def encode_kernel(items, *refs):
+    n, halves = items
+    resids, grads, base, out = refs[:n], refs[n:-2], refs[-2], refs[-1]
+    half = resids[0].shape[0] // 2
     wid = lax.axis_index("wid")
-    halves = [half_of(wid, rows), half_of(1 - wid, rows)]
-    resid = jnp.concatenate([r[h, :].astype(jnp.bfloat16) for h in halves for r in resids], axis=0)
-    grad = jnp.concatenate([g[: rows // 2, :].astype(jnp.bfloat16) for g in grads], axis=0)
+    spans = [half_of(wid, 2 * half), half_of(1 - wid, 2 * half)]
+    resid = jnp.concatenate(
+        [resids[q][spans[side], :].astype(jnp.bfloat16) for q, side in halves], axis=0
+    )
+    grad = jnp.concatenate([g[:half, :].astype(jnp.bfloat16) for g in grads], axis=0)
     total = base[...] + lax.dot_general(
         resid, grad, (((0,), (0,)), ((), ())), preferred_element_type=jnp.float32
     )
-    out[...] = total.astype(jnp.bfloat16)
-    lanes = total_of([g[rows // 2 :, :BLOCK] for g in grads])
+    out[...] = total.astype(out.dtype)
+
+
+def last_kernel(items, scale, n_early, *refs):
+    *refs, out, loss_out = refs
+    early, refs = refs[:n_early], refs[n_early:]
+    encode_kernel(items, *refs, out)
+    grads = list(early) + list(refs[items[0] : -1])
+    half = refs[0].shape[0] // 2
+    lanes = total_of([g[half:, :BLOCK] for g in grads])
     for m in range(LEVELS):
         loss_out[m] = jnp.sum(lanes[m : m + 1, :]) * scale
 
@@ -351,7 +373,7 @@
     )
     resids = [piece if q == 0 else across(piece, q) for q, piece in enumerate(pieces)]
 
-    order = [0, 1, 3, 2] if n_tok == 4 else list(range(n_tok))
+    order = [0, 3, 1, 2] if n_tok == 4 else list(range(n_tok))
     steps = n_tok + n_lat - 2
     places = list(range(1, n_lat))
     acts, errs, hands, gives, gacts, loss = {}, {}, [], [], [], ()
@@ -418,14 +440,16 @@
             if c < 0:
                 continue
             q = order[c]
-            errs[q], keep, give, loss_here = call(
-                error_kernel,
-                [bf16(count, rows, width)] + [f32(rows // 2, lats)] * 2 + [f32(LOSS_ROWS, BLOCK)],
+            errs[q], keep, *give, loss_here = call(
+                functools.partial(error_kernel, len(loss)),
+                [bf16(count, rows, width), f32(rows // 2, lats)]
+                + [f32(rows // 2 // GIVE_PARTS, lats)] * GIVE_PARTS
+                + [f32(LOSS_ROWS, BLOCK)],
                 (acts[q], dict_here, resids[q], bias_here, table, hands[c][1], hands[c][0], *loss),
                 after=sent if step < steps else (),
             )
             loss = (loss_here,)
-            gives.append((keep, swap(give)))
+            gives.append((keep, *[swap(g) for g in give]))
             ready.append(errs[q])
         stages = [1] if step == steps - 1 else [0, *range(2, n_tok)] if step == steps else []
         for c in stages:
@@ -433,7 +457,7 @@
                 continue
             q = order[c]
             added = call(
-                add_kernel, [f32(rows // 2, lats)], gives[c], after=sent if step < steps else ()
+                collect_kernel, [f32(rows // 2, lats)], gives[c], after=sent if step < steps else ()
             )[0]
             gacts.append(across(added, q) if q else added)
             ready.append(added)
@@ -460,10 +484,20 @@
     )[0]
     mine = [across(g_pre, q) if q else g_pre for q in range(n_tok)]
     others = [swap(g) for g in mine]
+    early = [(q, side) for side in range(2) for q in range(n_tok) if (q, side) != (1, 1)]
+    halves = [mine, others]
+    early_grads = [halves[side][q] for q, side in early]
+    encoded = call(
+        functools.partial(encode_kernel, (n_tok, early)),
+        [f32(width, lats)],
+        (*resids, *early_grads, decoded),
+    )[0]
     grad, losses = call(
-        functools.partial(encode_kernel, 1.0 / (rows * n_tok * half * n_wid)),
+        functools.partial(
+            last_kernel, (1, [(0, 1)]), 1.0 / (rows * n_tok * half * n_wid), len(early)
+        ),
         [bf16(width, lats), f32(LEVELS)],
-        (*resids, *mine, *others, decoded),
+        (*early_grads, resids[1], others[1], encoded),
         out_specs=[VMEM, SMEM],
     )
     return (losses, grad)

time: 86.5 us -> 87.7 us (1.014)
  starting transfers between devices: 57.2 us -> 60 us
  waiting for transfers between devices: 15.6 us -> 14.7 us
    ppermute x12, starting transfers between devices: 23.4 us -> 26.1 us  [body(): got[side].append((lax.ppermute(message, ('lat', 'wid'), pairs), 0))]
    ppermute x12, starting transfers between devices: 19.5 us -> 18 us  [across(): return lax.ppermute(array, 'tok', [(t, t ^ q) for t in range(n_tok)])]
    ppermute x2, waiting for transfers between devices: 5.25 us -> 4.02 us  [body(): other = lax.ppermute(loss, 'lat', [(p, p ^ gap) for p in range(n_lat)])]
    pallas_call x48 -> x49, Pallas kernels: 11.2 us -> 11.5 us  [call(): pl.pallas_call(run, out_shape=outs, in_specs=list(specs or [VMEM] * len(a...]
  transfers between devices with their start and end apart: 40 -> 40, of which waited for: 13 -> 12; matrix products, arithmetic and copies ran while one was open for 0% -> 0% of each run, Pallas kernels for 8% -> 8%
where the time goes in v8:
time: 87.7 us; the launch traced here: 87.3 us
  starting transfers between devices  60 us (68%)
  waiting for transfers between devices  14.7 us (17%)
  Pallas kernels  11.5 us (13%)
  between operations  1.25 us (1%)
    ppermute x12, starting transfers between devices, body(): got[side].append((lax.ppermute(message, ('lat', 'wid'), pairs), 0))  26.1 us
    ppermute x12, starting transfers between devices, across(): return lax.ppermute(array, 'tok', [(t, t ^ q) for t in range(n_tok)])  18 us
    ppermute x14, starting transfers between devices, swap(): return lax.ppermute(array, 'wid', [(w, w ^ 1) for w in range(n_wid)])  13.2 us
    pallas_call x49, Pallas kernels, call(): pl.pallas_call(run, out_shape=outs, in_specs=list(specs or [VMEM] * len(a...  11.5 us
    ppermute x12, waiting for transfers between devices, across(): return lax.ppermute(array, 'tok', [(t, t ^ q) for t in range(n_tok)])  6.16 us
    ppermute x2, waiting for transfers between devices, body(): other = lax.ppermute(loss, 'lat', [(p, p ^ gap) for p in range(n_lat)])  4.02 us
    ppermute x14, waiting for transfers between devices, swap(): return lax.ppermute(array, 'wid', [(w, w ^ 1) for w in range(n_wid)])  3.25 us
    ppermute x2, starting transfers between devices, body(): other = lax.ppermute(loss, 'lat', [(p, p ^ gap) for p in range(n_lat)])  2.71 us
  transfers between devices with their start and end apart: 40, of which 12 were waited for; matrix products, arithmetic and copies ran while one was open for 0% of the time, Pallas kernels for 8%

profile of v8, /device:TPU:0, one launch (start us, length us, event | category | flops | bytes accessed | tf_op | source)
XLA Modules:
  0.0 87.3 jit_solution(18317436483693346388)
XLA Ops:
  0.7 2.9 %shard_map.77 = (f32[128,512]{1,0:T(8,128)S(1)}, bf16[512,512]{1,0:T(8,128)(2,1)S(1)}) custom-call(bf16[128,2048]{1,0:T(8,128)(2,1)} %refs_0_.3, bf16[512,2048]{1,0:T(8,128)(2,1)} %refs_1_.1), custom_call_target="tpu_custom_call" | custom-call | bytes 1024 | tf_op jit(solution)/shard_map/pallas_call | solution.py:38
  4.1 1.2 %collective-permute-done.refs_2_.refs_1_ = f32[128,512]{1,0:T(8,128)S(1)} collective-permute-done((f32[128,512]{1,0:T(8,128)S(1)}, f32[128,512]{1,0:T(8,128)S(1)}, u32[]{:S(2)}, u32[]{:S(2)}) %collective-permute-start) | collective-permute-done | bytes 262176 | tf_op jit(solution)/shard_map/ppermute | solution.py:340
  6.1 3.7 %collective-permute-start.4 = (f32[128,512]{1,0:T(8,128)S(1)}, f32[128,512]{1,0:T(8,128)S(1)}, u32[]{:S(2)}, u32[]{:S(2)}) collective-permute-start(f32[128,512]{1,0:T(8,128)S(1)} %get-tuple-element.37.refs_0_.refs_2_), channel_id=1, source_target_pairs={{0,3},{1,2},{2,1},{3,0},{4,7},{5,6},{6,5},{7,4},{8,11},{9,10},{10,... | collective-permute-start | bytes 786440 | tf_op jit(solution)/shard_map/ppermute | solution.py:337
  10.1 3.5 %collective-permute-start.7 = (f32[128,512]{1,0:T(8,128)S(1)}, f32[128,512]{1,0:T(8,128)S(1)}, u32[]{:S(2)}, u32[]{:S(2)}) collective-permute-start(f32[128,512]{1,0:T(8,128)S(1)} %shard_map.87.refs_2_.refs_3_), channel_id=1, source_target_pairs={{0,8},{28,20},{1,9},{29,21},{2,10},{30,22},{3,11},{31,23}} | collective-permute-start | bytes 786440 | tf_op jit(solution)/shard_map/ppermute | solution.py:400
  13.9 1.3 %collective-permute-start.3 = (f32[128,512]{1,0:T(8,128)S(1)}, f32[128,512]{1,0:T(8,128)S(1)}, u32[]{:S(2)}, u32[]{:S(2)}) collective-permute-start(f32[128,512]{1,0:T(8,128)S(1)} %shard_map.81.refs_1_.refs_2_.refs_3_), channel_id=1, source_target_pairs={{0,8},{28,20},{1,9},{29,21},{2,10},{30,22},{3,11},{31,23}} | collective-permute-start | bytes 786440 | tf_op jit(solution)/shard_map/ppermute | solution.py:400
  15.8 1.1 %collective-permute-done.4.refs_0_ = f32[128,512]{1,0:T(8,128)S(1)} collective-permute-done((f32[128,512]{1,0:T(8,128)S(1)}, f32[128,512]{1,0:T(8,128)S(1)}, u32[]{:S(2)}, u32[]{:S(2)}) %collective-permute-start.4) | collective-permute-done | bytes 262176 | tf_op jit(solution)/shard_map/ppermute | solution.py:337
  17.4 4.4 %collective-permute-start.8 = (f32[128,512]{1,0:T(8,128)S(1)}, f32[128,512]{1,0:T(8,128)S(1)}, u32[]{:S(2)}, u32[]{:S(2)}) collective-permute-start(f32[128,512]{1,0:T(8,128)S(1)} %shard_map.89), channel_id=1, source_target_pairs={{0,8},{28,20},{8,16},{20,12},{1,9},{29,21},{9,17},{21,13},{2,10},{... | collective-permute-start | bytes 786440 | tf_op jit(solution)/shard_map/ppermute | solution.py:411
  22.2 2.9 %collective-permute-start.5 = (f32[128,512]{1,0:T(8,128)S(1)}, f32[128,512]{1,0:T(8,128)S(1)}, u32[]{:S(2)}, u32[]{:S(2)}) collective-permute-start(f32[128,512]{1,0:T(8,128)S(1)} %shard_map.84.refs_1_.refs_4_), channel_id=1, source_target_pairs={{0,8},{28,20},{8,16},{20,12},{1,9},{29,21},{9,17},{21,13},{2,10},{... | collective-permute-start | bytes 786440 | tf_op jit(solution)/shard_map/ppermute | solution.py:411
  25.1 1.6 %collective-permute-start.1 = (f32[128,512]{1,0:T(8,128)S(1)}, f32[128,512]{1,0:T(8,128)S(1)}, u32[]{:S(2)}, u32[]{:S(2)}) collective-permute-start(f32[128,512]{1,0:T(8,128)S(1)} %get-tuple-element.37.refs_0_.refs_2_), channel_id=1, source_target_pairs={{0,2},{1,3},{2,0},{3,1},{4,6},{5,7},{6,4},{7,5},{8,10},{9,11},{10,... | collective-permute-start | bytes 786440 | tf_op jit(solution)/shard_map/ppermute | solution.py:337
  26.7 1.5 %collective-permute-start.11 = (f32[128,512]{1,0:T(8,128)S(1)}, f32[128,512]{1,0:T(8,128)S(1)}, u32[]{:S(2)}, u32[]{:S(2)}) collective-permute-start(f32[128,512]{1,0:T(8,128)S(1)} %get-tuple-element.41), channel_id=1, source_target_pairs={{0,3},{1,2},{2,1},{3,0},{4,7},{5,6},{6,5},{7,4},{8,11},{9,10},{10,... | collective-permute-start | bytes 786440 | tf_op jit(solution)/shard_map/ppermute | solution.py:337
  28.6 1.9 %collective-permute-start.10 = (f32[128,512]{1,0:T(8,128)S(1)}, f32[128,512]{1,0:T(8,128)S(1)}, u32[]{:S(2)}, u32[]{:S(2)}) collective-permute-start(f32[128,512]{1,0:T(8,128)S(1)} %shard_map.91.refs_4_), channel_id=1, source_target_pairs={{0,8},{28,20},{8,16},{20,12},{16,24},{12,4},{1,9},{29,21},{9,17},{... | collective-permute-start | bytes 786440 | tf_op jit(solution)/shard_map/ppermute | solution.py:411
  30.9 2.5 %collective-permute-start.13 = (f32[128,512]{1,0:T(8,128)S(1)}, f32[128,512]{1,0:T(8,128)S(1)}, u32[]{:S(2)}, u32[]{:S(2)}) collective-permute-start(f32[128,512]{1,0:T(8,128)S(1)} %shard_map.92.refs_1_.refs_4_), channel_id=1, source_target_pairs={{0,8},{28,20},{8,16},{20,12},{16,24},{12,4},{1,9},{29,21},{9,17},{... | collective-permute-start | bytes 786440 | tf_op jit(solution)/shard_map/ppermute | solution.py:411
  33.4 1.6 %collective-permute-start.14 = (f32[128,512]{1,0:T(8,128)S(1)}, f32[128,512]{1,0:T(8,128)S(1)}, u32[]{:S(2)}, u32[]{:S(2)}) collective-permute-start(f32[128,512]{1,0:T(8,128)S(1)} %get-tuple-element.42), channel_id=1, source_target_pairs={{0,1},{1,0},{2,3},{3,2},{4,5},{5,4},{6,7},{7,6},{8,9},{9,8},{10,11... | collective-permute-start | bytes 786440 | tf_op jit(solution)/shard_map/ppermute | solution.py:337
  35.3 3.5 %collective-permute-start.12 = (f32[128,512]{1,0:T(8,128)S(1)}, f32[128,512]{1,0:T(8,128)S(1)}, u32[]{:S(2)}, u32[]{:S(2)}) collective-permute-start(f32[128,512]{1,0:T(8,128)S(1)} %shard_map.96.refs_4_), channel_id=1, source_target_pairs={{0,8},{28,20},{8,16},{20,12},{16,24},{12,4},{1,9},{29,21},{9,17},{... | collective-permute-start | bytes 786440 | tf_op jit(solution)/shard_map/ppermute | solution.py:411
  39.2 3.4 %collective-permute-start.16 = (f32[128,512]{1,0:T(8,128)S(1)}, f32[128,512]{1,0:T(8,128)S(1)}, u32[]{:S(2)}, u32[]{:S(2)}) collective-permute-start(f32[128,512]{1,0:T(8,128)S(1)} %shard_map.98.refs_3_), channel_id=1, source_target_pairs={{0,8},{28,20},{8,16},{20,12},{16,24},{12,4},{1,9},{29,21},{9,17},{... | collective-permute-start | bytes 786440 | tf_op jit(solution)/shard_map/ppermute | solution.py:411
  42.6 1.9 %collective-permute-start.9 = (f32[128,512]{1,0:T(8,128)S(1)}, f32[128,512]{1,0:T(8,128)S(1)}, u32[]{:S(2)}, u32[]{:S(2)}) collective-permute-start(f32[128,512]{1,0:T(8,128)S(1)} %get-tuple-element.39), channel_id=1, source_target_pairs={{0,2},{1,3},{2,0},{3,1},{4,6},{5,7},{6,4},{7,5},{8,10},{9,11},{10,... | collective-permute-start | bytes 786440 | tf_op jit(solution)/shard_map/ppermute | solution.py:337
  45.4 1.0 %collective-permute-done.16.refs_0_.refs_2_.refs_1_ = f32[128,512]{1,0:T(8,128)S(1)} collective-permute-done((f32[128,512]{1,0:T(8,128)S(1)}, f32[128,512]{1,0:T(8,128)S(1)}, u32[]{:S(2)}, u32[]{:S(2)}) %collective-permute-start.16) | collective-permute-done | bytes 262176 | tf_op jit(solution)/shard_map/ppermute | solution.py:411
  47.2 0.8 collective-permute-start.20
  51.1 6.0 %collective-permute-start.21 = (f32[64,512]{1,0:T(8,128)S(1)}, f32[64,512]{1,0:T(8,128)S(1)}, u32[]{:S(2)}, u32[]{:S(2)}) collective-permute-start(f32[64,512]{1,0:T(8,128)S(1)} %get-tuple-element.48), channel_id=1, source_target_pairs={{0,4},{4,0},{1,5},{5,1},{2,6},{6,2},{3,7},{7,3},{8,12},{12,8},{9,1... | collective-permute-start | bytes 393224 | tf_op jit(solution)/shard_map/ppermute | solution.py:340
  57.3 0.8 collective-permute-done.21.refs_1_
  58.3 4.0 %collective-permute-start.23 = (f32[128,512]{1,0:T(8,128)S(1)}, f32[128,512]{1,0:T(8,128)S(1)}, u32[]{:S(2)}, u32[]{:S(2)}) collective-permute-start(f32[128,512]{1,0:T(8,128)S(1)} %shard_map.113), channel_id=1, source_target_pairs={{0,4},{4,0},{1,5},{5,1},{2,6},{6,2},{3,7},{7,3},{8,12},{12,8},{9,1... | collective-permute-start | bytes 786440 | tf_op jit(solution)/shard_map/ppermute | solution.py:340
  64.7 1.5 %collective-permute-start.27 = (f32[64,512]{1,0:T(8,128)S(1)}, f32[64,512]{1,0:T(8,128)S(1)}, u32[]{:S(2)}, u32[]{:S(2)}) collective-permute-start(f32[64,512]{1,0:T(8,128)S(1)} %shard_map.111.refs_6_), channel_id=1, source_target_pairs={{0,3},{1,2},{2,1},{3,0},{4,7},{5,6},{6,5},{7,4},{8,11},{9,10},{10,... | collective-permute-start | bytes 393224 | tf_op jit(solution)/shard_map/ppermute | solution.py:337
  66.5 1.9 %collective-permute-start.32 = (f32[64,512]{1,0:T(8,128)S(1)}, f32[64,512]{1,0:T(8,128)S(1)}, u32[]{:S(2)}, u32[]{:S(2)}) collective-permute-start(f32[64,512]{1,0:T(8,128)S(1)} %shard_map.121), channel_id=1, source_target_pairs={{0,2},{1,3},{2,0},{3,1},{4,6},{5,7},{6,4},{7,5},{8,10},{9,11},{10,... | collective-permute-start | bytes 393224 | tf_op jit(solution)/shard_map/ppermute | solution.py:337
  68.5 2.1 %collective-permute-done.25.refs_1_ = f32[32,512]{1,0:T(8,128)S(1)} collective-permute-done((f32[32,512]{1,0:T(8,128)S(1)}, f32[32,512]{1,0:T(8,128)S(1)}, u32[]{:S(2)}, u32[]{:S(2)}) %collective-permute-start.25) | collective-permute-done | bytes 65568 | tf_op jit(solution)/shard_map/ppermute | solution.py:470
  70.5 2.7 %collective-permute-start.26 = (f32[32,512]{1,0:T(8,128)S(1)}, f32[32,512]{1,0:T(8,128)S(1)}, u32[]{:S(2)}, u32[]{:S(2)}) collective-permute-start(f32[32,512]{1,0:T(8,128)S(1)} %shard_map.117.refs_0_), channel_id=1, source_target_pairs={{0,16},{8,24},{16,0},{24,8},{1,17},{9,25},{17,1},{25,9},{2,18},{10... | collective-permute-start | bytes 196616 | tf_op jit(solution)/shard_map/ppermute | solution.py:470
  74.0 1.9 %collective-permute-done.26.refs_1_ = f32[32,512]{1,0:T(8,128)S(1)} collective-permute-done((f32[32,512]{1,0:T(8,128)S(1)}, f32[32,512]{1,0:T(8,128)S(1)}, u32[]{:S(2)}, u32[]{:S(2)}) %collective-permute-start.26) | collective-permute-done | bytes 65568 | tf_op jit(solution)/shard_map/ppermute | solution.py:470
  76.1 2.0 %collective-permute-start.35 = (f32[72,512]{1,0:T(8,128)S(1)}, f32[72,512]{1,0:T(8,128)S(1)}, u32[]{:S(2)}, u32[]{:S(2)}) collective-permute-start(f32[72,512]{1,0:T(8,128)S(1)} %shard_map.123.refs_4_.refs_0_), channel_id=1, source_target_pairs={{0,3},{1,2},{2,1},{3,0},{4,7},{5,6},{6,5},{7,4},{8,11},{9,10},{10,... | collective-permute-start | bytes 442376 | tf_op jit(solution)/shard_map/ppermute | solution.py:337
  78.4 1.3 %collective-permute-start.33 = (f32[72,512]{1,0:T(8,128)S(1)}, f32[72,512]{1,0:T(8,128)S(1)}, u32[]{:S(2)}, u32[]{:S(2)}) collective-permute-start(f32[72,512]{1,0:T(8,128)S(1)} %shard_map.123.refs_4_.refs_0_), channel_id=1, source_target_pairs={{0,1},{1,0},{2,3},{3,2},{4,5},{5,4},{6,7},{7,6},{8,9},{9,8},{10,11... | collective-permute-start | bytes 442376 | tf_op jit(solution)/shard_map/ppermute | solution.py:337
  79.7 3.2 %collective-permute-done.35.refs_7_.refs_3_ = f32[72,512]{1,0:T(8,128)S(1)} collective-permute-done((f32[72,512]{1,0:T(8,128)S(1)}, f32[72,512]{1,0:T(8,128)S(1)}, u32[]{:S(2)}, u32[]{:S(2)}) %collective-permute-start.35) | collective-permute-done | bytes 147488 | tf_op jit(solution)/shard_map/ppermute | solution.py:337
  82.9 1.5 %collective-permute-done.34.refs_6_.refs_2_ = f32[72,512]{1,0:T(8,128)S(1)} collective-permute-done((f32[72,512]{1,0:T(8,128)S(1)}, f32[72,512]{1,0:T(8,128)S(1)}, u32[]{:S(2)}, u32[]{:S(2)}) %collective-permute-start.34) | collective-permute-done | bytes 147488 | tf_op jit(solution)/shard_map/ppermute | solution.py:337
  84.9 0.9 collective-permute-done.37.refs_9_.refs_5_
  86.2 1.1 %shard_map.125 = (bf16[512,512]{1,0:T(8,128)(2,1)}, f32[4]{0:T(128)}) custom-call(f32[72,512]{1,0:T(8,128)S(1)} %shard_map.123.refs_4_.refs_0_, f32[72,512]{1,0:T(8,128)S(1)} %collective-permute-done.33.refs_5_.refs_1_, f32[72,512]{1,0:T(8,128)S(1)} %collective-permute-done.34.refs_6_.refs_2_, f32[72,512]{1,0:T(8,128)S(1)} %collective-permute-done.35.refs_7_.refs_3_, ...), custom_call_target="tpu_custom_call" | custom-call | bytes 1024 | tf_op jit(solution)/shard_map/pallas_call | solution.py:38
  (107 shorter events, 14.6 us)
Async XLA Ops:
  5.4 8.2 %collective-permute-start.2 = (f32[512,512]{1,0:T(8,128)S(1)}, f32[512,512]{1,0:T(8,128)S(1)}, u32[]{:S(2)}, u32[]{:S(2)}) collective-permute-start(f32[512,512]{1,0:T(8,128)S(1)} %get-tuple-element.34.refs_4_), channel_id=1, source_target_pairs={{0,4},{4,0},{1,5},{5,1},{2,6},{6,2},{3,7},{7,3},{8,12},{12,8},{9,1... | collective-permute-start | bytes 3145736 | tf_op jit(solution)/shard_map/ppermute | solution.py:340
  6.1 10.8 %collective-permute-start.4 = (f32[128,512]{1,0:T(8,128)S(1)}, f32[128,512]{1,0:T(8,128)S(1)}, u32[]{:S(2)}, u32[]{:S(2)}) collective-permute-start(f32[128,512]{1,0:T(8,128)S(1)} %get-tuple-element.37.refs_0_.refs_2_), channel_id=1, source_target_pairs={{0,3},{1,2},{2,1},{3,0},{4,7},{5,6},{6,5},{7,4},{8,11},{9,10},{10,... | collective-permute-start | bytes 786440 | tf_op jit(solution)/shard_map/ppermute | solution.py:337
  10.1 7.4 %collective-permute-start.7 = (f32[128,512]{1,0:T(8,128)S(1)}, f32[128,512]{1,0:T(8,128)S(1)}, u32[]{:S(2)}, u32[]{:S(2)}) collective-permute-start(f32[128,512]{1,0:T(8,128)S(1)} %shard_map.87.refs_2_.refs_3_), channel_id=1, source_target_pairs={{0,8},{28,20},{1,9},{29,21},{2,10},{30,22},{3,11},{31,23}} | collective-permute-start | bytes 786440 | tf_op jit(solution)/shard_map/ppermute | solution.py:400
  13.9 8.3 %collective-permute-start.3 = (f32[128,512]{1,0:T(8,128)S(1)}, f32[128,512]{1,0:T(8,128)S(1)}, u32[]{:S(2)}, u32[]{:S(2)}) collective-permute-start(f32[128,512]{1,0:T(8,128)S(1)} %shard_map.81.refs_1_.refs_2_.refs_3_), channel_id=1, source_target_pairs={{0,8},{28,20},{1,9},{29,21},{2,10},{30,22},{3,11},{31,23}} | collective-permute-start | bytes 786440 | tf_op jit(solution)/shard_map/ppermute | solution.py:400
  15.2 13.1 %collective-permute-start.6 = (f32[128,512]{1,0:T(8,128)S(1)}, f32[128,512]{1,0:T(8,128)S(1)}, u32[]{:S(2)}, u32[]{:S(2)}) collective-permute-start(f32[128,512]{1,0:T(8,128)S(1)} %get-tuple-element.37.refs_0_.refs_2_), channel_id=1, source_target_pairs={{0,1},{1,0},{2,3},{3,2},{4,5},{5,4},{6,7},{7,6},{8,9},{9,8},{10,11... | collective-permute-start | bytes 786440 | tf_op jit(solution)/shard_map/ppermute | solution.py:337
  17.4 11.1 %collective-permute-start.8 = (f32[128,512]{1,0:T(8,128)S(1)}, f32[128,512]{1,0:T(8,128)S(1)}, u32[]{:S(2)}, u32[]{:S(2)}) collective-permute-start(f32[128,512]{1,0:T(8,128)S(1)} %shard_map.89), channel_id=1, source_target_pairs={{0,8},{28,20},{8,16},{20,12},{1,9},{29,21},{9,17},{21,13},{2,10},{... | collective-permute-start | bytes 786440 | tf_op jit(solution)/shard_map/ppermute | solution.py:411
  22.2 8.6 %collective-permute-start.5 = (f32[128,512]{1,0:T(8,128)S(1)}, f32[128,512]{1,0:T(8,128)S(1)}, u32[]{:S(2)}, u32[]{:S(2)}) collective-permute-start(f32[128,512]{1,0:T(8,128)S(1)} %shard_map.84.refs_1_.refs_4_), channel_id=1, source_target_pairs={{0,8},{28,20},{8,16},{20,12},{1,9},{29,21},{9,17},{21,13},{2,10},{... | collective-permute-start | bytes 786440 | tf_op jit(solution)/shard_map/ppermute | solution.py:411
  25.1 9.9 %collective-permute-start.1 = (f32[128,512]{1,0:T(8,128)S(1)}, f32[128,512]{1,0:T(8,128)S(1)}, u32[]{:S(2)}, u32[]{:S(2)}) collective-permute-start(f32[128,512]{1,0:T(8,128)S(1)} %get-tuple-element.37.refs_0_.refs_2_), channel_id=1, source_target_pairs={{0,2},{1,3},{2,0},{3,1},{4,6},{5,7},{6,4},{7,5},{8,10},{9,11},{10,... | collective-permute-start | bytes 786440 | tf_op jit(solution)/shard_map/ppermute | solution.py:337
  26.7 8.5 %collective-permute-start.11 = (f32[128,512]{1,0:T(8,128)S(1)}, f32[128,512]{1,0:T(8,128)S(1)}, u32[]{:S(2)}, u32[]{:S(2)}) collective-permute-start(f32[128,512]{1,0:T(8,128)S(1)} %get-tuple-element.41), channel_id=1, source_target_pairs={{0,3},{1,2},{2,1},{3,0},{4,7},{5,6},{6,5},{7,4},{8,11},{9,10},{10,... | collective-permute-start | bytes 786440 | tf_op jit(solution)/shard_map/ppermute | solution.py:337
  28.6 6.7 %collective-permute-start.10 = (f32[128,512]{1,0:T(8,128)S(1)}, f32[128,512]{1,0:T(8,128)S(1)}, u32[]{:S(2)}, u32[]{:S(2)}) collective-permute-start(f32[128,512]{1,0:T(8,128)S(1)} %shard_map.91.refs_4_), channel_id=1, source_target_pairs={{0,8},{28,20},{8,16},{20,12},{16,24},{12,4},{1,9},{29,21},{9,17},{... | collective-permute-start | bytes 786440 | tf_op jit(solution)/shard_map/ppermute | solution.py:411
  30.9 8.3 %collective-permute-start.13 = (f32[128,512]{1,0:T(8,128)S(1)}, f32[128,512]{1,0:T(8,128)S(1)}, u32[]{:S(2)}, u32[]{:S(2)}) collective-permute-start(f32[128,512]{1,0:T(8,128)S(1)} %shard_map.92.refs_1_.refs_4_), channel_id=1, source_target_pairs={{0,8},{28,20},{8,16},{20,12},{16,24},{12,4},{1,9},{29,21},{9,17},{... | collective-permute-start | bytes 786440 | tf_op jit(solution)/shard_map/ppermute | solution.py:411
  33.4 11.3 %collective-permute-start.14 = (f32[128,512]{1,0:T(8,128)S(1)}, f32[128,512]{1,0:T(8,128)S(1)}, u32[]{:S(2)}, u32[]{:S(2)}) collective-permute-start(f32[128,512]{1,0:T(8,128)S(1)} %get-tuple-element.42), channel_id=1, source_target_pairs={{0,1},{1,0},{2,3},{3,2},{4,5},{5,4},{6,7},{7,6},{8,9},{9,8},{10,11... | collective-permute-start | bytes 786440 | tf_op jit(solution)/shard_map/ppermute | solution.py:337
  35.3 9.4 %collective-permute-start.12 = (f32[128,512]{1,0:T(8,128)S(1)}, f32[128,512]{1,0:T(8,128)S(1)}, u32[]{:S(2)}, u32[]{:S(2)}) collective-permute-start(f32[128,512]{1,0:T(8,128)S(1)} %shard_map.96.refs_4_), channel_id=1, source_target_pairs={{0,8},{28,20},{8,16},{20,12},{16,24},{12,4},{1,9},{29,21},{9,17},{... | collective-permute-start | bytes 786440 | tf_op jit(solution)/shard_map/ppermute | solution.py:411
  39.2 7.3 %collective-permute-start.16 = (f32[128,512]{1,0:T(8,128)S(1)}, f32[128,512]{1,0:T(8,128)S(1)}, u32[]{:S(2)}, u32[]{:S(2)}) collective-permute-start(f32[128,512]{1,0:T(8,128)S(1)} %shard_map.98.refs_3_), channel_id=1, source_target_pairs={{0,8},{28,20},{8,16},{20,12},{16,24},{12,4},{1,9},{29,21},{9,17},{... | collective-permute-start | bytes 786440 | tf_op jit(solution)/shard_map/ppermute | solution.py:411
  42.6 6.4 %collective-permute-start.9 = (f32[128,512]{1,0:T(8,128)S(1)}, f32[128,512]{1,0:T(8,128)S(1)}, u32[]{:S(2)}, u32[]{:S(2)}) collective-permute-start(f32[128,512]{1,0:T(8,128)S(1)} %get-tuple-element.39), channel_id=1, source_target_pairs={{0,2},{1,3},{2,0},{3,1},{4,6},{5,7},{6,4},{7,5},{8,10},{9,11},{10,... | collective-permute-start | bytes 786440 | tf_op jit(solution)/shard_map/ppermute | solution.py:337
  44.6 3.5 %collective-permute-start.17 = (f32[128,512]{1,0:T(8,128)S(1)}, f32[128,512]{1,0:T(8,128)S(1)}, u32[]{:S(2)}, u32[]{:S(2)}) collective-permute-start(f32[128,512]{1,0:T(8,128)S(1)} %shard_map.99.refs_5_), channel_id=1, source_target_pairs={{0,4},{4,0},{1,5},{5,1},{2,6},{6,2},{3,7},{7,3},{8,12},{12,8},{9,1... | collective-permute-start | bytes 786440 | tf_op jit(solution)/shard_map/ppermute | solution.py:340
  44.8 4.3 %collective-permute-start.15 = (f32[128,512]{1,0:T(8,128)S(1)}, f32[128,512]{1,0:T(8,128)S(1)}, u32[]{:S(2)}, u32[]{:S(2)}) collective-permute-start(f32[128,512]{1,0:T(8,128)S(1)} %shard_map.101.refs_3_), channel_id=1, source_target_pairs={{8,16},{20,12},{16,24},{12,4},{9,17},{21,13},{17,25},{13,5},{10,18... | collective-permute-start | bytes 786440 | tf_op jit(solution)/shard_map/ppermute | solution.py:411
  49.1 9.1 %collective-permute-start.18 = (f32[128,512]{1,0:T(8,128)S(1)}, f32[128,512]{1,0:T(8,128)S(1)}, u32[]{:S(2)}, u32[]{:S(2)}) collective-permute-start(f32[128,512]{1,0:T(8,128)S(1)} %shard_map.106.refs_2_), channel_id=1, source_target_pairs={{16,24},{12,4},{17,25},{13,5},{18,26},{14,6},{19,27},{15,7}} | collective-permute-start | bytes 786440 | tf_op jit(solution)/shard_map/ppermute | solution.py:411
  49.8 8.5 %collective-permute-start.22 = (f32[128,512]{1,0:T(8,128)S(1)}, f32[128,512]{1,0:T(8,128)S(1)}, u32[]{:S(2)}, u32[]{:S(2)}) collective-permute-start(f32[128,512]{1,0:T(8,128)S(1)} %shard_map.107.refs_3_.refs_8_.refs_2_), channel_id=1, source_target_pairs={{16,24},{12,4},{17,25},{13,5},{18,26},{14,6},{19,27},{15,7}} | collective-permute-start | bytes 786440 | tf_op jit(solution)/shard_map/ppermute | solution.py:411
  51.1 7.0 %collective-permute-start.21 = (f32[64,512]{1,0:T(8,128)S(1)}, f32[64,512]{1,0:T(8,128)S(1)}, u32[]{:S(2)}, u32[]{:S(2)}) collective-permute-start(f32[64,512]{1,0:T(8,128)S(1)} %get-tuple-element.48), channel_id=1, source_target_pairs={{0,4},{4,0},{1,5},{5,1},{2,6},{6,2},{3,7},{7,3},{8,12},{12,8},{9,1... | collective-permute-start | bytes 393224 | tf_op jit(solution)/shard_map/ppermute | solution.py:340
  57.2 5.2 %collective-permute-start.24 = (f32[128,512]{1,0:T(8,128)S(1)}, f32[128,512]{1,0:T(8,128)S(1)}, u32[]{:S(2)}, u32[]{:S(2)}) collective-permute-start(f32[128,512]{1,0:T(8,128)S(1)} %shard_map.108.refs_3_), channel_id=1, source_target_pairs={{0,4},{4,0},{1,5},{5,1},{2,6},{6,2},{3,7},{7,3},{8,12},{12,8},{9,1... | collective-permute-start | bytes 786440 | tf_op jit(solution)/shard_map/ppermute | solution.py:340
  58.3 5.2 %collective-permute-start.23 = (f32[128,512]{1,0:T(8,128)S(1)}, f32[128,512]{1,0:T(8,128)S(1)}, u32[]{:S(2)}, u32[]{:S(2)}) collective-permute-start(f32[128,512]{1,0:T(8,128)S(1)} %shard_map.113), channel_id=1, source_target_pairs={{0,4},{4,0},{1,5},{5,1},{2,6},{6,2},{3,7},{7,3},{8,12},{12,8},{9,1... | collective-permute-start | bytes 786440 | tf_op jit(solution)/shard_map/ppermute | solution.py:340
  64.6 8.6 %collective-permute-start.28 = (f32[64,512]{1,0:T(8,128)S(1)}, f32[64,512]{1,0:T(8,128)S(1)}, u32[]{:S(2)}, u32[]{:S(2)}) collective-permute-start(f32[64,512]{1,0:T(8,128)S(1)} %get-tuple-element.53), channel_id=1, source_target_pairs={{0,4},{4,0},{1,5},{5,1},{2,6},{6,2},{3,7},{7,3},{8,12},{12,8},{9,1... | collective-permute-start | bytes 393224 | tf_op jit(solution)/shard_map/ppermute | solution.py:340
  64.7 11.2 %collective-permute-start.27 = (f32[64,512]{1,0:T(8,128)S(1)}, f32[64,512]{1,0:T(8,128)S(1)}, u32[]{:S(2)}, u32[]{:S(2)}) collective-permute-start(f32[64,512]{1,0:T(8,128)S(1)} %shard_map.111.refs_6_), channel_id=1, source_target_pairs={{0,3},{1,2},{2,1},{3,0},{4,7},{5,6},{6,5},{7,4},{8,11},{9,10},{10,... | collective-permute-start | bytes 393224 | tf_op jit(solution)/shard_map/ppermute | solution.py:337
  66.3 4.3 %collective-permute-start.25 = (f32[32,512]{1,0:T(8,128)S(1)}, f32[32,512]{1,0:T(8,128)S(1)}, u32[]{:S(2)}, u32[]{:S(2)}) collective-permute-start(f32[32,512]{1,0:T(8,128)S(1)} %shard_map.116.refs_0_), channel_id=1, source_target_pairs={{0,8},{8,0},{16,24},{24,16},{1,9},{9,1},{17,25},{25,17},{2,10},{10... | collective-permute-start | bytes 196616 | tf_op jit(solution)/shard_map/ppermute | solution.py:470
  66.3 9.7 %collective-permute-start.30 = (f32[64,512]{1,0:T(8,128)S(1)}, f32[64,512]{1,0:T(8,128)S(1)}, u32[]{:S(2)}, u32[]{:S(2)}) collective-permute-start(f32[64,512]{1,0:T(8,128)S(1)} %shard_map.120), channel_id=1, source_target_pairs={{0,1},{1,0},{2,3},{3,2},{4,5},{5,4},{6,7},{7,6},{8,9},{9,8},{10,11... | collective-permute-start | bytes 393224 | tf_op jit(solution)/shard_map/ppermute | solution.py:337
  66.5 9.5 %collective-permute-start.32 = (f32[64,512]{1,0:T(8,128)S(1)}, f32[64,512]{1,0:T(8,128)S(1)}, u32[]{:S(2)}, u32[]{:S(2)}) collective-permute-start(f32[64,512]{1,0:T(8,128)S(1)} %shard_map.121), channel_id=1, source_target_pairs={{0,2},{1,3},{2,0},{3,1},{4,6},{5,7},{6,4},{7,5},{8,10},{9,11},{10,... | collective-permute-start | bytes 393224 | tf_op jit(solution)/shard_map/ppermute | solution.py:337
  70.5 5.4 %collective-permute-start.26 = (f32[32,512]{1,0:T(8,128)S(1)}, f32[32,512]{1,0:T(8,128)S(1)}, u32[]{:S(2)}, u32[]{:S(2)}) collective-permute-start(f32[32,512]{1,0:T(8,128)S(1)} %shard_map.117.refs_0_), channel_id=1, source_target_pairs={{0,16},{8,24},{16,0},{24,8},{1,17},{9,25},{17,1},{25,9},{2,18},{10... | collective-permute-start | bytes 196616 | tf_op jit(solution)/shard_map/ppermute | solution.py:470
  76.1 6.7 %collective-permute-start.35 = (f32[72,512]{1,0:T(8,128)S(1)}, f32[72,512]{1,0:T(8,128)S(1)}, u32[]{:S(2)}, u32[]{:S(2)}) collective-permute-start(f32[72,512]{1,0:T(8,128)S(1)} %shard_map.123.refs_4_.refs_0_), channel_id=1, source_target_pairs={{0,3},{1,2},{2,1},{3,0},{4,7},{5,6},{6,5},{7,4},{8,11},{9,10},{10,... | collective-permute-start | bytes 442376 | tf_op jit(solution)/shard_map/ppermute | solution.py:337
  78.1 6.2 %collective-permute-start.34 = (f32[72,512]{1,0:T(8,128)S(1)}, f32[72,512]{1,0:T(8,128)S(1)}, u32[]{:S(2)}, u32[]{:S(2)}) collective-permute-start(f32[72,512]{1,0:T(8,128)S(1)} %shard_map.123.refs_4_.refs_0_), channel_id=1, source_target_pairs={{0,2},{1,3},{2,0},{3,1},{4,6},{5,7},{6,4},{7,5},{8,10},{9,11},{10,... | collective-permute-start | bytes 442376 | tf_op jit(solution)/shard_map/ppermute | solution.py:337
  78.4 5.9 %collective-permute-start.33 = (f32[72,512]{1,0:T(8,128)S(1)}, f32[72,512]{1,0:T(8,128)S(1)}, u32[]{:S(2)}, u32[]{:S(2)}) collective-permute-start(f32[72,512]{1,0:T(8,128)S(1)} %shard_map.123.refs_4_.refs_0_), channel_id=1, source_target_pairs={{0,1},{1,0},{2,3},{3,2},{4,5},{5,4},{6,7},{7,6},{8,9},{9,8},{10,11... | collective-permute-start | bytes 442376 | tf_op jit(solution)/shard_map/ppermute | solution.py:337
  79.7 5.2 %collective-permute-start.36 = (f32[72,512]{1,0:T(8,128)S(1)}, f32[72,512]{1,0:T(8,128)S(1)}, u32[]{:S(2)}, u32[]{:S(2)}) collective-permute-start(f32[72,512]{1,0:T(8,128)S(1)} %shard_map.123.refs_4_.refs_0_), channel_id=1, source_target_pairs={{0,4},{4,0},{1,5},{5,1},{2,6},{6,2},{3,7},{7,3},{8,12},{12,8},{9,1... | collective-permute-start | bytes 442376 | tf_op jit(solution)/shard_map/ppermute | solution.py:340
  (13 other events, 53.5 us)

commit v9 on v8

--- a/solution.py
+++ b/solution.py
@@ -10,7 +10,6 @@
 LEVELS = 4
 BLOCK = 128
 LOSS_ROWS = 8
-LOSS_PART = 4
 GIVE_PARTS = 1
 GELU_C = 0.7978845608028654
 GELU_A = 0.044715
@@ -148,8 +147,8 @@
     return pl.ds(pl.multiple_of(wid * (rows // 2), rows // 2), rows // 2)
 
 
-def g_pre_kernel(pre_ref, mask, loss, *refs):
-    terms, out = refs[:-1], refs[-1]
+def g_pre_kernel(n_losses, pre_ref, mask, *refs):
+    losses, terms, out = refs[:n_losses], refs[n_losses:-1], refs[-1]
     mine = half_of(lax.axis_index("wid"), pre_ref.shape[0])
     pre = pre_ref[mine, :]
     inner = GELU_C * (pre + GELU_A * (pre * pre * pre))
@@ -160,7 +159,10 @@
     rows = pre.shape[0]
     out[:rows, :] = jnp.where(hit, deriv * total_of([t[...] for t in terms]), 0.0)
     out[rows:, :] = jnp.zeros_like(out[rows:, :])
-    out[rows:, :BLOCK] = loss[:LOSS_ROWS, :BLOCK]
+    loss = losses[0][...]
+    if n_losses > 1:
+        loss = jnp.where(lax.axis_index("wid") == 0, loss, 0.0) + losses[1][...] + losses[2][...]
+    out[rows:, :BLOCK] = loss
 
 
 def running_parts(act, dict_ref):
@@ -263,11 +265,6 @@
             give_out[:, cols] = given[part * size : (part + 1) * size, :]
 
 
-def spread_kernel(loss, out):
-    out[...] = jnp.zeros_like(out)
-    out[:LOSS_ROWS, :BLOCK] = loss[...]
-
-
 def collect_kernel(keep, *refs):
     parts, out = refs[:-1], refs[-1]
     for i, part in enumerate(parts):
@@ -373,7 +370,7 @@
     )
     resids = [piece if q == 0 else across(piece, q) for q, piece in enumerate(pieces)]
 
-    order = [0, 3, 1, 2] if n_tok == 4 else list(range(n_tok))
+    order = [0, 1, 3, 2] if n_tok == 4 else list(range(n_tok))
     steps = n_tok + n_lat - 2
     places = list(range(1, n_lat))
     acts, errs, hands, gives, gacts, loss = {}, {}, [], [], [], ()
@@ -465,11 +462,18 @@
             waits[step + 1] += ready
         ready_before = ready
 
-    loss, gap = call(spread_kernel, [f32(rows // LOSS_PART, lats)], loss)[0], 1
+    loss, gap = loss[0], 4 if n_lat % 4 == 0 else 1
     while gap < n_lat:
         other = lax.ppermute(loss, "lat", [(p, p ^ gap) for p in range(n_lat)])
         loss = call(add_kernel, [f32(*loss.shape)], (loss, other))[0]
         gap *= 2
+    losses = (loss,)
+    if n_lat % 4 == 0:
+        loss = call(add_kernel, [f32(*loss.shape)], (loss, swap(loss)))[0]
+        pairs = [(2 * p + w, 2 * (p ^ (1 + w)) + w) for p in range(n_lat) for w in range(2)]
+        near = lax.ppermute(loss, ("lat", "wid"), pairs)
+        pairs = [(2 * p + 1, 2 * (p ^ 3) + 1) for p in range(n_lat)]
+        losses = (loss, near, lax.ppermute(loss, ("lat", "wid"), pairs))
 
     decoded = call(
         decode_kernel,
@@ -477,9 +481,9 @@
         (*[errs[q] for q in order], *[acts[q] for q in order]),
     )[0]
     g_pre = call(
-        g_pre_kernel,
+        functools.partial(g_pre_kernel, len(losses)),
         [f32(rows // 2 + LOSS_ROWS, lats)],
-        (pre, mask, loss, *gacts),
+        (pre, mask, *losses, *gacts),
         after=(decoded,),
     )[0]
     mine = [across(g_pre, q) if q else g_pre for q in range(n_tok)]

time: 87.7 us -> 86.6 us (0.987)
  waiting for transfers between devices: 14.7 us -> 12.1 us
  starting transfers between devices: 60 us -> 61.4 us
    ppermute x14 -> x15, starting transfers between devices: 13.2 us -> 17.8 us  [swap(): return lax.ppermute(array, 'wid', [(w, w ^ 1) for w in range(n_wid)])]
    ppermute x2, waiting for transfers between devices: 4.02 us -> 0.51 us  [the longest x1 0.5 us: body(): near = lax.ppermute(loss, ('lat', 'wid'), pairs)]
    ppermute x12, starting transfers between devices: 26.1 us -> 23.4 us  [body(): got[side].append((lax.ppermute(message, ('lat', 'wid'), pairs), 0))]
    ppermute x2, starting transfers between devices: 2.71 us -> 0.72 us  [the longest x1 0.65 us: body(): losses = (loss, near, lax.ppermute(loss, ('lat', 'wid'), pairs))]
    ppermute x12, starting transfers between devices: 18 us -> 19.5 us  [across(): return lax.ppermute(array, 'tok', [(t, t ^ q) for t in range(n_tok)])]
    ppermute x14 -> x15, waiting for transfers between devices: 3.25 us -> 4.15 us  [swap(): return lax.ppermute(array, 'wid', [(w, w ^ 1) for w in range(n_wid)])]
    pallas_call x49 -> x47, Pallas kernels: 11.5 us -> 11.5 us  [call(): pl.pallas_call(run, out_shape=outs, in_specs=list(specs or [VMEM] * len(a...]
  transfers between devices with their start and end apart: 40 -> 41, of which waited for: 12 -> 14; matrix products, arithmetic and copies ran while one was open for 0% -> 0% of each run, Pallas kernels for 8% -> 8%
where the time goes in v9:
time: 86.6 us; the launch traced here: 86.2 us
  starting transfers between devices  61.4 us (71%)
  waiting for transfers between devices  12.1 us (14%)
  Pallas kernels  11.5 us (13%)
  between operations  1.25 us (1%)
    ppermute x12, starting transfers between devices, body(): got[side].append((lax.ppermute(message, ('lat', 'wid'), pairs), 0))  23.4 us
    ppermute x12, starting transfers between devices, across(): return lax.ppermute(array, 'tok', [(t, t ^ q) for t in range(n_tok)])  19.5 us
    ppermute x15, starting transfers between devices, swap(): return lax.ppermute(array, 'wid', [(w, w ^ 1) for w in range(n_wid)])  17.8 us
    pallas_call x47, Pallas kernels, call(): pl.pallas_call(run, out_shape=outs, in_specs=list(specs or [VMEM] * len(a...  11.5 us
    ppermute x12, waiting for transfers between devices, across(): return lax.ppermute(array, 'tok', [(t, t ^ q) for t in range(n_tok)])  5.87 us
    ppermute x15, waiting for transfers between devices, swap(): return lax.ppermute(array, 'wid', [(w, w ^ 1) for w in range(n_wid)])  4.15 us
  transfers between devices with their start and end apart: 41, of which 14 were waited for; matrix products, arithmetic and copies ran while one was open for 0% of the time, Pallas kernels for 8%

profile of v9, /device:TPU:0, one launch (start us, length us, event | category | flops | bytes accessed | tf_op | source)
XLA Modules:
  0.0 86.2 jit_solution(6072022412368663131)
XLA Ops:
  0.7 2.9 %shard_map.77 = (f32[128,512]{1,0:T(8,128)S(1)}, bf16[512,512]{1,0:T(8,128)(2,1)S(1)}) custom-call(bf16[128,2048]{1,0:T(8,128)(2,1)} %refs_0_.3, bf16[512,2048]{1,0:T(8,128)(2,1)} %refs_1_.1), custom_call_target="tpu_custom_call" | custom-call | bytes 1024 | tf_op jit(solution)/shard_map/pallas_call | solution.py:37
  4.1 1.2 %collective-permute-done.refs_2_.refs_1_ = f32[128,512]{1,0:T(8,128)S(1)} collective-permute-done((f32[128,512]{1,0:T(8,128)S(1)}, f32[128,512]{1,0:T(8,128)S(1)}, u32[]{:S(2)}, u32[]{:S(2)}) %collective-permute-start) | collective-permute-done | bytes 262176 | tf_op jit(solution)/shard_map/ppermute | solution.py:337
  6.1 2.7 %collective-permute-start.4 = (f32[128,512]{1,0:T(8,128)S(1)}, f32[128,512]{1,0:T(8,128)S(1)}, u32[]{:S(2)}, u32[]{:S(2)}) collective-permute-start(f32[128,512]{1,0:T(8,128)S(1)} %get-tuple-element.37.refs_0_.refs_2_), channel_id=1, source_target_pairs={{0,1},{1,0},{2,3},{3,2},{4,5},{5,4},{6,7},{7,6},{8,9},{9,8},{10,11... | collective-permute-start | bytes 786440 | tf_op jit(solution)/shard_map/ppermute | solution.py:334
  9.1 3.5 %collective-permute-start.7 = (f32[128,512]{1,0:T(8,128)S(1)}, f32[128,512]{1,0:T(8,128)S(1)}, u32[]{:S(2)}, u32[]{:S(2)}) collective-permute-start(f32[128,512]{1,0:T(8,128)S(1)} %shard_map.87.refs_2_.refs_3_), channel_id=1, source_target_pairs={{0,8},{28,20},{1,9},{29,21},{2,10},{30,22},{3,11},{31,23}} | collective-permute-start | bytes 786440 | tf_op jit(solution)/shard_map/ppermute | solution.py:397
  12.9 1.3 %collective-permute-start.3 = (f32[128,512]{1,0:T(8,128)S(1)}, f32[128,512]{1,0:T(8,128)S(1)}, u32[]{:S(2)}, u32[]{:S(2)}) collective-permute-start(f32[128,512]{1,0:T(8,128)S(1)} %shard_map.81.refs_1_.refs_2_.refs_3_), channel_id=1, source_target_pairs={{0,8},{28,20},{1,9},{29,21},{2,10},{30,22},{3,11},{31,23}} | collective-permute-start | bytes 786440 | tf_op jit(solution)/shard_map/ppermute | solution.py:397
  14.2 1.6 %collective-permute-start.6 = (f32[128,512]{1,0:T(8,128)S(1)}, f32[128,512]{1,0:T(8,128)S(1)}, u32[]{:S(2)}, u32[]{:S(2)}) collective-permute-start(f32[128,512]{1,0:T(8,128)S(1)} %get-tuple-element.37.refs_0_.refs_2_), channel_id=1, source_target_pairs={{0,3},{1,2},{2,1},{3,0},{4,7},{5,6},{6,5},{7,4},{8,11},{9,10},{10,... | collective-permute-start | bytes 786440 | tf_op jit(solution)/shard_map/ppermute | solution.py:334
  16.5 4.4 %collective-permute-start.8 = (f32[128,512]{1,0:T(8,128)S(1)}, f32[128,512]{1,0:T(8,128)S(1)}, u32[]{:S(2)}, u32[]{:S(2)}) collective-permute-start(f32[128,512]{1,0:T(8,128)S(1)} %shard_map.89), channel_id=1, source_target_pairs={{0,8},{28,20},{8,16},{20,12},{1,9},{29,21},{9,17},{21,13},{2,10},{... | collective-permute-start | bytes 786440 | tf_op jit(solution)/shard_map/ppermute | solution.py:408
  21.2 2.5 %collective-permute-start.5 = (f32[128,512]{1,0:T(8,128)S(1)}, f32[128,512]{1,0:T(8,128)S(1)}, u32[]{:S(2)}, u32[]{:S(2)}) collective-permute-start(f32[128,512]{1,0:T(8,128)S(1)} %shard_map.84.refs_1_.refs_4_), channel_id=1, source_target_pairs={{0,8},{28,20},{8,16},{20,12},{1,9},{29,21},{9,17},{21,13},{2,10},{... | collective-permute-start | bytes 786440 | tf_op jit(solution)/shard_map/ppermute | solution.py:408
  23.7 2.0 %collective-permute-start.1 = (f32[128,512]{1,0:T(8,128)S(1)}, f32[128,512]{1,0:T(8,128)S(1)}, u32[]{:S(2)}, u32[]{:S(2)}) collective-permute-start(f32[128,512]{1,0:T(8,128)S(1)} %get-tuple-element.37.refs_0_.refs_2_), channel_id=1, source_target_pairs={{0,2},{1,3},{2,0},{3,1},{4,6},{5,7},{6,4},{7,5},{8,10},{9,11},{10,... | collective-permute-start | bytes 786440 | tf_op jit(solution)/shard_map/ppermute | solution.py:334
  25.8 1.6 %collective-permute-start.11 = (f32[128,512]{1,0:T(8,128)S(1)}, f32[128,512]{1,0:T(8,128)S(1)}, u32[]{:S(2)}, u32[]{:S(2)}) collective-permute-start(f32[128,512]{1,0:T(8,128)S(1)} %get-tuple-element.41), channel_id=1, source_target_pairs={{0,1},{1,0},{2,3},{3,2},{4,5},{5,4},{6,7},{7,6},{8,9},{9,8},{10,11... | collective-permute-start | bytes 786440 | tf_op jit(solution)/shard_map/ppermute | solution.py:334
  27.8 1.9 %collective-permute-start.10 = (f32[128,512]{1,0:T(8,128)S(1)}, f32[128,512]{1,0:T(8,128)S(1)}, u32[]{:S(2)}, u32[]{:S(2)}) collective-permute-start(f32[128,512]{1,0:T(8,128)S(1)} %shard_map.91.refs_4_), channel_id=1, source_target_pairs={{0,8},{28,20},{8,16},{20,12},{16,24},{12,4},{1,9},{29,21},{9,17},{... | collective-permute-start | bytes 786440 | tf_op jit(solution)/shard_map/ppermute | solution.py:408
  30.1 2.0 %collective-permute-start.13 = (f32[128,512]{1,0:T(8,128)S(1)}, f32[128,512]{1,0:T(8,128)S(1)}, u32[]{:S(2)}, u32[]{:S(2)}) collective-permute-start(f32[128,512]{1,0:T(8,128)S(1)} %shard_map.92.refs_1_.refs_4_), channel_id=1, source_target_pairs={{0,8},{28,20},{8,16},{20,12},{16,24},{12,4},{1,9},{29,21},{9,17},{... | collective-permute-start | bytes 786440 | tf_op jit(solution)/shard_map/ppermute | solution.py:408
  32.0 2.9 %collective-permute-start.14 = (f32[128,512]{1,0:T(8,128)S(1)}, f32[128,512]{1,0:T(8,128)S(1)}, u32[]{:S(2)}, u32[]{:S(2)}) collective-permute-start(f32[128,512]{1,0:T(8,128)S(1)} %get-tuple-element.42), channel_id=1, source_target_pairs={{0,3},{1,2},{2,1},{3,0},{4,7},{5,6},{6,5},{7,4},{8,11},{9,10},{10,... | collective-permute-start | bytes 786440 | tf_op jit(solution)/shard_map/ppermute | solution.py:334
  35.4 2.6 %collective-permute-start.12 = (f32[128,512]{1,0:T(8,128)S(1)}, f32[128,512]{1,0:T(8,128)S(1)}, u32[]{:S(2)}, u32[]{:S(2)}) collective-permute-start(f32[128,512]{1,0:T(8,128)S(1)} %shard_map.96.refs_4_), channel_id=1, source_target_pairs={{0,8},{28,20},{8,16},{20,12},{16,24},{12,4},{1,9},{29,21},{9,17},{... | collective-permute-start | bytes 786440 | tf_op jit(solution)/shard_map/ppermute | solution.py:408
  38.4 2.4 %collective-permute-start.16 = (f32[128,512]{1,0:T(8,128)S(1)}, f32[128,512]{1,0:T(8,128)S(1)}, u32[]{:S(2)}, u32[]{:S(2)}) collective-permute-start(f32[128,512]{1,0:T(8,128)S(1)} %shard_map.98.refs_3_), channel_id=1, source_target_pairs={{0,8},{28,20},{8,16},{20,12},{16,24},{12,4},{1,9},{29,21},{9,17},{... | collective-permute-start | bytes 786440 | tf_op jit(solution)/shard_map/ppermute | solution.py:408
  40.8 1.5 %collective-permute-start.9 = (f32[128,512]{1,0:T(8,128)S(1)}, f32[128,512]{1,0:T(8,128)S(1)}, u32[]{:S(2)}, u32[]{:S(2)}) collective-permute-start(f32[128,512]{1,0:T(8,128)S(1)} %get-tuple-element.39), channel_id=1, source_target_pairs={{0,2},{1,3},{2,0},{3,1},{4,6},{5,7},{6,4},{7,5},{8,10},{9,11},{10,... | collective-permute-start | bytes 786440 | tf_op jit(solution)/shard_map/ppermute | solution.py:334
  43.3 1.4 %collective-permute-done.16.refs_0_.refs_2_.refs_1_ = f32[128,512]{1,0:T(8,128)S(1)} collective-permute-done((f32[128,512]{1,0:T(8,128)S(1)}, f32[128,512]{1,0:T(8,128)S(1)}, u32[]{:S(2)}, u32[]{:S(2)}) %collective-permute-start.16) | collective-permute-done | bytes 262176 | tf_op jit(solution)/shard_map/ppermute | solution.py:408
  46.5 0.7 collective-permute-done.9.refs_3_.refs_2_
  49.3 5.7 %collective-permute-start.21 = (f32[64,512]{1,0:T(8,128)S(1)}, f32[64,512]{1,0:T(8,128)S(1)}, u32[]{:S(2)}, u32[]{:S(2)}) collective-permute-start(f32[64,512]{1,0:T(8,128)S(1)} %get-tuple-element.48), channel_id=1, source_target_pairs={{0,4},{4,0},{1,5},{5,1},{2,6},{6,2},{3,7},{7,3},{8,12},{12,8},{9,1... | collective-permute-start | bytes 393224 | tf_op jit(solution)/shard_map/ppermute | solution.py:337
  55.2 0.8 collective-permute-done.21.refs_1_
  56.2 4.0 %collective-permute-start.23 = (f32[128,512]{1,0:T(8,128)S(1)}, f32[128,512]{1,0:T(8,128)S(1)}, u32[]{:S(2)}, u32[]{:S(2)}) collective-permute-start(f32[128,512]{1,0:T(8,128)S(1)} %shard_map.113), channel_id=1, source_target_pairs={{0,4},{4,0},{1,5},{5,1},{2,6},{6,2},{3,7},{7,3},{8,12},{12,8},{9,1... | collective-permute-start | bytes 786440 | tf_op jit(solution)/shard_map/ppermute | solution.py:337
  62.6 1.5 %collective-permute-start.28 = (f32[64,512]{1,0:T(8,128)S(1)}, f32[64,512]{1,0:T(8,128)S(1)}, u32[]{:S(2)}, u32[]{:S(2)}) collective-permute-start(f32[64,512]{1,0:T(8,128)S(1)} %shard_map.111.refs_6_), channel_id=1, source_target_pairs={{0,1},{1,0},{2,3},{3,2},{4,5},{5,4},{6,7},{7,6},{8,9},{9,8},{10,11... | collective-permute-start | bytes 393224 | tf_op jit(solution)/shard_map/ppermute | solution.py:334
  64.7 1.5 %collective-permute-start.33 = (f32[64,512]{1,0:T(8,128)S(1)}, f32[64,512]{1,0:T(8,128)S(1)}, u32[]{:S(2)}, u32[]{:S(2)}) collective-permute-start(f32[64,512]{1,0:T(8,128)S(1)} %shard_map.119), channel_id=1, source_target_pairs={{0,2},{1,3},{2,0},{3,1},{4,6},{5,7},{6,4},{7,5},{8,10},{9,11},{10,... | collective-permute-start | bytes 393224 | tf_op jit(solution)/shard_map/ppermute | solution.py:334
  66.3 1.2 %collective-permute-done.25.refs_1_ = f32[8,128]{1,0:T(8,128)S(1)} collective-permute-done((f32[8,128]{1,0:T(8,128)S(1)}, f32[8,128]{1,0:T(8,128)S(1)}, u32[]{:S(2)}, u32[]{:S(2)}) %collective-permute-start.25) | collective-permute-done | bytes 4128 | tf_op jit(solution)/shard_map/ppermute | solution.py:337
  68.2 0.8 shard_map.120.refs_9_.refs_11_
  69.0 2.3 %collective-permute-done.31.refs_7_ = f32[64,512]{1,0:T(8,128)S(1)} collective-permute-done((f32[64,512]{1,0:T(8,128)S(1)}, f32[64,512]{1,0:T(8,128)S(1)}, u32[]{:S(2)}, u32[]{:S(2)}) %collective-permute-start.31) | collective-permute-done | bytes 131104 | tf_op jit(solution)/shard_map/ppermute | solution.py:334
  71.8 1.0 %collective-permute-done.33.refs_8_ = f32[64,512]{1,0:T(8,128)S(1)} collective-permute-done((f32[64,512]{1,0:T(8,128)S(1)}, f32[64,512]{1,0:T(8,128)S(1)}, u32[]{:S(2)}, u32[]{:S(2)}) %collective-permute-start.33) | collective-permute-done | bytes 131104 | tf_op jit(solution)/shard_map/ppermute | solution.py:334
  72.9 2.5 %collective-permute-start.36 = (f32[72,512]{1,0:T(8,128)S(1)}, f32[72,512]{1,0:T(8,128)S(1)}, u32[]{:S(2)}, u32[]{:S(2)}) collective-permute-start(f32[72,512]{1,0:T(8,128)S(1)} %shard_map.121.refs_4_.refs_0_), channel_id=1, source_target_pairs={{0,3},{1,2},{2,1},{3,0},{4,7},{5,6},{6,5},{7,4},{8,11},{9,10},{10,... | collective-permute-start | bytes 442376 | tf_op jit(solution)/shard_map/ppermute | solution.py:334
  76.5 2.3 %collective-permute-start.37 = (f32[72,512]{1,0:T(8,128)S(1)}, f32[72,512]{1,0:T(8,128)S(1)}, u32[]{:S(2)}, u32[]{:S(2)}) collective-permute-start(f32[72,512]{1,0:T(8,128)S(1)} %shard_map.121.refs_4_.refs_0_), channel_id=1, source_target_pairs={{0,4},{4,0},{1,5},{5,1},{2,6},{6,2},{3,7},{7,3},{8,12},{12,8},{9,1... | collective-permute-start | bytes 442376 | tf_op jit(solution)/shard_map/ppermute | solution.py:337
  79.0 2.6 %collective-permute-start.39 = (f32[72,512]{1,0:T(8,128)S(1)}, f32[72,512]{1,0:T(8,128)S(1)}, u32[]{:S(2)}, u32[]{:S(2)}) collective-permute-start(f32[72,512]{1,0:T(8,128)S(1)} %collective-permute-done.36.refs_7_.refs_3_), channel_id=1, source_target_pairs={{0,4},{4,0},{1,5},{5,1},{2,6},{6,2},{3,7},{7,3},{8,12},{12,8},{9,1... | collective-permute-start | bytes 442376 | tf_op jit(solution)/shard_map/ppermute | solution.py:337
  81.6 1.3 %collective-permute-done.35.refs_6_.refs_2_ = f32[72,512]{1,0:T(8,128)S(1)} collective-permute-done((f32[72,512]{1,0:T(8,128)S(1)}, f32[72,512]{1,0:T(8,128)S(1)}, u32[]{:S(2)}, u32[]{:S(2)}) %collective-permute-start.35) | collective-permute-done | bytes 147488 | tf_op jit(solution)/shard_map/ppermute | solution.py:334
  85.1 1.1 %shard_map.123 = (bf16[512,512]{1,0:T(8,128)(2,1)}, f32[4]{0:T(128)}) custom-call(f32[72,512]{1,0:T(8,128)S(1)} %shard_map.121.refs_4_.refs_0_, f32[72,512]{1,0:T(8,128)S(1)} %collective-permute-done.34.refs_5_.refs_1_, f32[72,512]{1,0:T(8,128)S(1)} %collective-permute-done.35.refs_6_.refs_2_, f32[72,512]{1,0:T(8,128)S(1)} %collective-permute-done.36.refs_7_.refs_3_, ...), custom_call_target="tpu_custom_call" | custom-call | bytes 1024 | tf_op jit(solution)/shard_map/pallas_call | solution.py:37
  (107 shorter events, 17.2 us)
Async XLA Ops:
  5.4 7.2 %collective-permute-start.2 = (f32[512,512]{1,0:T(8,128)S(1)}, f32[512,512]{1,0:T(8,128)S(1)}, u32[]{:S(2)}, u32[]{:S(2)}) collective-permute-start(f32[512,512]{1,0:T(8,128)S(1)} %get-tuple-element.34.refs_4_), channel_id=1, source_target_pairs={{0,4},{4,0},{1,5},{5,1},{2,6},{6,2},{3,7},{7,3},{8,12},{12,8},{9,1... | collective-permute-start | bytes 3145736 | tf_op jit(solution)/shard_map/ppermute | solution.py:337
  6.1 9.8 %collective-permute-start.4 = (f32[128,512]{1,0:T(8,128)S(1)}, f32[128,512]{1,0:T(8,128)S(1)}, u32[]{:S(2)}, u32[]{:S(2)}) collective-permute-start(f32[128,512]{1,0:T(8,128)S(1)} %get-tuple-element.37.refs_0_.refs_2_), channel_id=1, source_target_pairs={{0,1},{1,0},{2,3},{3,2},{4,5},{5,4},{6,7},{7,6},{8,9},{9,8},{10,11... | collective-permute-start | bytes 786440 | tf_op jit(solution)/shard_map/ppermute | solution.py:334
  9.1 7.4 %collective-permute-start.7 = (f32[128,512]{1,0:T(8,128)S(1)}, f32[128,512]{1,0:T(8,128)S(1)}, u32[]{:S(2)}, u32[]{:S(2)}) collective-permute-start(f32[128,512]{1,0:T(8,128)S(1)} %shard_map.87.refs_2_.refs_3_), channel_id=1, source_target_pairs={{0,8},{28,20},{1,9},{29,21},{2,10},{30,22},{3,11},{31,23}} | collective-permute-start | bytes 786440 | tf_op jit(solution)/shard_map/ppermute | solution.py:397
  12.9 8.3 %collective-permute-start.3 = (f32[128,512]{1,0:T(8,128)S(1)}, f32[128,512]{1,0:T(8,128)S(1)}, u32[]{:S(2)}, u32[]{:S(2)}) collective-permute-start(f32[128,512]{1,0:T(8,128)S(1)} %shard_map.81.refs_1_.refs_2_.refs_3_), channel_id=1, source_target_pairs={{0,8},{28,20},{1,9},{29,21},{2,10},{30,22},{3,11},{31,23}} | collective-permute-start | bytes 786440 | tf_op jit(solution)/shard_map/ppermute | solution.py:397
  14.2 13.2 %collective-permute-start.6 = (f32[128,512]{1,0:T(8,128)S(1)}, f32[128,512]{1,0:T(8,128)S(1)}, u32[]{:S(2)}, u32[]{:S(2)}) collective-permute-start(f32[128,512]{1,0:T(8,128)S(1)} %get-tuple-element.37.refs_0_.refs_2_), channel_id=1, source_target_pairs={{0,3},{1,2},{2,1},{3,0},{4,7},{5,6},{6,5},{7,4},{8,11},{9,10},{10,... | collective-permute-start | bytes 786440 | tf_op jit(solution)/shard_map/ppermute | solution.py:334
  16.5 11.2 %collective-permute-start.8 = (f32[128,512]{1,0:T(8,128)S(1)}, f32[128,512]{1,0:T(8,128)S(1)}, u32[]{:S(2)}, u32[]{:S(2)}) collective-permute-start(f32[128,512]{1,0:T(8,128)S(1)} %shard_map.89), channel_id=1, source_target_pairs={{0,8},{28,20},{8,16},{20,12},{1,9},{29,21},{9,17},{21,13},{2,10},{... | collective-permute-start | bytes 786440 | tf_op jit(solution)/shard_map/ppermute | solution.py:408
  21.2 8.8 %collective-permute-start.5 = (f32[128,512]{1,0:T(8,128)S(1)}, f32[128,512]{1,0:T(8,128)S(1)}, u32[]{:S(2)}, u32[]{:S(2)}) collective-permute-start(f32[128,512]{1,0:T(8,128)S(1)} %shard_map.84.refs_1_.refs_4_), channel_id=1, source_target_pairs={{0,8},{28,20},{8,16},{20,12},{1,9},{29,21},{9,17},{21,13},{2,10},{... | collective-permute-start | bytes 786440 | tf_op jit(solution)/shard_map/ppermute | solution.py:408
  23.7 11.3 %collective-permute-start.1 = (f32[128,512]{1,0:T(8,128)S(1)}, f32[128,512]{1,0:T(8,128)S(1)}, u32[]{:S(2)}, u32[]{:S(2)}) collective-permute-start(f32[128,512]{1,0:T(8,128)S(1)} %get-tuple-element.37.refs_0_.refs_2_), channel_id=1, source_target_pairs={{0,2},{1,3},{2,0},{3,1},{4,6},{5,7},{6,4},{7,5},{8,10},{9,11},{10,... | collective-permute-start | bytes 786440 | tf_op jit(solution)/shard_map/ppermute | solution.py:334
  25.8 9.5 %collective-permute-start.11 = (f32[128,512]{1,0:T(8,128)S(1)}, f32[128,512]{1,0:T(8,128)S(1)}, u32[]{:S(2)}, u32[]{:S(2)}) collective-permute-start(f32[128,512]{1,0:T(8,128)S(1)} %get-tuple-element.41), channel_id=1, source_target_pairs={{0,1},{1,0},{2,3},{3,2},{4,5},{5,4},{6,7},{7,6},{8,9},{9,8},{10,11... | collective-permute-start | bytes 786440 | tf_op jit(solution)/shard_map/ppermute | solution.py:334
  27.8 7.5 %collective-permute-start.10 = (f32[128,512]{1,0:T(8,128)S(1)}, f32[128,512]{1,0:T(8,128)S(1)}, u32[]{:S(2)}, u32[]{:S(2)}) collective-permute-start(f32[128,512]{1,0:T(8,128)S(1)} %shard_map.91.refs_4_), channel_id=1, source_target_pairs={{0,8},{28,20},{8,16},{20,12},{16,24},{12,4},{1,9},{29,21},{9,17},{... | collective-permute-start | bytes 786440 | tf_op jit(solution)/shard_map/ppermute | solution.py:408
  30.1 8.3 %collective-permute-start.13 = (f32[128,512]{1,0:T(8,128)S(1)}, f32[128,512]{1,0:T(8,128)S(1)}, u32[]{:S(2)}, u32[]{:S(2)}) collective-permute-start(f32[128,512]{1,0:T(8,128)S(1)} %shard_map.92.refs_1_.refs_4_), channel_id=1, source_target_pairs={{0,8},{28,20},{8,16},{20,12},{16,24},{12,4},{1,9},{29,21},{9,17},{... | collective-permute-start | bytes 786440 | tf_op jit(solution)/shard_map/ppermute | solution.py:408
  32.0 10.5 %collective-permute-start.14 = (f32[128,512]{1,0:T(8,128)S(1)}, f32[128,512]{1,0:T(8,128)S(1)}, u32[]{:S(2)}, u32[]{:S(2)}) collective-permute-start(f32[128,512]{1,0:T(8,128)S(1)} %get-tuple-element.42), channel_id=1, source_target_pairs={{0,3},{1,2},{2,1},{3,0},{4,7},{5,6},{6,5},{7,4},{8,11},{9,10},{10,... | collective-permute-start | bytes 786440 | tf_op jit(solution)/shard_map/ppermute | solution.py:334
  35.4 7.2 %collective-permute-start.12 = (f32[128,512]{1,0:T(8,128)S(1)}, f32[128,512]{1,0:T(8,128)S(1)}, u32[]{:S(2)}, u32[]{:S(2)}) collective-permute-start(f32[128,512]{1,0:T(8,128)S(1)} %shard_map.96.refs_4_), channel_id=1, source_target_pairs={{0,8},{28,20},{8,16},{20,12},{16,24},{12,4},{1,9},{29,21},{9,17},{... | collective-permute-start | bytes 786440 | tf_op jit(solution)/shard_map/ppermute | solution.py:408
  38.4 6.3 %collective-permute-start.16 = (f32[128,512]{1,0:T(8,128)S(1)}, f32[128,512]{1,0:T(8,128)S(1)}, u32[]{:S(2)}, u32[]{:S(2)}) collective-permute-start(f32[128,512]{1,0:T(8,128)S(1)} %shard_map.98.refs_3_), channel_id=1, source_target_pairs={{0,8},{28,20},{8,16},{20,12},{16,24},{12,4},{1,9},{29,21},{9,17},{... | collective-permute-start | bytes 786440 | tf_op jit(solution)/shard_map/ppermute | solution.py:408
  40.8 6.4 %collective-permute-start.9 = (f32[128,512]{1,0:T(8,128)S(1)}, f32[128,512]{1,0:T(8,128)S(1)}, u32[]{:S(2)}, u32[]{:S(2)}) collective-permute-start(f32[128,512]{1,0:T(8,128)S(1)} %get-tuple-element.39), channel_id=1, source_target_pairs={{0,2},{1,3},{2,0},{3,1},{4,6},{5,7},{6,4},{7,5},{8,10},{9,11},{10,... | collective-permute-start | bytes 786440 | tf_op jit(solution)/shard_map/ppermute | solution.py:334
  42.6 4.7 %collective-permute-start.15 = (f32[128,512]{1,0:T(8,128)S(1)}, f32[128,512]{1,0:T(8,128)S(1)}, u32[]{:S(2)}, u32[]{:S(2)}) collective-permute-start(f32[128,512]{1,0:T(8,128)S(1)} %shard_map.101.refs_3_), channel_id=1, source_target_pairs={{8,16},{20,12},{16,24},{12,4},{9,17},{21,13},{17,25},{13,5},{10,18... | collective-permute-start | bytes 786440 | tf_op jit(solution)/shard_map/ppermute | solution.py:408
  47.3 8.8 %collective-permute-start.18 = (f32[128,512]{1,0:T(8,128)S(1)}, f32[128,512]{1,0:T(8,128)S(1)}, u32[]{:S(2)}, u32[]{:S(2)}) collective-permute-start(f32[128,512]{1,0:T(8,128)S(1)} %shard_map.106.refs_2_), channel_id=1, source_target_pairs={{16,24},{12,4},{17,25},{13,5},{18,26},{14,6},{19,27},{15,7}} | collective-permute-start | bytes 786440 | tf_op jit(solution)/shard_map/ppermute | solution.py:408
  48.0 8.1 %collective-permute-start.22 = (f32[128,512]{1,0:T(8,128)S(1)}, f32[128,512]{1,0:T(8,128)S(1)}, u32[]{:S(2)}, u32[]{:S(2)}) collective-permute-start(f32[128,512]{1,0:T(8,128)S(1)} %shard_map.107.refs_3_.refs_8_.refs_2_), channel_id=1, source_target_pairs={{16,24},{12,4},{17,25},{13,5},{18,26},{14,6},{19,27},{15,7}} | collective-permute-start | bytes 786440 | tf_op jit(solution)/shard_map/ppermute | solution.py:408
  49.3 6.7 %collective-permute-start.21 = (f32[64,512]{1,0:T(8,128)S(1)}, f32[64,512]{1,0:T(8,128)S(1)}, u32[]{:S(2)}, u32[]{:S(2)}) collective-permute-start(f32[64,512]{1,0:T(8,128)S(1)} %get-tuple-element.48), channel_id=1, source_target_pairs={{0,4},{4,0},{1,5},{5,1},{2,6},{6,2},{3,7},{7,3},{8,12},{12,8},{9,1... | collective-permute-start | bytes 393224 | tf_op jit(solution)/shard_map/ppermute | solution.py:337
  55.1 5.1 %collective-permute-start.24 = (f32[128,512]{1,0:T(8,128)S(1)}, f32[128,512]{1,0:T(8,128)S(1)}, u32[]{:S(2)}, u32[]{:S(2)}) collective-permute-start(f32[128,512]{1,0:T(8,128)S(1)} %shard_map.108.refs_3_), channel_id=1, source_target_pairs={{0,4},{4,0},{1,5},{5,1},{2,6},{6,2},{3,7},{7,3},{8,12},{12,8},{9,1... | collective-permute-start | bytes 786440 | tf_op jit(solution)/shard_map/ppermute | solution.py:337
  56.2 5.2 %collective-permute-start.23 = (f32[128,512]{1,0:T(8,128)S(1)}, f32[128,512]{1,0:T(8,128)S(1)}, u32[]{:S(2)}, u32[]{:S(2)}) collective-permute-start(f32[128,512]{1,0:T(8,128)S(1)} %shard_map.113), channel_id=1, source_target_pairs={{0,4},{4,0},{1,5},{5,1},{2,6},{6,2},{3,7},{7,3},{8,12},{12,8},{9,1... | collective-permute-start | bytes 786440 | tf_op jit(solution)/shard_map/ppermute | solution.py:337
  62.4 5.6 %collective-permute-start.29 = (f32[64,512]{1,0:T(8,128)S(1)}, f32[64,512]{1,0:T(8,128)S(1)}, u32[]{:S(2)}, u32[]{:S(2)}) collective-permute-start(f32[64,512]{1,0:T(8,128)S(1)} %get-tuple-element.53), channel_id=1, source_target_pairs={{0,4},{4,0},{1,5},{5,1},{2,6},{6,2},{3,7},{7,3},{8,12},{12,8},{9,1... | collective-permute-start | bytes 393224 | tf_op jit(solution)/shard_map/ppermute | solution.py:337
  62.6 6.4 %collective-permute-start.28 = (f32[64,512]{1,0:T(8,128)S(1)}, f32[64,512]{1,0:T(8,128)S(1)}, u32[]{:S(2)}, u32[]{:S(2)}) collective-permute-start(f32[64,512]{1,0:T(8,128)S(1)} %shard_map.111.refs_6_), channel_id=1, source_target_pairs={{0,1},{1,0},{2,3},{3,2},{4,5},{5,4},{6,7},{7,6},{8,9},{9,8},{10,11... | collective-permute-start | bytes 393224 | tf_op jit(solution)/shard_map/ppermute | solution.py:334
  64.1 7.2 %collective-permute-start.31 = (f32[64,512]{1,0:T(8,128)S(1)}, f32[64,512]{1,0:T(8,128)S(1)}, u32[]{:S(2)}, u32[]{:S(2)}) collective-permute-start(f32[64,512]{1,0:T(8,128)S(1)} %shard_map.118), channel_id=1, source_target_pairs={{0,3},{1,2},{2,1},{3,0},{4,7},{5,6},{6,5},{7,4},{8,11},{9,10},{10,... | collective-permute-start | bytes 393224 | tf_op jit(solution)/shard_map/ppermute | solution.py:334
  64.7 8.1 %collective-permute-start.33 = (f32[64,512]{1,0:T(8,128)S(1)}, f32[64,512]{1,0:T(8,128)S(1)}, u32[]{:S(2)}, u32[]{:S(2)}) collective-permute-start(f32[64,512]{1,0:T(8,128)S(1)} %shard_map.119), channel_id=1, source_target_pairs={{0,2},{1,3},{2,0},{3,1},{4,6},{5,7},{6,4},{7,5},{8,10},{9,11},{10,... | collective-permute-start | bytes 393224 | tf_op jit(solution)/shard_map/ppermute | solution.py:334
  67.4 3.8 %collective-permute-start.27 = (f32[8,128]{1,0:T(8,128)S(1)}, f32[8,128]{1,0:T(8,128)S(1)}, u32[]{:S(2)}, u32[]{:S(2)}) collective-permute-start(f32[8,128]{1,0:T(8,128)S(1)} %shard_map.116.refs_2_), channel_id=1, source_target_pairs={{4,28},{12,20},{20,12},{28,4},{5,29},{13,21},{21,13},{29,5},{6,30}... | collective-permute-start | bytes 12296 | tf_op jit(solution)/shard_map/ppermute | solution.py:476
  68.1 3.7 %collective-permute-start.26 = (f32[8,128]{1,0:T(8,128)S(1)}, f32[8,128]{1,0:T(8,128)S(1)}, u32[]{:S(2)}, u32[]{:S(2)}) collective-permute-start(f32[8,128]{1,0:T(8,128)S(1)} %shard_map.116.refs_2_), channel_id=1, source_target_pairs={{0,8},{4,20},{8,0},{12,28},{16,24},{20,4},{24,16},{28,12},{1,9},{5... | collective-permute-start | bytes 12296 | tf_op jit(solution)/shard_map/ppermute | solution.py:474
  72.9 6.1 %collective-permute-start.36 = (f32[72,512]{1,0:T(8,128)S(1)}, f32[72,512]{1,0:T(8,128)S(1)}, u32[]{:S(2)}, u32[]{:S(2)}) collective-permute-start(f32[72,512]{1,0:T(8,128)S(1)} %shard_map.121.refs_4_.refs_0_), channel_id=1, source_target_pairs={{0,3},{1,2},{2,1},{3,0},{4,7},{5,6},{6,5},{7,4},{8,11},{9,10},{10,... | collective-permute-start | bytes 442376 | tf_op jit(solution)/shard_map/ppermute | solution.py:334
  75.4 7.6 %collective-permute-start.35 = (f32[72,512]{1,0:T(8,128)S(1)}, f32[72,512]{1,0:T(8,128)S(1)}, u32[]{:S(2)}, u32[]{:S(2)}) collective-permute-start(f32[72,512]{1,0:T(8,128)S(1)} %shard_map.121.refs_4_.refs_0_), channel_id=1, source_target_pairs={{0,2},{1,3},{2,0},{3,1},{4,6},{5,7},{6,4},{7,5},{8,10},{9,11},{10,... | collective-permute-start | bytes 442376 | tf_op jit(solution)/shard_map/ppermute | solution.py:334
  75.9 7.7 %collective-permute-start.34 = (f32[72,512]{1,0:T(8,128)S(1)}, f32[72,512]{1,0:T(8,128)S(1)}, u32[]{:S(2)}, u32[]{:S(2)}) collective-permute-start(f32[72,512]{1,0:T(8,128)S(1)} %shard_map.121.refs_4_.refs_0_), channel_id=1, source_target_pairs={{0,1},{1,0},{2,3},{3,2},{4,5},{5,4},{6,7},{7,6},{8,9},{9,8},{10,11... | collective-permute-start | bytes 442376 | tf_op jit(solution)/shard_map/ppermute | solution.py:334
  76.5 7.5 %collective-permute-start.37 = (f32[72,512]{1,0:T(8,128)S(1)}, f32[72,512]{1,0:T(8,128)S(1)}, u32[]{:S(2)}, u32[]{:S(2)}) collective-permute-start(f32[72,512]{1,0:T(8,128)S(1)} %shard_map.121.refs_4_.refs_0_), channel_id=1, source_target_pairs={{0,4},{4,0},{1,5},{5,1},{2,6},{6,2},{3,7},{7,3},{8,12},{12,8},{9,1... | collective-permute-start | bytes 442376 | tf_op jit(solution)/shard_map/ppermute | solution.py:337
  79.0 5.0 %collective-permute-start.39 = (f32[72,512]{1,0:T(8,128)S(1)}, f32[72,512]{1,0:T(8,128)S(1)}, u32[]{:S(2)}, u32[]{:S(2)}) collective-permute-start(f32[72,512]{1,0:T(8,128)S(1)} %collective-permute-done.36.refs_7_.refs_3_), channel_id=1, source_target_pairs={{0,4},{4,0},{1,5},{5,1},{2,6},{6,2},{3,7},{7,3},{8,12},{12,8},{9,1... | collective-permute-start | bytes 442376 | tf_op jit(solution)/shard_map/ppermute | solution.py:337
  (14 other events, 56.5 us)

commit v10 on v9

--- a/solution.py
+++ b/solution.py
@@ -383,6 +383,16 @@
         shape = [f32(rows, width * len(dicts))]
         return call(project_kernel, shape, (acts[q], table, *dicts))[0]
 
+    def prepare(step, after):
+        if step + 1 >= n_tok:
+            return []
+        q = order[step + 1]
+        acts[q] = call(round_kernel, [bf16(rows, lats)], (gathered[q],), after=after)[0]
+        new = [project(q, (dict_ref,)) for dict_ref in (dict_here, dict_other)]
+        for side, piece in enumerate(new):
+            sums[side].append((piece, 0))
+        return new
+
     for step in range(steps + 1):
         at = [p for p in range(n_lat - 1) if 0 <= step - p < n_tok]
         pairs = []
@@ -403,15 +413,14 @@
                     functools.partial(message_kernel, at, [col for _, col in items]),
                     [f32(rows, width)],
                     [array for array, _ in items],
-                    after=sent + (waits[step] if side == 0 else []) if step > 1 else (),
+                    after=sent + (waits[step] if side == 0 else []) if step > 1 or side else (),
                 )[0]
                 got[side].append((lax.ppermute(message, ("lat", "wid"), pairs), 0))
                 sent = [message]
-        if step + 1 < n_tok:
-            q = order[step + 1]
-            acts[q] = call(round_kernel, [bf16(rows, lats)], (gathered[q],), after=sent)[0]
-            for side, dict_ref in enumerate((dict_here, dict_other)):
-                sums[side].append((project(q, (dict_ref,)), 0))
+                if side == 0:
+                    sent += prepare(step, sent)
+        if step == 0:
+            prepare(step, sent)
         ready = []
         c = step - (n_lat - 1)
         if c >= 0:

time: 86.6 us -> 89.7 us (1.036)
  waiting for transfers between devices: 12.1 us -> 13.8 us
  starting transfers between devices: 61.4 us -> 62.8 us
    ppermute x12, starting transfers between devices: 23.4 us -> 27.8 us  [body(): got[side].append((lax.ppermute(message, ('lat', 'wid'), pairs), 0))]
    ppermute x12, starting transfers between devices: 19.5 us -> 15.6 us  [across(): return lax.ppermute(array, 'tok', [(t, t ^ q) for t in range(n_tok)])]
    ppermute x12, waiting for transfers between devices: 5.87 us -> 7.01 us  [across(): return lax.ppermute(array, 'tok', [(t, t ^ q) for t in range(n_tok)])]
    ppermute x15, starting transfers between devices: 17.8 us -> 18.7 us  [swap(): return lax.ppermute(array, 'wid', [(w, w ^ 1) for w in range(n_wid)])]
  transfers between devices with their start and end apart: 41 -> 41, of which waited for: 14 -> 10; matrix products, arithmetic and copies ran while one was open for 0% -> 0% of each run, Pallas kernels for 8% -> 8%
where the time goes in v10:
time: 89.7 us; the launch traced here: 89.3 us
  starting transfers between devices  62.8 us (70%)
  waiting for transfers between devices  13.8 us (15%)
  Pallas kernels  11.4 us (13%)
  between operations  1.26 us (1%)
    ppermute x12, starting transfers between devices, body(): got[side].append((lax.ppermute(message, ('lat', 'wid'), pairs), 0))  27.8 us
    ppermute x15, starting transfers between devices, swap(): return lax.ppermute(array, 'wid', [(w, w ^ 1) for w in range(n_wid)])  18.7 us
    ppermute x12, starting transfers between devices, across(): return lax.ppermute(array, 'tok', [(t, t ^ q) for t in range(n_tok)])  15.6 us
    pallas_call x47, Pallas kernels, call(): pl.pallas_call(run, out_shape=outs, in_specs=list(specs or [VMEM] * len(a...  11.4 us
    ppermute x12, waiting for transfers between devices, across(): return lax.ppermute(array, 'tok', [(t, t ^ q) for t in range(n_tok)])  7.01 us
    ppermute x15, waiting for transfers between devices, swap(): return lax.ppermute(array, 'wid', [(w, w ^ 1) for w in range(n_wid)])  4.37 us
    ppermute x12, waiting for transfers between devices, body(): got[side].append((lax.ppermute(message, ('lat', 'wid'), pairs), 0))  2.4 us
  transfers between devices with their start and end apart: 41, of which 10 were waited for; matrix products, arithmetic and copies ran while one was open for 0% of the time, Pallas kernels for 8%

profile of v10, /device:TPU:0, one launch (start us, length us, event | category | flops | bytes accessed | tf_op | source)
XLA Modules:
  0.0 89.3 jit_solution(13382014719985508078)
XLA Ops:
  0.7 2.9 %shard_map.77 = (f32[128,512]{1,0:T(8,128)S(1)}, bf16[512,512]{1,0:T(8,128)(2,1)S(1)}) custom-call(bf16[128,2048]{1,0:T(8,128)(2,1)} %refs_0_.3, bf16[512,2048]{1,0:T(8,128)(2,1)} %refs_1_.1), custom_call_target="tpu_custom_call" | custom-call | bytes 1024 | tf_op jit(solution)/shard_map/pallas_call | solution.py:37
  4.1 1.2 %collective-permute-done.refs_2_.refs_1_ = f32[128,512]{1,0:T(8,128)S(1)} collective-permute-done((f32[128,512]{1,0:T(8,128)S(1)}, f32[128,512]{1,0:T(8,128)S(1)}, u32[]{:S(2)}, u32[]{:S(2)}) %collective-permute-start) | collective-permute-done | bytes 262176 | tf_op jit(solution)/shard_map/ppermute | solution.py:337
  6.1 2.7 %collective-permute-start.3 = (f32[128,512]{1,0:T(8,128)S(1)}, f32[128,512]{1,0:T(8,128)S(1)}, u32[]{:S(2)}, u32[]{:S(2)}) collective-permute-start(f32[128,512]{1,0:T(8,128)S(1)} %get-tuple-element.37.refs_0_.refs_2_), channel_id=1, source_target_pairs={{0,1},{1,0},{2,3},{3,2},{4,5},{5,4},{6,7},{7,6},{8,9},{9,8},{10,11... | collective-permute-start | bytes 786440 | tf_op jit(solution)/shard_map/ppermute | solution.py:334
  9.1 3.5 %collective-permute-start.2 = (f32[128,512]{1,0:T(8,128)S(1)}, f32[128,512]{1,0:T(8,128)S(1)}, u32[]{:S(2)}, u32[]{:S(2)}) collective-permute-start(f32[128,512]{1,0:T(8,128)S(1)} %shard_map.81.refs_2_.refs_3_), channel_id=1, source_target_pairs={{0,8},{28,20},{1,9},{29,21},{2,10},{30,22},{3,11},{31,23}} | collective-permute-start | bytes 786440 | tf_op jit(solution)/shard_map/ppermute | solution.py:407
  12.6 1.6 %collective-permute-start.6 = (f32[128,512]{1,0:T(8,128)S(1)}, f32[128,512]{1,0:T(8,128)S(1)}, u32[]{:S(2)}, u32[]{:S(2)}) collective-permute-start(f32[128,512]{1,0:T(8,128)S(1)} %get-tuple-element.37.refs_0_.refs_2_), channel_id=1, source_target_pairs={{0,3},{1,2},{2,1},{3,0},{4,7},{5,6},{6,5},{7,4},{8,11},{9,10},{10,... | collective-permute-start | bytes 786440 | tf_op jit(solution)/shard_map/ppermute | solution.py:334
  14.4 1.3 %collective-permute-start.7 = (f32[128,512]{1,0:T(8,128)S(1)}, f32[128,512]{1,0:T(8,128)S(1)}, u32[]{:S(2)}, u32[]{:S(2)}) collective-permute-start(f32[128,512]{1,0:T(8,128)S(1)} %shard_map.82.refs_1_.refs_2_.refs_3_), channel_id=1, source_target_pairs={{0,8},{28,20},{1,9},{29,21},{2,10},{30,22},{3,11},{31,23}} | collective-permute-start | bytes 786440 | tf_op jit(solution)/shard_map/ppermute | solution.py:407
  16.7 4.2 %collective-permute-start.5 = (f32[128,512]{1,0:T(8,128)S(1)}, f32[128,512]{1,0:T(8,128)S(1)}, u32[]{:S(2)}, u32[]{:S(2)}) collective-permute-start(f32[128,512]{1,0:T(8,128)S(1)} %shard_map.85.refs_1_.refs_3_), channel_id=1, source_target_pairs={{0,8},{28,20},{8,16},{20,12},{1,9},{29,21},{9,17},{21,13},{2,10},{... | collective-permute-start | bytes 786440 | tf_op jit(solution)/shard_map/ppermute | solution.py:418
  20.9 1.7 %collective-permute-done.6.refs_0_ = f32[128,512]{1,0:T(8,128)S(1)} collective-permute-done((f32[128,512]{1,0:T(8,128)S(1)}, f32[128,512]{1,0:T(8,128)S(1)}, u32[]{:S(2)}, u32[]{:S(2)}) %collective-permute-start.6) | collective-permute-done | bytes 262176 | tf_op jit(solution)/shard_map/ppermute | solution.py:334
  23.5 3.5 %collective-permute-start.10 = (f32[128,512]{1,0:T(8,128)S(1)}, f32[128,512]{1,0:T(8,128)S(1)}, u32[]{:S(2)}, u32[]{:S(2)}) collective-permute-start(f32[128,512]{1,0:T(8,128)S(1)} %shard_map.90.refs_4_), channel_id=1, source_target_pairs={{0,8},{28,20},{8,16},{20,12},{1,9},{29,21},{9,17},{21,13},{2,10},{... | collective-permute-start | bytes 786440 | tf_op jit(solution)/shard_map/ppermute | solution.py:418
  27.2 1.6 %collective-permute-start.11 = (f32[128,512]{1,0:T(8,128)S(1)}, f32[128,512]{1,0:T(8,128)S(1)}, u32[]{:S(2)}, u32[]{:S(2)}) collective-permute-start(f32[128,512]{1,0:T(8,128)S(1)} %get-tuple-element.41), channel_id=1, source_target_pairs={{0,1},{1,0},{2,3},{3,2},{4,5},{5,4},{6,7},{7,6},{8,9},{9,8},{10,11... | collective-permute-start | bytes 786440 | tf_op jit(solution)/shard_map/ppermute | solution.py:334
  28.8 3.5 %collective-permute-start.9 = (f32[128,512]{1,0:T(8,128)S(1)}, f32[128,512]{1,0:T(8,128)S(1)}, u32[]{:S(2)}, u32[]{:S(2)}) collective-permute-start(f32[128,512]{1,0:T(8,128)S(1)} %shard_map.91.refs_1_.refs_4_), channel_id=1, source_target_pairs={{0,8},{28,20},{8,16},{20,12},{16,24},{12,4},{1,9},{29,21},{9,17},{... | collective-permute-start | bytes 786440 | tf_op jit(solution)/shard_map/ppermute | solution.py:418
  32.9 2.4 %collective-permute-start.13 = (f32[128,512]{1,0:T(8,128)S(1)}, f32[128,512]{1,0:T(8,128)S(1)}, u32[]{:S(2)}, u32[]{:S(2)}) collective-permute-start(f32[128,512]{1,0:T(8,128)S(1)} %shard_map.96.refs_4_), channel_id=1, source_target_pairs={{0,8},{28,20},{8,16},{20,12},{16,24},{12,4},{1,9},{29,21},{9,17},{... | collective-permute-start | bytes 786440 | tf_op jit(solution)/shard_map/ppermute | solution.py:418
  35.4 1.5 %collective-permute-start.14 = (f32[128,512]{1,0:T(8,128)S(1)}, f32[128,512]{1,0:T(8,128)S(1)}, u32[]{:S(2)}, u32[]{:S(2)}) collective-permute-start(f32[128,512]{1,0:T(8,128)S(1)} %get-tuple-element.42), channel_id=1, source_target_pairs={{0,3},{1,2},{2,1},{3,0},{4,7},{5,6},{6,5},{7,4},{8,11},{9,10},{10,... | collective-permute-start | bytes 786440 | tf_op jit(solution)/shard_map/ppermute | solution.py:334
  36.9 3.6 %collective-permute-start.12 = (f32[128,512]{1,0:T(8,128)S(1)}, f32[128,512]{1,0:T(8,128)S(1)}, u32[]{:S(2)}, u32[]{:S(2)}) collective-permute-start(f32[128,512]{1,0:T(8,128)S(1)} %shard_map.97.refs_4_), channel_id=1, source_target_pairs={{0,8},{28,20},{8,16},{20,12},{16,24},{12,4},{1,9},{29,21},{9,17},{... | collective-permute-start | bytes 786440 | tf_op jit(solution)/shard_map/ppermute | solution.py:418
  40.6 3.1 %collective-permute-start.16 = (f32[128,512]{1,0:T(8,128)S(1)}, f32[128,512]{1,0:T(8,128)S(1)}, u32[]{:S(2)}, u32[]{:S(2)}) collective-permute-start(f32[128,512]{1,0:T(8,128)S(1)} %shard_map.98.refs_3_), channel_id=1, source_target_pairs={{0,8},{28,20},{8,16},{20,12},{16,24},{12,4},{1,9},{29,21},{9,17},{... | collective-permute-start | bytes 786440 | tf_op jit(solution)/shard_map/ppermute | solution.py:418
  45.2 2.4 %collective-permute-done.16.refs_0_.refs_2_.refs_1_ = f32[128,512]{1,0:T(8,128)S(1)} collective-permute-done((f32[128,512]{1,0:T(8,128)S(1)}, f32[128,512]{1,0:T(8,128)S(1)}, u32[]{:S(2)}, u32[]{:S(2)}) %collective-permute-start.16) | collective-permute-done | bytes 262176 | tf_op jit(solution)/shard_map/ppermute | solution.py:418
  49.0 1.1 %collective-permute-done.8.refs_3_.refs_2_ = f32[128,512]{1,0:T(8,128)S(1)} collective-permute-done((f32[128,512]{1,0:T(8,128)S(1)}, f32[128,512]{1,0:T(8,128)S(1)}, u32[]{:S(2)}, u32[]{:S(2)}) %collective-permute-start.8) | collective-permute-done | bytes 262176 | tf_op jit(solution)/shard_map/ppermute | solution.py:334
  52.2 4.7 %collective-permute-start.21 = (f32[64,512]{1,0:T(8,128)S(1)}, f32[64,512]{1,0:T(8,128)S(1)}, u32[]{:S(2)}, u32[]{:S(2)}) collective-permute-start(f32[64,512]{1,0:T(8,128)S(1)} %get-tuple-element.48), channel_id=1, source_target_pairs={{0,4},{4,0},{1,5},{5,1},{2,6},{6,2},{3,7},{7,3},{8,12},{12,8},{9,1... | collective-permute-start | bytes 393224 | tf_op jit(solution)/shard_map/ppermute | solution.py:337
  57.0 0.8 collective-permute-done.21.refs_1_
  58.0 4.5 %collective-permute-start.23 = (f32[128,512]{1,0:T(8,128)S(1)}, f32[128,512]{1,0:T(8,128)S(1)}, u32[]{:S(2)}, u32[]{:S(2)}) collective-permute-start(f32[128,512]{1,0:T(8,128)S(1)} %shard_map.113), channel_id=1, source_target_pairs={{0,4},{4,0},{1,5},{5,1},{2,6},{6,2},{3,7},{7,3},{8,12},{12,8},{9,1... | collective-permute-start | bytes 786440 | tf_op jit(solution)/shard_map/ppermute | solution.py:337
  64.9 1.5 %collective-permute-start.28 = (f32[64,512]{1,0:T(8,128)S(1)}, f32[64,512]{1,0:T(8,128)S(1)}, u32[]{:S(2)}, u32[]{:S(2)}) collective-permute-start(f32[64,512]{1,0:T(8,128)S(1)} %shard_map.111.refs_6_), channel_id=1, source_target_pairs={{0,1},{1,0},{2,3},{3,2},{4,5},{5,4},{6,7},{7,6},{8,9},{9,8},{10,11... | collective-permute-start | bytes 393224 | tf_op jit(solution)/shard_map/ppermute | solution.py:334
  66.5 1.1 %collective-permute-start.31 = (f32[64,512]{1,0:T(8,128)S(1)}, f32[64,512]{1,0:T(8,128)S(1)}, u32[]{:S(2)}, u32[]{:S(2)}) collective-permute-start(f32[64,512]{1,0:T(8,128)S(1)} %shard_map.118), channel_id=1, source_target_pairs={{0,3},{1,2},{2,1},{3,0},{4,7},{5,6},{6,5},{7,4},{8,11},{9,10},{10,... | collective-permute-start | bytes 393224 | tf_op jit(solution)/shard_map/ppermute | solution.py:334
  67.6 1.1 %collective-permute-start.33 = (f32[64,512]{1,0:T(8,128)S(1)}, f32[64,512]{1,0:T(8,128)S(1)}, u32[]{:S(2)}, u32[]{:S(2)}) collective-permute-start(f32[64,512]{1,0:T(8,128)S(1)} %shard_map.119), channel_id=1, source_target_pairs={{0,2},{1,3},{2,0},{3,1},{4,6},{5,7},{6,4},{7,5},{8,10},{9,11},{10,... | collective-permute-start | bytes 393224 | tf_op jit(solution)/shard_map/ppermute | solution.py:334
  68.6 1.2 %collective-permute-done.25.refs_1_ = f32[8,128]{1,0:T(8,128)S(1)} collective-permute-done((f32[8,128]{1,0:T(8,128)S(1)}, f32[8,128]{1,0:T(8,128)S(1)}, u32[]{:S(2)}, u32[]{:S(2)}) %collective-permute-start.25) | collective-permute-done | bytes 4128 | tf_op jit(solution)/shard_map/ppermute | solution.py:337
  71.3 2.8 %collective-permute-done.31.refs_7_ = f32[64,512]{1,0:T(8,128)S(1)} collective-permute-done((f32[64,512]{1,0:T(8,128)S(1)}, f32[64,512]{1,0:T(8,128)S(1)}, u32[]{:S(2)}, u32[]{:S(2)}) %collective-permute-start.31) | collective-permute-done | bytes 131104 | tf_op jit(solution)/shard_map/ppermute | solution.py:334
  74.1 1.5 %collective-permute-done.33.refs_8_ = f32[64,512]{1,0:T(8,128)S(1)} collective-permute-done((f32[64,512]{1,0:T(8,128)S(1)}, f32[64,512]{1,0:T(8,128)S(1)}, u32[]{:S(2)}, u32[]{:S(2)}) %collective-permute-start.33) | collective-permute-done | bytes 131104 | tf_op jit(solution)/shard_map/ppermute | solution.py:334
  75.8 2.0 %collective-permute-start.36 = (f32[72,512]{1,0:T(8,128)S(1)}, f32[72,512]{1,0:T(8,128)S(1)}, u32[]{:S(2)}, u32[]{:S(2)}) collective-permute-start(f32[72,512]{1,0:T(8,128)S(1)} %shard_map.121.refs_4_.refs_0_), channel_id=1, source_target_pairs={{0,3},{1,2},{2,1},{3,0},{4,7},{5,6},{6,5},{7,4},{8,11},{9,10},{10,... | collective-permute-start | bytes 442376 | tf_op jit(solution)/shard_map/ppermute | solution.py:334
  77.7 1.0 %collective-permute-start.35 = (f32[72,512]{1,0:T(8,128)S(1)}, f32[72,512]{1,0:T(8,128)S(1)}, u32[]{:S(2)}, u32[]{:S(2)}) collective-permute-start(f32[72,512]{1,0:T(8,128)S(1)} %shard_map.121.refs_4_.refs_0_), channel_id=1, source_target_pairs={{0,2},{1,3},{2,0},{3,1},{4,6},{5,7},{6,4},{7,5},{8,10},{9,11},{10,... | collective-permute-start | bytes 442376 | tf_op jit(solution)/shard_map/ppermute | solution.py:334
  79.3 3.4 %collective-permute-start.37 = (f32[72,512]{1,0:T(8,128)S(1)}, f32[72,512]{1,0:T(8,128)S(1)}, u32[]{:S(2)}, u32[]{:S(2)}) collective-permute-start(f32[72,512]{1,0:T(8,128)S(1)} %shard_map.121.refs_4_.refs_0_), channel_id=1, source_target_pairs={{0,4},{4,0},{1,5},{5,1},{2,6},{6,2},{3,7},{7,3},{8,12},{12,8},{9,1... | collective-permute-start | bytes 442376 | tf_op jit(solution)/shard_map/ppermute | solution.py:337
  82.7 3.1 %collective-permute-start.39 = (f32[72,512]{1,0:T(8,128)S(1)}, f32[72,512]{1,0:T(8,128)S(1)}, u32[]{:S(2)}, u32[]{:S(2)}) collective-permute-start(f32[72,512]{1,0:T(8,128)S(1)} %collective-permute-done.36.refs_7_.refs_3_), channel_id=1, source_target_pairs={{0,4},{4,0},{1,5},{5,1},{2,6},{6,2},{3,7},{7,3},{8,12},{12,8},{9,1... | collective-permute-start | bytes 442376 | tf_op jit(solution)/shard_map/ppermute | solution.py:337
  85.9 0.8 collective-permute-start.38
  88.2 1.1 %shard_map.123 = (bf16[512,512]{1,0:T(8,128)(2,1)}, f32[4]{0:T(128)}) custom-call(f32[72,512]{1,0:T(8,128)S(1)} %shard_map.121.refs_4_.refs_0_, f32[72,512]{1,0:T(8,128)S(1)} %collective-permute-done.34.refs_5_.refs_1_, f32[72,512]{1,0:T(8,128)S(1)} %collective-permute-done.35.refs_6_.refs_2_, f32[72,512]{1,0:T(8,128)S(1)} %collective-permute-done.36.refs_7_.refs_3_, ...), custom_call_target="tpu_custom_call" | custom-call | bytes 1024 | tf_op jit(solution)/shard_map/pallas_call | solution.py:37
  (107 shorter events, 15.9 us)
Async XLA Ops:
  5.4 8.8 %collective-permute-start.4 = (f32[512,512]{1,0:T(8,128)S(1)}, f32[512,512]{1,0:T(8,128)S(1)}, u32[]{:S(2)}, u32[]{:S(2)}) collective-permute-start(f32[512,512]{1,0:T(8,128)S(1)} %get-tuple-element.34.refs_4_), channel_id=1, source_target_pairs={{0,4},{4,0},{1,5},{5,1},{2,6},{6,2},{3,7},{7,3},{8,12},{12,8},{9,1... | collective-permute-start | bytes 3145736 | tf_op jit(solution)/shard_map/ppermute | solution.py:337
  6.1 10.2 %collective-permute-start.3 = (f32[128,512]{1,0:T(8,128)S(1)}, f32[128,512]{1,0:T(8,128)S(1)}, u32[]{:S(2)}, u32[]{:S(2)}) collective-permute-start(f32[128,512]{1,0:T(8,128)S(1)} %get-tuple-element.37.refs_0_.refs_2_), channel_id=1, source_target_pairs={{0,1},{1,0},{2,3},{3,2},{4,5},{5,4},{6,7},{7,6},{8,9},{9,8},{10,11... | collective-permute-start | bytes 786440 | tf_op jit(solution)/shard_map/ppermute | solution.py:334
  9.1 7.6 %collective-permute-start.2 = (f32[128,512]{1,0:T(8,128)S(1)}, f32[128,512]{1,0:T(8,128)S(1)}, u32[]{:S(2)}, u32[]{:S(2)}) collective-permute-start(f32[128,512]{1,0:T(8,128)S(1)} %shard_map.81.refs_2_.refs_3_), channel_id=1, source_target_pairs={{0,8},{28,20},{1,9},{29,21},{2,10},{30,22},{3,11},{31,23}} | collective-permute-start | bytes 786440 | tf_op jit(solution)/shard_map/ppermute | solution.py:407
  12.6 10.0 %collective-permute-start.6 = (f32[128,512]{1,0:T(8,128)S(1)}, f32[128,512]{1,0:T(8,128)S(1)}, u32[]{:S(2)}, u32[]{:S(2)}) collective-permute-start(f32[128,512]{1,0:T(8,128)S(1)} %get-tuple-element.37.refs_0_.refs_2_), channel_id=1, source_target_pairs={{0,3},{1,2},{2,1},{3,0},{4,7},{5,6},{6,5},{7,4},{8,11},{9,10},{10,... | collective-permute-start | bytes 786440 | tf_op jit(solution)/shard_map/ppermute | solution.py:334
  14.4 9.0 %collective-permute-start.7 = (f32[128,512]{1,0:T(8,128)S(1)}, f32[128,512]{1,0:T(8,128)S(1)}, u32[]{:S(2)}, u32[]{:S(2)}) collective-permute-start(f32[128,512]{1,0:T(8,128)S(1)} %shard_map.82.refs_1_.refs_2_.refs_3_), channel_id=1, source_target_pairs={{0,8},{28,20},{1,9},{29,21},{2,10},{30,22},{3,11},{31,23}} | collective-permute-start | bytes 786440 | tf_op jit(solution)/shard_map/ppermute | solution.py:407
  15.8 16.5 %collective-permute-start.1 = (f32[128,512]{1,0:T(8,128)S(1)}, f32[128,512]{1,0:T(8,128)S(1)}, u32[]{:S(2)}, u32[]{:S(2)}) collective-permute-start(f32[128,512]{1,0:T(8,128)S(1)} %get-tuple-element.37.refs_0_.refs_2_), channel_id=1, source_target_pairs={{0,2},{1,3},{2,0},{3,1},{4,6},{5,7},{6,4},{7,5},{8,10},{9,11},{10,... | collective-permute-start | bytes 786440 | tf_op jit(solution)/shard_map/ppermute | solution.py:334
  16.7 12.0 %collective-permute-start.5 = (f32[128,512]{1,0:T(8,128)S(1)}, f32[128,512]{1,0:T(8,128)S(1)}, u32[]{:S(2)}, u32[]{:S(2)}) collective-permute-start(f32[128,512]{1,0:T(8,128)S(1)} %shard_map.85.refs_1_.refs_3_), channel_id=1, source_target_pairs={{0,8},{28,20},{8,16},{20,12},{1,9},{29,21},{9,17},{21,13},{2,10},{... | collective-permute-start | bytes 786440 | tf_op jit(solution)/shard_map/ppermute | solution.py:418
  23.5 9.3 %collective-permute-start.10 = (f32[128,512]{1,0:T(8,128)S(1)}, f32[128,512]{1,0:T(8,128)S(1)}, u32[]{:S(2)}, u32[]{:S(2)}) collective-permute-start(f32[128,512]{1,0:T(8,128)S(1)} %shard_map.90.refs_4_), channel_id=1, source_target_pairs={{0,8},{28,20},{8,16},{20,12},{1,9},{29,21},{9,17},{21,13},{2,10},{... | collective-permute-start | bytes 786440 | tf_op jit(solution)/shard_map/ppermute | solution.py:418
  27.2 9.7 %collective-permute-start.11 = (f32[128,512]{1,0:T(8,128)S(1)}, f32[128,512]{1,0:T(8,128)S(1)}, u32[]{:S(2)}, u32[]{:S(2)}) collective-permute-start(f32[128,512]{1,0:T(8,128)S(1)} %get-tuple-element.41), channel_id=1, source_target_pairs={{0,1},{1,0},{2,3},{3,2},{4,5},{5,4},{6,7},{7,6},{8,9},{9,8},{10,11... | collective-permute-start | bytes 786440 | tf_op jit(solution)/shard_map/ppermute | solution.py:334
  28.8 8.1 %collective-permute-start.9 = (f32[128,512]{1,0:T(8,128)S(1)}, f32[128,512]{1,0:T(8,128)S(1)}, u32[]{:S(2)}, u32[]{:S(2)}) collective-permute-start(f32[128,512]{1,0:T(8,128)S(1)} %shard_map.91.refs_1_.refs_4_), channel_id=1, source_target_pairs={{0,8},{28,20},{8,16},{20,12},{16,24},{12,4},{1,9},{29,21},{9,17},{... | collective-permute-start | bytes 786440 | tf_op jit(solution)/shard_map/ppermute | solution.py:418
  32.9 7.6 %collective-permute-start.13 = (f32[128,512]{1,0:T(8,128)S(1)}, f32[128,512]{1,0:T(8,128)S(1)}, u32[]{:S(2)}, u32[]{:S(2)}) collective-permute-start(f32[128,512]{1,0:T(8,128)S(1)} %shard_map.96.refs_4_), channel_id=1, source_target_pairs={{0,8},{28,20},{8,16},{20,12},{16,24},{12,4},{1,9},{29,21},{9,17},{... | collective-permute-start | bytes 786440 | tf_op jit(solution)/shard_map/ppermute | solution.py:418
  35.4 9.1 %collective-permute-start.14 = (f32[128,512]{1,0:T(8,128)S(1)}, f32[128,512]{1,0:T(8,128)S(1)}, u32[]{:S(2)}, u32[]{:S(2)}) collective-permute-start(f32[128,512]{1,0:T(8,128)S(1)} %get-tuple-element.42), channel_id=1, source_target_pairs={{0,3},{1,2},{2,1},{3,0},{4,7},{5,6},{6,5},{7,4},{8,11},{9,10},{10,... | collective-permute-start | bytes 786440 | tf_op jit(solution)/shard_map/ppermute | solution.py:334
  36.9 7.5 %collective-permute-start.12 = (f32[128,512]{1,0:T(8,128)S(1)}, f32[128,512]{1,0:T(8,128)S(1)}, u32[]{:S(2)}, u32[]{:S(2)}) collective-permute-start(f32[128,512]{1,0:T(8,128)S(1)} %shard_map.97.refs_4_), channel_id=1, source_target_pairs={{0,8},{28,20},{8,16},{20,12},{16,24},{12,4},{1,9},{29,21},{9,17},{... | collective-permute-start | bytes 786440 | tf_op jit(solution)/shard_map/ppermute | solution.py:418
  40.6 6.9 %collective-permute-start.16 = (f32[128,512]{1,0:T(8,128)S(1)}, f32[128,512]{1,0:T(8,128)S(1)}, u32[]{:S(2)}, u32[]{:S(2)}) collective-permute-start(f32[128,512]{1,0:T(8,128)S(1)} %shard_map.98.refs_3_), channel_id=1, source_target_pairs={{0,8},{28,20},{8,16},{20,12},{16,24},{12,4},{1,9},{29,21},{9,17},{... | collective-permute-start | bytes 786440 | tf_op jit(solution)/shard_map/ppermute | solution.py:418
  43.7 6.4 %collective-permute-start.8 = (f32[128,512]{1,0:T(8,128)S(1)}, f32[128,512]{1,0:T(8,128)S(1)}, u32[]{:S(2)}, u32[]{:S(2)}) collective-permute-start(f32[128,512]{1,0:T(8,128)S(1)} %get-tuple-element.39), channel_id=1, source_target_pairs={{0,2},{1,3},{2,0},{3,1},{4,6},{5,7},{6,4},{7,5},{8,10},{9,11},{10,... | collective-permute-start | bytes 786440 | tf_op jit(solution)/shard_map/ppermute | solution.py:334
  44.3 4.1 %collective-permute-start.17 = (f32[128,512]{1,0:T(8,128)S(1)}, f32[128,512]{1,0:T(8,128)S(1)}, u32[]{:S(2)}, u32[]{:S(2)}) collective-permute-start(f32[128,512]{1,0:T(8,128)S(1)} %shard_map.99.refs_5_), channel_id=1, source_target_pairs={{0,4},{4,0},{1,5},{5,1},{2,6},{6,2},{3,7},{7,3},{8,12},{12,8},{9,1... | collective-permute-start | bytes 786440 | tf_op jit(solution)/shard_map/ppermute | solution.py:337
  44.5 5.6 %collective-permute-start.15 = (f32[128,512]{1,0:T(8,128)S(1)}, f32[128,512]{1,0:T(8,128)S(1)}, u32[]{:S(2)}, u32[]{:S(2)}) collective-permute-start(f32[128,512]{1,0:T(8,128)S(1)} %shard_map.101.refs_3_), channel_id=1, source_target_pairs={{8,16},{20,12},{16,24},{12,4},{9,17},{21,13},{17,25},{13,5},{10,18... | collective-permute-start | bytes 786440 | tf_op jit(solution)/shard_map/ppermute | solution.py:418
  50.1 7.8 %collective-permute-start.18 = (f32[128,512]{1,0:T(8,128)S(1)}, f32[128,512]{1,0:T(8,128)S(1)}, u32[]{:S(2)}, u32[]{:S(2)}) collective-permute-start(f32[128,512]{1,0:T(8,128)S(1)} %shard_map.106.refs_2_), channel_id=1, source_target_pairs={{16,24},{12,4},{17,25},{13,5},{18,26},{14,6},{19,27},{15,7}} | collective-permute-start | bytes 786440 | tf_op jit(solution)/shard_map/ppermute | solution.py:418
  50.8 7.1 %collective-permute-start.22 = (f32[128,512]{1,0:T(8,128)S(1)}, f32[128,512]{1,0:T(8,128)S(1)}, u32[]{:S(2)}, u32[]{:S(2)}) collective-permute-start(f32[128,512]{1,0:T(8,128)S(1)} %shard_map.107.refs_3_.refs_8_.refs_2_), channel_id=1, source_target_pairs={{16,24},{12,4},{17,25},{13,5},{18,26},{14,6},{19,27},{15,7}} | collective-permute-start | bytes 786440 | tf_op jit(solution)/shard_map/ppermute | solution.py:418
  52.2 5.7 %collective-permute-start.21 = (f32[64,512]{1,0:T(8,128)S(1)}, f32[64,512]{1,0:T(8,128)S(1)}, u32[]{:S(2)}, u32[]{:S(2)}) collective-permute-start(f32[64,512]{1,0:T(8,128)S(1)} %get-tuple-element.48), channel_id=1, source_target_pairs={{0,4},{4,0},{1,5},{5,1},{2,6},{6,2},{3,7},{7,3},{8,12},{12,8},{9,1... | collective-permute-start | bytes 393224 | tf_op jit(solution)/shard_map/ppermute | solution.py:337
  56.9 5.6 %collective-permute-start.24 = (f32[128,512]{1,0:T(8,128)S(1)}, f32[128,512]{1,0:T(8,128)S(1)}, u32[]{:S(2)}, u32[]{:S(2)}) collective-permute-start(f32[128,512]{1,0:T(8,128)S(1)} %shard_map.108.refs_3_), channel_id=1, source_target_pairs={{0,4},{4,0},{1,5},{5,1},{2,6},{6,2},{3,7},{7,3},{8,12},{12,8},{9,1... | collective-permute-start | bytes 786440 | tf_op jit(solution)/shard_map/ppermute | solution.py:337
  58.0 5.7 %collective-permute-start.23 = (f32[128,512]{1,0:T(8,128)S(1)}, f32[128,512]{1,0:T(8,128)S(1)}, u32[]{:S(2)}, u32[]{:S(2)}) collective-permute-start(f32[128,512]{1,0:T(8,128)S(1)} %shard_map.113), channel_id=1, source_target_pairs={{0,4},{4,0},{1,5},{5,1},{2,6},{6,2},{3,7},{7,3},{8,12},{12,8},{9,1... | collective-permute-start | bytes 786440 | tf_op jit(solution)/shard_map/ppermute | solution.py:337
  64.8 5.6 %collective-permute-start.29 = (f32[64,512]{1,0:T(8,128)S(1)}, f32[64,512]{1,0:T(8,128)S(1)}, u32[]{:S(2)}, u32[]{:S(2)}) collective-permute-start(f32[64,512]{1,0:T(8,128)S(1)} %get-tuple-element.53), channel_id=1, source_target_pairs={{0,4},{4,0},{1,5},{5,1},{2,6},{6,2},{3,7},{7,3},{8,12},{12,8},{9,1... | collective-permute-start | bytes 393224 | tf_op jit(solution)/shard_map/ppermute | solution.py:337
  64.9 6.4 %collective-permute-start.28 = (f32[64,512]{1,0:T(8,128)S(1)}, f32[64,512]{1,0:T(8,128)S(1)}, u32[]{:S(2)}, u32[]{:S(2)}) collective-permute-start(f32[64,512]{1,0:T(8,128)S(1)} %shard_map.111.refs_6_), channel_id=1, source_target_pairs={{0,1},{1,0},{2,3},{3,2},{4,5},{5,4},{6,7},{7,6},{8,9},{9,8},{10,11... | collective-permute-start | bytes 393224 | tf_op jit(solution)/shard_map/ppermute | solution.py:334
  66.5 7.6 %collective-permute-start.31 = (f32[64,512]{1,0:T(8,128)S(1)}, f32[64,512]{1,0:T(8,128)S(1)}, u32[]{:S(2)}, u32[]{:S(2)}) collective-permute-start(f32[64,512]{1,0:T(8,128)S(1)} %shard_map.118), channel_id=1, source_target_pairs={{0,3},{1,2},{2,1},{3,0},{4,7},{5,6},{6,5},{7,4},{8,11},{9,10},{10,... | collective-permute-start | bytes 393224 | tf_op jit(solution)/shard_map/ppermute | solution.py:334
  67.6 8.1 %collective-permute-start.33 = (f32[64,512]{1,0:T(8,128)S(1)}, f32[64,512]{1,0:T(8,128)S(1)}, u32[]{:S(2)}, u32[]{:S(2)}) collective-permute-start(f32[64,512]{1,0:T(8,128)S(1)} %shard_map.119), channel_id=1, source_target_pairs={{0,2},{1,3},{2,0},{3,1},{4,6},{5,7},{6,4},{7,5},{8,10},{9,11},{10,... | collective-permute-start | bytes 393224 | tf_op jit(solution)/shard_map/ppermute | solution.py:334
  69.8 4.3 %collective-permute-start.27 = (f32[8,128]{1,0:T(8,128)S(1)}, f32[8,128]{1,0:T(8,128)S(1)}, u32[]{:S(2)}, u32[]{:S(2)}) collective-permute-start(f32[8,128]{1,0:T(8,128)S(1)} %shard_map.116.refs_2_), channel_id=1, source_target_pairs={{4,28},{12,20},{20,12},{28,4},{5,29},{13,21},{21,13},{29,5},{6,30}... | collective-permute-start | bytes 12296 | tf_op jit(solution)/shard_map/ppermute | solution.py:485
  75.8 7.0 %collective-permute-start.36 = (f32[72,512]{1,0:T(8,128)S(1)}, f32[72,512]{1,0:T(8,128)S(1)}, u32[]{:S(2)}, u32[]{:S(2)}) collective-permute-start(f32[72,512]{1,0:T(8,128)S(1)} %shard_map.121.refs_4_.refs_0_), channel_id=1, source_target_pairs={{0,3},{1,2},{2,1},{3,0},{4,7},{5,6},{6,5},{7,4},{8,11},{9,10},{10,... | collective-permute-start | bytes 442376 | tf_op jit(solution)/shard_map/ppermute | solution.py:334
  77.7 8.1 %collective-permute-start.35 = (f32[72,512]{1,0:T(8,128)S(1)}, f32[72,512]{1,0:T(8,128)S(1)}, u32[]{:S(2)}, u32[]{:S(2)}) collective-permute-start(f32[72,512]{1,0:T(8,128)S(1)} %shard_map.121.refs_4_.refs_0_), channel_id=1, source_target_pairs={{0,2},{1,3},{2,0},{3,1},{4,6},{5,7},{6,4},{7,5},{8,10},{9,11},{10,... | collective-permute-start | bytes 442376 | tf_op jit(solution)/shard_map/ppermute | solution.py:334
  78.8 7.9 %collective-permute-start.34 = (f32[72,512]{1,0:T(8,128)S(1)}, f32[72,512]{1,0:T(8,128)S(1)}, u32[]{:S(2)}, u32[]{:S(2)}) collective-permute-start(f32[72,512]{1,0:T(8,128)S(1)} %shard_map.121.refs_4_.refs_0_), channel_id=1, source_target_pairs={{0,1},{1,0},{2,3},{3,2},{4,5},{5,4},{6,7},{7,6},{8,9},{9,8},{10,11... | collective-permute-start | bytes 442376 | tf_op jit(solution)/shard_map/ppermute | solution.py:334
  79.3 7.6 %collective-permute-start.37 = (f32[72,512]{1,0:T(8,128)S(1)}, f32[72,512]{1,0:T(8,128)S(1)}, u32[]{:S(2)}, u32[]{:S(2)}) collective-permute-start(f32[72,512]{1,0:T(8,128)S(1)} %shard_map.121.refs_4_.refs_0_), channel_id=1, source_target_pairs={{0,4},{4,0},{1,5},{5,1},{2,6},{6,2},{3,7},{7,3},{8,12},{12,8},{9,1... | collective-permute-start | bytes 442376 | tf_op jit(solution)/shard_map/ppermute | solution.py:337
  82.7 4.2 %collective-permute-start.39 = (f32[72,512]{1,0:T(8,128)S(1)}, f32[72,512]{1,0:T(8,128)S(1)}, u32[]{:S(2)}, u32[]{:S(2)}) collective-permute-start(f32[72,512]{1,0:T(8,128)S(1)} %collective-permute-done.36.refs_7_.refs_3_), channel_id=1, source_target_pairs={{0,4},{4,0},{1,5},{5,1},{2,6},{6,2},{3,7},{7,3},{8,12},{12,8},{9,1... | collective-permute-start | bytes 442376 | tf_op jit(solution)/shard_map/ppermute | solution.py:337
  (14 other events, 46.1 us)

commit v11 on v8

--- a/solution.py
+++ b/solution.py
@@ -10,8 +10,7 @@
 LEVELS = 4
 BLOCK = 128
 LOSS_ROWS = 8
-LOSS_PART = 4
-GIVE_PARTS = 1
+LOSS_PART = 2
 GELU_C = 0.7978845608028654
 GELU_A = 0.044715
 
@@ -148,8 +147,22 @@
     return pl.ds(pl.multiple_of(wid * (rows // 2), rows // 2), rows // 2)
 
 
-def g_pre_kernel(pre_ref, mask, loss, *refs):
-    terms, out = refs[:-1], refs[-1]
+def stacked(parts, extra, out):
+    rows, cols = parts.shape
+    for i in range(cols // BLOCK):
+        out[i * rows : (i + 1) * rows, :] = parts[:, i * BLOCK : (i + 1) * BLOCK]
+    out[-LOSS_ROWS:, :] = extra
+
+
+def unstacked(ref, cols):
+    rows = (ref.shape[0] - LOSS_ROWS) // (cols // BLOCK)
+    return jnp.concatenate(
+        [ref[i * rows : (i + 1) * rows, :] for i in range(cols // BLOCK)], axis=1
+    )
+
+
+def g_pre_kernel(pre_ref, mask, loss, keep, give, *refs):
+    *arrived, out, loss_out = refs
     mine = half_of(lax.axis_index("wid"), pre_ref.shape[0])
     pre = pre_ref[mine, :]
     inner = GELU_C * (pre + GELU_A * (pre * pre * pre))
@@ -157,10 +170,10 @@
     bend = jnp.tanh(inner)
     deriv = 0.5 * (1.0 + bend) + 0.5 * pre * (1.0 - bend * bend) * slope
     hit = mask[mine, :] > 0.0
-    rows = pre.shape[0]
-    out[:rows, :] = jnp.where(hit, deriv * total_of([t[...] for t in terms]), 0.0)
-    out[rows:, :] = jnp.zeros_like(out[rows:, :])
-    out[rows:, :BLOCK] = loss[:LOSS_ROWS, :BLOCK]
+    total = keep[...] + give[...] + total_of([unstacked(a, pre.shape[1]) for a in arrived])
+    out[...] = jnp.where(hit, deriv * total, 0.0)
+    loss_out[...] = jnp.zeros_like(loss_out)
+    loss_out[:LOSS_ROWS, :BLOCK] = loss[...] + total_of([a[-LOSS_ROWS:, :] for a in arrived])
 
 
 def running_parts(act, dict_ref):
@@ -235,7 +248,7 @@
 
 def error_kernel(loss_count, act, dictionary, resid, bias, table, mine, other, *refs):
     before, refs = refs[:loss_count], refs[loss_count:]
-    err_out, keep_out, *give_outs, loss_out = refs
+    err_out, keep_out, give_out, loss_out = refs
     upward = lax.axis_index("wid") == 0
     earlier = jnp.where(upward, mine[...], other[...])
     later = jnp.where(upward, other[...], mine[...])
@@ -257,22 +270,16 @@
         )
         half = gact.shape[0] // 2
         keep_out[:, cols] = jnp.where(upward, gact[:half, :], gact[half:, :])
-        given = jnp.where(upward, gact[half:, :], gact[:half, :])
-        for part, give_out in enumerate(give_outs):
-            size = give_out.shape[0]
-            give_out[:, cols] = given[part * size : (part + 1) * size, :]
-
-
-def spread_kernel(loss, out):
-    out[...] = jnp.zeros_like(out)
-    out[:LOSS_ROWS, :BLOCK] = loss[...]
-
-
-def collect_kernel(keep, *refs):
-    parts, out = refs[:-1], refs[-1]
-    for i, part in enumerate(parts):
-        span = slice(i * part.shape[0], (i + 1) * part.shape[0])
-        out[span, :] = keep[span, :] + part[...]
+        give_out[:, cols] = jnp.where(upward, gact[half:, :], gact[:half, :])
+
+
+def collect_kernel(keep, give, loss, out):
+    stacked(keep[...] + give[...], loss[...], out)
+
+
+def chip_losses_kernel(own, near, far, out):
+    first = jnp.where(lax.axis_index("wid") == 0, own[...], 0.0)
+    out[...] = first + near[...] + far[...]
 
 
 def add_kernel(*refs):
@@ -300,22 +307,18 @@
     resid = jnp.concatenate(
         [resids[q][spans[side], :].astype(jnp.bfloat16) for q, side in halves], axis=0
     )
-    grad = jnp.concatenate([g[:half, :].astype(jnp.bfloat16) for g in grads], axis=0)
+    grad = jnp.concatenate([g[...].astype(jnp.bfloat16) for g in grads], axis=0)
     total = base[...] + lax.dot_general(
         resid, grad, (((0,), (0,)), ((), ())), preferred_element_type=jnp.float32
     )
     out[...] = total.astype(out.dtype)
 
 
-def last_kernel(items, scale, n_early, *refs):
+def last_kernel(items, scale, one, two, *refs):
     *refs, out, loss_out = refs
-    early, refs = refs[:n_early], refs[n_early:]
     encode_kernel(items, *refs, out)
-    grads = list(early) + list(refs[items[0] : -1])
-    half = refs[0].shape[0] // 2
-    lanes = total_of([g[half:, :BLOCK] for g in grads])
     for m in range(LEVELS):
-        loss_out[m] = jnp.sum(lanes[m : m + 1, :]) * scale
+        loss_out[m] = jnp.sum(one[m : m + 1, :BLOCK] + two[m : m + 1, :BLOCK]) * scale
 
 
 def pick(index, choices):
@@ -373,7 +376,7 @@
     )
     resids = [piece if q == 0 else across(piece, q) for q, piece in enumerate(pieces)]
 
-    order = [0, 3, 1, 2] if n_tok == 4 else list(range(n_tok))
+    order = [0, 1, 3, 2] if n_tok == 4 else list(range(n_tok))
     steps = n_tok + n_lat - 2
     places = list(range(1, n_lat))
     acts, errs, hands, gives, gacts, loss = {}, {}, [], [], [], ()
@@ -440,50 +443,54 @@
             if c < 0:
                 continue
             q = order[c]
-            errs[q], keep, *give, loss_here = call(
+            errs[q], keep, give, loss_here = call(
                 functools.partial(error_kernel, len(loss)),
-                [bf16(count, rows, width), f32(rows // 2, lats)]
-                + [f32(rows // 2 // GIVE_PARTS, lats)] * GIVE_PARTS
-                + [f32(LOSS_ROWS, BLOCK)],
+                [bf16(count, rows, width)] + [f32(rows // 2, lats)] * 2 + [f32(LOSS_ROWS, BLOCK)],
                 (acts[q], dict_here, resids[q], bias_here, table, hands[c][1], hands[c][0], *loss),
                 after=sent if step < steps else (),
             )
             loss = (loss_here,)
-            gives.append((keep, *[swap(g) for g in give]))
+            gives.append((keep, swap(give)))
             ready.append(errs[q])
-        stages = [1] if step == steps - 1 else [0, *range(2, n_tok)] if step == steps else []
-        for c in stages:
-            if c < 0:
-                continue
-            q = order[c]
-            added = call(
-                collect_kernel, [f32(rows // 2, lats)], gives[c], after=sent if step < steps else ()
-            )[0]
-            gacts.append(across(added, q) if q else added)
-            ready.append(added)
         if step + 1 < steps:
             waits[step + 1] += ready
         ready_before = ready
 
-    loss, gap = call(spread_kernel, [f32(rows // LOSS_PART, lats)], loss)[0], 1
-    while gap < n_lat:
-        other = lax.ppermute(loss, "lat", [(p, p ^ gap) for p in range(n_lat)])
-        loss = call(add_kernel, [f32(*loss.shape)], (loss, other))[0]
-        gap *= 2
-
+    arrived = []
+    for c, q in enumerate(order[1:], 1):
+        message = call(
+            collect_kernel, [f32(rows // 2 * count + LOSS_ROWS, BLOCK)], (*gives[c], *loss)
+        )[0]
+        arrived.append(across(message, q))
     decoded = call(
         decode_kernel,
         [f32(width, lats)],
         (*[errs[q] for q in order], *[acts[q] for q in order]),
     )[0]
-    g_pre = call(
+    g_pre, losses = call(
         g_pre_kernel,
-        [f32(rows // 2 + LOSS_ROWS, lats)],
-        (pre, mask, loss, *gacts),
+        [f32(rows // 2, lats), f32(rows // LOSS_PART, lats)],
+        (pre, mask, *loss, *gives[0], *arrived),
         after=(decoded,),
-    )[0]
+    )
     mine = [across(g_pre, q) if q else g_pre for q in range(n_tok)]
     others = [swap(g) for g in mine]
+
+    def add(*arrays):
+        return call(add_kernel, [f32(*arrays[0].shape)], arrays)[0]
+
+    gap = 4 if n_lat % 4 == 0 else 1
+    while gap < n_lat:
+        losses = add(losses, lax.ppermute(losses, "lat", [(p, p ^ gap) for p in range(n_lat)]))
+        gap *= 2
+    if n_lat % 4 == 0:
+        losses = add(losses, swap(losses))
+        pairs = [(2 * p + w, 2 * (p ^ (1 + w)) + w) for p in range(n_lat) for w in range(2)]
+        near = lax.ppermute(losses, ("lat", "wid"), pairs)
+        pairs = [(2 * p + 1, 2 * (p ^ 3) + 1) for p in range(n_lat)]
+        far = lax.ppermute(losses, ("lat", "wid"), pairs)
+        losses = call(chip_losses_kernel, [f32(*losses.shape)], (losses, near, far))[0]
+    losses = (losses, swap(losses))
     early = [(q, side) for side in range(2) for q in range(n_tok) if (q, side) != (1, 1)]
     halves = [mine, others]
     early_grads = [halves[side][q] for q, side in early]
@@ -492,15 +499,13 @@
         [f32(width, lats)],
         (*resids, *early_grads, decoded),
     )[0]
-    grad, losses = call(
-        functools.partial(
-            last_kernel, (1, [(0, 1)]), 1.0 / (rows * n_tok * half * n_wid), len(early)
-        ),
+    grad, level_losses = call(
+        functools.partial(last_kernel, (1, [(0, 1)]), 1.0 / (rows * n_tok * half * n_wid)),
         [bf16(width, lats), f32(LEVELS)],
-        (*early_grads, resids[1], others[1], encoded),
+        (*losses, resids[1], others[1], encoded),
         out_specs=[VMEM, SMEM],
     )
-    return (losses, grad)
+    return (level_losses, grad)
 
 
 def solution(mesh):

time: 87.7 us -> 91 us (1.038)
  starting transfers between devices: 60 us -> 64.7 us
  waiting for transfers between devices: 14.7 us -> 13.2 us
    ppermute x14 -> x16, starting transfers between devices: 13.2 us -> 21 us  [swap(): return lax.ppermute(array, 'wid', [(w, w ^ 1) for w in range(n_wid)])]
    ppermute x2, waiting for transfers between devices: 4.02 us -> 0.01 us  [the longest x1 0.01 us: body(): far = lax.ppermute(losses, ('lat', 'wid'), pairs)]
    ppermute x12, waiting for transfers between devices: 6.16 us -> 9.37 us  [across(): return lax.ppermute(array, 'tok', [(t, t ^ q) for t in range(n_tok)])]
    ppermute x12, starting transfers between devices: 26.1 us -> 23.4 us  [body(): got[side].append((lax.ppermute(message, ('lat', 'wid'), pairs), 0))]
    ppermute x2, starting transfers between devices: 2.71 us -> 0.74 us  [the longest x1 0.67 us: body(): far = lax.ppermute(losses, ('lat', 'wid'), pairs)]
    ppermute x12, starting transfers between devices: 18 us -> 19.6 us  [across(): return lax.ppermute(array, 'tok', [(t, t ^ q) for t in range(n_tok)])]
    ppermute x14 -> x16, waiting for transfers between devices: 3.25 us -> 2.26 us  [swap(): return lax.ppermute(array, 'wid', [(w, w ^ 1) for w in range(n_wid)])]
    pallas_call x49 -> x47, Pallas kernels: 11.5 us -> 11.4 us  [call(): pl.pallas_call(run, out_shape=outs, in_specs=list(specs or [VMEM] * len(a...]
  transfers between devices with their start and end apart: 40 -> 42, of which waited for: 12 -> 12; matrix products, arithmetic and copies ran while one was open for 0% -> 0% of each run, Pallas kernels for 8% -> 8%
where the time goes in v11:
time: 91 us; the launch traced here: 90.6 us
  starting transfers between devices  64.7 us (71%)
  waiting for transfers between devices  13.2 us (15%)
  Pallas kernels  11.4 us (13%)
  between operations  1.25 us (1%)
    ppermute x12, starting transfers between devices, body(): got[side].append((lax.ppermute(message, ('lat', 'wid'), pairs), 0))  23.4 us
    ppermute x16, starting transfers between devices, swap(): return lax.ppermute(array, 'wid', [(w, w ^ 1) for w in range(n_wid)])  21 us
    ppermute x12, starting transfers between devices, across(): return lax.ppermute(array, 'tok', [(t, t ^ q) for t in range(n_tok)])  19.6 us
    pallas_call x47, Pallas kernels, call(): pl.pallas_call(run, out_shape=outs, in_specs=list(specs or [VMEM] * len(a...  11.4 us
    ppermute x12, waiting for transfers between devices, across(): return lax.ppermute(array, 'tok', [(t, t ^ q) for t in range(n_tok)])  9.37 us
    ppermute x16, waiting for transfers between devices, swap(): return lax.ppermute(array, 'wid', [(w, w ^ 1) for w in range(n_wid)])  2.26 us
  transfers between devices with their start and end apart: 42, of which 12 were waited for; matrix products, arithmetic and copies ran while one was open for 0% of the time, Pallas kernels for 8%

profile of v11, /device:TPU:0, one launch (start us, length us, event | category | flops | bytes accessed | tf_op | source)
XLA Modules:
  0.0 90.6 jit_solution(437686776703192517)
XLA Ops:
  0.7 2.9 %shard_map.77 = (f32[128,512]{1,0:T(8,128)S(1)}, bf16[512,512]{1,0:T(8,128)(2,1)S(1)}) custom-call(bf16[128,2048]{1,0:T(8,128)(2,1)} %refs_0_.3, bf16[512,2048]{1,0:T(8,128)(2,1)} %refs_1_.1), custom_call_target="tpu_custom_call" | custom-call | bytes 1024 | tf_op jit(solution)/shard_map/pallas_call | solution.py:37
  4.1 1.2 %collective-permute-done.refs_2_.refs_1_ = f32[128,512]{1,0:T(8,128)S(1)} collective-permute-done((f32[128,512]{1,0:T(8,128)S(1)}, f32[128,512]{1,0:T(8,128)S(1)}, u32[]{:S(2)}, u32[]{:S(2)}) %collective-permute-start) | collective-permute-done | bytes 262176 | tf_op jit(solution)/shard_map/ppermute | solution.py:343
  6.1 2.7 %collective-permute-start.4 = (f32[128,512]{1,0:T(8,128)S(1)}, f32[128,512]{1,0:T(8,128)S(1)}, u32[]{:S(2)}, u32[]{:S(2)}) collective-permute-start(f32[128,512]{1,0:T(8,128)S(1)} %get-tuple-element.39.refs_0_.refs_2_), channel_id=1, source_target_pairs={{0,1},{1,0},{2,3},{3,2},{4,5},{5,4},{6,7},{7,6},{8,9},{9,8},{10,11... | collective-permute-start | bytes 786440 | tf_op jit(solution)/shard_map/ppermute | solution.py:340
  9.1 3.5 %collective-permute-start.7 = (f32[128,512]{1,0:T(8,128)S(1)}, f32[128,512]{1,0:T(8,128)S(1)}, u32[]{:S(2)}, u32[]{:S(2)}) collective-permute-start(f32[128,512]{1,0:T(8,128)S(1)} %shard_map.87.refs_2_.refs_3_), channel_id=1, source_target_pairs={{0,8},{28,20},{1,9},{29,21},{2,10},{30,22},{3,11},{31,23}} | collective-permute-start | bytes 786440 | tf_op jit(solution)/shard_map/ppermute | solution.py:403
  12.9 1.3 %collective-permute-start.3 = (f32[128,512]{1,0:T(8,128)S(1)}, f32[128,512]{1,0:T(8,128)S(1)}, u32[]{:S(2)}, u32[]{:S(2)}) collective-permute-start(f32[128,512]{1,0:T(8,128)S(1)} %shard_map.81.refs_1_.refs_2_.refs_3_), channel_id=1, source_target_pairs={{0,8},{28,20},{1,9},{29,21},{2,10},{30,22},{3,11},{31,23}} | collective-permute-start | bytes 786440 | tf_op jit(solution)/shard_map/ppermute | solution.py:403
  14.2 1.6 %collective-permute-start.6 = (f32[128,512]{1,0:T(8,128)S(1)}, f32[128,512]{1,0:T(8,128)S(1)}, u32[]{:S(2)}, u32[]{:S(2)}) collective-permute-start(f32[128,512]{1,0:T(8,128)S(1)} %get-tuple-element.39.refs_0_.refs_2_), channel_id=1, source_target_pairs={{0,3},{1,2},{2,1},{3,0},{4,7},{5,6},{6,5},{7,4},{8,11},{9,10},{10,... | collective-permute-start | bytes 786440 | tf_op jit(solution)/shard_map/ppermute | solution.py:340
  16.5 4.4 %collective-permute-start.8 = (f32[128,512]{1,0:T(8,128)S(1)}, f32[128,512]{1,0:T(8,128)S(1)}, u32[]{:S(2)}, u32[]{:S(2)}) collective-permute-start(f32[128,512]{1,0:T(8,128)S(1)} %shard_map.89), channel_id=1, source_target_pairs={{0,8},{28,20},{8,16},{20,12},{1,9},{29,21},{9,17},{21,13},{2,10},{... | collective-permute-start | bytes 786440 | tf_op jit(solution)/shard_map/ppermute | solution.py:414
  21.2 2.5 %collective-permute-start.5 = (f32[128,512]{1,0:T(8,128)S(1)}, f32[128,512]{1,0:T(8,128)S(1)}, u32[]{:S(2)}, u32[]{:S(2)}) collective-permute-start(f32[128,512]{1,0:T(8,128)S(1)} %shard_map.84.refs_1_.refs_4_), channel_id=1, source_target_pairs={{0,8},{28,20},{8,16},{20,12},{1,9},{29,21},{9,17},{21,13},{2,10},{... | collective-permute-start | bytes 786440 | tf_op jit(solution)/shard_map/ppermute | solution.py:414
  23.7 2.0 %collective-permute-start.1 = (f32[128,512]{1,0:T(8,128)S(1)}, f32[128,512]{1,0:T(8,128)S(1)}, u32[]{:S(2)}, u32[]{:S(2)}) collective-permute-start(f32[128,512]{1,0:T(8,128)S(1)} %get-tuple-element.39.refs_0_.refs_2_), channel_id=1, source_target_pairs={{0,2},{1,3},{2,0},{3,1},{4,6},{5,7},{6,4},{7,5},{8,10},{9,11},{10,... | collective-permute-start | bytes 786440 | tf_op jit(solution)/shard_map/ppermute | solution.py:340
  25.8 1.6 %collective-permute-start.11 = (f32[128,512]{1,0:T(8,128)S(1)}, f32[128,512]{1,0:T(8,128)S(1)}, u32[]{:S(2)}, u32[]{:S(2)}) collective-permute-start(f32[128,512]{1,0:T(8,128)S(1)} %get-tuple-element.43), channel_id=1, source_target_pairs={{0,1},{1,0},{2,3},{3,2},{4,5},{5,4},{6,7},{7,6},{8,9},{9,8},{10,11... | collective-permute-start | bytes 786440 | tf_op jit(solution)/shard_map/ppermute | solution.py:340
  27.8 1.9 %collective-permute-start.10 = (f32[128,512]{1,0:T(8,128)S(1)}, f32[128,512]{1,0:T(8,128)S(1)}, u32[]{:S(2)}, u32[]{:S(2)}) collective-permute-start(f32[128,512]{1,0:T(8,128)S(1)} %shard_map.91.refs_4_), channel_id=1, source_target_pairs={{0,8},{28,20},{8,16},{20,12},{16,24},{12,4},{1,9},{29,21},{9,17},{... | collective-permute-start | bytes 786440 | tf_op jit(solution)/shard_map/ppermute | solution.py:414
  30.1 2.0 %collective-permute-start.13 = (f32[128,512]{1,0:T(8,128)S(1)}, f32[128,512]{1,0:T(8,128)S(1)}, u32[]{:S(2)}, u32[]{:S(2)}) collective-permute-start(f32[128,512]{1,0:T(8,128)S(1)} %shard_map.92.refs_1_.refs_4_), channel_id=1, source_target_pairs={{0,8},{28,20},{8,16},{20,12},{16,24},{12,4},{1,9},{29,21},{9,17},{... | collective-permute-start | bytes 786440 | tf_op jit(solution)/shard_map/ppermute | solution.py:414
  32.0 2.9 %collective-permute-start.14 = (f32[128,512]{1,0:T(8,128)S(1)}, f32[128,512]{1,0:T(8,128)S(1)}, u32[]{:S(2)}, u32[]{:S(2)}) collective-permute-start(f32[128,512]{1,0:T(8,128)S(1)} %get-tuple-element.44), channel_id=1, source_target_pairs={{0,3},{1,2},{2,1},{3,0},{4,7},{5,6},{6,5},{7,4},{8,11},{9,10},{10,... | collective-permute-start | bytes 786440 | tf_op jit(solution)/shard_map/ppermute | solution.py:340
  35.4 2.6 %collective-permute-start.12 = (f32[128,512]{1,0:T(8,128)S(1)}, f32[128,512]{1,0:T(8,128)S(1)}, u32[]{:S(2)}, u32[]{:S(2)}) collective-permute-start(f32[128,512]{1,0:T(8,128)S(1)} %shard_map.96.refs_4_), channel_id=1, source_target_pairs={{0,8},{28,20},{8,16},{20,12},{16,24},{12,4},{1,9},{29,21},{9,17},{... | collective-permute-start | bytes 786440 | tf_op jit(solution)/shard_map/ppermute | solution.py:414
  38.4 2.5 %collective-permute-start.16 = (f32[128,512]{1,0:T(8,128)S(1)}, f32[128,512]{1,0:T(8,128)S(1)}, u32[]{:S(2)}, u32[]{:S(2)}) collective-permute-start(f32[128,512]{1,0:T(8,128)S(1)} %shard_map.98.refs_3_), channel_id=1, source_target_pairs={{0,8},{28,20},{8,16},{20,12},{16,24},{12,4},{1,9},{29,21},{9,17},{... | collective-permute-start | bytes 786440 | tf_op jit(solution)/shard_map/ppermute | solution.py:414
  40.8 1.5 %collective-permute-start.9 = (f32[128,512]{1,0:T(8,128)S(1)}, f32[128,512]{1,0:T(8,128)S(1)}, u32[]{:S(2)}, u32[]{:S(2)}) collective-permute-start(f32[128,512]{1,0:T(8,128)S(1)} %get-tuple-element.41), channel_id=1, source_target_pairs={{0,2},{1,3},{2,0},{3,1},{4,6},{5,7},{6,4},{7,5},{8,10},{9,11},{10,... | collective-permute-start | bytes 786440 | tf_op jit(solution)/shard_map/ppermute | solution.py:340
  43.3 1.4 %collective-permute-done.16.refs_0_.refs_2_.refs_1_ = f32[128,512]{1,0:T(8,128)S(1)} collective-permute-done((f32[128,512]{1,0:T(8,128)S(1)}, f32[128,512]{1,0:T(8,128)S(1)}, u32[]{:S(2)}, u32[]{:S(2)}) %collective-permute-start.16) | collective-permute-done | bytes 262176 | tf_op jit(solution)/shard_map/ppermute | solution.py:414
  46.5 0.8 collective-permute-done.9.refs_3_.refs_2_
  48.7 5.7 %collective-permute-start.23 = (f32[128,512]{1,0:T(8,128)S(1)}, f32[128,512]{1,0:T(8,128)S(1)}, u32[]{:S(2)}, u32[]{:S(2)}) collective-permute-start(f32[128,512]{1,0:T(8,128)S(1)} %shard_map.108.refs_3_), channel_id=1, source_target_pairs={{0,4},{4,0},{1,5},{5,1},{2,6},{6,2},{3,7},{7,3},{8,12},{12,8},{9,1... | collective-permute-start | bytes 786440 | tf_op jit(solution)/shard_map/ppermute | solution.py:343
  55.2 5.0 %collective-permute-start.22 = (f32[128,512]{1,0:T(8,128)S(1)}, f32[128,512]{1,0:T(8,128)S(1)}, u32[]{:S(2)}, u32[]{:S(2)}) collective-permute-start(f32[128,512]{1,0:T(8,128)S(1)} %shard_map.112), channel_id=1, source_target_pairs={{0,4},{4,0},{1,5},{5,1},{2,6},{6,2},{3,7},{7,3},{8,12},{12,8},{9,1... | collective-permute-start | bytes 786440 | tf_op jit(solution)/shard_map/ppermute | solution.py:343
  62.4 1.6 %collective-permute-start.26 = (f32[264,128]{1,0:T(8,128)S(1)}, f32[264,128]{1,0:T(8,128)S(1)}, u32[]{:S(2)}, u32[]{:S(2)}) collective-permute-start(f32[264,128]{1,0:T(8,128)S(1)} %shard_map.115), channel_id=1, source_target_pairs={{0,1},{1,0},{2,3},{3,2},{4,5},{5,4},{6,7},{7,6},{8,9},{9,8},{10,11... | collective-permute-start | bytes 405512 | tf_op jit(solution)/shard_map/ppermute | solution.py:340
  64.6 1.5 %collective-permute-start.30 = (f32[264,128]{1,0:T(8,128)S(1)}, f32[264,128]{1,0:T(8,128)S(1)}, u32[]{:S(2)}, u32[]{:S(2)}) collective-permute-start(f32[264,128]{1,0:T(8,128)S(1)} %shard_map.117), channel_id=1, source_target_pairs={{0,2},{1,3},{2,0},{3,1},{4,6},{5,7},{6,4},{7,5},{8,10},{9,11},{10,... | collective-permute-start | bytes 405512 | tf_op jit(solution)/shard_map/ppermute | solution.py:340
  66.2 0.8 shard_map.118.refs_8_.refs_11_
  67.5 1.4 %collective-permute-done.26.refs_5_ = f32[264,128]{1,0:T(8,128)S(1)} collective-permute-done((f32[264,128]{1,0:T(8,128)S(1)}, f32[264,128]{1,0:T(8,128)S(1)}, u32[]{:S(2)}, u32[]{:S(2)}) %collective-permute-start.26) | collective-permute-done | bytes 135200 | tf_op jit(solution)/shard_map/ppermute | solution.py:340
  68.9 2.3 %collective-permute-done.28.refs_6_ = f32[264,128]{1,0:T(8,128)S(1)} collective-permute-done((f32[264,128]{1,0:T(8,128)S(1)}, f32[264,128]{1,0:T(8,128)S(1)}, u32[]{:S(2)}, u32[]{:S(2)}) %collective-permute-start.28) | collective-permute-done | bytes 135200 | tf_op jit(solution)/shard_map/ppermute | solution.py:340
  71.2 1.5 %collective-permute-done.30.refs_7_ = f32[264,128]{1,0:T(8,128)S(1)} collective-permute-done((f32[264,128]{1,0:T(8,128)S(1)}, f32[264,128]{1,0:T(8,128)S(1)}, u32[]{:S(2)}, u32[]{:S(2)}) %collective-permute-start.30) | collective-permute-done | bytes 135200 | tf_op jit(solution)/shard_map/ppermute | solution.py:340
  73.0 2.5 %collective-permute-start.38 = (f32[64,512]{1,0:T(8,128)S(1)}, f32[64,512]{1,0:T(8,128)S(1)}, u32[]{:S(2)}, u32[]{:S(2)}) collective-permute-start(f32[64,512]{1,0:T(8,128)S(1)} %get-tuple-element.63.refs_4_), channel_id=1, source_target_pairs={{0,3},{1,2},{2,1},{3,0},{4,7},{5,6},{6,5},{7,4},{8,11},{9,10},{10,... | collective-permute-start | bytes 393224 | tf_op jit(solution)/shard_map/ppermute | solution.py:340
  77.3 2.8 %collective-permute-done.38.refs_7_ = f32[64,512]{1,0:T(8,128)S(1)} collective-permute-done((f32[64,512]{1,0:T(8,128)S(1)}, f32[64,512]{1,0:T(8,128)S(1)}, u32[]{:S(2)}, u32[]{:S(2)}) %collective-permute-start.38) | collective-permute-done | bytes 131104 | tf_op jit(solution)/shard_map/ppermute | solution.py:340
  80.1 2.1 %collective-permute-start.39 = (f32[64,512]{1,0:T(8,128)S(1)}, f32[64,512]{1,0:T(8,128)S(1)}, u32[]{:S(2)}, u32[]{:S(2)}) collective-permute-start(f32[64,512]{1,0:T(8,128)S(1)} %get-tuple-element.63.refs_4_), channel_id=1, source_target_pairs={{0,4},{4,0},{1,5},{5,1},{2,6},{6,2},{3,7},{7,3},{8,12},{12,8},{9,1... | collective-permute-start | bytes 393224 | tf_op jit(solution)/shard_map/ppermute | solution.py:343
  83.1 2.7 %collective-permute-start.36 = (f32[64,512]{1,0:T(8,128)S(1)}, f32[64,512]{1,0:T(8,128)S(1)}, u32[]{:S(2)}, u32[]{:S(2)}) collective-permute-start(f32[64,512]{1,0:T(8,128)S(1)} %collective-permute-done.35.refs_5_), channel_id=1, source_target_pairs={{0,4},{4,0},{1,5},{5,1},{2,6},{6,2},{3,7},{7,3},{8,12},{12,8},{9,1... | collective-permute-start | bytes 393224 | tf_op jit(solution)/shard_map/ppermute | solution.py:343
  85.8 2.7 %collective-permute-start.34 = (f32[64,512]{1,0:T(8,128)S(1)}, f32[64,512]{1,0:T(8,128)S(1)}, u32[]{:S(2)}, u32[]{:S(2)}) collective-permute-start(f32[64,512]{1,0:T(8,128)S(1)} %shard_map.121.refs_0_), channel_id=1, source_target_pairs={{0,4},{4,0},{1,5},{5,1},{2,6},{6,2},{3,7},{7,3},{8,12},{12,8},{9,1... | collective-permute-start | bytes 393224 | tf_op jit(solution)/shard_map/ppermute | solution.py:343
  89.5 1.1 %shard_map.123 = (bf16[512,512]{1,0:T(8,128)(2,1)}, f32[4]{0:T(128)}) custom-call(f32[64,512]{1,0:T(8,128)S(1)} %shard_map.121.refs_0_, f32[64,512]{1,0:T(8,128)S(1)} %collective-permute-done.34.refs_1_, f32[128,512]{1,0:T(8,128)S(1)} %collective-permute-done.11.refs_5_.refs_2_.refs_1_, f32[64,512]{1,0:T(8,128)S(1)} %collective-permute-done.36.refs_3_, ...), custom_call_target="tpu_custom_call" | custom-call | bytes 1024 | tf_op jit(solution)/shard_map/pallas_call | solution.py:37
  (109 shorter events, 16.6 us)
Async XLA Ops:
  5.4 7.2 %collective-permute-start.2 = (f32[512,512]{1,0:T(8,128)S(1)}, f32[512,512]{1,0:T(8,128)S(1)}, u32[]{:S(2)}, u32[]{:S(2)}) collective-permute-start(f32[512,512]{1,0:T(8,128)S(1)} %get-tuple-element.36.refs_4_), channel_id=1, source_target_pairs={{0,4},{4,0},{1,5},{5,1},{2,6},{6,2},{3,7},{7,3},{8,12},{12,8},{9,1... | collective-permute-start | bytes 3145736 | tf_op jit(solution)/shard_map/ppermute | solution.py:343
  6.1 9.8 %collective-permute-start.4 = (f32[128,512]{1,0:T(8,128)S(1)}, f32[128,512]{1,0:T(8,128)S(1)}, u32[]{:S(2)}, u32[]{:S(2)}) collective-permute-start(f32[128,512]{1,0:T(8,128)S(1)} %get-tuple-element.39.refs_0_.refs_2_), channel_id=1, source_target_pairs={{0,1},{1,0},{2,3},{3,2},{4,5},{5,4},{6,7},{7,6},{8,9},{9,8},{10,11... | collective-permute-start | bytes 786440 | tf_op jit(solution)/shard_map/ppermute | solution.py:340
  9.1 7.4 %collective-permute-start.7 = (f32[128,512]{1,0:T(8,128)S(1)}, f32[128,512]{1,0:T(8,128)S(1)}, u32[]{:S(2)}, u32[]{:S(2)}) collective-permute-start(f32[128,512]{1,0:T(8,128)S(1)} %shard_map.87.refs_2_.refs_3_), channel_id=1, source_target_pairs={{0,8},{28,20},{1,9},{29,21},{2,10},{30,22},{3,11},{31,23}} | collective-permute-start | bytes 786440 | tf_op jit(solution)/shard_map/ppermute | solution.py:403
  12.9 8.3 %collective-permute-start.3 = (f32[128,512]{1,0:T(8,128)S(1)}, f32[128,512]{1,0:T(8,128)S(1)}, u32[]{:S(2)}, u32[]{:S(2)}) collective-permute-start(f32[128,512]{1,0:T(8,128)S(1)} %shard_map.81.refs_1_.refs_2_.refs_3_), channel_id=1, source_target_pairs={{0,8},{28,20},{1,9},{29,21},{2,10},{30,22},{3,11},{31,23}} | collective-permute-start | bytes 786440 | tf_op jit(solution)/shard_map/ppermute | solution.py:403
  14.2 13.2 %collective-permute-start.6 = (f32[128,512]{1,0:T(8,128)S(1)}, f32[128,512]{1,0:T(8,128)S(1)}, u32[]{:S(2)}, u32[]{:S(2)}) collective-permute-start(f32[128,512]{1,0:T(8,128)S(1)} %get-tuple-element.39.refs_0_.refs_2_), channel_id=1, source_target_pairs={{0,3},{1,2},{2,1},{3,0},{4,7},{5,6},{6,5},{7,4},{8,11},{9,10},{10,... | collective-permute-start | bytes 786440 | tf_op jit(solution)/shard_map/ppermute | solution.py:340
  16.5 11.2 %collective-permute-start.8 = (f32[128,512]{1,0:T(8,128)S(1)}, f32[128,512]{1,0:T(8,128)S(1)}, u32[]{:S(2)}, u32[]{:S(2)}) collective-permute-start(f32[128,512]{1,0:T(8,128)S(1)} %shard_map.89), channel_id=1, source_target_pairs={{0,8},{28,20},{8,16},{20,12},{1,9},{29,21},{9,17},{21,13},{2,10},{... | collective-permute-start | bytes 786440 | tf_op jit(solution)/shard_map/ppermute | solution.py:414
  21.2 8.8 %collective-permute-start.5 = (f32[128,512]{1,0:T(8,128)S(1)}, f32[128,512]{1,0:T(8,128)S(1)}, u32[]{:S(2)}, u32[]{:S(2)}) collective-permute-start(f32[128,512]{1,0:T(8,128)S(1)} %shard_map.84.refs_1_.refs_4_), channel_id=1, source_target_pairs={{0,8},{28,20},{8,16},{20,12},{1,9},{29,21},{9,17},{21,13},{2,10},{... | collective-permute-start | bytes 786440 | tf_op jit(solution)/shard_map/ppermute | solution.py:414
  23.7 11.3 %collective-permute-start.1 = (f32[128,512]{1,0:T(8,128)S(1)}, f32[128,512]{1,0:T(8,128)S(1)}, u32[]{:S(2)}, u32[]{:S(2)}) collective-permute-start(f32[128,512]{1,0:T(8,128)S(1)} %get-tuple-element.39.refs_0_.refs_2_), channel_id=1, source_target_pairs={{0,2},{1,3},{2,0},{3,1},{4,6},{5,7},{6,4},{7,5},{8,10},{9,11},{10,... | collective-permute-start | bytes 786440 | tf_op jit(solution)/shard_map/ppermute | solution.py:340
  25.8 9.5 %collective-permute-start.11 = (f32[128,512]{1,0:T(8,128)S(1)}, f32[128,512]{1,0:T(8,128)S(1)}, u32[]{:S(2)}, u32[]{:S(2)}) collective-permute-start(f32[128,512]{1,0:T(8,128)S(1)} %get-tuple-element.43), channel_id=1, source_target_pairs={{0,1},{1,0},{2,3},{3,2},{4,5},{5,4},{6,7},{7,6},{8,9},{9,8},{10,11... | collective-permute-start | bytes 786440 | tf_op jit(solution)/shard_map/ppermute | solution.py:340
  27.8 7.5 %collective-permute-start.10 = (f32[128,512]{1,0:T(8,128)S(1)}, f32[128,512]{1,0:T(8,128)S(1)}, u32[]{:S(2)}, u32[]{:S(2)}) collective-permute-start(f32[128,512]{1,0:T(8,128)S(1)} %shard_map.91.refs_4_), channel_id=1, source_target_pairs={{0,8},{28,20},{8,16},{20,12},{16,24},{12,4},{1,9},{29,21},{9,17},{... | collective-permute-start | bytes 786440 | tf_op jit(solution)/shard_map/ppermute | solution.py:414
  30.1 8.2 %collective-permute-start.13 = (f32[128,512]{1,0:T(8,128)S(1)}, f32[128,512]{1,0:T(8,128)S(1)}, u32[]{:S(2)}, u32[]{:S(2)}) collective-permute-start(f32[128,512]{1,0:T(8,128)S(1)} %shard_map.92.refs_1_.refs_4_), channel_id=1, source_target_pairs={{0,8},{28,20},{8,16},{20,12},{16,24},{12,4},{1,9},{29,21},{9,17},{... | collective-permute-start | bytes 786440 | tf_op jit(solution)/shard_map/ppermute | solution.py:414
  32.0 10.5 %collective-permute-start.14 = (f32[128,512]{1,0:T(8,128)S(1)}, f32[128,512]{1,0:T(8,128)S(1)}, u32[]{:S(2)}, u32[]{:S(2)}) collective-permute-start(f32[128,512]{1,0:T(8,128)S(1)} %get-tuple-element.44), channel_id=1, source_target_pairs={{0,3},{1,2},{2,1},{3,0},{4,7},{5,6},{6,5},{7,4},{8,11},{9,10},{10,... | collective-permute-start | bytes 786440 | tf_op jit(solution)/shard_map/ppermute | solution.py:340
  35.4 7.2 %collective-permute-start.12 = (f32[128,512]{1,0:T(8,128)S(1)}, f32[128,512]{1,0:T(8,128)S(1)}, u32[]{:S(2)}, u32[]{:S(2)}) collective-permute-start(f32[128,512]{1,0:T(8,128)S(1)} %shard_map.96.refs_4_), channel_id=1, source_target_pairs={{0,8},{28,20},{8,16},{20,12},{16,24},{12,4},{1,9},{29,21},{9,17},{... | collective-permute-start | bytes 786440 | tf_op jit(solution)/shard_map/ppermute | solution.py:414
  38.4 6.3 %collective-permute-start.16 = (f32[128,512]{1,0:T(8,128)S(1)}, f32[128,512]{1,0:T(8,128)S(1)}, u32[]{:S(2)}, u32[]{:S(2)}) collective-permute-start(f32[128,512]{1,0:T(8,128)S(1)} %shard_map.98.refs_3_), channel_id=1, source_target_pairs={{0,8},{28,20},{8,16},{20,12},{16,24},{12,4},{1,9},{29,21},{9,17},{... | collective-permute-start | bytes 786440 | tf_op jit(solution)/shard_map/ppermute | solution.py:414
  40.8 6.4 %collective-permute-start.9 = (f32[128,512]{1,0:T(8,128)S(1)}, f32[128,512]{1,0:T(8,128)S(1)}, u32[]{:S(2)}, u32[]{:S(2)}) collective-permute-start(f32[128,512]{1,0:T(8,128)S(1)} %get-tuple-element.41), channel_id=1, source_target_pairs={{0,2},{1,3},{2,0},{3,1},{4,6},{5,7},{6,4},{7,5},{8,10},{9,11},{10,... | collective-permute-start | bytes 786440 | tf_op jit(solution)/shard_map/ppermute | solution.py:340
  45.4 9.0 %collective-permute-start.20 = (f32[128,512]{1,0:T(8,128)S(1)}, f32[128,512]{1,0:T(8,128)S(1)}, u32[]{:S(2)}, u32[]{:S(2)}) collective-permute-start(f32[128,512]{1,0:T(8,128)S(1)} %shard_map.103.refs_4_), channel_id=1, source_target_pairs={{0,4},{4,0},{1,5},{5,1},{2,6},{6,2},{3,7},{7,3},{8,12},{12,8},{9,1... | collective-permute-start | bytes 786440 | tf_op jit(solution)/shard_map/ppermute | solution.py:343
  47.3 7.8 %collective-permute-start.18 = (f32[128,512]{1,0:T(8,128)S(1)}, f32[128,512]{1,0:T(8,128)S(1)}, u32[]{:S(2)}, u32[]{:S(2)}) collective-permute-start(f32[128,512]{1,0:T(8,128)S(1)} %shard_map.106.refs_2_), channel_id=1, source_target_pairs={{16,24},{12,4},{17,25},{13,5},{18,26},{14,6},{19,27},{15,7}} | collective-permute-start | bytes 786440 | tf_op jit(solution)/shard_map/ppermute | solution.py:414
  48.0 7.2 %collective-permute-start.21 = (f32[128,512]{1,0:T(8,128)S(1)}, f32[128,512]{1,0:T(8,128)S(1)}, u32[]{:S(2)}, u32[]{:S(2)}) collective-permute-start(f32[128,512]{1,0:T(8,128)S(1)} %shard_map.107.refs_3_.refs_8_), channel_id=1, source_target_pairs={{16,24},{12,4},{17,25},{13,5},{18,26},{14,6},{19,27},{15,7}} | collective-permute-start | bytes 786440 | tf_op jit(solution)/shard_map/ppermute | solution.py:414
  48.7 11.5 %collective-permute-start.23 = (f32[128,512]{1,0:T(8,128)S(1)}, f32[128,512]{1,0:T(8,128)S(1)}, u32[]{:S(2)}, u32[]{:S(2)}) collective-permute-start(f32[128,512]{1,0:T(8,128)S(1)} %shard_map.108.refs_3_), channel_id=1, source_target_pairs={{0,4},{4,0},{1,5},{5,1},{2,6},{6,2},{3,7},{7,3},{8,12},{12,8},{9,1... | collective-permute-start | bytes 786440 | tf_op jit(solution)/shard_map/ppermute | solution.py:343
  55.2 6.2 %collective-permute-start.22 = (f32[128,512]{1,0:T(8,128)S(1)}, f32[128,512]{1,0:T(8,128)S(1)}, u32[]{:S(2)}, u32[]{:S(2)}) collective-permute-start(f32[128,512]{1,0:T(8,128)S(1)} %shard_map.112), channel_id=1, source_target_pairs={{0,4},{4,0},{1,5},{5,1},{2,6},{6,2},{3,7},{7,3},{8,12},{12,8},{9,1... | collective-permute-start | bytes 786440 | tf_op jit(solution)/shard_map/ppermute | solution.py:343
  62.4 6.5 %collective-permute-start.26 = (f32[264,128]{1,0:T(8,128)S(1)}, f32[264,128]{1,0:T(8,128)S(1)}, u32[]{:S(2)}, u32[]{:S(2)}) collective-permute-start(f32[264,128]{1,0:T(8,128)S(1)} %shard_map.115), channel_id=1, source_target_pairs={{0,1},{1,0},{2,3},{3,2},{4,5},{5,4},{6,7},{7,6},{8,9},{9,8},{10,11... | collective-permute-start | bytes 405512 | tf_op jit(solution)/shard_map/ppermute | solution.py:340
  64.0 7.2 %collective-permute-start.28 = (f32[264,128]{1,0:T(8,128)S(1)}, f32[264,128]{1,0:T(8,128)S(1)}, u32[]{:S(2)}, u32[]{:S(2)}) collective-permute-start(f32[264,128]{1,0:T(8,128)S(1)} %shard_map.116), channel_id=1, source_target_pairs={{0,3},{1,2},{2,1},{3,0},{4,7},{5,6},{6,5},{7,4},{8,11},{9,10},{10,... | collective-permute-start | bytes 405512 | tf_op jit(solution)/shard_map/ppermute | solution.py:340
  64.6 8.1 %collective-permute-start.30 = (f32[264,128]{1,0:T(8,128)S(1)}, f32[264,128]{1,0:T(8,128)S(1)}, u32[]{:S(2)}, u32[]{:S(2)}) collective-permute-start(f32[264,128]{1,0:T(8,128)S(1)} %shard_map.117), channel_id=1, source_target_pairs={{0,2},{1,3},{2,0},{3,1},{4,6},{5,7},{6,4},{7,5},{8,10},{9,11},{10,... | collective-permute-start | bytes 405512 | tf_op jit(solution)/shard_map/ppermute | solution.py:340
  73.0 7.1 %collective-permute-start.38 = (f32[64,512]{1,0:T(8,128)S(1)}, f32[64,512]{1,0:T(8,128)S(1)}, u32[]{:S(2)}, u32[]{:S(2)}) collective-permute-start(f32[64,512]{1,0:T(8,128)S(1)} %get-tuple-element.63.refs_4_), channel_id=1, source_target_pairs={{0,3},{1,2},{2,1},{3,0},{4,7},{5,6},{6,5},{7,4},{8,11},{9,10},{10,... | collective-permute-start | bytes 393224 | tf_op jit(solution)/shard_map/ppermute | solution.py:340
  75.4 7.2 %collective-permute-start.37 = (f32[64,512]{1,0:T(8,128)S(1)}, f32[64,512]{1,0:T(8,128)S(1)}, u32[]{:S(2)}, u32[]{:S(2)}) collective-permute-start(f32[64,512]{1,0:T(8,128)S(1)} %get-tuple-element.63.refs_4_), channel_id=1, source_target_pairs={{0,2},{1,3},{2,0},{3,1},{4,6},{5,7},{6,4},{7,5},{8,10},{9,11},{10,... | collective-permute-start | bytes 393224 | tf_op jit(solution)/shard_map/ppermute | solution.py:340
  75.9 6.7 %collective-permute-start.35 = (f32[64,512]{1,0:T(8,128)S(1)}, f32[64,512]{1,0:T(8,128)S(1)}, u32[]{:S(2)}, u32[]{:S(2)}) collective-permute-start(f32[64,512]{1,0:T(8,128)S(1)} %get-tuple-element.63.refs_4_), channel_id=1, source_target_pairs={{0,1},{1,0},{2,3},{3,2},{4,5},{5,4},{6,7},{7,6},{8,9},{9,8},{10,11... | collective-permute-start | bytes 393224 | tf_op jit(solution)/shard_map/ppermute | solution.py:340
  76.5 6.6 %collective-permute-start.33 = (f32[64,512]{1,0:T(8,128)S(1)}, f32[64,512]{1,0:T(8,128)S(1)}, u32[]{:S(2)}, u32[]{:S(2)}) collective-permute-start(f32[64,512]{1,0:T(8,128)S(1)} %shard_map.120.refs_0_), channel_id=1, source_target_pairs={{4,28},{12,20},{20,12},{28,4},{5,29},{13,21},{21,13},{29,5},{6,30}... | collective-permute-start | bytes 393224 | tf_op jit(solution)/shard_map/ppermute | solution.py:491
  77.2 8.6 %collective-permute-start.32 = (f32[64,512]{1,0:T(8,128)S(1)}, f32[64,512]{1,0:T(8,128)S(1)}, u32[]{:S(2)}, u32[]{:S(2)}) collective-permute-start(f32[64,512]{1,0:T(8,128)S(1)} %shard_map.120.refs_0_), channel_id=1, source_target_pairs={{0,8},{4,20},{8,0},{12,28},{16,24},{20,4},{24,16},{28,12},{1,9},{5... | collective-permute-start | bytes 393224 | tf_op jit(solution)/shard_map/ppermute | solution.py:489
  80.1 8.4 %collective-permute-start.39 = (f32[64,512]{1,0:T(8,128)S(1)}, f32[64,512]{1,0:T(8,128)S(1)}, u32[]{:S(2)}, u32[]{:S(2)}) collective-permute-start(f32[64,512]{1,0:T(8,128)S(1)} %get-tuple-element.63.refs_4_), channel_id=1, source_target_pairs={{0,4},{4,0},{1,5},{5,1},{2,6},{6,2},{3,7},{7,3},{8,12},{12,8},{9,1... | collective-permute-start | bytes 393224 | tf_op jit(solution)/shard_map/ppermute | solution.py:343
  82.6 5.9 %collective-permute-start.41 = (f32[64,512]{1,0:T(8,128)S(1)}, f32[64,512]{1,0:T(8,128)S(1)}, u32[]{:S(2)}, u32[]{:S(2)}) collective-permute-start(f32[64,512]{1,0:T(8,128)S(1)} %collective-permute-done.38.refs_7_), channel_id=1, source_target_pairs={{0,4},{4,0},{1,5},{5,1},{2,6},{6,2},{3,7},{7,3},{8,12},{12,8},{9,1... | collective-permute-start | bytes 393224 | tf_op jit(solution)/shard_map/ppermute | solution.py:343
  82.6 5.9 %collective-permute-start.40 = (f32[64,512]{1,0:T(8,128)S(1)}, f32[64,512]{1,0:T(8,128)S(1)}, u32[]{:S(2)}, u32[]{:S(2)}) collective-permute-start(f32[64,512]{1,0:T(8,128)S(1)} %collective-permute-done.37.refs_6_), channel_id=1, source_target_pairs={{0,4},{4,0},{1,5},{5,1},{2,6},{6,2},{3,7},{7,3},{8,12},{12,8},{9,1... | collective-permute-start | bytes 393224 | tf_op jit(solution)/shard_map/ppermute | solution.py:343
  83.1 5.9 %collective-permute-start.36 = (f32[64,512]{1,0:T(8,128)S(1)}, f32[64,512]{1,0:T(8,128)S(1)}, u32[]{:S(2)}, u32[]{:S(2)}) collective-permute-start(f32[64,512]{1,0:T(8,128)S(1)} %collective-permute-done.35.refs_5_), channel_id=1, source_target_pairs={{0,4},{4,0},{1,5},{5,1},{2,6},{6,2},{3,7},{7,3},{8,12},{12,8},{9,1... | collective-permute-start | bytes 393224 | tf_op jit(solution)/shard_map/ppermute | solution.py:343
  (15 other events, 64.2 us)

commit v12 on v8

--- a/solution.py
+++ b/solution.py
@@ -10,8 +10,6 @@
 LEVELS = 4
 BLOCK = 128
 LOSS_ROWS = 8
-LOSS_PART = 4
-GIVE_PARTS = 1
 GELU_C = 0.7978845608028654
 GELU_A = 0.044715
 
@@ -148,6 +146,18 @@
     return pl.ds(pl.multiple_of(wid * (rows // 2), rows // 2), rows // 2)
 
 
+def stacked(parts, extra, out):
+    rows, cols = parts.shape
+    for i in range(cols // BLOCK):
+        out[i * rows : (i + 1) * rows, :] = parts[:, i * BLOCK : (i + 1) * BLOCK]
+    out[-LOSS_ROWS:, :] = extra
+
+
+def unstacked(ref, count):
+    rows = (ref.shape[0] - LOSS_ROWS) // count
+    return jnp.concatenate([ref[i * rows : (i + 1) * rows, :] for i in range(count)], axis=1)
+
+
 def g_pre_kernel(pre_ref, mask, loss, *refs):
     terms, out = refs[:-1], refs[-1]
     mine = half_of(lax.axis_index("wid"), pre_ref.shape[0])
@@ -157,10 +167,7 @@
     bend = jnp.tanh(inner)
     deriv = 0.5 * (1.0 + bend) + 0.5 * pre * (1.0 - bend * bend) * slope
     hit = mask[mine, :] > 0.0
-    rows = pre.shape[0]
-    out[:rows, :] = jnp.where(hit, deriv * total_of([t[...] for t in terms]), 0.0)
-    out[rows:, :] = jnp.zeros_like(out[rows:, :])
-    out[rows:, :BLOCK] = loss[:LOSS_ROWS, :BLOCK]
+    stacked(jnp.where(hit, deriv * total_of([t[...] for t in terms]), 0.0), loss[...], out)
 
 
 def running_parts(act, dict_ref):
@@ -235,7 +242,7 @@
 
 def error_kernel(loss_count, act, dictionary, resid, bias, table, mine, other, *refs):
     before, refs = refs[:loss_count], refs[loss_count:]
-    err_out, keep_out, *give_outs, loss_out = refs
+    err_out, keep_out, give_out, loss_out = refs
     upward = lax.axis_index("wid") == 0
     earlier = jnp.where(upward, mine[...], other[...])
     later = jnp.where(upward, other[...], mine[...])
@@ -257,22 +264,11 @@
         )
         half = gact.shape[0] // 2
         keep_out[:, cols] = jnp.where(upward, gact[:half, :], gact[half:, :])
-        given = jnp.where(upward, gact[half:, :], gact[:half, :])
-        for part, give_out in enumerate(give_outs):
-            size = give_out.shape[0]
-            give_out[:, cols] = given[part * size : (part + 1) * size, :]
-
-
-def spread_kernel(loss, out):
-    out[...] = jnp.zeros_like(out)
-    out[:LOSS_ROWS, :BLOCK] = loss[...]
-
-
-def collect_kernel(keep, *refs):
-    parts, out = refs[:-1], refs[-1]
-    for i, part in enumerate(parts):
-        span = slice(i * part.shape[0], (i + 1) * part.shape[0])
-        out[span, :] = keep[span, :] + part[...]
+        give_out[:, cols] = jnp.where(upward, gact[half:, :], gact[:half, :])
+
+
+def collect_kernel(keep, give, out):
+    out[...] = keep[...] + give[...]
 
 
 def add_kernel(*refs):
@@ -295,12 +291,13 @@
     n, halves = items
     resids, grads, base, out = refs[:n], refs[n:-2], refs[-2], refs[-1]
     half = resids[0].shape[0] // 2
+    count = out.shape[1] // BLOCK
     wid = lax.axis_index("wid")
     spans = [half_of(wid, 2 * half), half_of(1 - wid, 2 * half)]
     resid = jnp.concatenate(
         [resids[q][spans[side], :].astype(jnp.bfloat16) for q, side in halves], axis=0
     )
-    grad = jnp.concatenate([g[:half, :].astype(jnp.bfloat16) for g in grads], axis=0)
+    grad = jnp.concatenate([unstacked(g, count).astype(jnp.bfloat16) for g in grads], axis=0)
     total = base[...] + lax.dot_general(
         resid, grad, (((0,), (0,)), ((), ())), preferred_element_type=jnp.float32
     )
@@ -312,8 +309,7 @@
     early, refs = refs[:n_early], refs[n_early:]
     encode_kernel(items, *refs, out)
     grads = list(early) + list(refs[items[0] : -1])
-    half = refs[0].shape[0] // 2
-    lanes = total_of([g[half:, :BLOCK] for g in grads])
+    lanes = total_of([g[-LOSS_ROWS:, :] for g in grads])
     for m in range(LEVELS):
         loss_out[m] = jnp.sum(lanes[m : m + 1, :]) * scale
 
@@ -373,7 +369,7 @@
     )
     resids = [piece if q == 0 else across(piece, q) for q, piece in enumerate(pieces)]
 
-    order = [0, 3, 1, 2] if n_tok == 4 else list(range(n_tok))
+    order = [0, 1, 3, 2] if n_tok == 4 else list(range(n_tok))
     steps = n_tok + n_lat - 2
     places = list(range(1, n_lat))
     acts, errs, hands, gives, gacts, loss = {}, {}, [], [], [], ()
@@ -440,16 +436,14 @@
             if c < 0:
                 continue
             q = order[c]
-            errs[q], keep, *give, loss_here = call(
+            errs[q], keep, give, loss_here = call(
                 functools.partial(error_kernel, len(loss)),
-                [bf16(count, rows, width), f32(rows // 2, lats)]
-                + [f32(rows // 2 // GIVE_PARTS, lats)] * GIVE_PARTS
-                + [f32(LOSS_ROWS, BLOCK)],
+                [bf16(count, rows, width)] + [f32(rows // 2, lats)] * 2 + [f32(LOSS_ROWS, BLOCK)],
                 (acts[q], dict_here, resids[q], bias_here, table, hands[c][1], hands[c][0], *loss),
                 after=sent if step < steps else (),
             )
             loss = (loss_here,)
-            gives.append((keep, *[swap(g) for g in give]))
+            gives.append((keep, swap(give)))
             ready.append(errs[q])
         stages = [1] if step == steps - 1 else [0, *range(2, n_tok)] if step == steps else []
         for c in stages:
@@ -465,7 +459,7 @@
             waits[step + 1] += ready
         ready_before = ready
 
-    loss, gap = call(spread_kernel, [f32(rows // LOSS_PART, lats)], loss)[0], 1
+    loss, gap = loss[0], 1
     while gap < n_lat:
         other = lax.ppermute(loss, "lat", [(p, p ^ gap) for p in range(n_lat)])
         loss = call(add_kernel, [f32(*loss.shape)], (loss, other))[0]
@@ -478,7 +472,7 @@
     )[0]
     g_pre = call(
         g_pre_kernel,
-        [f32(rows // 2 + LOSS_ROWS, lats)],
+        [f32(rows // 2 * count + LOSS_ROWS, BLOCK)],
         (pre, mask, loss, *gacts),
         after=(decoded,),
     )[0]

time: 87.7 us -> 85.7 us (0.977)
  starting transfers between devices: 60 us -> 56.4 us
  waiting for transfers between devices: 14.7 us -> 16.1 us
    ppermute x12, starting transfers between devices: 26.1 us -> 23.3 us  [body(): got[side].append((lax.ppermute(message, ('lat', 'wid'), pairs), 0))]
    ppermute x2, waiting for transfers between devices: 4.02 us -> 5.91 us  [body(): other = lax.ppermute(loss, 'lat', [(p, p ^ gap) for p in range(n_lat)])]
    ppermute x12, starting transfers between devices: 18 us -> 19.5 us  [across(): return lax.ppermute(array, 'tok', [(t, t ^ q) for t in range(n_tok)])]
    ppermute x2, starting transfers between devices: 2.71 us -> 1.46 us  [body(): other = lax.ppermute(loss, 'lat', [(p, p ^ gap) for p in range(n_lat)])]
    ppermute x14, starting transfers between devices: 13.2 us -> 12.1 us  [swap(): return lax.ppermute(array, 'wid', [(w, w ^ 1) for w in range(n_wid)])]
    pallas_call x49 -> x48, Pallas kernels: 11.5 us -> 11.6 us  [call(): pl.pallas_call(run, out_shape=outs, in_specs=list(specs or [VMEM] * len(a...]
  transfers between devices with their start and end apart: 40 -> 40, of which waited for: 12 -> 13; matrix products, arithmetic and copies ran while one was open for 0% -> 0% of each run, Pallas kernels for 8% -> 9%
where the time goes in v12:
time: 85.7 us; the launch traced here: 85.3 us
  starting transfers between devices  56.4 us (66%)
  waiting for transfers between devices  16.1 us (19%)
  Pallas kernels  11.6 us (14%)
  between operations  1.23 us (1%)
    ppermute x12, starting transfers between devices, body(): got[side].append((lax.ppermute(message, ('lat', 'wid'), pairs), 0))  23.3 us
    ppermute x12, starting transfers between devices, across(): return lax.ppermute(array, 'tok', [(t, t ^ q) for t in range(n_tok)])  19.5 us
    ppermute x14, starting transfers between devices, swap(): return lax.ppermute(array, 'wid', [(w, w ^ 1) for w in range(n_wid)])  12.1 us
    pallas_call x48, Pallas kernels, call(): pl.pallas_call(run, out_shape=outs, in_specs=list(specs or [VMEM] * len(a...  11.6 us
    ppermute x2, waiting for transfers between devices, body(): other = lax.ppermute(loss, 'lat', [(p, p ^ gap) for p in range(n_lat)])  5.91 us
    ppermute x12, waiting for transfers between devices, across(): return lax.ppermute(array, 'tok', [(t, t ^ q) for t in range(n_tok)])  5.32 us
    ppermute x14, waiting for transfers between devices, swap(): return lax.ppermute(array, 'wid', [(w, w ^ 1) for w in range(n_wid)])  3.23 us
  transfers between devices with their start and end apart: 40, of which 13 were waited for; matrix products, arithmetic and copies ran while one was open for 0% of the time, Pallas kernels for 9%

profile of v12, /device:TPU:0, one launch (start us, length us, event | category | flops | bytes accessed | tf_op | source)
XLA Modules:
  0.0 85.3 jit_solution(15732146612273359265)
XLA Ops:
  0.7 2.9 %shard_map.77 = (f32[128,512]{1,0:T(8,128)S(1)}, bf16[512,512]{1,0:T(8,128)(2,1)S(1)}) custom-call(bf16[128,2048]{1,0:T(8,128)(2,1)} %refs_0_.3, bf16[512,2048]{1,0:T(8,128)(2,1)} %refs_1_.1), custom_call_target="tpu_custom_call" | custom-call | bytes 1024 | tf_op jit(solution)/shard_map/pallas_call | solution.py:36
  4.1 1.2 %collective-permute-done.refs_2_.refs_1_ = f32[128,512]{1,0:T(8,128)S(1)} collective-permute-done((f32[128,512]{1,0:T(8,128)S(1)}, f32[128,512]{1,0:T(8,128)S(1)}, u32[]{:S(2)}, u32[]{:S(2)}) %collective-permute-start) | collective-permute-done | bytes 262176 | tf_op jit(solution)/shard_map/ppermute | solution.py:336
  6.1 2.7 %collective-permute-start.4 = (f32[128,512]{1,0:T(8,128)S(1)}, f32[128,512]{1,0:T(8,128)S(1)}, u32[]{:S(2)}, u32[]{:S(2)}) collective-permute-start(f32[128,512]{1,0:T(8,128)S(1)} %get-tuple-element.37.refs_0_.refs_2_), channel_id=1, source_target_pairs={{0,1},{1,0},{2,3},{3,2},{4,5},{5,4},{6,7},{7,6},{8,9},{9,8},{10,11... | collective-permute-start | bytes 786440 | tf_op jit(solution)/shard_map/ppermute | solution.py:333
  9.1 3.5 %collective-permute-start.7 = (f32[128,512]{1,0:T(8,128)S(1)}, f32[128,512]{1,0:T(8,128)S(1)}, u32[]{:S(2)}, u32[]{:S(2)}) collective-permute-start(f32[128,512]{1,0:T(8,128)S(1)} %shard_map.87.refs_2_.refs_3_), channel_id=1, source_target_pairs={{0,8},{28,20},{1,9},{29,21},{2,10},{30,22},{3,11},{31,23}} | collective-permute-start | bytes 786440 | tf_op jit(solution)/shard_map/ppermute | solution.py:396
  12.9 1.3 %collective-permute-start.3 = (f32[128,512]{1,0:T(8,128)S(1)}, f32[128,512]{1,0:T(8,128)S(1)}, u32[]{:S(2)}, u32[]{:S(2)}) collective-permute-start(f32[128,512]{1,0:T(8,128)S(1)} %shard_map.81.refs_1_.refs_2_.refs_3_), channel_id=1, source_target_pairs={{0,8},{28,20},{1,9},{29,21},{2,10},{30,22},{3,11},{31,23}} | collective-permute-start | bytes 786440 | tf_op jit(solution)/shard_map/ppermute | solution.py:396
  14.2 1.6 %collective-permute-start.6 = (f32[128,512]{1,0:T(8,128)S(1)}, f32[128,512]{1,0:T(8,128)S(1)}, u32[]{:S(2)}, u32[]{:S(2)}) collective-permute-start(f32[128,512]{1,0:T(8,128)S(1)} %get-tuple-element.37.refs_0_.refs_2_), channel_id=1, source_target_pairs={{0,3},{1,2},{2,1},{3,0},{4,7},{5,6},{6,5},{7,4},{8,11},{9,10},{10,... | collective-permute-start | bytes 786440 | tf_op jit(solution)/shard_map/ppermute | solution.py:333
  16.5 4.4 %collective-permute-start.8 = (f32[128,512]{1,0:T(8,128)S(1)}, f32[128,512]{1,0:T(8,128)S(1)}, u32[]{:S(2)}, u32[]{:S(2)}) collective-permute-start(f32[128,512]{1,0:T(8,128)S(1)} %shard_map.89), channel_id=1, source_target_pairs={{0,8},{28,20},{8,16},{20,12},{1,9},{29,21},{9,17},{21,13},{2,10},{... | collective-permute-start | bytes 786440 | tf_op jit(solution)/shard_map/ppermute | solution.py:407
  21.3 2.5 %collective-permute-start.5 = (f32[128,512]{1,0:T(8,128)S(1)}, f32[128,512]{1,0:T(8,128)S(1)}, u32[]{:S(2)}, u32[]{:S(2)}) collective-permute-start(f32[128,512]{1,0:T(8,128)S(1)} %shard_map.84.refs_1_.refs_4_), channel_id=1, source_target_pairs={{0,8},{28,20},{8,16},{20,12},{1,9},{29,21},{9,17},{21,13},{2,10},{... | collective-permute-start | bytes 786440 | tf_op jit(solution)/shard_map/ppermute | solution.py:407
  23.7 2.0 %collective-permute-start.1 = (f32[128,512]{1,0:T(8,128)S(1)}, f32[128,512]{1,0:T(8,128)S(1)}, u32[]{:S(2)}, u32[]{:S(2)}) collective-permute-start(f32[128,512]{1,0:T(8,128)S(1)} %get-tuple-element.37.refs_0_.refs_2_), channel_id=1, source_target_pairs={{0,2},{1,3},{2,0},{3,1},{4,6},{5,7},{6,4},{7,5},{8,10},{9,11},{10,... | collective-permute-start | bytes 786440 | tf_op jit(solution)/shard_map/ppermute | solution.py:333
  25.8 1.6 %collective-permute-start.11 = (f32[128,512]{1,0:T(8,128)S(1)}, f32[128,512]{1,0:T(8,128)S(1)}, u32[]{:S(2)}, u32[]{:S(2)}) collective-permute-start(f32[128,512]{1,0:T(8,128)S(1)} %get-tuple-element.41), channel_id=1, source_target_pairs={{0,1},{1,0},{2,3},{3,2},{4,5},{5,4},{6,7},{7,6},{8,9},{9,8},{10,11... | collective-permute-start | bytes 786440 | tf_op jit(solution)/shard_map/ppermute | solution.py:333
  27.8 1.9 %collective-permute-start.10 = (f32[128,512]{1,0:T(8,128)S(1)}, f32[128,512]{1,0:T(8,128)S(1)}, u32[]{:S(2)}, u32[]{:S(2)}) collective-permute-start(f32[128,512]{1,0:T(8,128)S(1)} %shard_map.91.refs_4_), channel_id=1, source_target_pairs={{0,8},{28,20},{8,16},{20,12},{16,24},{12,4},{1,9},{29,21},{9,17},{... | collective-permute-start | bytes 786440 | tf_op jit(solution)/shard_map/ppermute | solution.py:407
  30.1 1.9 %collective-permute-start.13 = (f32[128,512]{1,0:T(8,128)S(1)}, f32[128,512]{1,0:T(8,128)S(1)}, u32[]{:S(2)}, u32[]{:S(2)}) collective-permute-start(f32[128,512]{1,0:T(8,128)S(1)} %shard_map.92.refs_1_.refs_4_), channel_id=1, source_target_pairs={{0,8},{28,20},{8,16},{20,12},{16,24},{12,4},{1,9},{29,21},{9,17},{... | collective-permute-start | bytes 786440 | tf_op jit(solution)/shard_map/ppermute | solution.py:407
  32.0 3.0 %collective-permute-start.14 = (f32[128,512]{1,0:T(8,128)S(1)}, f32[128,512]{1,0:T(8,128)S(1)}, u32[]{:S(2)}, u32[]{:S(2)}) collective-permute-start(f32[128,512]{1,0:T(8,128)S(1)} %get-tuple-element.42), channel_id=1, source_target_pairs={{0,3},{1,2},{2,1},{3,0},{4,7},{5,6},{6,5},{7,4},{8,11},{9,10},{10,... | collective-permute-start | bytes 786440 | tf_op jit(solution)/shard_map/ppermute | solution.py:333
  35.4 2.6 %collective-permute-start.12 = (f32[128,512]{1,0:T(8,128)S(1)}, f32[128,512]{1,0:T(8,128)S(1)}, u32[]{:S(2)}, u32[]{:S(2)}) collective-permute-start(f32[128,512]{1,0:T(8,128)S(1)} %shard_map.96.refs_4_), channel_id=1, source_target_pairs={{0,8},{28,20},{8,16},{20,12},{16,24},{12,4},{1,9},{29,21},{9,17},{... | collective-permute-start | bytes 786440 | tf_op jit(solution)/shard_map/ppermute | solution.py:407
  38.4 2.4 %collective-permute-start.16 = (f32[128,512]{1,0:T(8,128)S(1)}, f32[128,512]{1,0:T(8,128)S(1)}, u32[]{:S(2)}, u32[]{:S(2)}) collective-permute-start(f32[128,512]{1,0:T(8,128)S(1)} %shard_map.98.refs_3_), channel_id=1, source_target_pairs={{0,8},{28,20},{8,16},{20,12},{16,24},{12,4},{1,9},{29,21},{9,17},{... | collective-permute-start | bytes 786440 | tf_op jit(solution)/shard_map/ppermute | solution.py:407
  40.8 1.5 %collective-permute-start.9 = (f32[128,512]{1,0:T(8,128)S(1)}, f32[128,512]{1,0:T(8,128)S(1)}, u32[]{:S(2)}, u32[]{:S(2)}) collective-permute-start(f32[128,512]{1,0:T(8,128)S(1)} %get-tuple-element.39), channel_id=1, source_target_pairs={{0,2},{1,3},{2,0},{3,1},{4,6},{5,7},{6,4},{7,5},{8,10},{9,11},{10,... | collective-permute-start | bytes 786440 | tf_op jit(solution)/shard_map/ppermute | solution.py:333
  43.3 1.4 %collective-permute-done.16.refs_0_.refs_2_.refs_1_ = f32[128,512]{1,0:T(8,128)S(1)} collective-permute-done((f32[128,512]{1,0:T(8,128)S(1)}, f32[128,512]{1,0:T(8,128)S(1)}, u32[]{:S(2)}, u32[]{:S(2)}) %collective-permute-start.16) | collective-permute-done | bytes 262176 | tf_op jit(solution)/shard_map/ppermute | solution.py:407
  49.4 5.7 %collective-permute-start.21 = (f32[64,512]{1,0:T(8,128)S(1)}, f32[64,512]{1,0:T(8,128)S(1)}, u32[]{:S(2)}, u32[]{:S(2)}) collective-permute-start(f32[64,512]{1,0:T(8,128)S(1)} %get-tuple-element.48), channel_id=1, source_target_pairs={{0,4},{4,0},{1,5},{5,1},{2,6},{6,2},{3,7},{7,3},{8,12},{12,8},{9,1... | collective-permute-start | bytes 393224 | tf_op jit(solution)/shard_map/ppermute | solution.py:336
  55.2 0.8 collective-permute-done.21.refs_1_
  56.2 4.0 %collective-permute-start.23 = (f32[128,512]{1,0:T(8,128)S(1)}, f32[128,512]{1,0:T(8,128)S(1)}, u32[]{:S(2)}, u32[]{:S(2)}) collective-permute-start(f32[128,512]{1,0:T(8,128)S(1)} %shard_map.113), channel_id=1, source_target_pairs={{0,4},{4,0},{1,5},{5,1},{2,6},{6,2},{3,7},{7,3},{8,12},{12,8},{9,1... | collective-permute-start | bytes 786440 | tf_op jit(solution)/shard_map/ppermute | solution.py:336
  62.6 1.5 %collective-permute-start.27 = (f32[64,512]{1,0:T(8,128)S(1)}, f32[64,512]{1,0:T(8,128)S(1)}, u32[]{:S(2)}, u32[]{:S(2)}) collective-permute-start(f32[64,512]{1,0:T(8,128)S(1)} %shard_map.111.refs_6_), channel_id=1, source_target_pairs={{0,1},{1,0},{2,3},{3,2},{4,5},{5,4},{6,7},{7,6},{8,9},{9,8},{10,11... | collective-permute-start | bytes 393224 | tf_op jit(solution)/shard_map/ppermute | solution.py:333
  64.7 1.5 %collective-permute-start.32 = (f32[64,512]{1,0:T(8,128)S(1)}, f32[64,512]{1,0:T(8,128)S(1)}, u32[]{:S(2)}, u32[]{:S(2)}) collective-permute-start(f32[64,512]{1,0:T(8,128)S(1)} %shard_map.120), channel_id=1, source_target_pairs={{0,2},{1,3},{2,0},{3,1},{4,6},{5,7},{6,4},{7,5},{8,10},{9,11},{10,... | collective-permute-start | bytes 393224 | tf_op jit(solution)/shard_map/ppermute | solution.py:333
  66.3 3.6 %collective-permute-done.25.refs_1_ = f32[8,128]{1,0:T(8,128)S(1)} collective-permute-done((f32[8,128]{1,0:T(8,128)S(1)}, f32[8,128]{1,0:T(8,128)S(1)}, u32[]{:S(2)}, u32[]{:S(2)}) %collective-permute-start.25) | collective-permute-done | bytes 4128 | tf_op jit(solution)/shard_map/ppermute | solution.py:464
  69.9 1.5 %collective-permute-start.26 = (f32[8,128]{1,0:T(8,128)S(1)}, f32[8,128]{1,0:T(8,128)S(1)}, u32[]{:S(2)}, u32[]{:S(2)}) collective-permute-start(f32[8,128]{1,0:T(8,128)S(1)} %shard_map.116.refs_0_), channel_id=1, source_target_pairs={{0,16},{8,24},{16,0},{24,8},{1,17},{9,25},{17,1},{25,9},{2,18},{10... | collective-permute-start | bytes 12296 | tf_op jit(solution)/shard_map/ppermute | solution.py:464
  71.4 0.8 shard_map.121.refs_7_.refs_11_
  72.1 2.3 %collective-permute-done.26.refs_1_ = f32[8,128]{1,0:T(8,128)S(1)} collective-permute-done((f32[8,128]{1,0:T(8,128)S(1)}, f32[8,128]{1,0:T(8,128)S(1)}, u32[]{:S(2)}, u32[]{:S(2)}) %collective-permute-start.26) | collective-permute-done | bytes 4128 | tf_op jit(solution)/shard_map/ppermute | solution.py:464
  74.6 1.5 %collective-permute-start.35 = (f32[264,128]{1,0:T(8,128)S(1)}, f32[264,128]{1,0:T(8,128)S(1)}, u32[]{:S(2)}, u32[]{:S(2)}) collective-permute-start(f32[264,128]{1,0:T(8,128)S(1)} %shard_map.122.refs_4_.refs_0_), channel_id=1, source_target_pairs={{0,3},{1,2},{2,1},{3,0},{4,7},{5,6},{6,5},{7,4},{8,11},{9,10},{10,... | collective-permute-start | bytes 405512 | tf_op jit(solution)/shard_map/ppermute | solution.py:333
  76.1 1.5 %collective-permute-start.34 = (f32[264,128]{1,0:T(8,128)S(1)}, f32[264,128]{1,0:T(8,128)S(1)}, u32[]{:S(2)}, u32[]{:S(2)}) collective-permute-start(f32[264,128]{1,0:T(8,128)S(1)} %shard_map.122.refs_4_.refs_0_), channel_id=1, source_target_pairs={{0,2},{1,3},{2,0},{3,1},{4,6},{5,7},{6,4},{7,5},{8,10},{9,11},{10,... | collective-permute-start | bytes 405512 | tf_op jit(solution)/shard_map/ppermute | solution.py:333
  78.2 2.9 %collective-permute-done.35.refs_7_.refs_3_ = f32[264,128]{1,0:T(8,128)S(1)} collective-permute-done((f32[264,128]{1,0:T(8,128)S(1)}, f32[264,128]{1,0:T(8,128)S(1)}, u32[]{:S(2)}, u32[]{:S(2)}) %collective-permute-start.35) | collective-permute-done | bytes 135200 | tf_op jit(solution)/shard_map/ppermute | solution.py:333
  81.1 1.2 %collective-permute-done.34.refs_6_.refs_2_ = f32[264,128]{1,0:T(8,128)S(1)} collective-permute-done((f32[264,128]{1,0:T(8,128)S(1)}, f32[264,128]{1,0:T(8,128)S(1)}, u32[]{:S(2)}, u32[]{:S(2)}) %collective-permute-start.34) | collective-permute-done | bytes 135200 | tf_op jit(solution)/shard_map/ppermute | solution.py:333
  82.8 0.8 collective-permute-done.37.refs_9_.refs_5_
  84.2 1.1 %shard_map.124 = (bf16[512,512]{1,0:T(8,128)(2,1)}, f32[4]{0:T(128)}) custom-call(f32[264,128]{1,0:T(8,128)S(1)} %shard_map.122.refs_4_.refs_0_, f32[264,128]{1,0:T(8,128)S(1)} %collective-permute-done.33.refs_5_.refs_1_, f32[264,128]{1,0:T(8,128)S(1)} %collective-permute-done.34.refs_6_.refs_2_, f32[264,128]{1,0:T(8,128)S(1)} %collective-permute-done.35.refs_7_.refs_3_, ...), custom_call_target="tpu_custom_call" | custom-call | bytes 1024 | tf_op jit(solution)/shard_map/pallas_call | solution.py:36
  (106 shorter events, 14.9 us)
Async XLA Ops:
  5.4 7.2 %collective-permute-start.2 = (f32[512,512]{1,0:T(8,128)S(1)}, f32[512,512]{1,0:T(8,128)S(1)}, u32[]{:S(2)}, u32[]{:S(2)}) collective-permute-start(f32[512,512]{1,0:T(8,128)S(1)} %get-tuple-element.34.refs_4_), channel_id=1, source_target_pairs={{0,4},{4,0},{1,5},{5,1},{2,6},{6,2},{3,7},{7,3},{8,12},{12,8},{9,1... | collective-permute-start | bytes 3145736 | tf_op jit(solution)/shard_map/ppermute | solution.py:336
  6.1 9.8 %collective-permute-start.4 = (f32[128,512]{1,0:T(8,128)S(1)}, f32[128,512]{1,0:T(8,128)S(1)}, u32[]{:S(2)}, u32[]{:S(2)}) collective-permute-start(f32[128,512]{1,0:T(8,128)S(1)} %get-tuple-element.37.refs_0_.refs_2_), channel_id=1, source_target_pairs={{0,1},{1,0},{2,3},{3,2},{4,5},{5,4},{6,7},{7,6},{8,9},{9,8},{10,11... | collective-permute-start | bytes 786440 | tf_op jit(solution)/shard_map/ppermute | solution.py:333
  9.1 7.4 %collective-permute-start.7 = (f32[128,512]{1,0:T(8,128)S(1)}, f32[128,512]{1,0:T(8,128)S(1)}, u32[]{:S(2)}, u32[]{:S(2)}) collective-permute-start(f32[128,512]{1,0:T(8,128)S(1)} %shard_map.87.refs_2_.refs_3_), channel_id=1, source_target_pairs={{0,8},{28,20},{1,9},{29,21},{2,10},{30,22},{3,11},{31,23}} | collective-permute-start | bytes 786440 | tf_op jit(solution)/shard_map/ppermute | solution.py:396
  12.9 8.3 %collective-permute-start.3 = (f32[128,512]{1,0:T(8,128)S(1)}, f32[128,512]{1,0:T(8,128)S(1)}, u32[]{:S(2)}, u32[]{:S(2)}) collective-permute-start(f32[128,512]{1,0:T(8,128)S(1)} %shard_map.81.refs_1_.refs_2_.refs_3_), channel_id=1, source_target_pairs={{0,8},{28,20},{1,9},{29,21},{2,10},{30,22},{3,11},{31,23}} | collective-permute-start | bytes 786440 | tf_op jit(solution)/shard_map/ppermute | solution.py:396
  14.2 13.2 %collective-permute-start.6 = (f32[128,512]{1,0:T(8,128)S(1)}, f32[128,512]{1,0:T(8,128)S(1)}, u32[]{:S(2)}, u32[]{:S(2)}) collective-permute-start(f32[128,512]{1,0:T(8,128)S(1)} %get-tuple-element.37.refs_0_.refs_2_), channel_id=1, source_target_pairs={{0,3},{1,2},{2,1},{3,0},{4,7},{5,6},{6,5},{7,4},{8,11},{9,10},{10,... | collective-permute-start | bytes 786440 | tf_op jit(solution)/shard_map/ppermute | solution.py:333
  16.5 11.2 %collective-permute-start.8 = (f32[128,512]{1,0:T(8,128)S(1)}, f32[128,512]{1,0:T(8,128)S(1)}, u32[]{:S(2)}, u32[]{:S(2)}) collective-permute-start(f32[128,512]{1,0:T(8,128)S(1)} %shard_map.89), channel_id=1, source_target_pairs={{0,8},{28,20},{8,16},{20,12},{1,9},{29,21},{9,17},{21,13},{2,10},{... | collective-permute-start | bytes 786440 | tf_op jit(solution)/shard_map/ppermute | solution.py:407
  21.3 8.8 %collective-permute-start.5 = (f32[128,512]{1,0:T(8,128)S(1)}, f32[128,512]{1,0:T(8,128)S(1)}, u32[]{:S(2)}, u32[]{:S(2)}) collective-permute-start(f32[128,512]{1,0:T(8,128)S(1)} %shard_map.84.refs_1_.refs_4_), channel_id=1, source_target_pairs={{0,8},{28,20},{8,16},{20,12},{1,9},{29,21},{9,17},{21,13},{2,10},{... | collective-permute-start | bytes 786440 | tf_op jit(solution)/shard_map/ppermute | solution.py:407
  23.7 11.3 %collective-permute-start.1 = (f32[128,512]{1,0:T(8,128)S(1)}, f32[128,512]{1,0:T(8,128)S(1)}, u32[]{:S(2)}, u32[]{:S(2)}) collective-permute-start(f32[128,512]{1,0:T(8,128)S(1)} %get-tuple-element.37.refs_0_.refs_2_), channel_id=1, source_target_pairs={{0,2},{1,3},{2,0},{3,1},{4,6},{5,7},{6,4},{7,5},{8,10},{9,11},{10,... | collective-permute-start | bytes 786440 | tf_op jit(solution)/shard_map/ppermute | solution.py:333
  25.8 9.5 %collective-permute-start.11 = (f32[128,512]{1,0:T(8,128)S(1)}, f32[128,512]{1,0:T(8,128)S(1)}, u32[]{:S(2)}, u32[]{:S(2)}) collective-permute-start(f32[128,512]{1,0:T(8,128)S(1)} %get-tuple-element.41), channel_id=1, source_target_pairs={{0,1},{1,0},{2,3},{3,2},{4,5},{5,4},{6,7},{7,6},{8,9},{9,8},{10,11... | collective-permute-start | bytes 786440 | tf_op jit(solution)/shard_map/ppermute | solution.py:333
  27.8 7.6 %collective-permute-start.10 = (f32[128,512]{1,0:T(8,128)S(1)}, f32[128,512]{1,0:T(8,128)S(1)}, u32[]{:S(2)}, u32[]{:S(2)}) collective-permute-start(f32[128,512]{1,0:T(8,128)S(1)} %shard_map.91.refs_4_), channel_id=1, source_target_pairs={{0,8},{28,20},{8,16},{20,12},{16,24},{12,4},{1,9},{29,21},{9,17},{... | collective-permute-start | bytes 786440 | tf_op jit(solution)/shard_map/ppermute | solution.py:407
  30.1 8.3 %collective-permute-start.13 = (f32[128,512]{1,0:T(8,128)S(1)}, f32[128,512]{1,0:T(8,128)S(1)}, u32[]{:S(2)}, u32[]{:S(2)}) collective-permute-start(f32[128,512]{1,0:T(8,128)S(1)} %shard_map.92.refs_1_.refs_4_), channel_id=1, source_target_pairs={{0,8},{28,20},{8,16},{20,12},{16,24},{12,4},{1,9},{29,21},{9,17},{... | collective-permute-start | bytes 786440 | tf_op jit(solution)/shard_map/ppermute | solution.py:407
  32.0 10.5 %collective-permute-start.14 = (f32[128,512]{1,0:T(8,128)S(1)}, f32[128,512]{1,0:T(8,128)S(1)}, u32[]{:S(2)}, u32[]{:S(2)}) collective-permute-start(f32[128,512]{1,0:T(8,128)S(1)} %get-tuple-element.42), channel_id=1, source_target_pairs={{0,3},{1,2},{2,1},{3,0},{4,7},{5,6},{6,5},{7,4},{8,11},{9,10},{10,... | collective-permute-start | bytes 786440 | tf_op jit(solution)/shard_map/ppermute | solution.py:333
  35.4 7.2 %collective-permute-start.12 = (f32[128,512]{1,0:T(8,128)S(1)}, f32[128,512]{1,0:T(8,128)S(1)}, u32[]{:S(2)}, u32[]{:S(2)}) collective-permute-start(f32[128,512]{1,0:T(8,128)S(1)} %shard_map.96.refs_4_), channel_id=1, source_target_pairs={{0,8},{28,20},{8,16},{20,12},{16,24},{12,4},{1,9},{29,21},{9,17},{... | collective-permute-start | bytes 786440 | tf_op jit(solution)/shard_map/ppermute | solution.py:407
  38.4 6.3 %collective-permute-start.16 = (f32[128,512]{1,0:T(8,128)S(1)}, f32[128,512]{1,0:T(8,128)S(1)}, u32[]{:S(2)}, u32[]{:S(2)}) collective-permute-start(f32[128,512]{1,0:T(8,128)S(1)} %shard_map.98.refs_3_), channel_id=1, source_target_pairs={{0,8},{28,20},{8,16},{20,12},{16,24},{12,4},{1,9},{29,21},{9,17},{... | collective-permute-start | bytes 786440 | tf_op jit(solution)/shard_map/ppermute | solution.py:407
  40.8 6.4 %collective-permute-start.9 = (f32[128,512]{1,0:T(8,128)S(1)}, f32[128,512]{1,0:T(8,128)S(1)}, u32[]{:S(2)}, u32[]{:S(2)}) collective-permute-start(f32[128,512]{1,0:T(8,128)S(1)} %get-tuple-element.39), channel_id=1, source_target_pairs={{0,2},{1,3},{2,0},{3,1},{4,6},{5,7},{6,4},{7,5},{8,10},{9,11},{10,... | collective-permute-start | bytes 786440 | tf_op jit(solution)/shard_map/ppermute | solution.py:333
  42.4 3.5 %collective-permute-start.17 = (f32[128,512]{1,0:T(8,128)S(1)}, f32[128,512]{1,0:T(8,128)S(1)}, u32[]{:S(2)}, u32[]{:S(2)}) collective-permute-start(f32[128,512]{1,0:T(8,128)S(1)} %shard_map.99.refs_5_), channel_id=1, source_target_pairs={{0,4},{4,0},{1,5},{5,1},{2,6},{6,2},{3,7},{7,3},{8,12},{12,8},{9,1... | collective-permute-start | bytes 786440 | tf_op jit(solution)/shard_map/ppermute | solution.py:336
  42.6 4.7 %collective-permute-start.15 = (f32[128,512]{1,0:T(8,128)S(1)}, f32[128,512]{1,0:T(8,128)S(1)}, u32[]{:S(2)}, u32[]{:S(2)}) collective-permute-start(f32[128,512]{1,0:T(8,128)S(1)} %shard_map.101.refs_3_), channel_id=1, source_target_pairs={{8,16},{20,12},{16,24},{12,4},{9,17},{21,13},{17,25},{13,5},{10,18... | collective-permute-start | bytes 786440 | tf_op jit(solution)/shard_map/ppermute | solution.py:407
  47.3 8.8 %collective-permute-start.18 = (f32[128,512]{1,0:T(8,128)S(1)}, f32[128,512]{1,0:T(8,128)S(1)}, u32[]{:S(2)}, u32[]{:S(2)}) collective-permute-start(f32[128,512]{1,0:T(8,128)S(1)} %shard_map.106.refs_2_), channel_id=1, source_target_pairs={{16,24},{12,4},{17,25},{13,5},{18,26},{14,6},{19,27},{15,7}} | collective-permute-start | bytes 786440 | tf_op jit(solution)/shard_map/ppermute | solution.py:407
  48.0 8.1 %collective-permute-start.22 = (f32[128,512]{1,0:T(8,128)S(1)}, f32[128,512]{1,0:T(8,128)S(1)}, u32[]{:S(2)}, u32[]{:S(2)}) collective-permute-start(f32[128,512]{1,0:T(8,128)S(1)} %shard_map.107.refs_3_.refs_8_.refs_2_), channel_id=1, source_target_pairs={{16,24},{12,4},{17,25},{13,5},{18,26},{14,6},{19,27},{15,7}} | collective-permute-start | bytes 786440 | tf_op jit(solution)/shard_map/ppermute | solution.py:407
  49.4 6.7 %collective-permute-start.21 = (f32[64,512]{1,0:T(8,128)S(1)}, f32[64,512]{1,0:T(8,128)S(1)}, u32[]{:S(2)}, u32[]{:S(2)}) collective-permute-start(f32[64,512]{1,0:T(8,128)S(1)} %get-tuple-element.48), channel_id=1, source_target_pairs={{0,4},{4,0},{1,5},{5,1},{2,6},{6,2},{3,7},{7,3},{8,12},{12,8},{9,1... | collective-permute-start | bytes 393224 | tf_op jit(solution)/shard_map/ppermute | solution.py:336
  55.1 5.1 %collective-permute-start.24 = (f32[128,512]{1,0:T(8,128)S(1)}, f32[128,512]{1,0:T(8,128)S(1)}, u32[]{:S(2)}, u32[]{:S(2)}) collective-permute-start(f32[128,512]{1,0:T(8,128)S(1)} %shard_map.108.refs_3_), channel_id=1, source_target_pairs={{0,4},{4,0},{1,5},{5,1},{2,6},{6,2},{3,7},{7,3},{8,12},{12,8},{9,1... | collective-permute-start | bytes 786440 | tf_op jit(solution)/shard_map/ppermute | solution.py:336
  56.2 5.2 %collective-permute-start.23 = (f32[128,512]{1,0:T(8,128)S(1)}, f32[128,512]{1,0:T(8,128)S(1)}, u32[]{:S(2)}, u32[]{:S(2)}) collective-permute-start(f32[128,512]{1,0:T(8,128)S(1)} %shard_map.113), channel_id=1, source_target_pairs={{0,4},{4,0},{1,5},{5,1},{2,6},{6,2},{3,7},{7,3},{8,12},{12,8},{9,1... | collective-permute-start | bytes 786440 | tf_op jit(solution)/shard_map/ppermute | solution.py:336
  62.5 8.9 %collective-permute-start.28 = (f32[64,512]{1,0:T(8,128)S(1)}, f32[64,512]{1,0:T(8,128)S(1)}, u32[]{:S(2)}, u32[]{:S(2)}) collective-permute-start(f32[64,512]{1,0:T(8,128)S(1)} %get-tuple-element.53), channel_id=1, source_target_pairs={{0,4},{4,0},{1,5},{5,1},{2,6},{6,2},{3,7},{7,3},{8,12},{12,8},{9,1... | collective-permute-start | bytes 393224 | tf_op jit(solution)/shard_map/ppermute | solution.py:336
  62.6 11.8 %collective-permute-start.27 = (f32[64,512]{1,0:T(8,128)S(1)}, f32[64,512]{1,0:T(8,128)S(1)}, u32[]{:S(2)}, u32[]{:S(2)}) collective-permute-start(f32[64,512]{1,0:T(8,128)S(1)} %shard_map.111.refs_6_), channel_id=1, source_target_pairs={{0,1},{1,0},{2,3},{3,2},{4,5},{5,4},{6,7},{7,6},{8,9},{9,8},{10,11... | collective-permute-start | bytes 393224 | tf_op jit(solution)/shard_map/ppermute | solution.py:333
  64.1 10.3 %collective-permute-start.30 = (f32[64,512]{1,0:T(8,128)S(1)}, f32[64,512]{1,0:T(8,128)S(1)}, u32[]{:S(2)}, u32[]{:S(2)}) collective-permute-start(f32[64,512]{1,0:T(8,128)S(1)} %shard_map.119), channel_id=1, source_target_pairs={{0,3},{1,2},{2,1},{3,0},{4,7},{5,6},{6,5},{7,4},{8,11},{9,10},{10,... | collective-permute-start | bytes 393224 | tf_op jit(solution)/shard_map/ppermute | solution.py:333
  64.7 9.7 %collective-permute-start.32 = (f32[64,512]{1,0:T(8,128)S(1)}, f32[64,512]{1,0:T(8,128)S(1)}, u32[]{:S(2)}, u32[]{:S(2)}) collective-permute-start(f32[64,512]{1,0:T(8,128)S(1)} %shard_map.120), channel_id=1, source_target_pairs={{0,2},{1,3},{2,0},{3,1},{4,6},{5,7},{6,4},{7,5},{8,10},{9,11},{10,... | collective-permute-start | bytes 393224 | tf_op jit(solution)/shard_map/ppermute | solution.py:333
  66.3 3.6 %collective-permute-start.25 = (f32[8,128]{1,0:T(8,128)S(1)}, f32[8,128]{1,0:T(8,128)S(1)}, u32[]{:S(2)}, u32[]{:S(2)}) collective-permute-start(f32[8,128]{1,0:T(8,128)S(1)} %get-tuple-element.51.refs_0_), channel_id=1, source_target_pairs={{0,8},{8,0},{16,24},{24,16},{1,9},{9,1},{17,25},{25,17},{2,10},{10... | collective-permute-start | bytes 12296 | tf_op jit(solution)/shard_map/ppermute | solution.py:464
  69.9 4.5 %collective-permute-start.26 = (f32[8,128]{1,0:T(8,128)S(1)}, f32[8,128]{1,0:T(8,128)S(1)}, u32[]{:S(2)}, u32[]{:S(2)}) collective-permute-start(f32[8,128]{1,0:T(8,128)S(1)} %shard_map.116.refs_0_), channel_id=1, source_target_pairs={{0,16},{8,24},{16,0},{24,8},{1,17},{9,25},{17,1},{25,9},{2,18},{10... | collective-permute-start | bytes 12296 | tf_op jit(solution)/shard_map/ppermute | solution.py:464
  74.6 6.5 %collective-permute-start.35 = (f32[264,128]{1,0:T(8,128)S(1)}, f32[264,128]{1,0:T(8,128)S(1)}, u32[]{:S(2)}, u32[]{:S(2)}) collective-permute-start(f32[264,128]{1,0:T(8,128)S(1)} %shard_map.122.refs_4_.refs_0_), channel_id=1, source_target_pairs={{0,3},{1,2},{2,1},{3,0},{4,7},{5,6},{6,5},{7,4},{8,11},{9,10},{10,... | collective-permute-start | bytes 405512 | tf_op jit(solution)/shard_map/ppermute | solution.py:333
  76.1 6.2 %collective-permute-start.34 = (f32[264,128]{1,0:T(8,128)S(1)}, f32[264,128]{1,0:T(8,128)S(1)}, u32[]{:S(2)}, u32[]{:S(2)}) collective-permute-start(f32[264,128]{1,0:T(8,128)S(1)} %shard_map.122.refs_4_.refs_0_), channel_id=1, source_target_pairs={{0,2},{1,3},{2,0},{3,1},{4,6},{5,7},{6,4},{7,5},{8,10},{9,11},{10,... | collective-permute-start | bytes 405512 | tf_op jit(solution)/shard_map/ppermute | solution.py:333
  77.6 5.0 %collective-permute-start.33 = (f32[264,128]{1,0:T(8,128)S(1)}, f32[264,128]{1,0:T(8,128)S(1)}, u32[]{:S(2)}, u32[]{:S(2)}) collective-permute-start(f32[264,128]{1,0:T(8,128)S(1)} %shard_map.122.refs_4_.refs_0_), channel_id=1, source_target_pairs={{0,1},{1,0},{2,3},{3,2},{4,5},{5,4},{6,7},{7,6},{8,9},{9,8},{10,11... | collective-permute-start | bytes 405512 | tf_op jit(solution)/shard_map/ppermute | solution.py:333
  78.1 4.6 %collective-permute-start.36 = (f32[264,128]{1,0:T(8,128)S(1)}, f32[264,128]{1,0:T(8,128)S(1)}, u32[]{:S(2)}, u32[]{:S(2)}) collective-permute-start(f32[264,128]{1,0:T(8,128)S(1)} %shard_map.122.refs_4_.refs_0_), channel_id=1, source_target_pairs={{0,4},{4,0},{1,5},{5,1},{2,6},{6,2},{3,7},{7,3},{8,12},{12,8},{9,1... | collective-permute-start | bytes 405512 | tf_op jit(solution)/shard_map/ppermute | solution.py:336
  (13 other events, 53.3 us)

commit v13 on v12

--- a/solution.py
+++ b/solution.py
@@ -264,11 +264,19 @@
         )
         half = gact.shape[0] // 2
         keep_out[:, cols] = jnp.where(upward, gact[:half, :], gact[half:, :])
-        give_out[:, cols] = jnp.where(upward, gact[half:, :], gact[:half, :])
+        give_out[:half, cols] = jnp.where(upward, gact[half:, :], gact[:half, :])
+    if give_out.shape[0] > half:
+        give_out[half:, :] = jnp.zeros_like(give_out[half:, :])
+        give_out[half:, :BLOCK] = loss_out[...]
 
 
 def collect_kernel(keep, give, out):
-    out[...] = keep[...] + give[...]
+    out[...] = keep[...] + give[: keep.shape[0], :]
+
+
+def chip_losses_kernel(loss, give, out):
+    total = loss[...] + give[-LOSS_ROWS:, :BLOCK]
+    out[...] = jnp.where(lax.axis_index("wid") == 1, total, 0.0)
 
 
 def add_kernel(*refs):
@@ -438,7 +446,12 @@
             q = order[c]
             errs[q], keep, give, loss_here = call(
                 functools.partial(error_kernel, len(loss)),
-                [bf16(count, rows, width)] + [f32(rows // 2, lats)] * 2 + [f32(LOSS_ROWS, BLOCK)],
+                [
+                    bf16(count, rows, width),
+                    f32(rows // 2, lats),
+                    f32(rows // 2 + (LOSS_ROWS if c == n_tok - 1 else 0), lats),
+                    f32(LOSS_ROWS, BLOCK),
+                ],
                 (acts[q], dict_here, resids[q], bias_here, table, hands[c][1], hands[c][0], *loss),
                 after=sent if step < steps else (),
             )
@@ -459,9 +472,11 @@
             waits[step + 1] += ready
         ready_before = ready
 
-    loss, gap = loss[0], 1
+    loss = call(chip_losses_kernel, [f32(LOSS_ROWS, BLOCK)], (loss[0], gives[-1][1]))[0]
+    gap = 1
     while gap < n_lat:
-        other = lax.ppermute(loss, "lat", [(p, p ^ gap) for p in range(n_lat)])
+        pairs = [(2 * p + 1, 2 * (p ^ gap) + 1) for p in range(n_lat)]
+        other = lax.ppermute(loss, ("lat", "wid"), pairs)
         loss = call(add_kernel, [f32(*loss.shape)], (loss, other))[0]
         gap *= 2
 

time: 85.7 us -> 86.9 us (1.014)
  starting transfers between devices: 56.4 us -> 62.1 us
  waiting for transfers between devices: 16.1 us -> 11.5 us
    ppermute x2, waiting for transfers between devices: 5.91 us -> 0.01 us  [body(): other = lax.ppermute(loss, ('lat', 'wid'), pairs)]
    ppermute x14, starting transfers between devices: 12.1 us -> 17.6 us  [swap(): return lax.ppermute(array, 'wid', [(w, w ^ 1) for w in range(n_wid)])]
    ppermute x12, waiting for transfers between devices: 5.32 us -> 6.46 us  [across(): return lax.ppermute(array, 'tok', [(t, t ^ q) for t in range(n_tok)])]
    pallas_call x48 -> x49, Pallas kernels: 11.6 us -> 11.6 us  [call(): pl.pallas_call(run, out_shape=outs, in_specs=list(specs or [VMEM] * len(a...]
  transfers between devices with their start and end apart: 40 -> 40, of which waited for: 13 -> 13; matrix products, arithmetic and copies ran while one was open for 0% -> 0% of each run, Pallas kernels for 9% -> 8%
where the time goes in v13:
time: 86.9 us; the launch traced here: 86.5 us
  starting transfers between devices  62.1 us (71%)
  Pallas kernels  11.6 us (13%)
  waiting for transfers between devices  11.5 us (13%)
  between operations  1.26 us (1%)
    ppermute x12, starting transfers between devices, body(): got[side].append((lax.ppermute(message, ('lat', 'wid'), pairs), 0))  23.3 us
    ppermute x12, starting transfers between devices, across(): return lax.ppermute(array, 'tok', [(t, t ^ q) for t in range(n_tok)])  19.8 us
    ppermute x14, starting transfers between devices, swap(): return lax.ppermute(array, 'wid', [(w, w ^ 1) for w in range(n_wid)])  17.6 us
    pallas_call x49, Pallas kernels, call(): pl.pallas_call(run, out_shape=outs, in_specs=list(specs or [VMEM] * len(a...  11.6 us
    ppermute x12, waiting for transfers between devices, across(): return lax.ppermute(array, 'tok', [(t, t ^ q) for t in range(n_tok)])  6.46 us
    ppermute x14, waiting for transfers between devices, swap(): return lax.ppermute(array, 'wid', [(w, w ^ 1) for w in range(n_wid)])  3.44 us
  transfers between devices with their start and end apart: 40, of which 13 were waited for; matrix products, arithmetic and copies ran while one was open for 0% of the time, Pallas kernels for 8%

profile of v13, /device:TPU:0, one launch (start us, length us, event | category | flops | bytes accessed | tf_op | source)
XLA Modules:
  0.0 86.5 jit_solution(7251723403898884643)
XLA Ops:
  0.7 2.9 %shard_map.77 = (f32[128,512]{1,0:T(8,128)S(1)}, bf16[512,512]{1,0:T(8,128)(2,1)S(1)}) custom-call(bf16[128,2048]{1,0:T(8,128)(2,1)} %refs_0_.3, bf16[512,2048]{1,0:T(8,128)(2,1)} %refs_1_.1), custom_call_target="tpu_custom_call" | custom-call | bytes 1024 | tf_op jit(solution)/shard_map/pallas_call | solution.py:36
  4.1 1.2 %collective-permute-done.refs_2_.refs_1_ = f32[128,512]{1,0:T(8,128)S(1)} collective-permute-done((f32[128,512]{1,0:T(8,128)S(1)}, f32[128,512]{1,0:T(8,128)S(1)}, u32[]{:S(2)}, u32[]{:S(2)}) %collective-permute-start) | collective-permute-done | bytes 262176 | tf_op jit(solution)/shard_map/ppermute | solution.py:344
  6.1 2.7 %collective-permute-start.4 = (f32[128,512]{1,0:T(8,128)S(1)}, f32[128,512]{1,0:T(8,128)S(1)}, u32[]{:S(2)}, u32[]{:S(2)}) collective-permute-start(f32[128,512]{1,0:T(8,128)S(1)} %get-tuple-element.37.refs_0_.refs_2_), channel_id=1, source_target_pairs={{0,1},{1,0},{2,3},{3,2},{4,5},{5,4},{6,7},{7,6},{8,9},{9,8},{10,11... | collective-permute-start | bytes 786440 | tf_op jit(solution)/shard_map/ppermute | solution.py:341
  9.1 3.5 %collective-permute-start.7 = (f32[128,512]{1,0:T(8,128)S(1)}, f32[128,512]{1,0:T(8,128)S(1)}, u32[]{:S(2)}, u32[]{:S(2)}) collective-permute-start(f32[128,512]{1,0:T(8,128)S(1)} %shard_map.87.refs_2_.refs_3_), channel_id=1, source_target_pairs={{0,8},{28,20},{1,9},{29,21},{2,10},{30,22},{3,11},{31,23}} | collective-permute-start | bytes 786440 | tf_op jit(solution)/shard_map/ppermute | solution.py:404
  12.9 1.3 %collective-permute-start.3 = (f32[128,512]{1,0:T(8,128)S(1)}, f32[128,512]{1,0:T(8,128)S(1)}, u32[]{:S(2)}, u32[]{:S(2)}) collective-permute-start(f32[128,512]{1,0:T(8,128)S(1)} %shard_map.81.refs_1_.refs_2_.refs_3_), channel_id=1, source_target_pairs={{0,8},{28,20},{1,9},{29,21},{2,10},{30,22},{3,11},{31,23}} | collective-permute-start | bytes 786440 | tf_op jit(solution)/shard_map/ppermute | solution.py:404
  14.2 1.6 %collective-permute-start.6 = (f32[128,512]{1,0:T(8,128)S(1)}, f32[128,512]{1,0:T(8,128)S(1)}, u32[]{:S(2)}, u32[]{:S(2)}) collective-permute-start(f32[128,512]{1,0:T(8,128)S(1)} %get-tuple-element.37.refs_0_.refs_2_), channel_id=1, source_target_pairs={{0,3},{1,2},{2,1},{3,0},{4,7},{5,6},{6,5},{7,4},{8,11},{9,10},{10,... | collective-permute-start | bytes 786440 | tf_op jit(solution)/shard_map/ppermute | solution.py:341
  16.5 4.4 %collective-permute-start.8 = (f32[128,512]{1,0:T(8,128)S(1)}, f32[128,512]{1,0:T(8,128)S(1)}, u32[]{:S(2)}, u32[]{:S(2)}) collective-permute-start(f32[128,512]{1,0:T(8,128)S(1)} %shard_map.89), channel_id=1, source_target_pairs={{0,8},{28,20},{8,16},{20,12},{1,9},{29,21},{9,17},{21,13},{2,10},{... | collective-permute-start | bytes 786440 | tf_op jit(solution)/shard_map/ppermute | solution.py:415
  21.3 2.5 %collective-permute-start.5 = (f32[128,512]{1,0:T(8,128)S(1)}, f32[128,512]{1,0:T(8,128)S(1)}, u32[]{:S(2)}, u32[]{:S(2)}) collective-permute-start(f32[128,512]{1,0:T(8,128)S(1)} %shard_map.84.refs_1_.refs_4_), channel_id=1, source_target_pairs={{0,8},{28,20},{8,16},{20,12},{1,9},{29,21},{9,17},{21,13},{2,10},{... | collective-permute-start | bytes 786440 | tf_op jit(solution)/shard_map/ppermute | solution.py:415
  23.7 2.0 %collective-permute-start.1 = (f32[128,512]{1,0:T(8,128)S(1)}, f32[128,512]{1,0:T(8,128)S(1)}, u32[]{:S(2)}, u32[]{:S(2)}) collective-permute-start(f32[128,512]{1,0:T(8,128)S(1)} %get-tuple-element.37.refs_0_.refs_2_), channel_id=1, source_target_pairs={{0,2},{1,3},{2,0},{3,1},{4,6},{5,7},{6,4},{7,5},{8,10},{9,11},{10,... | collective-permute-start | bytes 786440 | tf_op jit(solution)/shard_map/ppermute | solution.py:341
  25.8 1.6 %collective-permute-start.11 = (f32[128,512]{1,0:T(8,128)S(1)}, f32[128,512]{1,0:T(8,128)S(1)}, u32[]{:S(2)}, u32[]{:S(2)}) collective-permute-start(f32[128,512]{1,0:T(8,128)S(1)} %get-tuple-element.41), channel_id=1, source_target_pairs={{0,1},{1,0},{2,3},{3,2},{4,5},{5,4},{6,7},{7,6},{8,9},{9,8},{10,11... | collective-permute-start | bytes 786440 | tf_op jit(solution)/shard_map/ppermute | solution.py:341
  27.8 1.9 %collective-permute-start.10 = (f32[128,512]{1,0:T(8,128)S(1)}, f32[128,512]{1,0:T(8,128)S(1)}, u32[]{:S(2)}, u32[]{:S(2)}) collective-permute-start(f32[128,512]{1,0:T(8,128)S(1)} %shard_map.91.refs_4_), channel_id=1, source_target_pairs={{0,8},{28,20},{8,16},{20,12},{16,24},{12,4},{1,9},{29,21},{9,17},{... | collective-permute-start | bytes 786440 | tf_op jit(solution)/shard_map/ppermute | solution.py:415
  30.1 1.9 %collective-permute-start.13 = (f32[128,512]{1,0:T(8,128)S(1)}, f32[128,512]{1,0:T(8,128)S(1)}, u32[]{:S(2)}, u32[]{:S(2)}) collective-permute-start(f32[128,512]{1,0:T(8,128)S(1)} %shard_map.92.refs_1_.refs_4_), channel_id=1, source_target_pairs={{0,8},{28,20},{8,16},{20,12},{16,24},{12,4},{1,9},{29,21},{9,17},{... | collective-permute-start | bytes 786440 | tf_op jit(solution)/shard_map/ppermute | solution.py:415
  32.0 3.0 %collective-permute-start.14 = (f32[128,512]{1,0:T(8,128)S(1)}, f32[128,512]{1,0:T(8,128)S(1)}, u32[]{:S(2)}, u32[]{:S(2)}) collective-permute-start(f32[128,512]{1,0:T(8,128)S(1)} %get-tuple-element.42), channel_id=1, source_target_pairs={{0,3},{1,2},{2,1},{3,0},{4,7},{5,6},{6,5},{7,4},{8,11},{9,10},{10,... | collective-permute-start | bytes 786440 | tf_op jit(solution)/shard_map/ppermute | solution.py:341
  35.4 2.6 %collective-permute-start.12 = (f32[128,512]{1,0:T(8,128)S(1)}, f32[128,512]{1,0:T(8,128)S(1)}, u32[]{:S(2)}, u32[]{:S(2)}) collective-permute-start(f32[128,512]{1,0:T(8,128)S(1)} %shard_map.96.refs_4_), channel_id=1, source_target_pairs={{0,8},{28,20},{8,16},{20,12},{16,24},{12,4},{1,9},{29,21},{9,17},{... | collective-permute-start | bytes 786440 | tf_op jit(solution)/shard_map/ppermute | solution.py:415
  38.4 2.4 %collective-permute-start.16 = (f32[128,512]{1,0:T(8,128)S(1)}, f32[128,512]{1,0:T(8,128)S(1)}, u32[]{:S(2)}, u32[]{:S(2)}) collective-permute-start(f32[128,512]{1,0:T(8,128)S(1)} %shard_map.98.refs_3_), channel_id=1, source_target_pairs={{0,8},{28,20},{8,16},{20,12},{16,24},{12,4},{1,9},{29,21},{9,17},{... | collective-permute-start | bytes 786440 | tf_op jit(solution)/shard_map/ppermute | solution.py:415
  40.8 1.5 %collective-permute-start.9 = (f32[128,512]{1,0:T(8,128)S(1)}, f32[128,512]{1,0:T(8,128)S(1)}, u32[]{:S(2)}, u32[]{:S(2)}) collective-permute-start(f32[128,512]{1,0:T(8,128)S(1)} %get-tuple-element.39), channel_id=1, source_target_pairs={{0,2},{1,3},{2,0},{3,1},{4,6},{5,7},{6,4},{7,5},{8,10},{9,11},{10,... | collective-permute-start | bytes 786440 | tf_op jit(solution)/shard_map/ppermute | solution.py:341
  43.3 1.4 %collective-permute-done.16.refs_0_.refs_2_.refs_1_ = f32[128,512]{1,0:T(8,128)S(1)} collective-permute-done((f32[128,512]{1,0:T(8,128)S(1)}, f32[128,512]{1,0:T(8,128)S(1)}, u32[]{:S(2)}, u32[]{:S(2)}) %collective-permute-start.16) | collective-permute-done | bytes 262176 | tf_op jit(solution)/shard_map/ppermute | solution.py:415
  49.4 5.7 %collective-permute-start.21 = (f32[64,512]{1,0:T(8,128)S(1)}, f32[64,512]{1,0:T(8,128)S(1)}, u32[]{:S(2)}, u32[]{:S(2)}) collective-permute-start(f32[64,512]{1,0:T(8,128)S(1)} %get-tuple-element.48), channel_id=1, source_target_pairs={{0,4},{4,0},{1,5},{5,1},{2,6},{6,2},{3,7},{7,3},{8,12},{12,8},{9,1... | collective-permute-start | bytes 393224 | tf_op jit(solution)/shard_map/ppermute | solution.py:344
  55.2 0.8 collective-permute-done.21.refs_1_
  56.2 4.0 %collective-permute-start.23 = (f32[128,512]{1,0:T(8,128)S(1)}, f32[128,512]{1,0:T(8,128)S(1)}, u32[]{:S(2)}, u32[]{:S(2)}) collective-permute-start(f32[128,512]{1,0:T(8,128)S(1)} %shard_map.113), channel_id=1, source_target_pairs={{0,4},{4,0},{1,5},{5,1},{2,6},{6,2},{3,7},{7,3},{8,12},{12,8},{9,1... | collective-permute-start | bytes 786440 | tf_op jit(solution)/shard_map/ppermute | solution.py:344
  63.0 1.5 %collective-permute-start.28 = (f32[64,512]{1,0:T(8,128)S(1)}, f32[64,512]{1,0:T(8,128)S(1)}, u32[]{:S(2)}, u32[]{:S(2)}) collective-permute-start(f32[64,512]{1,0:T(8,128)S(1)} %shard_map.111.refs_6_), channel_id=1, source_target_pairs={{0,1},{1,0},{2,3},{3,2},{4,5},{5,4},{6,7},{7,6},{8,9},{9,8},{10,11... | collective-permute-start | bytes 393224 | tf_op jit(solution)/shard_map/ppermute | solution.py:341
  64.5 0.8 collective-permute-start.31
  65.4 1.6 %collective-permute-start.32 = (f32[64,512]{1,0:T(8,128)S(1)}, f32[64,512]{1,0:T(8,128)S(1)}, u32[]{:S(2)}, u32[]{:S(2)}) collective-permute-start(f32[64,512]{1,0:T(8,128)S(1)} %shard_map.121), channel_id=1, source_target_pairs={{0,2},{1,3},{2,0},{3,1},{4,6},{5,7},{6,4},{7,5},{8,10},{9,11},{10,... | collective-permute-start | bytes 393224 | tf_op jit(solution)/shard_map/ppermute | solution.py:341
  68.3 0.8 shard_map.122.refs_7_.refs_11_
  69.3 2.1 %collective-permute-done.31.refs_5_ = f32[64,512]{1,0:T(8,128)S(1)} collective-permute-done((f32[64,512]{1,0:T(8,128)S(1)}, f32[64,512]{1,0:T(8,128)S(1)}, u32[]{:S(2)}, u32[]{:S(2)}) %collective-permute-start.31) | collective-permute-done | bytes 131104 | tf_op jit(solution)/shard_map/ppermute | solution.py:341
  71.4 2.1 %collective-permute-done.32.refs_6_ = f32[64,512]{1,0:T(8,128)S(1)} collective-permute-done((f32[64,512]{1,0:T(8,128)S(1)}, f32[64,512]{1,0:T(8,128)S(1)}, u32[]{:S(2)}, u32[]{:S(2)}) %collective-permute-start.32) | collective-permute-done | bytes 131104 | tf_op jit(solution)/shard_map/ppermute | solution.py:341
  73.7 1.9 %collective-permute-start.35 = (f32[264,128]{1,0:T(8,128)S(1)}, f32[264,128]{1,0:T(8,128)S(1)}, u32[]{:S(2)}, u32[]{:S(2)}) collective-permute-start(f32[264,128]{1,0:T(8,128)S(1)} %shard_map.123.refs_4_.refs_0_), channel_id=1, source_target_pairs={{0,3},{1,2},{2,1},{3,0},{4,7},{5,6},{6,5},{7,4},{8,11},{9,10},{10,... | collective-permute-start | bytes 405512 | tf_op jit(solution)/shard_map/ppermute | solution.py:341
  76.1 1.2 %collective-permute-start.33 = (f32[264,128]{1,0:T(8,128)S(1)}, f32[264,128]{1,0:T(8,128)S(1)}, u32[]{:S(2)}, u32[]{:S(2)}) collective-permute-start(f32[264,128]{1,0:T(8,128)S(1)} %shard_map.123.refs_4_.refs_0_), channel_id=1, source_target_pairs={{0,1},{1,0},{2,3},{3,2},{4,5},{5,4},{6,7},{7,6},{8,9},{9,8},{10,11... | collective-permute-start | bytes 405512 | tf_op jit(solution)/shard_map/ppermute | solution.py:341
  77.2 2.1 %collective-permute-start.36 = (f32[264,128]{1,0:T(8,128)S(1)}, f32[264,128]{1,0:T(8,128)S(1)}, u32[]{:S(2)}, u32[]{:S(2)}) collective-permute-start(f32[264,128]{1,0:T(8,128)S(1)} %shard_map.123.refs_4_.refs_0_), channel_id=1, source_target_pairs={{0,4},{4,0},{1,5},{5,1},{2,6},{6,2},{3,7},{7,3},{8,12},{12,8},{9,1... | collective-permute-start | bytes 405512 | tf_op jit(solution)/shard_map/ppermute | solution.py:344
  79.7 2.9 %collective-permute-start.38 = (f32[264,128]{1,0:T(8,128)S(1)}, f32[264,128]{1,0:T(8,128)S(1)}, u32[]{:S(2)}, u32[]{:S(2)}) collective-permute-start(f32[264,128]{1,0:T(8,128)S(1)} %collective-permute-done.35.refs_7_.refs_3_), channel_id=1, source_target_pairs={{0,4},{4,0},{1,5},{5,1},{2,6},{6,2},{3,7},{7,3},{8,12},{12,8},{9,1... | collective-permute-start | bytes 405512 | tf_op jit(solution)/shard_map/ppermute | solution.py:344
  83.9 0.9 %collective-permute-done.37.refs_9_.refs_5_ = f32[264,128]{1,0:T(8,128)S(1)} collective-permute-done((f32[264,128]{1,0:T(8,128)S(1)}, f32[264,128]{1,0:T(8,128)S(1)}, u32[]{:S(2)}, u32[]{:S(2)}) %collective-permute-start.37) | collective-permute-done | bytes 135200 | tf_op jit(solution)/shard_map/ppermute | solution.py:344
  85.3 1.1 %shard_map.125 = (bf16[512,512]{1,0:T(8,128)(2,1)}, f32[4]{0:T(128)}) custom-call(f32[264,128]{1,0:T(8,128)S(1)} %shard_map.123.refs_4_.refs_0_, f32[264,128]{1,0:T(8,128)S(1)} %collective-permute-done.33.refs_5_.refs_1_, f32[264,128]{1,0:T(8,128)S(1)} %collective-permute-done.34.refs_6_.refs_2_, f32[264,128]{1,0:T(8,128)S(1)} %collective-permute-done.35.refs_7_.refs_3_, ...), custom_call_target="tpu_custom_call" | custom-call | bytes 1024 | tf_op jit(solution)/shard_map/pallas_call | solution.py:36
  (107 shorter events, 17.3 us)
Async XLA Ops:
  5.4 7.2 %collective-permute-start.2 = (f32[512,512]{1,0:T(8,128)S(1)}, f32[512,512]{1,0:T(8,128)S(1)}, u32[]{:S(2)}, u32[]{:S(2)}) collective-permute-start(f32[512,512]{1,0:T(8,128)S(1)} %get-tuple-element.34.refs_4_), channel_id=1, source_target_pairs={{0,4},{4,0},{1,5},{5,1},{2,6},{6,2},{3,7},{7,3},{8,12},{12,8},{9,1... | collective-permute-start | bytes 3145736 | tf_op jit(solution)/shard_map/ppermute | solution.py:344
  6.1 9.8 %collective-permute-start.4 = (f32[128,512]{1,0:T(8,128)S(1)}, f32[128,512]{1,0:T(8,128)S(1)}, u32[]{:S(2)}, u32[]{:S(2)}) collective-permute-start(f32[128,512]{1,0:T(8,128)S(1)} %get-tuple-element.37.refs_0_.refs_2_), channel_id=1, source_target_pairs={{0,1},{1,0},{2,3},{3,2},{4,5},{5,4},{6,7},{7,6},{8,9},{9,8},{10,11... | collective-permute-start | bytes 786440 | tf_op jit(solution)/shard_map/ppermute | solution.py:341
  9.1 7.4 %collective-permute-start.7 = (f32[128,512]{1,0:T(8,128)S(1)}, f32[128,512]{1,0:T(8,128)S(1)}, u32[]{:S(2)}, u32[]{:S(2)}) collective-permute-start(f32[128,512]{1,0:T(8,128)S(1)} %shard_map.87.refs_2_.refs_3_), channel_id=1, source_target_pairs={{0,8},{28,20},{1,9},{29,21},{2,10},{30,22},{3,11},{31,23}} | collective-permute-start | bytes 786440 | tf_op jit(solution)/shard_map/ppermute | solution.py:404
  12.9 8.3 %collective-permute-start.3 = (f32[128,512]{1,0:T(8,128)S(1)}, f32[128,512]{1,0:T(8,128)S(1)}, u32[]{:S(2)}, u32[]{:S(2)}) collective-permute-start(f32[128,512]{1,0:T(8,128)S(1)} %shard_map.81.refs_1_.refs_2_.refs_3_), channel_id=1, source_target_pairs={{0,8},{28,20},{1,9},{29,21},{2,10},{30,22},{3,11},{31,23}} | collective-permute-start | bytes 786440 | tf_op jit(solution)/shard_map/ppermute | solution.py:404
  14.2 13.2 %collective-permute-start.6 = (f32[128,512]{1,0:T(8,128)S(1)}, f32[128,512]{1,0:T(8,128)S(1)}, u32[]{:S(2)}, u32[]{:S(2)}) collective-permute-start(f32[128,512]{1,0:T(8,128)S(1)} %get-tuple-element.37.refs_0_.refs_2_), channel_id=1, source_target_pairs={{0,3},{1,2},{2,1},{3,0},{4,7},{5,6},{6,5},{7,4},{8,11},{9,10},{10,... | collective-permute-start | bytes 786440 | tf_op jit(solution)/shard_map/ppermute | solution.py:341
  16.5 11.2 %collective-permute-start.8 = (f32[128,512]{1,0:T(8,128)S(1)}, f32[128,512]{1,0:T(8,128)S(1)}, u32[]{:S(2)}, u32[]{:S(2)}) collective-permute-start(f32[128,512]{1,0:T(8,128)S(1)} %shard_map.89), channel_id=1, source_target_pairs={{0,8},{28,20},{8,16},{20,12},{1,9},{29,21},{9,17},{21,13},{2,10},{... | collective-permute-start | bytes 786440 | tf_op jit(solution)/shard_map/ppermute | solution.py:415
  21.3 8.8 %collective-permute-start.5 = (f32[128,512]{1,0:T(8,128)S(1)}, f32[128,512]{1,0:T(8,128)S(1)}, u32[]{:S(2)}, u32[]{:S(2)}) collective-permute-start(f32[128,512]{1,0:T(8,128)S(1)} %shard_map.84.refs_1_.refs_4_), channel_id=1, source_target_pairs={{0,8},{28,20},{8,16},{20,12},{1,9},{29,21},{9,17},{21,13},{2,10},{... | collective-permute-start | bytes 786440 | tf_op jit(solution)/shard_map/ppermute | solution.py:415
  23.7 11.3 %collective-permute-start.1 = (f32[128,512]{1,0:T(8,128)S(1)}, f32[128,512]{1,0:T(8,128)S(1)}, u32[]{:S(2)}, u32[]{:S(2)}) collective-permute-start(f32[128,512]{1,0:T(8,128)S(1)} %get-tuple-element.37.refs_0_.refs_2_), channel_id=1, source_target_pairs={{0,2},{1,3},{2,0},{3,1},{4,6},{5,7},{6,4},{7,5},{8,10},{9,11},{10,... | collective-permute-start | bytes 786440 | tf_op jit(solution)/shard_map/ppermute | solution.py:341
  25.8 9.5 %collective-permute-start.11 = (f32[128,512]{1,0:T(8,128)S(1)}, f32[128,512]{1,0:T(8,128)S(1)}, u32[]{:S(2)}, u32[]{:S(2)}) collective-permute-start(f32[128,512]{1,0:T(8,128)S(1)} %get-tuple-element.41), channel_id=1, source_target_pairs={{0,1},{1,0},{2,3},{3,2},{4,5},{5,4},{6,7},{7,6},{8,9},{9,8},{10,11... | collective-permute-start | bytes 786440 | tf_op jit(solution)/shard_map/ppermute | solution.py:341
  27.8 7.6 %collective-permute-start.10 = (f32[128,512]{1,0:T(8,128)S(1)}, f32[128,512]{1,0:T(8,128)S(1)}, u32[]{:S(2)}, u32[]{:S(2)}) collective-permute-start(f32[128,512]{1,0:T(8,128)S(1)} %shard_map.91.refs_4_), channel_id=1, source_target_pairs={{0,8},{28,20},{8,16},{20,12},{16,24},{12,4},{1,9},{29,21},{9,17},{... | collective-permute-start | bytes 786440 | tf_op jit(solution)/shard_map/ppermute | solution.py:415
  30.1 8.3 %collective-permute-start.13 = (f32[128,512]{1,0:T(8,128)S(1)}, f32[128,512]{1,0:T(8,128)S(1)}, u32[]{:S(2)}, u32[]{:S(2)}) collective-permute-start(f32[128,512]{1,0:T(8,128)S(1)} %shard_map.92.refs_1_.refs_4_), channel_id=1, source_target_pairs={{0,8},{28,20},{8,16},{20,12},{16,24},{12,4},{1,9},{29,21},{9,17},{... | collective-permute-start | bytes 786440 | tf_op jit(solution)/shard_map/ppermute | solution.py:415
  32.0 10.5 %collective-permute-start.14 = (f32[128,512]{1,0:T(8,128)S(1)}, f32[128,512]{1,0:T(8,128)S(1)}, u32[]{:S(2)}, u32[]{:S(2)}) collective-permute-start(f32[128,512]{1,0:T(8,128)S(1)} %get-tuple-element.42), channel_id=1, source_target_pairs={{0,3},{1,2},{2,1},{3,0},{4,7},{5,6},{6,5},{7,4},{8,11},{9,10},{10,... | collective-permute-start | bytes 786440 | tf_op jit(solution)/shard_map/ppermute | solution.py:341
  35.4 7.2 %collective-permute-start.12 = (f32[128,512]{1,0:T(8,128)S(1)}, f32[128,512]{1,0:T(8,128)S(1)}, u32[]{:S(2)}, u32[]{:S(2)}) collective-permute-start(f32[128,512]{1,0:T(8,128)S(1)} %shard_map.96.refs_4_), channel_id=1, source_target_pairs={{0,8},{28,20},{8,16},{20,12},{16,24},{12,4},{1,9},{29,21},{9,17},{... | collective-permute-start | bytes 786440 | tf_op jit(solution)/shard_map/ppermute | solution.py:415
  38.4 6.3 %collective-permute-start.16 = (f32[128,512]{1,0:T(8,128)S(1)}, f32[128,512]{1,0:T(8,128)S(1)}, u32[]{:S(2)}, u32[]{:S(2)}) collective-permute-start(f32[128,512]{1,0:T(8,128)S(1)} %shard_map.98.refs_3_), channel_id=1, source_target_pairs={{0,8},{28,20},{8,16},{20,12},{16,24},{12,4},{1,9},{29,21},{9,17},{... | collective-permute-start | bytes 786440 | tf_op jit(solution)/shard_map/ppermute | solution.py:415
  40.8 6.4 %collective-permute-start.9 = (f32[128,512]{1,0:T(8,128)S(1)}, f32[128,512]{1,0:T(8,128)S(1)}, u32[]{:S(2)}, u32[]{:S(2)}) collective-permute-start(f32[128,512]{1,0:T(8,128)S(1)} %get-tuple-element.39), channel_id=1, source_target_pairs={{0,2},{1,3},{2,0},{3,1},{4,6},{5,7},{6,4},{7,5},{8,10},{9,11},{10,... | collective-permute-start | bytes 786440 | tf_op jit(solution)/shard_map/ppermute | solution.py:341
  42.4 3.5 %collective-permute-start.17 = (f32[128,512]{1,0:T(8,128)S(1)}, f32[128,512]{1,0:T(8,128)S(1)}, u32[]{:S(2)}, u32[]{:S(2)}) collective-permute-start(f32[128,512]{1,0:T(8,128)S(1)} %shard_map.99.refs_5_), channel_id=1, source_target_pairs={{0,4},{4,0},{1,5},{5,1},{2,6},{6,2},{3,7},{7,3},{8,12},{12,8},{9,1... | collective-permute-start | bytes 786440 | tf_op jit(solution)/shard_map/ppermute | solution.py:344
  42.6 4.7 %collective-permute-start.15 = (f32[128,512]{1,0:T(8,128)S(1)}, f32[128,512]{1,0:T(8,128)S(1)}, u32[]{:S(2)}, u32[]{:S(2)}) collective-permute-start(f32[128,512]{1,0:T(8,128)S(1)} %shard_map.101.refs_3_), channel_id=1, source_target_pairs={{8,16},{20,12},{16,24},{12,4},{9,17},{21,13},{17,25},{13,5},{10,18... | collective-permute-start | bytes 786440 | tf_op jit(solution)/shard_map/ppermute | solution.py:415
  47.3 8.8 %collective-permute-start.18 = (f32[128,512]{1,0:T(8,128)S(1)}, f32[128,512]{1,0:T(8,128)S(1)}, u32[]{:S(2)}, u32[]{:S(2)}) collective-permute-start(f32[128,512]{1,0:T(8,128)S(1)} %shard_map.106.refs_2_), channel_id=1, source_target_pairs={{16,24},{12,4},{17,25},{13,5},{18,26},{14,6},{19,27},{15,7}} | collective-permute-start | bytes 786440 | tf_op jit(solution)/shard_map/ppermute | solution.py:415
  48.0 8.1 %collective-permute-start.22 = (f32[128,512]{1,0:T(8,128)S(1)}, f32[128,512]{1,0:T(8,128)S(1)}, u32[]{:S(2)}, u32[]{:S(2)}) collective-permute-start(f32[128,512]{1,0:T(8,128)S(1)} %shard_map.107.refs_3_.refs_8_.refs_2_), channel_id=1, source_target_pairs={{16,24},{12,4},{17,25},{13,5},{18,26},{14,6},{19,27},{15,7}} | collective-permute-start | bytes 786440 | tf_op jit(solution)/shard_map/ppermute | solution.py:415
  49.4 6.7 %collective-permute-start.21 = (f32[64,512]{1,0:T(8,128)S(1)}, f32[64,512]{1,0:T(8,128)S(1)}, u32[]{:S(2)}, u32[]{:S(2)}) collective-permute-start(f32[64,512]{1,0:T(8,128)S(1)} %get-tuple-element.48), channel_id=1, source_target_pairs={{0,4},{4,0},{1,5},{5,1},{2,6},{6,2},{3,7},{7,3},{8,12},{12,8},{9,1... | collective-permute-start | bytes 393224 | tf_op jit(solution)/shard_map/ppermute | solution.py:344
  55.1 5.1 %collective-permute-start.24 = (f32[128,512]{1,0:T(8,128)S(1)}, f32[128,512]{1,0:T(8,128)S(1)}, u32[]{:S(2)}, u32[]{:S(2)}) collective-permute-start(f32[128,512]{1,0:T(8,128)S(1)} %shard_map.108.refs_3_), channel_id=1, source_target_pairs={{0,4},{4,0},{1,5},{5,1},{2,6},{6,2},{3,7},{7,3},{8,12},{12,8},{9,1... | collective-permute-start | bytes 786440 | tf_op jit(solution)/shard_map/ppermute | solution.py:344
  56.2 5.2 %collective-permute-start.23 = (f32[128,512]{1,0:T(8,128)S(1)}, f32[128,512]{1,0:T(8,128)S(1)}, u32[]{:S(2)}, u32[]{:S(2)}) collective-permute-start(f32[128,512]{1,0:T(8,128)S(1)} %shard_map.113), channel_id=1, source_target_pairs={{0,4},{4,0},{1,5},{5,1},{2,6},{6,2},{3,7},{7,3},{8,12},{12,8},{9,1... | collective-permute-start | bytes 786440 | tf_op jit(solution)/shard_map/ppermute | solution.py:344
  62.0 3.3 %collective-permute-start.25 = (f32[72,512]{1,0:T(8,128)S(1)}, f32[72,512]{1,0:T(8,128)S(1)}, u32[]{:S(2)}, u32[]{:S(2)}) collective-permute-start(f32[72,512]{1,0:T(8,128)S(1)} %get-tuple-element.52), channel_id=1, source_target_pairs={{0,4},{4,0},{1,5},{5,1},{2,6},{6,2},{3,7},{7,3},{8,12},{12,8},{9,1... | collective-permute-start | bytes 442376 | tf_op jit(solution)/shard_map/ppermute | solution.py:344
  62.6 5.7 %collective-permute-start.29 = (f32[64,512]{1,0:T(8,128)S(1)}, f32[64,512]{1,0:T(8,128)S(1)}, u32[]{:S(2)}, u32[]{:S(2)}) collective-permute-start(f32[64,512]{1,0:T(8,128)S(1)} %get-tuple-element.54), channel_id=1, source_target_pairs={{0,4},{4,0},{1,5},{5,1},{2,6},{6,2},{3,7},{7,3},{8,12},{12,8},{9,1... | collective-permute-start | bytes 393224 | tf_op jit(solution)/shard_map/ppermute | solution.py:344
  63.0 6.3 %collective-permute-start.28 = (f32[64,512]{1,0:T(8,128)S(1)}, f32[64,512]{1,0:T(8,128)S(1)}, u32[]{:S(2)}, u32[]{:S(2)}) collective-permute-start(f32[64,512]{1,0:T(8,128)S(1)} %shard_map.111.refs_6_), channel_id=1, source_target_pairs={{0,1},{1,0},{2,3},{3,2},{4,5},{5,4},{6,7},{7,6},{8,9},{9,8},{10,11... | collective-permute-start | bytes 393224 | tf_op jit(solution)/shard_map/ppermute | solution.py:341
  64.5 6.9 %collective-permute-start.31 = (f32[64,512]{1,0:T(8,128)S(1)}, f32[64,512]{1,0:T(8,128)S(1)}, u32[]{:S(2)}, u32[]{:S(2)}) collective-permute-start(f32[64,512]{1,0:T(8,128)S(1)} %shard_map.120), channel_id=1, source_target_pairs={{0,3},{1,2},{2,1},{3,0},{4,7},{5,6},{6,5},{7,4},{8,11},{9,10},{10,... | collective-permute-start | bytes 393224 | tf_op jit(solution)/shard_map/ppermute | solution.py:341
  65.4 8.2 %collective-permute-start.32 = (f32[64,512]{1,0:T(8,128)S(1)}, f32[64,512]{1,0:T(8,128)S(1)}, u32[]{:S(2)}, u32[]{:S(2)}) collective-permute-start(f32[64,512]{1,0:T(8,128)S(1)} %shard_map.121), channel_id=1, source_target_pairs={{0,2},{1,3},{2,0},{3,1},{4,6},{5,7},{6,4},{7,5},{8,10},{9,11},{10,... | collective-permute-start | bytes 393224 | tf_op jit(solution)/shard_map/ppermute | solution.py:341
  73.7 6.0 %collective-permute-start.35 = (f32[264,128]{1,0:T(8,128)S(1)}, f32[264,128]{1,0:T(8,128)S(1)}, u32[]{:S(2)}, u32[]{:S(2)}) collective-permute-start(f32[264,128]{1,0:T(8,128)S(1)} %shard_map.123.refs_4_.refs_0_), channel_id=1, source_target_pairs={{0,3},{1,2},{2,1},{3,0},{4,7},{5,6},{6,5},{7,4},{8,11},{9,10},{10,... | collective-permute-start | bytes 405512 | tf_op jit(solution)/shard_map/ppermute | solution.py:341
  75.6 7.8 %collective-permute-start.34 = (f32[264,128]{1,0:T(8,128)S(1)}, f32[264,128]{1,0:T(8,128)S(1)}, u32[]{:S(2)}, u32[]{:S(2)}) collective-permute-start(f32[264,128]{1,0:T(8,128)S(1)} %shard_map.123.refs_4_.refs_0_), channel_id=1, source_target_pairs={{0,2},{1,3},{2,0},{3,1},{4,6},{5,7},{6,4},{7,5},{8,10},{9,11},{10,... | collective-permute-start | bytes 405512 | tf_op jit(solution)/shard_map/ppermute | solution.py:341
  76.1 7.8 %collective-permute-start.33 = (f32[264,128]{1,0:T(8,128)S(1)}, f32[264,128]{1,0:T(8,128)S(1)}, u32[]{:S(2)}, u32[]{:S(2)}) collective-permute-start(f32[264,128]{1,0:T(8,128)S(1)} %shard_map.123.refs_4_.refs_0_), channel_id=1, source_target_pairs={{0,1},{1,0},{2,3},{3,2},{4,5},{5,4},{6,7},{7,6},{8,9},{9,8},{10,11... | collective-permute-start | bytes 405512 | tf_op jit(solution)/shard_map/ppermute | solution.py:341
  77.2 6.6 %collective-permute-start.36 = (f32[264,128]{1,0:T(8,128)S(1)}, f32[264,128]{1,0:T(8,128)S(1)}, u32[]{:S(2)}, u32[]{:S(2)}) collective-permute-start(f32[264,128]{1,0:T(8,128)S(1)} %shard_map.123.refs_4_.refs_0_), channel_id=1, source_target_pairs={{0,4},{4,0},{1,5},{5,1},{2,6},{6,2},{3,7},{7,3},{8,12},{12,8},{9,1... | collective-permute-start | bytes 405512 | tf_op jit(solution)/shard_map/ppermute | solution.py:344
  79.7 4.2 %collective-permute-start.38 = (f32[264,128]{1,0:T(8,128)S(1)}, f32[264,128]{1,0:T(8,128)S(1)}, u32[]{:S(2)}, u32[]{:S(2)}) collective-permute-start(f32[264,128]{1,0:T(8,128)S(1)} %collective-permute-done.35.refs_7_.refs_3_), channel_id=1, source_target_pairs={{0,4},{4,0},{1,5},{5,1},{2,6},{6,2},{3,7},{7,3},{8,12},{12,8},{9,1... | collective-permute-start | bytes 405512 | tf_op jit(solution)/shard_map/ppermute | solution.py:344
  (13 other events, 49.9 us)

commit v14 on v13

--- a/solution.py
+++ b/solution.py
@@ -10,6 +10,7 @@
 LEVELS = 4
 BLOCK = 128
 LOSS_ROWS = 8
+LOSS_AREA = 128
 GELU_C = 0.7978845608028654
 GELU_A = 0.044715
 
@@ -167,7 +168,9 @@
     bend = jnp.tanh(inner)
     deriv = 0.5 * (1.0 + bend) + 0.5 * pre * (1.0 - bend * bend) * slope
     hit = mask[mine, :] > 0.0
-    stacked(jnp.where(hit, deriv * total_of([t[...] for t in terms]), 0.0), loss[...], out)
+    stacked(
+        jnp.where(hit, deriv * total_of([t[...] for t in terms]), 0.0), loss[:LOSS_ROWS, :], out
+    )
 
 
 def running_parts(act, dict_ref):
@@ -276,7 +279,8 @@
 
 def chip_losses_kernel(loss, give, out):
     total = loss[...] + give[-LOSS_ROWS:, :BLOCK]
-    out[...] = jnp.where(lax.axis_index("wid") == 1, total, 0.0)
+    out[...] = jnp.zeros_like(out)
+    out[:LOSS_ROWS, :] = jnp.where(lax.axis_index("wid") == 1, total, 0.0)
 
 
 def add_kernel(*refs):
@@ -472,7 +476,7 @@
             waits[step + 1] += ready
         ready_before = ready
 
-    loss = call(chip_losses_kernel, [f32(LOSS_ROWS, BLOCK)], (loss[0], gives[-1][1]))[0]
+    loss = call(chip_losses_kernel, [f32(LOSS_AREA, BLOCK)], (loss[0], gives[-1][1]))[0]
     gap = 1
     while gap < n_lat:
         pairs = [(2 * p + 1, 2 * (p ^ gap) + 1) for p in range(n_lat)]

time: 86.9 us -> 88.6 us (1.020)
  waiting for transfers between devices: 11.5 us -> 18.4 us
  starting transfers between devices: 62.1 us -> 56.8 us
    ppermute x12, waiting for transfers between devices: 6.46 us -> 13.4 us  [across(): return lax.ppermute(array, 'tok', [(t, t ^ q) for t in range(n_tok)])]
    ppermute x14, starting transfers between devices: 17.6 us -> 12.7 us  [swap(): return lax.ppermute(array, 'wid', [(w, w ^ 1) for w in range(n_wid)])]
  transfers between devices with their start and end apart: 40 -> 40, of which waited for: 13 -> 12; matrix products, arithmetic and copies ran while one was open for 0% -> 0% of each run, Pallas kernels for 8% -> 8%
where the time goes in v14:
time: 88.6 us; the launch traced here: 88.1 us
  starting transfers between devices  56.8 us (64%)
  waiting for transfers between devices  18.4 us (21%)
  Pallas kernels  11.6 us (13%)
  between operations  1.28 us (1%)
    ppermute x12, starting transfers between devices, body(): got[side].append((lax.ppermute(message, ('lat', 'wid'), pairs), 0))  23.3 us
    ppermute x12, starting transfers between devices, across(): return lax.ppermute(array, 'tok', [(t, t ^ q) for t in range(n_tok)])  19.5 us
    ppermute x12, waiting for transfers between devices, across(): return lax.ppermute(array, 'tok', [(t, t ^ q) for t in range(n_tok)])  13.4 us
    ppermute x14, starting transfers between devices, swap(): return lax.ppermute(array, 'wid', [(w, w ^ 1) for w in range(n_wid)])  12.7 us
    pallas_call x49, Pallas kernels, call(): pl.pallas_call(run, out_shape=outs, in_specs=list(specs or [VMEM] * len(a...  11.6 us
    ppermute x14, waiting for transfers between devices, swap(): return lax.ppermute(array, 'wid', [(w, w ^ 1) for w in range(n_wid)])  3.32 us
  transfers between devices with their start and end apart: 40, of which 12 were waited for; matrix products, arithmetic and copies ran while one was open for 0% of the time, Pallas kernels for 8%

profile of v14, /device:TPU:0, one launch (start us, length us, event | category | flops | bytes accessed | tf_op | source)
XLA Modules:
  0.0 88.1 jit_solution(2020512249510039639)
XLA Ops:
  0.7 2.9 %shard_map.77 = (f32[128,512]{1,0:T(8,128)S(1)}, bf16[512,512]{1,0:T(8,128)(2,1)S(1)}) custom-call(bf16[128,2048]{1,0:T(8,128)(2,1)} %refs_0_.3, bf16[512,2048]{1,0:T(8,128)(2,1)} %refs_1_.1), custom_call_target="tpu_custom_call" | custom-call | bytes 1024 | tf_op jit(solution)/shard_map/pallas_call | solution.py:37
  4.1 1.2 %collective-permute-done.refs_2_.refs_1_ = f32[128,512]{1,0:T(8,128)S(1)} collective-permute-done((f32[128,512]{1,0:T(8,128)S(1)}, f32[128,512]{1,0:T(8,128)S(1)}, u32[]{:S(2)}, u32[]{:S(2)}) %collective-permute-start) | collective-permute-done | bytes 262176 | tf_op jit(solution)/shard_map/ppermute | solution.py:348
  6.1 2.7 %collective-permute-start.4 = (f32[128,512]{1,0:T(8,128)S(1)}, f32[128,512]{1,0:T(8,128)S(1)}, u32[]{:S(2)}, u32[]{:S(2)}) collective-permute-start(f32[128,512]{1,0:T(8,128)S(1)} %get-tuple-element.37.refs_0_.refs_2_), channel_id=1, source_target_pairs={{0,1},{1,0},{2,3},{3,2},{4,5},{5,4},{6,7},{7,6},{8,9},{9,8},{10,11... | collective-permute-start | bytes 786440 | tf_op jit(solution)/shard_map/ppermute | solution.py:345
  9.1 3.5 %collective-permute-start.7 = (f32[128,512]{1,0:T(8,128)S(1)}, f32[128,512]{1,0:T(8,128)S(1)}, u32[]{:S(2)}, u32[]{:S(2)}) collective-permute-start(f32[128,512]{1,0:T(8,128)S(1)} %shard_map.87.refs_2_.refs_3_), channel_id=1, source_target_pairs={{0,8},{28,20},{1,9},{29,21},{2,10},{30,22},{3,11},{31,23}} | collective-permute-start | bytes 786440 | tf_op jit(solution)/shard_map/ppermute | solution.py:408
  12.9 1.3 %collective-permute-start.3 = (f32[128,512]{1,0:T(8,128)S(1)}, f32[128,512]{1,0:T(8,128)S(1)}, u32[]{:S(2)}, u32[]{:S(2)}) collective-permute-start(f32[128,512]{1,0:T(8,128)S(1)} %shard_map.81.refs_1_.refs_2_.refs_3_), channel_id=1, source_target_pairs={{0,8},{28,20},{1,9},{29,21},{2,10},{30,22},{3,11},{31,23}} | collective-permute-start | bytes 786440 | tf_op jit(solution)/shard_map/ppermute | solution.py:408
  14.2 1.6 %collective-permute-start.6 = (f32[128,512]{1,0:T(8,128)S(1)}, f32[128,512]{1,0:T(8,128)S(1)}, u32[]{:S(2)}, u32[]{:S(2)}) collective-permute-start(f32[128,512]{1,0:T(8,128)S(1)} %get-tuple-element.37.refs_0_.refs_2_), channel_id=1, source_target_pairs={{0,3},{1,2},{2,1},{3,0},{4,7},{5,6},{6,5},{7,4},{8,11},{9,10},{10,... | collective-permute-start | bytes 786440 | tf_op jit(solution)/shard_map/ppermute | solution.py:345
  16.5 4.4 %collective-permute-start.8 = (f32[128,512]{1,0:T(8,128)S(1)}, f32[128,512]{1,0:T(8,128)S(1)}, u32[]{:S(2)}, u32[]{:S(2)}) collective-permute-start(f32[128,512]{1,0:T(8,128)S(1)} %shard_map.89), channel_id=1, source_target_pairs={{0,8},{28,20},{8,16},{20,12},{1,9},{29,21},{9,17},{21,13},{2,10},{... | collective-permute-start | bytes 786440 | tf_op jit(solution)/shard_map/ppermute | solution.py:419
  21.3 2.5 %collective-permute-start.5 = (f32[128,512]{1,0:T(8,128)S(1)}, f32[128,512]{1,0:T(8,128)S(1)}, u32[]{:S(2)}, u32[]{:S(2)}) collective-permute-start(f32[128,512]{1,0:T(8,128)S(1)} %shard_map.84.refs_1_.refs_4_), channel_id=1, source_target_pairs={{0,8},{28,20},{8,16},{20,12},{1,9},{29,21},{9,17},{21,13},{2,10},{... | collective-permute-start | bytes 786440 | tf_op jit(solution)/shard_map/ppermute | solution.py:419
  23.7 2.0 %collective-permute-start.1 = (f32[128,512]{1,0:T(8,128)S(1)}, f32[128,512]{1,0:T(8,128)S(1)}, u32[]{:S(2)}, u32[]{:S(2)}) collective-permute-start(f32[128,512]{1,0:T(8,128)S(1)} %get-tuple-element.37.refs_0_.refs_2_), channel_id=1, source_target_pairs={{0,2},{1,3},{2,0},{3,1},{4,6},{5,7},{6,4},{7,5},{8,10},{9,11},{10,... | collective-permute-start | bytes 786440 | tf_op jit(solution)/shard_map/ppermute | solution.py:345
  25.8 1.6 %collective-permute-start.11 = (f32[128,512]{1,0:T(8,128)S(1)}, f32[128,512]{1,0:T(8,128)S(1)}, u32[]{:S(2)}, u32[]{:S(2)}) collective-permute-start(f32[128,512]{1,0:T(8,128)S(1)} %get-tuple-element.41), channel_id=1, source_target_pairs={{0,1},{1,0},{2,3},{3,2},{4,5},{5,4},{6,7},{7,6},{8,9},{9,8},{10,11... | collective-permute-start | bytes 786440 | tf_op jit(solution)/shard_map/ppermute | solution.py:345
  27.8 1.9 %collective-permute-start.10 = (f32[128,512]{1,0:T(8,128)S(1)}, f32[128,512]{1,0:T(8,128)S(1)}, u32[]{:S(2)}, u32[]{:S(2)}) collective-permute-start(f32[128,512]{1,0:T(8,128)S(1)} %shard_map.91.refs_4_), channel_id=1, source_target_pairs={{0,8},{28,20},{8,16},{20,12},{16,24},{12,4},{1,9},{29,21},{9,17},{... | collective-permute-start | bytes 786440 | tf_op jit(solution)/shard_map/ppermute | solution.py:419
  30.1 1.9 %collective-permute-start.13 = (f32[128,512]{1,0:T(8,128)S(1)}, f32[128,512]{1,0:T(8,128)S(1)}, u32[]{:S(2)}, u32[]{:S(2)}) collective-permute-start(f32[128,512]{1,0:T(8,128)S(1)} %shard_map.92.refs_1_.refs_4_), channel_id=1, source_target_pairs={{0,8},{28,20},{8,16},{20,12},{16,24},{12,4},{1,9},{29,21},{9,17},{... | collective-permute-start | bytes 786440 | tf_op jit(solution)/shard_map/ppermute | solution.py:419
  32.0 3.0 %collective-permute-start.14 = (f32[128,512]{1,0:T(8,128)S(1)}, f32[128,512]{1,0:T(8,128)S(1)}, u32[]{:S(2)}, u32[]{:S(2)}) collective-permute-start(f32[128,512]{1,0:T(8,128)S(1)} %get-tuple-element.42), channel_id=1, source_target_pairs={{0,3},{1,2},{2,1},{3,0},{4,7},{5,6},{6,5},{7,4},{8,11},{9,10},{10,... | collective-permute-start | bytes 786440 | tf_op jit(solution)/shard_map/ppermute | solution.py:345
  35.4 2.6 %collective-permute-start.12 = (f32[128,512]{1,0:T(8,128)S(1)}, f32[128,512]{1,0:T(8,128)S(1)}, u32[]{:S(2)}, u32[]{:S(2)}) collective-permute-start(f32[128,512]{1,0:T(8,128)S(1)} %shard_map.96.refs_4_), channel_id=1, source_target_pairs={{0,8},{28,20},{8,16},{20,12},{16,24},{12,4},{1,9},{29,21},{9,17},{... | collective-permute-start | bytes 786440 | tf_op jit(solution)/shard_map/ppermute | solution.py:419
  38.4 2.4 %collective-permute-start.16 = (f32[128,512]{1,0:T(8,128)S(1)}, f32[128,512]{1,0:T(8,128)S(1)}, u32[]{:S(2)}, u32[]{:S(2)}) collective-permute-start(f32[128,512]{1,0:T(8,128)S(1)} %shard_map.98.refs_3_), channel_id=1, source_target_pairs={{0,8},{28,20},{8,16},{20,12},{16,24},{12,4},{1,9},{29,21},{9,17},{... | collective-permute-start | bytes 786440 | tf_op jit(solution)/shard_map/ppermute | solution.py:419
  40.8 1.5 %collective-permute-start.9 = (f32[128,512]{1,0:T(8,128)S(1)}, f32[128,512]{1,0:T(8,128)S(1)}, u32[]{:S(2)}, u32[]{:S(2)}) collective-permute-start(f32[128,512]{1,0:T(8,128)S(1)} %get-tuple-element.39), channel_id=1, source_target_pairs={{0,2},{1,3},{2,0},{3,1},{4,6},{5,7},{6,4},{7,5},{8,10},{9,11},{10,... | collective-permute-start | bytes 786440 | tf_op jit(solution)/shard_map/ppermute | solution.py:345
  43.3 1.4 %collective-permute-done.16.refs_0_.refs_2_.refs_1_ = f32[128,512]{1,0:T(8,128)S(1)} collective-permute-done((f32[128,512]{1,0:T(8,128)S(1)}, f32[128,512]{1,0:T(8,128)S(1)}, u32[]{:S(2)}, u32[]{:S(2)}) %collective-permute-start.16) | collective-permute-done | bytes 262176 | tf_op jit(solution)/shard_map/ppermute | solution.py:419
  49.4 5.7 %collective-permute-start.21 = (f32[64,512]{1,0:T(8,128)S(1)}, f32[64,512]{1,0:T(8,128)S(1)}, u32[]{:S(2)}, u32[]{:S(2)}) collective-permute-start(f32[64,512]{1,0:T(8,128)S(1)} %get-tuple-element.48), channel_id=1, source_target_pairs={{0,4},{4,0},{1,5},{5,1},{2,6},{6,2},{3,7},{7,3},{8,12},{12,8},{9,1... | collective-permute-start | bytes 393224 | tf_op jit(solution)/shard_map/ppermute | solution.py:348
  55.2 0.8 collective-permute-done.21.refs_1_
  56.2 4.0 %collective-permute-start.23 = (f32[128,512]{1,0:T(8,128)S(1)}, f32[128,512]{1,0:T(8,128)S(1)}, u32[]{:S(2)}, u32[]{:S(2)}) collective-permute-start(f32[128,512]{1,0:T(8,128)S(1)} %shard_map.113), channel_id=1, source_target_pairs={{0,4},{4,0},{1,5},{5,1},{2,6},{6,2},{3,7},{7,3},{8,12},{12,8},{9,1... | collective-permute-start | bytes 786440 | tf_op jit(solution)/shard_map/ppermute | solution.py:348
  63.0 1.5 %collective-permute-start.28 = (f32[64,512]{1,0:T(8,128)S(1)}, f32[64,512]{1,0:T(8,128)S(1)}, u32[]{:S(2)}, u32[]{:S(2)}) collective-permute-start(f32[64,512]{1,0:T(8,128)S(1)} %shard_map.111.refs_6_), channel_id=1, source_target_pairs={{0,1},{1,0},{2,3},{3,2},{4,5},{5,4},{6,7},{7,6},{8,9},{9,8},{10,11... | collective-permute-start | bytes 393224 | tf_op jit(solution)/shard_map/ppermute | solution.py:345
  65.8 1.5 %collective-permute-start.32 = (f32[64,512]{1,0:T(8,128)S(1)}, f32[64,512]{1,0:T(8,128)S(1)}, u32[]{:S(2)}, u32[]{:S(2)}) collective-permute-start(f32[64,512]{1,0:T(8,128)S(1)} %shard_map.121), channel_id=1, source_target_pairs={{0,2},{1,3},{2,0},{3,1},{4,6},{5,7},{6,4},{7,5},{8,10},{9,11},{10,... | collective-permute-start | bytes 393224 | tf_op jit(solution)/shard_map/ppermute | solution.py:345
  68.1 0.8 shard_map.122.refs_7_.refs_11_
  68.9 3.6 %collective-permute-done.31.refs_5_ = f32[64,512]{1,0:T(8,128)S(1)} collective-permute-done((f32[64,512]{1,0:T(8,128)S(1)}, f32[64,512]{1,0:T(8,128)S(1)}, u32[]{:S(2)}, u32[]{:S(2)}) %collective-permute-start.31) | collective-permute-done | bytes 131104 | tf_op jit(solution)/shard_map/ppermute | solution.py:345
  72.5 2.3 %collective-permute-done.32.refs_6_ = f32[64,512]{1,0:T(8,128)S(1)} collective-permute-done((f32[64,512]{1,0:T(8,128)S(1)}, f32[64,512]{1,0:T(8,128)S(1)}, u32[]{:S(2)}, u32[]{:S(2)}) %collective-permute-start.32) | collective-permute-done | bytes 131104 | tf_op jit(solution)/shard_map/ppermute | solution.py:345
  74.9 1.8 %collective-permute-start.35 = (f32[264,128]{1,0:T(8,128)S(1)}, f32[264,128]{1,0:T(8,128)S(1)}, u32[]{:S(2)}, u32[]{:S(2)}) collective-permute-start(f32[264,128]{1,0:T(8,128)S(1)} %shard_map.123.refs_4_.refs_0_), channel_id=1, source_target_pairs={{0,3},{1,2},{2,1},{3,0},{4,7},{5,6},{6,5},{7,4},{8,11},{9,10},{10,... | collective-permute-start | bytes 405512 | tf_op jit(solution)/shard_map/ppermute | solution.py:345
  76.7 0.8 collective-permute-start.34
  77.5 0.9 %collective-permute-start.33 = (f32[264,128]{1,0:T(8,128)S(1)}, f32[264,128]{1,0:T(8,128)S(1)}, u32[]{:S(2)}, u32[]{:S(2)}) collective-permute-start(f32[264,128]{1,0:T(8,128)S(1)} %shard_map.123.refs_4_.refs_0_), channel_id=1, source_target_pairs={{0,1},{1,0},{2,3},{3,2},{4,5},{5,4},{6,7},{7,6},{8,9},{9,8},{10,11... | collective-permute-start | bytes 405512 | tf_op jit(solution)/shard_map/ppermute | solution.py:345
  78.5 3.9 %collective-permute-done.35.refs_7_.refs_3_ = f32[264,128]{1,0:T(8,128)S(1)} collective-permute-done((f32[264,128]{1,0:T(8,128)S(1)}, f32[264,128]{1,0:T(8,128)S(1)}, u32[]{:S(2)}, u32[]{:S(2)}) %collective-permute-start.35) | collective-permute-done | bytes 135200 | tf_op jit(solution)/shard_map/ppermute | solution.py:345
  82.4 2.7 %collective-permute-done.34.refs_6_.refs_2_ = f32[264,128]{1,0:T(8,128)S(1)} collective-permute-done((f32[264,128]{1,0:T(8,128)S(1)}, f32[264,128]{1,0:T(8,128)S(1)}, u32[]{:S(2)}, u32[]{:S(2)}) %collective-permute-start.34) | collective-permute-done | bytes 135200 | tf_op jit(solution)/shard_map/ppermute | solution.py:345
  85.6 0.8 collective-permute-done.37.refs_9_.refs_5_
  87.0 1.1 %shard_map.125 = (bf16[512,512]{1,0:T(8,128)(2,1)}, f32[4]{0:T(128)}) custom-call(f32[264,128]{1,0:T(8,128)S(1)} %shard_map.123.refs_4_.refs_0_, f32[264,128]{1,0:T(8,128)S(1)} %collective-permute-done.33.refs_5_.refs_1_, f32[264,128]{1,0:T(8,128)S(1)} %collective-permute-done.34.refs_6_.refs_2_, f32[264,128]{1,0:T(8,128)S(1)} %collective-permute-done.35.refs_7_.refs_3_, ...), custom_call_target="tpu_custom_call" | custom-call | bytes 1024 | tf_op jit(solution)/shard_map/pallas_call | solution.py:37
  (107 shorter events, 16.1 us)
Async XLA Ops:
  5.4 7.2 %collective-permute-start.2 = (f32[512,512]{1,0:T(8,128)S(1)}, f32[512,512]{1,0:T(8,128)S(1)}, u32[]{:S(2)}, u32[]{:S(2)}) collective-permute-start(f32[512,512]{1,0:T(8,128)S(1)} %get-tuple-element.34.refs_4_), channel_id=1, source_target_pairs={{0,4},{4,0},{1,5},{5,1},{2,6},{6,2},{3,7},{7,3},{8,12},{12,8},{9,1... | collective-permute-start | bytes 3145736 | tf_op jit(solution)/shard_map/ppermute | solution.py:348
  6.1 9.8 %collective-permute-start.4 = (f32[128,512]{1,0:T(8,128)S(1)}, f32[128,512]{1,0:T(8,128)S(1)}, u32[]{:S(2)}, u32[]{:S(2)}) collective-permute-start(f32[128,512]{1,0:T(8,128)S(1)} %get-tuple-element.37.refs_0_.refs_2_), channel_id=1, source_target_pairs={{0,1},{1,0},{2,3},{3,2},{4,5},{5,4},{6,7},{7,6},{8,9},{9,8},{10,11... | collective-permute-start | bytes 786440 | tf_op jit(solution)/shard_map/ppermute | solution.py:345
  9.1 7.4 %collective-permute-start.7 = (f32[128,512]{1,0:T(8,128)S(1)}, f32[128,512]{1,0:T(8,128)S(1)}, u32[]{:S(2)}, u32[]{:S(2)}) collective-permute-start(f32[128,512]{1,0:T(8,128)S(1)} %shard_map.87.refs_2_.refs_3_), channel_id=1, source_target_pairs={{0,8},{28,20},{1,9},{29,21},{2,10},{30,22},{3,11},{31,23}} | collective-permute-start | bytes 786440 | tf_op jit(solution)/shard_map/ppermute | solution.py:408
  12.9 8.3 %collective-permute-start.3 = (f32[128,512]{1,0:T(8,128)S(1)}, f32[128,512]{1,0:T(8,128)S(1)}, u32[]{:S(2)}, u32[]{:S(2)}) collective-permute-start(f32[128,512]{1,0:T(8,128)S(1)} %shard_map.81.refs_1_.refs_2_.refs_3_), channel_id=1, source_target_pairs={{0,8},{28,20},{1,9},{29,21},{2,10},{30,22},{3,11},{31,23}} | collective-permute-start | bytes 786440 | tf_op jit(solution)/shard_map/ppermute | solution.py:408
  14.2 13.2 %collective-permute-start.6 = (f32[128,512]{1,0:T(8,128)S(1)}, f32[128,512]{1,0:T(8,128)S(1)}, u32[]{:S(2)}, u32[]{:S(2)}) collective-permute-start(f32[128,512]{1,0:T(8,128)S(1)} %get-tuple-element.37.refs_0_.refs_2_), channel_id=1, source_target_pairs={{0,3},{1,2},{2,1},{3,0},{4,7},{5,6},{6,5},{7,4},{8,11},{9,10},{10,... | collective-permute-start | bytes 786440 | tf_op jit(solution)/shard_map/ppermute | solution.py:345
  16.5 11.2 %collective-permute-start.8 = (f32[128,512]{1,0:T(8,128)S(1)}, f32[128,512]{1,0:T(8,128)S(1)}, u32[]{:S(2)}, u32[]{:S(2)}) collective-permute-start(f32[128,512]{1,0:T(8,128)S(1)} %shard_map.89), channel_id=1, source_target_pairs={{0,8},{28,20},{8,16},{20,12},{1,9},{29,21},{9,17},{21,13},{2,10},{... | collective-permute-start | bytes 786440 | tf_op jit(solution)/shard_map/ppermute | solution.py:419
  21.3 8.8 %collective-permute-start.5 = (f32[128,512]{1,0:T(8,128)S(1)}, f32[128,512]{1,0:T(8,128)S(1)}, u32[]{:S(2)}, u32[]{:S(2)}) collective-permute-start(f32[128,512]{1,0:T(8,128)S(1)} %shard_map.84.refs_1_.refs_4_), channel_id=1, source_target_pairs={{0,8},{28,20},{8,16},{20,12},{1,9},{29,21},{9,17},{21,13},{2,10},{... | collective-permute-start | bytes 786440 | tf_op jit(solution)/shard_map/ppermute | solution.py:419
  23.7 11.3 %collective-permute-start.1 = (f32[128,512]{1,0:T(8,128)S(1)}, f32[128,512]{1,0:T(8,128)S(1)}, u32[]{:S(2)}, u32[]{:S(2)}) collective-permute-start(f32[128,512]{1,0:T(8,128)S(1)} %get-tuple-element.37.refs_0_.refs_2_), channel_id=1, source_target_pairs={{0,2},{1,3},{2,0},{3,1},{4,6},{5,7},{6,4},{7,5},{8,10},{9,11},{10,... | collective-permute-start | bytes 786440 | tf_op jit(solution)/shard_map/ppermute | solution.py:345
  25.8 9.5 %collective-permute-start.11 = (f32[128,512]{1,0:T(8,128)S(1)}, f32[128,512]{1,0:T(8,128)S(1)}, u32[]{:S(2)}, u32[]{:S(2)}) collective-permute-start(f32[128,512]{1,0:T(8,128)S(1)} %get-tuple-element.41), channel_id=1, source_target_pairs={{0,1},{1,0},{2,3},{3,2},{4,5},{5,4},{6,7},{7,6},{8,9},{9,8},{10,11... | collective-permute-start | bytes 786440 | tf_op jit(solution)/shard_map/ppermute | solution.py:345
  27.8 7.6 %collective-permute-start.10 = (f32[128,512]{1,0:T(8,128)S(1)}, f32[128,512]{1,0:T(8,128)S(1)}, u32[]{:S(2)}, u32[]{:S(2)}) collective-permute-start(f32[128,512]{1,0:T(8,128)S(1)} %shard_map.91.refs_4_), channel_id=1, source_target_pairs={{0,8},{28,20},{8,16},{20,12},{16,24},{12,4},{1,9},{29,21},{9,17},{... | collective-permute-start | bytes 786440 | tf_op jit(solution)/shard_map/ppermute | solution.py:419
  30.1 8.3 %collective-permute-start.13 = (f32[128,512]{1,0:T(8,128)S(1)}, f32[128,512]{1,0:T(8,128)S(1)}, u32[]{:S(2)}, u32[]{:S(2)}) collective-permute-start(f32[128,512]{1,0:T(8,128)S(1)} %shard_map.92.refs_1_.refs_4_), channel_id=1, source_target_pairs={{0,8},{28,20},{8,16},{20,12},{16,24},{12,4},{1,9},{29,21},{9,17},{... | collective-permute-start | bytes 786440 | tf_op jit(solution)/shard_map/ppermute | solution.py:419
  32.0 10.5 %collective-permute-start.14 = (f32[128,512]{1,0:T(8,128)S(1)}, f32[128,512]{1,0:T(8,128)S(1)}, u32[]{:S(2)}, u32[]{:S(2)}) collective-permute-start(f32[128,512]{1,0:T(8,128)S(1)} %get-tuple-element.42), channel_id=1, source_target_pairs={{0,3},{1,2},{2,1},{3,0},{4,7},{5,6},{6,5},{7,4},{8,11},{9,10},{10,... | collective-permute-start | bytes 786440 | tf_op jit(solution)/shard_map/ppermute | solution.py:345
  35.4 7.2 %collective-permute-start.12 = (f32[128,512]{1,0:T(8,128)S(1)}, f32[128,512]{1,0:T(8,128)S(1)}, u32[]{:S(2)}, u32[]{:S(2)}) collective-permute-start(f32[128,512]{1,0:T(8,128)S(1)} %shard_map.96.refs_4_), channel_id=1, source_target_pairs={{0,8},{28,20},{8,16},{20,12},{16,24},{12,4},{1,9},{29,21},{9,17},{... | collective-permute-start | bytes 786440 | tf_op jit(solution)/shard_map/ppermute | solution.py:419
  38.4 6.3 %collective-permute-start.16 = (f32[128,512]{1,0:T(8,128)S(1)}, f32[128,512]{1,0:T(8,128)S(1)}, u32[]{:S(2)}, u32[]{:S(2)}) collective-permute-start(f32[128,512]{1,0:T(8,128)S(1)} %shard_map.98.refs_3_), channel_id=1, source_target_pairs={{0,8},{28,20},{8,16},{20,12},{16,24},{12,4},{1,9},{29,21},{9,17},{... | collective-permute-start | bytes 786440 | tf_op jit(solution)/shard_map/ppermute | solution.py:419
  40.8 6.4 %collective-permute-start.9 = (f32[128,512]{1,0:T(8,128)S(1)}, f32[128,512]{1,0:T(8,128)S(1)}, u32[]{:S(2)}, u32[]{:S(2)}) collective-permute-start(f32[128,512]{1,0:T(8,128)S(1)} %get-tuple-element.39), channel_id=1, source_target_pairs={{0,2},{1,3},{2,0},{3,1},{4,6},{5,7},{6,4},{7,5},{8,10},{9,11},{10,... | collective-permute-start | bytes 786440 | tf_op jit(solution)/shard_map/ppermute | solution.py:345
  42.4 3.5 %collective-permute-start.17 = (f32[128,512]{1,0:T(8,128)S(1)}, f32[128,512]{1,0:T(8,128)S(1)}, u32[]{:S(2)}, u32[]{:S(2)}) collective-permute-start(f32[128,512]{1,0:T(8,128)S(1)} %shard_map.99.refs_5_), channel_id=1, source_target_pairs={{0,4},{4,0},{1,5},{5,1},{2,6},{6,2},{3,7},{7,3},{8,12},{12,8},{9,1... | collective-permute-start | bytes 786440 | tf_op jit(solution)/shard_map/ppermute | solution.py:348
  42.6 4.7 %collective-permute-start.15 = (f32[128,512]{1,0:T(8,128)S(1)}, f32[128,512]{1,0:T(8,128)S(1)}, u32[]{:S(2)}, u32[]{:S(2)}) collective-permute-start(f32[128,512]{1,0:T(8,128)S(1)} %shard_map.101.refs_3_), channel_id=1, source_target_pairs={{8,16},{20,12},{16,24},{12,4},{9,17},{21,13},{17,25},{13,5},{10,18... | collective-permute-start | bytes 786440 | tf_op jit(solution)/shard_map/ppermute | solution.py:419
  44.7 3.3 %collective-permute-start.19 = (f32[128,512]{1,0:T(8,128)S(1)}, f32[128,512]{1,0:T(8,128)S(1)}, u32[]{:S(2)}, u32[]{:S(2)}) collective-permute-start(f32[128,512]{1,0:T(8,128)S(1)} %shard_map.102.refs_3_.refs_7_.refs_2_), channel_id=1, source_target_pairs={{8,16},{20,12},{16,24},{12,4},{9,17},{21,13},{17,25},{13,5},{10,18... | collective-permute-start | bytes 786440 | tf_op jit(solution)/shard_map/ppermute | solution.py:419
  47.3 8.8 %collective-permute-start.18 = (f32[128,512]{1,0:T(8,128)S(1)}, f32[128,512]{1,0:T(8,128)S(1)}, u32[]{:S(2)}, u32[]{:S(2)}) collective-permute-start(f32[128,512]{1,0:T(8,128)S(1)} %shard_map.106.refs_2_), channel_id=1, source_target_pairs={{16,24},{12,4},{17,25},{13,5},{18,26},{14,6},{19,27},{15,7}} | collective-permute-start | bytes 786440 | tf_op jit(solution)/shard_map/ppermute | solution.py:419
  48.0 8.1 %collective-permute-start.22 = (f32[128,512]{1,0:T(8,128)S(1)}, f32[128,512]{1,0:T(8,128)S(1)}, u32[]{:S(2)}, u32[]{:S(2)}) collective-permute-start(f32[128,512]{1,0:T(8,128)S(1)} %shard_map.107.refs_3_.refs_8_.refs_2_), channel_id=1, source_target_pairs={{16,24},{12,4},{17,25},{13,5},{18,26},{14,6},{19,27},{15,7}} | collective-permute-start | bytes 786440 | tf_op jit(solution)/shard_map/ppermute | solution.py:419
  49.4 6.7 %collective-permute-start.21 = (f32[64,512]{1,0:T(8,128)S(1)}, f32[64,512]{1,0:T(8,128)S(1)}, u32[]{:S(2)}, u32[]{:S(2)}) collective-permute-start(f32[64,512]{1,0:T(8,128)S(1)} %get-tuple-element.48), channel_id=1, source_target_pairs={{0,4},{4,0},{1,5},{5,1},{2,6},{6,2},{3,7},{7,3},{8,12},{12,8},{9,1... | collective-permute-start | bytes 393224 | tf_op jit(solution)/shard_map/ppermute | solution.py:348
  55.1 5.1 %collective-permute-start.24 = (f32[128,512]{1,0:T(8,128)S(1)}, f32[128,512]{1,0:T(8,128)S(1)}, u32[]{:S(2)}, u32[]{:S(2)}) collective-permute-start(f32[128,512]{1,0:T(8,128)S(1)} %shard_map.108.refs_3_), channel_id=1, source_target_pairs={{0,4},{4,0},{1,5},{5,1},{2,6},{6,2},{3,7},{7,3},{8,12},{12,8},{9,1... | collective-permute-start | bytes 786440 | tf_op jit(solution)/shard_map/ppermute | solution.py:348
  56.2 5.2 %collective-permute-start.23 = (f32[128,512]{1,0:T(8,128)S(1)}, f32[128,512]{1,0:T(8,128)S(1)}, u32[]{:S(2)}, u32[]{:S(2)}) collective-permute-start(f32[128,512]{1,0:T(8,128)S(1)} %shard_map.113), channel_id=1, source_target_pairs={{0,4},{4,0},{1,5},{5,1},{2,6},{6,2},{3,7},{7,3},{8,12},{12,8},{9,1... | collective-permute-start | bytes 786440 | tf_op jit(solution)/shard_map/ppermute | solution.py:348
  62.6 5.4 %collective-permute-start.29 = (f32[64,512]{1,0:T(8,128)S(1)}, f32[64,512]{1,0:T(8,128)S(1)}, u32[]{:S(2)}, u32[]{:S(2)}) collective-permute-start(f32[64,512]{1,0:T(8,128)S(1)} %get-tuple-element.54), channel_id=1, source_target_pairs={{0,4},{4,0},{1,5},{5,1},{2,6},{6,2},{3,7},{7,3},{8,12},{12,8},{9,1... | collective-permute-start | bytes 393224 | tf_op jit(solution)/shard_map/ppermute | solution.py:348
  63.0 5.9 %collective-permute-start.28 = (f32[64,512]{1,0:T(8,128)S(1)}, f32[64,512]{1,0:T(8,128)S(1)}, u32[]{:S(2)}, u32[]{:S(2)}) collective-permute-start(f32[64,512]{1,0:T(8,128)S(1)} %shard_map.111.refs_6_), channel_id=1, source_target_pairs={{0,1},{1,0},{2,3},{3,2},{4,5},{5,4},{6,7},{7,6},{8,9},{9,8},{10,11... | collective-permute-start | bytes 393224 | tf_op jit(solution)/shard_map/ppermute | solution.py:345
  65.2 7.3 %collective-permute-start.31 = (f32[64,512]{1,0:T(8,128)S(1)}, f32[64,512]{1,0:T(8,128)S(1)}, u32[]{:S(2)}, u32[]{:S(2)}) collective-permute-start(f32[64,512]{1,0:T(8,128)S(1)} %shard_map.120), channel_id=1, source_target_pairs={{0,3},{1,2},{2,1},{3,0},{4,7},{5,6},{6,5},{7,4},{8,11},{9,10},{10,... | collective-permute-start | bytes 393224 | tf_op jit(solution)/shard_map/ppermute | solution.py:345
  65.8 9.0 %collective-permute-start.32 = (f32[64,512]{1,0:T(8,128)S(1)}, f32[64,512]{1,0:T(8,128)S(1)}, u32[]{:S(2)}, u32[]{:S(2)}) collective-permute-start(f32[64,512]{1,0:T(8,128)S(1)} %shard_map.121), channel_id=1, source_target_pairs={{0,2},{1,3},{2,0},{3,1},{4,6},{5,7},{6,4},{7,5},{8,10},{9,11},{10,... | collective-permute-start | bytes 393224 | tf_op jit(solution)/shard_map/ppermute | solution.py:345
  74.9 7.5 %collective-permute-start.35 = (f32[264,128]{1,0:T(8,128)S(1)}, f32[264,128]{1,0:T(8,128)S(1)}, u32[]{:S(2)}, u32[]{:S(2)}) collective-permute-start(f32[264,128]{1,0:T(8,128)S(1)} %shard_map.123.refs_4_.refs_0_), channel_id=1, source_target_pairs={{0,3},{1,2},{2,1},{3,0},{4,7},{5,6},{6,5},{7,4},{8,11},{9,10},{10,... | collective-permute-start | bytes 405512 | tf_op jit(solution)/shard_map/ppermute | solution.py:345
  76.7 8.4 %collective-permute-start.34 = (f32[264,128]{1,0:T(8,128)S(1)}, f32[264,128]{1,0:T(8,128)S(1)}, u32[]{:S(2)}, u32[]{:S(2)}) collective-permute-start(f32[264,128]{1,0:T(8,128)S(1)} %shard_map.123.refs_4_.refs_0_), channel_id=1, source_target_pairs={{0,2},{1,3},{2,0},{3,1},{4,6},{5,7},{6,4},{7,5},{8,10},{9,11},{10,... | collective-permute-start | bytes 405512 | tf_op jit(solution)/shard_map/ppermute | solution.py:345
  77.5 7.7 %collective-permute-start.33 = (f32[264,128]{1,0:T(8,128)S(1)}, f32[264,128]{1,0:T(8,128)S(1)}, u32[]{:S(2)}, u32[]{:S(2)}) collective-permute-start(f32[264,128]{1,0:T(8,128)S(1)} %shard_map.123.refs_4_.refs_0_), channel_id=1, source_target_pairs={{0,1},{1,0},{2,3},{3,2},{4,5},{5,4},{6,7},{7,6},{8,9},{9,8},{10,11... | collective-permute-start | bytes 405512 | tf_op jit(solution)/shard_map/ppermute | solution.py:345
  78.5 7.2 %collective-permute-start.36 = (f32[264,128]{1,0:T(8,128)S(1)}, f32[264,128]{1,0:T(8,128)S(1)}, u32[]{:S(2)}, u32[]{:S(2)}) collective-permute-start(f32[264,128]{1,0:T(8,128)S(1)} %shard_map.123.refs_4_.refs_0_), channel_id=1, source_target_pairs={{0,4},{4,0},{1,5},{5,1},{2,6},{6,2},{3,7},{7,3},{8,12},{12,8},{9,1... | collective-permute-start | bytes 405512 | tf_op jit(solution)/shard_map/ppermute | solution.py:348
  82.4 3.3 %collective-permute-start.38 = (f32[264,128]{1,0:T(8,128)S(1)}, f32[264,128]{1,0:T(8,128)S(1)}, u32[]{:S(2)}, u32[]{:S(2)}) collective-permute-start(f32[264,128]{1,0:T(8,128)S(1)} %collective-permute-done.35.refs_7_.refs_3_), channel_id=1, source_target_pairs={{0,4},{4,0},{1,5},{5,1},{2,6},{6,2},{3,7},{7,3},{8,12},{12,8},{9,1... | collective-permute-start | bytes 405512 | tf_op jit(solution)/shard_map/ppermute | solution.py:348
  (13 other events, 52.2 us)

commit v15 on v12

--- a/solution.py
+++ b/solution.py
@@ -390,7 +390,7 @@
             pairs.append((2 * (n_lat - 1 - p) + 1, 2 * (n_lat - 2 - p) + 1))
         if step == 0:
             acts[order[0]] = call(round_kernel, [bf16(rows, lats)], (act,))[0]
-            for side, dict_ref in enumerate((dict_here, dict_other)):
+            for side, dict_ref in enumerate((dict_other, dict_here)):
                 message = project(order[0], (dict_ref,))
                 sums[side].append((message, 0))
                 got[side].append((lax.ppermute(message, ("lat", "wid"), pairs), 0))
@@ -409,13 +409,13 @@
         if step + 1 < n_tok:
             q = order[step + 1]
             acts[q] = call(round_kernel, [bf16(rows, lats)], (gathered[q],), after=sent)[0]
-            for side, dict_ref in enumerate((dict_here, dict_other)):
+            for side, dict_ref in enumerate((dict_other, dict_here)):
                 sums[side].append((project(q, (dict_ref,)), 0))
         ready = []
         c = step - (n_lat - 1)
         if c >= 0:
             chosen = []
-            for side in (1, 0) if step < steps else (0, 1):
+            for side in range(2):
                 items = [got[side][c + p - 1] for p in places]
                 if n_lat > 4:
                     items = [a[:, col * width : (col + 1) * width] for a, col in items]
@@ -428,8 +428,7 @@
                         after=sent if step < steps else ready_before + chosen,
                     )[0]
                 )
-            hand, mine = chosen if step < steps else chosen[::-1]
-            hands.append((swap(hand), mine))
+            hands.append((swap(chosen[0]), chosen[1]))
             ready += chosen
         stages = [c - 1] if step < steps else [c - 1, c]
         for c in stages:
@@ -445,7 +444,7 @@
             loss = (loss_here,)
             gives.append((keep, swap(give)))
             ready.append(errs[q])
-        stages = [1] if step == steps - 1 else [0, *range(2, n_tok)] if step == steps else []
+        stages = range(n_tok) if step == steps else []
         for c in stages:
             if c < 0:
                 continue

time: 85.7 us -> 84.8 us (0.989)
  waiting for transfers between devices: 16.1 us -> 14.9 us
    ppermute x12, starting transfers between devices: 23.3 us -> 26 us  [body(): got[side].append((lax.ppermute(message, ('lat', 'wid'), pairs), 0))]
    ppermute x12, starting transfers between devices: 19.5 us -> 17.4 us  [across(): return lax.ppermute(array, 'tok', [(t, t ^ q) for t in range(n_tok)])]
    ppermute x14, starting transfers between devices: 12.1 us -> 10.5 us  [swap(): return lax.ppermute(array, 'wid', [(w, w ^ 1) for w in range(n_wid)])]
    ppermute x14, waiting for transfers between devices: 3.23 us -> 2.03 us  [swap(): return lax.ppermute(array, 'wid', [(w, w ^ 1) for w in range(n_wid)])]
    ppermute x2, waiting for transfers between devices: 5.91 us -> 4.71 us  [body(): other = lax.ppermute(loss, 'lat', [(p, p ^ gap) for p in range(n_lat)])]
    ppermute x2, starting transfers between devices: 1.46 us -> 2.61 us  [body(): other = lax.ppermute(loss, 'lat', [(p, p ^ gap) for p in range(n_lat)])]
    ppermute x12, waiting for transfers between devices: 1.62 us -> 2.54 us  [body(): got[side].append((lax.ppermute(message, ('lat', 'wid'), pairs), 0))]
  transfers between devices with their start and end apart: 40 -> 40, of which waited for: 13 -> 8; matrix products, arithmetic and copies ran while one was open for 0% -> 0% of each run, Pallas kernels for 9% -> 9%
where the time goes in v15:
time: 84.8 us; the launch traced here: 84.4 us
  starting transfers between devices  56.5 us (67%)
  waiting for transfers between devices  14.9 us (18%)
  Pallas kernels  11.6 us (14%)
  between operations  1.24 us (1%)
    ppermute x12, starting transfers between devices, body(): got[side].append((lax.ppermute(message, ('lat', 'wid'), pairs), 0))  26 us
    ppermute x12, starting transfers between devices, across(): return lax.ppermute(array, 'tok', [(t, t ^ q) for t in range(n_tok)])  17.4 us
    pallas_call x48, Pallas kernels, call(): pl.pallas_call(run, out_shape=outs, in_specs=list(specs or [VMEM] * len(a...  11.6 us
    ppermute x14, starting transfers between devices, swap(): return lax.ppermute(array, 'wid', [(w, w ^ 1) for w in range(n_wid)])  10.5 us
    ppermute x12, waiting for transfers between devices, across(): return lax.ppermute(array, 'tok', [(t, t ^ q) for t in range(n_tok)])  5.67 us
    ppermute x2, waiting for transfers between devices, body(): other = lax.ppermute(loss, 'lat', [(p, p ^ gap) for p in range(n_lat)])  4.71 us
    ppermute x2, starting transfers between devices, body(): other = lax.ppermute(loss, 'lat', [(p, p ^ gap) for p in range(n_lat)])  2.61 us
    ppermute x12, waiting for transfers between devices, body(): got[side].append((lax.ppermute(message, ('lat', 'wid'), pairs), 0))  2.54 us
  transfers between devices with their start and end apart: 40, of which 8 were waited for; matrix products, arithmetic and copies ran while one was open for 0% of the time, Pallas kernels for 9%

profile of v15, /device:TPU:0, one launch (start us, length us, event | category | flops | bytes accessed | tf_op | source)
XLA Modules:
  0.0 84.4 jit_solution(13454637047400625011)
XLA Ops:
  0.7 2.9 %shard_map.77 = (f32[128,512]{1,0:T(8,128)S(1)}, bf16[512,512]{1,0:T(8,128)(2,1)S(1)}) custom-call(bf16[128,2048]{1,0:T(8,128)(2,1)} %refs_0_.3, bf16[512,2048]{1,0:T(8,128)(2,1)} %refs_1_.1), custom_call_target="tpu_custom_call" | custom-call | bytes 1024 | tf_op jit(solution)/shard_map/pallas_call | solution.py:36
  4.1 1.2 %collective-permute-done.refs_2_.refs_1_ = f32[128,512]{1,0:T(8,128)S(1)} collective-permute-done((f32[128,512]{1,0:T(8,128)S(1)}, f32[128,512]{1,0:T(8,128)S(1)}, u32[]{:S(2)}, u32[]{:S(2)}) %collective-permute-start) | collective-permute-done | bytes 262176 | tf_op jit(solution)/shard_map/ppermute | solution.py:336
  6.1 2.7 %collective-permute-start.3 = (f32[128,512]{1,0:T(8,128)S(1)}, f32[128,512]{1,0:T(8,128)S(1)}, u32[]{:S(2)}, u32[]{:S(2)}) collective-permute-start(f32[128,512]{1,0:T(8,128)S(1)} %get-tuple-element.37.refs_0_.refs_2_), channel_id=1, source_target_pairs={{0,1},{1,0},{2,3},{3,2},{4,5},{5,4},{6,7},{7,6},{8,9},{9,8},{10,11... | collective-permute-start | bytes 786440 | tf_op jit(solution)/shard_map/ppermute | solution.py:333
  9.1 4.2 %collective-permute-start.7 = (f32[128,512]{1,0:T(8,128)S(1)}, f32[128,512]{1,0:T(8,128)S(1)}, u32[]{:S(2)}, u32[]{:S(2)}) collective-permute-start(f32[128,512]{1,0:T(8,128)S(1)} %shard_map.87.refs_2_.refs_3_), channel_id=1, source_target_pairs={{0,8},{28,20},{1,9},{29,21},{2,10},{30,22},{3,11},{31,23}} | collective-permute-start | bytes 786440 | tf_op jit(solution)/shard_map/ppermute | solution.py:396
  13.6 1.3 %collective-permute-start.2 = (f32[128,512]{1,0:T(8,128)S(1)}, f32[128,512]{1,0:T(8,128)S(1)}, u32[]{:S(2)}, u32[]{:S(2)}) collective-permute-start(f32[128,512]{1,0:T(8,128)S(1)} %shard_map.81.refs_1_.refs_2_.refs_3_), channel_id=1, source_target_pairs={{0,8},{28,20},{1,9},{29,21},{2,10},{30,22},{3,11},{31,23}} | collective-permute-start | bytes 786440 | tf_op jit(solution)/shard_map/ppermute | solution.py:396
  14.9 2.5 %collective-permute-start.5 = (f32[128,512]{1,0:T(8,128)S(1)}, f32[128,512]{1,0:T(8,128)S(1)}, u32[]{:S(2)}, u32[]{:S(2)}) collective-permute-start(f32[128,512]{1,0:T(8,128)S(1)} %get-tuple-element.37.refs_0_.refs_2_), channel_id=1, source_target_pairs={{0,3},{1,2},{2,1},{3,0},{4,7},{5,6},{6,5},{7,4},{8,11},{9,10},{10,... | collective-permute-start | bytes 786440 | tf_op jit(solution)/shard_map/ppermute | solution.py:333
  17.8 3.8 %collective-permute-start.8 = (f32[128,512]{1,0:T(8,128)S(1)}, f32[128,512]{1,0:T(8,128)S(1)}, u32[]{:S(2)}, u32[]{:S(2)}) collective-permute-start(f32[128,512]{1,0:T(8,128)S(1)} %shard_map.89), channel_id=1, source_target_pairs={{0,8},{28,20},{8,16},{20,12},{1,9},{29,21},{9,17},{21,13},{2,10},{... | collective-permute-start | bytes 786440 | tf_op jit(solution)/shard_map/ppermute | solution.py:407
  21.6 1.6 %collective-permute-start.1 = (f32[128,512]{1,0:T(8,128)S(1)}, f32[128,512]{1,0:T(8,128)S(1)}, u32[]{:S(2)}, u32[]{:S(2)}) collective-permute-start(f32[128,512]{1,0:T(8,128)S(1)} %get-tuple-element.37.refs_0_.refs_2_), channel_id=1, source_target_pairs={{0,2},{1,3},{2,0},{3,1},{4,6},{5,7},{6,4},{7,5},{8,10},{9,11},{10,... | collective-permute-start | bytes 786440 | tf_op jit(solution)/shard_map/ppermute | solution.py:333
  23.5 2.1 %collective-permute-start.4 = (f32[128,512]{1,0:T(8,128)S(1)}, f32[128,512]{1,0:T(8,128)S(1)}, u32[]{:S(2)}, u32[]{:S(2)}) collective-permute-start(f32[128,512]{1,0:T(8,128)S(1)} %shard_map.84.refs_1_.refs_4_), channel_id=1, source_target_pairs={{0,8},{28,20},{8,16},{20,12},{1,9},{29,21},{9,17},{21,13},{2,10},{... | collective-permute-start | bytes 786440 | tf_op jit(solution)/shard_map/ppermute | solution.py:407
  25.7 1.6 %collective-permute-start.12 = (f32[128,512]{1,0:T(8,128)S(1)}, f32[128,512]{1,0:T(8,128)S(1)}, u32[]{:S(2)}, u32[]{:S(2)}) collective-permute-start(f32[128,512]{1,0:T(8,128)S(1)} %get-tuple-element.41), channel_id=1, source_target_pairs={{0,1},{1,0},{2,3},{3,2},{4,5},{5,4},{6,7},{7,6},{8,9},{9,8},{10,11... | collective-permute-start | bytes 786440 | tf_op jit(solution)/shard_map/ppermute | solution.py:333
  27.6 2.2 %collective-permute-start.11 = (f32[128,512]{1,0:T(8,128)S(1)}, f32[128,512]{1,0:T(8,128)S(1)}, u32[]{:S(2)}, u32[]{:S(2)}) collective-permute-start(f32[128,512]{1,0:T(8,128)S(1)} %shard_map.91.refs_4_), channel_id=1, source_target_pairs={{0,8},{28,20},{8,16},{20,12},{16,24},{12,4},{1,9},{29,21},{9,17},{... | collective-permute-start | bytes 786440 | tf_op jit(solution)/shard_map/ppermute | solution.py:407
  30.3 3.6 %collective-permute-start.10 = (f32[128,512]{1,0:T(8,128)S(1)}, f32[128,512]{1,0:T(8,128)S(1)}, u32[]{:S(2)}, u32[]{:S(2)}) collective-permute-start(f32[128,512]{1,0:T(8,128)S(1)} %shard_map.92.refs_1_.refs_4_), channel_id=1, source_target_pairs={{0,8},{28,20},{8,16},{20,12},{16,24},{12,4},{1,9},{29,21},{9,17},{... | collective-permute-start | bytes 786440 | tf_op jit(solution)/shard_map/ppermute | solution.py:407
  33.9 1.4 %collective-permute-start.15 = (f32[128,512]{1,0:T(8,128)S(1)}, f32[128,512]{1,0:T(8,128)S(1)}, u32[]{:S(2)}, u32[]{:S(2)}) collective-permute-start(f32[128,512]{1,0:T(8,128)S(1)} %get-tuple-element.42), channel_id=1, source_target_pairs={{0,3},{1,2},{2,1},{3,0},{4,7},{5,6},{6,5},{7,4},{8,11},{9,10},{10,... | collective-permute-start | bytes 786440 | tf_op jit(solution)/shard_map/ppermute | solution.py:333
  35.7 2.5 %collective-permute-start.14 = (f32[128,512]{1,0:T(8,128)S(1)}, f32[128,512]{1,0:T(8,128)S(1)}, u32[]{:S(2)}, u32[]{:S(2)}) collective-permute-start(f32[128,512]{1,0:T(8,128)S(1)} %shard_map.97.refs_4_), channel_id=1, source_target_pairs={{0,8},{28,20},{8,16},{20,12},{16,24},{12,4},{1,9},{29,21},{9,17},{... | collective-permute-start | bytes 786440 | tf_op jit(solution)/shard_map/ppermute | solution.py:407
  38.6 3.6 %collective-permute-start.13 = (f32[128,512]{1,0:T(8,128)S(1)}, f32[128,512]{1,0:T(8,128)S(1)}, u32[]{:S(2)}, u32[]{:S(2)}) collective-permute-start(f32[128,512]{1,0:T(8,128)S(1)} %shard_map.98.refs_3_), channel_id=1, source_target_pairs={{0,8},{28,20},{8,16},{20,12},{16,24},{12,4},{1,9},{29,21},{9,17},{... | collective-permute-start | bytes 786440 | tf_op jit(solution)/shard_map/ppermute | solution.py:407
  42.9 0.7 collective-permute-start.17
  43.6 2.5 %collective-permute-done.13.refs_0_.refs_2_.refs_1_ = f32[128,512]{1,0:T(8,128)S(1)} collective-permute-done((f32[128,512]{1,0:T(8,128)S(1)}, f32[128,512]{1,0:T(8,128)S(1)}, u32[]{:S(2)}, u32[]{:S(2)}) %collective-permute-start.13) | collective-permute-done | bytes 262176 | tf_op jit(solution)/shard_map/ppermute | solution.py:407
  47.6 1.0 %collective-permute-done.9.refs_3_.refs_2_ = f32[128,512]{1,0:T(8,128)S(1)} collective-permute-done((f32[128,512]{1,0:T(8,128)S(1)}, f32[128,512]{1,0:T(8,128)S(1)}, u32[]{:S(2)}, u32[]{:S(2)}) %collective-permute-start.9) | collective-permute-done | bytes 262176 | tf_op jit(solution)/shard_map/ppermute | solution.py:333
  50.1 4.6 %collective-permute-start.23 = (f32[128,512]{1,0:T(8,128)S(1)}, f32[128,512]{1,0:T(8,128)S(1)}, u32[]{:S(2)}, u32[]{:S(2)}) collective-permute-start(f32[128,512]{1,0:T(8,128)S(1)} %shard_map.108.refs_3_), channel_id=1, source_target_pairs={{0,4},{4,0},{1,5},{5,1},{2,6},{6,2},{3,7},{7,3},{8,12},{12,8},{9,1... | collective-permute-start | bytes 786440 | tf_op jit(solution)/shard_map/ppermute | solution.py:336
  55.4 2.2 %collective-permute-start.22 = (f32[128,512]{1,0:T(8,128)S(1)}, f32[128,512]{1,0:T(8,128)S(1)}, u32[]{:S(2)}, u32[]{:S(2)}) collective-permute-start(f32[128,512]{1,0:T(8,128)S(1)} %shard_map.111.refs_6_), channel_id=1, source_target_pairs={{0,4},{4,0},{1,5},{5,1},{2,6},{6,2},{3,7},{7,3},{8,12},{12,8},{9,1... | collective-permute-start | bytes 786440 | tf_op jit(solution)/shard_map/ppermute | solution.py:336
  59.6 1.5 %collective-permute-start.31 = (f32[64,512]{1,0:T(8,128)S(1)}, f32[64,512]{1,0:T(8,128)S(1)}, u32[]{:S(2)}, u32[]{:S(2)}) collective-permute-start(f32[64,512]{1,0:T(8,128)S(1)} %get-tuple-element.57), channel_id=1, source_target_pairs={{0,4},{4,0},{1,5},{5,1},{2,6},{6,2},{3,7},{7,3},{8,12},{12,8},{9,1... | collective-permute-start | bytes 393224 | tf_op jit(solution)/shard_map/ppermute | solution.py:336
  61.2 1.6 %collective-permute-start.28 = (f32[64,512]{1,0:T(8,128)S(1)}, f32[64,512]{1,0:T(8,128)S(1)}, u32[]{:S(2)}, u32[]{:S(2)}) collective-permute-start(f32[64,512]{1,0:T(8,128)S(1)} %shard_map.118), channel_id=1, source_target_pairs={{0,1},{1,0},{2,3},{3,2},{4,5},{5,4},{6,7},{7,6},{8,9},{9,8},{10,11... | collective-permute-start | bytes 393224 | tf_op jit(solution)/shard_map/ppermute | solution.py:333
  62.8 1.7 %collective-permute-start.30 = (f32[64,512]{1,0:T(8,128)S(1)}, f32[64,512]{1,0:T(8,128)S(1)}, u32[]{:S(2)}, u32[]{:S(2)}) collective-permute-start(f32[64,512]{1,0:T(8,128)S(1)} %shard_map.119), channel_id=1, source_target_pairs={{0,3},{1,2},{2,1},{3,0},{4,7},{5,6},{6,5},{7,4},{8,11},{9,10},{10,... | collective-permute-start | bytes 393224 | tf_op jit(solution)/shard_map/ppermute | solution.py:333
  65.0 3.6 %collective-permute-done.24.refs_1_ = f32[8,128]{1,0:T(8,128)S(1)} collective-permute-done((f32[8,128]{1,0:T(8,128)S(1)}, f32[8,128]{1,0:T(8,128)S(1)}, u32[]{:S(2)}, u32[]{:S(2)}) %collective-permute-start.24) | collective-permute-done | bytes 4128 | tf_op jit(solution)/shard_map/ppermute | solution.py:463
  68.6 2.6 %collective-permute-start.25 = (f32[8,128]{1,0:T(8,128)S(1)}, f32[8,128]{1,0:T(8,128)S(1)}, u32[]{:S(2)}, u32[]{:S(2)}) collective-permute-start(f32[8,128]{1,0:T(8,128)S(1)} %shard_map.115.refs_0_), channel_id=1, source_target_pairs={{0,16},{8,24},{16,0},{24,8},{1,17},{9,25},{17,1},{25,9},{2,18},{10... | collective-permute-start | bytes 12296 | tf_op jit(solution)/shard_map/ppermute | solution.py:463
  71.2 0.8 shard_map.121.refs_7_.refs_11_
  72.0 1.1 %collective-permute-done.25.refs_1_ = f32[8,128]{1,0:T(8,128)S(1)} collective-permute-done((f32[8,128]{1,0:T(8,128)S(1)}, f32[8,128]{1,0:T(8,128)S(1)}, u32[]{:S(2)}, u32[]{:S(2)}) %collective-permute-start.25) | collective-permute-done | bytes 4128 | tf_op jit(solution)/shard_map/ppermute | solution.py:463
  73.2 2.6 %collective-permute-start.35 = (f32[264,128]{1,0:T(8,128)S(1)}, f32[264,128]{1,0:T(8,128)S(1)}, u32[]{:S(2)}, u32[]{:S(2)}) collective-permute-start(f32[264,128]{1,0:T(8,128)S(1)} %shard_map.122.refs_4_.refs_0_), channel_id=1, source_target_pairs={{0,3},{1,2},{2,1},{3,0},{4,7},{5,6},{6,5},{7,4},{8,11},{9,10},{10,... | collective-permute-start | bytes 405512 | tf_op jit(solution)/shard_map/ppermute | solution.py:333
  76.8 3.2 %collective-permute-done.35.refs_7_.refs_3_ = f32[264,128]{1,0:T(8,128)S(1)} collective-permute-done((f32[264,128]{1,0:T(8,128)S(1)}, f32[264,128]{1,0:T(8,128)S(1)}, u32[]{:S(2)}, u32[]{:S(2)}) %collective-permute-start.35) | collective-permute-done | bytes 135200 | tf_op jit(solution)/shard_map/ppermute | solution.py:333
  80.0 1.4 %collective-permute-done.34.refs_6_.refs_2_ = f32[264,128]{1,0:T(8,128)S(1)} collective-permute-done((f32[264,128]{1,0:T(8,128)S(1)}, f32[264,128]{1,0:T(8,128)S(1)}, u32[]{:S(2)}, u32[]{:S(2)}) %collective-permute-start.34) | collective-permute-done | bytes 135200 | tf_op jit(solution)/shard_map/ppermute | solution.py:333
  81.9 0.8 collective-permute-done.37.refs_9_.refs_5_
  83.3 1.1 %shard_map.124 = (bf16[512,512]{1,0:T(8,128)(2,1)}, f32[4]{0:T(128)}) custom-call(f32[264,128]{1,0:T(8,128)S(1)} %shard_map.122.refs_4_.refs_0_, f32[264,128]{1,0:T(8,128)S(1)} %collective-permute-done.33.refs_5_.refs_1_, f32[264,128]{1,0:T(8,128)S(1)} %collective-permute-done.34.refs_6_.refs_2_, f32[264,128]{1,0:T(8,128)S(1)} %collective-permute-done.35.refs_7_.refs_3_, ...), custom_call_target="tpu_custom_call" | custom-call | bytes 1024 | tf_op jit(solution)/shard_map/pallas_call | solution.py:36
  (106 shorter events, 13.1 us)
Async XLA Ops:
  6.1 11.3 %collective-permute-start.3 = (f32[128,512]{1,0:T(8,128)S(1)}, f32[128,512]{1,0:T(8,128)S(1)}, u32[]{:S(2)}, u32[]{:S(2)}) collective-permute-start(f32[128,512]{1,0:T(8,128)S(1)} %get-tuple-element.37.refs_0_.refs_2_), channel_id=1, source_target_pairs={{0,1},{1,0},{2,3},{3,2},{4,5},{5,4},{6,7},{7,6},{8,9},{9,8},{10,11... | collective-permute-start | bytes 786440 | tf_op jit(solution)/shard_map/ppermute | solution.py:333
  9.1 8.7 %collective-permute-start.7 = (f32[128,512]{1,0:T(8,128)S(1)}, f32[128,512]{1,0:T(8,128)S(1)}, u32[]{:S(2)}, u32[]{:S(2)}) collective-permute-start(f32[128,512]{1,0:T(8,128)S(1)} %shard_map.87.refs_2_.refs_3_), channel_id=1, source_target_pairs={{0,8},{28,20},{1,9},{29,21},{2,10},{30,22},{3,11},{31,23}} | collective-permute-start | bytes 786440 | tf_op jit(solution)/shard_map/ppermute | solution.py:396
  13.6 9.9 %collective-permute-start.2 = (f32[128,512]{1,0:T(8,128)S(1)}, f32[128,512]{1,0:T(8,128)S(1)}, u32[]{:S(2)}, u32[]{:S(2)}) collective-permute-start(f32[128,512]{1,0:T(8,128)S(1)} %shard_map.81.refs_1_.refs_2_.refs_3_), channel_id=1, source_target_pairs={{0,8},{28,20},{1,9},{29,21},{2,10},{30,22},{3,11},{31,23}} | collective-permute-start | bytes 786440 | tf_op jit(solution)/shard_map/ppermute | solution.py:396
  14.9 12.4 %collective-permute-start.5 = (f32[128,512]{1,0:T(8,128)S(1)}, f32[128,512]{1,0:T(8,128)S(1)}, u32[]{:S(2)}, u32[]{:S(2)}) collective-permute-start(f32[128,512]{1,0:T(8,128)S(1)} %get-tuple-element.37.refs_0_.refs_2_), channel_id=1, source_target_pairs={{0,3},{1,2},{2,1},{3,0},{4,7},{5,6},{6,5},{7,4},{8,11},{9,10},{10,... | collective-permute-start | bytes 786440 | tf_op jit(solution)/shard_map/ppermute | solution.py:333
  17.8 9.8 %collective-permute-start.8 = (f32[128,512]{1,0:T(8,128)S(1)}, f32[128,512]{1,0:T(8,128)S(1)}, u32[]{:S(2)}, u32[]{:S(2)}) collective-permute-start(f32[128,512]{1,0:T(8,128)S(1)} %shard_map.89), channel_id=1, source_target_pairs={{0,8},{28,20},{8,16},{20,12},{1,9},{29,21},{9,17},{21,13},{2,10},{... | collective-permute-start | bytes 786440 | tf_op jit(solution)/shard_map/ppermute | solution.py:407
  21.6 13.7 %collective-permute-start.1 = (f32[128,512]{1,0:T(8,128)S(1)}, f32[128,512]{1,0:T(8,128)S(1)}, u32[]{:S(2)}, u32[]{:S(2)}) collective-permute-start(f32[128,512]{1,0:T(8,128)S(1)} %get-tuple-element.37.refs_0_.refs_2_), channel_id=1, source_target_pairs={{0,2},{1,3},{2,0},{3,1},{4,6},{5,7},{6,4},{7,5},{8,10},{9,11},{10,... | collective-permute-start | bytes 786440 | tf_op jit(solution)/shard_map/ppermute | solution.py:333
  23.5 6.7 %collective-permute-start.4 = (f32[128,512]{1,0:T(8,128)S(1)}, f32[128,512]{1,0:T(8,128)S(1)}, u32[]{:S(2)}, u32[]{:S(2)}) collective-permute-start(f32[128,512]{1,0:T(8,128)S(1)} %shard_map.84.refs_1_.refs_4_), channel_id=1, source_target_pairs={{0,8},{28,20},{8,16},{20,12},{1,9},{29,21},{9,17},{21,13},{2,10},{... | collective-permute-start | bytes 786440 | tf_op jit(solution)/shard_map/ppermute | solution.py:407
  25.7 9.9 %collective-permute-start.12 = (f32[128,512]{1,0:T(8,128)S(1)}, f32[128,512]{1,0:T(8,128)S(1)}, u32[]{:S(2)}, u32[]{:S(2)}) collective-permute-start(f32[128,512]{1,0:T(8,128)S(1)} %get-tuple-element.41), channel_id=1, source_target_pairs={{0,1},{1,0},{2,3},{3,2},{4,5},{5,4},{6,7},{7,6},{8,9},{9,8},{10,11... | collective-permute-start | bytes 786440 | tf_op jit(solution)/shard_map/ppermute | solution.py:333
  27.6 8.0 %collective-permute-start.11 = (f32[128,512]{1,0:T(8,128)S(1)}, f32[128,512]{1,0:T(8,128)S(1)}, u32[]{:S(2)}, u32[]{:S(2)}) collective-permute-start(f32[128,512]{1,0:T(8,128)S(1)} %shard_map.91.refs_4_), channel_id=1, source_target_pairs={{0,8},{28,20},{8,16},{20,12},{16,24},{12,4},{1,9},{29,21},{9,17},{... | collective-permute-start | bytes 786440 | tf_op jit(solution)/shard_map/ppermute | solution.py:407
  30.3 8.2 %collective-permute-start.10 = (f32[128,512]{1,0:T(8,128)S(1)}, f32[128,512]{1,0:T(8,128)S(1)}, u32[]{:S(2)}, u32[]{:S(2)}) collective-permute-start(f32[128,512]{1,0:T(8,128)S(1)} %shard_map.92.refs_1_.refs_4_), channel_id=1, source_target_pairs={{0,8},{28,20},{8,16},{20,12},{16,24},{12,4},{1,9},{29,21},{9,17},{... | collective-permute-start | bytes 786440 | tf_op jit(solution)/shard_map/ppermute | solution.py:407
  33.9 8.9 %collective-permute-start.15 = (f32[128,512]{1,0:T(8,128)S(1)}, f32[128,512]{1,0:T(8,128)S(1)}, u32[]{:S(2)}, u32[]{:S(2)}) collective-permute-start(f32[128,512]{1,0:T(8,128)S(1)} %get-tuple-element.42), channel_id=1, source_target_pairs={{0,3},{1,2},{2,1},{3,0},{4,7},{5,6},{6,5},{7,4},{8,11},{9,10},{10,... | collective-permute-start | bytes 786440 | tf_op jit(solution)/shard_map/ppermute | solution.py:333
  35.7 7.2 %collective-permute-start.14 = (f32[128,512]{1,0:T(8,128)S(1)}, f32[128,512]{1,0:T(8,128)S(1)}, u32[]{:S(2)}, u32[]{:S(2)}) collective-permute-start(f32[128,512]{1,0:T(8,128)S(1)} %shard_map.97.refs_4_), channel_id=1, source_target_pairs={{0,8},{28,20},{8,16},{20,12},{16,24},{12,4},{1,9},{29,21},{9,17},{... | collective-permute-start | bytes 786440 | tf_op jit(solution)/shard_map/ppermute | solution.py:407
  38.6 7.5 %collective-permute-start.13 = (f32[128,512]{1,0:T(8,128)S(1)}, f32[128,512]{1,0:T(8,128)S(1)}, u32[]{:S(2)}, u32[]{:S(2)}) collective-permute-start(f32[128,512]{1,0:T(8,128)S(1)} %shard_map.98.refs_3_), channel_id=1, source_target_pairs={{0,8},{28,20},{8,16},{20,12},{16,24},{12,4},{1,9},{29,21},{9,17},{... | collective-permute-start | bytes 786440 | tf_op jit(solution)/shard_map/ppermute | solution.py:407
  42.2 6.4 %collective-permute-start.9 = (f32[128,512]{1,0:T(8,128)S(1)}, f32[128,512]{1,0:T(8,128)S(1)}, u32[]{:S(2)}, u32[]{:S(2)}) collective-permute-start(f32[128,512]{1,0:T(8,128)S(1)} %get-tuple-element.39), channel_id=1, source_target_pairs={{0,2},{1,3},{2,0},{3,1},{4,6},{5,7},{6,4},{7,5},{8,10},{9,11},{10,... | collective-permute-start | bytes 786440 | tf_op jit(solution)/shard_map/ppermute | solution.py:333
  42.7 4.2 %collective-permute-start.18 = (f32[128,512]{1,0:T(8,128)S(1)}, f32[128,512]{1,0:T(8,128)S(1)}, u32[]{:S(2)}, u32[]{:S(2)}) collective-permute-start(f32[128,512]{1,0:T(8,128)S(1)} %shard_map.99.refs_5_), channel_id=1, source_target_pairs={{0,4},{4,0},{1,5},{5,1},{2,6},{6,2},{3,7},{7,3},{8,12},{12,8},{9,1... | collective-permute-start | bytes 786440 | tf_op jit(solution)/shard_map/ppermute | solution.py:336
  42.9 5.8 %collective-permute-start.17 = (f32[128,512]{1,0:T(8,128)S(1)}, f32[128,512]{1,0:T(8,128)S(1)}, u32[]{:S(2)}, u32[]{:S(2)}) collective-permute-start(f32[128,512]{1,0:T(8,128)S(1)} %shard_map.101.refs_3_), channel_id=1, source_target_pairs={{8,16},{20,12},{16,24},{12,4},{9,17},{21,13},{17,25},{13,5},{10,18... | collective-permute-start | bytes 786440 | tf_op jit(solution)/shard_map/ppermute | solution.py:407
  46.8 7.9 %collective-permute-start.20 = (f32[128,512]{1,0:T(8,128)S(1)}, f32[128,512]{1,0:T(8,128)S(1)}, u32[]{:S(2)}, u32[]{:S(2)}) collective-permute-start(f32[128,512]{1,0:T(8,128)S(1)} %shard_map.103.refs_4_), channel_id=1, source_target_pairs={{0,4},{4,0},{1,5},{5,1},{2,6},{6,2},{3,7},{7,3},{8,12},{12,8},{9,1... | collective-permute-start | bytes 786440 | tf_op jit(solution)/shard_map/ppermute | solution.py:336
  48.6 6.7 %collective-permute-start.21 = (f32[128,512]{1,0:T(8,128)S(1)}, f32[128,512]{1,0:T(8,128)S(1)}, u32[]{:S(2)}, u32[]{:S(2)}) collective-permute-start(f32[128,512]{1,0:T(8,128)S(1)} %shard_map.106.refs_2_), channel_id=1, source_target_pairs={{16,24},{12,4},{17,25},{13,5},{18,26},{14,6},{19,27},{15,7}} | collective-permute-start | bytes 786440 | tf_op jit(solution)/shard_map/ppermute | solution.py:407
  49.4 9.6 %collective-permute-start.19 = (f32[128,512]{1,0:T(8,128)S(1)}, f32[128,512]{1,0:T(8,128)S(1)}, u32[]{:S(2)}, u32[]{:S(2)}) collective-permute-start(f32[128,512]{1,0:T(8,128)S(1)} %shard_map.107.refs_3_.refs_8_), channel_id=1, source_target_pairs={{16,24},{12,4},{17,25},{13,5},{18,26},{14,6},{19,27},{15,7}} | collective-permute-start | bytes 786440 | tf_op jit(solution)/shard_map/ppermute | solution.py:407
  50.1 7.6 %collective-permute-start.23 = (f32[128,512]{1,0:T(8,128)S(1)}, f32[128,512]{1,0:T(8,128)S(1)}, u32[]{:S(2)}, u32[]{:S(2)}) collective-permute-start(f32[128,512]{1,0:T(8,128)S(1)} %shard_map.108.refs_3_), channel_id=1, source_target_pairs={{0,4},{4,0},{1,5},{5,1},{2,6},{6,2},{3,7},{7,3},{8,12},{12,8},{9,1... | collective-permute-start | bytes 786440 | tf_op jit(solution)/shard_map/ppermute | solution.py:336
  58.4 4.4 %collective-permute-start.29 = (f32[64,512]{1,0:T(8,128)S(1)}, f32[64,512]{1,0:T(8,128)S(1)}, u32[]{:S(2)}, u32[]{:S(2)}) collective-permute-start(f32[64,512]{1,0:T(8,128)S(1)} %get-tuple-element.55), channel_id=1, source_target_pairs={{0,4},{4,0},{1,5},{5,1},{2,6},{6,2},{3,7},{7,3},{8,12},{12,8},{9,1... | collective-permute-start | bytes 393224 | tf_op jit(solution)/shard_map/ppermute | solution.py:336
  59.6 4.9 %collective-permute-start.31 = (f32[64,512]{1,0:T(8,128)S(1)}, f32[64,512]{1,0:T(8,128)S(1)}, u32[]{:S(2)}, u32[]{:S(2)}) collective-permute-start(f32[64,512]{1,0:T(8,128)S(1)} %get-tuple-element.57), channel_id=1, source_target_pairs={{0,4},{4,0},{1,5},{5,1},{2,6},{6,2},{3,7},{7,3},{8,12},{12,8},{9,1... | collective-permute-start | bytes 393224 | tf_op jit(solution)/shard_map/ppermute | solution.py:336
  61.1 10.1 %collective-permute-start.26 = (f32[64,512]{1,0:T(8,128)S(1)}, f32[64,512]{1,0:T(8,128)S(1)}, u32[]{:S(2)}, u32[]{:S(2)}) collective-permute-start(f32[64,512]{1,0:T(8,128)S(1)} %get-tuple-element.51), channel_id=1, source_target_pairs={{0,4},{4,0},{1,5},{5,1},{2,6},{6,2},{3,7},{7,3},{8,12},{12,8},{9,1... | collective-permute-start | bytes 393224 | tf_op jit(solution)/shard_map/ppermute | solution.py:336
  61.2 11.9 %collective-permute-start.28 = (f32[64,512]{1,0:T(8,128)S(1)}, f32[64,512]{1,0:T(8,128)S(1)}, u32[]{:S(2)}, u32[]{:S(2)}) collective-permute-start(f32[64,512]{1,0:T(8,128)S(1)} %shard_map.118), channel_id=1, source_target_pairs={{0,1},{1,0},{2,3},{3,2},{4,5},{5,4},{6,7},{7,6},{8,9},{9,8},{10,11... | collective-permute-start | bytes 393224 | tf_op jit(solution)/shard_map/ppermute | solution.py:333
  62.8 10.3 %collective-permute-start.30 = (f32[64,512]{1,0:T(8,128)S(1)}, f32[64,512]{1,0:T(8,128)S(1)}, u32[]{:S(2)}, u32[]{:S(2)}) collective-permute-start(f32[64,512]{1,0:T(8,128)S(1)} %shard_map.119), channel_id=1, source_target_pairs={{0,3},{1,2},{2,1},{3,0},{4,7},{5,6},{6,5},{7,4},{8,11},{9,10},{10,... | collective-permute-start | bytes 393224 | tf_op jit(solution)/shard_map/ppermute | solution.py:333
  64.5 8.6 %collective-permute-start.32 = (f32[64,512]{1,0:T(8,128)S(1)}, f32[64,512]{1,0:T(8,128)S(1)}, u32[]{:S(2)}, u32[]{:S(2)}) collective-permute-start(f32[64,512]{1,0:T(8,128)S(1)} %shard_map.120), channel_id=1, source_target_pairs={{0,2},{1,3},{2,0},{3,1},{4,6},{5,7},{6,4},{7,5},{8,10},{9,11},{10,... | collective-permute-start | bytes 393224 | tf_op jit(solution)/shard_map/ppermute | solution.py:333
  65.0 3.6 %collective-permute-start.24 = (f32[8,128]{1,0:T(8,128)S(1)}, f32[8,128]{1,0:T(8,128)S(1)}, u32[]{:S(2)}, u32[]{:S(2)}) collective-permute-start(f32[8,128]{1,0:T(8,128)S(1)} %get-tuple-element.49.refs_0_), channel_id=1, source_target_pairs={{0,8},{8,0},{16,24},{24,16},{1,9},{9,1},{17,25},{25,17},{2,10},{10... | collective-permute-start | bytes 12296 | tf_op jit(solution)/shard_map/ppermute | solution.py:463
  68.6 4.5 %collective-permute-start.25 = (f32[8,128]{1,0:T(8,128)S(1)}, f32[8,128]{1,0:T(8,128)S(1)}, u32[]{:S(2)}, u32[]{:S(2)}) collective-permute-start(f32[8,128]{1,0:T(8,128)S(1)} %shard_map.115.refs_0_), channel_id=1, source_target_pairs={{0,16},{8,24},{16,0},{24,8},{1,17},{9,25},{17,1},{25,9},{2,18},{10... | collective-permute-start | bytes 12296 | tf_op jit(solution)/shard_map/ppermute | solution.py:463
  73.2 6.7 %collective-permute-start.35 = (f32[264,128]{1,0:T(8,128)S(1)}, f32[264,128]{1,0:T(8,128)S(1)}, u32[]{:S(2)}, u32[]{:S(2)}) collective-permute-start(f32[264,128]{1,0:T(8,128)S(1)} %shard_map.122.refs_4_.refs_0_), channel_id=1, source_target_pairs={{0,3},{1,2},{2,1},{3,0},{4,7},{5,6},{6,5},{7,4},{8,11},{9,10},{10,... | collective-permute-start | bytes 405512 | tf_op jit(solution)/shard_map/ppermute | solution.py:333
  75.9 5.5 %collective-permute-start.34 = (f32[264,128]{1,0:T(8,128)S(1)}, f32[264,128]{1,0:T(8,128)S(1)}, u32[]{:S(2)}, u32[]{:S(2)}) collective-permute-start(f32[264,128]{1,0:T(8,128)S(1)} %shard_map.122.refs_4_.refs_0_), channel_id=1, source_target_pairs={{0,2},{1,3},{2,0},{3,1},{4,6},{5,7},{6,4},{7,5},{8,10},{9,11},{10,... | collective-permute-start | bytes 405512 | tf_op jit(solution)/shard_map/ppermute | solution.py:333
  76.3 5.2 %collective-permute-start.33 = (f32[264,128]{1,0:T(8,128)S(1)}, f32[264,128]{1,0:T(8,128)S(1)}, u32[]{:S(2)}, u32[]{:S(2)}) collective-permute-start(f32[264,128]{1,0:T(8,128)S(1)} %shard_map.122.refs_4_.refs_0_), channel_id=1, source_target_pairs={{0,1},{1,0},{2,3},{3,2},{4,5},{5,4},{6,7},{7,6},{8,9},{9,8},{10,11... | collective-permute-start | bytes 405512 | tf_op jit(solution)/shard_map/ppermute | solution.py:333
  76.8 5.1 %collective-permute-start.36 = (f32[264,128]{1,0:T(8,128)S(1)}, f32[264,128]{1,0:T(8,128)S(1)}, u32[]{:S(2)}, u32[]{:S(2)}) collective-permute-start(f32[264,128]{1,0:T(8,128)S(1)} %shard_map.122.refs_4_.refs_0_), channel_id=1, source_target_pairs={{0,4},{4,0},{1,5},{5,1},{2,6},{6,2},{3,7},{7,3},{8,12},{12,8},{9,1... | collective-permute-start | bytes 405512 | tf_op jit(solution)/shard_map/ppermute | solution.py:336
  (13 other events, 51.9 us)

commit v16 on v15

--- a/solution.py
+++ b/solution.py
@@ -10,6 +10,7 @@
 LEVELS = 4
 BLOCK = 128
 LOSS_ROWS = 8
+LOSS_AREA = 192
 GELU_C = 0.7978845608028654
 GELU_A = 0.044715
 
@@ -167,7 +168,8 @@
     bend = jnp.tanh(inner)
     deriv = 0.5 * (1.0 + bend) + 0.5 * pre * (1.0 - bend * bend) * slope
     hit = mask[mine, :] > 0.0
-    stacked(jnp.where(hit, deriv * total_of([t[...] for t in terms]), 0.0), loss[...], out)
+    total = total_of([t[...] for t in terms])
+    stacked(jnp.where(hit, deriv * total, 0.0), loss[:LOSS_ROWS, :], out)
 
 
 def running_parts(act, dict_ref):
@@ -269,6 +271,11 @@
 
 def collect_kernel(keep, give, out):
     out[...] = keep[...] + give[...]
+
+
+def spread_kernel(loss, out):
+    out[...] = jnp.zeros_like(out)
+    out[:LOSS_ROWS, :] = loss[...]
 
 
 def add_kernel(*refs):
@@ -450,7 +457,10 @@
                 continue
             q = order[c]
             added = call(
-                collect_kernel, [f32(rows // 2, lats)], gives[c], after=sent if step < steps else ()
+                collect_kernel,
+                [f32(rows // 2, lats)],
+                gives[c],
+                after=gacts[1:2] if c == n_tok - 1 else (),
             )[0]
             gacts.append(across(added, q) if q else added)
             ready.append(added)
@@ -458,7 +468,7 @@
             waits[step + 1] += ready
         ready_before = ready
 
-    loss, gap = loss[0], 1
+    loss, gap = call(spread_kernel, [f32(LOSS_AREA, BLOCK)], loss)[0], 1
     while gap < n_lat:
         other = lax.ppermute(loss, "lat", [(p, p ^ gap) for p in range(n_lat)])
         loss = call(add_kernel, [f32(*loss.shape)], (loss, other))[0]

time: 84.8 us -> 86.8 us (1.024)
  waiting for transfers between devices: 14.9 us -> 17.3 us
    ppermute x14, starting transfers between devices: 10.5 us -> 8.88 us  [swap(): return lax.ppermute(array, 'wid', [(w, w ^ 1) for w in range(n_wid)])]
    ppermute x14, waiting for transfers between devices: 2.03 us -> 3.29 us  [swap(): return lax.ppermute(array, 'wid', [(w, w ^ 1) for w in range(n_wid)])]
    ppermute x12, starting transfers between devices: 17.4 us -> 18.5 us  [across(): return lax.ppermute(array, 'tok', [(t, t ^ q) for t in range(n_tok)])]
    pallas_call x48 -> x49, Pallas kernels: 11.6 us -> 11.7 us  [call(): pl.pallas_call(run, out_shape=outs, in_specs=list(specs or [VMEM] * len(a...]
  transfers between devices with their start and end apart: 40 -> 40, of which waited for: 8 -> 10; matrix products, arithmetic and copies ran while one was open for 0% -> 0% of each run, Pallas kernels for 9% -> 9%
where the time goes in v16:
time: 86.8 us; the launch traced here: 86.5 us
  starting transfers between devices  56.2 us (65%)
  waiting for transfers between devices  17.3 us (20%)
  Pallas kernels  11.7 us (13%)
  between operations  1.25 us (1%)
    ppermute x12, starting transfers between devices, body(): got[side].append((lax.ppermute(message, ('lat', 'wid'), pairs), 0))  26 us
    ppermute x12, starting transfers between devices, across(): return lax.ppermute(array, 'tok', [(t, t ^ q) for t in range(n_tok)])  18.5 us
    pallas_call x49, Pallas kernels, call(): pl.pallas_call(run, out_shape=outs, in_specs=list(specs or [VMEM] * len(a...  11.7 us
    ppermute x14, starting transfers between devices, swap(): return lax.ppermute(array, 'wid', [(w, w ^ 1) for w in range(n_wid)])  8.88 us
    ppermute x12, waiting for transfers between devices, across(): return lax.ppermute(array, 'tok', [(t, t ^ q) for t in range(n_tok)])  6.47 us
    ppermute x2, waiting for transfers between devices, body(): other = lax.ppermute(loss, 'lat', [(p, p ^ gap) for p in range(n_lat)])  5.03 us
    ppermute x14, waiting for transfers between devices, swap(): return lax.ppermute(array, 'wid', [(w, w ^ 1) for w in range(n_wid)])  3.29 us
    ppermute x2, starting transfers between devices, body(): other = lax.ppermute(loss, 'lat', [(p, p ^ gap) for p in range(n_lat)])  2.75 us
  transfers between devices with their start and end apart: 40, of which 10 were waited for; matrix products, arithmetic and copies ran while one was open for 0% of the time, Pallas kernels for 9%

profile of v16, /device:TPU:0, one launch (start us, length us, event | category | flops | bytes accessed | tf_op | source)
XLA Modules:
  0.0 86.5 jit_solution(1918751716991799550)
XLA Ops:
  0.7 2.9 %shard_map.77 = (f32[128,512]{1,0:T(8,128)S(1)}, bf16[512,512]{1,0:T(8,128)(2,1)S(1)}) custom-call(bf16[128,2048]{1,0:T(8,128)(2,1)} %refs_0_.3, bf16[512,2048]{1,0:T(8,128)(2,1)} %refs_1_.1), custom_call_target="tpu_custom_call" | custom-call | bytes 1024 | tf_op jit(solution)/shard_map/pallas_call | solution.py:37
  4.1 1.2 %collective-permute-done.refs_2_.refs_1_ = f32[128,512]{1,0:T(8,128)S(1)} collective-permute-done((f32[128,512]{1,0:T(8,128)S(1)}, f32[128,512]{1,0:T(8,128)S(1)}, u32[]{:S(2)}, u32[]{:S(2)}) %collective-permute-start) | collective-permute-done | bytes 262176 | tf_op jit(solution)/shard_map/ppermute | solution.py:343
  6.1 2.7 %collective-permute-start.3 = (f32[128,512]{1,0:T(8,128)S(1)}, f32[128,512]{1,0:T(8,128)S(1)}, u32[]{:S(2)}, u32[]{:S(2)}) collective-permute-start(f32[128,512]{1,0:T(8,128)S(1)} %get-tuple-element.37.refs_0_.refs_2_), channel_id=1, source_target_pairs={{0,1},{1,0},{2,3},{3,2},{4,5},{5,4},{6,7},{7,6},{8,9},{9,8},{10,11... | collective-permute-start | bytes 786440 | tf_op jit(solution)/shard_map/ppermute | solution.py:340
  9.1 4.2 %collective-permute-start.7 = (f32[128,512]{1,0:T(8,128)S(1)}, f32[128,512]{1,0:T(8,128)S(1)}, u32[]{:S(2)}, u32[]{:S(2)}) collective-permute-start(f32[128,512]{1,0:T(8,128)S(1)} %shard_map.87.refs_2_.refs_3_), channel_id=1, source_target_pairs={{0,8},{28,20},{1,9},{29,21},{2,10},{30,22},{3,11},{31,23}} | collective-permute-start | bytes 786440 | tf_op jit(solution)/shard_map/ppermute | solution.py:403
  13.6 1.3 %collective-permute-start.2 = (f32[128,512]{1,0:T(8,128)S(1)}, f32[128,512]{1,0:T(8,128)S(1)}, u32[]{:S(2)}, u32[]{:S(2)}) collective-permute-start(f32[128,512]{1,0:T(8,128)S(1)} %shard_map.81.refs_1_.refs_2_.refs_3_), channel_id=1, source_target_pairs={{0,8},{28,20},{1,9},{29,21},{2,10},{30,22},{3,11},{31,23}} | collective-permute-start | bytes 786440 | tf_op jit(solution)/shard_map/ppermute | solution.py:403
  14.9 2.5 %collective-permute-start.5 = (f32[128,512]{1,0:T(8,128)S(1)}, f32[128,512]{1,0:T(8,128)S(1)}, u32[]{:S(2)}, u32[]{:S(2)}) collective-permute-start(f32[128,512]{1,0:T(8,128)S(1)} %get-tuple-element.37.refs_0_.refs_2_), channel_id=1, source_target_pairs={{0,3},{1,2},{2,1},{3,0},{4,7},{5,6},{6,5},{7,4},{8,11},{9,10},{10,... | collective-permute-start | bytes 786440 | tf_op jit(solution)/shard_map/ppermute | solution.py:340
  17.8 3.8 %collective-permute-start.8 = (f32[128,512]{1,0:T(8,128)S(1)}, f32[128,512]{1,0:T(8,128)S(1)}, u32[]{:S(2)}, u32[]{:S(2)}) collective-permute-start(f32[128,512]{1,0:T(8,128)S(1)} %shard_map.89), channel_id=1, source_target_pairs={{0,8},{28,20},{8,16},{20,12},{1,9},{29,21},{9,17},{21,13},{2,10},{... | collective-permute-start | bytes 786440 | tf_op jit(solution)/shard_map/ppermute | solution.py:414
  21.6 1.6 %collective-permute-start.1 = (f32[128,512]{1,0:T(8,128)S(1)}, f32[128,512]{1,0:T(8,128)S(1)}, u32[]{:S(2)}, u32[]{:S(2)}) collective-permute-start(f32[128,512]{1,0:T(8,128)S(1)} %get-tuple-element.37.refs_0_.refs_2_), channel_id=1, source_target_pairs={{0,2},{1,3},{2,0},{3,1},{4,6},{5,7},{6,4},{7,5},{8,10},{9,11},{10,... | collective-permute-start | bytes 786440 | tf_op jit(solution)/shard_map/ppermute | solution.py:340
  23.5 2.1 %collective-permute-start.4 = (f32[128,512]{1,0:T(8,128)S(1)}, f32[128,512]{1,0:T(8,128)S(1)}, u32[]{:S(2)}, u32[]{:S(2)}) collective-permute-start(f32[128,512]{1,0:T(8,128)S(1)} %shard_map.84.refs_1_.refs_4_), channel_id=1, source_target_pairs={{0,8},{28,20},{8,16},{20,12},{1,9},{29,21},{9,17},{21,13},{2,10},{... | collective-permute-start | bytes 786440 | tf_op jit(solution)/shard_map/ppermute | solution.py:414
  25.7 1.6 %collective-permute-start.12 = (f32[128,512]{1,0:T(8,128)S(1)}, f32[128,512]{1,0:T(8,128)S(1)}, u32[]{:S(2)}, u32[]{:S(2)}) collective-permute-start(f32[128,512]{1,0:T(8,128)S(1)} %get-tuple-element.41), channel_id=1, source_target_pairs={{0,1},{1,0},{2,3},{3,2},{4,5},{5,4},{6,7},{7,6},{8,9},{9,8},{10,11... | collective-permute-start | bytes 786440 | tf_op jit(solution)/shard_map/ppermute | solution.py:340
  27.6 2.2 %collective-permute-start.11 = (f32[128,512]{1,0:T(8,128)S(1)}, f32[128,512]{1,0:T(8,128)S(1)}, u32[]{:S(2)}, u32[]{:S(2)}) collective-permute-start(f32[128,512]{1,0:T(8,128)S(1)} %shard_map.91.refs_4_), channel_id=1, source_target_pairs={{0,8},{28,20},{8,16},{20,12},{16,24},{12,4},{1,9},{29,21},{9,17},{... | collective-permute-start | bytes 786440 | tf_op jit(solution)/shard_map/ppermute | solution.py:414
  30.3 3.6 %collective-permute-start.10 = (f32[128,512]{1,0:T(8,128)S(1)}, f32[128,512]{1,0:T(8,128)S(1)}, u32[]{:S(2)}, u32[]{:S(2)}) collective-permute-start(f32[128,512]{1,0:T(8,128)S(1)} %shard_map.92.refs_1_.refs_4_), channel_id=1, source_target_pairs={{0,8},{28,20},{8,16},{20,12},{16,24},{12,4},{1,9},{29,21},{9,17},{... | collective-permute-start | bytes 786440 | tf_op jit(solution)/shard_map/ppermute | solution.py:414
  33.9 1.4 %collective-permute-start.15 = (f32[128,512]{1,0:T(8,128)S(1)}, f32[128,512]{1,0:T(8,128)S(1)}, u32[]{:S(2)}, u32[]{:S(2)}) collective-permute-start(f32[128,512]{1,0:T(8,128)S(1)} %get-tuple-element.42), channel_id=1, source_target_pairs={{0,3},{1,2},{2,1},{3,0},{4,7},{5,6},{6,5},{7,4},{8,11},{9,10},{10,... | collective-permute-start | bytes 786440 | tf_op jit(solution)/shard_map/ppermute | solution.py:340
  35.7 2.5 %collective-permute-start.14 = (f32[128,512]{1,0:T(8,128)S(1)}, f32[128,512]{1,0:T(8,128)S(1)}, u32[]{:S(2)}, u32[]{:S(2)}) collective-permute-start(f32[128,512]{1,0:T(8,128)S(1)} %shard_map.97.refs_4_), channel_id=1, source_target_pairs={{0,8},{28,20},{8,16},{20,12},{16,24},{12,4},{1,9},{29,21},{9,17},{... | collective-permute-start | bytes 786440 | tf_op jit(solution)/shard_map/ppermute | solution.py:414
  38.6 3.6 %collective-permute-start.13 = (f32[128,512]{1,0:T(8,128)S(1)}, f32[128,512]{1,0:T(8,128)S(1)}, u32[]{:S(2)}, u32[]{:S(2)}) collective-permute-start(f32[128,512]{1,0:T(8,128)S(1)} %shard_map.98.refs_3_), channel_id=1, source_target_pairs={{0,8},{28,20},{8,16},{20,12},{16,24},{12,4},{1,9},{29,21},{9,17},{... | collective-permute-start | bytes 786440 | tf_op jit(solution)/shard_map/ppermute | solution.py:414
  43.6 2.5 %collective-permute-done.13.refs_0_.refs_2_.refs_1_ = f32[128,512]{1,0:T(8,128)S(1)} collective-permute-done((f32[128,512]{1,0:T(8,128)S(1)}, f32[128,512]{1,0:T(8,128)S(1)}, u32[]{:S(2)}, u32[]{:S(2)}) %collective-permute-start.13) | collective-permute-done | bytes 262176 | tf_op jit(solution)/shard_map/ppermute | solution.py:414
  47.6 1.0 %collective-permute-done.9.refs_3_.refs_2_ = f32[128,512]{1,0:T(8,128)S(1)} collective-permute-done((f32[128,512]{1,0:T(8,128)S(1)}, f32[128,512]{1,0:T(8,128)S(1)}, u32[]{:S(2)}, u32[]{:S(2)}) %collective-permute-start.9) | collective-permute-done | bytes 262176 | tf_op jit(solution)/shard_map/ppermute | solution.py:340
  50.1 4.6 %collective-permute-start.23 = (f32[128,512]{1,0:T(8,128)S(1)}, f32[128,512]{1,0:T(8,128)S(1)}, u32[]{:S(2)}, u32[]{:S(2)}) collective-permute-start(f32[128,512]{1,0:T(8,128)S(1)} %shard_map.108.refs_3_), channel_id=1, source_target_pairs={{0,4},{4,0},{1,5},{5,1},{2,6},{6,2},{3,7},{7,3},{8,12},{12,8},{9,1... | collective-permute-start | bytes 786440 | tf_op jit(solution)/shard_map/ppermute | solution.py:343
  55.4 2.2 %collective-permute-start.22 = (f32[128,512]{1,0:T(8,128)S(1)}, f32[128,512]{1,0:T(8,128)S(1)}, u32[]{:S(2)}, u32[]{:S(2)}) collective-permute-start(f32[128,512]{1,0:T(8,128)S(1)} %shard_map.111.refs_6_), channel_id=1, source_target_pairs={{0,4},{4,0},{1,5},{5,1},{2,6},{6,2},{3,7},{7,3},{8,12},{12,8},{9,1... | collective-permute-start | bytes 786440 | tf_op jit(solution)/shard_map/ppermute | solution.py:343
  57.7 1.3 %collective-permute-done.27.refs_1_ = f32[64,512]{1,0:T(8,128)S(1)} collective-permute-done((f32[64,512]{1,0:T(8,128)S(1)}, f32[64,512]{1,0:T(8,128)S(1)}, u32[]{:S(2)}, u32[]{:S(2)}) %collective-permute-start.27) | collective-permute-done | bytes 131104 | tf_op jit(solution)/shard_map/ppermute | solution.py:343
  59.0 1.6 %collective-permute-start.28 = (f32[64,512]{1,0:T(8,128)S(1)}, f32[64,512]{1,0:T(8,128)S(1)}, u32[]{:S(2)}, u32[]{:S(2)}) collective-permute-start(f32[64,512]{1,0:T(8,128)S(1)} %shard_map.119), channel_id=1, source_target_pairs={{0,1},{1,0},{2,3},{3,2},{4,5},{5,4},{6,7},{7,6},{8,9},{9,8},{10,11... | collective-permute-start | bytes 393224 | tf_op jit(solution)/shard_map/ppermute | solution.py:340
  63.3 1.7 %collective-permute-start.30 = (f32[64,512]{1,0:T(8,128)S(1)}, f32[64,512]{1,0:T(8,128)S(1)}, u32[]{:S(2)}, u32[]{:S(2)}) collective-permute-start(f32[64,512]{1,0:T(8,128)S(1)} %shard_map.120), channel_id=1, source_target_pairs={{0,3},{1,2},{2,1},{3,0},{4,7},{5,6},{6,5},{7,4},{8,11},{9,10},{10,... | collective-permute-start | bytes 393224 | tf_op jit(solution)/shard_map/ppermute | solution.py:340
  65.0 1.6 %collective-permute-start.32 = (f32[64,512]{1,0:T(8,128)S(1)}, f32[64,512]{1,0:T(8,128)S(1)}, u32[]{:S(2)}, u32[]{:S(2)}) collective-permute-start(f32[64,512]{1,0:T(8,128)S(1)} %shard_map.121), channel_id=1, source_target_pairs={{0,2},{1,3},{2,0},{3,1},{4,6},{5,7},{6,4},{7,5},{8,10},{9,11},{10,... | collective-permute-start | bytes 393224 | tf_op jit(solution)/shard_map/ppermute | solution.py:340
  66.6 0.9 %collective-permute-done.24.refs_1_ = f32[192,128]{1,0:T(8,128)S(1)} collective-permute-done((f32[192,128]{1,0:T(8,128)S(1)}, f32[192,128]{1,0:T(8,128)S(1)}, u32[]{:S(2)}, u32[]{:S(2)}) %collective-permute-start.24) | collective-permute-done | bytes 98336 | tf_op jit(solution)/shard_map/ppermute | solution.py:473
  67.5 2.1 %collective-permute-start.25 = (f32[192,128]{1,0:T(8,128)S(1)}, f32[192,128]{1,0:T(8,128)S(1)}, u32[]{:S(2)}, u32[]{:S(2)}) collective-permute-start(f32[192,128]{1,0:T(8,128)S(1)} %shard_map.116.refs_0_), channel_id=1, source_target_pairs={{0,16},{8,24},{16,0},{24,8},{1,17},{9,25},{17,1},{25,9},{2,18},{10... | collective-permute-start | bytes 294920 | tf_op jit(solution)/shard_map/ppermute | solution.py:473
  70.4 4.1 %collective-permute-done.25.refs_1_ = f32[192,128]{1,0:T(8,128)S(1)} collective-permute-done((f32[192,128]{1,0:T(8,128)S(1)}, f32[192,128]{1,0:T(8,128)S(1)}, u32[]{:S(2)}, u32[]{:S(2)}) %collective-permute-start.25) | collective-permute-done | bytes 98336 | tf_op jit(solution)/shard_map/ppermute | solution.py:473
  74.7 1.7 %collective-permute-start.35 = (f32[264,128]{1,0:T(8,128)S(1)}, f32[264,128]{1,0:T(8,128)S(1)}, u32[]{:S(2)}, u32[]{:S(2)}) collective-permute-start(f32[264,128]{1,0:T(8,128)S(1)} %shard_map.123.refs_4_.refs_0_), channel_id=1, source_target_pairs={{0,3},{1,2},{2,1},{3,0},{4,7},{5,6},{6,5},{7,4},{8,11},{9,10},{10,... | collective-permute-start | bytes 405512 | tf_op jit(solution)/shard_map/ppermute | solution.py:340
  77.0 1.2 %collective-permute-start.33 = (f32[264,128]{1,0:T(8,128)S(1)}, f32[264,128]{1,0:T(8,128)S(1)}, u32[]{:S(2)}, u32[]{:S(2)}) collective-permute-start(f32[264,128]{1,0:T(8,128)S(1)} %shard_map.123.refs_4_.refs_0_), channel_id=1, source_target_pairs={{0,1},{1,0},{2,3},{3,2},{4,5},{5,4},{6,7},{7,6},{8,9},{9,8},{10,11... | collective-permute-start | bytes 405512 | tf_op jit(solution)/shard_map/ppermute | solution.py:340
  78.2 3.8 %collective-permute-done.35.refs_7_.refs_3_ = f32[264,128]{1,0:T(8,128)S(1)} collective-permute-done((f32[264,128]{1,0:T(8,128)S(1)}, f32[264,128]{1,0:T(8,128)S(1)}, u32[]{:S(2)}, u32[]{:S(2)}) %collective-permute-start.35) | collective-permute-done | bytes 135200 | tf_op jit(solution)/shard_map/ppermute | solution.py:340
  82.1 1.4 %collective-permute-done.34.refs_6_.refs_2_ = f32[264,128]{1,0:T(8,128)S(1)} collective-permute-done((f32[264,128]{1,0:T(8,128)S(1)}, f32[264,128]{1,0:T(8,128)S(1)}, u32[]{:S(2)}, u32[]{:S(2)}) %collective-permute-start.34) | collective-permute-done | bytes 135200 | tf_op jit(solution)/shard_map/ppermute | solution.py:340
  84.0 0.8 collective-permute-done.37.refs_9_.refs_5_
  85.3 1.1 %shard_map.125 = (bf16[512,512]{1,0:T(8,128)(2,1)}, f32[4]{0:T(128)}) custom-call(f32[264,128]{1,0:T(8,128)S(1)} %shard_map.123.refs_4_.refs_0_, f32[264,128]{1,0:T(8,128)S(1)} %collective-permute-done.33.refs_5_.refs_1_, f32[264,128]{1,0:T(8,128)S(1)} %collective-permute-done.34.refs_6_.refs_2_, f32[264,128]{1,0:T(8,128)S(1)} %collective-permute-done.35.refs_7_.refs_3_, ...), custom_call_target="tpu_custom_call" | custom-call | bytes 1024 | tf_op jit(solution)/shard_map/pallas_call | solution.py:37
  (107 shorter events, 14.5 us)
Async XLA Ops:
  5.4 3.4 %collective-permute-start.6 = (f32[512,512]{1,0:T(8,128)S(1)}, f32[512,512]{1,0:T(8,128)S(1)}, u32[]{:S(2)}, u32[]{:S(2)}) collective-permute-start(f32[512,512]{1,0:T(8,128)S(1)} %get-tuple-element.34.refs_4_), channel_id=1, source_target_pairs={{0,4},{4,0},{1,5},{5,1},{2,6},{6,2},{3,7},{7,3},{8,12},{12,8},{9,1... | collective-permute-start | bytes 3145736 | tf_op jit(solution)/shard_map/ppermute | solution.py:343
  6.1 11.3 %collective-permute-start.3 = (f32[128,512]{1,0:T(8,128)S(1)}, f32[128,512]{1,0:T(8,128)S(1)}, u32[]{:S(2)}, u32[]{:S(2)}) collective-permute-start(f32[128,512]{1,0:T(8,128)S(1)} %get-tuple-element.37.refs_0_.refs_2_), channel_id=1, source_target_pairs={{0,1},{1,0},{2,3},{3,2},{4,5},{5,4},{6,7},{7,6},{8,9},{9,8},{10,11... | collective-permute-start | bytes 786440 | tf_op jit(solution)/shard_map/ppermute | solution.py:340
  9.1 8.7 %collective-permute-start.7 = (f32[128,512]{1,0:T(8,128)S(1)}, f32[128,512]{1,0:T(8,128)S(1)}, u32[]{:S(2)}, u32[]{:S(2)}) collective-permute-start(f32[128,512]{1,0:T(8,128)S(1)} %shard_map.87.refs_2_.refs_3_), channel_id=1, source_target_pairs={{0,8},{28,20},{1,9},{29,21},{2,10},{30,22},{3,11},{31,23}} | collective-permute-start | bytes 786440 | tf_op jit(solution)/shard_map/ppermute | solution.py:403
  13.6 9.9 %collective-permute-start.2 = (f32[128,512]{1,0:T(8,128)S(1)}, f32[128,512]{1,0:T(8,128)S(1)}, u32[]{:S(2)}, u32[]{:S(2)}) collective-permute-start(f32[128,512]{1,0:T(8,128)S(1)} %shard_map.81.refs_1_.refs_2_.refs_3_), channel_id=1, source_target_pairs={{0,8},{28,20},{1,9},{29,21},{2,10},{30,22},{3,11},{31,23}} | collective-permute-start | bytes 786440 | tf_op jit(solution)/shard_map/ppermute | solution.py:403
  14.9 12.4 %collective-permute-start.5 = (f32[128,512]{1,0:T(8,128)S(1)}, f32[128,512]{1,0:T(8,128)S(1)}, u32[]{:S(2)}, u32[]{:S(2)}) collective-permute-start(f32[128,512]{1,0:T(8,128)S(1)} %get-tuple-element.37.refs_0_.refs_2_), channel_id=1, source_target_pairs={{0,3},{1,2},{2,1},{3,0},{4,7},{5,6},{6,5},{7,4},{8,11},{9,10},{10,... | collective-permute-start | bytes 786440 | tf_op jit(solution)/shard_map/ppermute | solution.py:340
  17.8 9.8 %collective-permute-start.8 = (f32[128,512]{1,0:T(8,128)S(1)}, f32[128,512]{1,0:T(8,128)S(1)}, u32[]{:S(2)}, u32[]{:S(2)}) collective-permute-start(f32[128,512]{1,0:T(8,128)S(1)} %shard_map.89), channel_id=1, source_target_pairs={{0,8},{28,20},{8,16},{20,12},{1,9},{29,21},{9,17},{21,13},{2,10},{... | collective-permute-start | bytes 786440 | tf_op jit(solution)/shard_map/ppermute | solution.py:414
  21.6 13.7 %collective-permute-start.1 = (f32[128,512]{1,0:T(8,128)S(1)}, f32[128,512]{1,0:T(8,128)S(1)}, u32[]{:S(2)}, u32[]{:S(2)}) collective-permute-start(f32[128,512]{1,0:T(8,128)S(1)} %get-tuple-element.37.refs_0_.refs_2_), channel_id=1, source_target_pairs={{0,2},{1,3},{2,0},{3,1},{4,6},{5,7},{6,4},{7,5},{8,10},{9,11},{10,... | collective-permute-start | bytes 786440 | tf_op jit(solution)/shard_map/ppermute | solution.py:340
  23.5 6.7 %collective-permute-start.4 = (f32[128,512]{1,0:T(8,128)S(1)}, f32[128,512]{1,0:T(8,128)S(1)}, u32[]{:S(2)}, u32[]{:S(2)}) collective-permute-start(f32[128,512]{1,0:T(8,128)S(1)} %shard_map.84.refs_1_.refs_4_), channel_id=1, source_target_pairs={{0,8},{28,20},{8,16},{20,12},{1,9},{29,21},{9,17},{21,13},{2,10},{... | collective-permute-start | bytes 786440 | tf_op jit(solution)/shard_map/ppermute | solution.py:414
  25.7 9.9 %collective-permute-start.12 = (f32[128,512]{1,0:T(8,128)S(1)}, f32[128,512]{1,0:T(8,128)S(1)}, u32[]{:S(2)}, u32[]{:S(2)}) collective-permute-start(f32[128,512]{1,0:T(8,128)S(1)} %get-tuple-element.41), channel_id=1, source_target_pairs={{0,1},{1,0},{2,3},{3,2},{4,5},{5,4},{6,7},{7,6},{8,9},{9,8},{10,11... | collective-permute-start | bytes 786440 | tf_op jit(solution)/shard_map/ppermute | solution.py:340
  27.6 8.0 %collective-permute-start.11 = (f32[128,512]{1,0:T(8,128)S(1)}, f32[128,512]{1,0:T(8,128)S(1)}, u32[]{:S(2)}, u32[]{:S(2)}) collective-permute-start(f32[128,512]{1,0:T(8,128)S(1)} %shard_map.91.refs_4_), channel_id=1, source_target_pairs={{0,8},{28,20},{8,16},{20,12},{16,24},{12,4},{1,9},{29,21},{9,17},{... | collective-permute-start | bytes 786440 | tf_op jit(solution)/shard_map/ppermute | solution.py:414
  30.3 8.2 %collective-permute-start.10 = (f32[128,512]{1,0:T(8,128)S(1)}, f32[128,512]{1,0:T(8,128)S(1)}, u32[]{:S(2)}, u32[]{:S(2)}) collective-permute-start(f32[128,512]{1,0:T(8,128)S(1)} %shard_map.92.refs_1_.refs_4_), channel_id=1, source_target_pairs={{0,8},{28,20},{8,16},{20,12},{16,24},{12,4},{1,9},{29,21},{9,17},{... | collective-permute-start | bytes 786440 | tf_op jit(solution)/shard_map/ppermute | solution.py:414
  33.9 8.9 %collective-permute-start.15 = (f32[128,512]{1,0:T(8,128)S(1)}, f32[128,512]{1,0:T(8,128)S(1)}, u32[]{:S(2)}, u32[]{:S(2)}) collective-permute-start(f32[128,512]{1,0:T(8,128)S(1)} %get-tuple-element.42), channel_id=1, source_target_pairs={{0,3},{1,2},{2,1},{3,0},{4,7},{5,6},{6,5},{7,4},{8,11},{9,10},{10,... | collective-permute-start | bytes 786440 | tf_op jit(solution)/shard_map/ppermute | solution.py:340
  35.7 7.2 %collective-permute-start.14 = (f32[128,512]{1,0:T(8,128)S(1)}, f32[128,512]{1,0:T(8,128)S(1)}, u32[]{:S(2)}, u32[]{:S(2)}) collective-permute-start(f32[128,512]{1,0:T(8,128)S(1)} %shard_map.97.refs_4_), channel_id=1, source_target_pairs={{0,8},{28,20},{8,16},{20,12},{16,24},{12,4},{1,9},{29,21},{9,17},{... | collective-permute-start | bytes 786440 | tf_op jit(solution)/shard_map/ppermute | solution.py:414
  38.6 7.5 %collective-permute-start.13 = (f32[128,512]{1,0:T(8,128)S(1)}, f32[128,512]{1,0:T(8,128)S(1)}, u32[]{:S(2)}, u32[]{:S(2)}) collective-permute-start(f32[128,512]{1,0:T(8,128)S(1)} %shard_map.98.refs_3_), channel_id=1, source_target_pairs={{0,8},{28,20},{8,16},{20,12},{16,24},{12,4},{1,9},{29,21},{9,17},{... | collective-permute-start | bytes 786440 | tf_op jit(solution)/shard_map/ppermute | solution.py:414
  42.2 6.4 %collective-permute-start.9 = (f32[128,512]{1,0:T(8,128)S(1)}, f32[128,512]{1,0:T(8,128)S(1)}, u32[]{:S(2)}, u32[]{:S(2)}) collective-permute-start(f32[128,512]{1,0:T(8,128)S(1)} %get-tuple-element.39), channel_id=1, source_target_pairs={{0,2},{1,3},{2,0},{3,1},{4,6},{5,7},{6,4},{7,5},{8,10},{9,11},{10,... | collective-permute-start | bytes 786440 | tf_op jit(solution)/shard_map/ppermute | solution.py:340
  42.7 4.2 %collective-permute-start.18 = (f32[128,512]{1,0:T(8,128)S(1)}, f32[128,512]{1,0:T(8,128)S(1)}, u32[]{:S(2)}, u32[]{:S(2)}) collective-permute-start(f32[128,512]{1,0:T(8,128)S(1)} %shard_map.99.refs_5_), channel_id=1, source_target_pairs={{0,4},{4,0},{1,5},{5,1},{2,6},{6,2},{3,7},{7,3},{8,12},{12,8},{9,1... | collective-permute-start | bytes 786440 | tf_op jit(solution)/shard_map/ppermute | solution.py:343
  42.9 5.8 %collective-permute-start.17 = (f32[128,512]{1,0:T(8,128)S(1)}, f32[128,512]{1,0:T(8,128)S(1)}, u32[]{:S(2)}, u32[]{:S(2)}) collective-permute-start(f32[128,512]{1,0:T(8,128)S(1)} %shard_map.101.refs_3_), channel_id=1, source_target_pairs={{8,16},{20,12},{16,24},{12,4},{9,17},{21,13},{17,25},{13,5},{10,18... | collective-permute-start | bytes 786440 | tf_op jit(solution)/shard_map/ppermute | solution.py:414
  46.8 7.9 %collective-permute-start.20 = (f32[128,512]{1,0:T(8,128)S(1)}, f32[128,512]{1,0:T(8,128)S(1)}, u32[]{:S(2)}, u32[]{:S(2)}) collective-permute-start(f32[128,512]{1,0:T(8,128)S(1)} %shard_map.103.refs_4_), channel_id=1, source_target_pairs={{0,4},{4,0},{1,5},{5,1},{2,6},{6,2},{3,7},{7,3},{8,12},{12,8},{9,1... | collective-permute-start | bytes 786440 | tf_op jit(solution)/shard_map/ppermute | solution.py:343
  48.6 6.7 %collective-permute-start.21 = (f32[128,512]{1,0:T(8,128)S(1)}, f32[128,512]{1,0:T(8,128)S(1)}, u32[]{:S(2)}, u32[]{:S(2)}) collective-permute-start(f32[128,512]{1,0:T(8,128)S(1)} %shard_map.106.refs_2_), channel_id=1, source_target_pairs={{16,24},{12,4},{17,25},{13,5},{18,26},{14,6},{19,27},{15,7}} | collective-permute-start | bytes 786440 | tf_op jit(solution)/shard_map/ppermute | solution.py:414
  49.4 12.0 %collective-permute-start.19 = (f32[128,512]{1,0:T(8,128)S(1)}, f32[128,512]{1,0:T(8,128)S(1)}, u32[]{:S(2)}, u32[]{:S(2)}) collective-permute-start(f32[128,512]{1,0:T(8,128)S(1)} %shard_map.107.refs_3_.refs_8_), channel_id=1, source_target_pairs={{16,24},{12,4},{17,25},{13,5},{18,26},{14,6},{19,27},{15,7}} | collective-permute-start | bytes 786440 | tf_op jit(solution)/shard_map/ppermute | solution.py:414
  50.1 10.5 %collective-permute-start.23 = (f32[128,512]{1,0:T(8,128)S(1)}, f32[128,512]{1,0:T(8,128)S(1)}, u32[]{:S(2)}, u32[]{:S(2)}) collective-permute-start(f32[128,512]{1,0:T(8,128)S(1)} %shard_map.108.refs_3_), channel_id=1, source_target_pairs={{0,4},{4,0},{1,5},{5,1},{2,6},{6,2},{3,7},{7,3},{8,12},{12,8},{9,1... | collective-permute-start | bytes 786440 | tf_op jit(solution)/shard_map/ppermute | solution.py:343
  55.4 6.0 %collective-permute-start.22 = (f32[128,512]{1,0:T(8,128)S(1)}, f32[128,512]{1,0:T(8,128)S(1)}, u32[]{:S(2)}, u32[]{:S(2)}) collective-permute-start(f32[128,512]{1,0:T(8,128)S(1)} %shard_map.111.refs_6_), channel_id=1, source_target_pairs={{0,4},{4,0},{1,5},{5,1},{2,6},{6,2},{3,7},{7,3},{8,12},{12,8},{9,1... | collective-permute-start | bytes 786440 | tf_op jit(solution)/shard_map/ppermute | solution.py:343
  59.0 6.0 %collective-permute-start.28 = (f32[64,512]{1,0:T(8,128)S(1)}, f32[64,512]{1,0:T(8,128)S(1)}, u32[]{:S(2)}, u32[]{:S(2)}) collective-permute-start(f32[64,512]{1,0:T(8,128)S(1)} %shard_map.119), channel_id=1, source_target_pairs={{0,1},{1,0},{2,3},{3,2},{4,5},{5,4},{6,7},{7,6},{8,9},{9,8},{10,11... | collective-permute-start | bytes 393224 | tf_op jit(solution)/shard_map/ppermute | solution.py:340
  62.6 4.9 %collective-permute-start.24 = (f32[192,128]{1,0:T(8,128)S(1)}, f32[192,128]{1,0:T(8,128)S(1)}, u32[]{:S(2)}, u32[]{:S(2)}) collective-permute-start(f32[192,128]{1,0:T(8,128)S(1)} %shard_map.115.refs_0_), channel_id=1, source_target_pairs={{0,8},{8,0},{16,24},{24,16},{1,9},{9,1},{17,25},{25,17},{2,10},{10... | collective-permute-start | bytes 294920 | tf_op jit(solution)/shard_map/ppermute | solution.py:473
  63.3 6.3 %collective-permute-start.26 = (f32[64,512]{1,0:T(8,128)S(1)}, f32[64,512]{1,0:T(8,128)S(1)}, u32[]{:S(2)}, u32[]{:S(2)}) collective-permute-start(f32[64,512]{1,0:T(8,128)S(1)} %get-tuple-element.51), channel_id=1, source_target_pairs={{0,4},{4,0},{1,5},{5,1},{2,6},{6,2},{3,7},{7,3},{8,12},{12,8},{9,1... | collective-permute-start | bytes 393224 | tf_op jit(solution)/shard_map/ppermute | solution.py:343
  63.3 11.2 %collective-permute-start.30 = (f32[64,512]{1,0:T(8,128)S(1)}, f32[64,512]{1,0:T(8,128)S(1)}, u32[]{:S(2)}, u32[]{:S(2)}) collective-permute-start(f32[64,512]{1,0:T(8,128)S(1)} %shard_map.120), channel_id=1, source_target_pairs={{0,3},{1,2},{2,1},{3,0},{4,7},{5,6},{6,5},{7,4},{8,11},{9,10},{10,... | collective-permute-start | bytes 393224 | tf_op jit(solution)/shard_map/ppermute | solution.py:340
  65.0 9.5 %collective-permute-start.32 = (f32[64,512]{1,0:T(8,128)S(1)}, f32[64,512]{1,0:T(8,128)S(1)}, u32[]{:S(2)}, u32[]{:S(2)}) collective-permute-start(f32[64,512]{1,0:T(8,128)S(1)} %shard_map.121), channel_id=1, source_target_pairs={{0,2},{1,3},{2,0},{3,1},{4,6},{5,7},{6,4},{7,5},{8,10},{9,11},{10,... | collective-permute-start | bytes 393224 | tf_op jit(solution)/shard_map/ppermute | solution.py:340
  67.5 7.0 %collective-permute-start.25 = (f32[192,128]{1,0:T(8,128)S(1)}, f32[192,128]{1,0:T(8,128)S(1)}, u32[]{:S(2)}, u32[]{:S(2)}) collective-permute-start(f32[192,128]{1,0:T(8,128)S(1)} %shard_map.116.refs_0_), channel_id=1, source_target_pairs={{0,16},{8,24},{16,0},{24,8},{1,17},{9,25},{17,1},{25,9},{2,18},{10... | collective-permute-start | bytes 294920 | tf_op jit(solution)/shard_map/ppermute | solution.py:473
  74.7 7.4 %collective-permute-start.35 = (f32[264,128]{1,0:T(8,128)S(1)}, f32[264,128]{1,0:T(8,128)S(1)}, u32[]{:S(2)}, u32[]{:S(2)}) collective-permute-start(f32[264,128]{1,0:T(8,128)S(1)} %shard_map.123.refs_4_.refs_0_), channel_id=1, source_target_pairs={{0,3},{1,2},{2,1},{3,0},{4,7},{5,6},{6,5},{7,4},{8,11},{9,10},{10,... | collective-permute-start | bytes 405512 | tf_op jit(solution)/shard_map/ppermute | solution.py:340
  76.4 7.1 %collective-permute-start.34 = (f32[264,128]{1,0:T(8,128)S(1)}, f32[264,128]{1,0:T(8,128)S(1)}, u32[]{:S(2)}, u32[]{:S(2)}) collective-permute-start(f32[264,128]{1,0:T(8,128)S(1)} %shard_map.123.refs_4_.refs_0_), channel_id=1, source_target_pairs={{0,2},{1,3},{2,0},{3,1},{4,6},{5,7},{6,4},{7,5},{8,10},{9,11},{10,... | collective-permute-start | bytes 405512 | tf_op jit(solution)/shard_map/ppermute | solution.py:340
  77.0 6.6 %collective-permute-start.33 = (f32[264,128]{1,0:T(8,128)S(1)}, f32[264,128]{1,0:T(8,128)S(1)}, u32[]{:S(2)}, u32[]{:S(2)}) collective-permute-start(f32[264,128]{1,0:T(8,128)S(1)} %shard_map.123.refs_4_.refs_0_), channel_id=1, source_target_pairs={{0,1},{1,0},{2,3},{3,2},{4,5},{5,4},{6,7},{7,6},{8,9},{9,8},{10,11... | collective-permute-start | bytes 405512 | tf_op jit(solution)/shard_map/ppermute | solution.py:340
  78.2 5.7 %collective-permute-start.36 = (f32[264,128]{1,0:T(8,128)S(1)}, f32[264,128]{1,0:T(8,128)S(1)}, u32[]{:S(2)}, u32[]{:S(2)}) collective-permute-start(f32[264,128]{1,0:T(8,128)S(1)} %shard_map.123.refs_4_.refs_0_), channel_id=1, source_target_pairs={{0,4},{4,0},{1,5},{5,1},{2,6},{6,2},{3,7},{7,3},{8,12},{12,8},{9,1... | collective-permute-start | bytes 405512 | tf_op jit(solution)/shard_map/ppermute | solution.py:343
  (13 other events, 47.4 us)

commit v17 on v15

--- a/solution.py
+++ b/solution.py
@@ -374,9 +374,10 @@
     places = list(range(1, n_lat))
     acts, errs, hands, gives, gacts, loss = {}, {}, [], [], [], ()
     sums, got, sent = ([], []), ([], []), []
-    waits = {step: [] for step in range(steps)}
+    waits = {step: ([], []) for step in range(steps)}
     for place, q in enumerate(order[1:]):
-        waits[min(3 + place, steps - 1)].append(resids[q])
+        waits[min(3 + place, steps - 1)][0].append(resids[q])
+    waits[2][0].append(gathered[order[-1]])
 
     def project(q, dicts):
         shape = [f32(rows, width * len(dicts))]
@@ -402,7 +403,7 @@
                     functools.partial(message_kernel, at, [col for _, col in items]),
                     [f32(rows, width)],
                     [array for array, _ in items],
-                    after=sent + (waits[step] if side == 0 else []) if step > 1 else (),
+                    after=sent + waits[step][side] if step > 1 else (),
                 )[0]
                 got[side].append((lax.ppermute(message, ("lat", "wid"), pairs), 0))
                 sent = [message]
@@ -455,7 +456,7 @@
             gacts.append(across(added, q) if q else added)
             ready.append(added)
         if step + 1 < steps:
-            waits[step + 1] += ready
+            waits[step + 1][0].extend(ready)
         ready_before = ready
 
     loss, gap = loss[0], 1

time: 84.8 us -> 87 us (1.026)
  starting transfers between devices: 56.5 us -> 58.9 us
    ppermute x12, starting transfers between devices: 26 us -> 27.7 us  [body(): got[side].append((lax.ppermute(message, ('lat', 'wid'), pairs), 0))]
    ppermute x2, starting transfers between devices: 2.61 us -> 3.9 us  [body(): other = lax.ppermute(loss, 'lat', [(p, p ^ gap) for p in range(n_lat)])]
    ppermute x12, starting transfers between devices: 17.4 us -> 16.4 us  [across(): return lax.ppermute(array, 'tok', [(t, t ^ q) for t in range(n_tok)])]
  transfers between devices with their start and end apart: 40 -> 40, of which waited for: 8 -> 10; matrix products, arithmetic and copies ran while one was open for 0% -> 0% of each run, Pallas kernels for 9% -> 8%
where the time goes in v17:
time: 87 us; the launch traced here: 86.6 us
  starting transfers between devices  58.9 us (68%)
  waiting for transfers between devices  14.9 us (17%)
  Pallas kernels  11.6 us (13%)
  between operations  1.24 us (1%)
    ppermute x12, starting transfers between devices, body(): got[side].append((lax.ppermute(message, ('lat', 'wid'), pairs), 0))  27.7 us
    ppermute x12, starting transfers between devices, across(): return lax.ppermute(array, 'tok', [(t, t ^ q) for t in range(n_tok)])  16.4 us
    pallas_call x48, Pallas kernels, call(): pl.pallas_call(run, out_shape=outs, in_specs=list(specs or [VMEM] * len(a...  11.6 us
    ppermute x14, starting transfers between devices, swap(): return lax.ppermute(array, 'wid', [(w, w ^ 1) for w in range(n_wid)])  10.9 us
    ppermute x12, waiting for transfers between devices, across(): return lax.ppermute(array, 'tok', [(t, t ^ q) for t in range(n_tok)])  6.2 us
    ppermute x2, waiting for transfers between devices, body(): other = lax.ppermute(loss, 'lat', [(p, p ^ gap) for p in range(n_lat)])  4.4 us
    ppermute x2, starting transfers between devices, body(): other = lax.ppermute(loss, 'lat', [(p, p ^ gap) for p in range(n_lat)])  3.9 us
    ppermute x12, waiting for transfers between devices, body(): got[side].append((lax.ppermute(message, ('lat', 'wid'), pairs), 0))  2.24 us
  transfers between devices with their start and end apart: 40, of which 10 were waited for; matrix products, arithmetic and copies ran while one was open for 0% of the time, Pallas kernels for 8%

profile of v17, /device:TPU:0, one launch (start us, length us, event | category | flops | bytes accessed | tf_op | source)
XLA Modules:
  0.0 86.6 jit_solution(16555105364394078899)
XLA Ops:
  0.7 2.9 %shard_map.77 = (f32[128,512]{1,0:T(8,128)S(1)}, bf16[512,512]{1,0:T(8,128)(2,1)S(1)}) custom-call(bf16[128,2048]{1,0:T(8,128)(2,1)} %refs_0_.3, bf16[512,2048]{1,0:T(8,128)(2,1)} %refs_1_.1), custom_call_target="tpu_custom_call" | custom-call | bytes 1024 | tf_op jit(solution)/shard_map/pallas_call | solution.py:36
  4.1 1.2 %collective-permute-done.refs_2_.refs_1_ = f32[128,512]{1,0:T(8,128)S(1)} collective-permute-done((f32[128,512]{1,0:T(8,128)S(1)}, f32[128,512]{1,0:T(8,128)S(1)}, u32[]{:S(2)}, u32[]{:S(2)}) %collective-permute-start) | collective-permute-done | bytes 262176 | tf_op jit(solution)/shard_map/ppermute | solution.py:336
  6.1 2.7 %collective-permute-start.3 = (f32[128,512]{1,0:T(8,128)S(1)}, f32[128,512]{1,0:T(8,128)S(1)}, u32[]{:S(2)}, u32[]{:S(2)}) collective-permute-start(f32[128,512]{1,0:T(8,128)S(1)} %get-tuple-element.37.refs_0_.refs_2_), channel_id=1, source_target_pairs={{0,1},{1,0},{2,3},{3,2},{4,5},{5,4},{6,7},{7,6},{8,9},{9,8},{10,11... | collective-permute-start | bytes 786440 | tf_op jit(solution)/shard_map/ppermute | solution.py:333
  9.1 4.2 %collective-permute-start.7 = (f32[128,512]{1,0:T(8,128)S(1)}, f32[128,512]{1,0:T(8,128)S(1)}, u32[]{:S(2)}, u32[]{:S(2)}) collective-permute-start(f32[128,512]{1,0:T(8,128)S(1)} %shard_map.87.refs_2_.refs_3_), channel_id=1, source_target_pairs={{0,8},{28,20},{1,9},{29,21},{2,10},{30,22},{3,11},{31,23}} | collective-permute-start | bytes 786440 | tf_op jit(solution)/shard_map/ppermute | solution.py:397
  13.6 1.3 %collective-permute-start.2 = (f32[128,512]{1,0:T(8,128)S(1)}, f32[128,512]{1,0:T(8,128)S(1)}, u32[]{:S(2)}, u32[]{:S(2)}) collective-permute-start(f32[128,512]{1,0:T(8,128)S(1)} %shard_map.81.refs_1_.refs_2_.refs_3_), channel_id=1, source_target_pairs={{0,8},{28,20},{1,9},{29,21},{2,10},{30,22},{3,11},{31,23}} | collective-permute-start | bytes 786440 | tf_op jit(solution)/shard_map/ppermute | solution.py:397
  14.9 2.5 %collective-permute-start.5 = (f32[128,512]{1,0:T(8,128)S(1)}, f32[128,512]{1,0:T(8,128)S(1)}, u32[]{:S(2)}, u32[]{:S(2)}) collective-permute-start(f32[128,512]{1,0:T(8,128)S(1)} %get-tuple-element.37.refs_0_.refs_2_), channel_id=1, source_target_pairs={{0,3},{1,2},{2,1},{3,0},{4,7},{5,6},{6,5},{7,4},{8,11},{9,10},{10,... | collective-permute-start | bytes 786440 | tf_op jit(solution)/shard_map/ppermute | solution.py:333
  18.3 3.3 %collective-permute-start.8 = (f32[128,512]{1,0:T(8,128)S(1)}, f32[128,512]{1,0:T(8,128)S(1)}, u32[]{:S(2)}, u32[]{:S(2)}) collective-permute-start(f32[128,512]{1,0:T(8,128)S(1)} %shard_map.89), channel_id=1, source_target_pairs={{0,8},{28,20},{8,16},{20,12},{1,9},{29,21},{9,17},{21,13},{2,10},{... | collective-permute-start | bytes 786440 | tf_op jit(solution)/shard_map/ppermute | solution.py:408
  21.9 2.4 %collective-permute-start.4 = (f32[128,512]{1,0:T(8,128)S(1)}, f32[128,512]{1,0:T(8,128)S(1)}, u32[]{:S(2)}, u32[]{:S(2)}) collective-permute-start(f32[128,512]{1,0:T(8,128)S(1)} %shard_map.84.refs_1_.refs_4_), channel_id=1, source_target_pairs={{0,8},{28,20},{8,16},{20,12},{1,9},{29,21},{9,17},{21,13},{2,10},{... | collective-permute-start | bytes 786440 | tf_op jit(solution)/shard_map/ppermute | solution.py:408
  24.5 1.6 %collective-permute-start.12 = (f32[128,512]{1,0:T(8,128)S(1)}, f32[128,512]{1,0:T(8,128)S(1)}, u32[]{:S(2)}, u32[]{:S(2)}) collective-permute-start(f32[128,512]{1,0:T(8,128)S(1)} %get-tuple-element.41), channel_id=1, source_target_pairs={{0,1},{1,0},{2,3},{3,2},{4,5},{5,4},{6,7},{7,6},{8,9},{9,8},{10,11... | collective-permute-start | bytes 786440 | tf_op jit(solution)/shard_map/ppermute | solution.py:333
  26.4 1.2 %collective-permute-done.1.refs_5_.refs_0_ = f32[128,512]{1,0:T(8,128)S(1)} collective-permute-done((f32[128,512]{1,0:T(8,128)S(1)}, f32[128,512]{1,0:T(8,128)S(1)}, u32[]{:S(2)}, u32[]{:S(2)}) %collective-permute-start.1) | collective-permute-done | bytes 262176 | tf_op jit(solution)/shard_map/ppermute | solution.py:333
  27.6 3.5 %collective-permute-start.11 = (f32[128,512]{1,0:T(8,128)S(1)}, f32[128,512]{1,0:T(8,128)S(1)}, u32[]{:S(2)}, u32[]{:S(2)}) collective-permute-start(f32[128,512]{1,0:T(8,128)S(1)} %shard_map.91.refs_4_), channel_id=1, source_target_pairs={{0,8},{28,20},{8,16},{20,12},{16,24},{12,4},{1,9},{29,21},{9,17},{... | collective-permute-start | bytes 786440 | tf_op jit(solution)/shard_map/ppermute | solution.py:408
  31.5 4.0 %collective-permute-start.10 = (f32[128,512]{1,0:T(8,128)S(1)}, f32[128,512]{1,0:T(8,128)S(1)}, u32[]{:S(2)}, u32[]{:S(2)}) collective-permute-start(f32[128,512]{1,0:T(8,128)S(1)} %shard_map.92.refs_1_.refs_4_), channel_id=1, source_target_pairs={{0,8},{28,20},{8,16},{20,12},{16,24},{12,4},{1,9},{29,21},{9,17},{... | collective-permute-start | bytes 786440 | tf_op jit(solution)/shard_map/ppermute | solution.py:408
  35.5 1.1 %collective-permute-start.15 = (f32[128,512]{1,0:T(8,128)S(1)}, f32[128,512]{1,0:T(8,128)S(1)}, u32[]{:S(2)}, u32[]{:S(2)}) collective-permute-start(f32[128,512]{1,0:T(8,128)S(1)} %get-tuple-element.42), channel_id=1, source_target_pairs={{0,3},{1,2},{2,1},{3,0},{4,7},{5,6},{6,5},{7,4},{8,11},{9,10},{10,... | collective-permute-start | bytes 786440 | tf_op jit(solution)/shard_map/ppermute | solution.py:333
  37.0 3.1 %collective-permute-start.14 = (f32[128,512]{1,0:T(8,128)S(1)}, f32[128,512]{1,0:T(8,128)S(1)}, u32[]{:S(2)}, u32[]{:S(2)}) collective-permute-start(f32[128,512]{1,0:T(8,128)S(1)} %shard_map.97.refs_4_), channel_id=1, source_target_pairs={{0,8},{28,20},{8,16},{20,12},{16,24},{12,4},{1,9},{29,21},{9,17},{... | collective-permute-start | bytes 786440 | tf_op jit(solution)/shard_map/ppermute | solution.py:408
  40.4 3.3 %collective-permute-start.13 = (f32[128,512]{1,0:T(8,128)S(1)}, f32[128,512]{1,0:T(8,128)S(1)}, u32[]{:S(2)}, u32[]{:S(2)}) collective-permute-start(f32[128,512]{1,0:T(8,128)S(1)} %shard_map.98.refs_3_), channel_id=1, source_target_pairs={{0,8},{28,20},{8,16},{20,12},{16,24},{12,4},{1,9},{29,21},{9,17},{... | collective-permute-start | bytes 786440 | tf_op jit(solution)/shard_map/ppermute | solution.py:408
  45.4 2.2 %collective-permute-done.13.refs_0_.refs_2_.refs_1_ = f32[128,512]{1,0:T(8,128)S(1)} collective-permute-done((f32[128,512]{1,0:T(8,128)S(1)}, f32[128,512]{1,0:T(8,128)S(1)}, u32[]{:S(2)}, u32[]{:S(2)}) %collective-permute-start.13) | collective-permute-done | bytes 262176 | tf_op jit(solution)/shard_map/ppermute | solution.py:408
  49.2 1.0 %collective-permute-done.9.refs_3_.refs_2_ = f32[128,512]{1,0:T(8,128)S(1)} collective-permute-done((f32[128,512]{1,0:T(8,128)S(1)}, f32[128,512]{1,0:T(8,128)S(1)}, u32[]{:S(2)}, u32[]{:S(2)}) %collective-permute-start.9) | collective-permute-done | bytes 262176 | tf_op jit(solution)/shard_map/ppermute | solution.py:333
  51.7 4.9 %collective-permute-start.23 = (f32[128,512]{1,0:T(8,128)S(1)}, f32[128,512]{1,0:T(8,128)S(1)}, u32[]{:S(2)}, u32[]{:S(2)}) collective-permute-start(f32[128,512]{1,0:T(8,128)S(1)} %shard_map.108.refs_3_), channel_id=1, source_target_pairs={{0,4},{4,0},{1,5},{5,1},{2,6},{6,2},{3,7},{7,3},{8,12},{12,8},{9,1... | collective-permute-start | bytes 786440 | tf_op jit(solution)/shard_map/ppermute | solution.py:336
  57.3 2.5 %collective-permute-start.22 = (f32[128,512]{1,0:T(8,128)S(1)}, f32[128,512]{1,0:T(8,128)S(1)}, u32[]{:S(2)}, u32[]{:S(2)}) collective-permute-start(f32[128,512]{1,0:T(8,128)S(1)} %shard_map.111.refs_6_), channel_id=1, source_target_pairs={{0,4},{4,0},{1,5},{5,1},{2,6},{6,2},{3,7},{7,3},{8,12},{12,8},{9,1... | collective-permute-start | bytes 786440 | tf_op jit(solution)/shard_map/ppermute | solution.py:336
  61.8 1.5 %collective-permute-start.31 = (f32[64,512]{1,0:T(8,128)S(1)}, f32[64,512]{1,0:T(8,128)S(1)}, u32[]{:S(2)}, u32[]{:S(2)}) collective-permute-start(f32[64,512]{1,0:T(8,128)S(1)} %get-tuple-element.57), channel_id=1, source_target_pairs={{0,4},{4,0},{1,5},{5,1},{2,6},{6,2},{3,7},{7,3},{8,12},{12,8},{9,1... | collective-permute-start | bytes 393224 | tf_op jit(solution)/shard_map/ppermute | solution.py:336
  63.4 1.0 %collective-permute-start.28 = (f32[64,512]{1,0:T(8,128)S(1)}, f32[64,512]{1,0:T(8,128)S(1)}, u32[]{:S(2)}, u32[]{:S(2)}) collective-permute-start(f32[64,512]{1,0:T(8,128)S(1)} %shard_map.118), channel_id=1, source_target_pairs={{0,1},{1,0},{2,3},{3,2},{4,5},{5,4},{6,7},{7,6},{8,9},{9,8},{10,11... | collective-permute-start | bytes 393224 | tf_op jit(solution)/shard_map/ppermute | solution.py:333
  64.4 1.6 %collective-permute-start.30 = (f32[64,512]{1,0:T(8,128)S(1)}, f32[64,512]{1,0:T(8,128)S(1)}, u32[]{:S(2)}, u32[]{:S(2)}) collective-permute-start(f32[64,512]{1,0:T(8,128)S(1)} %shard_map.119), channel_id=1, source_target_pairs={{0,3},{1,2},{2,1},{3,0},{4,7},{5,6},{6,5},{7,4},{8,11},{9,10},{10,... | collective-permute-start | bytes 393224 | tf_op jit(solution)/shard_map/ppermute | solution.py:333
  66.1 1.0 %collective-permute-start.32 = (f32[64,512]{1,0:T(8,128)S(1)}, f32[64,512]{1,0:T(8,128)S(1)}, u32[]{:S(2)}, u32[]{:S(2)}) collective-permute-start(f32[64,512]{1,0:T(8,128)S(1)} %shard_map.120), channel_id=1, source_target_pairs={{0,2},{1,3},{2,0},{3,1},{4,6},{5,7},{6,4},{7,5},{8,10},{9,11},{10,... | collective-permute-start | bytes 393224 | tf_op jit(solution)/shard_map/ppermute | solution.py:333
  67.1 3.6 %collective-permute-done.24.refs_1_ = f32[8,128]{1,0:T(8,128)S(1)} collective-permute-done((f32[8,128]{1,0:T(8,128)S(1)}, f32[8,128]{1,0:T(8,128)S(1)}, u32[]{:S(2)}, u32[]{:S(2)}) %collective-permute-start.24) | collective-permute-done | bytes 4128 | tf_op jit(solution)/shard_map/ppermute | solution.py:464
  70.7 3.9 %collective-permute-start.25 = (f32[8,128]{1,0:T(8,128)S(1)}, f32[8,128]{1,0:T(8,128)S(1)}, u32[]{:S(2)}, u32[]{:S(2)}) collective-permute-start(f32[8,128]{1,0:T(8,128)S(1)} %shard_map.115.refs_0_), channel_id=1, source_target_pairs={{0,16},{8,24},{16,0},{24,8},{1,17},{9,25},{17,1},{25,9},{2,18},{10... | collective-permute-start | bytes 12296 | tf_op jit(solution)/shard_map/ppermute | solution.py:464
  76.3 0.8 collective-permute-start.35
  77.2 1.7 %collective-permute-start.34 = (f32[264,128]{1,0:T(8,128)S(1)}, f32[264,128]{1,0:T(8,128)S(1)}, u32[]{:S(2)}, u32[]{:S(2)}) collective-permute-start(f32[264,128]{1,0:T(8,128)S(1)} %shard_map.122.refs_4_.refs_0_), channel_id=1, source_target_pairs={{0,2},{1,3},{2,0},{3,1},{4,6},{5,7},{6,4},{7,5},{8,10},{9,11},{10,... | collective-permute-start | bytes 405512 | tf_op jit(solution)/shard_map/ppermute | solution.py:333
  78.8 1.1 %collective-permute-start.33 = (f32[264,128]{1,0:T(8,128)S(1)}, f32[264,128]{1,0:T(8,128)S(1)}, u32[]{:S(2)}, u32[]{:S(2)}) collective-permute-start(f32[264,128]{1,0:T(8,128)S(1)} %shard_map.122.refs_4_.refs_0_), channel_id=1, source_target_pairs={{0,1},{1,0},{2,3},{3,2},{4,5},{5,4},{6,7},{7,6},{8,9},{9,8},{10,11... | collective-permute-start | bytes 405512 | tf_op jit(solution)/shard_map/ppermute | solution.py:333
  79.9 2.5 %collective-permute-done.35.refs_7_.refs_3_ = f32[264,128]{1,0:T(8,128)S(1)} collective-permute-done((f32[264,128]{1,0:T(8,128)S(1)}, f32[264,128]{1,0:T(8,128)S(1)}, u32[]{:S(2)}, u32[]{:S(2)}) %collective-permute-start.35) | collective-permute-done | bytes 135200 | tf_op jit(solution)/shard_map/ppermute | solution.py:333
  82.4 1.2 %collective-permute-done.34.refs_6_.refs_2_ = f32[264,128]{1,0:T(8,128)S(1)} collective-permute-done((f32[264,128]{1,0:T(8,128)S(1)}, f32[264,128]{1,0:T(8,128)S(1)}, u32[]{:S(2)}, u32[]{:S(2)}) %collective-permute-start.34) | collective-permute-done | bytes 135200 | tf_op jit(solution)/shard_map/ppermute | solution.py:333
  84.1 0.8 collective-permute-done.37.refs_9_.refs_5_
  85.5 1.1 %shard_map.124 = (bf16[512,512]{1,0:T(8,128)(2,1)}, f32[4]{0:T(128)}) custom-call(f32[264,128]{1,0:T(8,128)S(1)} %shard_map.122.refs_4_.refs_0_, f32[264,128]{1,0:T(8,128)S(1)} %collective-permute-done.33.refs_5_.refs_1_, f32[264,128]{1,0:T(8,128)S(1)} %collective-permute-done.34.refs_6_.refs_2_, f32[264,128]{1,0:T(8,128)S(1)} %collective-permute-done.35.refs_7_.refs_3_, ...), custom_call_target="tpu_custom_call" | custom-call | bytes 1024 | tf_op jit(solution)/shard_map/pallas_call | solution.py:36
  (106 shorter events, 14.7 us)
Async XLA Ops:
  6.1 11.8 %collective-permute-start.3 = (f32[128,512]{1,0:T(8,128)S(1)}, f32[128,512]{1,0:T(8,128)S(1)}, u32[]{:S(2)}, u32[]{:S(2)}) collective-permute-start(f32[128,512]{1,0:T(8,128)S(1)} %get-tuple-element.37.refs_0_.refs_2_), channel_id=1, source_target_pairs={{0,1},{1,0},{2,3},{3,2},{4,5},{5,4},{6,7},{7,6},{8,9},{9,8},{10,11... | collective-permute-start | bytes 786440 | tf_op jit(solution)/shard_map/ppermute | solution.py:333
  9.1 9.2 %collective-permute-start.7 = (f32[128,512]{1,0:T(8,128)S(1)}, f32[128,512]{1,0:T(8,128)S(1)}, u32[]{:S(2)}, u32[]{:S(2)}) collective-permute-start(f32[128,512]{1,0:T(8,128)S(1)} %shard_map.87.refs_2_.refs_3_), channel_id=1, source_target_pairs={{0,8},{28,20},{1,9},{29,21},{2,10},{30,22},{3,11},{31,23}} | collective-permute-start | bytes 786440 | tf_op jit(solution)/shard_map/ppermute | solution.py:397
  13.6 8.3 %collective-permute-start.2 = (f32[128,512]{1,0:T(8,128)S(1)}, f32[128,512]{1,0:T(8,128)S(1)}, u32[]{:S(2)}, u32[]{:S(2)}) collective-permute-start(f32[128,512]{1,0:T(8,128)S(1)} %shard_map.81.refs_1_.refs_2_.refs_3_), channel_id=1, source_target_pairs={{0,8},{28,20},{1,9},{29,21},{2,10},{30,22},{3,11},{31,23}} | collective-permute-start | bytes 786440 | tf_op jit(solution)/shard_map/ppermute | solution.py:397
  14.9 11.2 %collective-permute-start.5 = (f32[128,512]{1,0:T(8,128)S(1)}, f32[128,512]{1,0:T(8,128)S(1)}, u32[]{:S(2)}, u32[]{:S(2)}) collective-permute-start(f32[128,512]{1,0:T(8,128)S(1)} %get-tuple-element.37.refs_0_.refs_2_), channel_id=1, source_target_pairs={{0,3},{1,2},{2,1},{3,0},{4,7},{5,6},{6,5},{7,4},{8,11},{9,10},{10,... | collective-permute-start | bytes 786440 | tf_op jit(solution)/shard_map/ppermute | solution.py:333
  17.4 10.2 %collective-permute-start.1 = (f32[128,512]{1,0:T(8,128)S(1)}, f32[128,512]{1,0:T(8,128)S(1)}, u32[]{:S(2)}, u32[]{:S(2)}) collective-permute-start(f32[128,512]{1,0:T(8,128)S(1)} %get-tuple-element.37.refs_0_.refs_2_), channel_id=1, source_target_pairs={{0,2},{1,3},{2,0},{3,1},{4,6},{5,7},{6,4},{7,5},{8,10},{9,11},{10,... | collective-permute-start | bytes 786440 | tf_op jit(solution)/shard_map/ppermute | solution.py:333
  18.3 9.3 %collective-permute-start.8 = (f32[128,512]{1,0:T(8,128)S(1)}, f32[128,512]{1,0:T(8,128)S(1)}, u32[]{:S(2)}, u32[]{:S(2)}) collective-permute-start(f32[128,512]{1,0:T(8,128)S(1)} %shard_map.89), channel_id=1, source_target_pairs={{0,8},{28,20},{8,16},{20,12},{1,9},{29,21},{9,17},{21,13},{2,10},{... | collective-permute-start | bytes 786440 | tf_op jit(solution)/shard_map/ppermute | solution.py:408
  21.9 9.5 %collective-permute-start.4 = (f32[128,512]{1,0:T(8,128)S(1)}, f32[128,512]{1,0:T(8,128)S(1)}, u32[]{:S(2)}, u32[]{:S(2)}) collective-permute-start(f32[128,512]{1,0:T(8,128)S(1)} %shard_map.84.refs_1_.refs_4_), channel_id=1, source_target_pairs={{0,8},{28,20},{8,16},{20,12},{1,9},{29,21},{9,17},{21,13},{2,10},{... | collective-permute-start | bytes 786440 | tf_op jit(solution)/shard_map/ppermute | solution.py:408
  24.5 12.4 %collective-permute-start.12 = (f32[128,512]{1,0:T(8,128)S(1)}, f32[128,512]{1,0:T(8,128)S(1)}, u32[]{:S(2)}, u32[]{:S(2)}) collective-permute-start(f32[128,512]{1,0:T(8,128)S(1)} %get-tuple-element.41), channel_id=1, source_target_pairs={{0,1},{1,0},{2,3},{3,2},{4,5},{5,4},{6,7},{7,6},{8,9},{9,8},{10,11... | collective-permute-start | bytes 786440 | tf_op jit(solution)/shard_map/ppermute | solution.py:333
  27.6 9.3 %collective-permute-start.11 = (f32[128,512]{1,0:T(8,128)S(1)}, f32[128,512]{1,0:T(8,128)S(1)}, u32[]{:S(2)}, u32[]{:S(2)}) collective-permute-start(f32[128,512]{1,0:T(8,128)S(1)} %shard_map.91.refs_4_), channel_id=1, source_target_pairs={{0,8},{28,20},{8,16},{20,12},{16,24},{12,4},{1,9},{29,21},{9,17},{... | collective-permute-start | bytes 786440 | tf_op jit(solution)/shard_map/ppermute | solution.py:408
  31.5 8.9 %collective-permute-start.10 = (f32[128,512]{1,0:T(8,128)S(1)}, f32[128,512]{1,0:T(8,128)S(1)}, u32[]{:S(2)}, u32[]{:S(2)}) collective-permute-start(f32[128,512]{1,0:T(8,128)S(1)} %shard_map.92.refs_1_.refs_4_), channel_id=1, source_target_pairs={{0,8},{28,20},{8,16},{20,12},{16,24},{12,4},{1,9},{29,21},{9,17},{... | collective-permute-start | bytes 786440 | tf_op jit(solution)/shard_map/ppermute | solution.py:408
  35.5 9.2 %collective-permute-start.15 = (f32[128,512]{1,0:T(8,128)S(1)}, f32[128,512]{1,0:T(8,128)S(1)}, u32[]{:S(2)}, u32[]{:S(2)}) collective-permute-start(f32[128,512]{1,0:T(8,128)S(1)} %get-tuple-element.42), channel_id=1, source_target_pairs={{0,3},{1,2},{2,1},{3,0},{4,7},{5,6},{6,5},{7,4},{8,11},{9,10},{10,... | collective-permute-start | bytes 786440 | tf_op jit(solution)/shard_map/ppermute | solution.py:333
  37.0 7.7 %collective-permute-start.14 = (f32[128,512]{1,0:T(8,128)S(1)}, f32[128,512]{1,0:T(8,128)S(1)}, u32[]{:S(2)}, u32[]{:S(2)}) collective-permute-start(f32[128,512]{1,0:T(8,128)S(1)} %shard_map.97.refs_4_), channel_id=1, source_target_pairs={{0,8},{28,20},{8,16},{20,12},{16,24},{12,4},{1,9},{29,21},{9,17},{... | collective-permute-start | bytes 786440 | tf_op jit(solution)/shard_map/ppermute | solution.py:408
  40.4 7.2 %collective-permute-start.13 = (f32[128,512]{1,0:T(8,128)S(1)}, f32[128,512]{1,0:T(8,128)S(1)}, u32[]{:S(2)}, u32[]{:S(2)}) collective-permute-start(f32[128,512]{1,0:T(8,128)S(1)} %shard_map.98.refs_3_), channel_id=1, source_target_pairs={{0,8},{28,20},{8,16},{20,12},{16,24},{12,4},{1,9},{29,21},{9,17},{... | collective-permute-start | bytes 786440 | tf_op jit(solution)/shard_map/ppermute | solution.py:408
  43.8 6.4 %collective-permute-start.9 = (f32[128,512]{1,0:T(8,128)S(1)}, f32[128,512]{1,0:T(8,128)S(1)}, u32[]{:S(2)}, u32[]{:S(2)}) collective-permute-start(f32[128,512]{1,0:T(8,128)S(1)} %get-tuple-element.39), channel_id=1, source_target_pairs={{0,2},{1,3},{2,0},{3,1},{4,6},{5,7},{6,4},{7,5},{8,10},{9,11},{10,... | collective-permute-start | bytes 786440 | tf_op jit(solution)/shard_map/ppermute | solution.py:333
  44.5 3.9 %collective-permute-start.18 = (f32[128,512]{1,0:T(8,128)S(1)}, f32[128,512]{1,0:T(8,128)S(1)}, u32[]{:S(2)}, u32[]{:S(2)}) collective-permute-start(f32[128,512]{1,0:T(8,128)S(1)} %shard_map.99.refs_5_), channel_id=1, source_target_pairs={{0,4},{4,0},{1,5},{5,1},{2,6},{6,2},{3,7},{7,3},{8,12},{12,8},{9,1... | collective-permute-start | bytes 786440 | tf_op jit(solution)/shard_map/ppermute | solution.py:336
  44.7 5.5 %collective-permute-start.17 = (f32[128,512]{1,0:T(8,128)S(1)}, f32[128,512]{1,0:T(8,128)S(1)}, u32[]{:S(2)}, u32[]{:S(2)}) collective-permute-start(f32[128,512]{1,0:T(8,128)S(1)} %shard_map.101.refs_3_), channel_id=1, source_target_pairs={{8,16},{20,12},{16,24},{12,4},{9,17},{21,13},{17,25},{13,5},{10,18... | collective-permute-start | bytes 786440 | tf_op jit(solution)/shard_map/ppermute | solution.py:408
  48.4 8.2 %collective-permute-start.20 = (f32[128,512]{1,0:T(8,128)S(1)}, f32[128,512]{1,0:T(8,128)S(1)}, u32[]{:S(2)}, u32[]{:S(2)}) collective-permute-start(f32[128,512]{1,0:T(8,128)S(1)} %shard_map.103.refs_4_), channel_id=1, source_target_pairs={{0,4},{4,0},{1,5},{5,1},{2,6},{6,2},{3,7},{7,3},{8,12},{12,8},{9,1... | collective-permute-start | bytes 786440 | tf_op jit(solution)/shard_map/ppermute | solution.py:336
  50.2 7.0 %collective-permute-start.21 = (f32[128,512]{1,0:T(8,128)S(1)}, f32[128,512]{1,0:T(8,128)S(1)}, u32[]{:S(2)}, u32[]{:S(2)}) collective-permute-start(f32[128,512]{1,0:T(8,128)S(1)} %shard_map.106.refs_2_), channel_id=1, source_target_pairs={{16,24},{12,4},{17,25},{13,5},{18,26},{14,6},{19,27},{15,7}} | collective-permute-start | bytes 786440 | tf_op jit(solution)/shard_map/ppermute | solution.py:408
  50.9 10.1 %collective-permute-start.19 = (f32[128,512]{1,0:T(8,128)S(1)}, f32[128,512]{1,0:T(8,128)S(1)}, u32[]{:S(2)}, u32[]{:S(2)}) collective-permute-start(f32[128,512]{1,0:T(8,128)S(1)} %shard_map.107.refs_3_.refs_8_), channel_id=1, source_target_pairs={{16,24},{12,4},{17,25},{13,5},{18,26},{14,6},{19,27},{15,7}} | collective-permute-start | bytes 786440 | tf_op jit(solution)/shard_map/ppermute | solution.py:408
  51.7 8.2 %collective-permute-start.23 = (f32[128,512]{1,0:T(8,128)S(1)}, f32[128,512]{1,0:T(8,128)S(1)}, u32[]{:S(2)}, u32[]{:S(2)}) collective-permute-start(f32[128,512]{1,0:T(8,128)S(1)} %shard_map.108.refs_3_), channel_id=1, source_target_pairs={{0,4},{4,0},{1,5},{5,1},{2,6},{6,2},{3,7},{7,3},{8,12},{12,8},{9,1... | collective-permute-start | bytes 786440 | tf_op jit(solution)/shard_map/ppermute | solution.py:336
  57.3 3.8 %collective-permute-start.22 = (f32[128,512]{1,0:T(8,128)S(1)}, f32[128,512]{1,0:T(8,128)S(1)}, u32[]{:S(2)}, u32[]{:S(2)}) collective-permute-start(f32[128,512]{1,0:T(8,128)S(1)} %shard_map.111.refs_6_), channel_id=1, source_target_pairs={{0,4},{4,0},{1,5},{5,1},{2,6},{6,2},{3,7},{7,3},{8,12},{12,8},{9,1... | collective-permute-start | bytes 786440 | tf_op jit(solution)/shard_map/ppermute | solution.py:336
  60.5 3.9 %collective-permute-start.29 = (f32[64,512]{1,0:T(8,128)S(1)}, f32[64,512]{1,0:T(8,128)S(1)}, u32[]{:S(2)}, u32[]{:S(2)}) collective-permute-start(f32[64,512]{1,0:T(8,128)S(1)} %get-tuple-element.55), channel_id=1, source_target_pairs={{0,4},{4,0},{1,5},{5,1},{2,6},{6,2},{3,7},{7,3},{8,12},{12,8},{9,1... | collective-permute-start | bytes 393224 | tf_op jit(solution)/shard_map/ppermute | solution.py:336
  61.8 4.3 %collective-permute-start.31 = (f32[64,512]{1,0:T(8,128)S(1)}, f32[64,512]{1,0:T(8,128)S(1)}, u32[]{:S(2)}, u32[]{:S(2)}) collective-permute-start(f32[64,512]{1,0:T(8,128)S(1)} %get-tuple-element.57), channel_id=1, source_target_pairs={{0,4},{4,0},{1,5},{5,1},{2,6},{6,2},{3,7},{7,3},{8,12},{12,8},{9,1... | collective-permute-start | bytes 393224 | tf_op jit(solution)/shard_map/ppermute | solution.py:336
  63.3 11.3 %collective-permute-start.26 = (f32[64,512]{1,0:T(8,128)S(1)}, f32[64,512]{1,0:T(8,128)S(1)}, u32[]{:S(2)}, u32[]{:S(2)}) collective-permute-start(f32[64,512]{1,0:T(8,128)S(1)} %get-tuple-element.51), channel_id=1, source_target_pairs={{0,4},{4,0},{1,5},{5,1},{2,6},{6,2},{3,7},{7,3},{8,12},{12,8},{9,1... | collective-permute-start | bytes 393224 | tf_op jit(solution)/shard_map/ppermute | solution.py:336
  63.4 12.8 %collective-permute-start.28 = (f32[64,512]{1,0:T(8,128)S(1)}, f32[64,512]{1,0:T(8,128)S(1)}, u32[]{:S(2)}, u32[]{:S(2)}) collective-permute-start(f32[64,512]{1,0:T(8,128)S(1)} %shard_map.118), channel_id=1, source_target_pairs={{0,1},{1,0},{2,3},{3,2},{4,5},{5,4},{6,7},{7,6},{8,9},{9,8},{10,11... | collective-permute-start | bytes 393224 | tf_op jit(solution)/shard_map/ppermute | solution.py:333
  64.4 11.8 %collective-permute-start.30 = (f32[64,512]{1,0:T(8,128)S(1)}, f32[64,512]{1,0:T(8,128)S(1)}, u32[]{:S(2)}, u32[]{:S(2)}) collective-permute-start(f32[64,512]{1,0:T(8,128)S(1)} %shard_map.119), channel_id=1, source_target_pairs={{0,3},{1,2},{2,1},{3,0},{4,7},{5,6},{6,5},{7,4},{8,11},{9,10},{10,... | collective-permute-start | bytes 393224 | tf_op jit(solution)/shard_map/ppermute | solution.py:333
  66.1 10.1 %collective-permute-start.32 = (f32[64,512]{1,0:T(8,128)S(1)}, f32[64,512]{1,0:T(8,128)S(1)}, u32[]{:S(2)}, u32[]{:S(2)}) collective-permute-start(f32[64,512]{1,0:T(8,128)S(1)} %shard_map.120), channel_id=1, source_target_pairs={{0,2},{1,3},{2,0},{3,1},{4,6},{5,7},{6,4},{7,5},{8,10},{9,11},{10,... | collective-permute-start | bytes 393224 | tf_op jit(solution)/shard_map/ppermute | solution.py:333
  70.7 5.5 %collective-permute-start.25 = (f32[8,128]{1,0:T(8,128)S(1)}, f32[8,128]{1,0:T(8,128)S(1)}, u32[]{:S(2)}, u32[]{:S(2)}) collective-permute-start(f32[8,128]{1,0:T(8,128)S(1)} %shard_map.115.refs_0_), channel_id=1, source_target_pairs={{0,16},{8,24},{16,0},{24,8},{1,17},{9,25},{17,1},{25,9},{2,18},{10... | collective-permute-start | bytes 12296 | tf_op jit(solution)/shard_map/ppermute | solution.py:464
  76.3 6.1 %collective-permute-start.35 = (f32[264,128]{1,0:T(8,128)S(1)}, f32[264,128]{1,0:T(8,128)S(1)}, u32[]{:S(2)}, u32[]{:S(2)}) collective-permute-start(f32[264,128]{1,0:T(8,128)S(1)} %shard_map.122.refs_4_.refs_0_), channel_id=1, source_target_pairs={{0,3},{1,2},{2,1},{3,0},{4,7},{5,6},{6,5},{7,4},{8,11},{9,10},{10,... | collective-permute-start | bytes 405512 | tf_op jit(solution)/shard_map/ppermute | solution.py:333
  77.2 6.5 %collective-permute-start.34 = (f32[264,128]{1,0:T(8,128)S(1)}, f32[264,128]{1,0:T(8,128)S(1)}, u32[]{:S(2)}, u32[]{:S(2)}) collective-permute-start(f32[264,128]{1,0:T(8,128)S(1)} %shard_map.122.refs_4_.refs_0_), channel_id=1, source_target_pairs={{0,2},{1,3},{2,0},{3,1},{4,6},{5,7},{6,4},{7,5},{8,10},{9,11},{10,... | collective-permute-start | bytes 405512 | tf_op jit(solution)/shard_map/ppermute | solution.py:333
  78.8 5.0 %collective-permute-start.33 = (f32[264,128]{1,0:T(8,128)S(1)}, f32[264,128]{1,0:T(8,128)S(1)}, u32[]{:S(2)}, u32[]{:S(2)}) collective-permute-start(f32[264,128]{1,0:T(8,128)S(1)} %shard_map.122.refs_4_.refs_0_), channel_id=1, source_target_pairs={{0,1},{1,0},{2,3},{3,2},{4,5},{5,4},{6,7},{7,6},{8,9},{9,8},{10,11... | collective-permute-start | bytes 405512 | tf_op jit(solution)/shard_map/ppermute | solution.py:333
  79.9 4.2 %collective-permute-start.36 = (f32[264,128]{1,0:T(8,128)S(1)}, f32[264,128]{1,0:T(8,128)S(1)}, u32[]{:S(2)}, u32[]{:S(2)}) collective-permute-start(f32[264,128]{1,0:T(8,128)S(1)} %shard_map.122.refs_4_.refs_0_), channel_id=1, source_target_pairs={{0,4},{4,0},{1,5},{5,1},{2,6},{6,2},{3,7},{7,3},{8,12},{12,8},{9,1... | collective-permute-start | bytes 405512 | tf_op jit(solution)/shard_map/ppermute | solution.py:336
  (13 other events, 48.2 us)

commit v18 on v15

--- a/solution.py
+++ b/solution.py
@@ -360,23 +360,14 @@
         (partial, partial_other, enc_bias.reshape(1, lats), active_blocks.T),
         after=(dict_wide,),
     )
-    gathered = [act] + [across(act, q) for q in range(1, n_tok)]
-    bias_here, *pieces = call(
-        pieces_kernel,
-        [f32(1, width)] + [f32(rows, width)] * n_tok,
-        (resid, dec_bias.reshape(1, half)),
-        after=(act,),
-    )
-    resids = [piece if q == 0 else across(piece, q) for q, piece in enumerate(pieces)]
-
     order = [0, 1, 3, 2] if n_tok == 4 else list(range(n_tok))
     steps = n_tok + n_lat - 2
     places = list(range(1, n_lat))
     acts, errs, hands, gives, gacts, loss = {}, {}, [], [], [], ()
     sums, got, sent = ([], []), ([], []), []
     waits = {step: [] for step in range(steps)}
-    for place, q in enumerate(order[1:]):
-        waits[min(3 + place, steps - 1)].append(resids[q])
+
+    gathered = {q: across(act, q) for q in order[1:-1]}
 
     def project(q, dicts):
         shape = [f32(rows, width * len(dicts))]
@@ -409,6 +400,18 @@
         if step + 1 < n_tok:
             q = order[step + 1]
             acts[q] = call(round_kernel, [bf16(rows, lats)], (gathered[q],), after=sent)[0]
+            if step == 1:
+                late = call(add_kernel, [f32(rows, lats)], (act,), after=sent)[0]
+                gathered[order[-1]] = across(late, order[-1])
+                bias_here, *pieces = call(
+                    pieces_kernel,
+                    [f32(1, width)] + [f32(rows, width)] * n_tok,
+                    (resid, dec_bias.reshape(1, half)),
+                    after=(late,),
+                )
+                resids = [piece if r == 0 else across(piece, r) for r, piece in enumerate(pieces)]
+                for place, r in enumerate(order[1:]):
+                    waits[min(3 + place, steps - 1)].append(resids[r])
             for side, dict_ref in enumerate((dict_other, dict_here)):
                 sums[side].append((project(q, (dict_ref,)), 0))
         ready = []

time: 84.8 us -> 84.3 us (level)
    ppermute x12, starting transfers between devices: 26 us -> 23.8 us  [body(): got[side].append((lax.ppermute(message, ('lat', 'wid'), pairs), 0))]
    ppermute x12, starting transfers between devices: 17.4 us -> 19.6 us  [across(): return lax.ppermute(array, 'tok', [(t, t ^ q) for t in range(n_tok)])]
    ppermute x14, starting transfers between devices: 10.5 us -> 11.6 us  [swap(): return lax.ppermute(array, 'wid', [(w, w ^ 1) for w in range(n_wid)])]
    ppermute x2, waiting for transfers between devices: 4.71 us -> 5.82 us  [body(): other = lax.ppermute(loss, 'lat', [(p, p ^ gap) for p in range(n_lat)])]
    ppermute x12, waiting for transfers between devices: 2.54 us -> 1.43 us  [body(): got[side].append((lax.ppermute(message, ('lat', 'wid'), pairs), 0))]
    ppermute x2, starting transfers between devices: 2.61 us -> 1.51 us  [body(): other = lax.ppermute(loss, 'lat', [(p, p ^ gap) for p in range(n_lat)])]
    pallas_call x48 -> x49, Pallas kernels: 11.6 us -> 11.6 us  [call(): pl.pallas_call(run, out_shape=outs, in_specs=list(specs or [VMEM] * len(a...]
  transfers between devices with their start and end apart: 40 -> 40, of which waited for: 8 -> 9; matrix products, arithmetic and copies ran while one was open for 0% -> 0% of each run, Pallas kernels for 9% -> 9%
where the time goes in v18:
time: 84.3 us; the launch traced here: 83.9 us
  starting transfers between devices  56.5 us (67%)
  waiting for transfers between devices  14.5 us (17%)
  Pallas kernels  11.6 us (14%)
  between operations  1.23 us (1%)
    ppermute x12, starting transfers between devices, body(): got[side].append((lax.ppermute(message, ('lat', 'wid'), pairs), 0))  23.8 us
    ppermute x12, starting transfers between devices, across(): return lax.ppermute(array, 'tok', [(t, t ^ q) for t in range(n_tok)])  19.6 us
    ppermute x14, starting transfers between devices, swap(): return lax.ppermute(array, 'wid', [(w, w ^ 1) for w in range(n_wid)])  11.6 us
    pallas_call x49, Pallas kernels, call(): pl.pallas_call(run, out_shape=outs, in_specs=list(specs or [VMEM] * len(a...  11.6 us
    ppermute x2, waiting for transfers between devices, body(): other = lax.ppermute(loss, 'lat', [(p, p ^ gap) for p in range(n_lat)])  5.82 us
    ppermute x12, waiting for transfers between devices, across(): return lax.ppermute(array, 'tok', [(t, t ^ q) for t in range(n_tok)])  5.22 us
    ppermute x14, waiting for transfers between devices, swap(): return lax.ppermute(array, 'wid', [(w, w ^ 1) for w in range(n_wid)])  2.03 us
  transfers between devices with their start and end apart: 40, of which 9 were waited for; matrix products, arithmetic and copies ran while one was open for 0% of the time, Pallas kernels for 9%

profile of v18, /device:TPU:0, one launch (start us, length us, event | category | flops | bytes accessed | tf_op | source)
XLA Modules:
  0.0 83.9 jit_solution(14612810024342292448)
XLA Ops:
  0.7 2.9 %shard_map.77 = (f32[128,512]{1,0:T(8,128)S(1)}, bf16[512,512]{1,0:T(8,128)(2,1)S(1)}) custom-call(bf16[128,2048]{1,0:T(8,128)(2,1)} %refs_0_.3, bf16[512,2048]{1,0:T(8,128)(2,1)} %refs_1_.1), custom_call_target="tpu_custom_call" | custom-call | bytes 1024 | tf_op jit(solution)/shard_map/pallas_call | solution.py:36
  4.1 1.2 %collective-permute-done.refs_2_.refs_1_ = f32[128,512]{1,0:T(8,128)S(1)} collective-permute-done((f32[128,512]{1,0:T(8,128)S(1)}, f32[128,512]{1,0:T(8,128)S(1)}, u32[]{:S(2)}, u32[]{:S(2)}) %collective-permute-start) | collective-permute-done | bytes 262176 | tf_op jit(solution)/shard_map/ppermute | solution.py:336
  6.1 2.7 %collective-permute-start.2 = (f32[128,512]{1,0:T(8,128)S(1)}, f32[128,512]{1,0:T(8,128)S(1)}, u32[]{:S(2)}, u32[]{:S(2)}) collective-permute-start(f32[128,512]{1,0:T(8,128)S(1)} %get-tuple-element.37.refs_0_), channel_id=1, source_target_pairs={{0,1},{1,0},{2,3},{3,2},{4,5},{5,4},{6,7},{7,6},{8,9},{9,8},{10,11... | collective-permute-start | bytes 786440 | tf_op jit(solution)/shard_map/ppermute | solution.py:333
  9.1 4.2 %collective-permute-start.7 = (f32[128,512]{1,0:T(8,128)S(1)}, f32[128,512]{1,0:T(8,128)S(1)}, u32[]{:S(2)}, u32[]{:S(2)}) collective-permute-start(f32[128,512]{1,0:T(8,128)S(1)} %shard_map.88.refs_2_.refs_3_), channel_id=1, source_target_pairs={{0,8},{28,20},{1,9},{29,21},{2,10},{30,22},{3,11},{31,23}} | collective-permute-start | bytes 786440 | tf_op jit(solution)/shard_map/ppermute | solution.py:387
  13.6 1.3 %collective-permute-start.1 = (f32[128,512]{1,0:T(8,128)S(1)}, f32[128,512]{1,0:T(8,128)S(1)}, u32[]{:S(2)}, u32[]{:S(2)}) collective-permute-start(f32[128,512]{1,0:T(8,128)S(1)} %shard_map.81.refs_1_.refs_2_.refs_3_), channel_id=1, source_target_pairs={{0,8},{28,20},{1,9},{29,21},{2,10},{30,22},{3,11},{31,23}} | collective-permute-start | bytes 786440 | tf_op jit(solution)/shard_map/ppermute | solution.py:387
  14.9 2.5 %collective-permute-start.5 = (f32[128,512]{1,0:T(8,128)S(1)}, f32[128,512]{1,0:T(8,128)S(1)}, u32[]{:S(2)}, u32[]{:S(2)}) collective-permute-start(f32[128,512]{1,0:T(8,128)S(1)} %get-tuple-element.37.refs_0_), channel_id=1, source_target_pairs={{0,3},{1,2},{2,1},{3,0},{4,7},{5,6},{6,5},{7,4},{8,11},{9,10},{10,... | collective-permute-start | bytes 786440 | tf_op jit(solution)/shard_map/ppermute | solution.py:333
  17.8 3.8 %collective-permute-start.8 = (f32[128,512]{1,0:T(8,128)S(1)}, f32[128,512]{1,0:T(8,128)S(1)}, u32[]{:S(2)}, u32[]{:S(2)}) collective-permute-start(f32[128,512]{1,0:T(8,128)S(1)} %shard_map.90), channel_id=1, source_target_pairs={{0,8},{28,20},{8,16},{20,12},{1,9},{29,21},{9,17},{21,13},{2,10},{... | collective-permute-start | bytes 786440 | tf_op jit(solution)/shard_map/ppermute | solution.py:398
  22.0 2.4 %collective-permute-start.4 = (f32[128,512]{1,0:T(8,128)S(1)}, f32[128,512]{1,0:T(8,128)S(1)}, u32[]{:S(2)}, u32[]{:S(2)}) collective-permute-start(f32[128,512]{1,0:T(8,128)S(1)} %shard_map.84.refs_1_.refs_4_), channel_id=1, source_target_pairs={{0,8},{28,20},{8,16},{20,12},{1,9},{29,21},{9,17},{21,13},{2,10},{... | collective-permute-start | bytes 786440 | tf_op jit(solution)/shard_map/ppermute | solution.py:398
  24.4 1.6 %collective-permute-start.3 = (f32[128,512]{1,0:T(8,128)S(1)}, f32[128,512]{1,0:T(8,128)S(1)}, u32[]{:S(2)}, u32[]{:S(2)}) collective-permute-start(f32[128,512]{1,0:T(8,128)S(1)} %shard_map.85.refs_2_), channel_id=1, source_target_pairs={{0,2},{1,3},{2,0},{3,1},{4,6},{5,7},{6,4},{7,5},{8,10},{9,11},{10,... | collective-permute-start | bytes 786440 | tf_op jit(solution)/shard_map/ppermute | solution.py:333
  26.1 1.6 %collective-permute-start.12 = (f32[128,512]{1,0:T(8,128)S(1)}, f32[128,512]{1,0:T(8,128)S(1)}, u32[]{:S(2)}, u32[]{:S(2)}) collective-permute-start(f32[128,512]{1,0:T(8,128)S(1)} %get-tuple-element.41), channel_id=1, source_target_pairs={{0,1},{1,0},{2,3},{3,2},{4,5},{5,4},{6,7},{7,6},{8,9},{9,8},{10,11... | collective-permute-start | bytes 786440 | tf_op jit(solution)/shard_map/ppermute | solution.py:333
  28.0 1.9 %collective-permute-start.11 = (f32[128,512]{1,0:T(8,128)S(1)}, f32[128,512]{1,0:T(8,128)S(1)}, u32[]{:S(2)}, u32[]{:S(2)}) collective-permute-start(f32[128,512]{1,0:T(8,128)S(1)} %shard_map.92.refs_4_), channel_id=1, source_target_pairs={{0,8},{28,20},{8,16},{20,12},{16,24},{12,4},{1,9},{29,21},{9,17},{... | collective-permute-start | bytes 786440 | tf_op jit(solution)/shard_map/ppermute | solution.py:398
  30.3 2.4 %collective-permute-start.10 = (f32[128,512]{1,0:T(8,128)S(1)}, f32[128,512]{1,0:T(8,128)S(1)}, u32[]{:S(2)}, u32[]{:S(2)}) collective-permute-start(f32[128,512]{1,0:T(8,128)S(1)} %shard_map.93.refs_1_.refs_4_), channel_id=1, source_target_pairs={{0,8},{28,20},{8,16},{20,12},{16,24},{12,4},{1,9},{29,21},{9,17},{... | collective-permute-start | bytes 786440 | tf_op jit(solution)/shard_map/ppermute | solution.py:398
  32.7 2.5 %collective-permute-start.15 = (f32[128,512]{1,0:T(8,128)S(1)}, f32[128,512]{1,0:T(8,128)S(1)}, u32[]{:S(2)}, u32[]{:S(2)}) collective-permute-start(f32[128,512]{1,0:T(8,128)S(1)} %get-tuple-element.42), channel_id=1, source_target_pairs={{0,3},{1,2},{2,1},{3,0},{4,7},{5,6},{6,5},{7,4},{8,11},{9,10},{10,... | collective-permute-start | bytes 786440 | tf_op jit(solution)/shard_map/ppermute | solution.py:333
  35.6 2.6 %collective-permute-start.14 = (f32[128,512]{1,0:T(8,128)S(1)}, f32[128,512]{1,0:T(8,128)S(1)}, u32[]{:S(2)}, u32[]{:S(2)}) collective-permute-start(f32[128,512]{1,0:T(8,128)S(1)} %shard_map.98.refs_4_), channel_id=1, source_target_pairs={{0,8},{28,20},{8,16},{20,12},{16,24},{12,4},{1,9},{29,21},{9,17},{... | collective-permute-start | bytes 786440 | tf_op jit(solution)/shard_map/ppermute | solution.py:398
  38.6 2.4 %collective-permute-start.13 = (f32[128,512]{1,0:T(8,128)S(1)}, f32[128,512]{1,0:T(8,128)S(1)}, u32[]{:S(2)}, u32[]{:S(2)}) collective-permute-start(f32[128,512]{1,0:T(8,128)S(1)} %shard_map.99.refs_3_), channel_id=1, source_target_pairs={{0,8},{28,20},{8,16},{20,12},{16,24},{12,4},{1,9},{29,21},{9,17},{... | collective-permute-start | bytes 786440 | tf_op jit(solution)/shard_map/ppermute | solution.py:398
  41.1 1.5 %collective-permute-start.9 = (f32[128,512]{1,0:T(8,128)S(1)}, f32[128,512]{1,0:T(8,128)S(1)}, u32[]{:S(2)}, u32[]{:S(2)}) collective-permute-start(f32[128,512]{1,0:T(8,128)S(1)} %get-tuple-element.39), channel_id=1, source_target_pairs={{0,2},{1,3},{2,0},{3,1},{4,6},{5,7},{6,4},{7,5},{8,10},{9,11},{10,... | collective-permute-start | bytes 786440 | tf_op jit(solution)/shard_map/ppermute | solution.py:333
  43.5 1.4 %collective-permute-done.13.refs_0_.refs_2_.refs_1_ = f32[128,512]{1,0:T(8,128)S(1)} collective-permute-done((f32[128,512]{1,0:T(8,128)S(1)}, f32[128,512]{1,0:T(8,128)S(1)}, u32[]{:S(2)}, u32[]{:S(2)}) %collective-permute-start.13) | collective-permute-done | bytes 262176 | tf_op jit(solution)/shard_map/ppermute | solution.py:398
  49.0 5.7 %collective-permute-start.23 = (f32[128,512]{1,0:T(8,128)S(1)}, f32[128,512]{1,0:T(8,128)S(1)}, u32[]{:S(2)}, u32[]{:S(2)}) collective-permute-start(f32[128,512]{1,0:T(8,128)S(1)} %shard_map.109.refs_3_), channel_id=1, source_target_pairs={{0,4},{4,0},{1,5},{5,1},{2,6},{6,2},{3,7},{7,3},{8,12},{12,8},{9,1... | collective-permute-start | bytes 786440 | tf_op jit(solution)/shard_map/ppermute | solution.py:336
  55.4 2.2 %collective-permute-start.22 = (f32[128,512]{1,0:T(8,128)S(1)}, f32[128,512]{1,0:T(8,128)S(1)}, u32[]{:S(2)}, u32[]{:S(2)}) collective-permute-start(f32[128,512]{1,0:T(8,128)S(1)} %shard_map.112.refs_6_), channel_id=1, source_target_pairs={{0,4},{4,0},{1,5},{5,1},{2,6},{6,2},{3,7},{7,3},{8,12},{12,8},{9,1... | collective-permute-start | bytes 786440 | tf_op jit(solution)/shard_map/ppermute | solution.py:336
  59.6 1.5 %collective-permute-start.31 = (f32[64,512]{1,0:T(8,128)S(1)}, f32[64,512]{1,0:T(8,128)S(1)}, u32[]{:S(2)}, u32[]{:S(2)}) collective-permute-start(f32[64,512]{1,0:T(8,128)S(1)} %get-tuple-element.57), channel_id=1, source_target_pairs={{0,4},{4,0},{1,5},{5,1},{2,6},{6,2},{3,7},{7,3},{8,12},{12,8},{9,1... | collective-permute-start | bytes 393224 | tf_op jit(solution)/shard_map/ppermute | solution.py:336
  61.2 1.6 %collective-permute-start.28 = (f32[64,512]{1,0:T(8,128)S(1)}, f32[64,512]{1,0:T(8,128)S(1)}, u32[]{:S(2)}, u32[]{:S(2)}) collective-permute-start(f32[64,512]{1,0:T(8,128)S(1)} %shard_map.119), channel_id=1, source_target_pairs={{0,1},{1,0},{2,3},{3,2},{4,5},{5,4},{6,7},{7,6},{8,9},{9,8},{10,11... | collective-permute-start | bytes 393224 | tf_op jit(solution)/shard_map/ppermute | solution.py:333
  63.4 1.5 %collective-permute-start.32 = (f32[64,512]{1,0:T(8,128)S(1)}, f32[64,512]{1,0:T(8,128)S(1)}, u32[]{:S(2)}, u32[]{:S(2)}) collective-permute-start(f32[64,512]{1,0:T(8,128)S(1)} %shard_map.121), channel_id=1, source_target_pairs={{0,2},{1,3},{2,0},{3,1},{4,6},{5,7},{6,4},{7,5},{8,10},{9,11},{10,... | collective-permute-start | bytes 393224 | tf_op jit(solution)/shard_map/ppermute | solution.py:333
  64.9 3.6 %collective-permute-done.24.refs_1_ = f32[8,128]{1,0:T(8,128)S(1)} collective-permute-done((f32[8,128]{1,0:T(8,128)S(1)}, f32[8,128]{1,0:T(8,128)S(1)}, u32[]{:S(2)}, u32[]{:S(2)}) %collective-permute-start.24) | collective-permute-done | bytes 4128 | tf_op jit(solution)/shard_map/ppermute | solution.py:466
  68.6 1.5 %collective-permute-start.25 = (f32[8,128]{1,0:T(8,128)S(1)}, f32[8,128]{1,0:T(8,128)S(1)}, u32[]{:S(2)}, u32[]{:S(2)}) collective-permute-start(f32[8,128]{1,0:T(8,128)S(1)} %shard_map.116.refs_0_), channel_id=1, source_target_pairs={{0,16},{8,24},{16,0},{24,8},{1,17},{9,25},{17,1},{25,9},{2,18},{10... | collective-permute-start | bytes 12296 | tf_op jit(solution)/shard_map/ppermute | solution.py:466
  70.1 0.8 shard_map.122.refs_7_.refs_11_
  70.8 2.2 %collective-permute-done.25.refs_1_ = f32[8,128]{1,0:T(8,128)S(1)} collective-permute-done((f32[8,128]{1,0:T(8,128)S(1)}, f32[8,128]{1,0:T(8,128)S(1)}, u32[]{:S(2)}, u32[]{:S(2)}) %collective-permute-start.25) | collective-permute-done | bytes 4128 | tf_op jit(solution)/shard_map/ppermute | solution.py:466
  73.2 1.5 %collective-permute-start.35 = (f32[264,128]{1,0:T(8,128)S(1)}, f32[264,128]{1,0:T(8,128)S(1)}, u32[]{:S(2)}, u32[]{:S(2)}) collective-permute-start(f32[264,128]{1,0:T(8,128)S(1)} %shard_map.123.refs_4_.refs_0_), channel_id=1, source_target_pairs={{0,3},{1,2},{2,1},{3,0},{4,7},{5,6},{6,5},{7,4},{8,11},{9,10},{10,... | collective-permute-start | bytes 405512 | tf_op jit(solution)/shard_map/ppermute | solution.py:333
  74.7 1.5 %collective-permute-start.34 = (f32[264,128]{1,0:T(8,128)S(1)}, f32[264,128]{1,0:T(8,128)S(1)}, u32[]{:S(2)}, u32[]{:S(2)}) collective-permute-start(f32[264,128]{1,0:T(8,128)S(1)} %shard_map.123.refs_4_.refs_0_), channel_id=1, source_target_pairs={{0,2},{1,3},{2,0},{3,1},{4,6},{5,7},{6,4},{7,5},{8,10},{9,11},{10,... | collective-permute-start | bytes 405512 | tf_op jit(solution)/shard_map/ppermute | solution.py:333
  76.8 3.1 %collective-permute-done.35.refs_7_.refs_3_ = f32[264,128]{1,0:T(8,128)S(1)} collective-permute-done((f32[264,128]{1,0:T(8,128)S(1)}, f32[264,128]{1,0:T(8,128)S(1)}, u32[]{:S(2)}, u32[]{:S(2)}) %collective-permute-start.35) | collective-permute-done | bytes 135200 | tf_op jit(solution)/shard_map/ppermute | solution.py:333
  79.9 1.0 %collective-permute-done.34.refs_6_.refs_2_ = f32[264,128]{1,0:T(8,128)S(1)} collective-permute-done((f32[264,128]{1,0:T(8,128)S(1)}, f32[264,128]{1,0:T(8,128)S(1)}, u32[]{:S(2)}, u32[]{:S(2)}) %collective-permute-start.34) | collective-permute-done | bytes 135200 | tf_op jit(solution)/shard_map/ppermute | solution.py:333
  81.4 0.8 collective-permute-done.37.refs_9_.refs_5_
  82.8 1.1 %shard_map.125 = (bf16[512,512]{1,0:T(8,128)(2,1)}, f32[4]{0:T(128)}) custom-call(f32[264,128]{1,0:T(8,128)S(1)} %shard_map.123.refs_4_.refs_0_, f32[264,128]{1,0:T(8,128)S(1)} %collective-permute-done.33.refs_5_.refs_1_, f32[264,128]{1,0:T(8,128)S(1)} %collective-permute-done.34.refs_6_.refs_2_, f32[264,128]{1,0:T(8,128)S(1)} %collective-permute-done.35.refs_7_.refs_3_, ...), custom_call_target="tpu_custom_call" | custom-call | bytes 1024 | tf_op jit(solution)/shard_map/pallas_call | solution.py:36
  (107 shorter events, 14.1 us)
Async XLA Ops:
  6.1 11.3 %collective-permute-start.2 = (f32[128,512]{1,0:T(8,128)S(1)}, f32[128,512]{1,0:T(8,128)S(1)}, u32[]{:S(2)}, u32[]{:S(2)}) collective-permute-start(f32[128,512]{1,0:T(8,128)S(1)} %get-tuple-element.37.refs_0_), channel_id=1, source_target_pairs={{0,1},{1,0},{2,3},{3,2},{4,5},{5,4},{6,7},{7,6},{8,9},{9,8},{10,11... | collective-permute-start | bytes 786440 | tf_op jit(solution)/shard_map/ppermute | solution.py:333
  9.1 8.7 %collective-permute-start.7 = (f32[128,512]{1,0:T(8,128)S(1)}, f32[128,512]{1,0:T(8,128)S(1)}, u32[]{:S(2)}, u32[]{:S(2)}) collective-permute-start(f32[128,512]{1,0:T(8,128)S(1)} %shard_map.88.refs_2_.refs_3_), channel_id=1, source_target_pairs={{0,8},{28,20},{1,9},{29,21},{2,10},{30,22},{3,11},{31,23}} | collective-permute-start | bytes 786440 | tf_op jit(solution)/shard_map/ppermute | solution.py:387
  13.6 8.3 %collective-permute-start.1 = (f32[128,512]{1,0:T(8,128)S(1)}, f32[128,512]{1,0:T(8,128)S(1)}, u32[]{:S(2)}, u32[]{:S(2)}) collective-permute-start(f32[128,512]{1,0:T(8,128)S(1)} %shard_map.81.refs_1_.refs_2_.refs_3_), channel_id=1, source_target_pairs={{0,8},{28,20},{1,9},{29,21},{2,10},{30,22},{3,11},{31,23}} | collective-permute-start | bytes 786440 | tf_op jit(solution)/shard_map/ppermute | solution.py:387
  14.9 12.7 %collective-permute-start.5 = (f32[128,512]{1,0:T(8,128)S(1)}, f32[128,512]{1,0:T(8,128)S(1)}, u32[]{:S(2)}, u32[]{:S(2)}) collective-permute-start(f32[128,512]{1,0:T(8,128)S(1)} %get-tuple-element.37.refs_0_), channel_id=1, source_target_pairs={{0,3},{1,2},{2,1},{3,0},{4,7},{5,6},{6,5},{7,4},{8,11},{9,10},{10,... | collective-permute-start | bytes 786440 | tf_op jit(solution)/shard_map/ppermute | solution.py:333
  17.8 10.2 %collective-permute-start.8 = (f32[128,512]{1,0:T(8,128)S(1)}, f32[128,512]{1,0:T(8,128)S(1)}, u32[]{:S(2)}, u32[]{:S(2)}) collective-permute-start(f32[128,512]{1,0:T(8,128)S(1)} %shard_map.90), channel_id=1, source_target_pairs={{0,8},{28,20},{8,16},{20,12},{1,9},{29,21},{9,17},{21,13},{2,10},{... | collective-permute-start | bytes 786440 | tf_op jit(solution)/shard_map/ppermute | solution.py:398
  22.0 8.3 %collective-permute-start.4 = (f32[128,512]{1,0:T(8,128)S(1)}, f32[128,512]{1,0:T(8,128)S(1)}, u32[]{:S(2)}, u32[]{:S(2)}) collective-permute-start(f32[128,512]{1,0:T(8,128)S(1)} %shard_map.84.refs_1_.refs_4_), channel_id=1, source_target_pairs={{0,8},{28,20},{8,16},{20,12},{1,9},{29,21},{9,17},{21,13},{2,10},{... | collective-permute-start | bytes 786440 | tf_op jit(solution)/shard_map/ppermute | solution.py:398
  24.4 10.8 %collective-permute-start.3 = (f32[128,512]{1,0:T(8,128)S(1)}, f32[128,512]{1,0:T(8,128)S(1)}, u32[]{:S(2)}, u32[]{:S(2)}) collective-permute-start(f32[128,512]{1,0:T(8,128)S(1)} %shard_map.85.refs_2_), channel_id=1, source_target_pairs={{0,2},{1,3},{2,0},{3,1},{4,6},{5,7},{6,4},{7,5},{8,10},{9,11},{10,... | collective-permute-start | bytes 786440 | tf_op jit(solution)/shard_map/ppermute | solution.py:333
  26.1 9.5 %collective-permute-start.12 = (f32[128,512]{1,0:T(8,128)S(1)}, f32[128,512]{1,0:T(8,128)S(1)}, u32[]{:S(2)}, u32[]{:S(2)}) collective-permute-start(f32[128,512]{1,0:T(8,128)S(1)} %get-tuple-element.41), channel_id=1, source_target_pairs={{0,1},{1,0},{2,3},{3,2},{4,5},{5,4},{6,7},{7,6},{8,9},{9,8},{10,11... | collective-permute-start | bytes 786440 | tf_op jit(solution)/shard_map/ppermute | solution.py:333
  28.0 7.6 %collective-permute-start.11 = (f32[128,512]{1,0:T(8,128)S(1)}, f32[128,512]{1,0:T(8,128)S(1)}, u32[]{:S(2)}, u32[]{:S(2)}) collective-permute-start(f32[128,512]{1,0:T(8,128)S(1)} %shard_map.92.refs_4_), channel_id=1, source_target_pairs={{0,8},{28,20},{8,16},{20,12},{16,24},{12,4},{1,9},{29,21},{9,17},{... | collective-permute-start | bytes 786440 | tf_op jit(solution)/shard_map/ppermute | solution.py:398
  30.3 8.2 %collective-permute-start.10 = (f32[128,512]{1,0:T(8,128)S(1)}, f32[128,512]{1,0:T(8,128)S(1)}, u32[]{:S(2)}, u32[]{:S(2)}) collective-permute-start(f32[128,512]{1,0:T(8,128)S(1)} %shard_map.93.refs_1_.refs_4_), channel_id=1, source_target_pairs={{0,8},{28,20},{8,16},{20,12},{16,24},{12,4},{1,9},{29,21},{9,17},{... | collective-permute-start | bytes 786440 | tf_op jit(solution)/shard_map/ppermute | solution.py:398
  32.7 10.1 %collective-permute-start.15 = (f32[128,512]{1,0:T(8,128)S(1)}, f32[128,512]{1,0:T(8,128)S(1)}, u32[]{:S(2)}, u32[]{:S(2)}) collective-permute-start(f32[128,512]{1,0:T(8,128)S(1)} %get-tuple-element.42), channel_id=1, source_target_pairs={{0,3},{1,2},{2,1},{3,0},{4,7},{5,6},{6,5},{7,4},{8,11},{9,10},{10,... | collective-permute-start | bytes 786440 | tf_op jit(solution)/shard_map/ppermute | solution.py:333
  35.6 7.2 %collective-permute-start.14 = (f32[128,512]{1,0:T(8,128)S(1)}, f32[128,512]{1,0:T(8,128)S(1)}, u32[]{:S(2)}, u32[]{:S(2)}) collective-permute-start(f32[128,512]{1,0:T(8,128)S(1)} %shard_map.98.refs_4_), channel_id=1, source_target_pairs={{0,8},{28,20},{8,16},{20,12},{16,24},{12,4},{1,9},{29,21},{9,17},{... | collective-permute-start | bytes 786440 | tf_op jit(solution)/shard_map/ppermute | solution.py:398
  38.6 6.3 %collective-permute-start.13 = (f32[128,512]{1,0:T(8,128)S(1)}, f32[128,512]{1,0:T(8,128)S(1)}, u32[]{:S(2)}, u32[]{:S(2)}) collective-permute-start(f32[128,512]{1,0:T(8,128)S(1)} %shard_map.99.refs_3_), channel_id=1, source_target_pairs={{0,8},{28,20},{8,16},{20,12},{16,24},{12,4},{1,9},{29,21},{9,17},{... | collective-permute-start | bytes 786440 | tf_op jit(solution)/shard_map/ppermute | solution.py:398
  41.1 6.4 %collective-permute-start.9 = (f32[128,512]{1,0:T(8,128)S(1)}, f32[128,512]{1,0:T(8,128)S(1)}, u32[]{:S(2)}, u32[]{:S(2)}) collective-permute-start(f32[128,512]{1,0:T(8,128)S(1)} %get-tuple-element.39), channel_id=1, source_target_pairs={{0,2},{1,3},{2,0},{3,1},{4,6},{5,7},{6,4},{7,5},{8,10},{9,11},{10,... | collective-permute-start | bytes 786440 | tf_op jit(solution)/shard_map/ppermute | solution.py:333
  42.8 4.7 %collective-permute-start.17 = (f32[128,512]{1,0:T(8,128)S(1)}, f32[128,512]{1,0:T(8,128)S(1)}, u32[]{:S(2)}, u32[]{:S(2)}) collective-permute-start(f32[128,512]{1,0:T(8,128)S(1)} %shard_map.102.refs_3_), channel_id=1, source_target_pairs={{8,16},{20,12},{16,24},{12,4},{9,17},{21,13},{17,25},{13,5},{10,18... | collective-permute-start | bytes 786440 | tf_op jit(solution)/shard_map/ppermute | solution.py:398
  45.7 9.0 %collective-permute-start.20 = (f32[128,512]{1,0:T(8,128)S(1)}, f32[128,512]{1,0:T(8,128)S(1)}, u32[]{:S(2)}, u32[]{:S(2)}) collective-permute-start(f32[128,512]{1,0:T(8,128)S(1)} %shard_map.104.refs_4_), channel_id=1, source_target_pairs={{0,4},{4,0},{1,5},{5,1},{2,6},{6,2},{3,7},{7,3},{8,12},{12,8},{9,1... | collective-permute-start | bytes 786440 | tf_op jit(solution)/shard_map/ppermute | solution.py:336
  47.5 7.8 %collective-permute-start.21 = (f32[128,512]{1,0:T(8,128)S(1)}, f32[128,512]{1,0:T(8,128)S(1)}, u32[]{:S(2)}, u32[]{:S(2)}) collective-permute-start(f32[128,512]{1,0:T(8,128)S(1)} %shard_map.107.refs_2_), channel_id=1, source_target_pairs={{16,24},{12,4},{17,25},{13,5},{18,26},{14,6},{19,27},{15,7}} | collective-permute-start | bytes 786440 | tf_op jit(solution)/shard_map/ppermute | solution.py:398
  48.2 10.7 %collective-permute-start.19 = (f32[128,512]{1,0:T(8,128)S(1)}, f32[128,512]{1,0:T(8,128)S(1)}, u32[]{:S(2)}, u32[]{:S(2)}) collective-permute-start(f32[128,512]{1,0:T(8,128)S(1)} %shard_map.108.refs_3_.refs_8_), channel_id=1, source_target_pairs={{16,24},{12,4},{17,25},{13,5},{18,26},{14,6},{19,27},{15,7}} | collective-permute-start | bytes 786440 | tf_op jit(solution)/shard_map/ppermute | solution.py:398
  49.0 8.7 %collective-permute-start.23 = (f32[128,512]{1,0:T(8,128)S(1)}, f32[128,512]{1,0:T(8,128)S(1)}, u32[]{:S(2)}, u32[]{:S(2)}) collective-permute-start(f32[128,512]{1,0:T(8,128)S(1)} %shard_map.109.refs_3_), channel_id=1, source_target_pairs={{0,4},{4,0},{1,5},{5,1},{2,6},{6,2},{3,7},{7,3},{8,12},{12,8},{9,1... | collective-permute-start | bytes 786440 | tf_op jit(solution)/shard_map/ppermute | solution.py:336
  57.6 3.6 %collective-permute-start.27 = (f32[64,512]{1,0:T(8,128)S(1)}, f32[64,512]{1,0:T(8,128)S(1)}, u32[]{:S(2)}, u32[]{:S(2)}) collective-permute-start(f32[64,512]{1,0:T(8,128)S(1)} %get-tuple-element.53), channel_id=1, source_target_pairs={{0,4},{4,0},{1,5},{5,1},{2,6},{6,2},{3,7},{7,3},{8,12},{12,8},{9,1... | collective-permute-start | bytes 393224 | tf_op jit(solution)/shard_map/ppermute | solution.py:336
  58.4 4.4 %collective-permute-start.29 = (f32[64,512]{1,0:T(8,128)S(1)}, f32[64,512]{1,0:T(8,128)S(1)}, u32[]{:S(2)}, u32[]{:S(2)}) collective-permute-start(f32[64,512]{1,0:T(8,128)S(1)} %get-tuple-element.55), channel_id=1, source_target_pairs={{0,4},{4,0},{1,5},{5,1},{2,6},{6,2},{3,7},{7,3},{8,12},{12,8},{9,1... | collective-permute-start | bytes 393224 | tf_op jit(solution)/shard_map/ppermute | solution.py:336
  59.6 3.8 %collective-permute-start.31 = (f32[64,512]{1,0:T(8,128)S(1)}, f32[64,512]{1,0:T(8,128)S(1)}, u32[]{:S(2)}, u32[]{:S(2)}) collective-permute-start(f32[64,512]{1,0:T(8,128)S(1)} %get-tuple-element.57), channel_id=1, source_target_pairs={{0,4},{4,0},{1,5},{5,1},{2,6},{6,2},{3,7},{7,3},{8,12},{12,8},{9,1... | collective-permute-start | bytes 393224 | tf_op jit(solution)/shard_map/ppermute | solution.py:336
  61.1 9.0 %collective-permute-start.26 = (f32[64,512]{1,0:T(8,128)S(1)}, f32[64,512]{1,0:T(8,128)S(1)}, u32[]{:S(2)}, u32[]{:S(2)}) collective-permute-start(f32[64,512]{1,0:T(8,128)S(1)} %get-tuple-element.51), channel_id=1, source_target_pairs={{0,4},{4,0},{1,5},{5,1},{2,6},{6,2},{3,7},{7,3},{8,12},{12,8},{9,1... | collective-permute-start | bytes 393224 | tf_op jit(solution)/shard_map/ppermute | solution.py:336
  61.2 11.9 %collective-permute-start.28 = (f32[64,512]{1,0:T(8,128)S(1)}, f32[64,512]{1,0:T(8,128)S(1)}, u32[]{:S(2)}, u32[]{:S(2)}) collective-permute-start(f32[64,512]{1,0:T(8,128)S(1)} %shard_map.119), channel_id=1, source_target_pairs={{0,1},{1,0},{2,3},{3,2},{4,5},{5,4},{6,7},{7,6},{8,9},{9,8},{10,11... | collective-permute-start | bytes 393224 | tf_op jit(solution)/shard_map/ppermute | solution.py:333
  62.8 10.3 %collective-permute-start.30 = (f32[64,512]{1,0:T(8,128)S(1)}, f32[64,512]{1,0:T(8,128)S(1)}, u32[]{:S(2)}, u32[]{:S(2)}) collective-permute-start(f32[64,512]{1,0:T(8,128)S(1)} %shard_map.120), channel_id=1, source_target_pairs={{0,3},{1,2},{2,1},{3,0},{4,7},{5,6},{6,5},{7,4},{8,11},{9,10},{10,... | collective-permute-start | bytes 393224 | tf_op jit(solution)/shard_map/ppermute | solution.py:333
  63.4 9.7 %collective-permute-start.32 = (f32[64,512]{1,0:T(8,128)S(1)}, f32[64,512]{1,0:T(8,128)S(1)}, u32[]{:S(2)}, u32[]{:S(2)}) collective-permute-start(f32[64,512]{1,0:T(8,128)S(1)} %shard_map.121), channel_id=1, source_target_pairs={{0,2},{1,3},{2,0},{3,1},{4,6},{5,7},{6,4},{7,5},{8,10},{9,11},{10,... | collective-permute-start | bytes 393224 | tf_op jit(solution)/shard_map/ppermute | solution.py:333
  64.9 3.6 %collective-permute-start.24 = (f32[8,128]{1,0:T(8,128)S(1)}, f32[8,128]{1,0:T(8,128)S(1)}, u32[]{:S(2)}, u32[]{:S(2)}) collective-permute-start(f32[8,128]{1,0:T(8,128)S(1)} %get-tuple-element.49.refs_0_), channel_id=1, source_target_pairs={{0,8},{8,0},{16,24},{24,16},{1,9},{9,1},{17,25},{25,17},{2,10},{10... | collective-permute-start | bytes 12296 | tf_op jit(solution)/shard_map/ppermute | solution.py:466
  68.6 4.5 %collective-permute-start.25 = (f32[8,128]{1,0:T(8,128)S(1)}, f32[8,128]{1,0:T(8,128)S(1)}, u32[]{:S(2)}, u32[]{:S(2)}) collective-permute-start(f32[8,128]{1,0:T(8,128)S(1)} %shard_map.116.refs_0_), channel_id=1, source_target_pairs={{0,16},{8,24},{16,0},{24,8},{1,17},{9,25},{17,1},{25,9},{2,18},{10... | collective-permute-start | bytes 12296 | tf_op jit(solution)/shard_map/ppermute | solution.py:466
  73.2 6.6 %collective-permute-start.35 = (f32[264,128]{1,0:T(8,128)S(1)}, f32[264,128]{1,0:T(8,128)S(1)}, u32[]{:S(2)}, u32[]{:S(2)}) collective-permute-start(f32[264,128]{1,0:T(8,128)S(1)} %shard_map.123.refs_4_.refs_0_), channel_id=1, source_target_pairs={{0,3},{1,2},{2,1},{3,0},{4,7},{5,6},{6,5},{7,4},{8,11},{9,10},{10,... | collective-permute-start | bytes 405512 | tf_op jit(solution)/shard_map/ppermute | solution.py:333
  74.7 6.2 %collective-permute-start.34 = (f32[264,128]{1,0:T(8,128)S(1)}, f32[264,128]{1,0:T(8,128)S(1)}, u32[]{:S(2)}, u32[]{:S(2)}) collective-permute-start(f32[264,128]{1,0:T(8,128)S(1)} %shard_map.123.refs_4_.refs_0_), channel_id=1, source_target_pairs={{0,2},{1,3},{2,0},{3,1},{4,6},{5,7},{6,4},{7,5},{8,10},{9,11},{10,... | collective-permute-start | bytes 405512 | tf_op jit(solution)/shard_map/ppermute | solution.py:333
  76.2 5.0 %collective-permute-start.33 = (f32[264,128]{1,0:T(8,128)S(1)}, f32[264,128]{1,0:T(8,128)S(1)}, u32[]{:S(2)}, u32[]{:S(2)}) collective-permute-start(f32[264,128]{1,0:T(8,128)S(1)} %shard_map.123.refs_4_.refs_0_), channel_id=1, source_target_pairs={{0,1},{1,0},{2,3},{3,2},{4,5},{5,4},{6,7},{7,6},{8,9},{9,8},{10,11... | collective-permute-start | bytes 405512 | tf_op jit(solution)/shard_map/ppermute | solution.py:333
  76.8 4.6 %collective-permute-start.36 = (f32[264,128]{1,0:T(8,128)S(1)}, f32[264,128]{1,0:T(8,128)S(1)}, u32[]{:S(2)}, u32[]{:S(2)}) collective-permute-start(f32[264,128]{1,0:T(8,128)S(1)} %shard_map.123.refs_4_.refs_0_), channel_id=1, source_target_pairs={{0,4},{4,0},{1,5},{5,1},{2,6},{6,2},{3,7},{7,3},{8,12},{12,8},{9,1... | collective-permute-start | bytes 405512 | tf_op jit(solution)/shard_map/ppermute | solution.py:336
  (13 other events, 51.3 us)
